TPU v7x, 32 devices: a whole 2x2x4 slice. The times are simulated.
32 devices in a mesh: grp: 2 (over y), tp: 4 (over z), dp: 4 (over x, core).
Axes of the slice: x: 2, y: 2, z: 4, core: 2. Of those that a mesh axis runs over, the one named last changes fastest.
Arguments:
- tokens: bfloat16 [1024, 8192], P(('grp', 'dp'), 'tp'), parts along dimension 0, may hold values from -6 to 6
- frozen_up_weight: bfloat16 [8192, 28672], P('dp', 'tp'), may hold values from -0.0625 to 0.0625
- adapter_down: bfloat16 [32, 8192, 64], P('dp', 'tp'), may hold values from -0.0625 to 0.0625
- adapter_up: bfloat16 [32, 64, 28672], P('dp', None, 'tp'), may hold values from -0.03125 to 0.03125
- cotangent: bfloat16 [1024, 28672], P(('grp', 'dp'), 'tp'), parts along dimension 0, may hold values from -0.59765625 to 0.59765625
- block_adapter: int32 [8], P('grp'), parts along dimension 0, may hold values from 0 to 31
- block_length: int32 [8], P('grp'), parts along dimension 0, may hold values from 1 to 128, as said below
- adapter_slot: int32 [32], replicated, may hold values from 0 to 31, each once
Outputs:
- projected: bfloat16 [1024, 28672], P(('grp', 'dp'), 'tp'), parts along dimension 0
- tokens_grad: bfloat16 [1024, 8192], P(('grp', 'dp'), 'tp'), parts along dimension 0
- down_grad: float32 [64, 8192, 64], P(('grp', 'dp'), 'tp'), parts along dimension 0
- up_grad: float32 [64, 64, 28672], P(('grp', 'dp'), None, 'tp'), parts along dimension 0
There are 2 independent parts, one for each index of `grp`. A program takes and returns all parts, laid end to end along the dimension named above; an argument that names none is the same for every part. Nothing has to cross between parts.
Inputs may be any that keep to these rules, and one draw needn't show every extreme that they name: `block_adapter`: each block of 128 tokens serves the one adapter named here. The first block_length[k] tokens of block k are live, the rest are padding; some block is full. A permutation: adapter a's factors and gradients are entry adapter_slot[a] of the stores, held by dp index adapter_slot[a] // 8.
All inputs are finite; a program needn't handle non-finite values.
Results may differ from a plain program's by a relative error of at most 0.0028.
Values may be sent and summed in bfloat16 or wider, within the bound.
No kernel may reach another device: no remote copies, remote signals or barrier semaphores. Data moves between devices by JAX's collectives and lax.ppermute only.
A program may use at most 384 MiB of HBM per device.

v0:
```python
import jax
import jax.numpy as jnp
from jax import lax
from jax.sharding import PartitionSpec as P

SEGMENT_BLOCK = 128


adapter_scale = 2.0
highest_precision = lax.Precision.HIGHEST


def local(
    tokens,
    frozen_up_weight,
    adapter_down,
    adapter_up,
    cotangent,
    block_adapter,
    block_length,
    adapter_slot,
):
    token_rows, width_part = tokens.shape
    hidden_slice = frozen_up_weight.shape[1]
    per_owner = adapter_down.shape[0]
    rank_width = adapter_down.shape[2]
    tenant_groups = lax.axis_size("dp")
    my_group = lax.axis_index("dp")
    resident_blocks = token_rows // SEGMENT_BLOCK
    total_blocks = resident_blocks * tenant_groups
    table_match = (
        block_adapter[:, None] == jnp.arange(adapter_slot.shape[0], dtype=jnp.int32)[None, :]
    )
    slot_ids = jnp.sum(jnp.where(table_match, adapter_slot[None, :], 0), axis=1)
    owner_ids = slot_ids // per_owner
    local_ids = slot_ids % per_owner
    live_mask = (
        lax.broadcasted_iota(jnp.int32, (total_blocks, SEGMENT_BLOCK), 1) < block_length[:, None]
    )
    owned_here = owner_ids == my_group
    home_start = my_group * resident_blocks
    home_live = lax.dynamic_slice_in_dim(live_mask, home_start, resident_blocks, 0)
    home_owner = lax.dynamic_slice_in_dim(owner_ids, home_start, resident_blocks, 0)
    live_tok = home_live[:, :, None].astype(jnp.bfloat16)
    token_blocks = tokens.reshape(resident_blocks, SEGMENT_BLOCK, width_part) * live_tok
    cotangent_blocks = cotangent.reshape(resident_blocks, SEGMENT_BLOCK, hidden_slice) * live_tok
    targets = home_owner[None, :] == jnp.arange(tenant_groups, dtype=jnp.int32)[:, None]
    gathered = lax.all_gather(tokens, "tp", axis=1, tiled=True)
    full_weight = lax.all_gather(frozen_up_weight, "dp", axis=0, tiled=True)
    frozen_output = jnp.dot(gathered, full_weight, preferred_element_type=jnp.float32)
    partial_grad = lax.dot_general(
        cotangent, full_weight, (((1,), (1,)), ((), ())), preferred_element_type=jnp.float32
    )
    base_grad = lax.psum_scatter(partial_grad, "tp", scatter_dimension=1, tiled=True)
    down_send = jnp.where(
        owned_here[:, None, None], adapter_down[local_ids], jnp.zeros((), jnp.bfloat16)
    )
    up_send = jnp.where(
        owned_here[:, None, None], adapter_up[local_ids], jnp.zeros((), jnp.bfloat16)
    )
    down_send = down_send.reshape(tenant_groups, resident_blocks, width_part, rank_width)
    up_send = up_send.reshape(tenant_groups, resident_blocks, rank_width, hidden_slice)
    down_got, up_got = (
        lax.all_to_all(down_send, "dp", split_axis=0, concat_axis=0, tiled=True),
        lax.all_to_all(up_send, "dp", split_axis=0, concat_axis=0, tiled=True),
    )
    down_mine = jnp.sum(down_got, axis=0)
    up_mine = jnp.sum(up_got, axis=0)
    rank_inner = jnp.einsum(
        "nbd,ndr->nbr", token_blocks, down_mine, preferred_element_type=jnp.float32
    )
    rank_inner = lax.psum(rank_inner, "tp")
    inner_adapter_product = rank_inner.astype(jnp.bfloat16)
    adapter_delta = adapter_scale * jnp.einsum(
        "nbr,nrf->nbf", inner_adapter_product, up_mine, preferred_element_type=jnp.float32
    )
    adapter_delta = adapter_delta.reshape(token_rows, hidden_slice)
    rank_return = adapter_scale * jnp.einsum(
        "nbf,nrf->nbr", cotangent_blocks, up_mine, preferred_element_type=jnp.float32
    )
    rank_return = lax.psum(rank_return, "tp")
    back_b = rank_return.astype(jnp.bfloat16)
    correction = jnp.einsum("nbr,ndr->nbd", back_b, down_mine, preferred_element_type=jnp.float32)
    correction = correction.reshape(token_rows, width_part)
    up_local = adapter_scale * jnp.einsum(
        "nbr,nbf->nrf", inner_adapter_product, cotangent_blocks, preferred_element_type=jnp.float32
    )
    down_local = jnp.einsum(
        "nbd,nbr->ndr", token_blocks, back_b, preferred_element_type=jnp.float32
    )
    down_out = jnp.where(targets[:, :, None, None], down_local[None], 0.0)
    up_out = jnp.where(targets[:, :, None, None], up_local[None], 0.0)
    down_terms, up_products = (
        lax.all_to_all(down_out, "dp", split_axis=0, concat_axis=0, tiled=True),
        lax.all_to_all(up_out, "dp", split_axis=0, concat_axis=0, tiled=True),
    )
    down_terms = down_terms.reshape(total_blocks, width_part, rank_width)
    up_products = up_products.reshape(total_blocks, rank_width, hidden_slice)
    selector = (
        (local_ids[None, :] == jnp.arange(per_owner, dtype=jnp.int32)[:, None])
        & owned_here[None, :]
    ).astype(jnp.float32)
    down_grad = jnp.einsum("lg,gdr->ldr", selector, down_terms, precision=highest_precision)
    up_grad = jnp.einsum("lg,grf->lrf", selector, up_products, precision=highest_precision)
    projected = (frozen_output + adapter_delta).astype(jnp.bfloat16)
    tokens_grad = (base_grad + correction).astype(jnp.bfloat16)
    return (projected, tokens_grad, down_grad, up_grad)


def solution(mesh):
    placed = (
        P(("grp", "dp"), "tp"),
        P("dp", "tp"),
        P("dp", "tp", None),
        P("dp", None, "tp"),
        P(("grp", "dp"), "tp"),
        P("grp"),
        P("grp"),
        P(),
    )
    return jax.shard_map(
        local,
        mesh=mesh,
        in_specs=placed,
        out_specs=(
            P(("grp", "dp"), "tp"),
            P(("grp", "dp"), "tp"),
            P(("grp", "dp"), "tp", None),
            P(("grp", "dp"), None, "tp"),
        ),
        check_vma=False,
    )
```

profile of v0, /device:TPU:2, one launch (start us, length us, event | category | flops | bytes accessed | tf_op | source)
XLA Modules:
  0.0 959.3 jit_solution(18294200619951425308)
XLA Ops:
  7.2 0.0 copy-start
  7.2 0.0 copy-start.14
  7.2 0.0 copy-start.15
  7.2 0.0 all-gather.5.cloned.1.call-start
  7.2 0.7 all-gather.5.cloned.1.call-update
  7.9 0.0 copy-done.14
  8.0 0.0 copy-done.15
  8.0 0.2 select_reduce_fusion
  8.2 0.6 copy-done
  8.8 0.6 gather_fusion
  9.4 0.0 copy-start.7
  9.4 1.1 bitcast_select_fusion.1
  10.6 0.0 copy-done.12
  10.6 3.5 all-to-all-start
  14.1 6.4 gather_fusion.1
  20.5 0.0 copy-done.7
  20.5 6.6 bitcast_select_fusion
  27.0 0.0 all-to-all-done
  27.0 6.3 all-to-all-start.1
  33.4 0.0 all-gather.3.cloned.1.call-start
  33.4 0.7 all-gather.3.cloned.1.call-update
  34.1 0.6 dynamic_slice.7
  34.7 1.2 iota_compare_fusion.3
  35.9 0.0 copy-done.16
  35.9 0.1 iota_compare_fusion.2
  36.0 0.2 bitcast_reduce_fusion
  36.2 0.0 copy-start.4
  36.2 2.3 convolution_bitcast_fusion
  38.5 56.8 %all-to-all-done.1 = bf16[4,1,64,7168]{3,2,1,0:T(8,128)(2,1)} async-done(((bf16[4,1,64,7168]{3,2,1,0:T(8,128)(2,1)}), bf16[4,1,64,7168]{3,2,1,0:T(8,128)(2,1)}, u32[]{:S(2)}, u32[]{:S(2)}) %all-to-all-start.1) | async-done | bytes 3670048 | tf_op jit(solution)/shard_map/all_to_all | solution.py:65
  95.3 2.8 reduce_sum.38
  98.1 0.0 copy-done.10
  98.1 0.0 copy-done.2
  98.1 1.4 fusion.15
  99.5 0.0 copy-done.4
  99.5 22.5 %all-reduce = (bf16[1,128,64]{1,2,0:T(8,128)(2,1)}, bf16[1,128,64]{1,2,0:T(8,128)(2,1)S(1)}) all-reduce(f32[1,128,64]{1,2,0:T(8,128)} %convolution_bitcast_fusion, f32[1,128,64]{1,2,0:T(8,128)} %fusion.15), channel_id=1, replica_groups=mesh['grp'=2,'tp'=4,'dp'=4] {'tp'}, use_global_device_ids=true, to_apply=%region_2.3 | all-reduce | flops 16384 | bytes 98304 | tf_op jit(solution)/shard_map/psum | solution.py:72
  122.0 0.0 copy-done.3
  122.0 1.0 fusion.20
  123.0 0.0 copy-start.6
  123.0 0.0 copy-start.11
  123.0 2.3 broadcast_select_fusion.1
  125.3 5.8 all-to-all-start.2
  131.1 0.0 copy-done.6
  131.1 0.0 copy-done.11
  131.1 2.0 convolution_multiply_fusion.1
  133.1 0.0 copy-done.9
  133.1 3.9 broadcast_select_fusion
  137.1 40.7 %all-to-all-done.2 = f32[4,1,2048,64]{2,3,1,0:T(8,128)S(1)} async-done(((f32[4,1,2048,64]{2,3,1,0:T(8,128)}), f32[4,1,2048,64]{2,3,1,0:T(8,128)S(1)}, u32[]{:S(2)}, u32[]{:S(2)}) %all-to-all-start.2) | async-done | bytes 2097184 | tf_op jit(solution)/shard_map/all_to_all | solution.py:94
  177.7 7.2 all-to-all-start.3
  185.0 0.0 reduce-scatter.2.cloned.1.call-start
  185.0 626.2 %all-gather.5.cloned.1.call-done = bf16[8192,7168]{1,0:T(8,128)(2,1)} async-done(((bf16[2048,7168]{1,0:T(8,128)(2,1)}), bf16[8192,7168]{1,0:T(8,128)(2,1)}) %all-gather.5.cloned.1.call-update) | async-done | bytes 117440528 | tf_op jit(solution)/shard_map/all_gather | solution.py:49
  811.2 47.9 %fusion.41 = f32[128,8192]{1,0:T(8,128)} fusion(bf16[128,7168]{1,0:T(8,128)(2,1)} %param.12, bf16[8192,7168]{1,0:T(8,128)(2,1)} %all-gather.5.cloned.1.call-done), kind=kOutput, calls=%fused_computation.63 | convolution fusion | flops 15032385536 | bytes 123469824 | tf_op jit(solution)/shard_map/dot_general | solution.py:51
  859.1 0.0 reduce-scatter.2.cloned.1.call-update
  859.1 0.6 copy-done.13
  859.8 0.0 copy-done.8
  859.8 3.6 fusion.6
  863.5 4.4 copy.22
  867.9 0.0 all-to-all-done.3
  867.9 18.0 %fusion.2 = f32[8,64,7168]{2,0,1:T(8,128)} fusion(f32[4,1,64,7168]{3,2,1,0:T(8,128)} %all-to-all-done.3, s32[4]{0:T(128)S(1)} %and_select_fusion, pred[4]{0:T(512)(128)(4,1)S(1)} %copy-done.8), kind=kOutput, calls=%fused_computation.6 | convolution fusion | flops 176160832 | bytes 22020116 | tf_op jit(solution)/shard_map/lg,grf->lrf/dot_general | solution.py:104
  885.9 19.2 %copy.23 = f32[8,64,7168]{2,1,0:T(8,128)} copy(f32[8,64,7168]{2,0,1:T(8,128)} %fusion.2) | data formatting | bytes 29360128
  905.2 41.3 %fusion.40 = f32[128,7168]{1,0:T(8,128)} fusion(bf16[128,8192]{1,0:T(8,128)(2,1)} %all-gather.3.cloned.1.call-done, bf16[8192,7168]{1,0:T(8,128)(2,1)} %all-gather.5.cloned.1.call-done), kind=kOutput, calls=%fused_computation.62 | convolution fusion | flops 15032385536 | bytes 123207680 | tf_op jit(solution)/shard_map/dot_general | solution.py:50
  946.4 4.0 fusion.1
  950.4 0.0 copy-done.5
  950.4 2.4 fusion.5
  952.8 0.0 copy-done.1
  (17 shorter events, 0.1 us)
Async XLA Ops:
  7.2 1.6 copy-start
  7.2 0.8 copy-start.14
  7.2 0.8 copy-start.15
  7.2 804.0 %all-gather.5.cloned.1.call-start = ((), (), s32[]{:S(2)}) async-start(), calls=%async_computation.6 | async-start | bytes 146800640 | tf_op jit(solution)/shard_map/all_gather | solution.py:49
  8.2 2.4 copy-start.12
  9.4 11.0 %copy-start.7 = (pred[4]{0:T(512)(128)(4,1)}, pred[4]{0:T(512)(128)(4,1)S(1)}, u32[]{:S(2)}) copy-start(pred[4]{0:T(512)(128)(4,1)S(1)} %get-tuple-element.18) | copy-start | bytes 16
  10.6 16.5 %all-to-all-start = ((bf16[4,1,2048,64]{2,3,1,0:T(8,128)(2,1)}), bf16[4,1,2048,64]{2,3,1,0:T(8,128)(2,1)S(1)}, u32[]{:S(2)}, u32[]{:S(2)}) async-start(bf16[4,1,2048,64]{2,3,1,0:T(8,128)(2,1)} %bitcast_select_fusion.1), calls=%async_computation | async-start | bytes 2097152 | tf_op jit(solution)/shard_map/all_to_all | solution.py:64
  27.0 8.9 copy-start.16
  27.0 68.3 %all-to-all-start.1 = ((bf16[4,1,64,7168]{3,2,1,0:T(8,128)(2,1)}), bf16[4,1,64,7168]{3,2,1,0:T(8,128)(2,1)}, u32[]{:S(2)}, u32[]{:S(2)}) async-start(bf16[4,1,64,7168]{3,2,1,0:T(8,128)(2,1)} %bitcast_select_fusion), calls=%async_computation.1 | async-start | bytes 7340032 | tf_op jit(solution)/shard_map/all_to_all | solution.py:65
  33.4 64.7 %copy-start.2 = (bf16[128,7168]{1,0:T(8,128)(2,1)S(1)}, bf16[128,7168]{1,0:T(8,128)(2,1)}, u32[]{:S(2)}) copy-start(bf16[128,7168]{1,0:T(8,128)(2,1)} %param.12) | copy-start | bytes 5505028
  33.4 871.8 %all-gather.3.cloned.1.call-start = ((), (), s32[]{:S(2)}) async-start(), calls=%async_computation.5 | async-start | bytes 2621440 | tf_op jit(solution)/shard_map/all_gather | solution.py:48
  36.0 62.0 %copy-start.10 = (bf16[128]{0:T(256)(128)(2,1)}, bf16[128]{0:T(256)(128)(2,1)S(1)}, u32[]{:S(2)}) copy-start(bf16[128]{0:T(256)(128)(2,1)S(1)} %fusion.35) | copy-start | bytes 772
  36.2 63.3 %copy-start.4 = (bf16[2048,64]{0,1:T(8,128)(2,1)}, bf16[2048,64]{0,1:T(8,128)(2,1)S(1)}, u32[]{:S(2)}) copy-start(bf16[2048,64]{0,1:T(8,128)(2,1)S(1)} %bitcast_reduce_fusion) | copy-start | bytes 786436
  38.5 83.5 %copy-start.3 = (bf16[128,2048]{1,0:T(8,128)(2,1)S(1)}, bf16[128,2048]{1,0:T(8,128)(2,1)}, u32[]{:S(2)}) copy-start(bf16[128,2048]{1,0:T(8,128)(2,1)} %param.8) | copy-start | bytes 1572868
  123.0 8.2 copy-start.6
  123.0 8.1 copy-start.11
  125.3 7.8 copy-start.9
  125.3 52.4 %all-to-all-start.2 = ((f32[4,1,2048,64]{2,3,1,0:T(8,128)}), f32[4,1,2048,64]{2,3,1,0:T(8,128)S(1)}, u32[]{:S(2)}, u32[]{:S(2)}) async-start(f32[4,1,2048,64]{2,3,1,0:T(8,128)} %broadcast_select_fusion.1), calls=%async_computation.3 | async-start | bytes 4194304 | tf_op jit(solution)/shard_map/all_to_all | solution.py:94
  177.7 690.2 %all-to-all-start.3 = ((f32[4,1,64,7168]{3,2,1,0:T(8,128)}), f32[4,1,64,7168]{3,2,1,0:T(8,128)}, u32[]{:S(2)}, u32[]{:S(2)}) async-start(f32[4,1,64,7168]{3,2,1,0:T(8,128)} %broadcast_select_fusion), calls=%async_computation.4 | async-start | bytes 14680064 | tf_op jit(solution)/shard_map/all_to_all | solution.py:95
  185.0 765.4 %reduce-scatter.2.cloned.1.call-start = ((), (), s32[]{:S(2)}) async-start(), calls=%async_computation.7 | async-start | bytes 5242880 | tf_op jit(solution)/shard_map/reduce_scatter | solution.py:54
  859.1 0.7 copy-start.13
  859.1 0.7 copy-start.8
  905.1 47.6 %copy-start.1 = (bf16[8,2048,64]{1,2,0:T(8,128)(2,1)S(1)}, bf16[8,2048,64]{1,2,0:T(8,128)(2,1)}, u32[]{:S(2)}) copy-start(bf16[8,2048,64]{1,2,0:T(8,128)(2,1)} %param.10) | copy-start | bytes 6291460
  946.4 4.0 copy-start.5
Sparse Core Ops, SparseCore 0:
  9.6 801.5 all-gather.4
  812.8 48.0 all-gather.2
  863.2 75.4 reduce-scatter.1
where the time goes:
time: 963 us; the launch traced here: 959 us
  waiting for transfers between devices  725 us (75%)
  matrix products  124 us (13%)
  local copies, waits for them, and re-layouts  32.6 us (3%)
  starting transfers between devices  23 us (2%)
  blocking collectives  22.5 us (2%)
  other arithmetic  18.4 us (2%)
  between operations  13.9 us (1%)
    all_gather x1, waiting for transfers between devices, local(): full_weight = lax.all_gather(frozen_up_weight, 'dp', axis=0, tiled=True)  626 us
    all_to_all x1, waiting for transfers between devices, local(): lax.all_to_all(up_send, 'dp', split_axis=0, concat_axis=0, tiled=True)  56.8 us
    dot_general x1, matrix products, local(): lax.dot_general(cotangent, full_weight, (((1,), (1,)), ((), ())), preferr...  47.9 us
    dot_general x1, matrix products, local(): jnp.dot(gathered, full_weight, preferred_element_type=jnp.float32)  41.3 us
    all_to_all x1, waiting for transfers between devices, local(): lax.all_to_all(down_out, 'dp', split_axis=0, concat_axis=0, tiled=True)  40.7 us
    unnamed x36, local copies, waits for them, and re-layouts  25 us
    psum x1, blocking collectives, local(): rank_inner = lax.psum(rank_inner, 'tp')  22.5 us
  transfers between devices with their start and end apart: 7, of which 3 were waited for; matrix products, arithmetic and copies ran while one was open for 18% of the time, Pallas kernels for 0%

commit v1 on v0

v1 whole, which is shorter than its diff:
```python
import jax
import jax.numpy as jnp
from jax import lax
from jax.sharding import PartitionSpec as P

SEGMENT_BLOCK = 128

adapter_scale = 2.0
CHUNKS = 4


def dot(a, b, contract):
    return lax.dot_general(a, b, ((contract[:1], contract[1:]), ((), ())), preferred_element_type=jnp.float32)


def make_local(groups, shards):
    square = groups == shards
    bits = [1 << n for n in range((groups - 1).bit_length())]

    def swap(x, bit):
        return lax.ppermute(x, "dp", [(d, d ^ bit) for d in range(groups)])

    def gather(x):
        blocks = {0: x}
        for bit in reversed(bits):
            blocks.update({q | bit: swap(block, bit) for q, block in blocks.items()})
        return [blocks[q] for q in range(groups)]

    def transpose(x):
        pairs = [(c * groups + r, (r ^ c) * groups + c) for r in range(groups) for c in range(shards)]
        return lax.ppermute(x, ("tp", "dp"), pairs)

    def untranspose(x):
        pairs = [((r ^ c) * groups + c, c * groups + r) for r in range(groups) for c in range(shards)]
        return lax.ppermute(x, ("tp", "dp"), pairs)

    def local(tokens, weight, adapter_down, adapter_up, cotangent, block_adapter, block_length, adapter_slot):
        rows, width = tokens.shape
        depth, hidden = weight.shape
        per_owner, _, rank = adapter_down.shape
        i, j = lax.axis_index("dp"), lax.axis_index("tp")
        order = jnp.arange(groups, dtype=jnp.int32) ^ i
        match = block_adapter[:, None] == jnp.arange(adapter_slot.shape[0], dtype=jnp.int32)[None, :]
        slots = jnp.sum(jnp.where(match, adapter_slot[None, :], 0), axis=1)[order]
        lengths = block_length[order]
        owned = slots // per_owner == i
        local_ids = slots % per_owner
        live = (lax.broadcasted_iota(jnp.int32, (groups, rows), 1) < lengths[:, None]).astype(jnp.float32)
        down_t = jnp.swapaxes(adapter_down, 1, 2)
        zero = jnp.zeros((), jnp.bfloat16)

        def chosen(store):
            return [
                jnp.where(owned[q], lax.dynamic_index_in_dim(store, local_ids[q], 0, False), zero)
                for q in range(groups)
            ]

        down_sel, up_sel = chosen(down_t), chosen(adapter_up)
        if square:
            all_tokens = lax.all_gather(transpose(tokens), "tp", axis=0, tiled=True)
        else:
            whole = lax.all_gather(lax.all_gather(tokens, "dp", axis=0), "tp", axis=2, tiled=True)
            whole = lax.dynamic_slice_in_dim(whole, i * depth, depth, 2)
            all_tokens = whole[order].reshape(groups * rows, depth)
        token_blocks = gather(tokens)
        cot_blocks = gather(cotangent)
        cot_all = jnp.concatenate(cot_blocks, axis=0)
        tok_all = jnp.concatenate(token_blocks, axis=0)

        parts = list(down_sel)
        held = groups
        for bit in bits:
            parts = [parts[2 * n] + swap(parts[2 * n + 1], bit) for n in range(held // 2)]
            held //= 2
        down_mine = parts[0]

        inner = jnp.stack([dot(token_blocks[q], down_sel[q], (1, 1)) for q in range(groups)])
        inner = lax.psum(inner, "tp") * live[:, :, None]
        inner_b = inner.astype(jnp.bfloat16)
        back = jnp.stack([dot(cot_blocks[q], up_sel[q], (1, 1)) for q in range(groups)])
        back = lax.psum(back[order], ("tp", "dp"))[order] * (adapter_scale * live)[:, :, None]
        back_b = back.astype(jnp.bfloat16)

        one_hot = (local_ids[:, None] == jnp.arange(per_owner, dtype=jnp.int32)[None, :]) & owned[:, None]

        def spread(x):
            wide = jnp.where(one_hot[:, None, :, None], x[:, :, None, :], zero)
            return wide.reshape(groups * rows, per_owner * rank)

        inner_wide = spread(inner_b) * jnp.bfloat16(adapter_scale)
        back_wide = spread(back_b)
        up_flat = adapter_up.reshape(per_owner * rank, hidden)

        total = dot(cot_all, weight, (1, 1))
        if square:
            total = lax.psum_scatter(total, "tp", scatter_dimension=0, tiled=True)
            mine = lax.dynamic_index_in_dim(back_b, j, 0, False)
            total = total + dot(mine, transpose(down_mine), (1, 0))
            tokens_grad = untranspose(total.astype(jnp.bfloat16))
        else:
            placed = jnp.zeros((groups, rows, groups, depth), jnp.float32)
            placed = lax.dynamic_update_slice_in_dim(
                placed, total.reshape(groups, rows, 1, depth)[order], i, 2
            )
            placed = lax.psum_scatter(placed, "dp", scatter_dimension=0, tiled=False)
            placed = placed.reshape(rows, groups * depth)
            placed = lax.psum_scatter(placed, "tp", scatter_dimension=1, tiled=True)
            tokens_grad = (placed + dot(back_b[0], down_mine, (1, 0))).astype(jnp.bfloat16)

        pieces = CHUNKS if hidden % (CHUNKS * 128) == 0 else 1
        step = hidden // pieces
        outs = []
        for n in range(pieces):
            cols = slice(n * step, (n + 1) * step)
            part = dot(all_tokens, weight[:, cols], (1, 0)) + dot(inner_wide, up_flat[:, cols], (1, 0))
            parts = [part[q * rows : (q + 1) * rows] for q in range(groups)]
            held = groups
            for bit in bits:
                sent = [parts[2 * m + 1] for m in range(held // 2)]
                if bit == bits[-1]:
                    sent = [x.astype(jnp.bfloat16) for x in sent]
                parts = [parts[2 * m] + swap(sent[m], bit).astype(jnp.float32) for m in range(held // 2)]
                held //= 2
            outs.append(parts[0].astype(jnp.bfloat16))
        projected = jnp.concatenate(outs, axis=1)

        up_grad = dot(inner_wide, cot_all, (0, 0)).reshape(per_owner, rank, hidden)
        down_grad = dot(back_wide, tok_all, (0, 0)).reshape(per_owner, rank, width)
        return projected, tokens_grad, jnp.swapaxes(down_grad, 1, 2), up_grad

    return local


def solution(mesh):
    placed = (
        P(("grp", "dp"), "tp"),
        P("dp", "tp"),
        P("dp", "tp", None),
        P("dp", None, "tp"),
        P(("grp", "dp"), "tp"),
        P("grp"),
        P("grp"),
        P(),
    )
    return jax.shard_map(
        make_local(mesh.shape["dp"], mesh.shape["tp"]),
        mesh=mesh,
        in_specs=placed,
        out_specs=(
            P(("grp", "dp"), "tp"),
            P(("grp", "dp"), "tp"),
            P(("grp", "dp"), "tp", None),
            P(("grp", "dp"), None, "tp"),
        ),
        check_vma=False,
    )
```

time: 963 us -> 387 us (0.40)
  waiting for transfers between devices: 725 us -> 206 us
  blocking collectives: 22.5 us -> 0 us
  matrix products: 124 us -> 103 us
  local copies, waits for them, and re-layouts: 32.6 us -> 18.7 us
    all_gather x2 -> x1, waiting for transfers between devices: 626 us -> 34.7 us  [local(): all_tokens = lax.all_gather(transpose(tokens), 'tp', axis=0, tiled=True)]
    all_to_all x4 -> x0, waiting for transfers between devices: 97.4 us -> none  [the longest x1 56.8 us: local(): lax.all_to_all(up_send, 'dp', split_axis=0, concat_axis=0, tiled=True)]
    ppermute x0 -> x24, waiting for transfers between devices: none -> 96.3 us  [the longest x21 74.3 us: swap(): return lax.ppermute(x, 'dp', [(d, d ^ bit) for d in range(groups)])]
    psum x0 -> x2, waiting for transfers between devices: none -> 75.4 us  [the longest x1 59 us: local(): lax.psum(back[order], ('tp', 'dp'))[order]]
    all_to_all x4 -> x0, starting transfers between devices: 22.9 us -> none  [the longest x1 7.24 us: local(): lax.all_to_all(up_out, 'dp', split_axis=0, concat_axis=0, tiled=True)]
    psum x1 -> x0, blocking collectives: 22.5 us -> none  [local(): rank_inner = lax.psum(rank_inner, 'tp')]
    ppermute x0 -> x24, starting transfers between devices: none -> 21.9 us  [the longest x2 9.37 us: transpose(): return lax.ppermute(x, ('tp', 'dp'), pairs)]
    dot_general x10 -> x20, matrix products: 124 us -> 103 us  [dot(): lax.dot_general(a, b, ((contract[:1], contract[1:]), ((), ())), preferred...]
  transfers between devices with their start and end apart: 7 -> 28, of which waited for: 3 -> 9; matrix products, arithmetic and copies ran while one was open for 18% -> 34% of each run, Pallas kernels for 0% -> 0%
where the time goes in v1:
time: 387 us; the launch traced here: 386 us
  waiting for transfers between devices  206 us (53%)
  matrix products  103 us (27%)
  starting transfers between devices  22 us (6%)
  between operations  22 us (6%)
  local copies, waits for them, and re-layouts  18.7 us (5%)
  other arithmetic  14 us (4%)
    dot_general x20, matrix products, dot(): lax.dot_general(a, b, ((contract[:1], contract[1:]), ((), ())), preferred...  103 us
    ppermute x21, waiting for transfers between devices, swap(): return lax.ppermute(x, 'dp', [(d, d ^ bit) for d in range(groups)])  74.3 us
    psum x1, waiting for transfers between devices, local(): lax.psum(back[order], ('tp', 'dp'))[order]  59 us
    all_gather x1, waiting for transfers between devices, local(): all_tokens = lax.all_gather(transpose(tokens), 'tp', axis=0, tiled=True)  34.7 us
    ppermute x1, waiting for transfers between devices, untranspose(): return lax.ppermute(x, ('tp', 'dp'), pairs)  22 us
    psum x1, waiting for transfers between devices, local(): inner = lax.psum(inner, 'tp') * live[:, :, None]  16.4 us
    unnamed x22, local copies, waits for them, and re-layouts  10.4 us
    ppermute x2, starting transfers between devices, transpose(): return lax.ppermute(x, ('tp', 'dp'), pairs)  9.37 us
  transfers between devices with their start and end apart: 28, of which 9 were waited for; matrix products, arithmetic and copies ran while one was open for 34% of the time, Pallas kernels for 0%

profile of v1, /device:TPU:2, one launch (start us, length us, event | category | flops | bytes accessed | tf_op | source)
XLA Modules:
  0.0 385.9 jit_solution(2528707852992566958)
XLA Ops:
  7.4 2.0 collective-permute-start.17
  9.4 0.9 select_reduce_fusion
  10.3 0.6 gather_fusion
  11.0 0.6 fusion.96
  15.4 0.7 fusion.95
  16.1 2.4 select_bitcast_fusion.1
  18.5 0.6 collective-permute-start.20
  20.4 0.6 gather_fusion.1
  21.8 2.9 constant_dynamic-update-slice_fusion.3
  24.7 36.6 %collective-permute-done.17 = bf16[128,7168]{1,0:T(8,128)(2,1)} collective-permute-done((bf16[128,7168]{1,0:T(8,128)(2,1)}, bf16[128,7168]{1,0:T(8,128)(2,1)}, u32[]{:S(2)}, u32[]{:S(2)}) %collective-permute-start.17) | collective-permute-done | bytes 1835040 | tf_op jit(solution)/shard_map/ppermute | solution.py:21
  61.3 1.9 convolution_bitcast_fusion.8
  65.2 2.5 convolution_bitcast_fusion.4
  67.7 4.5 %collective-permute-start = (bf16[128,2048]{1,0:T(8,128)(2,1)S(1)}, bf16[128,2048]{1,0:T(8,128)(2,1)S(1)}, u32[]{:S(2)}, u32[]{:S(2)}) collective-permute-start(bf16[128,2048]{1,0:T(8,128)(2,1)S(1)} %copy-done.5), channel_id=1, source_target_pairs={{0,0},{4,5},{8,10},{12,15},{1,4},{5,1},{9,14},{13,11},{2,8},{6,13}... | collective-permute-start | bytes 1572872 | tf_op jit(solution)/shard_map/ppermute | solution.py:31
  72.2 1.2 collective-permute-start.3
  73.4 2.3 bitcast_add_fusion
  75.7 1.8 convolution_bitcast_fusion.6
  77.6 1.3 convolution_bitcast_fusion.7
  79.0 0.3 convolution_bitcast_fusion.5
  79.4 0.7 pad_maximum_fusion.1
  80.1 3.1 convolution_bitcast_fusion.2
  83.2 3.2 convolution_bitcast_fusion.3
  86.4 3.2 convolution_bitcast_fusion.1
  89.6 1.2 gather_fusion.2
  90.9 2.3 fusion.70
  93.2 4.9 %collective-permute-start.22 = (bf16[64,2048]{1,0:T(8,128)(2,1)}, bf16[64,2048]{1,0:T(8,128)(2,1)}, u32[]{:S(2)}, u32[]{:S(2)}) collective-permute-start(bf16[64,2048]{1,0:T(8,128)(2,1)} %fusion.70), channel_id=1, source_target_pairs={{0,0},{4,5},{8,10},{12,15},{1,4},{5,1},{9,14},{13,11},{2,8},{6,13}... | collective-permute-start | bytes 786440 | tf_op jit(solution)/shard_map/ppermute | solution.py:31
  98.2 0.8 copy-done.6
  99.1 16.4 %all-reduce.3.cloned.1.call-done = f32[4,128,64]{1,2,0:T(8,128)} async-done(((f32[4,128,64]{1,2,0:T(8,128)}), f32[4,128,64]{1,2,0:T(8,128)}) %all-reduce.3.cloned.1.call-update) | async-done | bytes 131088 | tf_op jit(solution)/shard_map/psum | solution.py:78
  115.4 0.9 multiply_convert_fusion.1
  116.4 2.8 constant_dynamic-update-slice_fusion.2
  119.3 2.9 constant_dynamic-update-slice_fusion.1
  122.1 2.8 constant_dynamic-update-slice_fusion
  125.0 22.2 %fusion.97 = f32[512,2048]{1,0:T(8,128)} fusion(bf16[512,7168]{1,0:T(8,128)(2,1)} %constant_dynamic-update-slice_fusion, bf16[2048,7168]{1,0:T(8,128)(2,1)} %param.9), kind=kOutput, calls=%fused_computation.142 | convolution fusion | flops 15032385536 | bytes 40894464 | tf_op jit(solution)/shard_map/dot_general | solution.py:13
  147.2 59.0 %all-reduce.5.cloned.1.call-done = f32[4,128,64]{1,2,0:T(8,128)} async-done(((f32[4,128,64]{1,2,0:T(8,128)}), f32[4,128,64]{1,2,0:T(8,128)}) %all-reduce.5.cloned.1.call-update) | async-done | bytes 131088 | tf_op jit(solution)/shard_map/psum | solution.py:81
  206.2 1.5 gather_fusion.3
  207.7 0.5 broadcast_select_fusion
  208.3 4.5 %fusion.34 = f32[512,1792]{1,0:T(8,128)} fusion(bf16[512,7168]{1,0:T(8,128)(2,1)} %bitcast.136, bf16[64,8,4,128]{3,2,1,0:T(4,128)(2,1)S(1)} %bitcast.132), kind=kOutput, calls=%fused_computation.32 | convolution fusion | flops 939524096 | bytes 6029312 | tf_op jit(solution)/shard_map/dot_general | solution.py:13
  212.8 4.5 %fusion.32 = f32[512,1792]{1,0:T(8,128)} fusion(bf16[512,7168]{1,0:T(8,128)(2,1)} %bitcast.137, bf16[64,8,4,128]{3,2,1,0:T(4,128)(2,1)S(1)} %bitcast.133), kind=kOutput, calls=%fused_computation.30 | convolution fusion | flops 939524096 | bytes 6029312 | tf_op jit(solution)/shard_map/dot_general | solution.py:13
  217.3 4.6 %fusion.30 = f32[512,1792]{1,0:T(8,128)} fusion(bf16[512,7168]{1,0:T(8,128)(2,1)} %bitcast.138, bf16[64,8,4,128]{3,2,1,0:T(4,128)(2,1)S(1)} %bitcast.134), kind=kOutput, calls=%fused_computation.28 | convolution fusion | flops 939524096 | bytes 6029312 | tf_op jit(solution)/shard_map/dot_general | solution.py:13
  221.9 34.7 %all-gather.2.cloned.1.call-done = bf16[512,2048]{1,0:T(8,128)(2,1)} async-done(((bf16[128,2048]{1,0:T(8,128)(2,1)}), bf16[512,2048]{1,0:T(8,128)(2,1)}) %all-gather.2.cloned.1.call-update) | async-done | bytes 2097168 | tf_op jit(solution)/shard_map/all_gather | solution.py:60
  256.6 8.8 %fusion.10 = f32[512,1792]{1,0:T(8,128)S(1)} fusion(f32[512,1792]{1,0:T(8,128)} %fusion.34, bf16[512,2048]{1,0:T(8,128)(2,1)} %all-gather.2.cloned.1.call-done, bf16[2048,7168]{1,0:T(8,128)(2,1)} %param.9), kind=kOutput, calls=%fused_computation.15 | convolution fusion | flops 3759013888 | bytes 16777216 | tf_op jit(solution)/shard_map/dot_general | solution.py:13
  265.6 7.2 %fusion.13 = f32[512,1792]{1,0:T(8,128)S(1)} fusion(f32[512,1792]{1,0:T(8,128)S(1)} %copy-done.3, bf16[512,2048]{1,0:T(8,128)(2,1)S(1)} %copy-done.7, bf16[2048,7168]{1,0:T(8,128)(2,1)} %param.9), kind=kOutput, calls=%fused_computation.16 | convolution fusion | flops 3759013888 | bytes 16777216 | tf_op jit(solution)/shard_map/dot_general | solution.py:13
  272.9 0.7 collective-permute-start.8
  273.6 7.4 %fusion.16 = f32[512,1792]{1,0:T(8,128)S(1)} fusion(f32[512,1792]{1,0:T(8,128)S(1)} %copy-done.2, bf16[512,2048]{1,0:T(8,128)(2,1)S(1)} %copy-done.7, bf16[2048,7168]{1,0:T(8,128)(2,1)} %param.9), kind=kOutput, calls=%fused_computation.17 | convolution fusion | flops 3759013888 | bytes 16777216 | tf_op jit(solution)/shard_map/dot_general | solution.py:13
  281.2 2.7 fusion.28
  283.9 7.1 %fusion.19 = f32[512,1792]{1,0:T(8,128)S(1)} fusion(f32[512,1792]{1,0:T(8,128)S(1)} %fusion.28, bf16[512,2048]{1,0:T(8,128)(2,1)S(1)} %copy-done.7, bf16[2048,7168]{1,0:T(8,128)(2,1)} %param.9), kind=kOutput, calls=%fused_computation.18 | convolution fusion | flops 3759013888 | bytes 16777216 | tf_op jit(solution)/shard_map/dot_general | solution.py:13
  291.0 0.5 collective-permute-start.14
  291.6 10.8 %fusion = f32[8,64,7168]{2,1,0:T(8,128)} fusion(bf16[8,64,512]{2,1,0:T(8,128)(2,1)S(1)} %bitcast.141, bf16[512,7168]{1,0:T(8,128)(2,1)} %constant_dynamic-update-slice_fusion), kind=kOutput, calls=%fused_computation.4 | convolution fusion | flops 3758096384 | bytes 22544384 | tf_op jit(solution)/shard_map/dot_general | solution.py:13
  302.4 1.3 fusion.73
  303.7 4.3 %convolution_bitcast_fusion = f32[8,2048,64]{1,2,0:T(8,128)} fusion(bf16[8,64,512]{2,1,0:T(8,128)(2,1)S(1)} %bitcast.142, bf16[128,2048]{1,0:T(8,128)(2,1)S(1)} %collective-permute-done.3, bf16[128,2048]{1,0:T(8,128)(2,1)S(1)} %collective-permute-done.2, bf16[128,2048]{1,0:T(8,128)(2,1)} %collective-permute-done.1, bf16[128,2048]{1,0:T(8,128)(2,1)S(1)} %copy-done.5), kind=kOutput, calls=%fused_computation.14 | convolution fusion | flops 1082130432 | bytes 6815744 | tf_op jit(solution)/shard_map/dot_general | solution.py:13
  308.1 0.1 fusion.45
  308.2 0.6 collective-permute-start.6
  309.0 1.5 collective-permute-start.9
  310.5 0.2 collective-permute-start.7
  310.9 0.6 collective-permute-start.12
  311.7 10.0 %collective-permute-done.6 = bf16[128,1792]{1,0:T(8,128)(2,1)S(1)} collective-permute-done((bf16[128,1792]{1,0:T(8,128)(2,1)S(1)}, bf16[128,1792]{1,0:T(8,128)(2,1)S(1)}, u32[]{:S(2)}, u32[]{:S(2)}) %collective-permute-start.6) | collective-permute-done | bytes 458784 | tf_op jit(solution)/shard_map/ppermute | solution.py:21
  321.6 0.6 collective-permute-start.15
  322.3 9.1 %collective-permute-done.9 = bf16[128,1792]{1,0:T(8,128)(2,1)S(1)} collective-permute-done((bf16[128,1792]{1,0:T(8,128)(2,1)S(1)}, bf16[128,1792]{1,0:T(8,128)(2,1)S(1)}, u32[]{:S(2)}, u32[]{:S(2)}) %collective-permute-start.9) | collective-permute-done | bytes 458784 | tf_op jit(solution)/shard_map/ppermute | solution.py:21
  331.6 9.7 %collective-permute-done.12 = bf16[128,1792]{1,0:T(8,128)(2,1)S(1)} collective-permute-done((bf16[128,1792]{1,0:T(8,128)(2,1)S(1)}, bf16[128,1792]{1,0:T(8,128)(2,1)S(1)}, u32[]{:S(2)}, u32[]{:S(2)}) %collective-permute-start.12) | collective-permute-done | bytes 458784 | tf_op jit(solution)/shard_map/ppermute | solution.py:21
  341.4 8.8 %collective-permute-done.15 = bf16[128,1792]{1,0:T(8,128)(2,1)S(1)} collective-permute-done((bf16[128,1792]{1,0:T(8,128)(2,1)S(1)}, bf16[128,1792]{1,0:T(8,128)(2,1)S(1)}, u32[]{:S(2)}, u32[]{:S(2)}) %collective-permute-start.15) | collective-permute-done | bytes 458784 | tf_op jit(solution)/shard_map/ppermute | solution.py:21
  350.4 1.4 add_convert_fusion
  351.8 3.4 collective-permute-start.23
  355.2 1.4 pad_maximum_fusion
  356.6 22.0 %collective-permute-done.23 = bf16[128,2048]{1,0:T(8,128)(2,1)S(1)} collective-permute-done((bf16[128,2048]{1,0:T(8,128)(2,1)S(1)}, bf16[128,2048]{1,0:T(8,128)(2,1)S(1)}, u32[]{:S(2)}, u32[]{:S(2)}) %collective-permute-start.23) | collective-permute-done | bytes 524320 | tf_op jit(solution)/shard_map/ppermute | solution.py:35
  378.6 0.8 copy.34
  (77 shorter events, 2.4 us)
Async XLA Ops:
  7.2 13.2 %copy-start = (s32[4]{0:T(128)S(1)}, s32[4]{0:T(128)}, u32[]{:S(2)}) copy-start(s32[4]{0:T(128)} %param.14) | copy-start | bytes 52
  7.2 54.1 %copy-start.5 = (bf16[128,2048]{1,0:T(8,128)(2,1)S(1)}, bf16[128,2048]{1,0:T(8,128)(2,1)}, u32[]{:S(2)}) copy-start(bf16[128,2048]{1,0:T(8,128)(2,1)} %param.8) | copy-start | bytes 1572868
  7.2 58.0 %copy-start.4 = (bf16[128,7168]{1,0:T(8,128)(2,1)S(1)}, bf16[128,7168]{1,0:T(8,128)(2,1)}, u32[]{:S(2)}) copy-start(bf16[128,7168]{1,0:T(8,128)(2,1)} %param.12) | copy-start | bytes 5505028
  7.2 108.2 %all-reduce.3.cloned.1.call-start = ((), (), s32[]{:S(2)}) async-start(), calls=%async_computation.2 | async-start | bytes 262144 | tf_op jit(solution)/shard_map/psum | solution.py:78
  7.2 70.3 %collective-permute-start.1 = (bf16[128,2048]{1,0:T(8,128)(2,1)}, bf16[128,2048]{1,0:T(8,128)(2,1)}, u32[]{:S(2)}, u32[]{:S(2)}) collective-permute-start(bf16[128,2048]{1,0:T(8,128)(2,1)} %param.8), channel_id=1, source_target_pairs={{0,1},{1,0},{2,3},{3,2},{4,5},{5,4},{6,7},{7,6},{8,9},{9,8},{10,11... | collective-permute-start | bytes 1572872 | tf_op jit(solution)/shard_map/ppermute | solution.py:21
  7.3 64.9 %collective-permute-start.2 = (bf16[128,2048]{1,0:T(8,128)(2,1)}, bf16[128,2048]{1,0:T(8,128)(2,1)S(1)}, u32[]{:S(2)}, u32[]{:S(2)}) collective-permute-start(bf16[128,2048]{1,0:T(8,128)(2,1)} %param.8), channel_id=1, source_target_pairs={{0,2},{1,3},{2,0},{3,1},{4,6},{5,7},{6,4},{7,5},{8,10},{9,11},{10,... | collective-permute-start | bytes 1572872 | tf_op jit(solution)/shard_map/ppermute | solution.py:21
  7.4 53.9 %collective-permute-start.17 = (bf16[128,7168]{1,0:T(8,128)(2,1)}, bf16[128,7168]{1,0:T(8,128)(2,1)}, u32[]{:S(2)}, u32[]{:S(2)}) collective-permute-start(bf16[128,7168]{1,0:T(8,128)(2,1)} %param.12), channel_id=1, source_target_pairs={{0,2},{1,3},{2,0},{3,1},{4,6},{5,7},{6,4},{7,5},{8,10},{9,11},{10,... | collective-permute-start | bytes 5505032 | tf_op jit(solution)/shard_map/ppermute | solution.py:21
  9.4 73.8 %collective-permute-start.16 = (bf16[128,7168]{1,0:T(8,128)(2,1)}, bf16[128,7168]{1,0:T(8,128)(2,1)}, u32[]{:S(2)}, u32[]{:S(2)}) collective-permute-start(bf16[128,7168]{1,0:T(8,128)(2,1)} %param.12), channel_id=1, source_target_pairs={{0,1},{1,0},{2,3},{3,2},{4,5},{5,4},{6,7},{7,6},{8,9},{9,8},{10,11... | collective-permute-start | bytes 5505032 | tf_op jit(solution)/shard_map/ppermute | solution.py:21
  18.5 49.2 %collective-permute-start.20 = (bf16[64,2048]{1,0:T(8,128)(2,1)S(1)}, bf16[64,2048]{1,0:T(8,128)(2,1)}, u32[]{:S(2)}, u32[]{:S(2)}) collective-permute-start(bf16[64,2048]{1,0:T(8,128)(2,1)S(1)} %get-tuple-element.13), channel_id=1, source_target_pairs={{0,1},{1,0},{2,3},{3,2},{4,5},{5,4},{6,7},{7,6},{8,9},{9,8},{10,11... | collective-permute-start | bytes 786440 | tf_op jit(solution)/shard_map/ppermute | solution.py:21
  61.3 25.1 %collective-permute-start.18 = (bf16[128,7168]{1,0:T(8,128)(2,1)}, bf16[128,7168]{1,0:T(8,128)(2,1)}, u32[]{:S(2)}, u32[]{:S(2)}) collective-permute-start(bf16[128,7168]{1,0:T(8,128)(2,1)} %collective-permute-done.17), channel_id=1, source_target_pairs={{0,1},{1,0},{2,3},{3,2},{4,5},{5,4},{6,7},{7,6},{8,9},{9,8},{10,11... | collective-permute-start | bytes 5505032 | tf_op jit(solution)/shard_map/ppermute | solution.py:21
  67.7 30.5 %collective-permute-start = (bf16[128,2048]{1,0:T(8,128)(2,1)S(1)}, bf16[128,2048]{1,0:T(8,128)(2,1)S(1)}, u32[]{:S(2)}, u32[]{:S(2)}) collective-permute-start(bf16[128,2048]{1,0:T(8,128)(2,1)S(1)} %copy-done.5), channel_id=1, source_target_pairs={{0,0},{4,5},{8,10},{12,15},{1,4},{5,1},{9,14},{13,11},{2,8},{6,13}... | collective-permute-start | bytes 1572872 | tf_op jit(solution)/shard_map/ppermute | solution.py:31
  72.2 6.8 %collective-permute-start.3 = (bf16[128,2048]{1,0:T(8,128)(2,1)S(1)}, bf16[128,2048]{1,0:T(8,128)(2,1)S(1)}, u32[]{:S(2)}, u32[]{:S(2)}) collective-permute-start(bf16[128,2048]{1,0:T(8,128)(2,1)S(1)} %collective-permute-done.2), channel_id=1, source_target_pairs={{0,1},{1,0},{2,3},{3,2},{4,5},{5,4},{6,7},{7,6},{8,9},{9,8},{10,11... | collective-permute-start | bytes 1572872 | tf_op jit(solution)/shard_map/ppermute | solution.py:21
  77.5 13.4 %collective-permute-start.19 = (bf16[64,2048]{1,0:T(8,128)(2,1)S(1)}, bf16[64,2048]{1,0:T(8,128)(2,1)S(1)}, u32[]{:S(2)}, u32[]{:S(2)}) collective-permute-start(bf16[64,2048]{1,0:T(8,128)(2,1)S(1)} %get-tuple-element.12), channel_id=1, source_target_pairs={{0,1},{1,0},{2,3},{3,2},{4,5},{5,4},{6,7},{7,6},{8,9},{9,8},{10,11... | collective-permute-start | bytes 786440 | tf_op jit(solution)/shard_map/ppermute | solution.py:21
  79.0 11.9 %collective-permute-start.21 = (bf16[64,2048]{1,0:T(8,128)(2,1)}, bf16[64,2048]{1,0:T(8,128)(2,1)S(1)}, u32[]{:S(2)}, u32[]{:S(2)}) collective-permute-start(bf16[64,2048]{1,0:T(8,128)(2,1)} %bitcast_add_fusion), channel_id=1, source_target_pairs={{0,2},{1,3},{2,0},{3,1},{4,6},{5,7},{6,4},{7,5},{8,10},{9,11},{10,... | collective-permute-start | bytes 786440 | tf_op jit(solution)/shard_map/ppermute | solution.py:21
  80.0 126.1 %all-reduce.5.cloned.1.call-start = ((), (), s32[]{:S(2)}) async-start(), calls=%async_computation.4 | async-start | bytes 262144 | tf_op jit(solution)/shard_map/psum | solution.py:81
  90.8 165.7 %all-gather.2.cloned.1.call-start = ((), (), s32[]{:S(2)}) async-start(), calls=%async_computation.1 | async-start | bytes 2621440 | tf_op jit(solution)/shard_map/all_gather | solution.py:60
  93.2 209.2 %collective-permute-start.22 = (bf16[64,2048]{1,0:T(8,128)(2,1)}, bf16[64,2048]{1,0:T(8,128)(2,1)}, u32[]{:S(2)}, u32[]{:S(2)}) collective-permute-start(bf16[64,2048]{1,0:T(8,128)(2,1)} %fusion.70), channel_id=1, source_target_pairs={{0,0},{4,5},{8,10},{12,15},{1,4},{5,1},{9,14},{13,11},{2,8},{6,13}... | collective-permute-start | bytes 786440 | tf_op jit(solution)/shard_map/ppermute | solution.py:31
  98.2 0.8 copy-start.6
  99.0 251.4 %reduce-scatter.2.cloned.1.call-start = ((), (), s32[]{:S(2)}) async-start(), calls=%async_computation.3 | async-start | bytes 5242880 | tf_op jit(solution)/shard_map/reduce_scatter | solution.py:96
  256.6 9.0 %copy-start.3 = (f32[512,1792]{1,0:T(8,128)S(1)}, f32[512,1792]{1,0:T(8,128)}, u32[]{:S(2)}) copy-start(f32[512,1792]{1,0:T(8,128)} %fusion.32) | copy-start | bytes 11010052
  256.6 9.0 %copy-start.7 = (bf16[512,2048]{1,0:T(8,128)(2,1)S(1)}, bf16[512,2048]{1,0:T(8,128)(2,1)}, u32[]{:S(2)}) copy-start(bf16[512,2048]{1,0:T(8,128)(2,1)} %all-gather.2.cloned.1.call-done) | copy-start | bytes 6291460
  265.5 8.2 %copy-start.2 = (f32[512,1792]{1,0:T(8,128)S(1)}, f32[512,1792]{1,0:T(8,128)}, u32[]{:S(2)}) copy-start(f32[512,1792]{1,0:T(8,128)} %fusion.30) | copy-start | bytes 11010052
  265.5 42.6 %collective-permute-start.5 = (f32[128,1792]{1,0:T(8,128)S(1)}, f32[128,1792]{1,0:T(8,128)S(1)}, u32[]{:S(2)}, u32[]{:S(2)}) collective-permute-start(f32[128,1792]{1,0:T(8,128)S(1)} %slice.148), channel_id=1, source_target_pairs={{0,1},{1,0},{2,3},{3,2},{4,5},{5,4},{6,7},{7,6},{8,9},{9,8},{10,11... | collective-permute-start | bytes 2752520 | tf_op jit(solution)/shard_map/ppermute | solution.py:21
  272.9 36.0 %collective-permute-start.8 = (f32[128,1792]{1,0:T(8,128)S(1)}, f32[128,1792]{1,0:T(8,128)S(1)}, u32[]{:S(2)}, u32[]{:S(2)}) collective-permute-start(f32[128,1792]{1,0:T(8,128)S(1)} %slice.153), channel_id=1, source_target_pairs={{0,1},{1,0},{2,3},{3,2},{4,5},{5,4},{6,7},{7,6},{8,9},{9,8},{10,11... | collective-permute-start | bytes 2752520 | tf_op jit(solution)/shard_map/ppermute | solution.py:21
  281.1 29.4 %collective-permute-start.11 = (f32[128,1792]{1,0:T(8,128)S(1)}, f32[128,1792]{1,0:T(8,128)S(1)}, u32[]{:S(2)}, u32[]{:S(2)}) collective-permute-start(f32[128,1792]{1,0:T(8,128)S(1)} %slice.158), channel_id=1, source_target_pairs={{0,1},{1,0},{2,3},{3,2},{4,5},{5,4},{6,7},{7,6},{8,9},{9,8},{10,11... | collective-permute-start | bytes 2752520 | tf_op jit(solution)/shard_map/ppermute | solution.py:21
  291.0 19.9 %collective-permute-start.14 = (f32[128,1792]{1,0:T(8,128)S(1)}, f32[128,1792]{1,0:T(8,128)S(1)}, u32[]{:S(2)}, u32[]{:S(2)}) collective-permute-start(f32[128,1792]{1,0:T(8,128)S(1)} %slice.163), channel_id=1, source_target_pairs={{0,1},{1,0},{2,3},{3,2},{4,5},{5,4},{6,7},{7,6},{8,9},{9,8},{10,11... | collective-permute-start | bytes 2752520 | tf_op jit(solution)/shard_map/ppermute | solution.py:21
  308.2 13.4 %collective-permute-start.6 = (bf16[128,1792]{1,0:T(8,128)(2,1)S(1)}, bf16[128,1792]{1,0:T(8,128)(2,1)S(1)}, u32[]{:S(2)}, u32[]{:S(2)}) collective-permute-start(bf16[128,1792]{1,0:T(8,128)(2,1)S(1)} %get-tuple-element.4), channel_id=1, source_target_pairs={{0,2},{1,3},{2,0},{3,1},{4,6},{5,7},{6,4},{7,5},{8,10},{9,11},{10,... | collective-permute-start | bytes 1376264 | tf_op jit(solution)/shard_map/ppermute | solution.py:21
  308.8 12.8 %collective-permute-start.4 = (f32[128,1792]{1,0:T(8,128)S(1)}, f32[128,1792]{1,0:T(8,128)S(1)}, u32[]{:S(2)}, u32[]{:S(2)}) collective-permute-start(f32[128,1792]{1,0:T(8,128)S(1)} %get-tuple-element.5), channel_id=1, source_target_pairs={{0,1},{1,0},{2,3},{3,2},{4,5},{5,4},{6,7},{7,6},{8,9},{9,8},{10,11... | collective-permute-start | bytes 2752520 | tf_op jit(solution)/shard_map/ppermute | solution.py:21
  309.0 22.5 %collective-permute-start.9 = (bf16[128,1792]{1,0:T(8,128)(2,1)S(1)}, bf16[128,1792]{1,0:T(8,128)(2,1)S(1)}, u32[]{:S(2)}, u32[]{:S(2)}) collective-permute-start(bf16[128,1792]{1,0:T(8,128)(2,1)S(1)} %get-tuple-element.6), channel_id=1, source_target_pairs={{0,2},{1,3},{2,0},{3,1},{4,6},{5,7},{6,4},{7,5},{8,10},{9,11},{10,... | collective-permute-start | bytes 1376264 | tf_op jit(solution)/shard_map/ppermute | solution.py:21
  310.5 21.0 %collective-permute-start.7 = (f32[128,1792]{1,0:T(8,128)S(1)}, f32[128,1792]{1,0:T(8,128)S(1)}, u32[]{:S(2)}, u32[]{:S(2)}) collective-permute-start(f32[128,1792]{1,0:T(8,128)S(1)} %get-tuple-element.7), channel_id=1, source_target_pairs={{0,1},{1,0},{2,3},{3,2},{4,5},{5,4},{6,7},{7,6},{8,9},{9,8},{10,11... | collective-permute-start | bytes 2752520 | tf_op jit(solution)/shard_map/ppermute | solution.py:21
  310.9 30.4 %collective-permute-start.12 = (bf16[128,1792]{1,0:T(8,128)(2,1)S(1)}, bf16[128,1792]{1,0:T(8,128)(2,1)S(1)}, u32[]{:S(2)}, u32[]{:S(2)}) collective-permute-start(bf16[128,1792]{1,0:T(8,128)(2,1)S(1)} %get-tuple-element.8), channel_id=1, source_target_pairs={{0,2},{1,3},{2,0},{3,1},{4,6},{5,7},{6,4},{7,5},{8,10},{9,11},{10,... | collective-permute-start | bytes 1376264 | tf_op jit(solution)/shard_map/ppermute | solution.py:21
  321.6 19.7 %collective-permute-start.10 = (f32[128,1792]{1,0:T(8,128)S(1)}, f32[128,1792]{1,0:T(8,128)S(1)}, u32[]{:S(2)}, u32[]{:S(2)}) collective-permute-start(f32[128,1792]{1,0:T(8,128)S(1)} %get-tuple-element.9), channel_id=1, source_target_pairs={{0,1},{1,0},{2,3},{3,2},{4,5},{5,4},{6,7},{7,6},{8,9},{9,8},{10,11... | collective-permute-start | bytes 2752520 | tf_op jit(solution)/shard_map/ppermute | solution.py:21
  321.6 28.6 %collective-permute-start.15 = (bf16[128,1792]{1,0:T(8,128)(2,1)S(1)}, bf16[128,1792]{1,0:T(8,128)(2,1)S(1)}, u32[]{:S(2)}, u32[]{:S(2)}) collective-permute-start(bf16[128,1792]{1,0:T(8,128)(2,1)S(1)} %get-tuple-element.10), channel_id=1, source_target_pairs={{0,2},{1,3},{2,0},{3,1},{4,6},{5,7},{6,4},{7,5},{8,10},{9,11},{10,... | collective-permute-start | bytes 1376264 | tf_op jit(solution)/shard_map/ppermute | solution.py:21
  331.5 18.8 %collective-permute-start.13 = (f32[128,1792]{1,0:T(8,128)S(1)}, f32[128,1792]{1,0:T(8,128)S(1)}, u32[]{:S(2)}, u32[]{:S(2)}) collective-permute-start(f32[128,1792]{1,0:T(8,128)S(1)} %get-tuple-element.11), channel_id=1, source_target_pairs={{0,1},{1,0},{2,3},{3,2},{4,5},{5,4},{6,7},{7,6},{8,9},{9,8},{10,11... | collective-permute-start | bytes 2752520 | tf_op jit(solution)/shard_map/ppermute | solution.py:21
  350.3 29.2 %copy-start.1 = (s32[4]{0:T(128)S(1)}, s32[4]{0:T(128)}, u32[]{:S(2)}) copy-start(s32[4]{0:T(128)} %param.14) | copy-start | bytes 52
  351.8 26.8 %collective-permute-start.23 = (bf16[128,2048]{1,0:T(8,128)(2,1)S(1)}, bf16[128,2048]{1,0:T(8,128)(2,1)S(1)}, u32[]{:S(2)}, u32[]{:S(2)}) collective-permute-start(bf16[128,2048]{1,0:T(8,128)(2,1)S(1)} %add_convert_fusion), channel_id=1, source_target_pairs={{0,0},{5,4},{10,8},{15,12},{4,1},{1,5},{14,9},{11,13},{8,2},{13,6}... | collective-permute-start | bytes 1572872 | tf_op jit(solution)/shard_map/ppermute | solution.py:35
Sparse Core Ops, SparseCore 0:
  80.2 35.2 all-reduce.2
  119.8 86.2 all-reduce.4
  208.4 48.1 all-gather.1
  258.8 75.4 reduce-scatter.1

commit v2 on v0

v2 whole, which is shorter than its diff:
```python
import functools

import jax
import jax.numpy as jnp
from jax import lax
from jax.experimental import pallas as pl
from jax.experimental.pallas import tpu as pltpu
from jax.sharding import PartitionSpec as P

SEGMENT_BLOCK = 128

adapter_scale = 2.0
CORE, CHIP = 1, 2
PLACE_BLOCK = (0, 2, 3, 1)
BLOCK_PLACE = (0, 3, 1, 2)
VMEM = 40 * 1024 * 1024


def dot(a, b, contract):
    return lax.dot_general(a, b, ((contract[:1], contract[1:]), ((), ())), preferred_element_type=jnp.float32)


def after(x, *others):
    return lax.optimization_barrier((x,) + others)[0]


def cost(flops, moved):
    return pl.CostEstimate(flops=flops, bytes_accessed=moved, transcendentals=0)


def project(first, second, wide, weight, up_flat, start, stop, block):
    rows, depth = first.shape
    span = wide.shape[1]
    count = (stop - start) // block
    base = start // block

    def kernel(a_ref, b_ref, wide_ref, w_ref, up_ref, keep_ref, send_ref, lhs):
        @pl.when(pl.program_id(0) == 0)
        def _():
            lhs[:rows] = a_ref[...]
            lhs[rows:] = b_ref[...]

        total = dot(lhs[...], w_ref[...], (1, 0)) + dot(wide_ref[...], up_ref[...], (1, 0))
        keep_ref[...] = total[:rows]
        send_ref[...] = total[rows:]

    whole = lambda n: (0, 0)
    return pl.pallas_call(
        kernel,
        grid=(count,),
        in_specs=[
            pl.BlockSpec((rows, depth), whole),
            pl.BlockSpec((rows, depth), whole),
            pl.BlockSpec((2 * rows, span), whole),
            pl.BlockSpec((depth, block), lambda n: (0, n + base)),
            pl.BlockSpec((span, block), lambda n: (0, n + base)),
        ],
        out_specs=[pl.BlockSpec((rows, block), lambda n: (0, n))] * 2,
        out_shape=[jax.ShapeDtypeStruct((rows, stop - start), jnp.float32)] * 2,
        scratch_shapes=[pltpu.VMEM((2 * rows, depth), first.dtype)],
        compiler_params=pltpu.CompilerParams(vmem_limit_bytes=VMEM),
        cost_estimate=cost(4 * rows * (depth + span) * (stop - start), 2 * (depth + span + 4 * rows) * (stop - start)),
        name="project",
    )(first, second, wide, weight, up_flat)


def return_grad(first, second, weight):
    rows, hidden = first.shape
    depth = weight.shape[0]
    block = 256

    def kernel(a_ref, b_ref, w_ref, out_ref, lhs):
        @pl.when(pl.program_id(0) == 0)
        def _():
            lhs[:rows] = a_ref[...]
            lhs[rows:] = b_ref[...]

        out_ref[...] = dot(lhs[...], w_ref[...], (1, 1))

    whole = lambda n: (0, 0)
    return pl.pallas_call(
        kernel,
        grid=(depth // block,),
        in_specs=[
            pl.BlockSpec((rows, hidden), whole),
            pl.BlockSpec((rows, hidden), whole),
            pl.BlockSpec((block, hidden), lambda n: (n, 0)),
        ],
        out_specs=pl.BlockSpec((2 * rows, block), lambda n: (0, n)),
        out_shape=jax.ShapeDtypeStruct((2 * rows, depth), jnp.float32),
        scratch_shapes=[pltpu.VMEM((2 * rows, hidden), first.dtype)],
        compiler_params=pltpu.CompilerParams(vmem_limit_bytes=VMEM),
        cost_estimate=cost(4 * rows * hidden * depth, 2 * hidden * (depth + 2 * rows)),
        name="return_grad",
    )(first, second, weight)


def rank_back(up_flat, blocks, one_hot, rank):
    span, hidden = up_flat.shape
    rows = blocks[0].shape[0]
    groups = len(blocks)
    block = 1024
    slots = span // rank

    def kernel(up_ref, *refs):
        cots, hot_ref, out_ref, total = refs[:groups], refs[groups], refs[groups + 1], refs[groups + 2]
        n = pl.program_id(0)

        @pl.when(n == 0)
        def _():
            total[...] = jnp.zeros_like(total)

        cot = jnp.concatenate([c[...] for c in cots], axis=0)
        total[...] += dot(up_ref[...], cot, (1, 1))

        @pl.when(n == pl.num_programs(0) - 1)
        def _():
            acc = jnp.zeros((rank, groups * rows), jnp.float32)
            for s in range(slots):
                part = slice(s * rank, (s + 1) * rank)
                acc += total[part] * hot_ref[s : s + 1, :]
            out_ref[...] = acc

    return pl.pallas_call(
        kernel,
        grid=(hidden // block,),
        in_specs=[pl.BlockSpec((span, block), lambda n: (0, n))]
        + [pl.BlockSpec((rows, block), lambda n: (0, n))] * groups
        + [pl.BlockSpec((slots, groups * rows), lambda n: (0, 0))],
        out_specs=pl.BlockSpec((rank, groups * rows), lambda n: (0, 0)),
        out_shape=jax.ShapeDtypeStruct((rank, groups * rows), jnp.float32),
        scratch_shapes=[pltpu.VMEM((span, groups * rows), jnp.float32)],
        compiler_params=pltpu.CompilerParams(vmem_limit_bytes=VMEM),
        cost_estimate=cost(2 * span * groups * rows * hidden, 2 * hidden * (span + groups * rows)),
        name="rank_back",
    )(up_flat, *blocks, one_hot)


def slot_grad(wide_t, blocks, block):
    span = wide_t.shape[0]
    rows, columns = blocks[0].shape
    groups = len(blocks)

    def kernel(wide_ref, *refs):
        values = jnp.concatenate([c[...] for c in refs[:groups]], axis=0)
        refs[groups][...] = dot(wide_ref[...], values, (1, 0))

    return pl.pallas_call(
        kernel,
        grid=(columns // block,),
        in_specs=[pl.BlockSpec((span, groups * rows), lambda n: (0, 0))]
        + [pl.BlockSpec((rows, block), lambda n: (0, n))] * groups,
        out_specs=pl.BlockSpec((span, block), lambda n: (0, n)),
        out_shape=jax.ShapeDtypeStruct((span, columns), jnp.float32),
        compiler_params=pltpu.CompilerParams(vmem_limit_bytes=VMEM),
        cost_estimate=cost(2 * span * groups * rows * columns, (4 * span + 2 * groups * rows) * columns),
        name="slot_grad",
    )(wide_t, *blocks)


def block_facts(block_adapter, block_length, adapter_slot, order, rows, per_owner, i):
    match = block_adapter[:, None] == jnp.arange(adapter_slot.shape[0], dtype=jnp.int32)[None, :]
    slots = jnp.sum(jnp.where(match, adapter_slot[None, :], 0), axis=1)[order]
    lengths = block_length[order]
    owned = slots // per_owner == i
    local_ids = slots % per_owner
    groups = order.shape[0]
    live = (lax.broadcasted_iota(jnp.int32, (groups, rows), 1) < lengths[:, None]).astype(jnp.float32)
    return owned, local_ids, live


def chosen(store, owned, local_ids):
    zero = jnp.zeros((), store.dtype)
    return [
        jnp.where(owned[q], lax.dynamic_index_in_dim(store, local_ids[q], 0, False), zero)
        for q in range(owned.shape[0])
    ]


def local_square(
    tokens, weight, adapter_down, adapter_up, cotangent, block_adapter, block_length, adapter_slot
):
    groups = shards = 4
    rows, width = tokens.shape
    depth, hidden = weight.shape
    per_owner, _, rank = adapter_down.shape
    span = per_owner * rank
    i, j = lax.axis_index("dp"), lax.axis_index("tp")
    order = jnp.arange(groups, dtype=jnp.int32) ^ i

    def swap(x, bit):
        return lax.ppermute(x, "dp", [(d, d ^ bit) for d in range(groups)])

    def along(x, pairs):
        return lax.ppermute(x, "tp", pairs)

    def turn(x, sources):
        pairs = [(c * groups + r, z * groups + d) for (r, c), (d, z) in sources]
        return lax.ppermute(x, ("tp", "dp"), pairs)

    everyone = [(r, c) for r in range(groups) for c in range(shards)]
    near = [(r, c) for r, c in everyone if r // CHIP == c // CHIP]

    tok_x = swap(tokens, CHIP)
    cot_c = swap(cotangent, CORE)
    cot_x = swap(after(cotangent, tok_x), CHIP)
    tok_c, tok_xc = swap(tokens, CORE), swap(tok_x, CORE)
    cot_xc = swap(cot_x, CORE)
    toks, cots = [tokens, tok_c, tok_x, tok_xc], [cotangent, cot_c, cot_x, cot_xc]

    owned, local_ids, live = block_facts(
        block_adapter, block_length, adapter_slot, order, rows, per_owner, i
    )
    one_hot = (jnp.arange(per_owner, dtype=jnp.int32)[:, None] == local_ids[None, :]) & owned[None, :]
    hot = jnp.repeat(one_hot.astype(jnp.float32), rows, axis=1)
    live_row = live.reshape(1, groups * rows)

    mid, low = (j == 1) | (j == 2), j < 2
    far = turn(tok_x, [((r, c), (c, BLOCK_PLACE[r ^ CHIP ^ c])) for r, c in near])
    own = turn(after(tokens, tok_x), [((r, c), (c, BLOCK_PLACE[r ^ c])) for r, c in near])
    grad01 = return_grad(after(cotangent, tok_x), cot_c, weight)
    far = after(far, grad01)

    def pair(a, b):
        return jnp.where(low, a, b), jnp.where(low, b, a)

    across = along(far, [(1, 2), (2, 1)])
    out = along(far, [(1, 0), (2, 3)])
    onward = along(across, [(1, 0), (2, 3)])
    rows2, rows3 = pair(jnp.where(mid, far, out), jnp.where(mid, across, onward))
    own = after(own, across)
    hop = along(own, [(0, 1), (3, 2)])
    skip = along(own, [(0, 2), (3, 1)])
    last = along(skip, [(2, 3), (1, 0)])
    rows0, rows1 = pair(jnp.where(mid, hop, own), jnp.where(mid, skip, last))

    down_sel = chosen(jnp.swapaxes(adapter_down, 1, 2), owned, local_ids)
    down_near = swap(jnp.stack([down_sel[1], down_sel[3]]), CORE)
    down_far = swap(down_sel[2] + down_near[1], CHIP)
    down_mine = turn(
        down_sel[0] + down_near[0] + down_far, [((r, c), (c, BLOCK_PLACE[r ^ c])) for r, c in everyone]
    )

    def total_tp(x):
        for bit in (1, 2):
            x = x + along(x, [(z, z ^ bit) for z in range(shards)])
        return x

    def spread(x):
        hot_b = hot.astype(jnp.bfloat16)
        return (hot_b[:, None, :] * x[None, :, :]).reshape(span, groups * rows)

    inner = jnp.concatenate([dot(down_sel[q], toks[q], (1, 1)) for q in range(groups)], axis=1)
    inner_b = (total_tp(inner) * live_row).astype(jnp.bfloat16)
    inner_wide = spread(inner_b * jnp.bfloat16(adapter_scale))
    inner_rows = inner_wide.T
    up_flat = adapter_up.reshape(span, hidden)

    block = 512
    steps = hidden // block
    pieces = 4 if steps >= 4 else 1
    edges = [(-(-steps * n // pieces)) * block for n in range(pieces + 1)]
    crossing, waiting = [], []

    def cross(point):
        keep, send = waiting.pop(0)
        summed = (after(keep, point) + swap(send, CORE)).astype(jnp.bfloat16)
        crossing.append(swap(summed, CHIP))
        return summed

    point = rows2
    for a, b in zip(edges, edges[1:]):
        waiting.append(project(after(rows2, point), rows3, inner_rows[2 * rows :], weight, up_flat, a, b, block))
        point = waiting[-1][0]
        if len(waiting) > 1:
            point = cross(point)
    grad01 = after(grad01, point)
    point = cross(point)
    grad23 = return_grad(after(cot_x, point), cot_xc, weight)

    def grad_block(both, at):
        return lax.dynamic_slice_in_dim(both, at * rows, rows, 0)

    b16 = jnp.bfloat16
    second = (j >= 2).astype(jnp.int32)
    early = [
        along(grad_block(grad01, second), [(1, 0), (2, 3)]),
        along(grad_block(grad01, 1 - second).astype(b16), [(2, 0), (1, 3)]),
        along(grad_block(grad01, 1 - second).astype(b16), [(3, 0), (0, 3)]),
    ]
    late = [
        along(grad_block(grad23, second), [(0, 1), (3, 2)]),
        along(grad_block(grad23, 1 - second).astype(b16), [(2, 1), (1, 2)]),
        along(grad_block(grad23, 1 - second).astype(b16), [(3, 1), (0, 2)]),
    ]

    back = rank_back(after(up_flat, grad23), cots, hot, rank)
    back_b = (total_tp(back) * (adapter_scale * live_row)).astype(b16)
    shared = [back_b[:, q * rows : (q + 1) * rows] for q in range(groups)]
    for bit in (CORE, CHIP):
        got = swap(jnp.stack(shared), bit)
        shared = [shared[q] + got[q ^ bit] for q in range(groups)]
    q_mine = jnp.asarray(PLACE_BLOCK, jnp.int32)[j]
    back_mine = lax.dynamic_index_in_dim(jnp.stack(shared), q_mine, 0, False)

    total = jnp.where(mid, grad_block(grad23, second), grad_block(grad01, second))
    for part in early + late:
        total = total + part.astype(jnp.float32)
    total = total + dot(back_mine, down_mine, (0, 0))
    tokens_grad = turn(
        total.astype(b16), [((c, BLOCK_PLACE[r ^ c]), (r, c)) for r, c in everyone]
    )

    keep, send = project(after(rows0, back), rows1, inner_rows[: 2 * rows], weight, up_flat, 0, hidden, block)
    mine = keep + swap(send, CORE)
    projected = jnp.concatenate(
        [
            (mine[:, a:b] + part.astype(jnp.float32)).astype(b16)
            for a, b, part in zip(edges, edges[1:], crossing)
        ],
        axis=1,
    )

    up_grad = slot_grad(after(inner_wide, keep), cots, 1024).reshape(per_owner, rank, hidden)
    down_grad = slot_grad(spread(back_b), toks, 1024).reshape(per_owner, rank, width)
    return projected, tokens_grad, jnp.swapaxes(down_grad, 1, 2), up_grad


def local_any(
    groups, tokens, weight, adapter_down, adapter_up, cotangent, block_adapter, block_length, adapter_slot
):
    bits = [1 << n for n in range((groups - 1).bit_length())]

    def swap(x, bit):
        return lax.ppermute(x, "dp", [(d, d ^ bit) for d in range(groups)])

    def gather(x):
        blocks = {0: x}
        for bit in reversed(bits):
            blocks.update({q | bit: swap(block, bit) for q, block in blocks.items()})
        return jnp.stack([blocks[q] for q in range(groups)])

    def combine(parts):
        for bit in bits:
            parts = [a + swap(b, bit) for a, b in zip(parts[::2], parts[1::2])]
        return parts[0]

    rows, width = tokens.shape
    depth, hidden = weight.shape
    per_owner, _, rank = adapter_down.shape
    i = lax.axis_index("dp")
    order = jnp.arange(groups, dtype=jnp.int32) ^ i
    owned, local_ids, live = block_facts(
        block_adapter, block_length, adapter_slot, order, rows, per_owner, i
    )
    down_sel = chosen(adapter_down, owned, local_ids)
    up_sel = chosen(adapter_up, owned, local_ids)
    all_tokens = lax.all_gather(lax.all_gather(tokens, "dp", axis=0), "tp", axis=2, tiled=True)
    all_tokens = lax.dynamic_slice_in_dim(all_tokens, i * depth, depth, 2)[order]
    all_tokens = all_tokens.reshape(groups * rows, depth)
    toks, cots = gather(tokens), gather(cotangent)
    tok_all, cot_all = toks.reshape(-1, width), cots.reshape(-1, hidden)
    down_mine = combine(down_sel)
    inner = jnp.stack([dot(toks[q], down_sel[q], (1, 0)) for q in range(groups)])
    inner_b = (lax.psum(inner, "tp") * live[:, :, None]).astype(jnp.bfloat16)
    back = jnp.stack([dot(cots[q], up_sel[q], (1, 1)) for q in range(groups)])
    back = lax.psum(back[order], ("tp", "dp"))[order] * (adapter_scale * live)[:, :, None]
    back_b = back.astype(jnp.bfloat16)
    one_hot = (local_ids[:, None] == jnp.arange(per_owner, dtype=jnp.int32)[None, :]) & owned[:, None]

    def spread(x):
        wide = jnp.where(one_hot[:, None, :, None], x[:, :, None, :], jnp.zeros((), x.dtype))
        return wide.reshape(groups * rows, per_owner * rank)

    inner_wide = spread(inner_b) * jnp.bfloat16(adapter_scale)
    total = dot(cot_all, weight, (1, 1)).reshape(groups, rows, 1, depth)[order]
    placed = jnp.zeros((groups, rows, groups, depth), jnp.float32)
    placed = lax.dynamic_update_slice_in_dim(placed, total, i, 2)
    placed = lax.psum_scatter(placed, "dp", scatter_dimension=0, tiled=False)
    placed = placed.reshape(rows, groups * depth)
    placed = lax.psum_scatter(placed, "tp", scatter_dimension=1, tiled=True)
    tokens_grad = (placed + dot(back_b[0], down_mine, (1, 1))).astype(jnp.bfloat16)
    part = dot(all_tokens, weight, (1, 0)) + dot(inner_wide, adapter_up.reshape(-1, hidden), (1, 0))
    projected = combine(list(part.reshape(groups, rows, hidden))).astype(jnp.bfloat16)
    up_grad = dot(inner_wide, cot_all, (0, 0)).reshape(per_owner, rank, hidden)
    down_grad = dot(spread(back_b), tok_all, (0, 0)).reshape(per_owner, rank, width)
    return projected, tokens_grad, jnp.swapaxes(down_grad, 1, 2), up_grad


def solution(mesh):
    placed = (
        P(("grp", "dp"), "tp"),
        P("dp", "tp"),
        P("dp", "tp", None),
        P("dp", None, "tp"),
        P(("grp", "dp"), "tp"),
        P("grp"),
        P("grp"),
        P(),
    )
    groups, shards = mesh.shape["dp"], mesh.shape["tp"]
    square = groups == shards == 4
    return jax.shard_map(
        local_square if square else functools.partial(local_any, groups),
        mesh=mesh,
        in_specs=placed,
        out_specs=(
            P(("grp", "dp"), "tp"),
            P(("grp", "dp"), "tp"),
            P(("grp", "dp"), "tp", None),
            P(("grp", "dp"), None, "tp"),
        ),
        check_vma=False,
    )
```

time: 963 us -> 331 us (0.34)
  waiting for transfers between devices: 725 us -> 95.8 us
  matrix products: 124 us -> 8.96 us
  Pallas kernels: 0 us -> 99.5 us
  starting transfers between devices: 23 us -> 60.1 us
  blocking collectives: 22.5 us -> 0 us
  local copies, waits for them, and re-layouts: 32.6 us -> 21.7 us
  other arithmetic: 18.4 us -> 28.3 us
    all_gather x2 -> x0, waiting for transfers between devices: 626 us -> none  [the longest x1 626 us: local(): full_weight = lax.all_gather(frozen_up_weight, 'dp', axis=0, tiled=True)]
    dot_general x10 -> x5, matrix products: 124 us -> 8.96 us  [dot(): lax.dot_general(a, b, ((contract[:1], contract[1:]), ((), ())), preferred...]
    pallas_call x0 -> x10, Pallas kernels: none -> 99.5 us  [the longest x5 44.9 us: project(): pl.pallas_call(kernel, grid=(count,), in_specs=[pl.BlockSpec((rows, depth...]
    all_to_all x4 -> x0, waiting for transfers between devices: 97.4 us -> none  [the longest x1 56.8 us: local(): lax.all_to_all(up_send, 'dp', split_axis=0, concat_axis=0, tiled=True)]
    ppermute x0 -> x39, waiting for transfers between devices: none -> 95.8 us  [the longest x16 68.5 us: along(): return lax.ppermute(x, 'tp', pairs)]
    ppermute x0 -> x39, starting transfers between devices: none -> 60.1 us  [the longest x16 41.4 us: along(): return lax.ppermute(x, 'tp', pairs)]
    all_to_all x4 -> x0, starting transfers between devices: 22.9 us -> none  [the longest x1 7.24 us: local(): lax.all_to_all(up_out, 'dp', split_axis=0, concat_axis=0, tiled=True)]
    psum x1 -> x0, blocking collectives: 22.5 us -> none  [local(): rank_inner = lax.psum(rank_inner, 'tp')]
  transfers between devices with their start and end apart: 7 -> 39, of which waited for: 3 -> 10; matrix products, arithmetic and copies ran while one was open for 18% -> 14% of each run, Pallas kernels for 0% -> 31%
where the time goes in v2:
time: 331 us; the launch traced here: 325 us
  Pallas kernels  99.5 us (30%)
  waiting for transfers between devices  95.8 us (29%)
  starting transfers between devices  60.1 us (18%)
  other arithmetic  28.3 us (9%)
  local copies, waits for them, and re-layouts  21.7 us (7%)
  between operations  10.8 us (3%)
  matrix products  8.96 us (3%)
    ppermute x16, waiting for transfers between devices, along(): return lax.ppermute(x, 'tp', pairs)  68.5 us
    pallas_call x5, Pallas kernels, project(): pl.pallas_call(kernel, grid=(count,), in_specs=[pl.BlockSpec((rows, depth...  44.9 us
    ppermute x16, starting transfers between devices, along(): return lax.ppermute(x, 'tp', pairs)  41.4 us
    pallas_call x2, Pallas kernels, return_grad(): pl.pallas_call(kernel, grid=(depth // block,), in_specs=[pl.BlockSpec((ro...  31.3 us
    ppermute x19, waiting for transfers between devices, swap(): return lax.ppermute(x, 'dp', [(d, d ^ bit) for d in range(groups)])  27.2 us
    pallas_call x2, Pallas kernels, slot_grad(): pl.pallas_call(kernel, grid=(columns // block,), in_specs=[pl.BlockSpec((...  13.8 us
    unnamed x63, local copies, waits for them, and re-layouts  13.3 us
    ppermute x4, starting transfers between devices, turn(): return lax.ppermute(x, ('tp', 'dp'), pairs)  10.1 us
  transfers between devices with their start and end apart: 39, of which 10 were waited for; matrix products, arithmetic and copies ran while one was open for 14% of the time, Pallas kernels for 31%

profile of v2, /device:TPU:2, one launch (start us, length us, event | category | flops | bytes accessed | tf_op | source)
XLA Modules:
  0.0 325.2 jit_solution(4520490304245618866)
XLA Ops:
  8.0 2.3 fusion.15
  13.3 2.0 fusion.13
  17.9 1.5 collective-permute-start.2
  19.3 1.8 fusion.9
  21.1 1.9 fusion.11
  23.0 1.9 fusion.7
  25.7 1.9 collective-permute-start.13
  27.6 15.3 %return_grad.2 = f32[256,2048]{1,0:T(8,128)S(1)} custom-call(bf16[128,7168]{1,0:T(8,128)(2,1)S(1)} %copy-done.5, bf16[128,7168]{1,0:T(8,128)(2,1)} %collective-permute-done.3.b_ref.refs_1_, bf16[2048,7168]{1,0:T(8,128)(2,1)} %w_ref.13), custom_call_target="tpu_custom_call" | custom-call | flops 7516192768 | bytes 33030144 | tf_op jit(solution)/shard_map/return_grad/pallas_call | solution.py:81
  42.9 1.3 copy-done.8
  46.6 5.4 %collective-permute-start.14 = (f32[64,512]{1,0:T(8,128)S(1)}, f32[64,512]{1,0:T(8,128)S(1)}, u32[]{:S(2)}, u32[]{:S(2)}) collective-permute-start(f32[64,512]{1,0:T(8,128)S(1)} %fusion.58), channel_id=1, source_target_pairs={{0,8},{4,12},{8,0},{12,4},{1,9},{5,13},{9,1},{13,5},{2,10},{6,14},... | collective-permute-start | bytes 393224 | tf_op jit(solution)/shard_map/ppermute | solution.py:195
  52.0 2.3 collective-permute-start.8
  54.3 1.3 collective-permute-start.1
  55.6 17.9 %collective-permute-done.14 = f32[64,512]{1,0:T(8,128)S(1)} collective-permute-done((f32[64,512]{1,0:T(8,128)S(1)}, f32[64,512]{1,0:T(8,128)S(1)}, u32[]{:S(2)}, u32[]{:S(2)}) %collective-permute-start.14) | collective-permute-done | bytes 131104 | tf_op jit(solution)/shard_map/ppermute | solution.py:195
  73.5 1.3 collective-permute-start.9
  74.8 1.3 collective-permute-start.10
  77.2 13.2 %collective-permute-done.9 = bf16[128,2048]{1,0:T(8,128)(2,1)S(1)} collective-permute-done((bf16[128,2048]{1,0:T(8,128)(2,1)}, bf16[128,2048]{1,0:T(8,128)(2,1)S(1)}, u32[]{:S(2)}, u32[]{:S(2)}) %collective-permute-start.9) | collective-permute-done | bytes 524320 | tf_op jit(solution)/shard_map/ppermute | solution.py:195
  91.2 10.4 %collective-permute-done.10 = bf16[128,2048]{1,0:T(8,128)(2,1)} collective-permute-done((bf16[128,2048]{1,0:T(8,128)(2,1)S(1)}, bf16[128,2048]{1,0:T(8,128)(2,1)}, u32[]{:S(2)}, u32[]{:S(2)}) %collective-permute-start.10) | collective-permute-done | bytes 524320 | tf_op jit(solution)/shard_map/ppermute | solution.py:195
  101.7 1.3 broadcast_select_fusion.5
  103.0 3.1 copy-done.2
  106.1 6.8 %project.5 = (f32[128,2048]{1,0:T(8,128)S(1)}, f32[128,2048]{1,0:T(8,128)}) custom-call(bf16[128,2048]{1,0:T(8,128)(2,1)S(1)} %get-tuple-element.45.a_ref, bf16[128,2048]{1,0:T(8,128)(2,1)S(1)} %get-tuple-element.66.b_ref, bf16[256,512]{1,0:T(8,128)(2,1)S(1)} %copy.23.wide_ref, bf16[2048,7168]{1,0:T(8,128)(2,1)} %w_ref.13, bf16[512,7168]{1,0:T(8,128)(2,1)S(1)} %bitcast.151), custom_call_target="tpu_custom_call" | custom-call | flops 2684354560 | bytes 12582912 | tf_op jit(solution)/shard_map/project/pallas_call | solution.py:48
  113.9 2.4 fusion.4
  116.4 4.8 %collective-permute-start.6 = (bf16[128,2048]{1,0:T(8,128)(2,1)}, bf16[128,2048]{1,0:T(8,128)(2,1)}, u32[]{:S(2)}, u32[]{:S(2)}) collective-permute-start(bf16[128,2048]{1,0:T(8,128)(2,1)} %collective-permute-done.1), channel_id=1, source_target_pairs={{0,8},{12,4},{1,9},{13,5},{2,10},{14,6},{3,11},{15,7},{16,24},{28,... | collective-permute-start | bytes 1572872 | tf_op jit(solution)/shard_map/ppermute | solution.py:195
  121.2 3.1 copy-done.3
  124.3 5.8 %project.6 = (f32[128,1536]{1,0:T(8,128)S(1)}, f32[128,1536]{1,0:T(8,128)}) custom-call(bf16[128,2048]{1,0:T(8,128)(2,1)S(1)} %get-tuple-element.45.a_ref, bf16[128,2048]{1,0:T(8,128)(2,1)S(1)} %get-tuple-element.66.b_ref, bf16[256,512]{1,0:T(8,128)(2,1)S(1)} %copy.23.wide_ref, bf16[2048,7168]{1,0:T(8,128)(2,1)} %w_ref.13, bf16[512,7168]{1,0:T(8,128)(2,1)S(1)} %bitcast.152), custom_call_target="tpu_custom_call" | custom-call | flops 2013265920 | bytes 9437184 | tf_op jit(solution)/shard_map/project/pallas_call | solution.py:48
  130.1 2.4 fusion.6
  132.5 1.9 collective-permute-start.37
  134.4 1.1 copy.27.wide_ref
  135.6 1.3 collective-permute-start.5
  137.5 1.3 collective-permute-start.7
  138.8 2.5 add_convert_fusion.2
  141.2 3.1 copy-done.4
  144.3 6.2 %project.7 = (f32[128,2048]{1,0:T(8,128)S(1)}, f32[128,2048]{1,0:T(8,128)S(1)}) custom-call(bf16[128,2048]{1,0:T(8,128)(2,1)S(1)} %get-tuple-element.45.a_ref, bf16[128,2048]{1,0:T(8,128)(2,1)S(1)} %get-tuple-element.66.b_ref, bf16[256,512]{1,0:T(8,128)(2,1)S(1)} %copy.23.wide_ref, bf16[2048,7168]{1,0:T(8,128)(2,1)} %w_ref.13, bf16[512,7168]{1,0:T(8,128)(2,1)S(1)} %bitcast.153), custom_call_target="tpu_custom_call" | custom-call | flops 2684354560 | bytes 12582912 | tf_op jit(solution)/shard_map/project/pallas_call | solution.py:48
  150.6 2.0 add_convert_fusion.4
  152.6 5.0 %project.8 = (f32[128,1536]{1,0:T(8,128)S(1)}, f32[128,1536]{1,0:T(8,128)S(1)}) custom-call(bf16[128,2048]{1,0:T(8,128)(2,1)S(1)} %get-tuple-element.45.a_ref, bf16[128,2048]{1,0:T(8,128)(2,1)S(1)} %get-tuple-element.66.b_ref, bf16[256,512]{1,0:T(8,128)(2,1)S(1)} %copy.23.wide_ref, bf16[2048,7168]{1,0:T(8,128)(2,1)} %w_ref.13, bf16[512,7168]{1,0:T(8,128)(2,1)S(1)} %bitcast.154), custom_call_target="tpu_custom_call" | custom-call | flops 2013265920 | bytes 9437184 | tf_op jit(solution)/shard_map/project/pallas_call | solution.py:48
  158.2 1.3 broadcast_select_fusion.4
  161.3 16.0 %return_grad.3 = f32[256,2048]{1,0:T(8,128)S(1)} custom-call(bf16[128,7168]{1,0:T(8,128)(2,1)} %collective-permute-done.8.a_ref.refs_2_, bf16[128,7168]{1,0:T(8,128)(2,1)S(1)} %collective-permute-done.19.b_ref.refs_3_, bf16[2048,7168]{1,0:T(8,128)(2,1)} %w_ref.13), custom_call_target="tpu_custom_call" | custom-call | flops 7516192768 | bytes 33030144 | tf_op jit(solution)/shard_map/return_grad/pallas_call | solution.py:81
  177.3 9.5 %rank_back.1 = f32[64,512]{1,0:T(8,128)S(1)} custom-call(bf16[512,7168]{1,0:T(8,128)(2,1)} %bitcast.149, bf16[128,7168]{1,0:T(8,128)(2,1)S(1)} %copy-done.5, bf16[128,7168]{1,0:T(8,128)(2,1)} %collective-permute-done.3.b_ref.refs_1_, bf16[128,7168]{1,0:T(8,128)(2,1)} %collective-permute-done.8.a_ref.refs_2_, ...), custom_call_target="tpu_custom_call" | custom-call | flops 3758096384 | bytes 14680064 | tf_op jit(solution)/shard_map/rank_back/pallas_call | solution.py:124
  186.8 2.8 collective-permute-start.31
  189.6 6.4 %collective-permute-start.27 = (bf16[128,2048]{1,0:T(8,128)(2,1)S(1)}, bf16[128,2048]{1,0:T(8,128)(2,1)}, u32[]{:S(2)}, u32[]{:S(2)}) collective-permute-start(bf16[128,2048]{1,0:T(8,128)(2,1)S(1)} %dynamic-slice_convert_fusion.1), channel_id=1, source_target_pairs={{12,0},{0,12},{13,1},{1,13},{14,2},{2,14},{15,3},{3,15},{28,16},{1... | collective-permute-start | bytes 1572872 | tf_op jit(solution)/shard_map/ppermute | solution.py:195
  196.0 1.3 collective-permute-start.26
  197.4 4.4 %collective-permute-start.32 = (f32[64,512]{1,0:T(8,128)S(1)}, f32[64,512]{1,0:T(8,128)S(1)}, u32[]{:S(2)}, u32[]{:S(2)}) collective-permute-start(f32[64,512]{1,0:T(8,128)S(1)} %add.173), channel_id=1, source_target_pairs={{0,8},{4,12},{8,0},{12,4},{1,9},{5,13},{9,1},{13,5},{2,10},{6,14},... | collective-permute-start | bytes 393224 | tf_op jit(solution)/shard_map/ppermute | solution.py:195
  201.8 21.1 %project.9 = (f32[128,7168]{1,0:T(8,128)S(1)}, f32[128,7168]{1,0:T(8,128)}) custom-call(bf16[128,2048]{1,0:T(8,128)(2,1)S(1)} %get-tuple-element.53.a_ref, bf16[128,2048]{1,0:T(8,128)(2,1)S(1)} %get-tuple-element.64.b_ref, bf16[256,512]{1,0:T(8,128)(2,1)S(1)} %copy.27.wide_ref, bf16[2048,7168]{1,0:T(8,128)(2,1)} %w_ref.13, bf16[512,7168]{1,0:T(8,128)(2,1)} %bitcast.150), custom_call_target="tpu_custom_call" | custom-call | flops 9395240960 | bytes 44040192 | tf_op jit(solution)/shard_map/project/pallas_call | solution.py:48
  222.9 2.8 collective-permute-done.32
  225.8 1.1 constant_dynamic-slice_fusion
  226.9 2.5 collective-permute-done.33
  229.6 1.1 constant_dynamic-slice_fusion.1
  230.6 1.3 collective-permute-start.25
  231.9 1.9 collective-permute-done.34
  233.8 3.7 %collective-permute-start.28 = (f32[128,2048]{1,0:T(8,128)}, f32[128,2048]{1,0:T(8,128)}, u32[]{:S(2)}, u32[]{:S(2)}) collective-permute-start(f32[128,2048]{1,0:T(8,128)} %constant_dynamic-slice_fusion.1), channel_id=1, source_target_pairs={{0,4},{12,8},{1,5},{13,9},{2,6},{14,10},{3,7},{15,11},{16,20},{28,... | collective-permute-start | bytes 3145736 | tf_op jit(solution)/shard_map/ppermute | solution.py:195
  238.4 2.1 collective-permute-start.30
  240.5 1.4 collective-permute-start.29
  245.0 1.3 fusion.26
  246.3 24.2 %collective-permute-done.30 = bf16[128,2048]{1,0:T(8,128)(2,1)} collective-permute-done((bf16[128,2048]{1,0:T(8,128)(2,1)}, bf16[128,2048]{1,0:T(8,128)(2,1)}, u32[]{:S(2)}, u32[]{:S(2)}) %collective-permute-start.30) | collective-permute-done | bytes 524320 | tf_op jit(solution)/shard_map/ppermute | solution.py:195
  270.5 1.7 collective-permute-start.21
  272.6 1.7 collective-permute-start.24
  274.3 3.3 %add_convert_fusion = bf16[128,2048]{1,0:T(8,128)(2,1)S(1)} fusion(f32[128,2048]{1,0:T(8,128)S(1)} %fusion.26, bf16[128,2048]{1,0:T(8,128)(2,1)} %collective-permute-done.30, bf16[128,2048]{1,0:T(8,128)(2,1)} %collective-permute-done.29, f32[128,2048]{1,0:T(8,128)} %collective-permute-done.28, bf16[128,2048]{1,0:T(8,128)(2,1)} %collective-permute-done.27, ...), kind=kLoop, calls=%fused_computation.7 | loop fusion | flops 3407872 | bytes 7864325 | tf_op jit(solution)/shard_map/convert_element_type | solution.py:311
  277.6 5.4 %collective-permute-start.38 = (bf16[128,2048]{1,0:T(8,128)(2,1)S(1)}, bf16[128,2048]{1,0:T(8,128)(2,1)S(1)}, u32[]{:S(2)}, u32[]{:S(2)}) collective-permute-start(bf16[128,2048]{1,0:T(8,128)(2,1)S(1)} %add_convert_fusion), channel_id=1, source_target_pairs={{0,0},{13,4},{6,8},{11,12},{12,1},{1,5},{10,9},{7,13},{4,2},{9,6},... | collective-permute-start | bytes 1572872 | tf_op jit(solution)/shard_map/ppermute | solution.py:199
  283.0 10.0 %slot_grad.3 = f32[512,7168]{1,0:T(8,128)} custom-call(bf16[512,512]{1,0:T(8,128)(2,1)S(1)} %bitcast.156, bf16[128,7168]{1,0:T(8,128)(2,1)S(1)} %copy-done.5, bf16[128,7168]{1,0:T(8,128)(2,1)} %collective-permute-done.3.b_ref.refs_1_, bf16[128,7168]{1,0:T(8,128)(2,1)} %collective-permute-done.8.a_ref.refs_2_, bf16[128,7168]{1,0:T(8,128)(2,1)S(1)} %copy-done.7), custom_call_target="tpu_custom_call" | custom-call | flops 3758096384 | bytes 22020096 | tf_op jit(solution)/shard_map/slot_grad/pallas_call | solution.py:148
  293.1 3.9 %slot_grad.2 = f32[512,2048]{1,0:T(8,128)} custom-call(bf16[512,512]{1,0:T(8,128)(2,1)S(1)} %bitcast.157, bf16[128,2048]{1,0:T(8,128)(2,1)} %refs_0_.4, bf16[128,2048]{1,0:T(8,128)(2,1)S(1)} %copy-done.18, bf16[128,2048]{1,0:T(8,128)(2,1)S(1)} %copy-done.16, bf16[128,2048]{1,0:T(8,128)(2,1)S(1)} %copy-done.20), custom_call_target="tpu_custom_call" | custom-call | flops 1073741824 | bytes 6291456 | tf_op jit(solution)/shard_map/slot_grad/pallas_call | solution.py:148
  297.0 2.7 add.161
  299.7 5.4 %collective-permute-done.22 = bf16[128,1536]{1,0:T(8,128)(2,1)S(1)} collective-permute-done((bf16[128,1536]{1,0:T(8,128)(2,1)}, bf16[128,1536]{1,0:T(8,128)(2,1)S(1)}, u32[]{:S(2)}, u32[]{:S(2)}) %collective-permute-start.22) | collective-permute-done | bytes 393248 | tf_op jit(solution)/shard_map/ppermute | solution.py:192
  305.1 8.4 %collective-permute-done.24 = bf16[128,1536]{1,0:T(8,128)(2,1)S(1)} collective-permute-done((bf16[128,1536]{1,0:T(8,128)(2,1)}, bf16[128,1536]{1,0:T(8,128)(2,1)S(1)}, u32[]{:S(2)}, u32[]{:S(2)}) %collective-permute-start.24) | collective-permute-done | bytes 393248 | tf_op jit(solution)/shard_map/ppermute | solution.py:192
  313.7 9.0 %collective-permute-done.23 = bf16[128,2048]{1,0:T(8,128)(2,1)S(1)} collective-permute-done((bf16[128,2048]{1,0:T(8,128)(2,1)S(1)}, bf16[128,2048]{1,0:T(8,128)(2,1)S(1)}, u32[]{:S(2)}, u32[]{:S(2)}) %collective-permute-start.23) | collective-permute-done | bytes 524320 | tf_op jit(solution)/shard_map/ppermute | solution.py:192
  323.0 1.4 pad_maximum_fusion
  (141 shorter events, 18.4 us)
Async XLA Ops:
  0.6 44.4 %copy-start = (s32[4]{0:T(128)S(1)}, s32[4]{0:T(128)}, u32[]{:S(2)}) copy-start(s32[4]{0:T(128)} %param.15) | copy-start | bytes 52
  0.6 14.7 %collective-permute-start = (bf16[128,2048]{1,0:T(8,128)(2,1)}, bf16[128,2048]{1,0:T(8,128)(2,1)S(1)}, u32[]{:S(2)}, u32[]{:S(2)}) collective-permute-start(bf16[128,2048]{1,0:T(8,128)(2,1)} %refs_0_.4), channel_id=1, source_target_pairs={{0,2},{1,3},{2,0},{3,1},{4,6},{5,7},{6,4},{7,5},{8,10},{9,11},{10,... | collective-permute-start | bytes 1572872 | tf_op jit(solution)/shard_map/ppermute | solution.py:192
  0.7 18.6 %collective-permute-start.11 = (bf16[128,2048]{1,0:T(8,128)(2,1)}, bf16[128,2048]{1,0:T(8,128)(2,1)S(1)}, u32[]{:S(2)}, u32[]{:S(2)}) collective-permute-start(bf16[128,2048]{1,0:T(8,128)(2,1)} %refs_0_.4), channel_id=1, source_target_pairs={{0,1},{1,0},{2,3},{3,2},{4,5},{5,4},{6,7},{7,6},{8,9},{9,8},{10,11... | collective-permute-start | bytes 1572872 | tf_op jit(solution)/shard_map/ppermute | solution.py:192
  0.8 26.8 %collective-permute-start.3 = (bf16[128,7168]{1,0:T(8,128)(2,1)}, bf16[128,7168]{1,0:T(8,128)(2,1)}, u32[]{:S(2)}, u32[]{:S(2)}) collective-permute-start(bf16[128,7168]{1,0:T(8,128)(2,1)} %refs_0_.5), channel_id=1, source_target_pairs={{0,1},{1,0},{2,3},{3,2},{4,5},{5,4},{6,7},{7,6},{8,9},{9,8},{10,11... | collective-permute-start | bytes 5505032 | tf_op jit(solution)/shard_map/ppermute | solution.py:192
  10.3 17.3 %copy-start.5 = (bf16[128,7168]{1,0:T(8,128)(2,1)S(1)}, bf16[128,7168]{1,0:T(8,128)(2,1)}, u32[]{:S(2)}) copy-start(bf16[128,7168]{1,0:T(8,128)(2,1)} %refs_0_.5) | copy-start | bytes 5505028
  11.2 102.7 %collective-permute-start.35 = (bf16[2,64,2048]{2,1,0:T(8,128)(2,1)}, bf16[2,64,2048]{2,1,0:T(8,128)(2,1)}, u32[]{:S(2)}, u32[]{:S(2)}) collective-permute-start(bf16[2,64,2048]{2,1,0:T(8,128)(2,1)} %pad_maximum_fusion.1), channel_id=1, source_target_pairs={{0,1},{1,0},{2,3},{3,2},{4,5},{5,4},{6,7},{7,6},{8,9},{9,8},{10,11... | collective-permute-start | bytes 1572872 | tf_op jit(solution)/shard_map/ppermute | solution.py:192
  15.3 27.6 %copy-start.15 = (bf16[128,2048]{1,0:T(8,128)(2,1)}, bf16[128,2048]{1,0:T(8,128)(2,1)S(1)}, u32[]{:S(2)}) copy-start(bf16[128,2048]{1,0:T(8,128)(2,1)S(1)} %collective-permute-done.refs_2_) | copy-start | bytes 1572868
  15.3 7.7 %collective-permute-start.12 = (bf16[128,2048]{1,0:T(8,128)(2,1)S(1)}, bf16[128,2048]{1,0:T(8,128)(2,1)S(1)}, u32[]{:S(2)}, u32[]{:S(2)}) collective-permute-start(bf16[128,2048]{1,0:T(8,128)(2,1)S(1)} %collective-permute-done.refs_2_), channel_id=1, source_target_pairs={{0,1},{1,0},{2,3},{3,2},{4,5},{5,4},{6,7},{7,6},{8,9},{9,8},{10,11... | collective-permute-start | bytes 1572872 | tf_op jit(solution)/shard_map/ppermute | solution.py:192
  17.9 26.4 %collective-permute-start.2 = (bf16[128,2048]{1,0:T(8,128)(2,1)S(1)}, bf16[128,2048]{1,0:T(8,128)(2,1)}, u32[]{:S(2)}, u32[]{:S(2)}) collective-permute-start(bf16[128,2048]{1,0:T(8,128)(2,1)S(1)} %collective-permute-done.refs_2_), channel_id=1, source_target_pairs={{0,4},{4,9},{1,8},{5,5},{10,6},{14,11},{11,10},{15,7},{16,20},{20,... | collective-permute-start | bytes 1572872 | tf_op jit(solution)/shard_map/ppermute | solution.py:199
  19.3 23.6 %copy-start.17 = (bf16[128,2048]{1,0:T(8,128)(2,1)}, bf16[128,2048]{1,0:T(8,128)(2,1)S(1)}, u32[]{:S(2)}) copy-start(bf16[128,2048]{1,0:T(8,128)(2,1)S(1)} %collective-permute-done.11.refs_1_) | copy-start | bytes 1572868
  23.0 19.9 %copy-start.19 = (bf16[128,2048]{1,0:T(8,128)(2,1)}, bf16[128,2048]{1,0:T(8,128)(2,1)S(1)}, u32[]{:S(2)}) copy-start(bf16[128,2048]{1,0:T(8,128)(2,1)S(1)} %collective-permute-done.12.refs_3_) | copy-start | bytes 1572868
  25.7 20.0 %collective-permute-start.13 = (f32[64,512]{1,0:T(8,128)}, f32[64,512]{1,0:T(8,128)}, u32[]{:S(2)}, u32[]{:S(2)}) collective-permute-start(f32[64,512]{1,0:T(8,128)} %pad_maximum_fusion.2), channel_id=1, source_target_pairs={{0,4},{4,0},{8,12},{12,8},{1,5},{5,1},{9,13},{13,9},{2,6},{6,2},{1... | collective-permute-start | bytes 393224 | tf_op jit(solution)/shard_map/ppermute | solution.py:195
  44.2 30.5 %collective-permute-start.4 = (bf16[128,2048]{1,0:T(8,128)(2,1)}, bf16[128,2048]{1,0:T(8,128)(2,1)S(1)}, u32[]{:S(2)}, u32[]{:S(2)}) collective-permute-start(bf16[128,2048]{1,0:T(8,128)(2,1)} %collective-permute-done.2), channel_id=1, source_target_pairs={{4,8},{8,4},{5,9},{9,5},{6,10},{10,6},{7,11},{11,7},{20,24},{24,20... | collective-permute-start | bytes 1572872 | tf_op jit(solution)/shard_map/ppermute | solution.py:195
  46.6 26.9 %collective-permute-start.14 = (f32[64,512]{1,0:T(8,128)S(1)}, f32[64,512]{1,0:T(8,128)S(1)}, u32[]{:S(2)}, u32[]{:S(2)}) collective-permute-start(f32[64,512]{1,0:T(8,128)S(1)} %fusion.58), channel_id=1, source_target_pairs={{0,8},{4,12},{8,0},{12,4},{1,9},{5,13},{9,1},{13,5},{2,10},{6,14},... | collective-permute-start | bytes 393224 | tf_op jit(solution)/shard_map/ppermute | solution.py:195
  52.0 83.5 %collective-permute-start.8 = (bf16[128,7168]{1,0:T(8,128)(2,1)S(1)}, bf16[128,7168]{1,0:T(8,128)(2,1)}, u32[]{:S(2)}, u32[]{:S(2)}) collective-permute-start(bf16[128,7168]{1,0:T(8,128)(2,1)S(1)} %copy-done.5), channel_id=1, source_target_pairs={{0,2},{1,3},{2,0},{3,1},{4,6},{5,7},{6,4},{7,5},{8,10},{9,11},{10,... | collective-permute-start | bytes 5505032 | tf_op jit(solution)/shard_map/ppermute | solution.py:192
  54.3 62.1 %collective-permute-start.1 = (bf16[128,2048]{1,0:T(8,128)(2,1)}, bf16[128,2048]{1,0:T(8,128)(2,1)}, u32[]{:S(2)}, u32[]{:S(2)}) collective-permute-start(bf16[128,2048]{1,0:T(8,128)(2,1)} %refs_0_.4), channel_id=1, source_target_pairs={{0,0},{4,13},{1,12},{5,1},{10,2},{14,15},{11,14},{15,3},{16,16},{2... | collective-permute-start | bytes 1572872 | tf_op jit(solution)/shard_map/ppermute | solution.py:199
  73.5 16.9 %collective-permute-start.9 = (bf16[128,2048]{1,0:T(8,128)(2,1)}, bf16[128,2048]{1,0:T(8,128)(2,1)S(1)}, u32[]{:S(2)}, u32[]{:S(2)}) collective-permute-start(bf16[128,2048]{1,0:T(8,128)(2,1)} %collective-permute-done.2), channel_id=1, source_target_pairs={{4,0},{8,12},{5,1},{9,13},{6,2},{10,14},{7,3},{11,15},{20,16},{24,... | collective-permute-start | bytes 1572872 | tf_op jit(solution)/shard_map/ppermute | solution.py:195
  74.8 15.6 %copy-start.26 = (bf16[128,2048]{1,0:T(8,128)(2,1)}, bf16[128,2048]{1,0:T(8,128)(2,1)S(1)}, u32[]{:S(2)}) copy-start(bf16[128,2048]{1,0:T(8,128)(2,1)S(1)} %collective-permute-done.4) | copy-start | bytes 1572868
  74.8 26.9 %collective-permute-start.10 = (bf16[128,2048]{1,0:T(8,128)(2,1)S(1)}, bf16[128,2048]{1,0:T(8,128)(2,1)}, u32[]{:S(2)}, u32[]{:S(2)}) collective-permute-start(bf16[128,2048]{1,0:T(8,128)(2,1)S(1)} %collective-permute-done.4), channel_id=1, source_target_pairs={{4,0},{8,12},{5,1},{9,13},{6,2},{10,14},{7,3},{11,15},{20,16},{24,... | collective-permute-start | bytes 1572872 | tf_op jit(solution)/shard_map/ppermute | solution.py:195
  103.0 3.1 copy-start.2
  113.9 23.6 %collective-permute-start.15 = (f32[128,2048]{1,0:T(8,128)}, f32[128,2048]{1,0:T(8,128)}, u32[]{:S(2)}, u32[]{:S(2)}) collective-permute-start(f32[128,2048]{1,0:T(8,128)} %get-tuple-element.40), channel_id=1, source_target_pairs={{0,1},{1,0},{2,3},{3,2},{4,5},{5,4},{6,7},{7,6},{8,9},{9,8},{10,11... | collective-permute-start | bytes 3145736 | tf_op jit(solution)/shard_map/ppermute | solution.py:192
  116.3 13.8 %collective-permute-start.36 = (bf16[64,2048]{1,0:T(8,128)(2,1)}, bf16[64,2048]{1,0:T(8,128)(2,1)S(1)}, u32[]{:S(2)}, u32[]{:S(2)}) collective-permute-start(bf16[64,2048]{1,0:T(8,128)(2,1)} %fusion.4), channel_id=1, source_target_pairs={{0,2},{1,3},{2,0},{3,1},{4,6},{5,7},{6,4},{7,5},{8,10},{9,11},{10,... | collective-permute-start | bytes 786440 | tf_op jit(solution)/shard_map/ppermute | solution.py:192
  116.4 20.5 %collective-permute-start.6 = (bf16[128,2048]{1,0:T(8,128)(2,1)}, bf16[128,2048]{1,0:T(8,128)(2,1)}, u32[]{:S(2)}, u32[]{:S(2)}) collective-permute-start(bf16[128,2048]{1,0:T(8,128)(2,1)} %collective-permute-done.1), channel_id=1, source_target_pairs={{0,8},{12,4},{1,9},{13,5},{2,10},{14,6},{3,11},{15,7},{16,24},{28,... | collective-permute-start | bytes 1572872 | tf_op jit(solution)/shard_map/ppermute | solution.py:195
  121.2 3.1 copy-start.3
  130.1 4.3 %copy-start.22 = (f32[128,1536]{1,0:T(8,128)}, f32[128,1536]{1,0:T(8,128)S(1)}, u32[]{:S(2)}) copy-start(f32[128,1536]{1,0:T(8,128)S(1)} %get-tuple-element.43) | copy-start | bytes 2359300
  130.1 20.4 %collective-permute-start.16 = (f32[128,1536]{1,0:T(8,128)}, f32[128,1536]{1,0:T(8,128)}, u32[]{:S(2)}, u32[]{:S(2)}) collective-permute-start(f32[128,1536]{1,0:T(8,128)} %get-tuple-element.44), channel_id=1, source_target_pairs={{0,1},{1,0},{2,3},{3,2},{4,5},{5,4},{6,7},{7,6},{8,9},{9,8},{10,11... | collective-permute-start | bytes 2359304 | tf_op jit(solution)/shard_map/ppermute | solution.py:192
  132.5 98.1 %collective-permute-start.37 = (bf16[64,2048]{1,0:T(8,128)(2,1)}, bf16[64,2048]{1,0:T(8,128)(2,1)}, u32[]{:S(2)}, u32[]{:S(2)}) collective-permute-start(bf16[64,2048]{1,0:T(8,128)(2,1)} %fusion.6), channel_id=1, source_target_pairs={{0,0},{4,13},{8,6},{12,11},{1,12},{5,1},{9,10},{13,7},{2,4},{6,9},... | collective-permute-start | bytes 786440 | tf_op jit(solution)/shard_map/ppermute | solution.py:199
  135.6 22.1 %collective-permute-start.5 = (bf16[128,2048]{1,0:T(8,128)(2,1)}, bf16[128,2048]{1,0:T(8,128)(2,1)S(1)}, u32[]{:S(2)}, u32[]{:S(2)}) collective-permute-start(bf16[128,2048]{1,0:T(8,128)(2,1)} %collective-permute-done.1), channel_id=1, source_target_pairs={{0,4},{12,8},{1,5},{13,9},{2,6},{14,10},{3,7},{15,11},{16,20},{28,... | collective-permute-start | bytes 1572872 | tf_op jit(solution)/shard_map/ppermute | solution.py:195
  136.9 24.4 %collective-permute-start.19 = (bf16[128,7168]{1,0:T(8,128)(2,1)}, bf16[128,7168]{1,0:T(8,128)(2,1)S(1)}, u32[]{:S(2)}, u32[]{:S(2)}) collective-permute-start(bf16[128,7168]{1,0:T(8,128)(2,1)} %collective-permute-done.8.a_ref.refs_2_), channel_id=1, source_target_pairs={{0,1},{1,0},{2,3},{3,2},{4,5},{5,4},{6,7},{7,6},{8,9},{9,8},{10,11... | collective-permute-start | bytes 5505032 | tf_op jit(solution)/shard_map/ppermute | solution.py:192
  137.5 20.7 %collective-permute-start.7 = (bf16[128,2048]{1,0:T(8,128)(2,1)}, bf16[128,2048]{1,0:T(8,128)(2,1)S(1)}, u32[]{:S(2)}, u32[]{:S(2)}) collective-permute-start(bf16[128,2048]{1,0:T(8,128)(2,1)} %collective-permute-done.6), channel_id=1, source_target_pairs={{8,12},{4,0},{9,13},{5,1},{10,14},{6,2},{11,15},{7,3},{24,28},{20,... | collective-permute-start | bytes 1572872 | tf_op jit(solution)/shard_map/ppermute | solution.py:195
  141.2 3.1 copy-start.4
  144.3 6.3 %copy-start.23 = (f32[128,1536]{1,0:T(8,128)S(1)}, f32[128,1536]{1,0:T(8,128)}, u32[]{:S(2)}) copy-start(f32[128,1536]{1,0:T(8,128)} %copy-done.22) | copy-start | bytes 2359300
  150.5 9.0 %collective-permute-start.17 = (f32[128,2048]{1,0:T(8,128)S(1)}, f32[128,2048]{1,0:T(8,128)S(1)}, u32[]{:S(2)}, u32[]{:S(2)}) collective-permute-start(f32[128,2048]{1,0:T(8,128)S(1)} %get-tuple-element.48), channel_id=1, source_target_pairs={{0,1},{1,0},{2,3},{3,2},{4,5},{5,4},{6,7},{7,6},{8,9},{9,8},{10,11... | collective-permute-start | bytes 3145736 | tf_op jit(solution)/shard_map/ppermute | solution.py:192
  157.6 2.7 collective-permute-start.18
  161.3 16.0 %copy-start.6 = (bf16[128,7168]{1,0:T(8,128)(2,1)}, bf16[128,7168]{1,0:T(8,128)(2,1)S(1)}, u32[]{:S(2)}) copy-start(bf16[128,7168]{1,0:T(8,128)(2,1)S(1)} %collective-permute-done.19.b_ref.refs_3_) | copy-start | bytes 5505028
  177.3 60.3 %copy-start.10 = (f32[256,2048]{1,0:T(8,128)}, f32[256,2048]{1,0:T(8,128)S(1)}, u32[]{:S(2)}) copy-start(f32[256,2048]{1,0:T(8,128)S(1)} %return_grad.3) | copy-start | bytes 6291460
  177.3 12.3 %copy-start.9 = (f32[256,2048]{1,0:T(8,128)S(1)}, f32[256,2048]{1,0:T(8,128)}, u32[]{:S(2)}) copy-start(f32[256,2048]{1,0:T(8,128)} %copy-done.8) | copy-start | bytes 6291460
  186.8 10.6 %collective-permute-start.31 = (f32[64,512]{1,0:T(8,128)S(1)}, f32[64,512]{1,0:T(8,128)S(1)}, u32[]{:S(2)}, u32[]{:S(2)}) collective-permute-start(f32[64,512]{1,0:T(8,128)S(1)} %rank_back.1), channel_id=1, source_target_pairs={{0,4},{4,0},{8,12},{12,8},{1,5},{5,1},{9,13},{13,9},{2,6},{6,2},{1... | collective-permute-start | bytes 393224 | tf_op jit(solution)/shard_map/ppermute | solution.py:195
  189.6 48.8 %collective-permute-start.27 = (bf16[128,2048]{1,0:T(8,128)(2,1)S(1)}, bf16[128,2048]{1,0:T(8,128)(2,1)}, u32[]{:S(2)}, u32[]{:S(2)}) collective-permute-start(bf16[128,2048]{1,0:T(8,128)(2,1)S(1)} %dynamic-slice_convert_fusion.1), channel_id=1, source_target_pairs={{12,0},{0,12},{13,1},{1,13},{14,2},{2,14},{15,3},{3,15},{28,16},{1... | collective-permute-start | bytes 1572872 | tf_op jit(solution)/shard_map/ppermute | solution.py:195
  196.0 44.5 %collective-permute-start.26 = (bf16[128,2048]{1,0:T(8,128)(2,1)S(1)}, bf16[128,2048]{1,0:T(8,128)(2,1)}, u32[]{:S(2)}, u32[]{:S(2)}) collective-permute-start(bf16[128,2048]{1,0:T(8,128)(2,1)S(1)} %dynamic-slice_convert_fusion.1), channel_id=1, source_target_pairs={{8,0},{4,12},{9,1},{5,13},{10,2},{6,14},{11,3},{7,15},{24,16},{20,... | collective-permute-start | bytes 1572872 | tf_op jit(solution)/shard_map/ppermute | solution.py:195
  197.4 28.3 %collective-permute-start.32 = (f32[64,512]{1,0:T(8,128)S(1)}, f32[64,512]{1,0:T(8,128)S(1)}, u32[]{:S(2)}, u32[]{:S(2)}) collective-permute-start(f32[64,512]{1,0:T(8,128)S(1)} %add.173), channel_id=1, source_target_pairs={{0,8},{4,12},{8,0},{12,4},{1,9},{5,13},{9,1},{13,5},{2,10},{6,14},... | collective-permute-start | bytes 393224 | tf_op jit(solution)/shard_map/ppermute | solution.py:195
  222.9 7.7 %copy-start.13 = (f32[128,7168]{1,0:T(8,128)}, f32[128,7168]{1,0:T(8,128)S(1)}, u32[]{:S(2)}) copy-start(f32[128,7168]{1,0:T(8,128)S(1)} %get-tuple-element.54) | copy-start | bytes 11010052
  222.9 74.1 %collective-permute-start.20 = (f32[128,7168]{1,0:T(8,128)}, f32[128,7168]{1,0:T(8,128)}, u32[]{:S(2)}, u32[]{:S(2)}) collective-permute-start(f32[128,7168]{1,0:T(8,128)} %get-tuple-element.55), channel_id=1, source_target_pairs={{0,1},{1,0},{2,3},{3,2},{4,5},{5,4},{6,7},{7,6},{8,9},{9,8},{10,11... | collective-permute-start | bytes 11010056 | tf_op jit(solution)/shard_map/ppermute | solution.py:192
  225.8 3.7 %collective-permute-start.33 = (bf16[4,64,128]{2,1,0:T(8,128)(2,1)S(1)}, bf16[4,64,128]{2,1,0:T(8,128)(2,1)S(1)}, u32[]{:S(2)}, u32[]{:S(2)}) collective-permute-start(bf16[4,64,128]{2,1,0:T(8,128)(2,1)S(1)} %pad_maximum_fusion.3), channel_id=1, source_target_pairs={{0,1},{1,0},{2,3},{3,2},{4,5},{5,4},{6,7},{7,6},{8,9},{9,8},{10,11... | collective-permute-start | bytes 196616 | tf_op jit(solution)/shard_map/ppermute | solution.py:192
  226.9 15.1 %copy-start.30 = (s32[4]{0:T(128)S(1)}, s32[4]{0:T(128)}, u32[]{:S(2)}) copy-start(s32[4]{0:T(128)} %constant.75.clone) | copy-start | bytes 52
  229.5 41.1 %copy-start.24 = (bf16[128,2048]{1,0:T(8,128)(2,1)S(1)}, bf16[128,2048]{1,0:T(8,128)(2,1)}, u32[]{:S(2)}) copy-start(bf16[128,2048]{1,0:T(8,128)(2,1)} %add_convert_fusion.2) | copy-start | bytes 1572868
  229.5 4.3 %collective-permute-start.34 = (bf16[4,64,128]{2,1,0:T(8,128)(2,1)S(1)}, bf16[4,64,128]{2,1,0:T(8,128)(2,1)S(1)}, u32[]{:S(2)}, u32[]{:S(2)}) collective-permute-start(bf16[4,64,128]{2,1,0:T(8,128)(2,1)S(1)} %pad_maximum_fusion.4), channel_id=1, source_target_pairs={{0,2},{1,3},{2,0},{3,1},{4,6},{5,7},{6,4},{7,5},{8,10},{9,11},{10,... | collective-permute-start | bytes 196616 | tf_op jit(solution)/shard_map/ppermute | solution.py:192
  230.6 41.9 %collective-permute-start.25 = (f32[128,2048]{1,0:T(8,128)}, f32[128,2048]{1,0:T(8,128)S(1)}, u32[]{:S(2)}, u32[]{:S(2)}) collective-permute-start(f32[128,2048]{1,0:T(8,128)} %constant_dynamic-slice_fusion), channel_id=1, source_target_pairs={{4,0},{8,12},{5,1},{9,13},{6,2},{10,14},{7,3},{11,15},{20,16},{24,... | collective-permute-start | bytes 3145736 | tf_op jit(solution)/shard_map/ppermute | solution.py:195
  233.8 6.7 %copy-start.29 = (bf16[4,64,128]{2,1,0:T(8,128)(2,1)}, bf16[4,64,128]{2,1,0:T(8,128)(2,1)S(1)}, u32[]{:S(2)}) copy-start(bf16[4,64,128]{2,1,0:T(8,128)(2,1)S(1)} %collective-permute-done.34) | copy-start | bytes 196612
  233.8 40.5 %collective-permute-start.28 = (f32[128,2048]{1,0:T(8,128)}, f32[128,2048]{1,0:T(8,128)}, u32[]{:S(2)}, u32[]{:S(2)}) collective-permute-start(f32[128,2048]{1,0:T(8,128)} %constant_dynamic-slice_fusion.1), channel_id=1, source_target_pairs={{0,4},{12,8},{1,5},{13,9},{2,6},{14,10},{3,7},{15,11},{16,20},{28,... | collective-permute-start | bytes 3145736 | tf_op jit(solution)/shard_map/ppermute | solution.py:195
  238.4 32.1 %collective-permute-start.30 = (bf16[128,2048]{1,0:T(8,128)(2,1)}, bf16[128,2048]{1,0:T(8,128)(2,1)}, u32[]{:S(2)}, u32[]{:S(2)}) collective-permute-start(bf16[128,2048]{1,0:T(8,128)(2,1)} %dynamic-slice_convert_fusion), channel_id=1, source_target_pairs={{12,4},{0,8},{13,5},{1,9},{14,6},{2,10},{15,7},{3,11},{28,20},{16,... | collective-permute-start | bytes 1572872 | tf_op jit(solution)/shard_map/ppermute | solution.py:195
  240.5 31.8 %collective-permute-start.29 = (bf16[128,2048]{1,0:T(8,128)(2,1)}, bf16[128,2048]{1,0:T(8,128)(2,1)}, u32[]{:S(2)}, u32[]{:S(2)}) collective-permute-start(bf16[128,2048]{1,0:T(8,128)(2,1)} %dynamic-slice_convert_fusion), channel_id=1, source_target_pairs={{8,4},{4,8},{9,5},{5,9},{10,6},{6,10},{11,7},{7,11},{24,20},{20,24... | collective-permute-start | bytes 1572872 | tf_op jit(solution)/shard_map/ppermute | solution.py:195
  246.3 36.7 %copy-start.7 = (bf16[128,7168]{1,0:T(8,128)(2,1)S(1)}, bf16[128,7168]{1,0:T(8,128)(2,1)}, u32[]{:S(2)}) copy-start(bf16[128,7168]{1,0:T(8,128)(2,1)} %copy-done.6) | copy-start | bytes 5505028
  246.3 36.7 %copy-start.12 = (bf16[8,64,512]{2,1,0:T(8,128)(2,1)S(1)}, bf16[8,64,512]{2,1,0:T(8,128)(2,1)}, u32[]{:S(2)}) copy-start(bf16[8,64,512]{2,1,0:T(8,128)(2,1)} %copy-done.11) | copy-start | bytes 1572868
  270.5 43.2 %collective-permute-start.21 = (bf16[128,2048]{1,0:T(8,128)(2,1)S(1)}, bf16[128,2048]{1,0:T(8,128)(2,1)S(1)}, u32[]{:S(2)}, u32[]{:S(2)}) collective-permute-start(bf16[128,2048]{1,0:T(8,128)(2,1)S(1)} %copy-done.24), channel_id=1, source_target_pairs={{0,2},{1,3},{2,0},{3,1},{4,6},{5,7},{6,4},{7,5},{8,10},{9,11},{10,... | collective-permute-start | bytes 1572872 | tf_op jit(solution)/shard_map/ppermute | solution.py:192
  272.3 32.8 %collective-permute-start.22 = (bf16[128,1536]{1,0:T(8,128)(2,1)}, bf16[128,1536]{1,0:T(8,128)(2,1)S(1)}, u32[]{:S(2)}, u32[]{:S(2)}) collective-permute-start(bf16[128,1536]{1,0:T(8,128)(2,1)} %add_convert_fusion.4), channel_id=1, source_target_pairs={{0,2},{1,3},{2,0},{3,1},{4,6},{5,7},{6,4},{7,5},{8,10},{9,11},{10,... | collective-permute-start | bytes 1179656 | tf_op jit(solution)/shard_map/ppermute | solution.py:192
  272.6 40.9 %collective-permute-start.24 = (bf16[128,1536]{1,0:T(8,128)(2,1)}, bf16[128,1536]{1,0:T(8,128)(2,1)S(1)}, u32[]{:S(2)}, u32[]{:S(2)}) collective-permute-start(bf16[128,1536]{1,0:T(8,128)(2,1)} %add_convert_fusion.3), channel_id=1, source_target_pairs={{0,2},{1,3},{2,0},{3,1},{4,6},{5,7},{6,4},{7,5},{8,10},{9,11},{10,... | collective-permute-start | bytes 1179656 | tf_op jit(solution)/shard_map/ppermute | solution.py:192
  277.6 15.5 %copy-start.16 = (bf16[128,2048]{1,0:T(8,128)(2,1)S(1)}, bf16[128,2048]{1,0:T(8,128)(2,1)}, u32[]{:S(2)}) copy-start(bf16[128,2048]{1,0:T(8,128)(2,1)} %copy-done.15) | copy-start | bytes 1572868
  277.6 15.5 %copy-start.18 = (bf16[128,2048]{1,0:T(8,128)(2,1)S(1)}, bf16[128,2048]{1,0:T(8,128)(2,1)}, u32[]{:S(2)}) copy-start(bf16[128,2048]{1,0:T(8,128)(2,1)} %copy-done.17) | copy-start | bytes 1572868
  277.6 15.5 %copy-start.20 = (bf16[128,2048]{1,0:T(8,128)(2,1)S(1)}, bf16[128,2048]{1,0:T(8,128)(2,1)}, u32[]{:S(2)}) copy-start(bf16[128,2048]{1,0:T(8,128)(2,1)} %copy-done.19) | copy-start | bytes 1572868
  277.6 19.4 %collective-permute-start.38 = (bf16[128,2048]{1,0:T(8,128)(2,1)S(1)}, bf16[128,2048]{1,0:T(8,128)(2,1)S(1)}, u32[]{:S(2)}, u32[]{:S(2)}) collective-permute-start(bf16[128,2048]{1,0:T(8,128)(2,1)S(1)} %add_convert_fusion), channel_id=1, source_target_pairs={{0,0},{13,4},{6,8},{11,12},{12,1},{1,5},{10,9},{7,13},{4,2},{9,6},... | collective-permute-start | bytes 1572872 | tf_op jit(solution)/shard_map/ppermute | solution.py:199
  293.1 3.9 %copy-start.25 = (bf16[128,2048]{1,0:T(8,128)(2,1)S(1)}, bf16[128,2048]{1,0:T(8,128)(2,1)}, u32[]{:S(2)}) copy-start(bf16[128,2048]{1,0:T(8,128)(2,1)} %add_convert_fusion.1) | copy-start | bytes 1572868
  293.1 3.9 %copy-start.14 = (f32[128,7168]{1,0:T(8,128)S(1)}, f32[128,7168]{1,0:T(8,128)}, u32[]{:S(2)}) copy-start(f32[128,7168]{1,0:T(8,128)} %copy-done.13) | copy-start | bytes 11010052
  297.0 25.7 %collective-permute-start.23 = (bf16[128,2048]{1,0:T(8,128)(2,1)S(1)}, bf16[128,2048]{1,0:T(8,128)(2,1)S(1)}, u32[]{:S(2)}, u32[]{:S(2)}) collective-permute-start(bf16[128,2048]{1,0:T(8,128)(2,1)S(1)} %copy-done.25), channel_id=1, source_target_pairs={{0,2},{1,3},{2,0},{3,1},{4,6},{5,7},{6,4},{7,5},{8,10},{9,11},{10,... | collective-permute-start | bytes 1572872 | tf_op jit(solution)/shard_map/ppermute | solution.py:192
  (6 other events, 8.7 us)

commit v3 on v2

v3 whole, which is shorter than its diff:
```python
import functools

import jax
import jax.numpy as jnp
from jax import lax
from jax.experimental import pallas as pl
from jax.experimental.pallas import tpu as pltpu
from jax.sharding import PartitionSpec as P

SEGMENT_BLOCK = 128

adapter_scale = 2.0
CORE, CHIP = 1, 2
VMEM = 48 * 1024 * 1024


def dot(a, b, contract):
    return lax.dot_general(a, b, ((contract[:1], contract[1:]), ((), ())), preferred_element_type=jnp.float32)


def after(x, *others):
    return lax.optimization_barrier((x,) + others)[0]


def cost(flops, moved):
    return pl.CostEstimate(flops=flops // 256, bytes_accessed=moved // 256, transcendentals=0)


def project(tokens, wide, weight, up_flat, start, stop, block):
    rows, depth = tokens.shape
    span = wide.shape[1]
    quarter = rows // 4
    base = start // block

    def kernel(tok_ref, wide_ref, w_ref, up_ref, keep_ref, send_ref):
        total = dot(tok_ref[...], w_ref[...], (1, 0)) + dot(wide_ref[...], up_ref[...], (1, 0))
        keep_ref[0] = total[:quarter]
        send_ref[0] = total[quarter : 2 * quarter]
        keep_ref[1] = total[2 * quarter : 3 * quarter]
        send_ref[1] = total[3 * quarter :]

    whole = lambda n: (0, 0)
    return pl.pallas_call(
        kernel,
        grid=((stop - start) // block,),
        in_specs=[
            pl.BlockSpec((rows, depth), whole),
            pl.BlockSpec((rows, span), whole),
            pl.BlockSpec((depth, block), lambda n: (0, n + base)),
            pl.BlockSpec((span, block), lambda n: (0, n + base)),
        ],
        out_specs=[pl.BlockSpec((2, quarter, block), lambda n: (0, 0, n))] * 2,
        out_shape=[jax.ShapeDtypeStruct((2, quarter, stop - start), jnp.float32)] * 2,
        compiler_params=pltpu.CompilerParams(vmem_limit_bytes=VMEM),
        cost_estimate=cost(2 * rows * (depth + span) * (stop - start), (2 * depth + 2 * span + 4 * rows) * (stop - start)),
        name="project",
    )(tokens, wide, weight, up_flat)


def return_grad(first, second, weight, half, sums=()):
    rows, hidden = first.shape
    depth = weight.shape[0]
    block = 512

    def kernel(a_ref, b_ref, w_ref, *refs):
        out_ref, sums_ref, rhs = refs[-3:]

        @pl.when(pl.program_id(0) == 0)
        def _():
            rhs[:rows] = a_ref[...]
            rhs[rows:] = b_ref[...]

        total = dot(w_ref[...], rhs[...], (1, 1)).T
        out_ref[...] = total
        sums_ref[...] = total.astype(sums_ref.dtype)

    whole = lambda n: (0, 0)
    return pl.pallas_call(
        kernel,
        grid=(depth // block,),
        in_specs=[
            pl.BlockSpec((rows, hidden), whole),
            pl.BlockSpec((rows, hidden), whole),
            pl.BlockSpec((block, hidden), lambda n: (n, 0)),
        ]
        + [pl.BlockSpec(memory_space=pl.ANY)] * len(sums),
        out_specs=[
            pl.BlockSpec((2 * rows, block), lambda n: (0, n)),
            pl.BlockSpec((2 * rows, block), lambda n: (half, n)),
        ],
        out_shape=[
            jax.ShapeDtypeStruct((2 * rows, depth), jnp.float32),
            jax.ShapeDtypeStruct((4 * rows, depth), first.dtype),
        ],
        input_output_aliases={3: 1} if sums else {},
        scratch_shapes=[pltpu.VMEM((2 * rows, hidden), first.dtype)],
        compiler_params=pltpu.CompilerParams(vmem_limit_bytes=VMEM),
        cost_estimate=cost(4 * rows * hidden * depth, 2 * hidden * (depth + 2 * rows)),
        name="return_grad",
    )(first, second, weight, *sums)


def rank_sum(facts, flat, blocks, places, rank, scale, block):
    span, columns = flat.shape
    rows = blocks[0].shape[0]
    count = len(blocks)
    slots = span // rank
    groups = facts.shape[0] // 2

    def kernel(facts_ref, flat_ref, *refs):
        out_ref, total = refs[count], refs[count + 1]
        n = pl.program_id(0)
        values = jnp.concatenate([c[...] for c in refs[:count]], axis=0)
        product = dot(flat_ref[...], values, (1, 1))

        @pl.when(n == 0)
        def _():
            total[...] = product

        @pl.when(n > 0)
        def _():
            total[...] += product

        @pl.when(n == pl.num_programs(0) - 1)
        def _():
            for at, place in enumerate(places):
                acc = jnp.zeros((rank, rows), jnp.float32)
                for s in range(slots):
                    part = total[s * rank : (s + 1) * rank, at * rows : (at + 1) * rows]
                    acc = jnp.where(facts_ref[place] == s, part, acc)
                alive = lax.broadcasted_iota(jnp.int32, (rank, rows), 1) < facts_ref[groups + place]
                out_ref[:, at * rows : (at + 1) * rows] = jnp.where(alive, acc * scale, 0.0)

    return pl.pallas_call(
        kernel,
        grid=(columns // block,),
        in_specs=[pl.BlockSpec(memory_space=pltpu.SMEM), pl.BlockSpec((span, block), lambda n: (0, n))]
        + [pl.BlockSpec((rows, block), lambda n: (0, n))] * count,
        out_specs=pl.BlockSpec((rank, count * rows), lambda n: (0, 0)),
        out_shape=jax.ShapeDtypeStruct((rank, count * rows), jnp.float32),
        scratch_shapes=[pltpu.VMEM((span, count * rows), jnp.float32)],
        compiler_params=pltpu.CompilerParams(vmem_limit_bytes=VMEM),
        cost_estimate=cost(2 * span * count * rows * columns, 2 * columns * (span + count * rows)),
        name="rank_sum",
    )(facts, flat, *blocks)


def spread(facts, here, there, slots, scale):
    rank, tokens = here.shape
    groups = facts.shape[0] // 2
    rows = tokens // groups

    def kernel(facts_ref, a_ref, b_ref, wide_ref, turned_ref, sum_ref):
        x = (a_ref[...] + b_ref[...]).astype(jnp.bfloat16)
        sum_ref[...] = x
        x = x.astype(jnp.float32) * scale
        for q in range(groups):
            part = x[:, q * rows : (q + 1) * rows]
            for s in range(slots):
                value = jnp.where(facts_ref[q] == s, part, 0.0)
                wide_ref[s * rank : (s + 1) * rank, q * rows : (q + 1) * rows] = value.astype(jnp.bfloat16)
        turned_ref[...] = wide_ref[...].astype(jnp.float32).T.astype(jnp.bfloat16)

    return pl.pallas_call(
        kernel,
        in_specs=[pl.BlockSpec(memory_space=pltpu.SMEM)] + [pl.BlockSpec(memory_space=pltpu.VMEM)] * 2,
        out_specs=[pl.BlockSpec(memory_space=pltpu.VMEM)] * 3,
        out_shape=[
            jax.ShapeDtypeStruct((slots * rank, tokens), jnp.bfloat16),
            jax.ShapeDtypeStruct((tokens, slots * rank), jnp.bfloat16),
            jax.ShapeDtypeStruct((rank, tokens), jnp.bfloat16),
        ],
        compiler_params=pltpu.CompilerParams(vmem_limit_bytes=VMEM),
        cost_estimate=cost(0, 8 * slots * rank * tokens),
        name="spread",
    )(facts, here, there)


def slot_grad(wide_t, blocks, block):
    span = wide_t.shape[0]
    rows, columns = blocks[0].shape
    groups = len(blocks)

    def kernel(wide_ref, *refs):
        values = jnp.concatenate([c[...] for c in refs[:groups]], axis=0)
        refs[groups][...] = dot(wide_ref[...], values, (1, 0))

    return pl.pallas_call(
        kernel,
        grid=(columns // block,),
        in_specs=[pl.BlockSpec((span, groups * rows), lambda n: (0, 0))]
        + [pl.BlockSpec((rows, block), lambda n: (0, n))] * groups,
        out_specs=pl.BlockSpec((span, block), lambda n: (0, n)),
        out_shape=jax.ShapeDtypeStruct((span, columns), jnp.float32),
        compiler_params=pltpu.CompilerParams(vmem_limit_bytes=VMEM),
        cost_estimate=cost(2 * span * groups * rows * columns, (4 * span + 2 * groups * rows) * columns),
        name="slot_grad",
    )(wide_t, *blocks)


def block_facts(block_adapter, block_length, adapter_slot, order, rows, per_owner, i):
    match = block_adapter[:, None] == jnp.arange(adapter_slot.shape[0], dtype=jnp.int32)[None, :]
    slots = jnp.sum(jnp.where(match, adapter_slot[None, :], 0), axis=1)[order]
    lengths = block_length[order]
    owned = slots // per_owner == i
    local_ids = slots % per_owner
    groups = order.shape[0]
    live = (lax.broadcasted_iota(jnp.int32, (groups, rows), 1) < lengths[:, None]).astype(jnp.float32)
    return owned, local_ids, live


def chosen(store, owned, local_ids):
    zero = jnp.zeros((), store.dtype)
    return [
        jnp.where(owned[q], lax.dynamic_index_in_dim(store, local_ids[q], 0, False), zero)
        for q in range(owned.shape[0])
    ]


def own_facts(block_adapter, block_length, adapter_slot, groups, per_owner, i):
    place = jnp.arange(groups, dtype=jnp.int32)
    at = ((place[:, None] ^ i) == place[None, :]).astype(jnp.int32)
    named = jnp.sum(at * block_adapter[None, :], axis=1)
    match = named[:, None] == jnp.arange(adapter_slot.shape[0], dtype=jnp.int32)[None, :]
    slots = jnp.sum(jnp.where(match, adapter_slot[None, :], 0), axis=1)
    here = slots - i * per_owner
    here = jnp.where((here >= 0) & (here < per_owner), here, -1)
    return jnp.concatenate([here, jnp.sum(at * block_length[None, :], axis=1)])


def local_square(
    tokens, weight, adapter_down, adapter_up, cotangent, block_adapter, block_length, adapter_slot
):
    groups = shards = 4
    rows, width = tokens.shape
    depth, hidden = weight.shape
    per_owner, _, rank = adapter_down.shape
    span = per_owner * rank
    b16 = jnp.bfloat16
    i, j = lax.axis_index("dp"), lax.axis_index("tp")

    def swap(x, bit):
        return lax.ppermute(x, "dp", [(d, d ^ bit) for d in range(groups)])

    def along(x, bit):
        return lax.ppermute(x, "tp", [(z, z ^ bit) for z in range(shards)])

    forth = [(c * groups + r, (r ^ c) * groups + c) for r in range(groups) for c in range(shards)]
    back_again = [(b, a) for a, b in forth]

    def turn(x, pairs):
        return lax.ppermute(x, ("tp", "dp"), pairs)

    turned = turn(tokens, forth)
    tok_x = swap(tokens, CHIP)
    cot_c = swap(cotangent, CORE)
    facts = own_facts(block_adapter, block_length, adapter_slot, groups, per_owner, i)
    down_flat = jnp.swapaxes(adapter_down, 1, 2).reshape(span, width)
    up_flat = adapter_up.reshape(span, hidden)

    def chosen(q):
        at = jnp.maximum(facts[q], 0) * rank
        return jnp.where(facts[q] >= 0, lax.dynamic_slice_in_dim(down_flat, at, rank, 0), jnp.zeros((), b16))

    all_tokens = lax.all_gather(turned, "tp", axis=0, tiled=True)
    cot_x = swap(after(cotangent, tok_x, turned), CHIP)

    mixed = swap(jnp.concatenate([tokens, after(tok_x, turned), chosen(1), chosen(3)], axis=0), CORE)
    toks = [tokens, mixed[:rows], tok_x, mixed[rows : 2 * rows]]
    down_x = swap(chosen(2) + mixed[2 * rows + rank :], CHIP)
    inner = rank_sum(facts, down_flat, toks, (0, 1, 2, 3), rank, 1.0, width)
    inner = inner + along(inner, 1)
    down_mine = turn(chosen(0) + mixed[2 * rows : 2 * rows + rank] + down_x, forth)
    inner_wide, inner_rows, _ = spread(facts, after(inner, down_mine), along(inner, 2), per_owner, adapter_scale)

    grad01, parts = return_grad(after(cotangent, inner_rows), cot_c, weight, 0)
    back01 = rank_sum(facts, after(up_flat, grad01), [cotangent, cot_c], (0, 1), rank, adapter_scale, 1024)
    all_tokens = after(all_tokens, back01)
    cot_xc = swap(after(cot_x, all_tokens), CORE)
    grad23, parts = return_grad(cot_x, cot_xc, weight, 1, (parts,))
    parts = lax.all_to_all(parts.reshape(shards, rows, depth), "tp", 0, 0, tiled=True)
    back23 = rank_sum(facts, after(up_flat, grad23), [cot_x, cot_xc], (2, 3), rank, adapter_scale, 1024)
    back = jnp.concatenate([back01, back23], axis=1)

    def grad_block(q):
        low = lax.dynamic_slice_in_dim(grad01, (q & 1) * rows, rows, 0)
        high = lax.dynamic_slice_in_dim(grad23, (q & 1) * rows, rows, 0)
        return jnp.where(q < 2, low, high)

    def share(x, got, bit):
        return x + jnp.concatenate([got[:, (q ^ bit) * rows : ((q ^ bit) + 1) * rows] for q in range(groups)], axis=1)

    block = 512
    steps = hidden // block
    pieces = 4
    edges = [(-(-steps * n // pieces)) * block for n in range(pieces + 1)]
    kept, sent, got_c, got_x, done = [], [], [], [], []

    def make(n, *points):
        keep, send = project(after(all_tokens, *points), inner_rows, weight, up_flat, edges[n], edges[n + 1], block)
        kept.append(keep)
        got_c.append(swap(send, CORE))
        return keep

    def cross(n, *points):
        summed = (after(kept[n], *points)[1] + got_c[n][1]).astype(b16)
        got_x.append(swap(summed, CHIP))
        return summed

    def finish(n, *points):
        done.append((after(kept[n], *points)[0] + got_c[n][0] + got_x[n].astype(jnp.float32)).astype(b16))
        return done[-1]

    point = make(0, back23)
    back = back + along(back, 1)
    point = make(1, point, back)
    back_wide, _, back_b = spread(facts, after(back, point), along(back, 2), per_owner, 1.0)
    point = cross(0, back_b)
    point = make(2, point)
    back_b = share(after(back_b, point), swap(back_b, CORE), CORE)
    point = cross(1, back_b)
    point = finish(0, point)
    point = make(3, point)
    back_b = share(after(back_b, point), swap(back_b, CHIP), CHIP)
    point = cross(2, back_b)
    point = finish(1, point)
    down_wide = slot_grad(after(back_wide, point), toks, 1024)
    point = cross(3, down_wide)
    up_wide = slot_grad(after(inner_wide, point), [cotangent, cot_c, cot_x, cot_xc], 1024)
    point = finish(2, up_wide)

    back_mine = lax.dynamic_slice_in_dim(back_b, j * rows, rows, 1)
    total = grad_block(j)
    for m in range(1, shards):
        total = total + lax.dynamic_index_in_dim(parts, j ^ m, 0, False).astype(jnp.float32)
    total = total + dot(after(back_mine, point), down_mine, (0, 0))
    tokens_grad = turn(total.astype(b16), back_again)
    finish(3, total)
    projected = jnp.concatenate(done, axis=1)
    up_grad = up_wide.reshape(per_owner, rank, hidden)
    down_grad = jnp.swapaxes(down_wide.reshape(per_owner, rank, width), 1, 2)
    return projected, tokens_grad, down_grad, up_grad


def local_any(
    groups, tokens, weight, adapter_down, adapter_up, cotangent, block_adapter, block_length, adapter_slot
):
    bits = [1 << n for n in range((groups - 1).bit_length())]

    def swap(x, bit):
        return lax.ppermute(x, "dp", [(d, d ^ bit) for d in range(groups)])

    def gather(x):
        blocks = {0: x}
        for bit in reversed(bits):
            blocks.update({q | bit: swap(block, bit) for q, block in blocks.items()})
        return jnp.stack([blocks[q] for q in range(groups)])

    def combine(parts):
        for bit in bits:
            parts = [a + swap(b, bit) for a, b in zip(parts[::2], parts[1::2])]
        return parts[0]

    rows, width = tokens.shape
    depth, hidden = weight.shape
    per_owner, _, rank = adapter_down.shape
    i = lax.axis_index("dp")
    order = jnp.arange(groups, dtype=jnp.int32) ^ i
    owned, local_ids, live = block_facts(
        block_adapter, block_length, adapter_slot, order, rows, per_owner, i
    )
    down_sel = chosen(adapter_down, owned, local_ids)
    up_sel = chosen(adapter_up, owned, local_ids)
    all_tokens = lax.all_gather(lax.all_gather(tokens, "dp", axis=0), "tp", axis=2, tiled=True)
    all_tokens = lax.dynamic_slice_in_dim(all_tokens, i * depth, depth, 2)[order]
    all_tokens = all_tokens.reshape(groups * rows, depth)
    toks, cots = gather(tokens), gather(cotangent)
    tok_all, cot_all = toks.reshape(-1, width), cots.reshape(-1, hidden)
    down_mine = combine(down_sel)
    inner = jnp.stack([dot(toks[q], down_sel[q], (1, 0)) for q in range(groups)])
    inner_b = (lax.psum(inner, "tp") * live[:, :, None]).astype(jnp.bfloat16)
    back = jnp.stack([dot(cots[q], up_sel[q], (1, 1)) for q in range(groups)])
    back = lax.psum(back[order], ("tp", "dp"))[order] * (adapter_scale * live)[:, :, None]
    back_b = back.astype(jnp.bfloat16)
    one_hot = (local_ids[:, None] == jnp.arange(per_owner, dtype=jnp.int32)[None, :]) & owned[:, None]

    def spread(x):
        wide = jnp.where(one_hot[:, None, :, None], x[:, :, None, :], jnp.zeros((), x.dtype))
        return wide.reshape(groups * rows, per_owner * rank)

    inner_wide = spread(inner_b) * jnp.bfloat16(adapter_scale)
    total = dot(cot_all, weight, (1, 1)).reshape(groups, rows, 1, depth)[order]
    placed = jnp.zeros((groups, rows, groups, depth), jnp.float32)
    placed = lax.dynamic_update_slice_in_dim(placed, total, i, 2)
    placed = lax.psum_scatter(placed, "dp", scatter_dimension=0, tiled=False)
    placed = placed.reshape(rows, groups * depth)
    placed = lax.psum_scatter(placed, "tp", scatter_dimension=1, tiled=True)
    tokens_grad = (placed + dot(back_b[0], down_mine, (1, 1))).astype(jnp.bfloat16)
    part = dot(all_tokens, weight, (1, 0)) + dot(inner_wide, adapter_up.reshape(-1, hidden), (1, 0))
    projected = combine(list(part.reshape(groups, rows, hidden))).astype(jnp.bfloat16)
    up_grad = dot(inner_wide, cot_all, (0, 0)).reshape(per_owner, rank, hidden)
    down_grad = dot(spread(back_b), tok_all, (0, 0)).reshape(per_owner, rank, width)
    return projected, tokens_grad, jnp.swapaxes(down_grad, 1, 2), up_grad


def solution(mesh):
    placed = (
        P(("grp", "dp"), "tp"),
        P("dp", "tp"),
        P("dp", "tp", None),
        P("dp", None, "tp"),
        P(("grp", "dp"), "tp"),
        P("grp"),
        P("grp"),
        P(),
    )
    groups, shards = mesh.shape["dp"], mesh.shape["tp"]
    square = groups == shards == 4
    return jax.shard_map(
        local_square if square else functools.partial(local_any, groups),
        mesh=mesh,
        in_specs=placed,
        out_specs=(
            P(("grp", "dp"), "tp"),
            P(("grp", "dp"), "tp"),
            P(("grp", "dp"), "tp", None),
            P(("grp", "dp"), None, "tp"),
        ),
        check_vma=False,
    )
```

time: 331 us -> 301 us (0.909); the launches traced: 325 us -> 300 us
  starting transfers between devices: 60.1 us -> 24.6 us
  waiting for transfers between devices: 95.8 us -> 128 us
  local copies, waits for them, and re-layouts: 21.7 us -> 9.31 us
  between operations: 10.8 us -> 19.8 us
  other arithmetic: 28.3 us -> 19.4 us
  matrix products: 8.96 us -> 2.51 us
    ppermute x4 -> x3, waiting for transfers between devices: 0.01 us -> 40.1 us  [turn(): return lax.ppermute(x, ('tp', 'dp'), pairs)]
    ppermute x16 -> x4, waiting for transfers between devices: 68.5 us -> 28.5 us  [along(): return lax.ppermute(x, 'tp', [(z, z ^ bit) for z in range(shards)])]
    ppermute x16 -> x4, starting transfers between devices: 41.4 us -> 3.34 us  [along(): return lax.ppermute(x, 'tp', [(z, z ^ bit) for z in range(shards)])]
    ppermute x19 -> x16, waiting for transfers between devices: 27.2 us -> 55.3 us  [swap(): return lax.ppermute(x, 'dp', [(d, d ^ bit) for d in range(groups)])]
    dot_general x5 -> x1, matrix products: 8.96 us -> 2.51 us  [dot(): lax.dot_general(a, b, ((contract[:1], contract[1:]), ((), ())), preferred...]
    add x5 -> x6, other arithmetic: 8.41 us -> 2.26 us  [the longest x1 1.11 us: local_square(): down_x = swap(chosen(2) + mixed[2 * rows + rank:], CHIP)]
    unnamed x63 -> x61, local copies, waits for them, and re-layouts: 13.3 us -> 7.32 us
    all_to_all x0 -> x1, starting transfers between devices: none -> 4.62 us  [local_square(): lax.all_to_all(parts.reshape(shards, rows, depth), 'tp', 0, 0, tiled=True)]
  transfers between devices with their start and end apart: 39 -> 25, of which waited for: 10 -> 12; matrix products, arithmetic and copies ran while one was open for 14% -> 7% of each run, Pallas kernels for 31% -> 22%
where the time goes in v3:
time: 301 us; the launch traced here: 300 us
  waiting for transfers between devices  128 us (43%)
  Pallas kernels  96.2 us (32%)
  starting transfers between devices  24.6 us (8%)
  between operations  19.8 us (7%)
  other arithmetic  19.4 us (6%)
  local copies, waits for them, and re-layouts  9.31 us (3%)
    ppermute x16, waiting for transfers between devices, swap(): return lax.ppermute(x, 'dp', [(d, d ^ bit) for d in range(groups)])  55.3 us
    ppermute x3, waiting for transfers between devices, turn(): return lax.ppermute(x, ('tp', 'dp'), pairs)  40.1 us
    pallas_call x4, Pallas kernels, project(): pl.pallas_call(kernel, grid=((stop - start) // block,), in_specs=[pl.Bloc...  33.1 us
    pallas_call x2, Pallas kernels, return_grad(): pl.pallas_call(kernel, grid=(depth // block,), in_specs=[pl.BlockSpec((ro...  30 us
    ppermute x4, waiting for transfers between devices, along(): return lax.ppermute(x, 'tp', [(z, z ^ bit) for z in range(shards)])  28.5 us
    pallas_call x3, Pallas kernels, rank_sum(): pl.pallas_call(kernel, grid=(columns // block,), in_specs=[pl.BlockSpec(m...  16.5 us
    pallas_call x2, Pallas kernels, slot_grad(): pl.pallas_call(kernel, grid=(columns // block,), in_specs=[pl.BlockSpec((...  13.6 us
    ppermute x3, starting transfers between devices, turn(): return lax.ppermute(x, ('tp', 'dp'), pairs)  10.2 us
  transfers between devices with their start and end apart: 25, of which 12 were waited for; matrix products, arithmetic and copies ran while one was open for 7% of the time, Pallas kernels for 22%

profile of v3, /device:TPU:2, one launch (start us, length us, event | category | flops | bytes accessed | tf_op | source)
XLA Modules:
  0.0 299.9 jit_solution(13485218872392570693)
XLA Ops:
  7.2 4.5 %collective-permute-start = (bf16[128,2048]{1,0:T(8,128)(2,1)}, bf16[128,2048]{1,0:T(8,128)(2,1)S(1)}, u32[]{:S(2)}, u32[]{:S(2)}) collective-permute-start(bf16[128,2048]{1,0:T(8,128)(2,1)} %refs_0_.6), channel_id=1, source_target_pairs={{0,0},{4,5},{8,10},{12,15},{1,4},{5,1},{9,14},{13,11},{2,8},{6,13}... | collective-permute-start | bytes 1572872 | tf_op jit(solution)/shard_map/ppermute | solution.py:252
  11.8 0.9 select_reduce_fusion.2
  12.7 0.8 select_reduce_fusion.1
  13.5 0.6 fusion.25
  16.7 1.1 dynamic-slice_select_fusion.1
  17.9 17.9 %collective-permute-done = bf16[128,2048]{1,0:T(8,128)(2,1)S(1)} collective-permute-done((bf16[128,2048]{1,0:T(8,128)(2,1)}, bf16[128,2048]{1,0:T(8,128)(2,1)S(1)}, u32[]{:S(2)}, u32[]{:S(2)}) %collective-permute-start) | collective-permute-done | bytes 524320 | tf_op jit(solution)/shard_map/ppermute | solution.py:252
  35.8 2.5 pad_maximum_fusion.1
  38.4 0.6 collective-permute-start.7
  41.6 1.6 collective-permute-done.2
  43.2 1.1 slice_add_fusion.8
  44.3 0.6 collective-permute-start.4
  45.0 1.4 fusion.22
  46.4 1.8 rank_sum.3
  48.2 38.3 %collective-permute-done.4 = bf16[64,2048]{1,0:T(8,128)(2,1)S(1)} collective-permute-done((bf16[64,2048]{1,0:T(8,128)(2,1)S(1)}, bf16[64,2048]{1,0:T(8,128)(2,1)S(1)}, u32[]{:S(2)}, u32[]{:S(2)}) %collective-permute-start.4) | collective-permute-done | bytes 262176 | tf_op jit(solution)/shard_map/ppermute | solution.py:243
  86.5 1.1 fusion.20
  87.6 3.6 %collective-permute-start.5 = (bf16[64,2048]{1,0:T(8,128)(2,1)S(1)}, bf16[64,2048]{1,0:T(8,128)(2,1)S(1)}, u32[]{:S(2)}, u32[]{:S(2)}) collective-permute-start(bf16[64,2048]{1,0:T(8,128)(2,1)S(1)} %fusion.20), channel_id=1, source_target_pairs={{0,0},{4,5},{8,10},{12,15},{1,4},{5,1},{9,14},{13,11},{2,8},{6,13}... | collective-permute-start | bytes 786440 | tf_op jit(solution)/shard_map/ppermute | solution.py:252
  91.3 0.7 collective-permute-start.3
  92.0 8.2 %collective-permute-done.3 = f32[64,512]{1,0:T(8,128)S(1)} collective-permute-done((f32[64,512]{1,0:T(8,128)S(1)}, f32[64,512]{1,0:T(8,128)S(1)}, u32[]{:S(2)}, u32[]{:S(2)}) %collective-permute-start.3) | collective-permute-done | bytes 131104 | tf_op jit(solution)/shard_map/ppermute | solution.py:246
  100.2 1.8 collective-permute-start.6
  102.0 1.4 collective-permute-done.5
  103.4 0.7 copy-done.28
  104.1 6.0 %collective-permute-done.6.b_ref = f32[64,512]{1,0:T(8,128)S(1)} collective-permute-done((f32[64,512]{1,0:T(8,128)S(1)}, f32[64,512]{1,0:T(8,128)S(1)}, u32[]{:S(2)}, u32[]{:S(2)}) %collective-permute-start.6) | collective-permute-done | bytes 131104 | tf_op jit(solution)/shard_map/ppermute | solution.py:246
  110.1 1.4 spread.2
  111.5 0.9 copy-done.17
  112.4 14.7 %return_grad.2 = (f32[256,2048]{1,0:T(8,128)S(1)}, bf16[512,2048]{1,0:T(8,128)(2,1)}) custom-call(bf16[128,7168]{1,0:T(8,128)(2,1)S(1)} %copy-done.2, bf16[128,7168]{1,0:T(8,128)(2,1)} %collective-permute-done.7.b_ref.refs_1_, bf16[2048,7168]{1,0:T(8,128)(2,1)} %w_ref.11), custom_call_target="tpu_custom_call" | custom-call | flops 29360128 | bytes 129024 | tf_op jit(solution)/shard_map/return_grad/pallas_call | solution.py:78
  127.1 1.4 copy-done.19
  128.4 7.4 %rank_sum.4 = f32[64,256]{1,0:T(8,128)S(1)} custom-call(s32[8]{0:T(128)S(1)} %pad_add_fusion.facts_ref, bf16[512,7168]{1,0:T(8,128)(2,1)} %bitcast.64, bf16[128,7168]{1,0:T(8,128)(2,1)S(1)} %copy-done.2, bf16[128,7168]{1,0:T(8,128)(2,1)} %collective-permute-done.7.b_ref.refs_1_), custom_call_target="tpu_custom_call" | custom-call | flops 7340032 | bytes 43008 | tf_op jit(solution)/shard_map/rank_sum/pallas_call | solution.py:134
  135.9 4.0 %collective-permute-done.9.b_ref.refs_1_.refs_3_ = bf16[128,7168]{1,0:T(8,128)(2,1)S(1)} collective-permute-done((bf16[128,7168]{1,0:T(8,128)(2,1)}, bf16[128,7168]{1,0:T(8,128)(2,1)S(1)}, u32[]{:S(2)}, u32[]{:S(2)}) %collective-permute-start.9) | collective-permute-done | bytes 1835040 | tf_op jit(solution)/shard_map/ppermute | solution.py:243
  139.9 15.3 %return_grad.3 = (f32[256,2048]{1,0:T(8,128)S(1)}, bf16[512,2048]{1,0:T(8,128)(2,1)}) custom-call(bf16[128,7168]{1,0:T(8,128)(2,1)} %collective-permute-done.8.a_ref.refs_0_.refs_2_, bf16[128,7168]{1,0:T(8,128)(2,1)S(1)} %collective-permute-done.9.b_ref.refs_1_.refs_3_, bf16[2048,7168]{1,0:T(8,128)(2,1)} %w_ref.11, ...), custom_call_target="tpu_custom_call", output_to_operand_aliasing={{1}: (3, {})} | custom-call | flops 29360128 | bytes 129024 | tf_op jit(solution)/shard_map/return_grad/pallas_call | solution.py:78
  155.2 1.4 copy-done.20
  156.6 7.3 %rank_sum.5 = f32[64,256]{1,0:T(8,128)S(1)} custom-call(s32[8]{0:T(128)S(1)} %pad_add_fusion.facts_ref, bf16[512,7168]{1,0:T(8,128)(2,1)} %bitcast.65, bf16[128,7168]{1,0:T(8,128)(2,1)} %collective-permute-done.8.a_ref.refs_0_.refs_2_, bf16[128,7168]{1,0:T(8,128)(2,1)S(1)} %collective-permute-done.9.b_ref.refs_1_.refs_3_), custom_call_target="tpu_custom_call" | custom-call | flops 7340032 | bytes 43008 | tf_op jit(solution)/shard_map/rank_sum/pallas_call | solution.py:134
  163.9 9.1 %project.4 = (f32[2,128,2048]{2,1,0:T(8,128)S(1)}, f32[2,128,2048]{2,1,0:T(8,128)S(1)}) custom-call(bf16[512,2048]{1,0:T(8,128)(2,1)} %all-gather.2.cloned.1.call-done.tok_ref, bf16[512,512]{1,0:T(8,128)(2,1)S(1)} %get-tuple-element.48.wide_ref, bf16[2048,7168]{1,0:T(8,128)(2,1)} %w_ref.11, bf16[512,7168]{1,0:T(8,128)(2,1)} %bitcast.66), custom_call_target="tpu_custom_call" | custom-call | flops 20971520 | bytes 57344 | tf_op jit(solution)/shard_map/project/pallas_call | solution.py:43
  173.0 0.2 collective-permute-start.12
  173.3 5.8 %collective-permute-done.10 = f32[64,512]{1,0:T(8,128)S(1)} collective-permute-done((f32[64,512]{1,0:T(8,128)S(1)}, f32[64,512]{1,0:T(8,128)S(1)}, u32[]{:S(2)}, u32[]{:S(2)}) %collective-permute-start.10) | collective-permute-done | bytes 131104 | tf_op jit(solution)/shard_map/ppermute | solution.py:246
  179.1 7.5 %project.5 = (f32[2,128,1536]{2,1,0:T(8,128)S(1)}, f32[2,128,1536]{2,1,0:T(8,128)}) custom-call(bf16[512,2048]{1,0:T(8,128)(2,1)S(1)} %copy-done, bf16[512,512]{1,0:T(8,128)(2,1)S(1)} %get-tuple-element.48.wide_ref, bf16[2048,7168]{1,0:T(8,128)(2,1)} %w_ref.11, bf16[512,7168]{1,0:T(8,128)(2,1)} %bitcast.67), custom_call_target="tpu_custom_call" | custom-call | flops 15728640 | bytes 43008 | tf_op jit(solution)/shard_map/project/pallas_call | solution.py:43
  186.6 0.8 collective-permute-start.11
  187.4 8.6 %collective-permute-done.11.b_ref = f32[64,512]{1,0:T(8,128)S(1)} collective-permute-done((f32[64,512]{1,0:T(8,128)S(1)}, f32[64,512]{1,0:T(8,128)S(1)}, u32[]{:S(2)}, u32[]{:S(2)}) %collective-permute-start.11) | collective-permute-done | bytes 131104 | tf_op jit(solution)/shard_map/ppermute | solution.py:246
  196.0 1.6 spread.3
  197.6 0.8 copy-done.21
  198.5 1.0 fusion.16
  199.5 9.8 %project.6 = (f32[2,128,2048]{2,1,0:T(8,128)S(1)}, f32[2,128,2048]{2,1,0:T(8,128)}) custom-call(bf16[512,2048]{1,0:T(8,128)(2,1)} %all-gather.2.cloned.1.call-done.tok_ref, bf16[512,512]{1,0:T(8,128)(2,1)S(1)} %get-tuple-element.48.wide_ref, bf16[2048,7168]{1,0:T(8,128)(2,1)} %w_ref.11, bf16[512,7168]{1,0:T(8,128)(2,1)} %bitcast.68), custom_call_target="tpu_custom_call" | custom-call | flops 20971520 | bytes 57344 | tf_op jit(solution)/shard_map/project/pallas_call | solution.py:43
  209.4 1.3 copy-done.11
  210.7 0.4 collective-permute-start.17
  211.1 4.6 %all-to-all-start = ((bf16[4,128,2048]{2,1,0:T(8,128)(2,1)}), bf16[4,128,2048]{2,1,0:T(8,128)(2,1)}, u32[]{:S(2)}, u32[]{:S(2)}) async-start(bf16[4,128,2048]{2,1,0:T(8,128)(2,1)} %bitcast.71), calls=%async_computation | async-start | bytes 4194304 | tf_op jit(solution)/shard_map/all_to_all | solution.py:281
  215.9 1.4 fusion.18
  217.3 2.1 collective-permute-start.18
  219.3 0.1 collective-permute-start.16
  219.4 11.4 %collective-permute-done.15 = bf16[128,2048]{1,0:T(8,128)(2,1)S(1)} collective-permute-done((bf16[128,2048]{1,0:T(8,128)(2,1)}, bf16[128,2048]{1,0:T(8,128)(2,1)S(1)}, u32[]{:S(2)}, u32[]{:S(2)}) %collective-permute-start.15) | collective-permute-done | bytes 524320 | tf_op jit(solution)/shard_map/ppermute | solution.py:243
  230.8 2.2 fusion.6
  233.1 6.7 %project.7 = (f32[2,128,1536]{2,1,0:T(8,128)S(1)}, f32[2,128,1536]{2,1,0:T(8,128)S(1)}) custom-call(bf16[512,2048]{1,0:T(8,128)(2,1)S(1)} %copy-done.1, bf16[512,512]{1,0:T(8,128)(2,1)S(1)} %get-tuple-element.48.wide_ref, bf16[2048,7168]{1,0:T(8,128)(2,1)} %w_ref.11, bf16[512,7168]{1,0:T(8,128)(2,1)} %bitcast.69), custom_call_target="tpu_custom_call" | custom-call | flops 15728640 | bytes 43008 | tf_op jit(solution)/shard_map/project/pallas_call | solution.py:43
  240.0 1.8 fusion.17
  241.9 1.3 fusion.14
  243.2 2.9 slot_grad.2
  246.1 0.1 fusion.19
  246.2 2.1 collective-permute-start.21
  248.3 10.6 %slot_grad.3 = f32[512,7168]{1,0:T(8,128)} custom-call(bf16[512,512]{1,0:T(8,128)(2,1)S(1)} %copy-done.18, bf16[128,7168]{1,0:T(8,128)(2,1)S(1)} %copy-done.3, bf16[128,7168]{1,0:T(8,128)(2,1)} %collective-permute-done.7.b_ref.refs_1_, bf16[128,7168]{1,0:T(8,128)(2,1)} %collective-permute-done.8.a_ref.refs_0_.refs_2_, bf16[128,7168]{1,0:T(8,128)(2,1)} %copy-done.4), custom_call_target="tpu_custom_call" | custom-call | flops 14680064 | bytes 86016 | tf_op jit(solution)/shard_map/slot_grad/pallas_call | solution.py:188
  258.9 1.4 fusion.2
  260.4 3.9 %all-to-all-done = bf16[4,128,2048]{2,1,0:T(8,128)(2,1)} async-done(((bf16[4,128,2048]{2,1,0:T(8,128)(2,1)}), bf16[4,128,2048]{2,1,0:T(8,128)(2,1)}, u32[]{:S(2)}, u32[]{:S(2)}) %all-to-all-start) | async-done | bytes 2097184 | tf_op jit(solution)/shard_map/all_to_all | solution.py:281
  264.3 2.5 convolution_add_fusion
  266.9 2.1 collective-permute-start.22
  269.0 1.1 fusion.10
  270.1 1.4 pad_maximum_fusion
  271.5 20.8 %collective-permute-done.22 = bf16[128,2048]{1,0:T(8,128)(2,1)S(1)} collective-permute-done((bf16[128,2048]{1,0:T(8,128)(2,1)S(1)}, bf16[128,2048]{1,0:T(8,128)(2,1)S(1)}, u32[]{:S(2)}, u32[]{:S(2)}) %collective-permute-start.22) | collective-permute-done | bytes 524320 | tf_op jit(solution)/shard_map/ppermute | solution.py:252
  292.3 0.8 copy.15
  (90 shorter events, 0.9 us)
Async XLA Ops:
  7.2 128.6 %all-gather.2.cloned.1.call-start = ((), (), s32[]{:S(2)}) async-start(), calls=%async_computation.1 | async-start | bytes 2621440 | tf_op jit(solution)/shard_map/all_gather | solution.py:265
  7.2 28.6 %collective-permute-start = (bf16[128,2048]{1,0:T(8,128)(2,1)}, bf16[128,2048]{1,0:T(8,128)(2,1)S(1)}, u32[]{:S(2)}, u32[]{:S(2)}) collective-permute-start(bf16[128,2048]{1,0:T(8,128)(2,1)} %refs_0_.6), channel_id=1, source_target_pairs={{0,0},{4,5},{8,10},{12,15},{1,4},{5,1},{9,14},{13,11},{2,8},{6,13}... | collective-permute-start | bytes 1572872 | tf_op jit(solution)/shard_map/ppermute | solution.py:252
  11.7 24.1 %collective-permute-start.1 = (bf16[128,2048]{1,0:T(8,128)(2,1)}, bf16[128,2048]{1,0:T(8,128)(2,1)S(1)}, u32[]{:S(2)}, u32[]{:S(2)}) collective-permute-start(bf16[128,2048]{1,0:T(8,128)(2,1)} %refs_0_.6), channel_id=1, source_target_pairs={{0,2},{1,3},{2,0},{3,1},{4,6},{5,7},{6,4},{7,5},{8,10},{9,11},{10,... | collective-permute-start | bytes 1572872 | tf_op jit(solution)/shard_map/ppermute | solution.py:243
  17.9 20.5 %copy-start.2 = (bf16[128,7168]{1,0:T(8,128)(2,1)S(1)}, bf16[128,7168]{1,0:T(8,128)(2,1)}, u32[]{:S(2)}) copy-start(bf16[128,7168]{1,0:T(8,128)(2,1)} %refs_0_.7) | copy-start | bytes 5505028
  35.8 2.5 copy-start.27
  38.3 8.0 %copy-start.6 = (bf16[128,2048]{1,0:T(8,128)(2,1)S(1)}, bf16[128,2048]{1,0:T(8,128)(2,1)}, u32[]{:S(2)}) copy-start(bf16[128,2048]{1,0:T(8,128)(2,1)} %refs_0_.6) | copy-start | bytes 1572868
  38.3 4.9 %collective-permute-start.2 = (bf16[384,2048]{1,0:T(8,128)(2,1)}, bf16[384,2048]{1,0:T(8,128)(2,1)}, u32[]{:S(2)}, u32[]{:S(2)}) collective-permute-start(bf16[384,2048]{1,0:T(8,128)(2,1)} %pad_maximum_fusion.1), channel_id=1, source_target_pairs={{0,1},{1,0},{2,3},{3,2},{4,5},{5,4},{6,7},{7,6},{8,9},{9,8},{10,11... | collective-permute-start | bytes 4718600 | tf_op jit(solution)/shard_map/ppermute | solution.py:243
  38.4 74.0 %collective-permute-start.7 = (bf16[128,7168]{1,0:T(8,128)(2,1)S(1)}, bf16[128,7168]{1,0:T(8,128)(2,1)}, u32[]{:S(2)}, u32[]{:S(2)}) collective-permute-start(bf16[128,7168]{1,0:T(8,128)(2,1)S(1)} %copy-done.2), channel_id=1, source_target_pairs={{0,1},{1,0},{2,3},{3,2},{4,5},{5,4},{6,7},{7,6},{8,9},{9,8},{10,11... | collective-permute-start | bytes 5505032 | tf_op jit(solution)/shard_map/ppermute | solution.py:243
  38.9 96.9 %collective-permute-start.8 = (bf16[128,7168]{1,0:T(8,128)(2,1)S(1)}, bf16[128,7168]{1,0:T(8,128)(2,1)}, u32[]{:S(2)}, u32[]{:S(2)}) collective-permute-start(bf16[128,7168]{1,0:T(8,128)(2,1)S(1)} %copy-done.2), channel_id=1, source_target_pairs={{0,2},{1,3},{2,0},{3,1},{4,6},{5,7},{6,4},{7,5},{8,10},{9,11},{10,... | collective-permute-start | bytes 5505032 | tf_op jit(solution)/shard_map/ppermute | solution.py:243
  41.5 4.8 %copy-start.5 = (bf16[8,2048,64]{1,2,0:T(8,128)(2,1)S(1)}, bf16[8,2048,64]{1,2,0:T(8,128)(2,1)}, u32[]{:S(2)}) copy-start(bf16[8,2048,64]{1,2,0:T(8,128)(2,1)} %param.10) | copy-start | bytes 6291460
  44.3 42.2 %collective-permute-start.4 = (bf16[64,2048]{1,0:T(8,128)(2,1)S(1)}, bf16[64,2048]{1,0:T(8,128)(2,1)S(1)}, u32[]{:S(2)}, u32[]{:S(2)}) collective-permute-start(bf16[64,2048]{1,0:T(8,128)(2,1)S(1)} %slice_add_fusion.8), channel_id=1, source_target_pairs={{0,2},{1,3},{2,0},{3,1},{4,6},{5,7},{6,4},{7,5},{8,10},{9,11},{10,... | collective-permute-start | bytes 786440 | tf_op jit(solution)/shard_map/ppermute | solution.py:243
  46.3 1.9 copy-start.7
  46.3 1.9 copy-start.9
  87.6 15.8 %collective-permute-start.5 = (bf16[64,2048]{1,0:T(8,128)(2,1)S(1)}, bf16[64,2048]{1,0:T(8,128)(2,1)S(1)}, u32[]{:S(2)}, u32[]{:S(2)}) collective-permute-start(bf16[64,2048]{1,0:T(8,128)(2,1)S(1)} %fusion.20), channel_id=1, source_target_pairs={{0,0},{4,5},{8,10},{12,15},{1,4},{5,1},{9,14},{13,11},{2,8},{6,13}... | collective-permute-start | bytes 786440 | tf_op jit(solution)/shard_map/ppermute | solution.py:252
  91.3 8.9 %collective-permute-start.3 = (f32[64,512]{1,0:T(8,128)S(1)}, f32[64,512]{1,0:T(8,128)S(1)}, u32[]{:S(2)}, u32[]{:S(2)}) collective-permute-start(f32[64,512]{1,0:T(8,128)S(1)} %rank_sum.3), channel_id=1, source_target_pairs={{0,4},{4,0},{8,12},{12,8},{1,5},{5,1},{9,13},{13,9},{2,6},{6,2},{1... | collective-permute-start | bytes 393224 | tf_op jit(solution)/shard_map/ppermute | solution.py:246
  100.2 9.9 %collective-permute-start.6 = (f32[64,512]{1,0:T(8,128)S(1)}, f32[64,512]{1,0:T(8,128)S(1)}, u32[]{:S(2)}, u32[]{:S(2)}) collective-permute-start(f32[64,512]{1,0:T(8,128)S(1)} %add.116.a_ref), channel_id=1, source_target_pairs={{0,8},{4,12},{8,0},{12,4},{1,9},{5,13},{9,1},{13,5},{2,10},{6,14},... | collective-permute-start | bytes 393224 | tf_op jit(solution)/shard_map/ppermute | solution.py:246
  103.4 0.7 copy-start.28
  111.5 0.9 copy-start.17
  127.1 1.4 copy-start.19
  135.8 4.1 %collective-permute-start.9 = (bf16[128,7168]{1,0:T(8,128)(2,1)}, bf16[128,7168]{1,0:T(8,128)(2,1)S(1)}, u32[]{:S(2)}, u32[]{:S(2)}) collective-permute-start(bf16[128,7168]{1,0:T(8,128)(2,1)} %collective-permute-done.8.a_ref.refs_0_.refs_2_), channel_id=1, source_target_pairs={{0,1},{1,0},{2,3},{3,2},{4,5},{5,4},{6,7},{7,6},{8,9},{9,8},{10,11... | collective-permute-start | bytes 5505032 | tf_op jit(solution)/shard_map/ppermute | solution.py:243
  139.9 16.7 %copy-start.4 = (bf16[128,7168]{1,0:T(8,128)(2,1)}, bf16[128,7168]{1,0:T(8,128)(2,1)S(1)}, u32[]{:S(2)}) copy-start(bf16[128,7168]{1,0:T(8,128)(2,1)S(1)} %collective-permute-done.9.b_ref.refs_1_.refs_3_) | copy-start | bytes 5505028
  155.2 1.4 copy-start.20
  163.9 15.2 %copy-start = (bf16[512,2048]{1,0:T(8,128)(2,1)S(1)}, bf16[512,2048]{1,0:T(8,128)(2,1)}, u32[]{:S(2)}) copy-start(bf16[512,2048]{1,0:T(8,128)(2,1)} %all-gather.2.cloned.1.call-done.tok_ref) | copy-start | bytes 6291460
  173.0 25.5 %copy-start.13 = (f32[2,128,2048]{2,1,0:T(8,128)}, f32[2,128,2048]{2,1,0:T(8,128)S(1)}, u32[]{:S(2)}) copy-start(f32[2,128,2048]{2,1,0:T(8,128)S(1)} %get-tuple-element.71) | copy-start | bytes 6291460
  173.0 25.5 %collective-permute-start.12 = (f32[2,128,2048]{2,1,0:T(8,128)S(1)}, f32[2,128,2048]{2,1,0:T(8,128)S(1)}, u32[]{:S(2)}, u32[]{:S(2)}) collective-permute-start(f32[2,128,2048]{2,1,0:T(8,128)S(1)} %get-tuple-element.65), channel_id=1, source_target_pairs={{0,1},{1,0},{2,3},{3,2},{4,5},{5,4},{6,7},{7,6},{8,9},{9,8},{10,11... | collective-permute-start | bytes 6291464 | tf_op jit(solution)/shard_map/ppermute | solution.py:243
  173.2 5.8 %collective-permute-start.10 = (f32[64,512]{1,0:T(8,128)S(1)}, f32[64,512]{1,0:T(8,128)S(1)}, u32[]{:S(2)}, u32[]{:S(2)}) collective-permute-start(f32[64,512]{1,0:T(8,128)S(1)} %pad_maximum_fusion.2), channel_id=1, source_target_pairs={{0,4},{4,0},{8,12},{12,8},{1,5},{5,1},{9,13},{13,9},{2,6},{6,2},{1... | collective-permute-start | bytes 393224 | tf_op jit(solution)/shard_map/ppermute | solution.py:246
  186.6 29.3 %collective-permute-start.14 = (f32[2,128,1536]{2,1,0:T(8,128)}, f32[2,128,1536]{2,1,0:T(8,128)}, u32[]{:S(2)}, u32[]{:S(2)}) collective-permute-start(f32[2,128,1536]{2,1,0:T(8,128)} %get-tuple-element.70), channel_id=1, source_target_pairs={{0,1},{1,0},{2,3},{3,2},{4,5},{5,4},{6,7},{7,6},{8,9},{9,8},{10,11... | collective-permute-start | bytes 4718600 | tf_op jit(solution)/shard_map/ppermute | solution.py:243
  186.6 9.3 %collective-permute-start.11 = (f32[64,512]{1,0:T(8,128)S(1)}, f32[64,512]{1,0:T(8,128)S(1)}, u32[]{:S(2)}, u32[]{:S(2)}) collective-permute-start(f32[64,512]{1,0:T(8,128)S(1)} %fusion.21.a_ref), channel_id=1, source_target_pairs={{0,8},{4,12},{8,0},{12,4},{1,9},{5,13},{9,1},{13,5},{2,10},{6,14},... | collective-permute-start | bytes 393224 | tf_op jit(solution)/shard_map/ppermute | solution.py:246
  197.6 0.8 copy-start.21
  198.4 17.3 %collective-permute-start.13 = (bf16[64,512]{1,0:T(8,128)(2,1)S(1)}, bf16[64,512]{1,0:T(8,128)(2,1)S(1)}, u32[]{:S(2)}, u32[]{:S(2)}) collective-permute-start(bf16[64,512]{1,0:T(8,128)(2,1)S(1)} %get-tuple-element.68), channel_id=1, source_target_pairs={{0,1},{1,0},{2,3},{3,2},{4,5},{5,4},{6,7},{7,6},{8,9},{9,8},{10,11... | collective-permute-start | bytes 196616 | tf_op jit(solution)/shard_map/ppermute | solution.py:243
  198.5 10.9 %copy-start.23 = (f32[2,128,2048]{2,1,0:T(8,128)}, f32[2,128,2048]{2,1,0:T(8,128)S(1)}, u32[]{:S(2)}) copy-start(f32[2,128,2048]{2,1,0:T(8,128)S(1)} %collective-permute-done.12) | copy-start | bytes 6291460
  209.4 1.3 copy-start.11
  210.7 29.3 %collective-permute-start.17 = (f32[2,128,2048]{2,1,0:T(8,128)}, f32[2,128,2048]{2,1,0:T(8,128)}, u32[]{:S(2)}, u32[]{:S(2)}) collective-permute-start(f32[2,128,2048]{2,1,0:T(8,128)} %get-tuple-element.76), channel_id=1, source_target_pairs={{0,1},{1,0},{2,3},{3,2},{4,5},{5,4},{6,7},{7,6},{8,9},{9,8},{10,11... | collective-permute-start | bytes 6291464 | tf_op jit(solution)/shard_map/ppermute | solution.py:243
  211.1 53.2 %all-to-all-start = ((bf16[4,128,2048]{2,1,0:T(8,128)(2,1)}), bf16[4,128,2048]{2,1,0:T(8,128)(2,1)}, u32[]{:S(2)}, u32[]{:S(2)}) async-start(bf16[4,128,2048]{2,1,0:T(8,128)(2,1)} %bitcast.71), calls=%async_computation | async-start | bytes 4194304 | tf_op jit(solution)/shard_map/all_to_all | solution.py:281
  215.7 15.1 %copy-start.14 = (f32[2,128,2048]{2,1,0:T(8,128)S(1)}, f32[2,128,2048]{2,1,0:T(8,128)}, u32[]{:S(2)}) copy-start(f32[2,128,2048]{2,1,0:T(8,128)} %copy-done.13) | copy-start | bytes 6291460
  215.8 15.1 %collective-permute-start.15 = (bf16[128,2048]{1,0:T(8,128)(2,1)}, bf16[128,2048]{1,0:T(8,128)(2,1)S(1)}, u32[]{:S(2)}, u32[]{:S(2)}) collective-permute-start(bf16[128,2048]{1,0:T(8,128)(2,1)} %fusion.16), channel_id=1, source_target_pairs={{0,2},{1,3},{2,0},{3,1},{4,6},{5,7},{6,4},{7,5},{8,10},{9,11},{10,... | collective-permute-start | bytes 1572872 | tf_op jit(solution)/shard_map/ppermute | solution.py:243
  215.9 17.2 %copy-start.1 = (bf16[512,2048]{1,0:T(8,128)(2,1)S(1)}, bf16[512,2048]{1,0:T(8,128)(2,1)}, u32[]{:S(2)}) copy-start(bf16[512,2048]{1,0:T(8,128)(2,1)} %all-gather.2.cloned.1.call-done.tok_ref) | copy-start | bytes 6291460
  217.3 24.6 %collective-permute-start.18 = (bf16[128,1536]{1,0:T(8,128)(2,1)S(1)}, bf16[128,1536]{1,0:T(8,128)(2,1)S(1)}, u32[]{:S(2)}, u32[]{:S(2)}) collective-permute-start(bf16[128,1536]{1,0:T(8,128)(2,1)S(1)} %fusion.18), channel_id=1, source_target_pairs={{0,2},{1,3},{2,0},{3,1},{4,6},{5,7},{6,4},{7,5},{8,10},{9,11},{10,... | collective-permute-start | bytes 1179656 | tf_op jit(solution)/shard_map/ppermute | solution.py:243
  219.3 20.5 %collective-permute-start.16 = (bf16[64,512]{1,0:T(8,128)(2,1)S(1)}, bf16[64,512]{1,0:T(8,128)(2,1)S(1)}, u32[]{:S(2)}, u32[]{:S(2)}) collective-permute-start(bf16[64,512]{1,0:T(8,128)(2,1)S(1)} %maximum_add_fusion), channel_id=1, source_target_pairs={{0,2},{1,3},{2,0},{3,1},{4,6},{5,7},{6,4},{7,5},{8,10},{9,11},{10,... | collective-permute-start | bytes 196616 | tf_op jit(solution)/shard_map/ppermute | solution.py:243
  233.1 6.9 %copy-start.12 = (f32[2,128,2048]{2,1,0:T(8,128)S(1)}, f32[2,128,2048]{2,1,0:T(8,128)}, u32[]{:S(2)}) copy-start(f32[2,128,2048]{2,1,0:T(8,128)} %copy-done.11) | copy-start | bytes 6291460
  239.8 6.3 %copy-start.15 = (f32[2,128,1536]{2,1,0:T(8,128)}, f32[2,128,1536]{2,1,0:T(8,128)S(1)}, u32[]{:S(2)}) copy-start(f32[2,128,1536]{2,1,0:T(8,128)S(1)} %get-tuple-element.87) | copy-start | bytes 4718596
  239.8 6.3 %collective-permute-start.19 = (f32[2,128,1536]{2,1,0:T(8,128)S(1)}, f32[2,128,1536]{2,1,0:T(8,128)S(1)}, u32[]{:S(2)}, u32[]{:S(2)}) collective-permute-start(f32[2,128,1536]{2,1,0:T(8,128)S(1)} %get-tuple-element.82), channel_id=1, source_target_pairs={{0,1},{1,0},{2,3},{3,2},{4,5},{5,4},{6,7},{7,6},{8,9},{9,8},{10,11... | collective-permute-start | bytes 4718600 | tf_op jit(solution)/shard_map/ppermute | solution.py:243
  239.9 3.2 %copy-start.8 = (bf16[128,2048]{1,0:T(8,128)(2,1)S(1)}, bf16[128,2048]{1,0:T(8,128)(2,1)}, u32[]{:S(2)}) copy-start(bf16[128,2048]{1,0:T(8,128)(2,1)} %copy-done.7) | copy-start | bytes 1572868
  240.0 3.2 %copy-start.10 = (bf16[128,2048]{1,0:T(8,128)(2,1)S(1)}, bf16[128,2048]{1,0:T(8,128)(2,1)}, u32[]{:S(2)}) copy-start(bf16[128,2048]{1,0:T(8,128)(2,1)} %copy-done.9) | copy-start | bytes 1572868
  240.0 3.2 %copy-start.22 = (bf16[512,512]{1,0:T(8,128)(2,1)S(1)}, bf16[512,512]{1,0:T(8,128)(2,1)}, u32[]{:S(2)}) copy-start(bf16[512,512]{1,0:T(8,128)(2,1)} %copy-done.21) | copy-start | bytes 1572868
  241.8 17.1 %collective-permute-start.20 = (bf16[128,2048]{1,0:T(8,128)(2,1)S(1)}, bf16[128,2048]{1,0:T(8,128)(2,1)S(1)}, u32[]{:S(2)}, u32[]{:S(2)}) collective-permute-start(bf16[128,2048]{1,0:T(8,128)(2,1)S(1)} %fusion.17), channel_id=1, source_target_pairs={{0,2},{1,3},{2,0},{3,1},{4,6},{5,7},{6,4},{7,5},{8,10},{9,11},{10,... | collective-permute-start | bytes 1572872 | tf_op jit(solution)/shard_map/ppermute | solution.py:243
  243.2 5.1 %copy-start.18 = (bf16[512,512]{1,0:T(8,128)(2,1)S(1)}, bf16[512,512]{1,0:T(8,128)(2,1)}, u32[]{:S(2)}) copy-start(bf16[512,512]{1,0:T(8,128)(2,1)} %copy-done.17) | copy-start | bytes 1572868
  246.1 2.2 copy-start.3
  246.1 12.8 %copy-start.25 = (f32[2,128,1536]{2,1,0:T(8,128)}, f32[2,128,1536]{2,1,0:T(8,128)S(1)}, u32[]{:S(2)}) copy-start(f32[2,128,1536]{2,1,0:T(8,128)S(1)} %collective-permute-done.19) | copy-start | bytes 4718596
  246.2 22.7 %collective-permute-start.21 = (bf16[128,1536]{1,0:T(8,128)(2,1)S(1)}, bf16[128,1536]{1,0:T(8,128)(2,1)}, u32[]{:S(2)}, u32[]{:S(2)}) collective-permute-start(bf16[128,1536]{1,0:T(8,128)(2,1)S(1)} %fusion.19), channel_id=1, source_target_pairs={{0,2},{1,3},{2,0},{3,1},{4,6},{5,7},{6,4},{7,5},{8,10},{9,11},{10,... | collective-permute-start | bytes 1179656 | tf_op jit(solution)/shard_map/ppermute | solution.py:243
  258.9 5.4 %copy-start.29 = (bf16[64,2048]{1,0:T(8,128)(2,1)S(1)}, bf16[64,2048]{1,0:T(8,128)(2,1)}, u32[]{:S(2)}) copy-start(bf16[64,2048]{1,0:T(8,128)(2,1)} %copy-done.28) | copy-start | bytes 786436
  260.4 8.6 %copy-start.16 = (f32[2,128,1536]{2,1,0:T(8,128)S(1)}, f32[2,128,1536]{2,1,0:T(8,128)}, u32[]{:S(2)}) copy-start(f32[2,128,1536]{2,1,0:T(8,128)} %copy-done.15) | copy-start | bytes 4718596
  264.3 4.6 %copy-start.26 = (f32[2,128,1536]{2,1,0:T(8,128)S(1)}, f32[2,128,1536]{2,1,0:T(8,128)}, u32[]{:S(2)}) copy-start(f32[2,128,1536]{2,1,0:T(8,128)} %copy-done.25) | copy-start | bytes 4718596
  266.9 3.2 %copy-start.24 = (bf16[128,2048]{1,0:T(8,128)(2,1)S(1)}, bf16[128,2048]{1,0:T(8,128)(2,1)}, u32[]{:S(2)}) copy-start(bf16[128,2048]{1,0:T(8,128)(2,1)} %fusion.6) | copy-start | bytes 1572868
  266.9 25.4 %collective-permute-start.22 = (bf16[128,2048]{1,0:T(8,128)(2,1)S(1)}, bf16[128,2048]{1,0:T(8,128)(2,1)S(1)}, u32[]{:S(2)}, u32[]{:S(2)}) collective-permute-start(bf16[128,2048]{1,0:T(8,128)(2,1)S(1)} %convolution_add_fusion), channel_id=1, source_target_pairs={{0,0},{5,4},{10,8},{15,12},{4,1},{1,5},{14,9},{11,13},{8,2},{13,6}... | collective-permute-start | bytes 1572872 | tf_op jit(solution)/shard_map/ppermute | solution.py:252
Sparse Core Ops, SparseCore 0:
  38.5 45.7 all-gather.1

commit v4 on v3

--- a/solution.py
+++ b/solution.py
@@ -26,92 +26,102 @@
     return pl.CostEstimate(flops=flops // 256, bytes_accessed=moved // 256, transcendentals=0)
 
 
-def project(tokens, wide, weight, up_flat, start, stop, block):
-    rows, depth = tokens.shape
+def project(facts, near, far, wide, weight, up_flat, start, stop, block):
+    _, rows, depth = near.shape
+    groups = 4
     span = wide.shape[1]
-    quarter = rows // 4
     base = start // block
 
-    def kernel(tok_ref, wide_ref, w_ref, up_ref, keep_ref, send_ref):
-        total = dot(tok_ref[...], w_ref[...], (1, 0)) + dot(wide_ref[...], up_ref[...], (1, 0))
-        keep_ref[0] = total[:quarter]
-        send_ref[0] = total[quarter : 2 * quarter]
-        keep_ref[1] = total[2 * quarter : 3 * quarter]
-        send_ref[1] = total[3 * quarter :]
+    def kernel(facts_ref, near_ref, far_ref, wide_ref, w_ref, up_ref, keep_ref, send_ref, lhs):
+        @pl.when(pl.program_id(0) == 0)
+        def _():
+            for m in range(groups):
+                at = pl.multiple_of((facts_ref[2 * groups] ^ m) * rows, rows)
+                lhs[pl.ds(at, rows)] = (far_ref if m & 1 else near_ref)[m >> 1]
+
+        total = dot(lhs[...], w_ref[...], (1, 0)) + dot(wide_ref[...], up_ref[...], (1, 0))
+        keep_ref[0] = total[:rows]
+        send_ref[0] = total[rows : 2 * rows]
+        keep_ref[1] = total[2 * rows : 3 * rows]
+        send_ref[1] = total[3 * rows :]
+
+    whole = lambda n: (0, 0, 0)
+    return pl.pallas_call(
+        kernel,
+        grid=((stop - start) // block,),
+        in_specs=[
+            pl.BlockSpec(memory_space=pltpu.SMEM),
+            pl.BlockSpec((2, rows, depth), whole),
+            pl.BlockSpec((2, rows, depth), whole),
+            pl.BlockSpec((groups * rows, span), lambda n: (0, 0)),
+            pl.BlockSpec((depth, block), lambda n: (0, n + base)),
+            pl.BlockSpec((span, block), lambda n: (0, n + base)),
+        ],
+        out_specs=[pl.BlockSpec((2, rows, block), lambda n: (0, 0, n))] * 2,
+        out_shape=[jax.ShapeDtypeStruct((2, rows, stop - start), jnp.float32)] * 2,
+        scratch_shapes=[pltpu.VMEM((groups * rows, depth), near.dtype)],
+        compiler_params=pltpu.CompilerParams(vmem_limit_bytes=VMEM),
+        cost_estimate=cost(2 * groups * rows * (depth + span) * (stop - start), 2 * (depth + span + 2 * groups * rows) * (stop - start)),
+        name="project",
+    )(facts, near, far, wide, weight, up_flat)
+
+
+def return_grad(first, second, weight, half, start, stop, sums=()):
+    rows, hidden = first.shape
+    depth = weight.shape[0]
+    block = 256
+    base = start // block
+
+    def kernel(a_ref, b_ref, w_ref, *refs):
+        out_ref, sums_ref, rhs = refs[-3:]
+
+        @pl.when(pl.program_id(0) == 0)
+        def _():
+            rhs[:rows] = a_ref[...]
+            rhs[rows:] = b_ref[...]
+
+        total = dot(w_ref[...], rhs[...], (1, 1)).T
+        out_ref[...] = total
+        sums_ref[...] = total.astype(sums_ref.dtype)
 
     whole = lambda n: (0, 0)
     return pl.pallas_call(
         kernel,
         grid=((stop - start) // block,),
         in_specs=[
-            pl.BlockSpec((rows, depth), whole),
-            pl.BlockSpec((rows, span), whole),
-            pl.BlockSpec((depth, block), lambda n: (0, n + base)),
-            pl.BlockSpec((span, block), lambda n: (0, n + base)),
-        ],
-        out_specs=[pl.BlockSpec((2, quarter, block), lambda n: (0, 0, n))] * 2,
-        out_shape=[jax.ShapeDtypeStruct((2, quarter, stop - start), jnp.float32)] * 2,
-        compiler_params=pltpu.CompilerParams(vmem_limit_bytes=VMEM),
-        cost_estimate=cost(2 * rows * (depth + span) * (stop - start), (2 * depth + 2 * span + 4 * rows) * (stop - start)),
-        name="project",
-    )(tokens, wide, weight, up_flat)
-
-
-def return_grad(first, second, weight, half, sums=()):
-    rows, hidden = first.shape
-    depth = weight.shape[0]
-    block = 512
-
-    def kernel(a_ref, b_ref, w_ref, *refs):
-        out_ref, sums_ref, rhs = refs[-3:]
-
-        @pl.when(pl.program_id(0) == 0)
-        def _():
-            rhs[:rows] = a_ref[...]
-            rhs[rows:] = b_ref[...]
-
-        total = dot(w_ref[...], rhs[...], (1, 1)).T
-        out_ref[...] = total
-        sums_ref[...] = total.astype(sums_ref.dtype)
-
-    whole = lambda n: (0, 0)
-    return pl.pallas_call(
-        kernel,
-        grid=(depth // block,),
-        in_specs=[
             pl.BlockSpec((rows, hidden), whole),
             pl.BlockSpec((rows, hidden), whole),
-            pl.BlockSpec((block, hidden), lambda n: (n, 0)),
+            pl.BlockSpec((block, hidden), lambda n: (n + base, 0)),
         ]
         + [pl.BlockSpec(memory_space=pl.ANY)] * len(sums),
         out_specs=[
             pl.BlockSpec((2 * rows, block), lambda n: (0, n)),
-            pl.BlockSpec((2 * rows, block), lambda n: (half, n)),
+            pl.BlockSpec((2 * rows, block), lambda n: (half, n + base)),
         ],
         out_shape=[
-            jax.ShapeDtypeStruct((2 * rows, depth), jnp.float32),
+            jax.ShapeDtypeStruct((2 * rows, stop - start), jnp.float32),
             jax.ShapeDtypeStruct((4 * rows, depth), first.dtype),
         ],
         input_output_aliases={3: 1} if sums else {},
         scratch_shapes=[pltpu.VMEM((2 * rows, hidden), first.dtype)],
         compiler_params=pltpu.CompilerParams(vmem_limit_bytes=VMEM),
-        cost_estimate=cost(4 * rows * hidden * depth, 2 * hidden * (depth + 2 * rows)),
+        cost_estimate=cost(4 * rows * hidden * (stop - start), 2 * hidden * (stop - start + 2 * rows)),
         name="return_grad",
     )(first, second, weight, *sums)
 
 
-def rank_sum(facts, flat, blocks, places, rank, scale, block):
-    span, columns = flat.shape
+def rank_back(facts, store, blocks, places, block):
+    _, rank, columns = store.shape
     rows = blocks[0].shape[0]
     count = len(blocks)
-    slots = span // rank
     groups = facts.shape[0] // 2
 
-    def kernel(facts_ref, flat_ref, *refs):
-        out_ref, total = refs[count], refs[count + 1]
+    def kernel(facts_ref, *refs):
+        slots, values, out_ref, total = refs[:count], refs[count : 2 * count], refs[-2], refs[-1]
         n = pl.program_id(0)
-        values = jnp.concatenate([c[...] for c in refs[:count]], axis=0)
-        product = dot(flat_ref[...], values, (1, 1))
+        left = jnp.concatenate([r[0] for r in slots], axis=0)
+        right = jnp.concatenate([r[...] for r in values], axis=0)
+        product = dot(left, right, (1, 1))
 
         @pl.when(n == 0)
         def _():
@@ -124,34 +134,40 @@
         @pl.when(n == pl.num_programs(0) - 1)
         def _():
             for at, place in enumerate(places):
-                acc = jnp.zeros((rank, rows), jnp.float32)
-                for s in range(slots):
-                    part = total[s * rank : (s + 1) * rank, at * rows : (at + 1) * rows]
-                    acc = jnp.where(facts_ref[place] == s, part, acc)
+                part = total[at * rank : (at + 1) * rank, at * rows : (at + 1) * rows]
                 alive = lax.broadcasted_iota(jnp.int32, (rank, rows), 1) < facts_ref[groups + place]
-                out_ref[:, at * rows : (at + 1) * rows] = jnp.where(alive, acc * scale, 0.0)
+                alive = alive & (facts_ref[place] >= 0)
+                out_ref[:, at * rows : (at + 1) * rows] = jnp.where(alive, part * adapter_scale, 0.0)
+
+    def chosen_slot(place):
+        return lambda n, facts_ref: (jnp.maximum(facts_ref[place], 0), 0, n)
 
     return pl.pallas_call(
         kernel,
-        grid=(columns // block,),
-        in_specs=[pl.BlockSpec(memory_space=pltpu.SMEM), pl.BlockSpec((span, block), lambda n: (0, n))]
-        + [pl.BlockSpec((rows, block), lambda n: (0, n))] * count,
-        out_specs=pl.BlockSpec((rank, count * rows), lambda n: (0, 0)),
+        grid_spec=pltpu.PrefetchScalarGridSpec(
+            num_scalar_prefetch=1,
+            grid=(columns // block,),
+            in_specs=[pl.BlockSpec((1, rank, block), chosen_slot(place)) for place in places]
+            + [pl.BlockSpec((rows, block), lambda n, facts_ref: (0, n))] * count,
+            out_specs=pl.BlockSpec((rank, count * rows), lambda n, facts_ref: (0, 0)),
+            scratch_shapes=[pltpu.VMEM((count * rank, count * rows), jnp.float32)],
+        ),
         out_shape=jax.ShapeDtypeStruct((rank, count * rows), jnp.float32),
-        scratch_shapes=[pltpu.VMEM((span, count * rows), jnp.float32)],
         compiler_params=pltpu.CompilerParams(vmem_limit_bytes=VMEM),
-        cost_estimate=cost(2 * span * count * rows * columns, 2 * columns * (span + count * rows)),
-        name="rank_sum",
-    )(facts, flat, *blocks)
+        cost_estimate=cost(2 * count * rank * count * rows * columns, 2 * columns * count * (rank + rows)),
+        name="rank_back",
+    )(facts, *[store] * count, *blocks)
 
 
 def spread(facts, here, there, slots, scale):
     rank, tokens = here.shape
     groups = facts.shape[0] // 2
     rows = tokens // groups
-
-    def kernel(facts_ref, a_ref, b_ref, wide_ref, turned_ref, sum_ref):
-        x = (a_ref[...] + b_ref[...]).astype(jnp.bfloat16)
+    values = [here] if there is None else [here, there]
+
+    def kernel(facts_ref, *refs):
+        wide_ref, turned_ref, sum_ref = refs[-3:]
+        x = sum(r[...] for r in refs[:-3]).astype(jnp.bfloat16)
         sum_ref[...] = x
         x = x.astype(jnp.float32) * scale
         for q in range(groups):
@@ -163,7 +179,7 @@
 
     return pl.pallas_call(
         kernel,
-        in_specs=[pl.BlockSpec(memory_space=pltpu.SMEM)] + [pl.BlockSpec(memory_space=pltpu.VMEM)] * 2,
+        in_specs=[pl.BlockSpec(memory_space=pltpu.SMEM)] + [pl.BlockSpec(memory_space=pltpu.VMEM)] * len(values),
         out_specs=[pl.BlockSpec(memory_space=pltpu.VMEM)] * 3,
         out_shape=[
             jax.ShapeDtypeStruct((slots * rank, tokens), jnp.bfloat16),
@@ -173,7 +189,7 @@
         compiler_params=pltpu.CompilerParams(vmem_limit_bytes=VMEM),
         cost_estimate=cost(0, 8 * slots * rank * tokens),
         name="spread",
-    )(facts, here, there)
+    )(facts, *values)
 
 
 def slot_grad(wide_t, blocks, block):
@@ -217,15 +233,60 @@
     ]
 
 
-def own_facts(block_adapter, block_length, adapter_slot, groups, per_owner, i):
-    place = jnp.arange(groups, dtype=jnp.int32)
-    at = ((place[:, None] ^ i) == place[None, :]).astype(jnp.int32)
-    named = jnp.sum(at * block_adapter[None, :], axis=1)
-    match = named[:, None] == jnp.arange(adapter_slot.shape[0], dtype=jnp.int32)[None, :]
-    slots = jnp.sum(jnp.where(match, adapter_slot[None, :], 0), axis=1)
-    here = slots - i * per_owner
-    here = jnp.where((here >= 0) & (here < per_owner), here, -1)
-    return jnp.concatenate([here, jnp.sum(at * block_length[None, :], axis=1)])
+def choose(block_adapter, block_length, adapter_slot, here, store):
+    slots, rank, width = store.shape
+    groups = block_adapter.shape[0]
+
+    def block_of(step):
+        return jnp.clip(jnp.where(step < 2, 2 * step + 1, 6 - 2 * step), 0, groups - 1)
+
+    def slot_of(q, adapter_ref, slot_ref, here_ref):
+        return slot_ref[adapter_ref[q ^ here_ref[0]]] - here_ref[0] * slots
+
+    def kernel(adapter_ref, length_ref, slot_ref, here_ref, store_ref, near_ref, rest_ref, facts_ref):
+        step = pl.program_id(0)
+
+        @pl.when(step == 0)
+        def _():
+            for q in range(groups):
+                at = slot_of(q, adapter_ref, slot_ref, here_ref)
+                facts_ref[q] = jnp.where((at >= 0) & (at < slots), at, -1)
+                facts_ref[groups + q] = length_ref[q ^ here_ref[0]]
+            facts_ref[2 * groups] = here_ref[1]
+
+        at = slot_of(block_of(step), adapter_ref, slot_ref, here_ref)
+        value = store_ref[0] * ((at >= 0) & (at < slots)).astype(store_ref.dtype)
+
+        @pl.when(step < 2)
+        def _():
+            near_ref[...] = value
+
+        @pl.when(step >= 2)
+        def _():
+            rest_ref[...] = value
+
+    def stored(step, adapter_ref, length_ref, slot_ref, here_ref):
+        at = slot_of(block_of(step), adapter_ref, slot_ref, here_ref)
+        return jnp.clip(at, 0, slots - 1), 0, 0
+
+    return pl.pallas_call(
+        kernel,
+        grid_spec=pltpu.PrefetchScalarGridSpec(
+            num_scalar_prefetch=4,
+            grid=(groups,),
+            in_specs=[pl.BlockSpec((1, rank, width), stored)],
+            out_specs=[
+                pl.BlockSpec((rank, width), lambda step, *refs: (jnp.minimum(step, 1), 0)),
+                pl.BlockSpec((rank, width), lambda step, *refs: (jnp.maximum(step - 2, 0), 0)),
+                pl.BlockSpec(memory_space=pltpu.SMEM),
+            ],
+        ),
+        out_shape=[jax.ShapeDtypeStruct((2 * rank, width), store.dtype)] * 2
+        + [jax.ShapeDtypeStruct((2 * groups + 1,), jnp.int32)],
+        compiler_params=pltpu.CompilerParams(vmem_limit_bytes=VMEM),
+        cost_estimate=cost(0, 8 * rank * width * groups),
+        name="choose",
+    )(block_adapter, block_length, adapter_slot, here, store)
 
 
 def local_square(
@@ -252,40 +313,52 @@
         return lax.ppermute(x, ("tp", "dp"), pairs)
 
     turned = turn(tokens, forth)
-    tok_x = swap(tokens, CHIP)
     cot_c = swap(cotangent, CORE)
-    facts = own_facts(block_adapter, block_length, adapter_slot, groups, per_owner, i)
-    down_flat = jnp.swapaxes(adapter_down, 1, 2).reshape(span, width)
+    here = jnp.stack([i, j]).astype(jnp.int32)
+    down_t = jnp.swapaxes(adapter_down, 1, 2)
+    near, rest, facts = choose(block_adapter, block_length, adapter_slot, here, down_t)
     up_flat = adapter_up.reshape(span, hidden)
-
-    def chosen(q):
-        at = jnp.maximum(facts[q], 0) * rank
-        return jnp.where(facts[q] >= 0, lax.dynamic_slice_in_dim(down_flat, at, rank, 0), jnp.zeros((), b16))
-
-    all_tokens = lax.all_gather(turned, "tp", axis=0, tiled=True)
-    cot_x = swap(after(cotangent, tok_x, turned), CHIP)
-
-    mixed = swap(jnp.concatenate([tokens, after(tok_x, turned), chosen(1), chosen(3)], axis=0), CORE)
-    toks = [tokens, mixed[:rows], tok_x, mixed[rows : 2 * rows]]
-    down_x = swap(chosen(2) + mixed[2 * rows + rank :], CHIP)
-    inner = rank_sum(facts, down_flat, toks, (0, 1, 2, 3), rank, 1.0, width)
-    inner = inner + along(inner, 1)
-    down_mine = turn(chosen(0) + mixed[2 * rows : 2 * rows + rank] + down_x, forth)
-    inner_wide, inner_rows, _ = spread(facts, after(inner, down_mine), along(inner, 2), per_owner, adapter_scale)
-
-    grad01, parts = return_grad(after(cotangent, inner_rows), cot_c, weight, 0)
-    back01 = rank_sum(facts, after(up_flat, grad01), [cotangent, cot_c], (0, 1), rank, adapter_scale, 1024)
-    all_tokens = after(all_tokens, back01)
-    cot_xc = swap(after(cot_x, all_tokens), CORE)
-    grad23, parts = return_grad(cot_x, cot_xc, weight, 1, (parts,))
-    parts = lax.all_to_all(parts.reshape(shards, rows, depth), "tp", 0, 0, tiled=True)
-    back23 = rank_sum(facts, after(up_flat, grad23), [cot_x, cot_xc], (2, 3), rank, adapter_scale, 1024)
+    half = depth // 2
+
+    near = swap(near, CORE)
+    down_x = swap(rest[:rank] + near[rank:], CHIP)
+    cot_x = swap(after(cotangent, near), CHIP)
+    down_own = rest[rank:] + near[:rank] + down_x
+    inner = dot(down_own, after(tokens, turned), (1, 1))
+
+    grad01, parts = return_grad(after(cotangent, inner), cot_c, weight, 0, 0, half)
+    inner = inner + after(along(inner, 1), grad01)
+    tok_2 = along(after(turned, inner), 2)
+    more01, parts = return_grad(after(cotangent, inner, turned), cot_c, weight, 0, half, depth, (parts,))
+    inner = inner + after(along(inner, 2), more01)
+    inner = jnp.where(lax.broadcasted_iota(jnp.int32, (rank, rows), 1) < facts[groups], inner, 0.0).astype(b16)
+    back01 = rank_back(facts, after(adapter_up, inner), [cotangent, cot_c], (0, 1), hidden // 4)
+    inner = jnp.concatenate([inner, swap(inner, CORE)], axis=1)
+    tok_near = jnp.stack([turned, after(tok_2, back01)])
+    tok_far = along(tok_near, 1)
+
+    cot_xc = swap(after(cot_x, tok_near), CORE)
+    tok_x = swap(after(tokens, cot_x), CHIP)
+    inner = jnp.concatenate([inner, swap(after(inner, cot_x), CHIP)], axis=1)
+    back23 = rank_back(facts, adapter_up, [cot_x, cot_xc], (2, 3), hidden // 4)
     back = jnp.concatenate([back01, back23], axis=1)
+    grad23, parts = return_grad(after(cot_x, back), cot_xc, weight, 1, 0, half, (parts,))
+    back = after(back, grad23) + along(back, 1)
+    more23, parts = return_grad(after(cot_x, back), cot_xc, weight, 1, half, depth, (parts,))
+    back_wide, _, back_b = spread(facts, after(back, more23), along(back, 2), per_owner, 1.0)
+    parts = after(parts, back_b).reshape(shards, rows, depth)
+    parts = [lax.all_to_all(x, "tp", 0, 0, tiled=True) for x in (parts[:, :, :half], parts[:, :, half:])]
+    mixed = swap(jnp.concatenate([tokens, after(tok_x, back_b)], axis=0), CORE)
+    toks = [tokens, mixed[:rows], tok_x, mixed[rows:]]
+    down_mine = turn(after(down_own, cot_x), forth)
+    inner_wide, inner_rows, _ = spread(facts, after(inner, back_b), None, per_owner, adapter_scale)
 
     def grad_block(q):
-        low = lax.dynamic_slice_in_dim(grad01, (q & 1) * rows, rows, 0)
-        high = lax.dynamic_slice_in_dim(grad23, (q & 1) * rows, rows, 0)
-        return jnp.where(q < 2, low, high)
+        halves = [
+            [lax.dynamic_slice_in_dim(x, (q & 1) * rows, rows, 0) for x in both]
+            for both in ((grad01, grad23), (more01, more23))
+        ]
+        return jnp.concatenate([jnp.where(q < 2, low, high) for low, high in halves], axis=1)
 
     def share(x, got, bit):
         return x + jnp.concatenate([got[:, (q ^ bit) * rows : ((q ^ bit) + 1) * rows] for q in range(groups)], axis=1)
@@ -297,7 +370,7 @@
     kept, sent, got_c, got_x, done = [], [], [], [], []
 
     def make(n, *points):
-        keep, send = project(after(all_tokens, *points), inner_rows, weight, up_flat, edges[n], edges[n + 1], block)
+        keep, send = project(facts, after(tok_near, *points), tok_far, inner_rows, weight, up_flat, edges[n], edges[n + 1], block)
         kept.append(keep)
         got_c.append(swap(send, CORE))
         return keep
@@ -311,31 +384,30 @@
         done.append((after(kept[n], *points)[0] + got_c[n][0] + got_x[n].astype(jnp.float32)).astype(b16))
         return done[-1]
 
-    point = make(0, back23)
-    back = back + along(back, 1)
-    point = make(1, point, back)
-    back_wide, _, back_b = spread(facts, after(back, point), along(back, 2), per_owner, 1.0)
+    point = make(0, tok_x, down_mine)
+    back_b = share(after(back_b, point), swap(back_b, CORE), CORE)
+    point = make(1, back_b)
+    back_b = share(after(back_b, point), swap(back_b, CHIP), CHIP)
     point = cross(0, back_b)
-    point = make(2, point)
-    back_b = share(after(back_b, point), swap(back_b, CORE), CORE)
-    point = cross(1, back_b)
+    point = make(2, point, mixed, parts[0])
+    point = cross(1, point)
     point = finish(0, point)
     point = make(3, point)
-    back_b = share(after(back_b, point), swap(back_b, CHIP), CHIP)
-    point = cross(2, back_b)
+    point = cross(2, point)
     point = finish(1, point)
     down_wide = slot_grad(after(back_wide, point), toks, 1024)
     point = cross(3, down_wide)
-    up_wide = slot_grad(after(inner_wide, point), [cotangent, cot_c, cot_x, cot_xc], 1024)
+    back_mine = lax.dynamic_slice_in_dim(back_b, j * rows, rows, 1)
+    total = after(grad_block(j), point, parts[1])
+    for m in range(1, shards):
+        total = total + jnp.concatenate(
+            [lax.dynamic_index_in_dim(x, j ^ m, 0, False).astype(jnp.float32) for x in parts], axis=1
+        )
+    total = (total + dot(back_mine, down_mine, (0, 0))).astype(b16)
+    tokens_grad = turn(total, back_again)
+    up_wide = slot_grad(after(inner_wide, total), [cotangent, cot_c, cot_x, cot_xc], 1024)
     point = finish(2, up_wide)
-
-    back_mine = lax.dynamic_slice_in_dim(back_b, j * rows, rows, 1)
-    total = grad_block(j)
-    for m in range(1, shards):
-        total = total + lax.dynamic_index_in_dim(parts, j ^ m, 0, False).astype(jnp.float32)
-    total = total + dot(after(back_mine, point), down_mine, (0, 0))
-    tokens_grad = turn(total.astype(b16), back_again)
-    finish(3, total)
+    finish(3, point)
     projected = jnp.concatenate(done, axis=1)
     up_grad = up_wide.reshape(per_owner, rank, hidden)
     down_grad = jnp.swapaxes(down_wide.reshape(per_owner, rank, width), 1, 2)

time: 301 us -> 295 us (0.980)
  waiting for transfers between devices: 128 us -> 104 us
  starting transfers between devices: 24.6 us -> 45.4 us
  between operations: 19.8 us -> 1.28 us
  local copies, waits for them, and re-layouts: 9.31 us -> 22.2 us
    ppermute x3, waiting for transfers between devices: 40.1 us -> 28 us  [turn(): return lax.ppermute(x, ('tp', 'dp'), pairs)]
    ppermute x4 -> x6, starting transfers between devices: 3.34 us -> 15.3 us  [along(): return lax.ppermute(x, 'tp', [(z, z ^ bit) for z in range(shards)])]
    ppermute x16 -> x19, waiting for transfers between devices: 55.3 us -> 44.3 us  [swap(): return lax.ppermute(x, 'dp', [(d, d ^ bit) for d in range(groups)])]
    unnamed x61 -> x93, local copies, waits for them, and re-layouts: 7.32 us -> 14 us
    ppermute x4 -> x6, waiting for transfers between devices: 28.5 us -> 22.9 us  [along(): return lax.ppermute(x, 'tp', [(z, z ^ bit) for z in range(shards)])]
    all_to_all x1 -> x2, waiting for transfers between devices: 3.95 us -> 9.15 us  [local_square(): lax.all_to_all(x, 'tp', 0, 0, tiled=True)]
    all_to_all x1 -> x2, starting transfers between devices: 4.62 us -> 8.69 us  [local_square(): lax.all_to_all(x, 'tp', 0, 0, tiled=True)]
    convert_element_type x4, other arithmetic: 4.26 us -> 7.95 us  [cross(): summed = (after(kept[n], *points)[1] + got_c[n][1]).astype(b16)]
  transfers between devices with their start and end apart: 25 -> 30, of which waited for: 12 -> 11; matrix products, arithmetic and copies ran while one was open for 7% -> 10% of each run, Pallas kernels for 22% -> 29%
where the time goes in v4:
time: 295 us; the launch traced here: 292 us
  waiting for transfers between devices  104 us (35%)
  Pallas kernels  97.1 us (33%)
  starting transfers between devices  45.4 us (15%)
  local copies, waits for them, and re-layouts  22.2 us (8%)
  other arithmetic  20.6 us (7%)
    ppermute x19, waiting for transfers between devices, swap(): return lax.ppermute(x, 'dp', [(d, d ^ bit) for d in range(groups)])  44.3 us
    pallas_call x4, Pallas kernels, return_grad(): pl.pallas_call(kernel, grid=((stop - start) // block,), in_specs=[pl.Bloc...  36.8 us
    pallas_call x4, Pallas kernels, project(): pl.pallas_call(kernel, grid=((stop - start) // block,), in_specs=[pl.Bloc...  34.5 us
    ppermute x3, waiting for transfers between devices, turn(): return lax.ppermute(x, ('tp', 'dp'), pairs)  28 us
    ppermute x6, waiting for transfers between devices, along(): return lax.ppermute(x, 'tp', [(z, z ^ bit) for z in range(shards)])  22.9 us
    ppermute x6, starting transfers between devices, along(): return lax.ppermute(x, 'tp', [(z, z ^ bit) for z in range(shards)])  15.3 us
    unnamed x93, local copies, waits for them, and re-layouts  14 us
    pallas_call x2, Pallas kernels, slot_grad(): pl.pallas_call(kernel, grid=(columns // block,), in_specs=[pl.BlockSpec((...  12.6 us
  transfers between devices with their start and end apart: 30, of which 11 were waited for; matrix products, arithmetic and copies ran while one was open for 10% of the time, Pallas kernels for 29%

profile of v4, /device:TPU:2, one launch (start us, length us, event | category | flops | bytes accessed | tf_op | source)
XLA Modules:
  0.0 292.4 jit_solution(1945611007343324602)
XLA Ops:
  0.7 1.7 copy-done.16
  4.4 1.5 choose.1
  6.5 4.5 %collective-permute-start = (bf16[128,2048]{1,0:T(8,128)(2,1)}, bf16[128,2048]{1,0:T(8,128)(2,1)S(1)}, u32[]{:S(2)}, u32[]{:S(2)}) collective-permute-start(bf16[128,2048]{1,0:T(8,128)(2,1)} %refs_0_.5), channel_id=1, source_target_pairs={{0,0},{4,5},{8,10},{12,15},{1,4},{5,1},{9,14},{13,11},{2,8},{6,13}... | collective-permute-start | bytes 1572872 | tf_op jit(solution)/shard_map/ppermute | solution.py:313
  11.1 2.1 collective-permute-start.2
  13.2 21.9 %collective-permute-done = bf16[128,2048]{1,0:T(8,128)(2,1)S(1)} collective-permute-done((bf16[128,2048]{1,0:T(8,128)(2,1)}, bf16[128,2048]{1,0:T(8,128)(2,1)S(1)}, u32[]{:S(2)}, u32[]{:S(2)}) %collective-permute-start) | collective-permute-done | bytes 524320 | tf_op jit(solution)/shard_map/ppermute | solution.py:313
  35.1 24.3 %collective-permute-done.2 = bf16[64,2048]{1,0:T(8,128)(2,1)S(1)} collective-permute-done((bf16[64,2048]{1,0:T(8,128)(2,1)S(1)}, bf16[64,2048]{1,0:T(8,128)(2,1)S(1)}, u32[]{:S(2)}, u32[]{:S(2)}) %collective-permute-start.2) | collective-permute-done | bytes 262176 | tf_op jit(solution)/shard_map/ppermute | solution.py:304
  59.9 9.6 %return_grad.4 = (f32[256,1024]{1,0:T(8,128)S(1)}, bf16[512,2048]{1,0:T(8,128)(2,1)}) custom-call(bf16[128,7168]{1,0:T(8,128)(2,1)S(1)} %copy-done, bf16[128,7168]{1,0:T(8,128)(2,1)S(1)} %collective-permute-done.4.b_ref.refs_3_.refs_1_, bf16[2048,7168]{1,0:T(8,128)(2,1)} %w_ref.15), custom_call_target="tpu_custom_call" | custom-call | flops 14680064 | bytes 71680 | tf_op jit(solution)/shard_map/return_grad/pallas_call | solution.py:88
  69.5 1.0 copy-done.29
  70.5 12.2 %collective-permute-start.5 = (bf16[128,2048]{1,0:T(8,128)(2,1)S(1)}, bf16[128,2048]{1,0:T(8,128)(2,1)S(1)}, u32[]{:S(2)}, u32[]{:S(2)}) collective-permute-start(bf16[128,2048]{1,0:T(8,128)(2,1)S(1)} %collective-permute-done), channel_id=1, source_target_pairs={{0,8},{4,12},{8,0},{12,4},{1,9},{5,13},{9,1},{13,5},{2,10},{6,14},... | collective-permute-start | bytes 1572872 | tf_op jit(solution)/shard_map/ppermute | solution.py:307
  83.9 9.0 %return_grad.5 = (f32[256,1024]{1,0:T(8,128)S(1)}, bf16[512,2048]{1,0:T(8,128)(2,1)}) custom-call(bf16[128,7168]{1,0:T(8,128)(2,1)S(1)} %copy-done, bf16[128,7168]{1,0:T(8,128)(2,1)S(1)} %collective-permute-done.4.b_ref.refs_3_.refs_1_, bf16[2048,7168]{1,0:T(8,128)(2,1)} %w_ref.15, ...), custom_call_target="tpu_custom_call", output_to_operand_aliasing={{1}: (3, {})} | custom-call | flops 14680064 | bytes 71680 | tf_op jit(solution)/shard_map/return_grad/pallas_call | solution.py:88
  92.9 1.0 copy-done.31
  93.9 11.5 %collective-permute-done.6 = f32[64,128]{1,0:T(8,128)S(1)} collective-permute-done((f32[64,128]{1,0:T(8,128)S(1)}, f32[64,128]{1,0:T(8,128)S(1)}, u32[]{:S(2)}, u32[]{:S(2)}) %collective-permute-start.6) | collective-permute-done | bytes 32800 | tf_op jit(solution)/shard_map/ppermute | solution.py:307
  105.4 4.3 %rank_back.2 = f32[64,256]{1,0:T(8,128)S(1)} custom-call(s32[9]{0:T(128)S(1)} %get-tuple-element.64.facts_ref, bf16[8,64,7168]{2,1,0:T(8,128)(2,1)} %refs_1_.2, bf16[8,64,7168]{2,1,0:T(8,128)(2,1)} %refs_1_.2, bf16[128,7168]{1,0:T(8,128)(2,1)S(1)} %copy-done, bf16[128,7168]{1,0:T(8,128)(2,1)S(1)} %collective-permute-done.4.b_ref.refs_3_.refs_1_), custom_call_target="tpu_custom_call" | custom-call | flops 1835008 | bytes 21504 | tf_op jit(solution)/shard_map/rank_back/pallas_call | solution.py:145
  110.6 2.5 collective-permute-start.8
  113.1 4.9 %collective-permute-start.9 = (bf16[64,2048]{1,0:T(8,128)(2,1)S(1)}, bf16[64,2048]{1,0:T(8,128)(2,1)S(1)}, u32[]{:S(2)}, u32[]{:S(2)}) collective-permute-start(bf16[64,2048]{1,0:T(8,128)(2,1)S(1)} %fusion.21), channel_id=1, source_target_pairs={{0,0},{4,5},{8,10},{12,15},{1,4},{5,1},{9,14},{13,11},{2,8},{6,13}... | collective-permute-start | bytes 786440 | tf_op jit(solution)/shard_map/ppermute | solution.py:313
  118.0 4.4 %rank_back.3 = f32[64,256]{1,0:T(8,128)S(1)} custom-call(s32[9]{0:T(128)S(1)} %get-tuple-element.64.facts_ref, bf16[8,64,7168]{2,1,0:T(8,128)(2,1)} %refs_1_.2, bf16[8,64,7168]{2,1,0:T(8,128)(2,1)} %refs_1_.2, bf16[128,7168]{1,0:T(8,128)(2,1)S(1)} %collective-permute-done.7.refs_2_.a_ref, bf16[128,7168]{1,0:T(8,128)(2,1)S(1)} %collective-permute-done.13.refs_3_.b_ref), custom_call_target="tpu_custom_call" | custom-call | flops 1835008 | bytes 21504 | tf_op jit(solution)/shard_map/rank_back/pallas_call | solution.py:145
  122.6 9.0 %return_grad.6 = (f32[256,1024]{1,0:T(8,128)S(1)}, bf16[512,2048]{1,0:T(8,128)(2,1)}) custom-call(bf16[128,7168]{1,0:T(8,128)(2,1)S(1)} %collective-permute-done.7.refs_2_.a_ref, bf16[128,7168]{1,0:T(8,128)(2,1)S(1)} %collective-permute-done.13.refs_3_.b_ref, bf16[2048,7168]{1,0:T(8,128)(2,1)} %w_ref.15, ...), custom_call_target="tpu_custom_call", output_to_operand_aliasing={{1}: (3, {})} | custom-call | flops 14680064 | bytes 71680 | tf_op jit(solution)/shard_map/return_grad/pallas_call | solution.py:88
  131.6 1.0 copy-done.33
  132.6 11.4 %collective-permute-done.14 = f32[64,512]{1,0:T(8,128)S(1)} collective-permute-done((f32[64,512]{1,0:T(8,128)S(1)}, f32[64,512]{1,0:T(8,128)S(1)}, u32[]{:S(2)}, u32[]{:S(2)}) %collective-permute-start.14) | collective-permute-done | bytes 131104 | tf_op jit(solution)/shard_map/ppermute | solution.py:307
  144.0 2.3 collective-permute-start.15
  146.3 9.2 %return_grad.7 = (f32[256,1024]{1,0:T(8,128)S(1)}, bf16[512,2048]{1,0:T(8,128)(2,1)}) custom-call(bf16[128,7168]{1,0:T(8,128)(2,1)S(1)} %collective-permute-done.7.refs_2_.a_ref, bf16[128,7168]{1,0:T(8,128)(2,1)S(1)} %collective-permute-done.13.refs_3_.b_ref, bf16[2048,7168]{1,0:T(8,128)(2,1)} %w_ref.15, ...), custom_call_target="tpu_custom_call", output_to_operand_aliasing={{1}: (3, {})} | custom-call | flops 14680064 | bytes 71680 | tf_op jit(solution)/shard_map/return_grad/pallas_call | solution.py:88
  155.6 1.0 copy-done.35
  156.6 1.6 spread.2
  158.2 0.9 copy-done.27
  159.1 1.4 spread.3
  160.5 0.8 copy-done.25
  161.3 9.7 %project.4 = (f32[2,128,2048]{2,1,0:T(8,128)S(1)}, f32[2,128,2048]{2,1,0:T(8,128)}) custom-call(s32[9]{0:T(128)S(1)} %get-tuple-element.64.facts_ref, bf16[2,128,2048]{2,1,0:T(8,128)(2,1)S(1)} %pad_maximum_fusion.1.near_ref, bf16[2,128,2048]{2,1,0:T(8,128)(2,1)S(1)} %collective-permute-done.10.far_ref, bf16[512,512]{1,0:T(8,128)(2,1)S(1)} %get-tuple-element.94.wide_ref, ...), custom_call_target="tpu_custom_call" | custom-call | flops 20971520 | bytes 57344 | tf_op jit(solution)/shard_map/project/pallas_call | solution.py:49
  171.6 1.6 fusion.24
  173.2 4.4 %all-to-all-start = ((bf16[4,128,1024]{2,1,0:T(8,128)(2,1)}), bf16[4,128,1024]{2,1,0:T(8,128)(2,1)}, u32[]{:S(2)}, u32[]{:S(2)}) async-start(bf16[4,128,1024]{2,1,0:T(8,128)(2,1)} %get-tuple-element.125), calls=%async_computation | async-start | bytes 2097152 | tf_op jit(solution)/shard_map/all_to_all | solution.py:350
  177.7 1.2 copy-done.7
  178.9 7.8 %project.5 = (f32[2,128,1536]{2,1,0:T(8,128)S(1)}, f32[2,128,1536]{2,1,0:T(8,128)}) custom-call(s32[9]{0:T(128)S(1)} %get-tuple-element.64.facts_ref, bf16[2,128,2048]{2,1,0:T(8,128)(2,1)S(1)} %pad_maximum_fusion.1.near_ref, bf16[2,128,2048]{2,1,0:T(8,128)(2,1)S(1)} %copy-done.7, bf16[512,512]{1,0:T(8,128)(2,1)S(1)} %get-tuple-element.94.wide_ref, ...), custom_call_target="tpu_custom_call" | custom-call | flops 15728640 | bytes 43008 | tf_op jit(solution)/shard_map/project/pallas_call | solution.py:49
  186.8 1.2 pad_maximum_fusion.2
  188.3 4.5 %collective-permute-done.17 = bf16[64,512]{1,0:T(8,128)(2,1)} collective-permute-done((bf16[64,512]{1,0:T(8,128)(2,1)S(1)}, bf16[64,512]{1,0:T(8,128)(2,1)}, u32[]{:S(2)}, u32[]{:S(2)}) %collective-permute-start.17) | collective-permute-done | bytes 65568 | tf_op jit(solution)/shard_map/ppermute | solution.py:304
  192.8 0.8 fusion.26
  194.2 2.5 fusion.17
  196.6 7.1 %all-to-all-done = bf16[4,128,1024]{2,1,0:T(8,128)(2,1)} async-done(((bf16[4,128,1024]{2,1,0:T(8,128)(2,1)}), bf16[4,128,1024]{2,1,0:T(8,128)(2,1)}, u32[]{:S(2)}, u32[]{:S(2)}) %all-to-all-start) | async-done | bytes 1048608 | tf_op jit(solution)/shard_map/all_to_all | solution.py:350
  203.8 1.2 copy-done.8
  205.0 9.5 %project.6 = (f32[2,128,2048]{2,1,0:T(8,128)S(1)}, f32[2,128,2048]{2,1,0:T(8,128)}) custom-call(s32[9]{0:T(128)S(1)} %get-tuple-element.64.facts_ref, bf16[2,128,2048]{2,1,0:T(8,128)(2,1)S(1)} %pad_maximum_fusion.1.near_ref, bf16[2,128,2048]{2,1,0:T(8,128)(2,1)S(1)} %copy-done.8, bf16[512,512]{1,0:T(8,128)(2,1)S(1)} %get-tuple-element.94.wide_ref, ...), custom_call_target="tpu_custom_call" | custom-call | flops 20971520 | bytes 57344 | tf_op jit(solution)/shard_map/project/pallas_call | solution.py:49
  214.8 1.4 pad_maximum_fusion.3
  216.2 4.3 %all-to-all-start.1 = ((bf16[4,128,1024]{2,1,0:T(8,128)(2,1)}), bf16[4,128,1024]{2,1,0:T(8,128)(2,1)}, u32[]{:S(2)}, u32[]{:S(2)}) async-start(bf16[4,128,1024]{2,1,0:T(8,128)(2,1)} %get-tuple-element.124), calls=%async_computation.1 | async-start | bytes 2097152 | tf_op jit(solution)/shard_map/all_to_all | solution.py:350
  220.4 2.3 fusion.19
  222.7 6.7 %collective-permute-done.21 = bf16[128,2048]{1,0:T(8,128)(2,1)} collective-permute-done((bf16[128,2048]{1,0:T(8,128)(2,1)}, bf16[128,2048]{1,0:T(8,128)(2,1)}, u32[]{:S(2)}, u32[]{:S(2)}) %collective-permute-start.21) | collective-permute-done | bytes 524320 | tf_op jit(solution)/shard_map/ppermute | solution.py:304
  229.4 2.7 fusion.7
  232.1 7.6 %project.7 = (f32[2,128,1536]{2,1,0:T(8,128)S(1)}, f32[2,128,1536]{2,1,0:T(8,128)}) custom-call(s32[9]{0:T(128)S(1)} %get-tuple-element.64.facts_ref, bf16[2,128,2048]{2,1,0:T(8,128)(2,1)S(1)} %pad_maximum_fusion.1.near_ref, bf16[2,128,2048]{2,1,0:T(8,128)(2,1)S(1)} %copy-done.9, bf16[512,512]{1,0:T(8,128)(2,1)S(1)} %get-tuple-element.94.wide_ref, ...), custom_call_target="tpu_custom_call" | custom-call | flops 15728640 | bytes 43008 | tf_op jit(solution)/shard_map/project/pallas_call | solution.py:49
  239.7 1.2 copy-done.23
  240.9 2.1 fusion.25
  242.9 1.9 dynamic-slice_bitcast_fusion.1
  244.8 2.0 all-to-all-done.1
  246.8 1.3 dynamic-slice_bitcast_fusion
  248.1 1.8 collective-permute-start.23
  249.9 1.8 fusion.18
  252.1 8.3 %collective-permute-done.23 = bf16[128,1536]{1,0:T(8,128)(2,1)S(1)} collective-permute-done((bf16[128,1536]{1,0:T(8,128)(2,1)}, bf16[128,1536]{1,0:T(8,128)(2,1)S(1)}, u32[]{:S(2)}, u32[]{:S(2)}) %collective-permute-start.23) | collective-permute-done | bytes 393248 | tf_op jit(solution)/shard_map/ppermute | solution.py:304
  260.4 1.3 fusion.15
  261.8 3.0 %slot_grad.2 = f32[512,2048]{1,0:T(8,128)} custom-call(bf16[512,512]{1,0:T(8,128)(2,1)S(1)} %copy-done.28, bf16[128,2048]{1,0:T(8,128)(2,1)S(1)} %copy-done.12, bf16[128,2048]{1,0:T(8,128)(2,1)S(1)} %copy-done.20, bf16[128,2048]{1,0:T(8,128)(2,1)S(1)} %copy-done.19, bf16[128,2048]{1,0:T(8,128)(2,1)S(1)} %get-tuple-element.132.refs_3_), custom_call_target="tpu_custom_call" | custom-call | flops 4194304 | bytes 24576 | tf_op jit(solution)/shard_map/slot_grad/pallas_call | solution.py:204
  264.8 1.4 fusion.20
  266.2 1.8 collective-permute-start.26
  268.0 1.1 fusion
  269.2 1.9 collective-permute-start.27
  271.1 9.6 %slot_grad.3 = f32[512,7168]{1,0:T(8,128)} custom-call(bf16[512,512]{1,0:T(8,128)(2,1)S(1)} %copy-done.26, bf16[128,7168]{1,0:T(8,128)(2,1)S(1)} %copy-done, bf16[128,7168]{1,0:T(8,128)(2,1)S(1)} %copy-done.2, bf16[128,7168]{1,0:T(8,128)(2,1)S(1)} %copy-done.4, bf16[128,7168]{1,0:T(8,128)(2,1)} %copy-done.5), custom_call_target="tpu_custom_call" | custom-call | flops 14680064 | bytes 86016 | tf_op jit(solution)/shard_map/slot_grad/pallas_call | solution.py:204
  280.7 1.5 fusion.3
  282.8 1.3 fusion.11
  284.1 1.4 pad_maximum_fusion
  285.5 6.1 %collective-permute-done.27 = bf16[128,2048]{1,0:T(8,128)(2,1)S(1)} collective-permute-done((bf16[128,2048]{1,0:T(8,128)(2,1)S(1)}, bf16[128,2048]{1,0:T(8,128)(2,1)S(1)}, u32[]{:S(2)}, u32[]{:S(2)}) %collective-permute-start.27) | collective-permute-done | bytes 524320 | tf_op jit(solution)/shard_map/ppermute | solution.py:313
  291.6 0.8 copy.19
  (138 shorter events, 8.4 us)
Async XLA Ops:
  0.6 5.4 %copy-start = (bf16[128,7168]{1,0:T(8,128)(2,1)S(1)}, bf16[128,7168]{1,0:T(8,128)(2,1)}, u32[]{:S(2)}) copy-start(bf16[128,7168]{1,0:T(8,128)(2,1)} %refs_0_.6) | copy-start | bytes 5505028
  0.6 58.8 %copy-start.10 = (bf16[128,2048]{1,0:T(8,128)(2,1)S(1)}, bf16[128,2048]{1,0:T(8,128)(2,1)}, u32[]{:S(2)}) copy-start(bf16[128,2048]{1,0:T(8,128)(2,1)} %refs_0_.5) | copy-start | bytes 1572868
  0.7 1.7 copy-start.16
  5.9 5.0 %collective-permute-start.1 = (bf16[128,2048]{1,0:T(8,128)(2,1)S(1)}, bf16[128,2048]{1,0:T(8,128)(2,1)S(1)}, u32[]{:S(2)}, u32[]{:S(2)}) collective-permute-start(bf16[128,2048]{1,0:T(8,128)(2,1)S(1)} %get-tuple-element.66), channel_id=1, source_target_pairs={{0,1},{1,0},{2,3},{3,2},{4,5},{5,4},{6,7},{7,6},{8,9},{9,8},{10,11... | collective-permute-start | bytes 1572872 | tf_op jit(solution)/shard_map/ppermute | solution.py:304
  6.0 53.8 %collective-permute-start.4 = (bf16[128,7168]{1,0:T(8,128)(2,1)S(1)}, bf16[128,7168]{1,0:T(8,128)(2,1)S(1)}, u32[]{:S(2)}, u32[]{:S(2)}) collective-permute-start(bf16[128,7168]{1,0:T(8,128)(2,1)S(1)} %copy-done), channel_id=1, source_target_pairs={{0,1},{1,0},{2,3},{3,2},{4,5},{5,4},{6,7},{7,6},{8,9},{9,8},{10,11... | collective-permute-start | bytes 5505032 | tf_op jit(solution)/shard_map/ppermute | solution.py:304
  6.5 28.6 %collective-permute-start = (bf16[128,2048]{1,0:T(8,128)(2,1)}, bf16[128,2048]{1,0:T(8,128)(2,1)S(1)}, u32[]{:S(2)}, u32[]{:S(2)}) collective-permute-start(bf16[128,2048]{1,0:T(8,128)(2,1)} %refs_0_.5), channel_id=1, source_target_pairs={{0,0},{4,5},{8,10},{12,15},{1,4},{5,1},{9,14},{13,11},{2,8},{6,13}... | collective-permute-start | bytes 1572872 | tf_op jit(solution)/shard_map/ppermute | solution.py:313
  11.0 98.9 %collective-permute-start.7 = (bf16[128,7168]{1,0:T(8,128)(2,1)S(1)}, bf16[128,7168]{1,0:T(8,128)(2,1)S(1)}, u32[]{:S(2)}, u32[]{:S(2)}) collective-permute-start(bf16[128,7168]{1,0:T(8,128)(2,1)S(1)} %copy-done), channel_id=1, source_target_pairs={{0,2},{1,3},{2,0},{3,1},{4,6},{5,7},{6,4},{7,5},{8,10},{9,11},{10,... | collective-permute-start | bytes 5505032 | tf_op jit(solution)/shard_map/ppermute | solution.py:304
  11.1 48.3 %collective-permute-start.2 = (bf16[64,2048]{1,0:T(8,128)(2,1)S(1)}, bf16[64,2048]{1,0:T(8,128)(2,1)S(1)}, u32[]{:S(2)}, u32[]{:S(2)}) collective-permute-start(bf16[64,2048]{1,0:T(8,128)(2,1)S(1)} %slice_add_fusion.8), channel_id=1, source_target_pairs={{0,2},{1,3},{2,0},{3,1},{4,6},{5,7},{6,4},{7,5},{8,10},{9,11},{10,... | collective-permute-start | bytes 786440 | tf_op jit(solution)/shard_map/ppermute | solution.py:304
  59.8 10.7 %collective-permute-start.3 = (f32[64,128]{1,0:T(8,128)S(1)}, f32[64,128]{1,0:T(8,128)S(1)}, u32[]{:S(2)}, u32[]{:S(2)}) collective-permute-start(f32[64,128]{1,0:T(8,128)S(1)} %fusion.28), channel_id=1, source_target_pairs={{0,4},{4,0},{8,12},{12,8},{1,5},{5,1},{9,13},{13,9},{2,6},{6,2},{1... | collective-permute-start | bytes 98312 | tf_op jit(solution)/shard_map/ppermute | solution.py:307
  59.9 45.6 %copy-start.1 = (bf16[128,7168]{1,0:T(8,128)(2,1)}, bf16[128,7168]{1,0:T(8,128)(2,1)S(1)}, u32[]{:S(2)}) copy-start(bf16[128,7168]{1,0:T(8,128)(2,1)S(1)} %collective-permute-done.4.b_ref.refs_3_.refs_1_) | copy-start | bytes 5505028
  70.5 39.2 %collective-permute-start.5 = (bf16[128,2048]{1,0:T(8,128)(2,1)S(1)}, bf16[128,2048]{1,0:T(8,128)(2,1)S(1)}, u32[]{:S(2)}, u32[]{:S(2)}) collective-permute-start(bf16[128,2048]{1,0:T(8,128)(2,1)S(1)} %collective-permute-done), channel_id=1, source_target_pairs={{0,8},{4,12},{8,0},{12,4},{1,9},{5,13},{9,1},{13,5},{2,10},{6,14},... | collective-permute-start | bytes 1572872 | tf_op jit(solution)/shard_map/ppermute | solution.py:307
  83.3 22.2 %collective-permute-start.6 = (f32[64,128]{1,0:T(8,128)S(1)}, f32[64,128]{1,0:T(8,128)S(1)}, u32[]{:S(2)}, u32[]{:S(2)}) collective-permute-start(f32[64,128]{1,0:T(8,128)S(1)} %add.113), channel_id=1, source_target_pairs={{0,8},{4,12},{8,0},{12,4},{1,9},{5,13},{9,1},{13,5},{2,10},{6,14},... | collective-permute-start | bytes 98312 | tf_op jit(solution)/shard_map/ppermute | solution.py:307
  109.9 36.4 %copy-start.3 = (bf16[128,7168]{1,0:T(8,128)(2,1)}, bf16[128,7168]{1,0:T(8,128)(2,1)S(1)}, u32[]{:S(2)}) copy-start(bf16[128,7168]{1,0:T(8,128)(2,1)S(1)} %collective-permute-done.7.refs_2_.a_ref) | copy-start | bytes 5505028
  109.9 8.1 %collective-permute-start.13 = (bf16[128,7168]{1,0:T(8,128)(2,1)S(1)}, bf16[128,7168]{1,0:T(8,128)(2,1)S(1)}, u32[]{:S(2)}, u32[]{:S(2)}) collective-permute-start(bf16[128,7168]{1,0:T(8,128)(2,1)S(1)} %collective-permute-done.7.refs_2_.a_ref), channel_id=1, source_target_pairs={{0,1},{1,0},{2,3},{3,2},{4,5},{5,4},{6,7},{7,6},{8,9},{9,8},{10,11... | collective-permute-start | bytes 5505032 | tf_op jit(solution)/shard_map/ppermute | solution.py:304
  110.0 51.3 %collective-permute-start.10 = (bf16[2,128,2048]{2,1,0:T(8,128)(2,1)S(1)}, bf16[2,128,2048]{2,1,0:T(8,128)(2,1)S(1)}, u32[]{:S(2)}, u32[]{:S(2)}) collective-permute-start(bf16[2,128,2048]{2,1,0:T(8,128)(2,1)S(1)} %pad_maximum_fusion.1.near_ref), channel_id=1, source_target_pairs={{0,4},{4,0},{8,12},{12,8},{1,5},{5,1},{9,13},{13,9},{2,6},{6,2},{1... | collective-permute-start | bytes 3145736 | tf_op jit(solution)/shard_map/ppermute | solution.py:307
  110.6 35.7 %collective-permute-start.8 = (bf16[128,2048]{1,0:T(8,128)(2,1)S(1)}, bf16[128,2048]{1,0:T(8,128)(2,1)S(1)}, u32[]{:S(2)}, u32[]{:S(2)}) collective-permute-start(bf16[128,2048]{1,0:T(8,128)(2,1)S(1)} %copy-done.10), channel_id=1, source_target_pairs={{0,2},{1,3},{2,0},{3,1},{4,6},{5,7},{6,4},{7,5},{8,10},{9,11},{10,... | collective-permute-start | bytes 1572872 | tf_op jit(solution)/shard_map/ppermute | solution.py:304
  113.1 9.5 %collective-permute-start.11 = (bf16[64,128]{1,0:T(8,128)(2,1)S(1)}, bf16[64,128]{1,0:T(8,128)(2,1)S(1)}, u32[]{:S(2)}, u32[]{:S(2)}) collective-permute-start(bf16[64,128]{1,0:T(8,128)(2,1)S(1)} %select_convert_fusion), channel_id=1, source_target_pairs={{0,1},{1,0},{2,3},{3,2},{4,5},{5,4},{6,7},{7,6},{8,9},{9,8},{10,11... | collective-permute-start | bytes 49160 | tf_op jit(solution)/shard_map/ppermute | solution.py:304
  113.1 33.2 %collective-permute-start.9 = (bf16[64,2048]{1,0:T(8,128)(2,1)S(1)}, bf16[64,2048]{1,0:T(8,128)(2,1)S(1)}, u32[]{:S(2)}, u32[]{:S(2)}) collective-permute-start(bf16[64,2048]{1,0:T(8,128)(2,1)S(1)} %fusion.21), channel_id=1, source_target_pairs={{0,0},{4,5},{8,10},{12,15},{1,4},{5,1},{9,14},{13,11},{2,8},{6,13}... | collective-permute-start | bytes 786440 | tf_op jit(solution)/shard_map/ppermute | solution.py:313
  118.0 28.4 %copy-start.5 = (bf16[128,7168]{1,0:T(8,128)(2,1)}, bf16[128,7168]{1,0:T(8,128)(2,1)S(1)}, u32[]{:S(2)}) copy-start(bf16[128,7168]{1,0:T(8,128)(2,1)S(1)} %collective-permute-done.13.refs_3_.b_ref) | copy-start | bytes 5505028
  122.4 21.6 %collective-permute-start.14 = (f32[64,512]{1,0:T(8,128)S(1)}, f32[64,512]{1,0:T(8,128)S(1)}, u32[]{:S(2)}, u32[]{:S(2)}) collective-permute-start(f32[64,512]{1,0:T(8,128)S(1)} %pad_maximum_fusion.4), channel_id=1, source_target_pairs={{0,4},{4,0},{8,12},{12,8},{1,5},{5,1},{9,13},{13,9},{2,6},{6,2},{1... | collective-permute-start | bytes 393224 | tf_op jit(solution)/shard_map/ppermute | solution.py:307
  122.5 23.7 %collective-permute-start.12 = (bf16[64,256]{1,0:T(8,128)(2,1)S(1)}, bf16[64,256]{1,0:T(8,128)(2,1)S(1)}, u32[]{:S(2)}, u32[]{:S(2)}) collective-permute-start(bf16[64,256]{1,0:T(8,128)(2,1)S(1)} %pad_maximum_fusion.6), channel_id=1, source_target_pairs={{0,2},{1,3},{2,0},{3,1},{4,6},{5,7},{6,4},{7,5},{8,10},{9,11},{10,... | collective-permute-start | bytes 98312 | tf_op jit(solution)/shard_map/ppermute | solution.py:304
  144.0 12.6 %collective-permute-start.15 = (f32[64,512]{1,0:T(8,128)S(1)}, f32[64,512]{1,0:T(8,128)S(1)}, u32[]{:S(2)}, u32[]{:S(2)}) collective-permute-start(f32[64,512]{1,0:T(8,128)S(1)} %add.115.refs_0_), channel_id=1, source_target_pairs={{0,8},{4,12},{8,0},{12,4},{1,9},{5,13},{9,1},{13,5},{2,10},{6,14},... | collective-permute-start | bytes 393224 | tf_op jit(solution)/shard_map/ppermute | solution.py:307
  146.3 9.3 %copy-start.44 = (bf16[64,2048]{1,0:T(8,128)(2,1)}, bf16[64,2048]{1,0:T(8,128)(2,1)S(1)}, u32[]{:S(2)}) copy-start(bf16[64,2048]{1,0:T(8,128)(2,1)S(1)} %collective-permute-done.9) | copy-start | bytes 786436
  146.3 9.3 %copy-start.17 = (bf16[128,2048]{1,0:T(8,128)(2,1)}, bf16[128,2048]{1,0:T(8,128)(2,1)S(1)}, u32[]{:S(2)}) copy-start(bf16[128,2048]{1,0:T(8,128)(2,1)S(1)} %collective-permute-done.8.refs_2_) | copy-start | bytes 1572868
  161.3 9.7 %copy-start.6 = (bf16[2,128,2048]{2,1,0:T(8,128)(2,1)}, bf16[2,128,2048]{2,1,0:T(8,128)(2,1)S(1)}, u32[]{:S(2)}) copy-start(bf16[2,128,2048]{2,1,0:T(8,128)(2,1)S(1)} %collective-permute-done.10.far_ref) | copy-start | bytes 3145732
  161.3 10.3 %copy-start.40 = (bf16[512,2048]{1,0:T(8,128)(2,1)S(1)}, bf16[512,2048]{1,0:T(8,128)(2,1)}, u32[]{:S(2)}) copy-start(bf16[512,2048]{1,0:T(8,128)(2,1)} %get-tuple-element.104) | copy-start | bytes 6291460
  171.0 2.2 copy-start.13
  171.0 23.1 %collective-permute-start.18 = (f32[2,128,2048]{2,1,0:T(8,128)}, f32[2,128,2048]{2,1,0:T(8,128)}, u32[]{:S(2)}, u32[]{:S(2)}) collective-permute-start(f32[2,128,2048]{2,1,0:T(8,128)} %get-tuple-element.101), channel_id=1, source_target_pairs={{0,1},{1,0},{2,3},{3,2},{4,5},{5,4},{6,7},{7,6},{8,9},{9,8},{10,11... | collective-permute-start | bytes 6291464 | tf_op jit(solution)/shard_map/ppermute | solution.py:304
  171.1 6.5 %collective-permute-start.16 = (bf16[64,512]{1,0:T(8,128)(2,1)S(1)}, bf16[64,512]{1,0:T(8,128)(2,1)S(1)}, u32[]{:S(2)}, u32[]{:S(2)}) collective-permute-start(bf16[64,512]{1,0:T(8,128)(2,1)S(1)} %get-tuple-element.96), channel_id=1, source_target_pairs={{0,1},{1,0},{2,3},{3,2},{4,5},{5,4},{6,7},{7,6},{8,9},{9,8},{10,11... | collective-permute-start | bytes 196616 | tf_op jit(solution)/shard_map/ppermute | solution.py:304
  173.2 30.6 %all-to-all-start = ((bf16[4,128,1024]{2,1,0:T(8,128)(2,1)}), bf16[4,128,1024]{2,1,0:T(8,128)(2,1)}, u32[]{:S(2)}, u32[]{:S(2)}) async-start(bf16[4,128,1024]{2,1,0:T(8,128)(2,1)} %get-tuple-element.125), calls=%async_computation | async-start | bytes 2097152 | tf_op jit(solution)/shard_map/all_to_all | solution.py:350
  178.9 7.8 %copy-start.11 = (bf16[128,2048]{1,0:T(8,128)(2,1)S(1)}, bf16[128,2048]{1,0:T(8,128)(2,1)}, u32[]{:S(2)}) copy-start(bf16[128,2048]{1,0:T(8,128)(2,1)} %refs_0_.5) | copy-start | bytes 1572868
  178.9 7.8 %copy-start.18 = (bf16[128,2048]{1,0:T(8,128)(2,1)S(1)}, bf16[128,2048]{1,0:T(8,128)(2,1)}, u32[]{:S(2)}) copy-start(bf16[128,2048]{1,0:T(8,128)(2,1)} %copy-done.17) | copy-start | bytes 1572868
  186.7 1.5 copy-start.21
  186.7 33.8 %collective-permute-start.20 = (f32[2,128,1536]{2,1,0:T(8,128)}, f32[2,128,1536]{2,1,0:T(8,128)}, u32[]{:S(2)}, u32[]{:S(2)}) collective-permute-start(f32[2,128,1536]{2,1,0:T(8,128)} %get-tuple-element.108), channel_id=1, source_target_pairs={{0,1},{1,0},{2,3},{3,2},{4,5},{5,4},{6,7},{7,6},{8,9},{9,8},{10,11... | collective-permute-start | bytes 4718600 | tf_op jit(solution)/shard_map/ppermute | solution.py:304
  188.1 8.5 %collective-permute-start.19 = (bf16[256,2048]{1,0:T(8,128)(2,1)}, bf16[256,2048]{1,0:T(8,128)(2,1)}, u32[]{:S(2)}, u32[]{:S(2)}) collective-permute-start(bf16[256,2048]{1,0:T(8,128)(2,1)} %pad_maximum_fusion.2), channel_id=1, source_target_pairs={{0,1},{1,0},{2,3},{3,2},{4,5},{5,4},{6,7},{7,6},{8,9},{9,8},{10,11... | collective-permute-start | bytes 3145736 | tf_op jit(solution)/shard_map/ppermute | solution.py:304
  188.3 4.5 %collective-permute-start.17 = (bf16[64,512]{1,0:T(8,128)(2,1)S(1)}, bf16[64,512]{1,0:T(8,128)(2,1)}, u32[]{:S(2)}, u32[]{:S(2)}) collective-permute-start(bf16[64,512]{1,0:T(8,128)(2,1)S(1)} %maximum_add_fusion), channel_id=1, source_target_pairs={{0,2},{1,3},{2,0},{3,1},{4,6},{5,7},{6,4},{7,5},{8,10},{9,11},{10,... | collective-permute-start | bytes 196616 | tf_op jit(solution)/shard_map/ppermute | solution.py:304
  205.0 9.5 %copy-start.30 = (f32[256,1024]{1,0:T(8,128)S(1)}, f32[256,1024]{1,0:T(8,128)}, u32[]{:S(2)}) copy-start(f32[256,1024]{1,0:T(8,128)} %copy-done.29) | copy-start | bytes 3145732
  205.0 9.5 %copy-start.32 = (f32[256,1024]{1,0:T(8,128)S(1)}, f32[256,1024]{1,0:T(8,128)}, u32[]{:S(2)}) copy-start(f32[256,1024]{1,0:T(8,128)} %copy-done.31) | copy-start | bytes 3145732
  205.0 9.5 %copy-start.34 = (f32[256,1024]{1,0:T(8,128)S(1)}, f32[256,1024]{1,0:T(8,128)}, u32[]{:S(2)}) copy-start(f32[256,1024]{1,0:T(8,128)} %copy-done.33) | copy-start | bytes 3145732
  205.0 9.5 %copy-start.36 = (f32[256,1024]{1,0:T(8,128)S(1)}, f32[256,1024]{1,0:T(8,128)}, u32[]{:S(2)}) copy-start(f32[256,1024]{1,0:T(8,128)} %copy-done.35) | copy-start | bytes 3145732
  214.4 1.7 copy-start.14
  214.5 35.5 %collective-permute-start.22 = (f32[2,128,2048]{2,1,0:T(8,128)}, f32[2,128,2048]{2,1,0:T(8,128)}, u32[]{:S(2)}, u32[]{:S(2)}) collective-permute-start(f32[2,128,2048]{2,1,0:T(8,128)} %get-tuple-element.113), channel_id=1, source_target_pairs={{0,1},{1,0},{2,3},{3,2},{4,5},{5,4},{6,7},{7,6},{8,9},{9,8},{10,11... | collective-permute-start | bytes 6291464 | tf_op jit(solution)/shard_map/ppermute | solution.py:304
  214.7 14.7 %collective-permute-start.21 = (bf16[128,2048]{1,0:T(8,128)(2,1)}, bf16[128,2048]{1,0:T(8,128)(2,1)}, u32[]{:S(2)}, u32[]{:S(2)}) collective-permute-start(bf16[128,2048]{1,0:T(8,128)(2,1)} %fusion.17), channel_id=1, source_target_pairs={{0,2},{1,3},{2,0},{3,1},{4,6},{5,7},{6,4},{7,5},{8,10},{9,11},{10,... | collective-permute-start | bytes 1572872 | tf_op jit(solution)/shard_map/ppermute | solution.py:304
  216.2 30.7 %all-to-all-start.1 = ((bf16[4,128,1024]{2,1,0:T(8,128)(2,1)}), bf16[4,128,1024]{2,1,0:T(8,128)(2,1)}, u32[]{:S(2)}, u32[]{:S(2)}) async-start(bf16[4,128,1024]{2,1,0:T(8,128)(2,1)} %get-tuple-element.124), calls=%async_computation.1 | async-start | bytes 2097152 | tf_op jit(solution)/shard_map/all_to_all | solution.py:350
  220.4 11.6 %copy-start.9 = (bf16[2,128,2048]{2,1,0:T(8,128)(2,1)S(1)}, bf16[2,128,2048]{2,1,0:T(8,128)(2,1)}, u32[]{:S(2)}) copy-start(bf16[2,128,2048]{2,1,0:T(8,128)(2,1)} %copy-done.6) | copy-start | bytes 3145732
  240.8 23.9 %collective-permute-start.24 = (f32[2,128,1536]{2,1,0:T(8,128)}, f32[2,128,1536]{2,1,0:T(8,128)}, u32[]{:S(2)}, u32[]{:S(2)}) collective-permute-start(f32[2,128,1536]{2,1,0:T(8,128)} %get-tuple-element.119), channel_id=1, source_target_pairs={{0,1},{1,0},{2,3},{3,2},{4,5},{5,4},{6,7},{7,6},{8,9},{9,8},{10,11... | collective-permute-start | bytes 4718600 | tf_op jit(solution)/shard_map/ppermute | solution.py:304
  246.8 13.6 %copy-start.22 = (f32[2,128,1536]{2,1,0:T(8,128)S(1)}, f32[2,128,1536]{2,1,0:T(8,128)}, u32[]{:S(2)}) copy-start(f32[2,128,1536]{2,1,0:T(8,128)} %copy-done.21) | copy-start | bytes 4718596
  248.1 12.3 %collective-permute-start.23 = (bf16[128,1536]{1,0:T(8,128)(2,1)}, bf16[128,1536]{1,0:T(8,128)(2,1)S(1)}, u32[]{:S(2)}, u32[]{:S(2)}) collective-permute-start(bf16[128,1536]{1,0:T(8,128)(2,1)} %fusion.19), channel_id=1, source_target_pairs={{0,2},{1,3},{2,0},{3,1},{4,6},{5,7},{6,4},{7,5},{8,10},{9,11},{10,... | collective-permute-start | bytes 1179656 | tf_op jit(solution)/shard_map/ppermute | solution.py:304
  249.9 11.9 %copy-start.12 = (bf16[128,2048]{1,0:T(8,128)(2,1)S(1)}, bf16[128,2048]{1,0:T(8,128)(2,1)}, u32[]{:S(2)}) copy-start(bf16[128,2048]{1,0:T(8,128)(2,1)} %refs_0_.5) | copy-start | bytes 1572868
  249.9 11.9 %copy-start.19 = (bf16[128,2048]{1,0:T(8,128)(2,1)S(1)}, bf16[128,2048]{1,0:T(8,128)(2,1)}, u32[]{:S(2)}) copy-start(bf16[128,2048]{1,0:T(8,128)(2,1)} %copy-done.17) | copy-start | bytes 1572868
  249.9 11.9 %copy-start.20 = (bf16[128,2048]{1,0:T(8,128)(2,1)S(1)}, bf16[128,2048]{1,0:T(8,128)(2,1)}, u32[]{:S(2)}) copy-start(bf16[128,2048]{1,0:T(8,128)(2,1)} %get-tuple-element.133.refs_1_) | copy-start | bytes 1572868
  249.9 11.9 %copy-start.28 = (bf16[512,512]{1,0:T(8,128)(2,1)S(1)}, bf16[512,512]{1,0:T(8,128)(2,1)}, u32[]{:S(2)}) copy-start(bf16[512,512]{1,0:T(8,128)(2,1)} %copy-done.27) | copy-start | bytes 1572868
  251.7 29.0 %collective-permute-start.25 = (bf16[128,2048]{1,0:T(8,128)(2,1)S(1)}, bf16[128,2048]{1,0:T(8,128)(2,1)S(1)}, u32[]{:S(2)}, u32[]{:S(2)}) collective-permute-start(bf16[128,2048]{1,0:T(8,128)(2,1)S(1)} %fusion.18), channel_id=1, source_target_pairs={{0,2},{1,3},{2,0},{3,1},{4,6},{5,7},{6,4},{7,5},{8,10},{9,11},{10,... | collective-permute-start | bytes 1572872 | tf_op jit(solution)/shard_map/ppermute | solution.py:304
  261.8 3.0 %copy-start.24 = (f32[2,128,1536]{2,1,0:T(8,128)S(1)}, f32[2,128,1536]{2,1,0:T(8,128)}, u32[]{:S(2)}) copy-start(f32[2,128,1536]{2,1,0:T(8,128)} %copy-done.23) | copy-start | bytes 4718596
  261.8 6.2 %copy-start.43 = (bf16[128,1024]{1,0:T(8,128)(2,1)S(1)}, bf16[128,1024]{1,0:T(8,128)(2,1)}, u32[]{:S(2)}) copy-start(bf16[128,1024]{1,0:T(8,128)(2,1)} %get-tuple-element.128) | copy-start | bytes 786436
  261.8 6.2 %copy-start.45 = (bf16[64,2048]{1,0:T(8,128)(2,1)S(1)}, bf16[64,2048]{1,0:T(8,128)(2,1)}, u32[]{:S(2)}) copy-start(bf16[64,2048]{1,0:T(8,128)(2,1)} %copy-done.44) | copy-start | bytes 786436
  264.8 3.3 %copy-start.41 = (f32[128,2048]{1,0:T(8,128)S(1)}, f32[128,2048]{1,0:T(8,128)}, u32[]{:S(2)}) copy-start(f32[128,2048]{1,0:T(8,128)} %pad_maximum_fusion.3) | copy-start | bytes 3145732
  264.8 6.3 %copy-start.4 = (bf16[128,7168]{1,0:T(8,128)(2,1)S(1)}, bf16[128,7168]{1,0:T(8,128)(2,1)}, u32[]{:S(2)}) copy-start(bf16[128,7168]{1,0:T(8,128)(2,1)} %copy-done.3) | copy-start | bytes 5505028
  266.2 4.9 %copy-start.2 = (bf16[128,7168]{1,0:T(8,128)(2,1)S(1)}, bf16[128,7168]{1,0:T(8,128)(2,1)}, u32[]{:S(2)}) copy-start(bf16[128,7168]{1,0:T(8,128)(2,1)} %copy-done.1) | copy-start | bytes 5505028
  266.2 4.9 %copy-start.26 = (bf16[512,512]{1,0:T(8,128)(2,1)S(1)}, bf16[512,512]{1,0:T(8,128)(2,1)}, u32[]{:S(2)}) copy-start(bf16[512,512]{1,0:T(8,128)(2,1)} %copy-done.25) | copy-start | bytes 1572868
  266.2 16.5 %collective-permute-start.26 = (bf16[128,1536]{1,0:T(8,128)(2,1)S(1)}, bf16[128,1536]{1,0:T(8,128)(2,1)S(1)}, u32[]{:S(2)}, u32[]{:S(2)}) collective-permute-start(bf16[128,1536]{1,0:T(8,128)(2,1)S(1)} %fusion.20), channel_id=1, source_target_pairs={{0,2},{1,3},{2,0},{3,1},{4,6},{5,7},{6,4},{7,5},{8,10},{9,11},{10,... | collective-permute-start | bytes 1179656 | tf_op jit(solution)/shard_map/ppermute | solution.py:304
  269.2 22.5 %collective-permute-start.27 = (bf16[128,2048]{1,0:T(8,128)(2,1)S(1)}, bf16[128,2048]{1,0:T(8,128)(2,1)S(1)}, u32[]{:S(2)}, u32[]{:S(2)}) collective-permute-start(bf16[128,2048]{1,0:T(8,128)(2,1)S(1)} %fusion), channel_id=1, source_target_pairs={{0,0},{5,4},{10,8},{15,12},{4,1},{1,5},{14,9},{11,13},{8,2},{13,6}... | collective-permute-start | bytes 1572872 | tf_op jit(solution)/shard_map/ppermute | solution.py:313
  271.1 9.6 %copy-start.15 = (f32[2,128,2048]{2,1,0:T(8,128)S(1)}, f32[2,128,2048]{2,1,0:T(8,128)}, u32[]{:S(2)}) copy-start(f32[2,128,2048]{2,1,0:T(8,128)} %copy-done.14) | copy-start | bytes 6291460
  280.7 3.4 %copy-start.42 = (bf16[128,2048]{1,0:T(8,128)(2,1)S(1)}, bf16[128,2048]{1,0:T(8,128)(2,1)}, u32[]{:S(2)}) copy-start(bf16[128,2048]{1,0:T(8,128)(2,1)} %fusion.7) | copy-start | bytes 1572868
  (12 other events, 11.3 us)

commit v5 on v4

--- a/solution.py
+++ b/solution.py
@@ -22,8 +22,8 @@
     return lax.optimization_barrier((x,) + others)[0]
 
 
-def cost(flops, moved):
-    return pl.CostEstimate(flops=flops // 256, bytes_accessed=moved // 256, transcendentals=0)
+def cost(flops, moved, share=16):
+    return pl.CostEstimate(flops=flops // share, bytes_accessed=moved // share, transcendentals=0)
 
 
 def project(facts, near, far, wide, weight, up_flat, start, stop, block):
@@ -61,7 +61,7 @@
         out_shape=[jax.ShapeDtypeStruct((2, rows, stop - start), jnp.float32)] * 2,
         scratch_shapes=[pltpu.VMEM((groups * rows, depth), near.dtype)],
         compiler_params=pltpu.CompilerParams(vmem_limit_bytes=VMEM),
-        cost_estimate=cost(2 * groups * rows * (depth + span) * (stop - start), 2 * (depth + span + 2 * groups * rows) * (stop - start)),
+        cost_estimate=cost(2 * groups * rows * (depth + span) * (stop - start), 2 * (depth + span + 2 * groups * rows) * (stop - start), 1),
         name="project",
     )(facts, near, far, wide, weight, up_flat)
 
@@ -209,7 +209,7 @@
         out_specs=pl.BlockSpec((span, block), lambda n: (0, n)),
         out_shape=jax.ShapeDtypeStruct((span, columns), jnp.float32),
         compiler_params=pltpu.CompilerParams(vmem_limit_bytes=VMEM),
-        cost_estimate=cost(2 * span * groups * rows * columns, (4 * span + 2 * groups * rows) * columns),
+        cost_estimate=cost(2 * span * groups * rows * columns, (4 * span + 2 * groups * rows) * columns, 1),
         name="slot_grad",
     )(wide_t, *blocks)
 
@@ -322,7 +322,7 @@
 
     near = swap(near, CORE)
     down_x = swap(rest[:rank] + near[rank:], CHIP)
-    cot_x = swap(after(cotangent, near), CHIP)
+    cot_x = swap(after(cotangent, down_x), CHIP)
     down_own = rest[rank:] + near[:rank] + down_x
     inner = dot(down_own, after(tokens, turned), (1, 1))
 
@@ -390,13 +390,14 @@
     back_b = share(after(back_b, point), swap(back_b, CHIP), CHIP)
     point = cross(0, back_b)
     point = make(2, point, mixed, parts[0])
+    point = finish(0, point)
     point = cross(1, point)
-    point = finish(0, point)
     point = make(3, point)
+    point = finish(1, point)
     point = cross(2, point)
-    point = finish(1, point)
-    down_wide = slot_grad(after(back_wide, point), toks, 1024)
-    point = cross(3, down_wide)
+    point = cross(3, point)
+    up_wide = slot_grad(after(inner_wide, point), [cotangent, cot_c, cot_x, cot_xc], 1024)
+    point = finish(2, up_wide)
     back_mine = lax.dynamic_slice_in_dim(back_b, j * rows, rows, 1)
     total = after(grad_block(j), point, parts[1])
     for m in range(1, shards):
@@ -405,9 +406,8 @@
         )
     total = (total + dot(back_mine, down_mine, (0, 0))).astype(b16)
     tokens_grad = turn(total, back_again)
-    up_wide = slot_grad(after(inner_wide, total), [cotangent, cot_c, cot_x, cot_xc], 1024)
-    point = finish(2, up_wide)
-    finish(3, point)
+    down_wide = slot_grad(after(back_wide, total), toks, 1024)
+    finish(3, down_wide)
     projected = jnp.concatenate(done, axis=1)
     up_grad = up_wide.reshape(per_owner, rank, hidden)
     down_grad = jnp.swapaxes(down_wide.reshape(per_owner, rank, width), 1, 2)

time: 295 us -> 261 us (0.88)
  waiting for transfers between devices: 104 us -> 79.9 us
  starting transfers between devices: 45.4 us -> 37 us
    ppermute x19, waiting for transfers between devices: 44.3 us -> 5.82 us  [swap(): return lax.ppermute(x, 'dp', [(d, d ^ bit) for d in range(groups)])]
    ppermute x3, waiting for transfers between devices: 28 us -> 38.8 us  [turn(): return lax.ppermute(x, ('tp', 'dp'), pairs)]
    ppermute x6, starting transfers between devices: 15.3 us -> 5.05 us  [along(): return lax.ppermute(x, 'tp', [(z, z ^ bit) for z in range(shards)])]
    ppermute x3, starting transfers between devices: 11.3 us -> 16.3 us  [turn(): return lax.ppermute(x, ('tp', 'dp'), pairs)]
    ppermute x19, starting transfers between devices: 10.1 us -> 6.97 us  [swap(): return lax.ppermute(x, 'dp', [(d, d ^ bit) for d in range(groups)])]
    unnamed x93 -> x89, local copies, waits for them, and re-layouts: 14 us -> 15.1 us
  transfers between devices with their start and end apart: 30 -> 30, of which waited for: 11 -> 8; matrix products, arithmetic and copies ran while one was open for 10% -> 11% of each run, Pallas kernels for 29% -> 33%
where the time goes in v5:
time: 261 us; the launch traced here: 259 us
  Pallas kernels  96.9 us (37%)
  waiting for transfers between devices  79.9 us (31%)
  starting transfers between devices  37 us (14%)
  other arithmetic  22 us (8%)
  local copies, waits for them, and re-layouts  21.7 us (8%)
    ppermute x3, waiting for transfers between devices, turn(): return lax.ppermute(x, ('tp', 'dp'), pairs)  38.8 us
    pallas_call x4, Pallas kernels, return_grad(): pl.pallas_call(kernel, grid=((stop - start) // block,), in_specs=[pl.Bloc...  36.7 us
    pallas_call x4, Pallas kernels, project(): pl.pallas_call(kernel, grid=((stop - start) // block,), in_specs=[pl.Bloc...  34.5 us
    ppermute x6, waiting for transfers between devices, along(): return lax.ppermute(x, 'tp', [(z, z ^ bit) for z in range(shards)])  23.8 us
    ppermute x3, starting transfers between devices, turn(): return lax.ppermute(x, ('tp', 'dp'), pairs)  16.3 us
    unnamed x89, local copies, waits for them, and re-layouts  15.1 us
    pallas_call x2, Pallas kernels, slot_grad(): pl.pallas_call(kernel, grid=(columns // block,), in_specs=[pl.BlockSpec((...  12.4 us
    all_to_all x2, waiting for transfers between devices, local_square(): lax.all_to_all(x, 'tp', 0, 0, tiled=True)  11.4 us
  transfers between devices with their start and end apart: 30, of which 8 were waited for; matrix products, arithmetic and copies ran while one was open for 11% of the time, Pallas kernels for 33%

profile of v5, /device:TPU:2, one launch (start us, length us, event | category | flops | bytes accessed | tf_op | source)
XLA Modules:
  0.0 259.4 jit_solution(2840487413632122532)
XLA Ops:
  0.7 1.7 copy-done.17
  2.5 0.7 copy-done.33
  3.1 0.7 copy-done.34
  3.8 0.7 copy-done.35
  4.4 1.5 choose.1
  6.5 1.4 collective-permute-done.1
  8.0 5.9 %collective-permute-start = (bf16[128,2048]{1,0:T(8,128)(2,1)S(1)}, bf16[128,2048]{1,0:T(8,128)(2,1)S(1)}, u32[]{:S(2)}, u32[]{:S(2)}) collective-permute-start(bf16[128,2048]{1,0:T(8,128)(2,1)S(1)} %copy-done.9), channel_id=1, source_target_pairs={{0,0},{4,5},{8,10},{12,15},{1,4},{5,1},{9,14},{13,11},{2,8},{6,13}... | collective-permute-start | bytes 1572872 | tf_op jit(solution)/shard_map/ppermute | solution.py:313
  14.0 2.4 collective-permute-done.2
  16.7 20.3 %collective-permute-done = bf16[128,2048]{1,0:T(8,128)(2,1)S(1)} collective-permute-done((bf16[128,2048]{1,0:T(8,128)(2,1)S(1)}, bf16[128,2048]{1,0:T(8,128)(2,1)S(1)}, u32[]{:S(2)}, u32[]{:S(2)}) %collective-permute-start) | collective-permute-done | bytes 524320 | tf_op jit(solution)/shard_map/ppermute | solution.py:313
  37.8 9.6 %return_grad.4 = (f32[256,1024]{1,0:T(8,128)S(1)}, bf16[512,2048]{1,0:T(8,128)(2,1)}) custom-call(bf16[128,7168]{1,0:T(8,128)(2,1)S(1)} %copy-done, bf16[128,7168]{1,0:T(8,128)(2,1)S(1)} %collective-permute-done.4.b_ref.refs_3_.refs_1_, bf16[2048,7168]{1,0:T(8,128)(2,1)} %w_ref.15), custom_call_target="tpu_custom_call" | custom-call | flops 234881024 | bytes 1146880 | tf_op jit(solution)/shard_map/return_grad/pallas_call | solution.py:88
  47.4 1.0 copy-done.29
  49.0 2.9 %collective-permute-start.6 = (f32[64,128]{1,0:T(8,128)S(1)}, f32[64,128]{1,0:T(8,128)S(1)}, u32[]{:S(2)}, u32[]{:S(2)}) collective-permute-start(f32[64,128]{1,0:T(8,128)S(1)} %add.113), channel_id=1, source_target_pairs={{0,8},{4,12},{8,0},{12,4},{1,9},{5,13},{9,1},{13,5},{2,10},{6,14},... | collective-permute-start | bytes 98312 | tf_op jit(solution)/shard_map/ppermute | solution.py:307
  51.9 0.6 iota_compare_fusion
  52.6 9.0 %return_grad.5 = (f32[256,1024]{1,0:T(8,128)S(1)}, bf16[512,2048]{1,0:T(8,128)(2,1)}) custom-call(bf16[128,7168]{1,0:T(8,128)(2,1)S(1)} %copy-done, bf16[128,7168]{1,0:T(8,128)(2,1)S(1)} %collective-permute-done.4.b_ref.refs_3_.refs_1_, bf16[2048,7168]{1,0:T(8,128)(2,1)} %w_ref.15, ...), custom_call_target="tpu_custom_call", output_to_operand_aliasing={{1}: (3, {})} | custom-call | flops 234881024 | bytes 1146880 | tf_op jit(solution)/shard_map/return_grad/pallas_call | solution.py:88
  61.6 1.0 copy-done.30
  62.5 10.9 %collective-permute-done.6 = f32[64,128]{1,0:T(8,128)S(1)} collective-permute-done((f32[64,128]{1,0:T(8,128)S(1)}, f32[64,128]{1,0:T(8,128)S(1)}, u32[]{:S(2)}, u32[]{:S(2)}) %collective-permute-start.6) | collective-permute-done | bytes 32800 | tf_op jit(solution)/shard_map/ppermute | solution.py:307
  73.5 4.3 %rank_back.2 = f32[64,256]{1,0:T(8,128)S(1)} custom-call(s32[9]{0:T(128)S(1)} %get-tuple-element.64.facts_ref, bf16[8,64,7168]{2,1,0:T(8,128)(2,1)} %refs_1_.2, bf16[8,64,7168]{2,1,0:T(8,128)(2,1)} %refs_1_.2, bf16[128,7168]{1,0:T(8,128)(2,1)S(1)} %copy-done, bf16[128,7168]{1,0:T(8,128)(2,1)S(1)} %collective-permute-done.4.b_ref.refs_3_.refs_1_), custom_call_target="tpu_custom_call" | custom-call | flops 29360128 | bytes 344064 | tf_op jit(solution)/shard_map/rank_back/pallas_call | solution.py:145
  78.5 5.9 %collective-permute-start.9 = (bf16[64,2048]{1,0:T(8,128)(2,1)S(1)}, bf16[64,2048]{1,0:T(8,128)(2,1)S(1)}, u32[]{:S(2)}, u32[]{:S(2)}) collective-permute-start(bf16[64,2048]{1,0:T(8,128)(2,1)S(1)} %fusion.21), channel_id=1, source_target_pairs={{0,0},{4,5},{8,10},{12,15},{1,4},{5,1},{9,14},{13,11},{2,8},{6,13}... | collective-permute-start | bytes 786440 | tf_op jit(solution)/shard_map/ppermute | solution.py:313
  84.4 4.3 %rank_back.3 = f32[64,256]{1,0:T(8,128)S(1)} custom-call(s32[9]{0:T(128)S(1)} %get-tuple-element.64.facts_ref, bf16[8,64,7168]{2,1,0:T(8,128)(2,1)} %refs_1_.2, bf16[8,64,7168]{2,1,0:T(8,128)(2,1)} %refs_1_.2, bf16[128,7168]{1,0:T(8,128)(2,1)S(1)} %collective-permute-done.7.refs_2_.a_ref, bf16[128,7168]{1,0:T(8,128)(2,1)S(1)} %collective-permute-done.13.refs_3_.b_ref), custom_call_target="tpu_custom_call" | custom-call | flops 29360128 | bytes 344064 | tf_op jit(solution)/shard_map/rank_back/pallas_call | solution.py:145
  89.1 9.0 %return_grad.6 = (f32[256,1024]{1,0:T(8,128)S(1)}, bf16[512,2048]{1,0:T(8,128)(2,1)}) custom-call(bf16[128,7168]{1,0:T(8,128)(2,1)S(1)} %collective-permute-done.7.refs_2_.a_ref, bf16[128,7168]{1,0:T(8,128)(2,1)S(1)} %collective-permute-done.13.refs_3_.b_ref, bf16[2048,7168]{1,0:T(8,128)(2,1)} %w_ref.15, ...), custom_call_target="tpu_custom_call", output_to_operand_aliasing={{1}: (3, {})} | custom-call | flops 234881024 | bytes 1146880 | tf_op jit(solution)/shard_map/return_grad/pallas_call | solution.py:88
  98.1 1.0 copy-done.31
  99.1 12.9 %collective-permute-done.14 = f32[64,512]{1,0:T(8,128)S(1)} collective-permute-done((f32[64,512]{1,0:T(8,128)S(1)}, f32[64,512]{1,0:T(8,128)S(1)}, u32[]{:S(2)}, u32[]{:S(2)}) %collective-permute-start.14) | collective-permute-done | bytes 131104 | tf_op jit(solution)/shard_map/ppermute | solution.py:307
  112.0 1.3 collective-permute-start.15
  113.4 9.2 %return_grad.7 = (f32[256,1024]{1,0:T(8,128)S(1)}, bf16[512,2048]{1,0:T(8,128)(2,1)}) custom-call(bf16[128,7168]{1,0:T(8,128)(2,1)S(1)} %collective-permute-done.7.refs_2_.a_ref, bf16[128,7168]{1,0:T(8,128)(2,1)S(1)} %collective-permute-done.13.refs_3_.b_ref, bf16[2048,7168]{1,0:T(8,128)(2,1)} %w_ref.15, ...), custom_call_target="tpu_custom_call", output_to_operand_aliasing={{1}: (3, {})} | custom-call | flops 234881024 | bytes 1146880 | tf_op jit(solution)/shard_map/return_grad/pallas_call | solution.py:88
  122.6 1.0 copy-done.32
  123.5 1.6 spread.2
  125.2 0.8 copy-done.27
  126.0 1.4 spread.3
  127.4 0.8 copy-done.25
  128.2 9.7 %project.4 = (f32[2,128,2048]{2,1,0:T(8,128)S(1)}, f32[2,128,2048]{2,1,0:T(8,128)}) custom-call(s32[9]{0:T(128)S(1)} %get-tuple-element.64.facts_ref, bf16[2,128,2048]{2,1,0:T(8,128)(2,1)S(1)} %pad_maximum_fusion.1.near_ref, bf16[2,128,2048]{2,1,0:T(8,128)(2,1)S(1)} %collective-permute-done.10.far_ref, bf16[512,512]{1,0:T(8,128)(2,1)S(1)} %get-tuple-element.94.wide_ref, ...), custom_call_target="tpu_custom_call" | custom-call | flops 5368709120 | bytes 14680064 | tf_op jit(solution)/shard_map/project/pallas_call | solution.py:49
  137.9 1.3 copy-done.12
  139.2 2.8 %dynamic-slice_select_fusion = (f32[128,1024]{1,0:T(8,128)}, f32[128,1024]{1,0:T(8,128)}) fusion(f32[256,1024]{1,0:T(8,128)} %copy-done.32, s32[]{:T(128)S(6)} %select_n.40, f32[256,1024]{1,0:T(8,128)} %copy-done.30, pred[]{:T(512)S(6)} %lt.35, f32[256,1024]{1,0:T(8,128)} %copy-done.31, f32[256,1024]{1,0:T(8,128)} %copy-done.29), kind=kLoop, calls=%fused_computation.32 | loop fusion | flops 262144 | bytes 3145733 | tf_op jit(solution)/shard_map/jit(_where)/select_n | solution.py:361
  142.6 1.1 pad_maximum_fusion.2
  143.7 1.5 fusion.24
  145.2 4.2 %all-to-all-start = ((bf16[4,128,1024]{2,1,0:T(8,128)(2,1)}), bf16[4,128,1024]{2,1,0:T(8,128)(2,1)}, u32[]{:S(2)}, u32[]{:S(2)}) async-start(bf16[4,128,1024]{2,1,0:T(8,128)(2,1)} %get-tuple-element.125), calls=%async_computation | async-start | bytes 2097152 | tf_op jit(solution)/shard_map/all_to_all | solution.py:350
  149.6 1.2 copy-done.7
  150.8 7.8 %project.5 = (f32[2,128,1536]{2,1,0:T(8,128)S(1)}, f32[2,128,1536]{2,1,0:T(8,128)}) custom-call(s32[9]{0:T(128)S(1)} %get-tuple-element.64.facts_ref, bf16[2,128,2048]{2,1,0:T(8,128)(2,1)S(1)} %pad_maximum_fusion.1.near_ref, bf16[2,128,2048]{2,1,0:T(8,128)(2,1)S(1)} %copy-done.7, bf16[512,512]{1,0:T(8,128)(2,1)S(1)} %get-tuple-element.94.wide_ref, ...), custom_call_target="tpu_custom_call" | custom-call | flops 4026531840 | bytes 11010048 | tf_op jit(solution)/shard_map/project/pallas_call | solution.py:49
  159.2 2.4 fusion.17
  161.6 2.0 collective-permute-start.20
  163.6 1.1 pad_maximum_fusion.3
  164.7 11.4 %all-to-all-done = bf16[4,128,1024]{2,1,0:T(8,128)(2,1)} async-done(((bf16[4,128,1024]{2,1,0:T(8,128)(2,1)}), bf16[4,128,1024]{2,1,0:T(8,128)(2,1)}, u32[]{:S(2)}, u32[]{:S(2)}) %all-to-all-start) | async-done | bytes 1048608 | tf_op jit(solution)/shard_map/all_to_all | solution.py:350
  176.2 4.4 %all-to-all-start.1 = ((bf16[4,128,1024]{2,1,0:T(8,128)(2,1)}), bf16[4,128,1024]{2,1,0:T(8,128)(2,1)}, u32[]{:S(2)}, u32[]{:S(2)}) async-start(bf16[4,128,1024]{2,1,0:T(8,128)(2,1)} %get-tuple-element.124), calls=%async_computation.1 | async-start | bytes 2097152 | tf_op jit(solution)/shard_map/all_to_all | solution.py:350
  180.6 1.2 copy-done.8
  181.8 9.4 %project.6 = (f32[2,128,2048]{2,1,0:T(8,128)S(1)}, f32[2,128,2048]{2,1,0:T(8,128)}) custom-call(s32[9]{0:T(128)S(1)} %get-tuple-element.64.facts_ref, bf16[2,128,2048]{2,1,0:T(8,128)(2,1)S(1)} %pad_maximum_fusion.1.near_ref, bf16[2,128,2048]{2,1,0:T(8,128)(2,1)S(1)} %copy-done.8, bf16[512,512]{1,0:T(8,128)(2,1)S(1)} %get-tuple-element.94.wide_ref, ...), custom_call_target="tpu_custom_call" | custom-call | flops 5368709120 | bytes 14680064 | tf_op jit(solution)/shard_map/project/pallas_call | solution.py:49
  191.3 3.1 %fusion.7 = bf16[128,2048]{1,0:T(8,128)(2,1)} fusion(f32[2,128,2048]{2,1,0:T(8,128)} %collective-permute-done.18, bf16[128,2048]{1,0:T(8,128)(2,1)} %collective-permute-done.20, f32[2,128,2048]{2,1,0:T(8,128)S(1)} %copy-done.14), kind=kLoop, calls=%fused_computation.12 | loop fusion | flops 1048576 | bytes 3145728 | tf_op jit(solution)/shard_map/convert_element_type | solution.py:384
  194.4 2.0 fusion.19
  196.4 7.7 %project.7 = (f32[2,128,1536]{2,1,0:T(8,128)S(1)}, f32[2,128,1536]{2,1,0:T(8,128)}) custom-call(s32[9]{0:T(128)S(1)} %get-tuple-element.64.facts_ref, bf16[2,128,2048]{2,1,0:T(8,128)(2,1)S(1)} %pad_maximum_fusion.1.near_ref, bf16[2,128,2048]{2,1,0:T(8,128)(2,1)S(1)} %copy-done.8, bf16[512,512]{1,0:T(8,128)(2,1)S(1)} %get-tuple-element.94.wide_ref, ...), custom_call_target="tpu_custom_call" | custom-call | flops 4026531840 | bytes 11010048 | tf_op jit(solution)/shard_map/project/pallas_call | solution.py:49
  204.0 1.2 copy-done.23
  205.3 1.3 fusion.25
  206.6 1.9 dynamic-slice_bitcast_fusion.1
  208.5 1.3 dynamic-slice_bitcast_fusion
  209.8 1.7 fusion.15
  211.6 1.5 fusion.18
  213.1 1.9 collective-permute-start.25
  215.1 1.2 fusion.20
  216.5 9.5 %slot_grad.2 = f32[512,7168]{1,0:T(8,128)} custom-call(bf16[512,512]{1,0:T(8,128)(2,1)S(1)} %copy-done.26, bf16[128,7168]{1,0:T(8,128)(2,1)S(1)} %copy-done, bf16[128,7168]{1,0:T(8,128)(2,1)S(1)} %copy-done.2, bf16[128,7168]{1,0:T(8,128)(2,1)S(1)} %copy-done.4, bf16[128,7168]{1,0:T(8,128)(2,1)} %copy-done.5), custom_call_target="tpu_custom_call" | custom-call | flops 3758096384 | bytes 22020096 | tf_op jit(solution)/shard_map/slot_grad/pallas_call | solution.py:204
  226.0 2.0 collective-permute-done.25
  228.0 1.4 fusion.3
  229.9 4.5 %collective-permute-start.27 = (bf16[128,2048]{1,0:T(8,128)(2,1)S(1)}, bf16[128,2048]{1,0:T(8,128)(2,1)S(1)}, u32[]{:S(2)}, u32[]{:S(2)}) collective-permute-start(bf16[128,2048]{1,0:T(8,128)(2,1)S(1)} %fusion), channel_id=1, source_target_pairs={{0,0},{5,4},{10,8},{15,12},{4,1},{1,5},{14,9},{11,13},{8,2},{13,6}... | collective-permute-start | bytes 1572872 | tf_op jit(solution)/shard_map/ppermute | solution.py:313
  234.4 2.9 %slot_grad.3 = f32[512,2048]{1,0:T(8,128)} custom-call(bf16[512,512]{1,0:T(8,128)(2,1)S(1)} %copy-done.28, bf16[128,2048]{1,0:T(8,128)(2,1)S(1)} %copy-done.11, bf16[128,2048]{1,0:T(8,128)(2,1)S(1)} %get-tuple-element.127.refs_1_, bf16[128,2048]{1,0:T(8,128)(2,1)S(1)} %copy-done.20, bf16[128,2048]{1,0:T(8,128)(2,1)S(1)} %get-tuple-element.126.refs_3_), custom_call_target="tpu_custom_call" | custom-call | flops 1073741824 | bytes 6291456 | tf_op jit(solution)/shard_map/slot_grad/pallas_call | solution.py:204
  237.3 1.3 fusion.11
  238.7 1.4 pad_maximum_fusion
  240.0 18.6 %collective-permute-done.27 = bf16[128,2048]{1,0:T(8,128)(2,1)S(1)} collective-permute-done((bf16[128,2048]{1,0:T(8,128)(2,1)S(1)}, bf16[128,2048]{1,0:T(8,128)(2,1)S(1)}, u32[]{:S(2)}, u32[]{:S(2)}) %collective-permute-start.27) | collective-permute-done | bytes 524320 | tf_op jit(solution)/shard_map/ppermute | solution.py:313
  258.6 0.8 copy.19
  (134 shorter events, 5.8 us)
Async XLA Ops:
  0.6 5.4 %copy-start = (bf16[128,7168]{1,0:T(8,128)(2,1)S(1)}, bf16[128,7168]{1,0:T(8,128)(2,1)}, u32[]{:S(2)}) copy-start(bf16[128,7168]{1,0:T(8,128)(2,1)} %refs_0_.5) | copy-start | bytes 5505028
  0.6 7.4 %copy-start.9 = (bf16[128,2048]{1,0:T(8,128)(2,1)S(1)}, bf16[128,2048]{1,0:T(8,128)(2,1)}, u32[]{:S(2)}) copy-start(bf16[128,2048]{1,0:T(8,128)(2,1)} %refs_0_.6) | copy-start | bytes 1572868
  0.7 1.7 copy-start.17
  5.9 2.0 collective-permute-start.1
  6.0 31.7 %collective-permute-start.4 = (bf16[128,7168]{1,0:T(8,128)(2,1)S(1)}, bf16[128,7168]{1,0:T(8,128)(2,1)S(1)}, u32[]{:S(2)}, u32[]{:S(2)}) collective-permute-start(bf16[128,7168]{1,0:T(8,128)(2,1)S(1)} %copy-done), channel_id=1, source_target_pairs={{0,1},{1,0},{2,3},{3,2},{4,5},{5,4},{6,7},{7,6},{8,9},{9,8},{10,11... | collective-permute-start | bytes 5505032 | tf_op jit(solution)/shard_map/ppermute | solution.py:304
  8.0 8.4 %collective-permute-start.2 = (bf16[64,2048]{1,0:T(8,128)(2,1)S(1)}, bf16[64,2048]{1,0:T(8,128)(2,1)S(1)}, u32[]{:S(2)}, u32[]{:S(2)}) collective-permute-start(bf16[64,2048]{1,0:T(8,128)(2,1)S(1)} %slice_add_fusion.8), channel_id=1, source_target_pairs={{0,2},{1,3},{2,0},{3,1},{4,6},{5,7},{6,4},{7,5},{8,10},{9,11},{10,... | collective-permute-start | bytes 786440 | tf_op jit(solution)/shard_map/ppermute | solution.py:304
  8.0 28.9 %collective-permute-start = (bf16[128,2048]{1,0:T(8,128)(2,1)S(1)}, bf16[128,2048]{1,0:T(8,128)(2,1)S(1)}, u32[]{:S(2)}, u32[]{:S(2)}) collective-permute-start(bf16[128,2048]{1,0:T(8,128)(2,1)S(1)} %copy-done.9), channel_id=1, source_target_pairs={{0,0},{4,5},{8,10},{12,15},{1,4},{5,1},{9,14},{13,11},{2,8},{6,13}... | collective-permute-start | bytes 1572872 | tf_op jit(solution)/shard_map/ppermute | solution.py:313
  16.4 61.5 %collective-permute-start.7 = (bf16[128,7168]{1,0:T(8,128)(2,1)S(1)}, bf16[128,7168]{1,0:T(8,128)(2,1)S(1)}, u32[]{:S(2)}, u32[]{:S(2)}) collective-permute-start(bf16[128,7168]{1,0:T(8,128)(2,1)S(1)} %copy-done), channel_id=1, source_target_pairs={{0,2},{1,3},{2,0},{3,1},{4,6},{5,7},{6,4},{7,5},{8,10},{9,11},{10,... | collective-permute-start | bytes 5505032 | tf_op jit(solution)/shard_map/ppermute | solution.py:304
  37.3 11.1 %collective-permute-start.3 = (f32[64,128]{1,0:T(8,128)S(1)}, f32[64,128]{1,0:T(8,128)S(1)}, u32[]{:S(2)}, u32[]{:S(2)}) collective-permute-start(f32[64,128]{1,0:T(8,128)S(1)} %fusion.28), channel_id=1, source_target_pairs={{0,4},{4,0},{8,12},{12,8},{1,5},{5,1},{9,13},{13,9},{2,6},{6,2},{1... | collective-permute-start | bytes 98312 | tf_op jit(solution)/shard_map/ppermute | solution.py:307
  37.8 35.7 %copy-start.1 = (bf16[128,7168]{1,0:T(8,128)(2,1)}, bf16[128,7168]{1,0:T(8,128)(2,1)S(1)}, u32[]{:S(2)}) copy-start(bf16[128,7168]{1,0:T(8,128)(2,1)S(1)} %collective-permute-done.4.b_ref.refs_3_.refs_1_) | copy-start | bytes 5505028
  48.4 29.4 %collective-permute-start.5 = (bf16[128,2048]{1,0:T(8,128)(2,1)S(1)}, bf16[128,2048]{1,0:T(8,128)(2,1)S(1)}, u32[]{:S(2)}, u32[]{:S(2)}) collective-permute-start(bf16[128,2048]{1,0:T(8,128)(2,1)S(1)} %collective-permute-done), channel_id=1, source_target_pairs={{0,8},{4,12},{8,0},{12,4},{1,9},{5,13},{9,1},{13,5},{2,10},{6,14},... | collective-permute-start | bytes 1572872 | tf_op jit(solution)/shard_map/ppermute | solution.py:307
  49.0 24.4 %collective-permute-start.6 = (f32[64,128]{1,0:T(8,128)S(1)}, f32[64,128]{1,0:T(8,128)S(1)}, u32[]{:S(2)}, u32[]{:S(2)}) collective-permute-start(f32[64,128]{1,0:T(8,128)S(1)} %add.113), channel_id=1, source_target_pairs={{0,8},{4,12},{8,0},{12,4},{1,9},{5,13},{9,1},{13,5},{2,10},{6,14},... | collective-permute-start | bytes 98312 | tf_op jit(solution)/shard_map/ppermute | solution.py:307
  77.9 35.4 %copy-start.3 = (bf16[128,7168]{1,0:T(8,128)(2,1)}, bf16[128,7168]{1,0:T(8,128)(2,1)S(1)}, u32[]{:S(2)}) copy-start(bf16[128,7168]{1,0:T(8,128)(2,1)S(1)} %collective-permute-done.7.refs_2_.a_ref) | copy-start | bytes 5505028
  77.9 6.5 %collective-permute-start.13 = (bf16[128,7168]{1,0:T(8,128)(2,1)S(1)}, bf16[128,7168]{1,0:T(8,128)(2,1)S(1)}, u32[]{:S(2)}, u32[]{:S(2)}) collective-permute-start(bf16[128,7168]{1,0:T(8,128)(2,1)S(1)} %collective-permute-done.7.refs_2_.a_ref), channel_id=1, source_target_pairs={{0,1},{1,0},{2,3},{3,2},{4,5},{5,4},{6,7},{7,6},{8,9},{9,8},{10,11... | collective-permute-start | bytes 5505032 | tf_op jit(solution)/shard_map/ppermute | solution.py:304
  78.0 50.2 %collective-permute-start.10 = (bf16[2,128,2048]{2,1,0:T(8,128)(2,1)S(1)}, bf16[2,128,2048]{2,1,0:T(8,128)(2,1)S(1)}, u32[]{:S(2)}, u32[]{:S(2)}) collective-permute-start(bf16[2,128,2048]{2,1,0:T(8,128)(2,1)S(1)} %pad_maximum_fusion.1.near_ref), channel_id=1, source_target_pairs={{0,4},{4,0},{8,12},{12,8},{1,5},{5,1},{9,13},{13,9},{2,6},{6,2},{1... | collective-permute-start | bytes 3145736 | tf_op jit(solution)/shard_map/ppermute | solution.py:307
  78.1 35.2 %collective-permute-start.8 = (bf16[128,2048]{1,0:T(8,128)(2,1)S(1)}, bf16[128,2048]{1,0:T(8,128)(2,1)S(1)}, u32[]{:S(2)}, u32[]{:S(2)}) collective-permute-start(bf16[128,2048]{1,0:T(8,128)(2,1)S(1)} %copy-done.9), channel_id=1, source_target_pairs={{0,2},{1,3},{2,0},{3,1},{4,6},{5,7},{6,4},{7,5},{8,10},{9,11},{10,... | collective-permute-start | bytes 1572872 | tf_op jit(solution)/shard_map/ppermute | solution.py:304
  78.1 10.9 %collective-permute-start.11 = (bf16[64,128]{1,0:T(8,128)(2,1)S(1)}, bf16[64,128]{1,0:T(8,128)(2,1)S(1)}, u32[]{:S(2)}, u32[]{:S(2)}) collective-permute-start(bf16[64,128]{1,0:T(8,128)(2,1)S(1)} %select_convert_fusion), channel_id=1, source_target_pairs={{0,1},{1,0},{2,3},{3,2},{4,5},{5,4},{6,7},{7,6},{8,9},{9,8},{10,11... | collective-permute-start | bytes 49160 | tf_op jit(solution)/shard_map/ppermute | solution.py:304
  78.5 34.8 %collective-permute-start.9 = (bf16[64,2048]{1,0:T(8,128)(2,1)S(1)}, bf16[64,2048]{1,0:T(8,128)(2,1)S(1)}, u32[]{:S(2)}, u32[]{:S(2)}) collective-permute-start(bf16[64,2048]{1,0:T(8,128)(2,1)S(1)} %fusion.21), channel_id=1, source_target_pairs={{0,0},{4,5},{8,10},{12,15},{1,4},{5,1},{9,14},{13,11},{2,8},{6,13}... | collective-permute-start | bytes 786440 | tf_op jit(solution)/shard_map/ppermute | solution.py:313
  84.4 29.0 %copy-start.5 = (bf16[128,7168]{1,0:T(8,128)(2,1)}, bf16[128,7168]{1,0:T(8,128)(2,1)S(1)}, u32[]{:S(2)}) copy-start(bf16[128,7168]{1,0:T(8,128)(2,1)S(1)} %collective-permute-done.13.refs_3_.b_ref) | copy-start | bytes 5505028
  88.8 23.2 %collective-permute-start.14 = (f32[64,512]{1,0:T(8,128)S(1)}, f32[64,512]{1,0:T(8,128)S(1)}, u32[]{:S(2)}, u32[]{:S(2)}) collective-permute-start(f32[64,512]{1,0:T(8,128)S(1)} %pad_maximum_fusion.4), channel_id=1, source_target_pairs={{0,4},{4,0},{8,12},{12,8},{1,5},{5,1},{9,13},{13,9},{2,6},{6,2},{1... | collective-permute-start | bytes 393224 | tf_op jit(solution)/shard_map/ppermute | solution.py:307
  89.1 24.2 %collective-permute-start.12 = (bf16[64,256]{1,0:T(8,128)(2,1)S(1)}, bf16[64,256]{1,0:T(8,128)(2,1)S(1)}, u32[]{:S(2)}, u32[]{:S(2)}) collective-permute-start(bf16[64,256]{1,0:T(8,128)(2,1)S(1)} %pad_maximum_fusion.6), channel_id=1, source_target_pairs={{0,2},{1,3},{2,0},{3,1},{4,6},{5,7},{6,4},{7,5},{8,10},{9,11},{10,... | collective-permute-start | bytes 98312 | tf_op jit(solution)/shard_map/ppermute | solution.py:304
  112.0 11.5 %collective-permute-start.15 = (f32[64,512]{1,0:T(8,128)S(1)}, f32[64,512]{1,0:T(8,128)S(1)}, u32[]{:S(2)}, u32[]{:S(2)}) collective-permute-start(f32[64,512]{1,0:T(8,128)S(1)} %add.115.refs_0_), channel_id=1, source_target_pairs={{0,8},{4,12},{8,0},{12,4},{1,9},{5,13},{9,1},{13,5},{2,10},{6,14},... | collective-permute-start | bytes 393224 | tf_op jit(solution)/shard_map/ppermute | solution.py:307
  113.3 9.3 %copy-start.42 = (bf16[64,2048]{1,0:T(8,128)(2,1)}, bf16[64,2048]{1,0:T(8,128)(2,1)S(1)}, u32[]{:S(2)}) copy-start(bf16[64,2048]{1,0:T(8,128)(2,1)S(1)} %collective-permute-done.9) | copy-start | bytes 786436
  113.3 9.2 %copy-start.18 = (bf16[128,2048]{1,0:T(8,128)(2,1)}, bf16[128,2048]{1,0:T(8,128)(2,1)S(1)}, u32[]{:S(2)}) copy-start(bf16[128,2048]{1,0:T(8,128)(2,1)S(1)} %collective-permute-done.8.refs_2_) | copy-start | bytes 1572868
  128.2 9.7 %copy-start.6 = (bf16[2,128,2048]{2,1,0:T(8,128)(2,1)}, bf16[2,128,2048]{2,1,0:T(8,128)(2,1)S(1)}, u32[]{:S(2)}) copy-start(bf16[2,128,2048]{2,1,0:T(8,128)(2,1)S(1)} %collective-permute-done.10.far_ref) | copy-start | bytes 3145732
  137.9 1.3 copy-start.12
  139.2 20.0 %collective-permute-start.18 = (f32[2,128,2048]{2,1,0:T(8,128)}, f32[2,128,2048]{2,1,0:T(8,128)}, u32[]{:S(2)}, u32[]{:S(2)}) collective-permute-start(f32[2,128,2048]{2,1,0:T(8,128)} %get-tuple-element.101), channel_id=1, source_target_pairs={{0,1},{1,0},{2,3},{3,2},{4,5},{5,4},{6,7},{7,6},{8,9},{9,8},{10,11... | collective-permute-start | bytes 6291464 | tf_op jit(solution)/shard_map/ppermute | solution.py:304
  139.2 3.4 %copy-start.10 = (bf16[128,2048]{1,0:T(8,128)(2,1)S(1)}, bf16[128,2048]{1,0:T(8,128)(2,1)}, u32[]{:S(2)}) copy-start(bf16[128,2048]{1,0:T(8,128)(2,1)} %refs_0_.6) | copy-start | bytes 1572868
  139.2 3.4 %copy-start.19 = (bf16[128,2048]{1,0:T(8,128)(2,1)S(1)}, bf16[128,2048]{1,0:T(8,128)(2,1)}, u32[]{:S(2)}) copy-start(bf16[128,2048]{1,0:T(8,128)(2,1)} %copy-done.18) | copy-start | bytes 1572868
  139.2 4.5 %copy-start.36 = (bf16[512,2048]{1,0:T(8,128)(2,1)S(1)}, bf16[512,2048]{1,0:T(8,128)(2,1)}, u32[]{:S(2)}) copy-start(bf16[512,2048]{1,0:T(8,128)(2,1)} %get-tuple-element.104) | copy-start | bytes 6291460
  142.1 7.4 %collective-permute-start.16 = (bf16[64,512]{1,0:T(8,128)(2,1)S(1)}, bf16[64,512]{1,0:T(8,128)(2,1)S(1)}, u32[]{:S(2)}, u32[]{:S(2)}) collective-permute-start(bf16[64,512]{1,0:T(8,128)(2,1)S(1)} %get-tuple-element.96), channel_id=1, source_target_pairs={{0,1},{1,0},{2,3},{3,2},{4,5},{5,4},{6,7},{7,6},{8,9},{9,8},{10,11... | collective-permute-start | bytes 196616 | tf_op jit(solution)/shard_map/ppermute | solution.py:304
  143.7 36.9 %collective-permute-start.19 = (bf16[256,2048]{1,0:T(8,128)(2,1)}, bf16[256,2048]{1,0:T(8,128)(2,1)}, u32[]{:S(2)}, u32[]{:S(2)}) collective-permute-start(bf16[256,2048]{1,0:T(8,128)(2,1)} %pad_maximum_fusion.2), channel_id=1, source_target_pairs={{0,1},{1,0},{2,3},{3,2},{4,5},{5,4},{6,7},{7,6},{8,9},{9,8},{10,11... | collective-permute-start | bytes 3145736 | tf_op jit(solution)/shard_map/ppermute | solution.py:304
  145.2 31.0 %all-to-all-start = ((bf16[4,128,1024]{2,1,0:T(8,128)(2,1)}), bf16[4,128,1024]{2,1,0:T(8,128)(2,1)}, u32[]{:S(2)}, u32[]{:S(2)}) async-start(bf16[4,128,1024]{2,1,0:T(8,128)(2,1)} %get-tuple-element.125), calls=%async_computation | async-start | bytes 2097152 | tf_op jit(solution)/shard_map/all_to_all | solution.py:350
  149.5 9.7 %collective-permute-start.17 = (bf16[64,512]{1,0:T(8,128)(2,1)S(1)}, bf16[64,512]{1,0:T(8,128)(2,1)S(1)}, u32[]{:S(2)}, u32[]{:S(2)}) collective-permute-start(bf16[64,512]{1,0:T(8,128)(2,1)S(1)} %maximum_add_fusion), channel_id=1, source_target_pairs={{0,2},{1,3},{2,0},{3,1},{4,6},{5,7},{6,4},{7,5},{8,10},{9,11},{10,... | collective-permute-start | bytes 196616 | tf_op jit(solution)/shard_map/ppermute | solution.py:304
  149.6 1.2 copy-start.7
  150.8 8.4 %copy-start.13 = (f32[2,128,2048]{2,1,0:T(8,128)S(1)}, f32[2,128,2048]{2,1,0:T(8,128)}, u32[]{:S(2)}) copy-start(f32[2,128,2048]{2,1,0:T(8,128)} %copy-done.12) | copy-start | bytes 6291460
  158.6 3.0 %copy-start.21 = (f32[2,128,1536]{2,1,0:T(8,128)}, f32[2,128,1536]{2,1,0:T(8,128)S(1)}, u32[]{:S(2)}) copy-start(f32[2,128,1536]{2,1,0:T(8,128)S(1)} %get-tuple-element.112) | copy-start | bytes 4718596
  158.6 5.0 %copy-start.39 = (f32[128,1024]{1,0:T(8,128)S(1)}, f32[128,1024]{1,0:T(8,128)}, u32[]{:S(2)}) copy-start(f32[128,1024]{1,0:T(8,128)} %get-tuple-element.140) | copy-start | bytes 1572868
  158.6 5.0 %copy-start.40 = (f32[128,1024]{1,0:T(8,128)S(1)}, f32[128,1024]{1,0:T(8,128)}, u32[]{:S(2)}) copy-start(f32[128,1024]{1,0:T(8,128)} %get-tuple-element.141) | copy-start | bytes 1572868
  158.6 35.8 %collective-permute-start.21 = (f32[2,128,1536]{2,1,0:T(8,128)}, f32[2,128,1536]{2,1,0:T(8,128)}, u32[]{:S(2)}, u32[]{:S(2)}) collective-permute-start(f32[2,128,1536]{2,1,0:T(8,128)} %get-tuple-element.109), channel_id=1, source_target_pairs={{0,1},{1,0},{2,3},{3,2},{4,5},{5,4},{6,7},{7,6},{8,9},{9,8},{10,11... | collective-permute-start | bytes 4718600 | tf_op jit(solution)/shard_map/ppermute | solution.py:304
  161.6 29.7 %collective-permute-start.20 = (bf16[128,2048]{1,0:T(8,128)(2,1)}, bf16[128,2048]{1,0:T(8,128)(2,1)}, u32[]{:S(2)}, u32[]{:S(2)}) collective-permute-start(bf16[128,2048]{1,0:T(8,128)(2,1)} %fusion.17), channel_id=1, source_target_pairs={{0,2},{1,3},{2,0},{3,1},{4,6},{5,7},{6,4},{7,5},{8,10},{9,11},{10,... | collective-permute-start | bytes 1572872 | tf_op jit(solution)/shard_map/ppermute | solution.py:304
  176.2 32.4 %all-to-all-start.1 = ((bf16[4,128,1024]{2,1,0:T(8,128)(2,1)}), bf16[4,128,1024]{2,1,0:T(8,128)(2,1)}, u32[]{:S(2)}, u32[]{:S(2)}) async-start(bf16[4,128,1024]{2,1,0:T(8,128)(2,1)} %get-tuple-element.124), calls=%async_computation.1 | async-start | bytes 2097152 | tf_op jit(solution)/shard_map/all_to_all | solution.py:350
  180.6 1.2 copy-start.8
  181.8 9.5 %copy-start.14 = (f32[2,128,2048]{2,1,0:T(8,128)S(1)}, f32[2,128,2048]{2,1,0:T(8,128)}, u32[]{:S(2)}) copy-start(f32[2,128,2048]{2,1,0:T(8,128)} %copy-done.12) | copy-start | bytes 6291460
  191.3 5.1 %copy-start.15 = (f32[2,128,2048]{2,1,0:T(8,128)}, f32[2,128,2048]{2,1,0:T(8,128)S(1)}, u32[]{:S(2)}) copy-start(f32[2,128,2048]{2,1,0:T(8,128)S(1)} %get-tuple-element.119) | copy-start | bytes 6291460
  191.3 3.1 %copy-start.22 = (f32[2,128,1536]{2,1,0:T(8,128)S(1)}, f32[2,128,1536]{2,1,0:T(8,128)}, u32[]{:S(2)}) copy-start(f32[2,128,1536]{2,1,0:T(8,128)} %copy-done.21) | copy-start | bytes 4718596
  191.3 20.3 %collective-permute-start.23 = (f32[2,128,2048]{2,1,0:T(8,128)}, f32[2,128,2048]{2,1,0:T(8,128)}, u32[]{:S(2)}, u32[]{:S(2)}) collective-permute-start(f32[2,128,2048]{2,1,0:T(8,128)} %get-tuple-element.115), channel_id=1, source_target_pairs={{0,1},{1,0},{2,3},{3,2},{4,5},{5,4},{6,7},{7,6},{8,9},{9,8},{10,11... | collective-permute-start | bytes 6291464 | tf_op jit(solution)/shard_map/ppermute | solution.py:304
  196.4 13.5 %collective-permute-start.22 = (bf16[128,1536]{1,0:T(8,128)(2,1)}, bf16[128,1536]{1,0:T(8,128)(2,1)}, u32[]{:S(2)}, u32[]{:S(2)}) collective-permute-start(bf16[128,1536]{1,0:T(8,128)(2,1)} %fusion.19), channel_id=1, source_target_pairs={{0,2},{1,3},{2,0},{3,1},{4,6},{5,7},{6,4},{7,5},{8,10},{9,11},{10,... | collective-permute-start | bytes 1179656 | tf_op jit(solution)/shard_map/ppermute | solution.py:304
  205.2 9.9 %collective-permute-start.24 = (f32[2,128,1536]{2,1,0:T(8,128)}, f32[2,128,1536]{2,1,0:T(8,128)}, u32[]{:S(2)}, u32[]{:S(2)}) collective-permute-start(f32[2,128,1536]{2,1,0:T(8,128)} %get-tuple-element.117), channel_id=1, source_target_pairs={{0,1},{1,0},{2,3},{3,2},{4,5},{5,4},{6,7},{7,6},{8,9},{9,8},{10,11... | collective-permute-start | bytes 4718600 | tf_op jit(solution)/shard_map/ppermute | solution.py:304
  208.5 3.1 %copy-start.16 = (f32[2,128,2048]{2,1,0:T(8,128)S(1)}, f32[2,128,2048]{2,1,0:T(8,128)}, u32[]{:S(2)}) copy-start(f32[2,128,2048]{2,1,0:T(8,128)} %copy-done.15) | copy-start | bytes 6291460
  209.8 5.3 %copy-start.24 = (f32[2,128,1536]{2,1,0:T(8,128)S(1)}, f32[2,128,1536]{2,1,0:T(8,128)}, u32[]{:S(2)}) copy-start(f32[2,128,1536]{2,1,0:T(8,128)} %copy-done.23) | copy-start | bytes 4718596
  211.6 5.0 %copy-start.2 = (bf16[128,7168]{1,0:T(8,128)(2,1)S(1)}, bf16[128,7168]{1,0:T(8,128)(2,1)}, u32[]{:S(2)}) copy-start(bf16[128,7168]{1,0:T(8,128)(2,1)} %copy-done.1) | copy-start | bytes 5505028
  211.6 5.0 %copy-start.4 = (bf16[128,7168]{1,0:T(8,128)(2,1)S(1)}, bf16[128,7168]{1,0:T(8,128)(2,1)}, u32[]{:S(2)}) copy-start(bf16[128,7168]{1,0:T(8,128)(2,1)} %copy-done.3) | copy-start | bytes 5505028
  211.6 4.9 %copy-start.26 = (bf16[512,512]{1,0:T(8,128)(2,1)S(1)}, bf16[512,512]{1,0:T(8,128)(2,1)}, u32[]{:S(2)}) copy-start(bf16[512,512]{1,0:T(8,128)(2,1)} %copy-done.25) | copy-start | bytes 1572868
  213.1 14.9 %collective-permute-start.25 = (bf16[128,2048]{1,0:T(8,128)(2,1)S(1)}, bf16[128,2048]{1,0:T(8,128)(2,1)S(1)}, u32[]{:S(2)}, u32[]{:S(2)}) collective-permute-start(bf16[128,2048]{1,0:T(8,128)(2,1)S(1)} %fusion.18), channel_id=1, source_target_pairs={{0,2},{1,3},{2,0},{3,1},{4,6},{5,7},{6,4},{7,5},{8,10},{9,11},{10,... | collective-permute-start | bytes 1572872 | tf_op jit(solution)/shard_map/ppermute | solution.py:304
  216.3 21.0 %collective-permute-start.26 = (bf16[128,1536]{1,0:T(8,128)(2,1)S(1)}, bf16[128,1536]{1,0:T(8,128)(2,1)S(1)}, u32[]{:S(2)}, u32[]{:S(2)}) collective-permute-start(bf16[128,1536]{1,0:T(8,128)(2,1)S(1)} %fusion.20), channel_id=1, source_target_pairs={{0,2},{1,3},{2,0},{3,1},{4,6},{5,7},{6,4},{7,5},{8,10},{9,11},{10,... | collective-permute-start | bytes 1179656 | tf_op jit(solution)/shard_map/ppermute | solution.py:304
  226.0 3.4 %copy-start.37 = (f32[128,2048]{1,0:T(8,128)S(1)}, f32[128,2048]{1,0:T(8,128)}, u32[]{:S(2)}) copy-start(f32[128,2048]{1,0:T(8,128)} %pad_maximum_fusion.3) | copy-start | bytes 3145732
  226.0 3.4 %copy-start.41 = (bf16[128,1024]{1,0:T(8,128)(2,1)S(1)}, bf16[128,1024]{1,0:T(8,128)(2,1)}, u32[]{:S(2)}) copy-start(bf16[128,1024]{1,0:T(8,128)(2,1)} %get-tuple-element.130) | copy-start | bytes 786436
  226.0 3.4 %copy-start.43 = (bf16[64,2048]{1,0:T(8,128)(2,1)S(1)}, bf16[64,2048]{1,0:T(8,128)(2,1)}, u32[]{:S(2)}) copy-start(bf16[64,2048]{1,0:T(8,128)(2,1)} %copy-done.42) | copy-start | bytes 786436
  229.4 5.0 %copy-start.11 = (bf16[128,2048]{1,0:T(8,128)(2,1)S(1)}, bf16[128,2048]{1,0:T(8,128)(2,1)}, u32[]{:S(2)}) copy-start(bf16[128,2048]{1,0:T(8,128)(2,1)} %refs_0_.6) | copy-start | bytes 1572868
  229.4 5.0 %copy-start.20 = (bf16[128,2048]{1,0:T(8,128)(2,1)S(1)}, bf16[128,2048]{1,0:T(8,128)(2,1)}, u32[]{:S(2)}) copy-start(bf16[128,2048]{1,0:T(8,128)(2,1)} %copy-done.18) | copy-start | bytes 1572868
  229.4 5.0 %copy-start.28 = (bf16[512,512]{1,0:T(8,128)(2,1)S(1)}, bf16[512,512]{1,0:T(8,128)(2,1)}, u32[]{:S(2)}) copy-start(bf16[512,512]{1,0:T(8,128)(2,1)} %copy-done.27) | copy-start | bytes 1572868
  229.9 28.7 %collective-permute-start.27 = (bf16[128,2048]{1,0:T(8,128)(2,1)S(1)}, bf16[128,2048]{1,0:T(8,128)(2,1)S(1)}, u32[]{:S(2)}, u32[]{:S(2)}) collective-permute-start(bf16[128,2048]{1,0:T(8,128)(2,1)S(1)} %fusion), channel_id=1, source_target_pairs={{0,0},{5,4},{10,8},{15,12},{4,1},{1,5},{14,9},{11,13},{8,2},{13,6}... | collective-permute-start | bytes 1572872 | tf_op jit(solution)/shard_map/ppermute | solution.py:313
  237.3 1.3 copy-start.38
  (10 other events, 8.7 us)

commit v6 on v5

--- a/solution.py
+++ b/solution.py
@@ -11,7 +11,7 @@
 
 adapter_scale = 2.0
 CORE, CHIP = 1, 2
-VMEM = 48 * 1024 * 1024
+VMEM = 36 * 1024 * 1024
 
 
 def dot(a, b, contract):
@@ -23,21 +23,30 @@
 
 
 def cost(flops, moved, share=16):
-    return pl.CostEstimate(flops=flops // share, bytes_accessed=moved // share, transcendentals=0)
-
-
-def project(facts, near, far, wide, weight, up_flat, start, stop, block):
-    _, rows, depth = near.shape
-    groups = 4
+    return pl.CostEstimate(flops=flops // share // 8, bytes_accessed=moved // share // 8, transcendentals=0)
+
+
+def project(facts, pieces, wide, weight, up_flat, start, stop, block):
+    rows2, depth = pieces[0][0].shape
+    rows = rows2 // 2
+    groups, ways = 4, len(pieces[0])
     span = wide.shape[1]
     base = start // block
-
-    def kernel(facts_ref, near_ref, far_ref, wide_ref, w_ref, up_ref, keep_ref, send_ref, lhs):
+    token_arrays = [x for piece in pieces for x in piece]
+
+    def kernel(facts_ref, *refs):
+        tok_refs = refs[: 2 * ways]
+        wide_ref, w_ref, up_ref, keep_ref, send_ref, lhs = refs[2 * ways :]
+
         @pl.when(pl.program_id(0) == 0)
         def _():
-            for m in range(groups):
-                at = pl.multiple_of((facts_ref[2 * groups] ^ m) * rows, rows)
-                lhs[pl.ds(at, rows)] = (far_ref if m & 1 else near_ref)[m >> 1]
+            for way in range(ways):
+
+                @pl.when(facts_ref[2 * groups] == way)
+                def _():
+                    for n in range(2):
+                        lhs[n * rows : (n + 1) * rows] = tok_refs[n * ways + way][:rows]
+                        lhs[(n + 2) * rows : (n + 3) * rows] = tok_refs[n * ways + way][rows:]
 
         total = dot(lhs[...], w_ref[...], (1, 0)) + dot(wide_ref[...], up_ref[...], (1, 0))
         keep_ref[0] = total[:rows]
@@ -45,35 +54,35 @@
         keep_ref[1] = total[2 * rows : 3 * rows]
         send_ref[1] = total[3 * rows :]
 
-    whole = lambda n: (0, 0, 0)
+    whole = lambda n: (0, 0)
     return pl.pallas_call(
         kernel,
         grid=((stop - start) // block,),
-        in_specs=[
-            pl.BlockSpec(memory_space=pltpu.SMEM),
-            pl.BlockSpec((2, rows, depth), whole),
-            pl.BlockSpec((2, rows, depth), whole),
-            pl.BlockSpec((groups * rows, span), lambda n: (0, 0)),
+        in_specs=[pl.BlockSpec(memory_space=pltpu.SMEM)]
+        + [pl.BlockSpec((rows2, depth), whole)] * (2 * ways)
+        + [
+            pl.BlockSpec((groups * rows, span), whole),
             pl.BlockSpec((depth, block), lambda n: (0, n + base)),
             pl.BlockSpec((span, block), lambda n: (0, n + base)),
         ],
         out_specs=[pl.BlockSpec((2, rows, block), lambda n: (0, 0, n))] * 2,
         out_shape=[jax.ShapeDtypeStruct((2, rows, stop - start), jnp.float32)] * 2,
-        scratch_shapes=[pltpu.VMEM((groups * rows, depth), near.dtype)],
+        scratch_shapes=[pltpu.VMEM((groups * rows, depth), token_arrays[0].dtype)],
         compiler_params=pltpu.CompilerParams(vmem_limit_bytes=VMEM),
         cost_estimate=cost(2 * groups * rows * (depth + span) * (stop - start), 2 * (depth + span + 2 * groups * rows) * (stop - start), 1),
         name="project",
-    )(facts, near, far, wide, weight, up_flat)
-
-
-def return_grad(first, second, weight, half, start, stop, sums=()):
+    )(facts, *token_arrays, wide, weight, up_flat)
+
+
+def return_grad(first, second, weight, half, rows_of, columns_of, carried=(), added=False, send=True):
     rows, hidden = first.shape
     depth = weight.shape[0]
     block = 256
-    base = start // block
+    base, column = rows_of[0] // block, columns_of[0] // hidden
+    steps = (rows_of[1] - rows_of[0]) // block
 
     def kernel(a_ref, b_ref, w_ref, *refs):
-        out_ref, sums_ref, rhs = refs[-3:]
+        out_ref, rhs = refs[len(carried)], refs[-1]
 
         @pl.when(pl.program_id(0) == 0)
         def _():
@@ -81,40 +90,81 @@
             rhs[rows:] = b_ref[...]
 
         total = dot(w_ref[...], rhs[...], (1, 1)).T
+        if added:
+            total += refs[0][...]
         out_ref[...] = total
-        sums_ref[...] = total.astype(sums_ref.dtype)
+        if send:
+            refs[-2][...] = total.astype(first.dtype)
 
     whole = lambda n: (0, 0)
-    return pl.pallas_call(
-        kernel,
-        grid=((stop - start) // block,),
+    tile = pl.BlockSpec((2 * rows, block), lambda n: (0, n + base))
+    outs = [(tile, jax.ShapeDtypeStruct((2 * rows, depth), jnp.float32))]
+    if send:
+        outs.append(
+            (
+                pl.BlockSpec((2 * rows, block), lambda n: (half, n + base)),
+                jax.ShapeDtypeStruct((4 * rows, depth), first.dtype),
+            )
+        )
+    anywhere = pl.BlockSpec(memory_space=pl.ANY)
+    taken = [tile if added and x.dtype == jnp.float32 else anywhere for x in carried]
+    target = {jnp.dtype(jnp.float32): 0, jnp.dtype(first.dtype): 1}
+    return pl.pallas_call(
+        kernel,
+        grid=(steps,),
         in_specs=[
             pl.BlockSpec((rows, hidden), whole),
             pl.BlockSpec((rows, hidden), whole),
-            pl.BlockSpec((block, hidden), lambda n: (n + base, 0)),
+            pl.BlockSpec((block, hidden), lambda n: (n + base, column)),
         ]
-        + [pl.BlockSpec(memory_space=pl.ANY)] * len(sums),
-        out_specs=[
-            pl.BlockSpec((2 * rows, block), lambda n: (0, n)),
-            pl.BlockSpec((2 * rows, block), lambda n: (half, n + base)),
-        ],
-        out_shape=[
-            jax.ShapeDtypeStruct((2 * rows, stop - start), jnp.float32),
-            jax.ShapeDtypeStruct((4 * rows, depth), first.dtype),
-        ],
-        input_output_aliases={3: 1} if sums else {},
+        + taken,
+        out_specs=[o[0] for o in outs],
+        out_shape=[o[1] for o in outs],
+        input_output_aliases={3 + n: target[jnp.dtype(x.dtype)] for n, x in enumerate(carried)},
         scratch_shapes=[pltpu.VMEM((2 * rows, hidden), first.dtype)],
         compiler_params=pltpu.CompilerParams(vmem_limit_bytes=VMEM),
-        cost_estimate=cost(4 * rows * hidden * (stop - start), 2 * hidden * (stop - start + 2 * rows)),
+        cost_estimate=cost(4 * rows * hidden * block * steps, 2 * hidden * (block * steps + 2 * rows)),
         name="return_grad",
-    )(first, second, weight, *sums)
-
-
-def rank_back(facts, store, blocks, places, block):
-    _, rank, columns = store.shape
-    rows = blocks[0].shape[0]
+    )(first, second, weight, *carried)
+
+
+def rank_inner(facts, flat, blocks, rank):
+    span, width = flat.shape
+    arrays, places = [x for x, _ in blocks], [n for _, n in blocks]
+    groups = len(blocks)
+    rows = arrays[0].shape[0] // 2
+    slots = span // rank
+
+    def kernel(facts_ref, flat_ref, *refs):
+        out_ref = refs[-1]
+        total = dot(flat_ref[...], jnp.concatenate([r[...] for r in refs[:-1]], axis=0), (1, 1))
+        for q in range(groups):
+            acc = jnp.zeros((rank, rows), jnp.float32)
+            for s in range(slots):
+                acc = jnp.where(facts_ref[q] == s, total[s * rank : (s + 1) * rank, q * rows : (q + 1) * rows], acc)
+            alive = lax.broadcasted_iota(jnp.int32, (rank, rows), 1) < facts_ref[groups + q]
+            out_ref[:, q * rows : (q + 1) * rows] = jnp.where(alive, acc, 0.0)
+
+    return pl.pallas_call(
+        kernel,
+        grid=(1,),
+        in_specs=[pl.BlockSpec(memory_space=pltpu.SMEM), pl.BlockSpec((span, width), lambda n: (0, 0))]
+        + [pl.BlockSpec((rows, width), lambda n, place=place: (place, 0)) for place in places],
+        out_specs=pl.BlockSpec((rank, groups * rows), lambda n: (0, 0)),
+        out_shape=jax.ShapeDtypeStruct((rank, groups * rows), jnp.float32),
+        compiler_params=pltpu.CompilerParams(vmem_limit_bytes=VMEM),
+        cost_estimate=cost(2 * span * groups * rows * width, 2 * width * (span + groups * rows)),
+        name="rank_inner",
+    )(facts, flat, *arrays)
+
+
+def rank_back(facts, store, blocks, places, block, start=0, before=None):
+    rank = store.shape[1]
+    rows, columns = blocks[0].shape
     count = len(blocks)
     groups = facts.shape[0] // 2
+    base = start // block
+    earlier = [] if before is None else [before]
 
     def kernel(facts_ref, *refs):
         slots, values, out_ref, total = refs[:count], refs[count : 2 * count], refs[-2], refs[-1]
@@ -137,26 +187,31 @@
                 part = total[at * rank : (at + 1) * rank, at * rows : (at + 1) * rows]
                 alive = lax.broadcasted_iota(jnp.int32, (rank, rows), 1) < facts_ref[groups + place]
                 alive = alive & (facts_ref[place] >= 0)
-                out_ref[:, at * rows : (at + 1) * rows] = jnp.where(alive, part * adapter_scale, 0.0)
+                part = jnp.where(alive, part * adapter_scale, 0.0)
+                if earlier:
+                    part += refs[2 * count][:, at * rows : (at + 1) * rows]
+                out_ref[:, at * rows : (at + 1) * rows] = part
 
     def chosen_slot(place):
-        return lambda n, facts_ref: (jnp.maximum(facts_ref[place], 0), 0, n)
-
+        return lambda n, facts_ref: (jnp.maximum(facts_ref[place], 0), 0, n + base)
+
+    small = pl.BlockSpec((rank, count * rows), lambda n, facts_ref: (0, 0))
     return pl.pallas_call(
         kernel,
         grid_spec=pltpu.PrefetchScalarGridSpec(
             num_scalar_prefetch=1,
             grid=(columns // block,),
             in_specs=[pl.BlockSpec((1, rank, block), chosen_slot(place)) for place in places]
-            + [pl.BlockSpec((rows, block), lambda n, facts_ref: (0, n))] * count,
-            out_specs=pl.BlockSpec((rank, count * rows), lambda n, facts_ref: (0, 0)),
+            + [pl.BlockSpec((rows, block), lambda n, facts_ref: (0, n))] * count
+            + [small] * len(earlier),
+            out_specs=small,
             scratch_shapes=[pltpu.VMEM((count * rank, count * rows), jnp.float32)],
         ),
         out_shape=jax.ShapeDtypeStruct((rank, count * rows), jnp.float32),
         compiler_params=pltpu.CompilerParams(vmem_limit_bytes=VMEM),
         cost_estimate=cost(2 * count * rank * count * rows * columns, 2 * columns * count * (rank + rows)),
         name="rank_back",
-    )(facts, *[store] * count, *blocks)
+    )(facts, *[store] * count, *blocks, *earlier)
 
 
 def spread(facts, here, there, slots, scale):
@@ -193,25 +248,43 @@
 
 
 def slot_grad(wide_t, blocks, block):
-    span = wide_t.shape[0]
-    rows, columns = blocks[0].shape
+    span, tokens = wide_t.shape
     groups = len(blocks)
+    rows = tokens // groups
+    columns = sum(x.shape[1] for x in blocks[0][0])
+    arrays, specs = [], []
+    for parts, place in blocks:
+        first = 0
+        for x in parts:
+            count = x.shape[1] // block
+            specs.append(
+                pl.BlockSpec((rows, block), lambda n, a=first, b=count - 1, place=place: (place, jnp.clip(n - a, 0, b)))
+            )
+            arrays.append(x)
+            first += count
 
     def kernel(wide_ref, *refs):
-        values = jnp.concatenate([c[...] for c in refs[:groups]], axis=0)
-        refs[groups][...] = dot(wide_ref[...], values, (1, 0))
+        n = pl.program_id(0)
+        values, at = [], 0
+        for parts, _ in blocks:
+            value, first = refs[at][...], parts[0].shape[1] // block
+            for more, x in enumerate(parts[1:], 1):
+                value = jnp.where(n >= first, refs[at + more][...], value)
+                first += x.shape[1] // block
+            values.append(value)
+            at += len(parts)
+        refs[-1][...] = dot(wide_ref[...], jnp.concatenate(values, axis=0), (1, 0))
 
     return pl.pallas_call(
         kernel,
         grid=(columns // block,),
-        in_specs=[pl.BlockSpec((span, groups * rows), lambda n: (0, 0))]
-        + [pl.BlockSpec((rows, block), lambda n: (0, n))] * groups,
+        in_specs=[pl.BlockSpec((span, tokens), lambda n: (0, 0))] + specs,
         out_specs=pl.BlockSpec((span, block), lambda n: (0, n)),
         out_shape=jax.ShapeDtypeStruct((span, columns), jnp.float32),
         compiler_params=pltpu.CompilerParams(vmem_limit_bytes=VMEM),
-        cost_estimate=cost(2 * span * groups * rows * columns, (4 * span + 2 * groups * rows) * columns, 1),
+        cost_estimate=cost(2 * span * tokens * columns, (4 * span + 2 * tokens) * columns, 1),
         name="slot_grad",
-    )(wide_t, *blocks)
+    )(wide_t, *arrays)
 
 
 def block_facts(block_adapter, block_length, adapter_slot, order, rows, per_owner, i):
@@ -306,62 +379,67 @@
     def along(x, bit):
         return lax.ppermute(x, "tp", [(z, z ^ bit) for z in range(shards)])
 
-    forth = [(c * groups + r, (r ^ c) * groups + c) for r in range(groups) for c in range(shards)]
-    back_again = [(b, a) for a, b in forth]
-
-    def turn(x, pairs):
+    place = [(c * groups + r, (r ^ c) * groups + c) for r in range(groups) for c in range(shards)]
+    hop = [(d * groups + d, (d ^ 2) * groups + d) for d in range(groups)]
+    hops = [(z * groups + d, (z ^ 1) * groups + d) for d in range(groups) for z in (d, d ^ 2)]
+
+    def share(x, got, bit):
+        return x + jnp.concatenate([got[:, (q ^ bit) * rows : ((q ^ bit) + 1) * rows] for q in range(groups)], axis=1)
+
+    def both(x, pairs):
         return lax.ppermute(x, ("tp", "dp"), pairs)
 
-    turned = turn(tokens, forth)
+    tok_x = swap(tokens, CHIP)
     cot_c = swap(cotangent, CORE)
-    here = jnp.stack([i, j]).astype(jnp.int32)
+    middle = hidden // 2
+    cot_a = swap(after(cotangent[:, :middle], tok_x), CHIP)
+    cot_b = swap(after(cotangent[:, middle:], tok_x), CHIP)
+    far = i ^ j
+    here = jnp.stack([i, jnp.minimum(jnp.where(far == 2, 1, 2 * (far & 1)), 2)]).astype(jnp.int32)
     down_t = jnp.swapaxes(adapter_down, 1, 2)
     near, rest, facts = choose(block_adapter, block_length, adapter_slot, here, down_t)
     up_flat = adapter_up.reshape(span, hidden)
     half = depth // 2
 
-    near = swap(near, CORE)
-    down_x = swap(rest[:rank] + near[rank:], CHIP)
-    cot_x = swap(after(cotangent, down_x), CHIP)
-    down_own = rest[rank:] + near[:rank] + down_x
-    inner = dot(down_own, after(tokens, turned), (1, 1))
-
-    grad01, parts = return_grad(after(cotangent, inner), cot_c, weight, 0, 0, half)
-    inner = inner + after(along(inner, 1), grad01)
-    tok_2 = along(after(turned, inner), 2)
-    more01, parts = return_grad(after(cotangent, inner, turned), cot_c, weight, 0, half, depth, (parts,))
-    inner = inner + after(along(inner, 2), more01)
-    inner = jnp.where(lax.broadcasted_iota(jnp.int32, (rank, rows), 1) < facts[groups], inner, 0.0).astype(b16)
-    back01 = rank_back(facts, after(adapter_up, inner), [cotangent, cot_c], (0, 1), hidden // 4)
-    inner = jnp.concatenate([inner, swap(inner, CORE)], axis=1)
-    tok_near = jnp.stack([turned, after(tok_2, back01)])
-    tok_far = along(tok_near, 1)
-
-    cot_xc = swap(after(cot_x, tok_near), CORE)
-    tok_x = swap(after(tokens, cot_x), CHIP)
-    inner = jnp.concatenate([inner, swap(after(inner, cot_x), CHIP)], axis=1)
-    back23 = rank_back(facts, adapter_up, [cot_x, cot_xc], (2, 3), hidden // 4)
+    even = jnp.concatenate([tokens, after(tok_x, facts)], axis=0)
+    odd = swap(even, CORE)
+    even_far = both(even, hop)
+    grad01, parts = return_grad(after(cotangent, even), cot_c, weight, 0, (0, depth), (0, hidden))
+    odd = after(odd, grad01)
+    odd_far = both(odd, hop)
+    toks = [(even, 0), (odd, 0), (even, 1), (odd, 1)]
+    inner = rank_inner(facts, down_t.reshape(span, width), toks, rank)
+    cot_ac = swap(after(cot_a, inner), CORE)
+    back01 = rank_back(facts, after(adapter_up, inner, cot_a), [cotangent, cot_c], (0, 1), hidden // 4)
+    inner = after(inner, back01) + along(inner, 1)
+    inner_far = along(inner, 2)
+    even_mid = jnp.where(i == j, even, after(even_far, inner))
+    even_all = both(even_mid, hops)
+    near = swap(after(near, cot_a), CORE)
+    grad23, = return_grad(
+        after(cot_a, even_mid), cot_ac, weight, 1, (0, depth), (0, middle), send=False
+    )
+    back23 = rank_back(facts, after(adapter_up, grad23), [cot_a, cot_ac], (2, 3), hidden // 4)
+    cot_bc = swap(after(cot_b, back23), CORE)
+    odd_mid = jnp.where(i == j, odd, after(odd_far, back23, cot_b))
+    odd_all = both(odd_mid, hops)
+    down_x = rest[:rank] + near[rank:]
+    grad23, parts = return_grad(
+        after(cot_b, odd_mid, even_all, down_x), cot_bc, weight, 1, (0, depth), (middle, hidden), (grad23, parts), added=True
+    )
+    back23 = rank_back(facts, after(adapter_up, grad23), [cot_b, cot_bc], (2, 3), hidden // 4, middle, back23)
     back = jnp.concatenate([back01, back23], axis=1)
-    grad23, parts = return_grad(after(cot_x, back), cot_xc, weight, 1, 0, half, (parts,))
-    back = after(back, grad23) + along(back, 1)
-    more23, parts = return_grad(after(cot_x, back), cot_xc, weight, 1, half, depth, (parts,))
-    back_wide, _, back_b = spread(facts, after(back, more23), along(back, 2), per_owner, 1.0)
-    parts = after(parts, back_b).reshape(shards, rows, depth)
-    parts = [lax.all_to_all(x, "tp", 0, 0, tiled=True) for x in (parts[:, :, :half], parts[:, :, half:])]
-    mixed = swap(jnp.concatenate([tokens, after(tok_x, back_b)], axis=0), CORE)
-    toks = [tokens, mixed[:rows], tok_x, mixed[rows:]]
-    down_mine = turn(after(down_own, cot_x), forth)
-    inner_wide, inner_rows, _ = spread(facts, after(inner, back_b), None, per_owner, adapter_scale)
+    back = back + along(back, 1)
+    down_x = swap(after(down_x, cot_b), CHIP)
+    back_wide, _, back_b = spread(facts, after(back, down_x), along(back, 2), per_owner, 1.0)
+    inner_wide, inner_rows, _ = spread(facts, after(inner, back_b), inner_far, per_owner, adapter_scale)
+    back_b = share(after(back_b, inner_wide), swap(back_b, CORE), CORE)
+    parts = lax.all_to_all(after(parts, back_b).reshape(shards, rows, depth), "tp", 0, 0, tiled=True)
+    down_mine = both(rest[rank:] + near[:rank] + after(down_x, back_b), place)
 
     def grad_block(q):
-        halves = [
-            [lax.dynamic_slice_in_dim(x, (q & 1) * rows, rows, 0) for x in both]
-            for both in ((grad01, grad23), (more01, more23))
-        ]
-        return jnp.concatenate([jnp.where(q < 2, low, high) for low, high in halves], axis=1)
-
-    def share(x, got, bit):
-        return x + jnp.concatenate([got[:, (q ^ bit) * rows : ((q ^ bit) + 1) * rows] for q in range(groups)], axis=1)
+        low, high = [lax.dynamic_slice_in_dim(x, (q & 1) * rows, rows, 0) for x in (grad01, grad23)]
+        return jnp.where(q < 2, low, high)
 
     block = 512
     steps = hidden // block
@@ -370,7 +448,7 @@
     kept, sent, got_c, got_x, done = [], [], [], [], []
 
     def make(n, *points):
-        keep, send = project(facts, after(tok_near, *points), tok_far, inner_rows, weight, up_flat, edges[n], edges[n + 1], block)
+        keep, send = project(facts, [(even, even_far, even_all), (odd, odd_far, after(odd_all, *points))], inner_rows, weight, up_flat, edges[n], edges[n + 1], block)
         kept.append(keep)
         got_c.append(swap(send, CORE))
         return keep
@@ -384,29 +462,27 @@
         done.append((after(kept[n], *points)[0] + got_c[n][0] + got_x[n].astype(jnp.float32)).astype(b16))
         return done[-1]
 
-    point = make(0, tok_x, down_mine)
-    back_b = share(after(back_b, point), swap(back_b, CORE), CORE)
-    point = make(1, back_b)
+    point = make(0, back_b)
     back_b = share(after(back_b, point), swap(back_b, CHIP), CHIP)
-    point = cross(0, back_b)
-    point = make(2, point, mixed, parts[0])
+    point = make(1, point)
+    point = cross(0, point)
+    point = make(2, point, down_mine, back_b)
     point = finish(0, point)
     point = cross(1, point)
     point = make(3, point)
     point = finish(1, point)
     point = cross(2, point)
     point = cross(3, point)
-    up_wide = slot_grad(after(inner_wide, point), [cotangent, cot_c, cot_x, cot_xc], 1024)
+    cots = [([cotangent], 0), ([cot_c], 0), ([cot_a, cot_b], 0), ([cot_ac, cot_bc], 0)]
+    up_wide = slot_grad(after(inner_wide, point), cots, hidden // 4)
     point = finish(2, up_wide)
     back_mine = lax.dynamic_slice_in_dim(back_b, j * rows, rows, 1)
-    total = after(grad_block(j), point, parts[1])
+    total = grad_block(j)
     for m in range(1, shards):
-        total = total + jnp.concatenate(
-            [lax.dynamic_index_in_dim(x, j ^ m, 0, False).astype(jnp.float32) for x in parts], axis=1
-        )
+        total = total + lax.dynamic_index_in_dim(after(parts, point), j ^ m, 0, False).astype(jnp.float32)
     total = (total + dot(back_mine, down_mine, (0, 0))).astype(b16)
-    tokens_grad = turn(total, back_again)
-    down_wide = slot_grad(after(back_wide, total), toks, 1024)
+    tokens_grad = both(total, [(b, a) for a, b in place])
+    down_wide = slot_grad(after(back_wide, total), [([x], n) for x, n in toks], width // 2)
     finish(3, down_wide)
     projected = jnp.concatenate(done, axis=1)
     up_grad = up_wide.reshape(per_owner, rank, hidden)

time: 261 us -> 252 us (0.966)
  starting transfers between devices: 37 us -> 28.6 us
  waiting for transfers between devices: 79.9 us -> 73.8 us
  other arithmetic: 22 us -> 16.2 us
  local copies, waits for them, and re-layouts: 21.7 us -> 25.7 us
  Pallas kernels: 96.9 us -> 99.7 us
    ppermute x19, waiting for transfers between devices: 5.82 us -> 23.5 us  [swap(): return lax.ppermute(x, 'dp', [(d, d ^ bit) for d in range(groups)])]
    ppermute x6 -> x4, waiting for transfers between devices: 23.8 us -> 10.5 us  [along(): return lax.ppermute(x, 'tp', [(z, z ^ bit) for z in range(shards)])]
    all_to_all x2 -> x1, waiting for transfers between devices: 11.4 us -> 0.01 us  [local_square(): lax.all_to_all(after(parts, back_b).reshape(shards, rows, depth), 'tp', 0...]
    unnamed x89 -> x96, local copies, waits for them, and re-layouts: 15.1 us -> 22.8 us
    ppermute x3 -> x6, starting transfers between devices: 16.3 us -> 10.9 us  [both(): return lax.ppermute(x, ('tp', 'dp'), pairs)]
    all_to_all x2 -> x1, starting transfers between devices: 8.69 us -> 4.64 us  [local_square(): lax.all_to_all(after(parts, back_b).reshape(shards, rows, depth), 'tp', 0...]
    pallas_call x4, Pallas kernels: 36.7 us -> 39.9 us  [the longest x3 38.1 us: return_grad(): pl.pallas_call(kernel, grid=(steps,), in_specs=[pl.BlockSpec((rows, hidde...]
    convert_element_type x2 -> x0, local copies, waits for them, and re-layouts: 3.18 us -> none  [local_square(): lax.dynamic_index_in_dim(x, j ^ m, 0, False).astype(jnp.float32)]
  transfers between devices with their start and end apart: 30 -> 30, of which waited for: 8 -> 9; matrix products, arithmetic and copies ran while one was open for 11% -> 9% of each run, Pallas kernels for 33% -> 37%
where the time goes in v6:
time: 252 us; the launch traced here: 248 us
  Pallas kernels  99.7 us (40%)
  waiting for transfers between devices  73.8 us (29%)
  starting transfers between devices  28.6 us (11%)
  local copies, waits for them, and re-layouts  25.7 us (10%)
  other arithmetic  16.2 us (6%)
  matrix products  2.56 us (1%)
    ppermute x6, waiting for transfers between devices, both(): return lax.ppermute(x, ('tp', 'dp'), pairs)  39.8 us
    pallas_call x3, Pallas kernels, return_grad(): pl.pallas_call(kernel, grid=(steps,), in_specs=[pl.BlockSpec((rows, hidde...  38.1 us
    pallas_call x4, Pallas kernels, project(): pl.pallas_call(kernel, grid=((stop - start) // block,), in_specs=[pl.Bloc...  32.9 us
    ppermute x19, waiting for transfers between devices, swap(): return lax.ppermute(x, 'dp', [(d, d ^ bit) for d in range(groups)])  23.5 us
    unnamed x96, local copies, waits for them, and re-layouts  22.8 us
    pallas_call x2, Pallas kernels, slot_grad(): pl.pallas_call(kernel, grid=(columns // block,), in_specs=[pl.BlockSpec((...  12.3 us
    ppermute x6, starting transfers between devices, both(): return lax.ppermute(x, ('tp', 'dp'), pairs)  10.9 us
    ppermute x4, waiting for transfers between devices, along(): return lax.ppermute(x, 'tp', [(z, z ^ bit) for z in range(shards)])  10.5 us
  transfers between devices with their start and end apart: 30, of which 9 were waited for; matrix products, arithmetic and copies ran while one was open for 9% of the time, Pallas kernels for 37%

profile of v6, /device:TPU:2, one launch (start us, length us, event | category | flops | bytes accessed | tf_op | source)
XLA Modules:
  0.0 247.8 jit_solution(4323213806121832548)
XLA Ops:
  0.9 1.6 copy-done.14
  4.4 1.5 choose.1
  6.0 1.5 constant_dynamic-update-slice_fusion.1
  7.4 7.2 %collective-permute-done = bf16[128,2048]{1,0:T(8,128)(2,1)} collective-permute-done((bf16[128,2048]{1,0:T(8,128)(2,1)}, bf16[128,2048]{1,0:T(8,128)(2,1)}, u32[]{:S(2)}, u32[]{:S(2)}) %collective-permute-start) | collective-permute-done | bytes 524320 | tf_op jit(solution)/shard_map/ppermute | solution.py:377
  14.7 1.1 constant_dynamic-update-slice_fusion.refs_0_.refs_2_
  15.9 1.0 fusion.25
  17.2 1.4 collective-permute-start.1
  18.6 15.7 %return_grad.3 = (f32[256,2048]{1,0:T(8,128)S(1)}, bf16[512,2048]{1,0:T(8,128)(2,1)S(1)}) custom-call(bf16[128,7168]{1,0:T(8,128)(2,1)S(1)} %copy-done.2, bf16[128,7168]{1,0:T(8,128)(2,1)} %collective-permute-done.3.b_ref.refs_3_.refs_1_, bf16[2048,7168]{1,0:T(8,128)(2,1)} %refs_7_.7), custom_call_target="tpu_custom_call" | custom-call | flops 58720256 | bytes 258048 | tf_op jit(solution)/shard_map/return_grad/pallas_call | solution.py:112
  34.4 1.8 rank_inner.1
  36.4 3.4 %collective-permute-done.4.a_ref.refs_2_ = bf16[128,3584]{1,0:T(8,128)(2,1)} collective-permute-done((bf16[128,3584]{1,0:T(8,128)(2,1)S(1)}, bf16[128,3584]{1,0:T(8,128)(2,1)}, u32[]{:S(2)}, u32[]{:S(2)}) %collective-permute-start.4) | collective-permute-done | bytes 917536 | tf_op jit(solution)/shard_map/ppermute | solution.py:377
  39.8 1.6 collective-permute-start.9
  41.3 1.4 collective-permute-start.5
  42.8 3.1 %copy-done = bf16[8,64,7168]{2,1,0:T(8,128)(2,1)S(1)} copy-done((bf16[8,64,7168]{2,1,0:T(8,128)(2,1)S(1)}, bf16[8,64,7168]{2,1,0:T(8,128)(2,1)}, u32[]{:S(2)}) %copy-start) | copy-done | bytes 7340056
  45.8 1.5 copy-done.3
  47.3 4.3 %rank_back.3 = f32[64,256]{1,0:T(8,128)S(1)} custom-call(s32[9]{0:T(128)S(1)} %get-tuple-element.61.facts_ref, bf16[8,64,7168]{2,1,0:T(8,128)(2,1)S(1)} %copy-done, bf16[8,64,7168]{2,1,0:T(8,128)(2,1)S(1)} %copy-done, bf16[128,7168]{1,0:T(8,128)(2,1)S(1)} %copy-done.3, bf16[128,7168]{1,0:T(8,128)(2,1)} %collective-permute-done.3.b_ref.refs_3_.refs_1_), custom_call_target="tpu_custom_call" | custom-call | flops 3670016 | bytes 43008 | tf_op jit(solution)/shard_map/rank_back/pallas_call | solution.py:199
  51.7 1.3 collective-permute-start.7
  53.2 2.4 collective-permute-start.6
  55.6 11.0 %return_grad.4.refs_0_ = f32[256,2048]{1,0:T(8,128)S(1)} custom-call(bf16[128,3584]{1,0:T(8,128)(2,1)} %collective-permute-done.4.a_ref.refs_2_, bf16[128,3584]{1,0:T(8,128)(2,1)} %collective-permute-done.8.b_ref.refs_3_.refs_4_, bf16[2048,7168]{1,0:T(8,128)(2,1)} %refs_7_.7), custom_call_target="tpu_custom_call" | custom-call | flops 29360128 | bytes 129024 | tf_op jit(solution)/shard_map/return_grad/pallas_call | solution.py:112
  66.6 2.7 %rank_back.4.refs_4_ = f32[64,256]{1,0:T(8,128)S(1)} custom-call(s32[9]{0:T(128)S(1)} %get-tuple-element.61.facts_ref, bf16[8,64,7168]{2,1,0:T(8,128)(2,1)S(1)} %bitcast.54, bf16[8,64,7168]{2,1,0:T(8,128)(2,1)S(1)} %bitcast.54, bf16[128,3584]{1,0:T(8,128)(2,1)} %collective-permute-done.4.a_ref.refs_2_, ...), custom_call_target="tpu_custom_call" | custom-call | flops 1835008 | bytes 21504 | tf_op jit(solution)/shard_map/rank_back/pallas_call | solution.py:199
  69.5 10.7 %collective-permute-done.7.refs_4_ = bf16[256,2048]{1,0:T(8,128)(2,1)S(1)} collective-permute-done((bf16[256,2048]{1,0:T(8,128)(2,1)S(1)}, bf16[256,2048]{1,0:T(8,128)(2,1)S(1)}, u32[]{:S(2)}, u32[]{:S(2)}) %collective-permute-start.7) | collective-permute-done | bytes 1048608 | tf_op jit(solution)/shard_map/ppermute | solution.py:390
  80.3 1.4 collective-permute-start.10
  81.7 11.4 %return_grad.5 = (f32[256,2048]{1,0:T(8,128)S(1)}, bf16[512,2048]{1,0:T(8,128)(2,1)S(1)}) custom-call(bf16[128,3584]{1,0:T(8,128)(2,1)} %collective-permute-done.9.a_ref.refs_2_.refs_3_, bf16[128,3584]{1,0:T(8,128)(2,1)S(1)} %collective-permute-done.12.b_ref.refs_3_.refs_5_, ...), custom_call_target="tpu_custom_call", output_to_operand_aliasing={{0}: (3, {}), {1}: (4, {})} | custom-call | flops 29360128 | bytes 129024 | tf_op jit(solution)/shard_map/return_grad/pallas_call | solution.py:112
  93.1 3.0 %rank_back.5 = f32[64,256]{1,0:T(8,128)S(1)} custom-call(s32[9]{0:T(128)S(1)} %get-tuple-element.61.facts_ref, bf16[8,64,7168]{2,1,0:T(8,128)(2,1)S(1)} %bitcast.54, bf16[8,64,7168]{2,1,0:T(8,128)(2,1)S(1)} %bitcast.54, bf16[128,3584]{1,0:T(8,128)(2,1)} %collective-permute-done.9.a_ref.refs_2_.refs_3_, ...), custom_call_target="tpu_custom_call" | custom-call | flops 1835008 | bytes 21504 | tf_op jit(solution)/shard_map/rank_back/pallas_call | solution.py:199
  96.2 1.2 collective-permute-start.14
  97.4 3.8 %collective-permute-done.13 = f32[64,512]{1,0:T(8,128)S(1)} collective-permute-done((f32[64,512]{1,0:T(8,128)S(1)}, f32[64,512]{1,0:T(8,128)S(1)}, u32[]{:S(2)}, u32[]{:S(2)}) %collective-permute-start.13) | collective-permute-done | bytes 131104 | tf_op jit(solution)/shard_map/ppermute | solution.py:380
  101.3 2.9 %collective-permute-start.16 = (f32[64,512]{1,0:T(8,128)S(1)}, f32[64,512]{1,0:T(8,128)S(1)}, u32[]{:S(2)}, u32[]{:S(2)}) collective-permute-start(f32[64,512]{1,0:T(8,128)S(1)} %add.102.refs_0_), channel_id=1, source_target_pairs={{0,8},{4,12},{8,0},{12,4},{1,9},{5,13},{9,1},{13,5},{2,10},{6,14},... | collective-permute-start | bytes 393224 | tf_op jit(solution)/shard_map/ppermute | solution.py:380
  104.2 6.7 %collective-permute-done.15.refs_1_ = f32[64,512]{1,0:T(8,128)S(1)} collective-permute-done((f32[64,512]{1,0:T(8,128)S(1)}, f32[64,512]{1,0:T(8,128)S(1)}, u32[]{:S(2)}, u32[]{:S(2)}) %collective-permute-start.15) | collective-permute-done | bytes 131104 | tf_op jit(solution)/shard_map/ppermute | solution.py:380
  110.9 1.6 spread.2
  112.5 0.9 copy-done.31
  113.4 1.4 spread.3
  114.8 0.8 copy-done.33
  115.7 8.7 %project.4 = (f32[2,128,2048]{2,1,0:T(8,128)S(1)}, f32[2,128,2048]{2,1,0:T(8,128)S(1)}) custom-call(s32[9]{0:T(128)S(1)} %get-tuple-element.61.facts_ref, bf16[256,2048]{1,0:T(8,128)(2,1)S(1)} %constant_dynamic-update-slice_fusion.refs_0_.refs_2_, bf16[256,2048]{1,0:T(8,128)(2,1)S(1)} %collective-permute-done.1.refs_1_, ...), custom_call_target="tpu_custom_call" | custom-call | flops 671088640 | bytes 1835008 | tf_op jit(solution)/shard_map/project/pallas_call | solution.py:58
  125.0 1.9 collective-permute-start.20
  126.9 7.5 %project.5 = (f32[2,128,1536]{2,1,0:T(8,128)S(1)}, f32[2,128,1536]{2,1,0:T(8,128)}) custom-call(s32[9]{0:T(128)S(1)} %get-tuple-element.61.facts_ref, bf16[256,2048]{1,0:T(8,128)(2,1)S(1)} %constant_dynamic-update-slice_fusion.refs_0_.refs_2_, bf16[256,2048]{1,0:T(8,128)(2,1)S(1)} %collective-permute-done.1.refs_1_, ...), custom_call_target="tpu_custom_call" | custom-call | flops 503316480 | bytes 1376256 | tf_op jit(solution)/shard_map/project/pallas_call | solution.py:58
  134.4 1.1 fusion.17
  136.8 2.5 %collective-permute-start.19 = (bf16[64,2048]{1,0:T(8,128)(2,1)}, bf16[64,2048]{1,0:T(8,128)(2,1)S(1)}, u32[]{:S(2)}, u32[]{:S(2)}) collective-permute-start(bf16[64,2048]{1,0:T(8,128)(2,1)} %fusion.21), channel_id=1, source_target_pairs={{0,0},{4,5},{8,10},{12,15},{1,4},{5,1},{9,14},{13,11},{2,8},{6,13}... | collective-permute-start | bytes 786440 | tf_op jit(solution)/shard_map/ppermute | solution.py:390
  139.4 4.6 %all-to-all-start = ((bf16[4,128,2048]{2,1,0:T(8,128)(2,1)}), bf16[4,128,2048]{2,1,0:T(8,128)(2,1)}, u32[]{:S(2)}, u32[]{:S(2)}) async-start(bf16[4,128,2048]{2,1,0:T(8,128)(2,1)} %bitcast.61), calls=%async_computation | async-start | bytes 4194304 | tf_op jit(solution)/shard_map/all_to_all | solution.py:437
  145.5 19.0 %collective-permute-done.19 = bf16[64,2048]{1,0:T(8,128)(2,1)S(1)} collective-permute-done((bf16[64,2048]{1,0:T(8,128)(2,1)}, bf16[64,2048]{1,0:T(8,128)(2,1)S(1)}, u32[]{:S(2)}, u32[]{:S(2)}) %collective-permute-start.19) | collective-permute-done | bytes 262176 | tf_op jit(solution)/shard_map/ppermute | solution.py:390
  164.4 3.1 %copy-done.1 = bf16[8,64,7168]{2,1,0:T(8,128)(2,1)S(1)} copy-done((bf16[8,64,7168]{2,1,0:T(8,128)(2,1)S(1)}, bf16[8,64,7168]{2,1,0:T(8,128)(2,1)}, u32[]{:S(2)}) %copy-start.1) | copy-done | bytes 7340056
  167.5 1.2 copy-done.6
  168.8 1.2 copy-done.8
  170.0 1.2 copy-done.10
  171.2 1.0 copy-done.13
  172.3 9.2 %project.6 = (f32[2,128,2048]{2,1,0:T(8,128)S(1)}, f32[2,128,2048]{2,1,0:T(8,128)}) custom-call(s32[9]{0:T(128)S(1)} %get-tuple-element.61.facts_ref, bf16[256,2048]{1,0:T(8,128)(2,1)S(1)} %constant_dynamic-update-slice_fusion.refs_0_.refs_2_, bf16[256,2048]{1,0:T(8,128)(2,1)S(1)} %collective-permute-done.1.refs_1_, bf16[256,2048]{1,0:T(8,128)(2,1)S(1)} %copy-done.8, ...), custom_call_target="tpu_custom_call" | custom-call | flops 671088640 | bytes 1835008 | tf_op jit(solution)/shard_map/project/pallas_call | solution.py:58
  181.5 1.3 copy-done.21
  182.9 2.1 fusion.7
  185.0 2.0 fusion.19
  187.0 7.4 %project.7 = (f32[2,128,1536]{2,1,0:T(8,128)S(1)}, f32[2,128,1536]{2,1,0:T(8,128)}) custom-call(s32[9]{0:T(128)S(1)} %get-tuple-element.61.facts_ref, bf16[256,2048]{1,0:T(8,128)(2,1)S(1)} %constant_dynamic-update-slice_fusion.refs_0_.refs_2_, bf16[256,2048]{1,0:T(8,128)(2,1)S(1)} %collective-permute-done.1.refs_1_, bf16[256,2048]{1,0:T(8,128)(2,1)S(1)} %copy-done.8, ...), custom_call_target="tpu_custom_call" | custom-call | flops 503316480 | bytes 1376256 | tf_op jit(solution)/shard_map/project/pallas_call | solution.py:58
  194.4 1.1 copy-done.27
  195.9 11.4 %collective-permute-done.23 = bf16[128,1536]{1,0:T(8,128)(2,1)S(1)} collective-permute-done((bf16[128,1536]{1,0:T(8,128)(2,1)}, bf16[128,1536]{1,0:T(8,128)(2,1)S(1)}, u32[]{:S(2)}, u32[]{:S(2)}) %collective-permute-start.23) | collective-permute-done | bytes 393248 | tf_op jit(solution)/shard_map/ppermute | solution.py:377
  207.3 1.5 fusion.15
  208.8 1.5 fusion.18
  210.7 2.0 fusion.20
  212.6 1.7 collective-permute-start.27
  214.4 9.3 %slot_grad.2 = f32[512,7168]{1,0:T(8,128)} custom-call(bf16[512,512]{1,0:T(8,128)(2,1)S(1)} %copy-done.34, bf16[128,7168]{1,0:T(8,128)(2,1)S(1)} %copy-done.4, bf16[128,7168]{1,0:T(8,128)(2,1)} %collective-permute-done.3.b_ref.refs_3_.refs_1_, bf16[128,3584]{1,0:T(8,128)(2,1)} %collective-permute-done.4.a_ref.refs_2_, ...), custom_call_target="tpu_custom_call" | custom-call | flops 469762048 | bytes 2752512 | tf_op jit(solution)/shard_map/slot_grad/pallas_call | solution.py:278
  223.7 1.5 collective-permute-done.26
  225.3 1.4 fusion.3
  226.7 2.6 %fusion = bf16[128,2048]{1,0:T(8,128)(2,1)S(1)} fusion(bf16[64,2048]{1,0:T(8,128)(2,1)} %copy-done.44, f32[256,2048]{1,0:T(8,128)} %copy-done.11, s32[]{:T(128)S(6)} %select_n.46, f32[256,2048]{1,0:T(8,128)} %copy-done.30, bf16[4,128,2048]{2,1,0:T(8,128)(2,1)} %all-to-all-done, s32[]{:T(128)S(6)} %select_n.50, s32[]{:T(128)S(6)} %select_n.49, ...), kind=kOutput, calls=%fused_computation.1 | convolution fusion | flops 35913728 | bytes 4472853 | tf_op jit(solution)/shard_map/dot_general | solution.py:18
  229.2 1.9 collective-permute-start.28
  231.2 3.0 %slot_grad.3 = f32[512,2048]{1,0:T(8,128)} custom-call(bf16[512,512]{1,0:T(8,128)(2,1)S(1)} %copy-done.32, bf16[256,2048]{1,0:T(8,128)(2,1)S(1)} %constant_dynamic-update-slice_fusion.refs_0_.refs_2_, bf16[256,2048]{1,0:T(8,128)(2,1)S(1)} %collective-permute-done.2.refs_1_.refs_3_, bf16[256,2048]{1,0:T(8,128)(2,1)S(1)} %constant_dynamic-update-slice_fusion.refs_0_.refs_2_, ...), custom_call_target="tpu_custom_call" | custom-call | flops 134217728 | bytes 786432 | tf_op jit(solution)/shard_map/slot_grad/pallas_call | solution.py:278
  234.1 1.4 fusion.11
  235.6 1.4 pad_maximum_fusion
  237.0 10.1 %collective-permute-done.28 = bf16[128,2048]{1,0:T(8,128)(2,1)S(1)} collective-permute-done((bf16[128,2048]{1,0:T(8,128)(2,1)S(1)}, bf16[128,2048]{1,0:T(8,128)(2,1)S(1)}, u32[]{:S(2)}, u32[]{:S(2)}) %collective-permute-start.28) | collective-permute-done | bytes 524320 | tf_op jit(solution)/shard_map/ppermute | solution.py:390
  247.1 0.8 copy.18
  (133 shorter events, 7.5 us)
Async XLA Ops:
  0.6 14.0 %collective-permute-start = (bf16[128,2048]{1,0:T(8,128)(2,1)}, bf16[128,2048]{1,0:T(8,128)(2,1)}, u32[]{:S(2)}, u32[]{:S(2)}) collective-permute-start(bf16[128,2048]{1,0:T(8,128)(2,1)} %param.8), channel_id=1, source_target_pairs={{0,2},{1,3},{2,0},{3,1},{4,6},{5,7},{6,4},{7,5},{8,10},{9,11},{10,... | collective-permute-start | bytes 1572872 | tf_op jit(solution)/shard_map/ppermute | solution.py:377
  0.7 17.9 %collective-permute-start.3 = (bf16[128,7168]{1,0:T(8,128)(2,1)}, bf16[128,7168]{1,0:T(8,128)(2,1)}, u32[]{:S(2)}, u32[]{:S(2)}) collective-permute-start(bf16[128,7168]{1,0:T(8,128)(2,1)} %refs_0_.4), channel_id=1, source_target_pairs={{0,1},{1,0},{2,3},{3,2},{4,5},{5,4},{6,7},{7,6},{8,9},{9,8},{10,11... | collective-permute-start | bytes 5505032 | tf_op jit(solution)/shard_map/ppermute | solution.py:377
  0.9 1.6 copy-start.14
  4.4 11.4 %copy-start.2 = (bf16[128,7168]{1,0:T(8,128)(2,1)S(1)}, bf16[128,7168]{1,0:T(8,128)(2,1)}, u32[]{:S(2)}) copy-start(bf16[128,7168]{1,0:T(8,128)(2,1)} %refs_0_.4) | copy-start | bytes 5505028
  6.0 10.9 %copy-start.35 = (bf16[128,2048]{1,0:T(8,128)(2,1)}, bf16[128,2048]{1,0:T(8,128)(2,1)S(1)}, u32[]{:S(2)}) copy-start(bf16[128,2048]{1,0:T(8,128)(2,1)S(1)} %get-tuple-element.75) | copy-start | bytes 1572868
  6.0 10.9 %copy-start.40 = (bf16[128,2048]{1,0:T(8,128)(2,1)}, bf16[128,2048]{1,0:T(8,128)(2,1)S(1)}, u32[]{:S(2)}) copy-start(bf16[128,2048]{1,0:T(8,128)(2,1)S(1)} %get-tuple-element.77) | copy-start | bytes 1572868
  15.8 18.6 %collective-permute-start.2 = (bf16[256,2048]{1,0:T(8,128)(2,1)S(1)}, bf16[256,2048]{1,0:T(8,128)(2,1)S(1)}, u32[]{:S(2)}, u32[]{:S(2)}) collective-permute-start(bf16[256,2048]{1,0:T(8,128)(2,1)S(1)} %constant_dynamic-update-slice_fusion.refs_0_.refs_2_), channel_id=1, source_target_pairs={{0,1},{1,0},{2,3},{3,2},{4,5},{5,4},{6,7},{7,6},{8,9},{9,8},{10,11... | collective-permute-start | bytes 3145736 | tf_op jit(solution)/shard_map/ppermute | solution.py:377
  16.9 17.5 %copy-start.15 = (bf16[8,2048,64]{1,2,0:T(8,128)(2,1)S(1)}, bf16[8,2048,64]{1,2,0:T(8,128)(2,1)}, u32[]{:S(2)}) copy-start(bf16[8,2048,64]{1,2,0:T(8,128)(2,1)} %param.10) | copy-start | bytes 6291460
  16.9 22.8 %collective-permute-start.4 = (bf16[128,3584]{1,0:T(8,128)(2,1)S(1)}, bf16[128,3584]{1,0:T(8,128)(2,1)}, u32[]{:S(2)}, u32[]{:S(2)}) collective-permute-start(bf16[128,3584]{1,0:T(8,128)(2,1)S(1)} %get-tuple-element.66), channel_id=1, source_target_pairs={{0,2},{1,3},{2,0},{3,1},{4,6},{5,7},{6,4},{7,5},{8,10},{9,11},{10,... | collective-permute-start | bytes 2752520 | tf_op jit(solution)/shard_map/ppermute | solution.py:377
  17.2 35.8 %collective-permute-start.1 = (bf16[256,2048]{1,0:T(8,128)(2,1)S(1)}, bf16[256,2048]{1,0:T(8,128)(2,1)S(1)}, u32[]{:S(2)}, u32[]{:S(2)}) collective-permute-start(bf16[256,2048]{1,0:T(8,128)(2,1)S(1)} %constant_dynamic-update-slice_fusion.refs_0_.refs_2_), channel_id=1, source_target_pairs={{0,8},{5,13},{10,2},{15,7},{16,24},{21,29},{26,18},{31,23}} | collective-permute-start | bytes 3145736 | tf_op jit(solution)/shard_map/ppermute | solution.py:390
  34.4 1.9 copy-start.16
  34.4 2.0 copy-start.30
  39.8 15.8 %collective-permute-start.8 = (bf16[128,3584]{1,0:T(8,128)(2,1)}, bf16[128,3584]{1,0:T(8,128)(2,1)}, u32[]{:S(2)}, u32[]{:S(2)}) collective-permute-start(bf16[128,3584]{1,0:T(8,128)(2,1)} %collective-permute-done.4.a_ref.refs_2_), channel_id=1, source_target_pairs={{0,1},{1,0},{2,3},{3,2},{4,5},{5,4},{6,7},{7,6},{8,9},{9,8},{10,11... | collective-permute-start | bytes 2752520 | tf_op jit(solution)/shard_map/ppermute | solution.py:377
  39.8 29.6 %collective-permute-start.9 = (bf16[128,3584]{1,0:T(8,128)(2,1)}, bf16[128,3584]{1,0:T(8,128)(2,1)}, u32[]{:S(2)}, u32[]{:S(2)}) collective-permute-start(bf16[128,3584]{1,0:T(8,128)(2,1)} %get-tuple-element.73), channel_id=1, source_target_pairs={{0,2},{1,3},{2,0},{3,1},{4,6},{5,7},{6,4},{7,5},{8,10},{9,11},{10,... | collective-permute-start | bytes 2752520 | tf_op jit(solution)/shard_map/ppermute | solution.py:377
  41.3 10.4 %collective-permute-start.5 = (f32[64,512]{1,0:T(8,128)S(1)}, f32[64,512]{1,0:T(8,128)S(1)}, u32[]{:S(2)}, u32[]{:S(2)}) collective-permute-start(f32[64,512]{1,0:T(8,128)S(1)} %rank_inner.1), channel_id=1, source_target_pairs={{0,4},{4,0},{8,12},{12,8},{1,5},{5,1},{9,13},{13,9},{2,6},{6,2},{1... | collective-permute-start | bytes 393224 | tf_op jit(solution)/shard_map/ppermute | solution.py:380
  42.8 26.7 %collective-permute-start.11 = (bf16[128,2048]{1,0:T(8,128)(2,1)}, bf16[128,2048]{1,0:T(8,128)(2,1)S(1)}, u32[]{:S(2)}, u32[]{:S(2)}) collective-permute-start(bf16[128,2048]{1,0:T(8,128)(2,1)} %copy-done.40), channel_id=1, source_target_pairs={{0,1},{1,0},{2,3},{3,2},{4,5},{5,4},{6,7},{7,6},{8,9},{9,8},{10,11... | collective-permute-start | bytes 1572872 | tf_op jit(solution)/shard_map/ppermute | solution.py:377
  42.8 3.1 %copy-start = (bf16[8,64,7168]{2,1,0:T(8,128)(2,1)S(1)}, bf16[8,64,7168]{2,1,0:T(8,128)(2,1)}, u32[]{:S(2)}) copy-start(bf16[8,64,7168]{2,1,0:T(8,128)(2,1)} %refs_1_.2) | copy-start | bytes 22020100
  45.8 1.5 copy-start.3
  51.7 28.5 %collective-permute-start.7 = (bf16[256,2048]{1,0:T(8,128)(2,1)S(1)}, bf16[256,2048]{1,0:T(8,128)(2,1)S(1)}, u32[]{:S(2)}, u32[]{:S(2)}) collective-permute-start(bf16[256,2048]{1,0:T(8,128)(2,1)S(1)} %collective-permute-done.2.refs_1_.refs_3_), channel_id=1, source_target_pairs={{0,8},{5,13},{10,2},{15,7},{16,24},{21,29},{26,18},{31,23}} | collective-permute-start | bytes 3145736 | tf_op jit(solution)/shard_map/ppermute | solution.py:390
  53.0 13.5 %slice-start = ((s8[7340032]{0:T(1024)(128)(4,1)}), s8[4194304]{0:T(1024)(128)(4,1)S(1)}, s32[]{:S(2)}) async-start(s8[7340032]{0:T(1024)(128)(4,1)} %bitcast.53), calls=%async_computation.1 | async-start | bytes 8388608
  53.2 13.4 %slice-start.1 = ((s8[7340032]{0:T(1024)(128)(4,1)}), s8[3145728]{0:T(1024)(128)(4,1)S(1)}, s32[]{:S(2)}) async-start(s8[7340032]{0:T(1024)(128)(4,1)} %bitcast.53), calls=%async_computation.2 | async-start | bytes 6291456
  53.2 28.5 %collective-permute-start.6 = (bf16[256,2048]{1,0:T(8,128)(2,1)S(1)}, bf16[256,2048]{1,0:T(8,128)(2,1)S(1)}, u32[]{:S(2)}, u32[]{:S(2)}) collective-permute-start(bf16[256,2048]{1,0:T(8,128)(2,1)S(1)} %broadcast_select_fusion.1), channel_id=1, source_target_pairs={{0,4},{8,12},{5,1},{13,9},{10,14},{2,6},{15,11},{7,3},{16,20},{24,... | collective-permute-start | bytes 3145736 | tf_op jit(solution)/shard_map/ppermute | solution.py:390
  66.6 2.9 %copy-start.36 = (bf16[128,2048]{1,0:T(8,128)(2,1)S(1)}, bf16[128,2048]{1,0:T(8,128)(2,1)}, u32[]{:S(2)}) copy-start(bf16[128,2048]{1,0:T(8,128)(2,1)} %copy-done.35) | copy-start | bytes 1572868
  69.3 12.4 %copy-start.17 = (bf16[512,2048]{1,0:T(8,128)(2,1)S(1)}, bf16[512,2048]{1,0:T(8,128)(2,1)}, u32[]{:S(2)}) copy-start(bf16[512,2048]{1,0:T(8,128)(2,1)} %copy-done.16) | copy-start | bytes 6291460
  69.4 12.3 %collective-permute-start.12 = (bf16[128,3584]{1,0:T(8,128)(2,1)}, bf16[128,3584]{1,0:T(8,128)(2,1)S(1)}, u32[]{:S(2)}, u32[]{:S(2)}) collective-permute-start(bf16[128,3584]{1,0:T(8,128)(2,1)} %collective-permute-done.9.a_ref.refs_2_.refs_3_), channel_id=1, source_target_pairs={{0,1},{1,0},{2,3},{3,2},{4,5},{5,4},{6,7},{7,6},{8,9},{9,8},{10,11... | collective-permute-start | bytes 2752520 | tf_op jit(solution)/shard_map/ppermute | solution.py:377
  80.2 46.7 %copy-start.5 = (bf16[256,2048]{1,0:T(8,128)(2,1)}, bf16[256,2048]{1,0:T(8,128)(2,1)S(1)}, u32[]{:S(2)}) copy-start(bf16[256,2048]{1,0:T(8,128)(2,1)S(1)} %collective-permute-done.7.refs_4_) | copy-start | bytes 3145732
  80.3 35.4 %collective-permute-start.10 = (bf16[256,2048]{1,0:T(8,128)(2,1)S(1)}, bf16[256,2048]{1,0:T(8,128)(2,1)S(1)}, u32[]{:S(2)}, u32[]{:S(2)}) collective-permute-start(bf16[256,2048]{1,0:T(8,128)(2,1)S(1)} %broadcast_select_fusion), channel_id=1, source_target_pairs={{0,4},{8,12},{5,1},{13,9},{10,14},{2,6},{15,11},{7,3},{16,20},{24,... | collective-permute-start | bytes 3145736 | tf_op jit(solution)/shard_map/ppermute | solution.py:390
  81.7 45.2 %copy-start.7 = (bf16[256,2048]{1,0:T(8,128)(2,1)}, bf16[256,2048]{1,0:T(8,128)(2,1)S(1)}, u32[]{:S(2)}) copy-start(bf16[256,2048]{1,0:T(8,128)(2,1)S(1)} %collective-permute-done.6.refs_2_) | copy-start | bytes 3145732
  81.7 11.4 %copy-start.19 = (bf16[128,3584]{1,0:T(8,128)(2,1)}, bf16[128,3584]{1,0:T(8,128)(2,1)S(1)}, u32[]{:S(2)}) copy-start(bf16[128,3584]{1,0:T(8,128)(2,1)S(1)} %collective-permute-done.12.b_ref.refs_3_.refs_5_) | copy-start | bytes 2752516
  93.1 3.0 %copy-start.11 = (f32[256,2048]{1,0:T(8,128)}, f32[256,2048]{1,0:T(8,128)S(1)}, u32[]{:S(2)}) copy-start(f32[256,2048]{1,0:T(8,128)S(1)} %get-tuple-element.81) | copy-start | bytes 6291460
  93.1 3.0 %copy-start.18 = (bf16[512,2048]{1,0:T(8,128)(2,1)}, bf16[512,2048]{1,0:T(8,128)(2,1)S(1)}, u32[]{:S(2)}) copy-start(bf16[512,2048]{1,0:T(8,128)(2,1)S(1)} %get-tuple-element.114) | copy-start | bytes 6291460
  96.2 5.0 %collective-permute-start.13 = (f32[64,512]{1,0:T(8,128)S(1)}, f32[64,512]{1,0:T(8,128)S(1)}, u32[]{:S(2)}, u32[]{:S(2)}) collective-permute-start(f32[64,512]{1,0:T(8,128)S(1)} %pad_maximum_fusion.1), channel_id=1, source_target_pairs={{0,4},{4,0},{8,12},{12,8},{1,5},{5,1},{9,13},{13,9},{2,6},{6,2},{1... | collective-permute-start | bytes 393224 | tf_op jit(solution)/shard_map/ppermute | solution.py:380
  96.2 8.0 %collective-permute-start.14 = (bf16[64,2048]{1,0:T(8,128)(2,1)S(1)}, bf16[64,2048]{1,0:T(8,128)(2,1)S(1)}, u32[]{:S(2)}, u32[]{:S(2)}) collective-permute-start(bf16[64,2048]{1,0:T(8,128)(2,1)S(1)} %slice_add_fusion.9), channel_id=1, source_target_pairs={{0,2},{1,3},{2,0},{3,1},{4,6},{5,7},{6,4},{7,5},{8,10},{9,11},{10,... | collective-permute-start | bytes 786440 | tf_op jit(solution)/shard_map/ppermute | solution.py:377
  101.2 9.7 %collective-permute-start.15 = (f32[64,512]{1,0:T(8,128)S(1)}, f32[64,512]{1,0:T(8,128)S(1)}, u32[]{:S(2)}, u32[]{:S(2)}) collective-permute-start(f32[64,512]{1,0:T(8,128)S(1)} %fusion.24.refs_0_), channel_id=1, source_target_pairs={{0,8},{4,12},{8,0},{12,4},{1,9},{5,13},{9,1},{13,5},{2,10},{6,14},... | collective-permute-start | bytes 393224 | tf_op jit(solution)/shard_map/ppermute | solution.py:380
  101.3 12.1 %collective-permute-start.16 = (f32[64,512]{1,0:T(8,128)S(1)}, f32[64,512]{1,0:T(8,128)S(1)}, u32[]{:S(2)}, u32[]{:S(2)}) collective-permute-start(f32[64,512]{1,0:T(8,128)S(1)} %add.102.refs_0_), channel_id=1, source_target_pairs={{0,8},{4,12},{8,0},{12,4},{1,9},{5,13},{9,1},{13,5},{2,10},{6,14},... | collective-permute-start | bytes 393224 | tf_op jit(solution)/shard_map/ppermute | solution.py:380
  113.4 2.3 collective-permute-start.17
  115.6 11.3 %copy-start.12 = (bf16[512,512]{1,0:T(8,128)(2,1)}, bf16[512,512]{1,0:T(8,128)(2,1)S(1)}, u32[]{:S(2)}) copy-start(bf16[512,512]{1,0:T(8,128)(2,1)S(1)} %get-tuple-element.90.refs_6_) | copy-start | bytes 1572868
  115.7 11.2 %copy-start.9 = (bf16[256,2048]{1,0:T(8,128)(2,1)}, bf16[256,2048]{1,0:T(8,128)(2,1)S(1)}, u32[]{:S(2)}) copy-start(bf16[256,2048]{1,0:T(8,128)(2,1)S(1)} %collective-permute-done.10.refs_5_) | copy-start | bytes 3145732
  124.5 9.9 %copy-start.23 = (f32[2,128,2048]{2,1,0:T(8,128)}, f32[2,128,2048]{2,1,0:T(8,128)S(1)}, u32[]{:S(2)}) copy-start(f32[2,128,2048]{2,1,0:T(8,128)S(1)} %get-tuple-element.100) | copy-start | bytes 6291460
  124.5 9.9 %collective-permute-start.18 = (f32[2,128,2048]{2,1,0:T(8,128)S(1)}, f32[2,128,2048]{2,1,0:T(8,128)S(1)}, u32[]{:S(2)}, u32[]{:S(2)}) collective-permute-start(f32[2,128,2048]{2,1,0:T(8,128)S(1)} %get-tuple-element.95), channel_id=1, source_target_pairs={{0,1},{1,0},{2,3},{3,2},{4,5},{5,4},{6,7},{7,6},{8,9},{9,8},{10,11... | collective-permute-start | bytes 6291464 | tf_op jit(solution)/shard_map/ppermute | solution.py:377
  125.0 19.0 %collective-permute-start.20 = (bf16[64,512]{1,0:T(8,128)(2,1)S(1)}, bf16[64,512]{1,0:T(8,128)(2,1)}, u32[]{:S(2)}, u32[]{:S(2)}) collective-permute-start(bf16[64,512]{1,0:T(8,128)(2,1)S(1)} %maximum_add_fusion), channel_id=1, source_target_pairs={{0,2},{1,3},{2,0},{3,1},{4,6},{5,7},{6,4},{7,5},{8,10},{9,11},{10,... | collective-permute-start | bytes 196616 | tf_op jit(solution)/shard_map/ppermute | solution.py:377
  134.4 50.6 %collective-permute-start.22 = (f32[2,128,1536]{2,1,0:T(8,128)}, f32[2,128,1536]{2,1,0:T(8,128)}, u32[]{:S(2)}, u32[]{:S(2)}) collective-permute-start(f32[2,128,1536]{2,1,0:T(8,128)} %get-tuple-element.102), channel_id=1, source_target_pairs={{0,1},{1,0},{2,3},{3,2},{4,5},{5,4},{6,7},{7,6},{8,9},{9,8},{10,11... | collective-permute-start | bytes 4718600 | tf_op jit(solution)/shard_map/ppermute | solution.py:377
  134.4 2.5 copy-start.41
  135.7 47.1 %collective-permute-start.21 = (bf16[128,2048]{1,0:T(8,128)(2,1)}, bf16[128,2048]{1,0:T(8,128)(2,1)}, u32[]{:S(2)}, u32[]{:S(2)}) collective-permute-start(bf16[128,2048]{1,0:T(8,128)(2,1)} %fusion.17), channel_id=1, source_target_pairs={{0,2},{1,3},{2,0},{3,1},{4,6},{5,7},{6,4},{7,5},{8,10},{9,11},{10,... | collective-permute-start | bytes 1572872 | tf_op jit(solution)/shard_map/ppermute | solution.py:377
  136.8 27.6 %collective-permute-start.19 = (bf16[64,2048]{1,0:T(8,128)(2,1)}, bf16[64,2048]{1,0:T(8,128)(2,1)S(1)}, u32[]{:S(2)}, u32[]{:S(2)}) collective-permute-start(bf16[64,2048]{1,0:T(8,128)(2,1)} %fusion.21), channel_id=1, source_target_pairs={{0,0},{4,5},{8,10},{12,15},{1,4},{5,1},{9,14},{13,11},{2,8},{6,13}... | collective-permute-start | bytes 786440 | tf_op jit(solution)/shard_map/ppermute | solution.py:390
  139.4 87.3 %all-to-all-start = ((bf16[4,128,2048]{2,1,0:T(8,128)(2,1)}), bf16[4,128,2048]{2,1,0:T(8,128)(2,1)}, u32[]{:S(2)}, u32[]{:S(2)}) async-start(bf16[4,128,2048]{2,1,0:T(8,128)(2,1)} %bitcast.61), calls=%async_computation | async-start | bytes 4194304 | tf_op jit(solution)/shard_map/all_to_all | solution.py:437
  164.4 3.1 %copy-start.1 = (bf16[8,64,7168]{2,1,0:T(8,128)(2,1)S(1)}, bf16[8,64,7168]{2,1,0:T(8,128)(2,1)}, u32[]{:S(2)}) copy-start(bf16[8,64,7168]{2,1,0:T(8,128)(2,1)} %refs_1_.2) | copy-start | bytes 22020100
  172.2 9.3 %copy-start.44 = (bf16[64,2048]{1,0:T(8,128)(2,1)}, bf16[64,2048]{1,0:T(8,128)(2,1)S(1)}, u32[]{:S(2)}) copy-start(bf16[64,2048]{1,0:T(8,128)(2,1)S(1)} %collective-permute-done.19) | copy-start | bytes 786436
  172.3 10.6 %copy-start.24 = (f32[2,128,2048]{2,1,0:T(8,128)S(1)}, f32[2,128,2048]{2,1,0:T(8,128)}, u32[]{:S(2)}) copy-start(f32[2,128,2048]{2,1,0:T(8,128)} %copy-done.23) | copy-start | bytes 6291460
  172.3 10.6 %copy-start.42 = (f32[2,128,2048]{2,1,0:T(8,128)S(1)}, f32[2,128,2048]{2,1,0:T(8,128)}, u32[]{:S(2)}) copy-start(f32[2,128,2048]{2,1,0:T(8,128)} %copy-done.41) | copy-start | bytes 6291460
  182.8 2.2 copy-start.26
  182.8 26.0 %collective-permute-start.24 = (f32[2,128,2048]{2,1,0:T(8,128)}, f32[2,128,2048]{2,1,0:T(8,128)}, u32[]{:S(2)}, u32[]{:S(2)}) collective-permute-start(f32[2,128,2048]{2,1,0:T(8,128)} %get-tuple-element.107), channel_id=1, source_target_pairs={{0,1},{1,0},{2,3},{3,2},{4,5},{5,4},{6,7},{7,6},{8,9},{9,8},{10,11... | collective-permute-start | bytes 6291464 | tf_op jit(solution)/shard_map/ppermute | solution.py:377
  195.5 15.1 %collective-permute-start.25 = (f32[2,128,1536]{2,1,0:T(8,128)}, f32[2,128,1536]{2,1,0:T(8,128)}, u32[]{:S(2)}, u32[]{:S(2)}) collective-permute-start(f32[2,128,1536]{2,1,0:T(8,128)} %get-tuple-element.109), channel_id=1, source_target_pairs={{0,1},{1,0},{2,3},{3,2},{4,5},{5,4},{6,7},{7,6},{8,9},{9,8},{10,11... | collective-permute-start | bytes 4718600 | tf_op jit(solution)/shard_map/ppermute | solution.py:377
  195.9 11.4 %collective-permute-start.23 = (bf16[128,1536]{1,0:T(8,128)(2,1)}, bf16[128,1536]{1,0:T(8,128)(2,1)S(1)}, u32[]{:S(2)}, u32[]{:S(2)}) collective-permute-start(bf16[128,1536]{1,0:T(8,128)(2,1)} %fusion.19), channel_id=1, source_target_pairs={{0,2},{1,3},{2,0},{3,1},{4,6},{5,7},{6,4},{7,5},{8,10},{9,11},{10,... | collective-permute-start | bytes 1179656 | tf_op jit(solution)/shard_map/ppermute | solution.py:377
  195.9 12.9 %copy-start.22 = (f32[2,128,2048]{2,1,0:T(8,128)S(1)}, f32[2,128,2048]{2,1,0:T(8,128)}, u32[]{:S(2)}) copy-start(f32[2,128,2048]{2,1,0:T(8,128)} %copy-done.21) | copy-start | bytes 6291460
  195.9 14.8 %copy-start.28 = (f32[2,128,1536]{2,1,0:T(8,128)S(1)}, f32[2,128,1536]{2,1,0:T(8,128)}, u32[]{:S(2)}) copy-start(f32[2,128,1536]{2,1,0:T(8,128)} %copy-done.27) | copy-start | bytes 4718596
  208.8 5.6 %copy-start.4 = (bf16[128,7168]{1,0:T(8,128)(2,1)S(1)}, bf16[128,7168]{1,0:T(8,128)(2,1)}, u32[]{:S(2)}) copy-start(bf16[128,7168]{1,0:T(8,128)(2,1)} %refs_0_.4) | copy-start | bytes 5505028
  208.8 5.6 %copy-start.20 = (bf16[128,3584]{1,0:T(8,128)(2,1)S(1)}, bf16[128,3584]{1,0:T(8,128)(2,1)}, u32[]{:S(2)}) copy-start(bf16[128,3584]{1,0:T(8,128)(2,1)} %copy-done.19) | copy-start | bytes 2752516
  208.8 5.6 %copy-start.34 = (bf16[512,512]{1,0:T(8,128)(2,1)S(1)}, bf16[512,512]{1,0:T(8,128)(2,1)}, u32[]{:S(2)}) copy-start(bf16[512,512]{1,0:T(8,128)(2,1)} %copy-done.33) | copy-start | bytes 1572868
  210.3 14.9 %collective-permute-start.26 = (bf16[128,2048]{1,0:T(8,128)(2,1)S(1)}, bf16[128,2048]{1,0:T(8,128)(2,1)S(1)}, u32[]{:S(2)}, u32[]{:S(2)}) collective-permute-start(bf16[128,2048]{1,0:T(8,128)(2,1)S(1)} %fusion.18), channel_id=1, source_target_pairs={{0,2},{1,3},{2,0},{3,1},{4,6},{5,7},{6,4},{7,5},{8,10},{9,11},{10,... | collective-permute-start | bytes 1572872 | tf_op jit(solution)/shard_map/ppermute | solution.py:377
  212.6 21.5 %collective-permute-start.27 = (bf16[128,1536]{1,0:T(8,128)(2,1)}, bf16[128,1536]{1,0:T(8,128)(2,1)}, u32[]{:S(2)}, u32[]{:S(2)}) collective-permute-start(bf16[128,1536]{1,0:T(8,128)(2,1)} %fusion.20), channel_id=1, source_target_pairs={{0,2},{1,3},{2,0},{3,1},{4,6},{5,7},{6,4},{7,5},{8,10},{9,11},{10,... | collective-permute-start | bytes 1179656 | tf_op jit(solution)/shard_map/ppermute | solution.py:377
  226.7 4.5 %copy-start.32 = (bf16[512,512]{1,0:T(8,128)(2,1)S(1)}, bf16[512,512]{1,0:T(8,128)(2,1)}, u32[]{:S(2)}) copy-start(bf16[512,512]{1,0:T(8,128)(2,1)} %copy-done.31) | copy-start | bytes 1572868
  229.2 17.8 %collective-permute-start.28 = (bf16[128,2048]{1,0:T(8,128)(2,1)S(1)}, bf16[128,2048]{1,0:T(8,128)(2,1)S(1)}, u32[]{:S(2)}, u32[]{:S(2)}) collective-permute-start(bf16[128,2048]{1,0:T(8,128)(2,1)S(1)} %fusion), channel_id=1, source_target_pairs={{0,0},{5,4},{10,8},{15,12},{4,1},{1,5},{14,9},{11,13},{8,2},{13,6}... | collective-permute-start | bytes 1572872 | tf_op jit(solution)/shard_map/ppermute | solution.py:390
  231.2 3.0 %copy-start.29 = (f32[2,128,1536]{2,1,0:T(8,128)S(1)}, f32[2,128,1536]{2,1,0:T(8,128)}, u32[]{:S(2)}) copy-start(f32[2,128,1536]{2,1,0:T(8,128)} %copy-done.27) | copy-start | bytes 4718596
  (13 other events, 13.6 us)

commit v7 on v6

--- a/solution.py
+++ b/solution.py
@@ -22,110 +22,126 @@
     return lax.optimization_barrier((x,) + others)[0]
 
 
-def cost(flops, moved, share=16):
-    return pl.CostEstimate(flops=flops // share // 8, bytes_accessed=moved // share // 8, transcendentals=0)
-
-
-def project(facts, pieces, wide, weight, up_flat, start, stop, block):
-    rows2, depth = pieces[0][0].shape
-    rows = rows2 // 2
-    groups, ways = 4, len(pieces[0])
+def cost(flops, moved, share=64):
+    return pl.CostEstimate(flops=flops // share, bytes_accessed=moved // share, transcendentals=0)
+
+
+def project(tokens, wide, weight, up_flat, start, stop, block):
+    rows, depth = tokens.shape
     span = wide.shape[1]
     base = start // block
-    token_arrays = [x for piece in pieces for x in piece]
-
-    def kernel(facts_ref, *refs):
-        tok_refs = refs[: 2 * ways]
-        wide_ref, w_ref, up_ref, keep_ref, send_ref, lhs = refs[2 * ways :]
-
-        @pl.when(pl.program_id(0) == 0)
-        def _():
-            for way in range(ways):
-
-                @pl.when(facts_ref[2 * groups] == way)
-                def _():
-                    for n in range(2):
-                        lhs[n * rows : (n + 1) * rows] = tok_refs[n * ways + way][:rows]
-                        lhs[(n + 2) * rows : (n + 3) * rows] = tok_refs[n * ways + way][rows:]
-
-        total = dot(lhs[...], w_ref[...], (1, 0)) + dot(wide_ref[...], up_ref[...], (1, 0))
-        keep_ref[0] = total[:rows]
-        send_ref[0] = total[rows : 2 * rows]
-        keep_ref[1] = total[2 * rows : 3 * rows]
-        send_ref[1] = total[3 * rows :]
+
+    def kernel(tok_ref, wide_ref, w_ref, up_ref, keep_ref, send_ref):
+        total = dot(tok_ref[...], w_ref[...], (1, 0)) + dot(wide_ref[...], up_ref[...], (1, 0))
+        keep_ref[...] = total[: rows // 2]
+        send_ref[...] = total[rows // 2 :]
 
     whole = lambda n: (0, 0)
     return pl.pallas_call(
         kernel,
         grid=((stop - start) // block,),
-        in_specs=[pl.BlockSpec(memory_space=pltpu.SMEM)]
-        + [pl.BlockSpec((rows2, depth), whole)] * (2 * ways)
-        + [
-            pl.BlockSpec((groups * rows, span), whole),
+        in_specs=[
+            pl.BlockSpec((rows, depth), whole),
+            pl.BlockSpec((rows, span), whole),
             pl.BlockSpec((depth, block), lambda n: (0, n + base)),
             pl.BlockSpec((span, block), lambda n: (0, n + base)),
         ],
-        out_specs=[pl.BlockSpec((2, rows, block), lambda n: (0, 0, n))] * 2,
-        out_shape=[jax.ShapeDtypeStruct((2, rows, stop - start), jnp.float32)] * 2,
-        scratch_shapes=[pltpu.VMEM((groups * rows, depth), token_arrays[0].dtype)],
+        out_specs=[pl.BlockSpec((rows // 2, block), lambda n: (0, n))] * 2,
+        out_shape=[jax.ShapeDtypeStruct((rows // 2, stop - start), jnp.float32)] * 2,
         compiler_params=pltpu.CompilerParams(vmem_limit_bytes=VMEM),
-        cost_estimate=cost(2 * groups * rows * (depth + span) * (stop - start), 2 * (depth + span + 2 * groups * rows) * (stop - start), 1),
+        cost_estimate=cost(2 * rows * (depth + span) * (stop - start), 2 * (depth + span + 2 * rows) * (stop - start)),
         name="project",
-    )(facts, *token_arrays, wide, weight, up_flat)
-
-
-def return_grad(first, second, weight, half, rows_of, columns_of, carried=(), added=False, send=True):
+    )(tokens, wide, weight, up_flat)
+
+
+def return_grad(facts, first, second, weight, store, places, features, units, block, before=(), grads=None, finish=True):
     rows, hidden = first.shape
-    depth = weight.shape[0]
-    block = 256
-    base, column = rows_of[0] // block, columns_of[0] // hidden
-    steps = (rows_of[1] - rows_of[0]) // block
-
-    def kernel(a_ref, b_ref, w_ref, *refs):
-        out_ref, rhs = refs[len(carried)], refs[-1]
-
-        @pl.when(pl.program_id(0) == 0)
+    depth, rank = weight.shape[0], store.shape[1]
+    groups = facts.shape[0] // 2
+    count, part = features[1] - features[0], features[0] // (features[1] - features[0])
+    base, half = units[0] // block, places[0] // 2
+    grads = tuple(grads or ())
+
+    def kernel(facts_ref, a_ref, b_ref, w_ref, up_a_ref, up_b_ref, *refs):
+        before_refs = refs[: len(before)]
+        outs, (total, ranks) = refs[len(before) + len(grads) : -2], refs[-2:]
+        n = pl.program_id(0)
+        rhs = jnp.concatenate([a_ref[...], b_ref[...]], axis=0)
+        product = dot(w_ref[...], rhs, (1, 1))
+        ranked = dot(jnp.concatenate([up_a_ref[0], up_b_ref[0]], axis=0), rhs, (1, 1))
+
+        @pl.when(n == 0)
         def _():
-            rhs[:rows] = a_ref[...]
-            rhs[rows:] = b_ref[...]
-
-        total = dot(w_ref[...], rhs[...], (1, 1)).T
-        if added:
-            total += refs[0][...]
-        out_ref[...] = total
-        if send:
-            refs[-2][...] = total.astype(first.dtype)
-
-    whole = lambda n: (0, 0)
-    tile = pl.BlockSpec((2 * rows, block), lambda n: (0, n + base))
-    outs = [(tile, jax.ShapeDtypeStruct((2 * rows, depth), jnp.float32))]
-    if send:
-        outs.append(
+            total[...] = product + before_refs[0][...] if before else product
+            ranks[...] = ranked
+
+        @pl.when(n > 0)
+        def _():
+            total[...] += product
+            ranks[...] += ranked
+
+        @pl.when(n == pl.num_programs(0) - 1)
+        def _():
+            for at, place in enumerate(places):
+                value = ranks[at * rank : (at + 1) * rank, at * rows : (at + 1) * rows]
+                alive = lax.broadcasted_iota(jnp.int32, (rank, rows), 1) < facts_ref[groups + place]
+                alive = alive & (facts_ref[place] >= 0)
+                value = jnp.where(alive, value * adapter_scale, 0.0)
+                if before:
+                    value += before_refs[1][:, at * rows : (at + 1) * rows]
+                outs[0][:, at * rows : (at + 1) * rows] = value
+            if finish:
+                for m in range(0, count, 256):
+                    turned = total[m : m + 256].T
+                    outs[1][:, m : m + 256] = turned
+                    outs[2][:, m : m + 256] = turned.astype(first.dtype)
+            else:
+                outs[1][...] = total[...]
+
+    def chosen_slot(place):
+        return lambda n, facts_ref: (jnp.maximum(facts_ref[place], 0), 0, n + base)
+
+    whole = lambda n, facts_ref: (0, 0)
+    outs = [(pl.BlockSpec((rank, 2 * rows), whole), jax.ShapeDtypeStruct((rank, 2 * rows), jnp.float32))]
+    if finish:
+        outs += [
             (
-                pl.BlockSpec((2 * rows, block), lambda n: (half, n + base)),
+                pl.BlockSpec((2 * rows, count), lambda n, facts_ref: (0, part)),
+                jax.ShapeDtypeStruct((2 * rows, depth), jnp.float32),
+            ),
+            (
+                pl.BlockSpec((2 * rows, count), lambda n, facts_ref: (half, part)),
                 jax.ShapeDtypeStruct((4 * rows, depth), first.dtype),
-            )
-        )
-    anywhere = pl.BlockSpec(memory_space=pl.ANY)
-    taken = [tile if added and x.dtype == jnp.float32 else anywhere for x in carried]
-    target = {jnp.dtype(jnp.float32): 0, jnp.dtype(first.dtype): 1}
+            ),
+        ]
+    else:
+        outs += [(pl.BlockSpec((count, 2 * rows), whole), jax.ShapeDtypeStruct((count, 2 * rows), jnp.float32))]
+    at = 6 + len(before)
     return pl.pallas_call(
         kernel,
-        grid=(steps,),
-        in_specs=[
-            pl.BlockSpec((rows, hidden), whole),
-            pl.BlockSpec((rows, hidden), whole),
-            pl.BlockSpec((block, hidden), lambda n: (n + base, column)),
-        ]
-        + taken,
-        out_specs=[o[0] for o in outs],
+        grid_spec=pltpu.PrefetchScalarGridSpec(
+            num_scalar_prefetch=1,
+            grid=(hidden // block,),
+            in_specs=[
+                pl.BlockSpec((rows, block), lambda n, facts_ref: (0, n)),
+                pl.BlockSpec((rows, block), lambda n, facts_ref: (0, n)),
+                pl.BlockSpec((count, block), lambda n, facts_ref: (part, n + base)),
+                *[pl.BlockSpec((1, rank, block), chosen_slot(place)) for place in places],
+                *[pl.BlockSpec(x.shape, whole) for x in before],
+                *[pl.BlockSpec(memory_space=pl.ANY)] * len(grads),
+            ],
+            out_specs=[o[0] for o in outs],
+            scratch_shapes=[
+                pltpu.VMEM((count, 2 * rows), jnp.float32),
+                pltpu.VMEM((2 * rank, 2 * rows), jnp.float32),
+            ],
+        ),
         out_shape=[o[1] for o in outs],
-        input_output_aliases={3 + n: target[jnp.dtype(x.dtype)] for n, x in enumerate(carried)},
-        scratch_shapes=[pltpu.VMEM((2 * rows, hidden), first.dtype)],
+        input_output_aliases={at + n: (1 if x.dtype == jnp.float32 else 2) for n, x in enumerate(grads)},
         compiler_params=pltpu.CompilerParams(vmem_limit_bytes=VMEM),
-        cost_estimate=cost(4 * rows * hidden * block * steps, 2 * hidden * (block * steps + 2 * rows)),
+        cost_estimate=cost(4 * rows * hidden * count, 2 * hidden * (count + 2 * rows)),
         name="return_grad",
-    )(first, second, weight, *carried)
+    )(facts, first, second, weight, store, store, *before, *grads)
 
 
 def rank_inner(facts, flat, blocks, rank):
@@ -158,62 +174,6 @@
     )(facts, flat, *arrays)
 
 
-def rank_back(facts, store, blocks, places, block, start=0, before=None):
-    rank = store.shape[1]
-    rows, columns = blocks[0].shape
-    count = len(blocks)
-    groups = facts.shape[0] // 2
-    base = start // block
-    earlier = [] if before is None else [before]
-
-    def kernel(facts_ref, *refs):
-        slots, values, out_ref, total = refs[:count], refs[count : 2 * count], refs[-2], refs[-1]
-        n = pl.program_id(0)
-        left = jnp.concatenate([r[0] for r in slots], axis=0)
-        right = jnp.concatenate([r[...] for r in values], axis=0)
-        product = dot(left, right, (1, 1))
-
-        @pl.when(n == 0)
-        def _():
-            total[...] = product
-
-        @pl.when(n > 0)
-        def _():
-            total[...] += product
-
-        @pl.when(n == pl.num_programs(0) - 1)
-        def _():
-            for at, place in enumerate(places):
-                part = total[at * rank : (at + 1) * rank, at * rows : (at + 1) * rows]
-                alive = lax.broadcasted_iota(jnp.int32, (rank, rows), 1) < facts_ref[groups + place]
-                alive = alive & (facts_ref[place] >= 0)
-                part = jnp.where(alive, part * adapter_scale, 0.0)
-                if earlier:
-                    part += refs[2 * count][:, at * rows : (at + 1) * rows]
-                out_ref[:, at * rows : (at + 1) * rows] = part
-
-    def chosen_slot(place):
-        return lambda n, facts_ref: (jnp.maximum(facts_ref[place], 0), 0, n + base)
-
-    small = pl.BlockSpec((rank, count * rows), lambda n, facts_ref: (0, 0))
-    return pl.pallas_call(
-        kernel,
-        grid_spec=pltpu.PrefetchScalarGridSpec(
-            num_scalar_prefetch=1,
-            grid=(columns // block,),
-            in_specs=[pl.BlockSpec((1, rank, block), chosen_slot(place)) for place in places]
-            + [pl.BlockSpec((rows, block), lambda n, facts_ref: (0, n))] * count
-            + [small] * len(earlier),
-            out_specs=small,
-            scratch_shapes=[pltpu.VMEM((count * rank, count * rows), jnp.float32)],
-        ),
-        out_shape=jax.ShapeDtypeStruct((rank, count * rows), jnp.float32),
-        compiler_params=pltpu.CompilerParams(vmem_limit_bytes=VMEM),
-        cost_estimate=cost(2 * count * rank * count * rows * columns, 2 * columns * count * (rank + rows)),
-        name="rank_back",
-    )(facts, *[store] * count, *blocks, *earlier)
-
-
 def spread(facts, here, there, slots, scale):
     rank, tokens = here.shape
     groups = facts.shape[0] // 2
@@ -230,7 +190,9 @@
             for s in range(slots):
                 value = jnp.where(facts_ref[q] == s, part, 0.0)
                 wide_ref[s * rank : (s + 1) * rank, q * rows : (q + 1) * rows] = value.astype(jnp.bfloat16)
-        turned_ref[...] = wide_ref[...].astype(jnp.float32).T.astype(jnp.bfloat16)
+        for n, q in enumerate((0, 2, 1, 3)):
+            part = wide_ref[:, q * rows : (q + 1) * rows]
+            turned_ref[n * rows : (n + 1) * rows] = part.astype(jnp.float32).T.astype(jnp.bfloat16)
 
     return pl.pallas_call(
         kernel,
@@ -282,7 +244,7 @@
         out_specs=pl.BlockSpec((span, block), lambda n: (0, n)),
         out_shape=jax.ShapeDtypeStruct((span, columns), jnp.float32),
         compiler_params=pltpu.CompilerParams(vmem_limit_bytes=VMEM),
-        cost_estimate=cost(2 * span * tokens * columns, (4 * span + 2 * tokens) * columns, 1),
+        cost_estimate=cost(2 * span * tokens * columns, (4 * span + 2 * tokens) * columns),
         name="slot_grad",
     )(wide_t, *arrays)
 
@@ -391,51 +353,55 @@
 
     tok_x = swap(tokens, CHIP)
     cot_c = swap(cotangent, CORE)
-    middle = hidden // 2
-    cot_a = swap(after(cotangent[:, :middle], tok_x), CHIP)
-    cot_b = swap(after(cotangent[:, middle:], tok_x), CHIP)
-    far = i ^ j
-    here = jnp.stack([i, jnp.minimum(jnp.where(far == 2, 1, 2 * (far & 1)), 2)]).astype(jnp.int32)
+    middle, half = hidden // 2, depth // 2
+    away = i ^ j
+    here = jnp.stack([i, away]).astype(jnp.int32)
     down_t = jnp.swapaxes(adapter_down, 1, 2)
     near, rest, facts = choose(block_adapter, block_length, adapter_slot, here, down_t)
     up_flat = adapter_up.reshape(span, hidden)
-    half = depth // 2
-
-    even = jnp.concatenate([tokens, after(tok_x, facts)], axis=0)
+    near = swap(near, CORE)
+
+    back01, *grads = return_grad(
+        facts, after(cotangent, near), cot_c, weight, adapter_up, (0, 1), (0, half), (0, hidden), 1024
+    )
+    down_x = swap(rest[:rank] + near[rank:], CHIP)
+    even = jnp.concatenate([tokens, after(tok_x, grads[0], down_x)], axis=0)
     odd = swap(even, CORE)
     even_far = both(even, hop)
-    grad01, parts = return_grad(after(cotangent, even), cot_c, weight, 0, (0, depth), (0, hidden))
+    cot_a = swap(after(cotangent[:, :middle], even), CHIP)
+    cot_b = swap(after(cotangent[:, middle:], even), CHIP)
+    _, grad01, parts = return_grad(
+        facts, after(cotangent, even), cot_c, weight, adapter_up, (0, 1), (half, depth), (0, hidden), 1024, grads=grads
+    )
     odd = after(odd, grad01)
     odd_far = both(odd, hop)
     toks = [(even, 0), (odd, 0), (even, 1), (odd, 1)]
     inner = rank_inner(facts, down_t.reshape(span, width), toks, rank)
+    down_mine = both(rest[rank:] + near[:rank] + down_x, place)
     cot_ac = swap(after(cot_a, inner), CORE)
-    back01 = rank_back(facts, after(adapter_up, inner, cot_a), [cotangent, cot_c], (0, 1), hidden // 4)
-    inner = after(inner, back01) + along(inner, 1)
+    inner = inner + along(inner, 1)
     inner_far = along(inner, 2)
-    even_mid = jnp.where(i == j, even, after(even_far, inner))
+    even_mid = jnp.where(away == 0, even, after(even_far, inner, down_mine))
     even_all = both(even_mid, hops)
-    near = swap(after(near, cot_a), CORE)
-    grad23, = return_grad(
-        after(cot_a, even_mid), cot_ac, weight, 1, (0, depth), (0, middle), send=False
-    )
-    back23 = rank_back(facts, after(adapter_up, grad23), [cot_a, cot_ac], (2, 3), hidden // 4)
-    cot_bc = swap(after(cot_b, back23), CORE)
-    odd_mid = jnp.where(i == j, odd, after(odd_far, back23, cot_b))
+    back23, sums = return_grad(
+        facts, after(cot_a, even_mid), cot_ac, weight, adapter_up, (2, 3), (0, depth), (0, middle), 512, finish=False
+    )
+    cot_bc = swap(after(cot_b, sums), CORE)
+    odd_mid = jnp.where(away == 0, odd, after(odd_far, sums, cot_b))
     odd_all = both(odd_mid, hops)
-    down_x = rest[:rank] + near[rank:]
-    grad23, parts = return_grad(
-        after(cot_b, odd_mid, even_all, down_x), cot_bc, weight, 1, (0, depth), (middle, hidden), (grad23, parts), added=True
-    )
-    back23 = rank_back(facts, after(adapter_up, grad23), [cot_b, cot_bc], (2, 3), hidden // 4, middle, back23)
+    back23, grad23, parts = return_grad(
+        facts, after(cot_b, odd_mid, even_all), cot_bc, weight, adapter_up, (2, 3), (0, depth), (middle, hidden), 512,
+        before=(sums, back23), grads=(parts,),
+    )
     back = jnp.concatenate([back01, back23], axis=1)
     back = back + along(back, 1)
-    down_x = swap(after(down_x, cot_b), CHIP)
-    back_wide, _, back_b = spread(facts, after(back, down_x), along(back, 2), per_owner, 1.0)
+    all_even = jnp.where(away == 0, even, jnp.where(away == 2, even_far, after(even_all, back)))
+    back_wide, _, back_b = spread(facts, after(back, all_even), along(back, 2), per_owner, 1.0)
     inner_wide, inner_rows, _ = spread(facts, after(inner, back_b), inner_far, per_owner, adapter_scale)
     back_b = share(after(back_b, inner_wide), swap(back_b, CORE), CORE)
     parts = lax.all_to_all(after(parts, back_b).reshape(shards, rows, depth), "tp", 0, 0, tiled=True)
-    down_mine = both(rest[rank:] + near[:rank] + after(down_x, back_b), place)
+    all_odd = jnp.where(away == 0, odd, jnp.where(away == 2, odd_far, after(odd_all, back_b)))
+    all_tokens = jnp.concatenate([all_even, all_odd], axis=0)
 
     def grad_block(q):
         low, high = [lax.dynamic_slice_in_dim(x, (q & 1) * rows, rows, 0) for x in (grad01, grad23)]
@@ -448,25 +414,26 @@
     kept, sent, got_c, got_x, done = [], [], [], [], []
 
     def make(n, *points):
-        keep, send = project(facts, [(even, even_far, even_all), (odd, odd_far, after(odd_all, *points))], inner_rows, weight, up_flat, edges[n], edges[n + 1], block)
+        keep, send = project(after(all_tokens, *points), inner_rows, weight, up_flat, edges[n], edges[n + 1], block)
         kept.append(keep)
         got_c.append(swap(send, CORE))
         return keep
 
     def cross(n, *points):
-        summed = (after(kept[n], *points)[1] + got_c[n][1]).astype(b16)
+        summed = (after(kept[n], *points)[rows:] + got_c[n][rows:]).astype(b16)
         got_x.append(swap(summed, CHIP))
         return summed
 
     def finish(n, *points):
-        done.append((after(kept[n], *points)[0] + got_c[n][0] + got_x[n].astype(jnp.float32)).astype(b16))
+        own = after(kept[n], *points)[:rows] + got_c[n][:rows] + got_x[n].astype(jnp.float32)
+        done.append(own.astype(b16))
         return done[-1]
 
     point = make(0, back_b)
     back_b = share(after(back_b, point), swap(back_b, CHIP), CHIP)
     point = make(1, point)
     point = cross(0, point)
-    point = make(2, point, down_mine, back_b)
+    point = make(2, point, back_b)
     point = finish(0, point)
     point = cross(1, point)
     point = make(3, point)

time: 252 us -> 248 us (0.984); the launches traced: 248 us -> 247 us
  starting transfers between devices: 28.6 us -> 34.1 us
  waiting for transfers between devices: 73.8 us -> 68.4 us
  other arithmetic: 16.2 us -> 20.6 us
  local copies, waits for them, and re-layouts: 25.7 us -> 22.9 us
    ppermute x6, waiting for transfers between devices: 39.8 us -> 24.8 us  [both(): return lax.ppermute(x, ('tp', 'dp'), pairs)]
    ppermute x4, waiting for transfers between devices: 10.5 us -> 20.1 us  [along(): return lax.ppermute(x, 'tp', [(z, z ^ bit) for z in range(shards)])]
    ppermute x6, starting transfers between devices: 10.9 us -> 19.4 us  [both(): return lax.ppermute(x, ('tp', 'dp'), pairs)]
    select_n x2 -> x4, other arithmetic: 0.22 us -> 4.17 us  [the longest x1 1.52 us: local_square(): jnp.where(away == 0, even, jnp.where(away == 2, even_far, after(even_all,...]
    unnamed x96 -> x101, local copies, waits for them, and re-layouts: 22.8 us -> 21.8 us
    pallas_call x6 -> x4, Pallas kernels: 48.1 us -> 48 us  [return_grad(): pl.pallas_call(kernel, grid_spec=pltpu.PrefetchScalarGridSpec(num_scalar_...]
  transfers between devices with their start and end apart: 30 -> 30, of which waited for: 9 -> 11; matrix products, arithmetic and copies ran while one was open for 9% -> 10% of each run, Pallas kernels for 37% -> 31%
where the time goes in v7:
time: 248 us; the launch traced here: 247 us
  Pallas kernels  97.3 us (39%)
  waiting for transfers between devices  68.4 us (28%)
  starting transfers between devices  34.1 us (14%)
  local copies, waits for them, and re-layouts  22.9 us (9%)
  other arithmetic  20.6 us (8%)
    pallas_call x4, Pallas kernels, return_grad(): pl.pallas_call(kernel, grid_spec=pltpu.PrefetchScalarGridSpec(num_scalar_...  48 us
    pallas_call x4, Pallas kernels, project(): pl.pallas_call(kernel, grid=((stop - start) // block,), in_specs=[pl.Bloc...  30.8 us
    ppermute x6, waiting for transfers between devices, both(): return lax.ppermute(x, ('tp', 'dp'), pairs)  24.8 us
    ppermute x19, waiting for transfers between devices, swap(): return lax.ppermute(x, 'dp', [(d, d ^ bit) for d in range(groups)])  23.4 us
    unnamed x101, local copies, waits for them, and re-layouts  21.8 us
    ppermute x4, waiting for transfers between devices, along(): return lax.ppermute(x, 'tp', [(z, z ^ bit) for z in range(shards)])  20.1 us
    ppermute x6, starting transfers between devices, both(): return lax.ppermute(x, ('tp', 'dp'), pairs)  19.4 us
    pallas_call x2, Pallas kernels, slot_grad(): pl.pallas_call(kernel, grid=(columns // block,), in_specs=[pl.BlockSpec((...  12.1 us
  transfers between devices with their start and end apart: 30, of which 11 were waited for; matrix products, arithmetic and copies ran while one was open for 10% of the time, Pallas kernels for 31%

profile of v7, /device:TPU:2, one launch (start us, length us, event | category | flops | bytes accessed | tf_op | source)
XLA Modules:
  0.0 246.8 jit_solution(7128484028118347992)
XLA Ops:
  0.8 1.7 copy-done.13
  2.5 0.7 copy-done.34
  3.2 0.7 copy-done.35
  4.5 1.5 choose.1
  6.4 1.5 collective-permute-done.1
  8.6 3.1 %copy-done = bf16[8,64,7168]{2,1,0:T(8,128)(2,1)S(1)} copy-done((bf16[8,64,7168]{2,1,0:T(8,128)(2,1)S(1)}, bf16[8,64,7168]{2,1,0:T(8,128)(2,1)}, u32[]{:S(2)}) %copy-start) | copy-done | bytes 7340056
  11.7 11.9 %return_grad.4 = (f32[64,256]{1,0:T(8,128)S(1)}, f32[256,2048]{1,0:T(8,128)S(1)}, bf16[512,2048]{1,0:T(8,128)(2,1)S(1)}) custom-call(s32[9]{0:T(128)S(1)} %get-tuple-element.63.facts_ref, bf16[128,7168]{1,0:T(8,128)(2,1)S(1)} %copy-done.5, bf16[128,7168]{1,0:T(8,128)(2,1)} %collective-permute-done.2.b_ref.refs_1_, bf16[2048,7168]{1,0:T(8,128)(2,1)} %w_ref.15, ...), custom_call_target="tpu_custom_call" | custom-call | flops 58720256 | bytes 286720 | tf_op jit(solution)/shard_map/return_grad/pallas_call | solution.py:120
  23.7 2.5 %collective-permute-done.3 = bf16[64,2048]{1,0:T(8,128)(2,1)S(1)} collective-permute-done((bf16[64,2048]{1,0:T(8,128)(2,1)S(1)}, bf16[64,2048]{1,0:T(8,128)(2,1)S(1)}, u32[]{:S(2)}, u32[]{:S(2)}) %collective-permute-start.3) | collective-permute-done | bytes 262176 | tf_op jit(solution)/shard_map/ppermute | solution.py:339
  26.3 1.0 fusion.16
  27.7 1.3 collective-permute-start.4
  29.0 12.5 %return_grad.5 = (f32[64,256]{1,0:T(8,128)}, f32[256,2048]{1,0:T(8,128)S(1)}, bf16[512,2048]{1,0:T(8,128)(2,1)S(1)}) custom-call(s32[9]{0:T(128)S(1)} %get-tuple-element.63.facts_ref, bf16[128,7168]{1,0:T(8,128)(2,1)S(1)} %copy-done.6, bf16[128,7168]{1,0:T(8,128)(2,1)} %collective-permute-done.2.b_ref.refs_1_, ...), custom_call_target="tpu_custom_call", output_to_operand_aliasing={{1}: (6, {}), {2}: (7, {})} | custom-call | flops 58720256 | bytes 286720 | tf_op jit(solution)/shard_map/return_grad/pallas_call | solution.py:120
  41.5 1.8 rank_inner.1
  43.5 6.7 %collective-permute-done.11.a_ref.refs_2_ = bf16[128,3584]{1,0:T(8,128)(2,1)S(1)} collective-permute-done((bf16[128,3584]{1,0:T(8,128)(2,1)S(1)}, bf16[128,3584]{1,0:T(8,128)(2,1)S(1)}, u32[]{:S(2)}, u32[]{:S(2)}) %collective-permute-start.11) | collective-permute-done | bytes 917536 | tf_op jit(solution)/shard_map/ppermute | solution.py:339
  50.1 0.8 fusion.13
  51.0 4.5 %collective-permute-start.7 = (bf16[64,2048]{1,0:T(8,128)(2,1)}, bf16[64,2048]{1,0:T(8,128)(2,1)}, u32[]{:S(2)}, u32[]{:S(2)}) collective-permute-start(bf16[64,2048]{1,0:T(8,128)(2,1)} %fusion.13), channel_id=1, source_target_pairs={{0,0},{4,5},{8,10},{12,15},{1,4},{5,1},{9,14},{13,11},{2,8},{6,13}... | collective-permute-start | bytes 786440 | tf_op jit(solution)/shard_map/ppermute | solution.py:352
  55.5 1.7 collective-permute-start.6
  57.2 7.6 %collective-permute-done.6 = f32[64,512]{1,0:T(8,128)S(1)} collective-permute-done((f32[64,512]{1,0:T(8,128)S(1)}, f32[64,512]{1,0:T(8,128)S(1)}, u32[]{:S(2)}, u32[]{:S(2)}) %collective-permute-start.6) | collective-permute-done | bytes 131104 | tf_op jit(solution)/shard_map/ppermute | solution.py:342
  64.8 1.3 collective-permute-start.10
  66.1 2.3 collective-permute-done.7
  68.4 1.3 broadcast_select_fusion.1
  69.7 3.1 %collective-permute-start.8 = (bf16[256,2048]{1,0:T(8,128)(2,1)S(1)}, bf16[256,2048]{1,0:T(8,128)(2,1)}, u32[]{:S(2)}, u32[]{:S(2)}) collective-permute-start(bf16[256,2048]{1,0:T(8,128)(2,1)S(1)} %broadcast_select_fusion.1), channel_id=1, source_target_pairs={{0,4},{8,12},{5,1},{13,9},{10,14},{2,6},{15,11},{7,3},{16,20},{24,... | collective-permute-start | bytes 3145736 | tf_op jit(solution)/shard_map/ppermute | solution.py:352
  72.9 3.1 %copy-done.1 = bf16[8,64,7168]{2,1,0:T(8,128)(2,1)S(1)} copy-done((bf16[8,64,7168]{2,1,0:T(8,128)(2,1)S(1)}, bf16[8,64,7168]{2,1,0:T(8,128)(2,1)}, u32[]{:S(2)}) %copy-start.1) | copy-done | bytes 7340056
  76.0 11.5 %return_grad.6 = (f32[64,256]{1,0:T(8,128)S(1)}, f32[2048,256]{1,0:T(8,128)S(1)}) custom-call(s32[9]{0:T(128)S(1)} %get-tuple-element.63.facts_ref, bf16[128,3584]{1,0:T(8,128)(2,1)S(1)} %collective-permute-done.11.a_ref.refs_2_, bf16[128,3584]{1,0:T(8,128)(2,1)} %collective-permute-done.12.b_ref.refs_4_, bf16[2048,7168]{1,0:T(8,128)(2,1)} %w_ref.15, ...), custom_call_target="tpu_custom_call" | custom-call | flops 58720256 | bytes 258048 | tf_op jit(solution)/shard_map/return_grad/pallas_call | solution.py:120
  87.6 6.0 %collective-permute-done.10 = bf16[256,2048]{1,0:T(8,128)(2,1)S(1)} collective-permute-done((bf16[256,2048]{1,0:T(8,128)(2,1)S(1)}, bf16[256,2048]{1,0:T(8,128)(2,1)S(1)}, u32[]{:S(2)}, u32[]{:S(2)}) %collective-permute-start.10) | collective-permute-done | bytes 1048608 | tf_op jit(solution)/shard_map/ppermute | solution.py:352
  93.6 1.2 broadcast_select_fusion
  94.9 12.0 %return_grad.7 = (f32[64,256]{1,0:T(8,128)S(1)}, f32[256,2048]{1,0:T(8,128)S(1)}, bf16[512,2048]{1,0:T(8,128)(2,1)S(1)}) custom-call(s32[9]{0:T(128)S(1)} %get-tuple-element.63.facts_ref, bf16[128,3584]{1,0:T(8,128)(2,1)} %collective-permute-done.9.a_ref.refs_3_, ...), custom_call_target="tpu_custom_call", output_to_operand_aliasing={{2}: (8, {})} | custom-call | flops 58720256 | bytes 258048 | tf_op jit(solution)/shard_map/return_grad/pallas_call | solution.py:120
  107.0 1.3 copy-done.10
  108.3 1.3 copy-done.29
  109.7 4.1 %collective-permute-start.15 = (bf16[256,2048]{1,0:T(8,128)(2,1)}, bf16[256,2048]{1,0:T(8,128)(2,1)S(1)}, u32[]{:S(2)}, u32[]{:S(2)}) collective-permute-start(bf16[256,2048]{1,0:T(8,128)(2,1)} %broadcast_select_fusion), channel_id=1, source_target_pairs={{0,4},{8,12},{5,1},{13,9},{10,14},{2,6},{15,11},{7,3},{16,20},{24,... | collective-permute-start | bytes 3145736 | tf_op jit(solution)/shard_map/ppermute | solution.py:352
  113.8 2.0 collective-permute-done.14
  115.8 1.0 collective-permute-start.16
  116.9 1.5 select_select_fusion.1
  118.4 10.5 %collective-permute-done.16.refs_1_ = f32[64,512]{1,0:T(8,128)S(1)} collective-permute-done((f32[64,512]{1,0:T(8,128)S(1)}, f32[64,512]{1,0:T(8,128)S(1)}, u32[]{:S(2)}, u32[]{:S(2)}) %collective-permute-start.16) | collective-permute-done | bytes 131104 | tf_op jit(solution)/shard_map/ppermute | solution.py:342
  128.9 1.7 spread.2
  130.6 0.8 copy-done.30
  131.4 1.4 spread.3
  132.8 0.8 copy-done.32
  134.0 1.7 slice-done.1
  135.7 8.0 %project.4 = (f32[256,2048]{1,0:T(8,128)S(1)}, f32[256,2048]{1,0:T(8,128)S(1)}) custom-call(bf16[512,2048]{1,0:T(8,128)(2,1)S(1)} %pad_maximum_fusion.tok_ref, bf16[512,512]{1,0:T(8,128)(2,1)S(1)} %get-tuple-element.94.wide_ref, bf16[2048,7168]{1,0:T(8,128)(2,1)} %w_ref.15, bf16[512,7168]{1,0:T(8,128)(2,1)S(1)} %bitcast.23), custom_call_target="tpu_custom_call" | custom-call | flops 83886080 | bytes 229376 | tf_op jit(solution)/shard_map/project/pallas_call | solution.py:40
  144.3 7.4 %project.5 = (f32[256,1536]{1,0:T(8,128)S(1)}, f32[256,1536]{1,0:T(8,128)}) custom-call(bf16[512,2048]{1,0:T(8,128)(2,1)S(1)} %pad_maximum_fusion.tok_ref, bf16[512,512]{1,0:T(8,128)(2,1)S(1)} %get-tuple-element.94.wide_ref, bf16[2048,7168]{1,0:T(8,128)(2,1)} %w_ref.15, bf16[512,7168]{1,0:T(8,128)(2,1)S(1)} %bitcast.24), custom_call_target="tpu_custom_call" | custom-call | flops 62914560 | bytes 172032 | tf_op jit(solution)/shard_map/project/pallas_call | solution.py:40
  152.3 1.1 fusion.6
  153.4 1.9 collective-permute-start.21
  155.3 4.7 %all-to-all-start = ((bf16[4,128,2048]{2,1,0:T(8,128)(2,1)}), bf16[4,128,2048]{2,1,0:T(8,128)(2,1)}, u32[]{:S(2)}, u32[]{:S(2)}) async-start(bf16[4,128,2048]{2,1,0:T(8,128)(2,1)} %bitcast.27), calls=%async_computation | async-start | bytes 4194304 | tf_op jit(solution)/shard_map/all_to_all | solution.py:402
  160.0 3.1 %copy-done.2 = bf16[8,64,7168]{2,1,0:T(8,128)(2,1)S(1)} copy-done((bf16[8,64,7168]{2,1,0:T(8,128)(2,1)S(1)}, bf16[8,64,7168]{2,1,0:T(8,128)(2,1)}, u32[]{:S(2)}) %copy-start.2) | copy-done | bytes 7340056
  163.1 1.0 copy-done.12
  164.1 8.2 %project.6 = (f32[256,2048]{1,0:T(8,128)S(1)}, f32[256,2048]{1,0:T(8,128)S(1)}) custom-call(bf16[512,2048]{1,0:T(8,128)(2,1)S(1)} %pad_maximum_fusion.tok_ref, bf16[512,512]{1,0:T(8,128)(2,1)S(1)} %copy-done.12, bf16[2048,7168]{1,0:T(8,128)(2,1)} %w_ref.15, bf16[512,7168]{1,0:T(8,128)(2,1)S(1)} %bitcast.25), custom_call_target="tpu_custom_call" | custom-call | flops 83886080 | bytes 229376 | tf_op jit(solution)/shard_map/project/pallas_call | solution.py:40
  172.4 2.8 %fusion.5 = bf16[128,2048]{1,0:T(8,128)(2,1)} fusion(f32[256,2048]{1,0:T(8,128)S(1)} %copy-done.42, bf16[128,2048]{1,0:T(8,128)(2,1)} %collective-permute-done.21, f32[256,2048]{1,0:T(8,128)S(1)} %copy-done.24), kind=kLoop, calls=%fused_computation.11 | loop fusion | flops 1048576 | bytes 3145728 | tf_op jit(solution)/shard_map/convert_element_type | solution.py:429
  175.3 1.2 fusion.12
  176.5 7.3 %project.7 = (f32[256,1536]{1,0:T(8,128)S(1)}, f32[256,1536]{1,0:T(8,128)}) custom-call(bf16[512,2048]{1,0:T(8,128)(2,1)S(1)} %pad_maximum_fusion.tok_ref, bf16[512,512]{1,0:T(8,128)(2,1)S(1)} %copy-done.12, bf16[2048,7168]{1,0:T(8,128)(2,1)} %w_ref.15, bf16[512,7168]{1,0:T(8,128)(2,1)S(1)} %bitcast.26), custom_call_target="tpu_custom_call" | custom-call | flops 62914560 | bytes 172032 | tf_op jit(solution)/shard_map/project/pallas_call | solution.py:40
  184.2 11.1 %collective-permute-done.23 = bf16[128,1536]{1,0:T(8,128)(2,1)S(1)} collective-permute-done((bf16[128,1536]{1,0:T(8,128)(2,1)S(1)}, bf16[128,1536]{1,0:T(8,128)(2,1)S(1)}, u32[]{:S(2)}, u32[]{:S(2)}) %collective-permute-start.23) | collective-permute-done | bytes 393248 | tf_op jit(solution)/shard_map/ppermute | solution.py:339
  195.3 2.0 fusion.11
  197.4 0.9 fusion.3
  199.3 2.3 fusion.9
  201.6 1.6 collective-permute-start.27
  203.2 9.2 %slot_grad.2 = f32[512,7168]{1,0:T(8,128)} custom-call(bf16[512,512]{1,0:T(8,128)(2,1)S(1)} %copy-done.33, bf16[128,7168]{1,0:T(8,128)(2,1)S(1)} %copy-done.7, bf16[128,7168]{1,0:T(8,128)(2,1)} %collective-permute-done.2.b_ref.refs_1_, bf16[128,3584]{1,0:T(8,128)(2,1)S(1)} %copy-done.18, bf16[128,3584]{1,0:T(8,128)(2,1)} %collective-permute-done.9.a_ref.refs_3_, ...), custom_call_target="tpu_custom_call" | custom-call | flops 58720256 | bytes 344064 | tf_op jit(solution)/shard_map/slot_grad/pallas_call | solution.py:240
  212.4 1.6 collective-permute-done.26
  214.0 2.0 fusion.2
  216.0 2.3 fusion
  218.3 5.2 %collective-permute-start.28 = (bf16[128,2048]{1,0:T(8,128)(2,1)S(1)}, bf16[128,2048]{1,0:T(8,128)(2,1)S(1)}, u32[]{:S(2)}, u32[]{:S(2)}) collective-permute-start(bf16[128,2048]{1,0:T(8,128)(2,1)S(1)} %fusion), channel_id=1, source_target_pairs={{0,0},{5,4},{10,8},{15,12},{4,1},{1,5},{14,9},{11,13},{8,2},{13,6}... | collective-permute-start | bytes 1572872 | tf_op jit(solution)/shard_map/ppermute | solution.py:352
  223.5 2.9 %slot_grad.3 = f32[512,2048]{1,0:T(8,128)} custom-call(bf16[512,512]{1,0:T(8,128)(2,1)S(1)} %copy-done.31, bf16[256,2048]{1,0:T(8,128)(2,1)S(1)} %constant_dynamic-update-slice_fusion.refs_0_.refs_2_, bf16[256,2048]{1,0:T(8,128)(2,1)S(1)} %copy-done.4, bf16[256,2048]{1,0:T(8,128)(2,1)S(1)} %constant_dynamic-update-slice_fusion.refs_0_.refs_2_, ...), custom_call_target="tpu_custom_call" | custom-call | flops 16777216 | bytes 98304 | tf_op jit(solution)/shard_map/slot_grad/pallas_call | solution.py:240
  226.5 1.5 fusion.8
  228.1 1.4 pad_maximum_fusion.1
  229.5 16.5 %collective-permute-done.28 = bf16[128,2048]{1,0:T(8,128)(2,1)S(1)} collective-permute-done((bf16[128,2048]{1,0:T(8,128)(2,1)S(1)}, bf16[128,2048]{1,0:T(8,128)(2,1)S(1)}, u32[]{:S(2)}, u32[]{:S(2)}) %collective-permute-start.28) | collective-permute-done | bytes 524320 | tf_op jit(solution)/shard_map/ppermute | solution.py:352
  246.1 0.8 copy.21
  (139 shorter events, 6.2 us)
Async XLA Ops:
  0.6 8.0 %copy-start.5 = (bf16[128,7168]{1,0:T(8,128)(2,1)S(1)}, bf16[128,7168]{1,0:T(8,128)(2,1)}, u32[]{:S(2)}) copy-start(bf16[128,7168]{1,0:T(8,128)(2,1)} %refs_0_.1) | copy-start | bytes 5505028
  0.6 8.0 %collective-permute-start.2 = (bf16[128,7168]{1,0:T(8,128)(2,1)}, bf16[128,7168]{1,0:T(8,128)(2,1)}, u32[]{:S(2)}, u32[]{:S(2)}) collective-permute-start(bf16[128,7168]{1,0:T(8,128)(2,1)} %refs_0_.1), channel_id=1, source_target_pairs={{0,1},{1,0},{2,3},{3,2},{4,5},{5,4},{6,7},{7,6},{8,9},{9,8},{10,11... | collective-permute-start | bytes 5505032 | tf_op jit(solution)/shard_map/ppermute | solution.py:339
  4.5 4.1 %copy-start.46 = (bf16[128,2048]{1,0:T(8,128)(2,1)S(1)}, bf16[128,2048]{1,0:T(8,128)(2,1)}, u32[]{:S(2)}) copy-start(bf16[128,2048]{1,0:T(8,128)(2,1)} %param.8) | copy-start | bytes 1572868
  6.0 2.0 collective-permute-start.1
  6.4 17.2 %collective-permute-start = (bf16[128,2048]{1,0:T(8,128)(2,1)}, bf16[128,2048]{1,0:T(8,128)(2,1)S(1)}, u32[]{:S(2)}, u32[]{:S(2)}) collective-permute-start(bf16[128,2048]{1,0:T(8,128)(2,1)} %param.8), channel_id=1, source_target_pairs={{0,2},{1,3},{2,0},{3,1},{4,6},{5,7},{6,4},{7,5},{8,10},{9,11},{10,... | collective-permute-start | bytes 1572872 | tf_op jit(solution)/shard_map/ppermute | solution.py:339
  8.0 18.2 %collective-permute-start.3 = (bf16[64,2048]{1,0:T(8,128)(2,1)S(1)}, bf16[64,2048]{1,0:T(8,128)(2,1)S(1)}, u32[]{:S(2)}, u32[]{:S(2)}) collective-permute-start(bf16[64,2048]{1,0:T(8,128)(2,1)S(1)} %slice_add_fusion.9), channel_id=1, source_target_pairs={{0,2},{1,3},{2,0},{3,1},{4,6},{5,7},{6,4},{7,5},{8,10},{9,11},{10,... | collective-permute-start | bytes 786440 | tf_op jit(solution)/shard_map/ppermute | solution.py:339
  8.6 3.1 %copy-start = (bf16[8,64,7168]{2,1,0:T(8,128)(2,1)S(1)}, bf16[8,64,7168]{2,1,0:T(8,128)(2,1)}, u32[]{:S(2)}) copy-start(bf16[8,64,7168]{2,1,0:T(8,128)(2,1)} %up_b_ref.7) | copy-start | bytes 22020100
  11.7 14.6 %copy-start.6 = (bf16[128,7168]{1,0:T(8,128)(2,1)S(1)}, bf16[128,7168]{1,0:T(8,128)(2,1)}, u32[]{:S(2)}) copy-start(bf16[128,7168]{1,0:T(8,128)(2,1)} %refs_0_.1) | copy-start | bytes 5505028
  26.3 15.2 %collective-permute-start.5 = (bf16[256,2048]{1,0:T(8,128)(2,1)S(1)}, bf16[256,2048]{1,0:T(8,128)(2,1)S(1)}, u32[]{:S(2)}, u32[]{:S(2)}) collective-permute-start(bf16[256,2048]{1,0:T(8,128)(2,1)S(1)} %constant_dynamic-update-slice_fusion.refs_0_.refs_2_), channel_id=1, source_target_pairs={{0,1},{1,0},{2,3},{3,2},{4,5},{5,4},{6,7},{7,6},{8,9},{9,8},{10,11... | collective-permute-start | bytes 3145736 | tf_op jit(solution)/shard_map/ppermute | solution.py:339
  27.4 22.7 %collective-permute-start.11 = (bf16[128,3584]{1,0:T(8,128)(2,1)S(1)}, bf16[128,3584]{1,0:T(8,128)(2,1)S(1)}, u32[]{:S(2)}, u32[]{:S(2)}) collective-permute-start(bf16[128,3584]{1,0:T(8,128)(2,1)S(1)} %get-tuple-element.76), channel_id=1, source_target_pairs={{0,2},{1,3},{2,0},{3,1},{4,6},{5,7},{6,4},{7,5},{8,10},{9,11},{10,... | collective-permute-start | bytes 2752520 | tf_op jit(solution)/shard_map/ppermute | solution.py:339
  27.7 40.7 %collective-permute-start.4 = (bf16[256,2048]{1,0:T(8,128)(2,1)S(1)}, bf16[256,2048]{1,0:T(8,128)(2,1)}, u32[]{:S(2)}, u32[]{:S(2)}) collective-permute-start(bf16[256,2048]{1,0:T(8,128)(2,1)S(1)} %constant_dynamic-update-slice_fusion.refs_0_.refs_2_), channel_id=1, source_target_pairs={{0,8},{5,13},{10,2},{15,7},{16,24},{21,29},{26,18},{31,23}} | collective-permute-start | bytes 3145736 | tf_op jit(solution)/shard_map/ppermute | solution.py:352
  29.0 12.5 %copy-start.14 = (bf16[8,2048,64]{1,2,0:T(8,128)(2,1)S(1)}, bf16[8,2048,64]{1,2,0:T(8,128)(2,1)}, u32[]{:S(2)}) copy-start(bf16[8,2048,64]{1,2,0:T(8,128)(2,1)} %param.10) | copy-start | bytes 6291460
  41.5 1.9 copy-start.8
  41.5 2.0 copy-start.15
  41.5 92.2 %copy-start.3 = (bf16[256,2048]{1,0:T(8,128)(2,1)}, bf16[256,2048]{1,0:T(8,128)(2,1)S(1)}, u32[]{:S(2)}) copy-start(bf16[256,2048]{1,0:T(8,128)(2,1)S(1)} %collective-permute-done.5.refs_1_.refs_3_) | copy-start | bytes 3145732
  50.1 22.7 %copy-start.17 = (bf16[128,3584]{1,0:T(8,128)(2,1)}, bf16[128,3584]{1,0:T(8,128)(2,1)S(1)}, u32[]{:S(2)}) copy-start(bf16[128,3584]{1,0:T(8,128)(2,1)S(1)} %collective-permute-done.11.a_ref.refs_2_) | copy-start | bytes 2752516
  50.1 22.7 %collective-permute-start.12 = (bf16[128,3584]{1,0:T(8,128)(2,1)S(1)}, bf16[128,3584]{1,0:T(8,128)(2,1)}, u32[]{:S(2)}, u32[]{:S(2)}) collective-permute-start(bf16[128,3584]{1,0:T(8,128)(2,1)S(1)} %collective-permute-done.11.a_ref.refs_2_), channel_id=1, source_target_pairs={{0,1},{1,0},{2,3},{3,2},{4,5},{5,4},{6,7},{7,6},{8,9},{9,8},{10,11... | collective-permute-start | bytes 2752520 | tf_op jit(solution)/shard_map/ppermute | solution.py:339
  51.0 17.4 %collective-permute-start.7 = (bf16[64,2048]{1,0:T(8,128)(2,1)}, bf16[64,2048]{1,0:T(8,128)(2,1)}, u32[]{:S(2)}, u32[]{:S(2)}) collective-permute-start(bf16[64,2048]{1,0:T(8,128)(2,1)} %fusion.13), channel_id=1, source_target_pairs={{0,0},{4,5},{8,10},{12,15},{1,4},{5,1},{9,14},{13,11},{2,8},{6,13}... | collective-permute-start | bytes 786440 | tf_op jit(solution)/shard_map/ppermute | solution.py:352
  55.4 32.1 %collective-permute-start.9 = (bf16[128,3584]{1,0:T(8,128)(2,1)}, bf16[128,3584]{1,0:T(8,128)(2,1)}, u32[]{:S(2)}, u32[]{:S(2)}) collective-permute-start(bf16[128,3584]{1,0:T(8,128)(2,1)} %get-tuple-element.75), channel_id=1, source_target_pairs={{0,2},{1,3},{2,0},{3,1},{4,6},{5,7},{6,4},{7,5},{8,10},{9,11},{10,... | collective-permute-start | bytes 2752520 | tf_op jit(solution)/shard_map/ppermute | solution.py:339
  55.5 9.3 %collective-permute-start.6 = (f32[64,512]{1,0:T(8,128)S(1)}, f32[64,512]{1,0:T(8,128)S(1)}, u32[]{:S(2)}, u32[]{:S(2)}) collective-permute-start(f32[64,512]{1,0:T(8,128)S(1)} %rank_inner.1), channel_id=1, source_target_pairs={{0,4},{4,0},{8,12},{12,8},{1,5},{5,1},{9,13},{13,9},{2,6},{6,2},{1... | collective-permute-start | bytes 393224 | tf_op jit(solution)/shard_map/ppermute | solution.py:342
  64.8 28.8 %collective-permute-start.10 = (bf16[256,2048]{1,0:T(8,128)(2,1)S(1)}, bf16[256,2048]{1,0:T(8,128)(2,1)S(1)}, u32[]{:S(2)}, u32[]{:S(2)}) collective-permute-start(bf16[256,2048]{1,0:T(8,128)(2,1)S(1)} %collective-permute-done.5.refs_1_.refs_3_), channel_id=1, source_target_pairs={{0,8},{5,13},{10,2},{15,7},{16,24},{21,29},{26,18},{31,23}} | collective-permute-start | bytes 3145736 | tf_op jit(solution)/shard_map/ppermute | solution.py:352
  69.7 25.1 %collective-permute-start.8 = (bf16[256,2048]{1,0:T(8,128)(2,1)S(1)}, bf16[256,2048]{1,0:T(8,128)(2,1)}, u32[]{:S(2)}, u32[]{:S(2)}) collective-permute-start(bf16[256,2048]{1,0:T(8,128)(2,1)S(1)} %broadcast_select_fusion.1), channel_id=1, source_target_pairs={{0,4},{8,12},{5,1},{13,9},{10,14},{2,6},{15,11},{7,3},{16,20},{24,... | collective-permute-start | bytes 3145736 | tf_op jit(solution)/shard_map/ppermute | solution.py:352
  72.9 3.1 %copy-start.1 = (bf16[8,64,7168]{2,1,0:T(8,128)(2,1)S(1)}, bf16[8,64,7168]{2,1,0:T(8,128)(2,1)}, u32[]{:S(2)}) copy-start(bf16[8,64,7168]{2,1,0:T(8,128)(2,1)} %up_b_ref.7) | copy-start | bytes 22020100
  87.5 7.4 %copy-start.9 = (bf16[512,2048]{1,0:T(8,128)(2,1)S(1)}, bf16[512,2048]{1,0:T(8,128)(2,1)}, u32[]{:S(2)}) copy-start(bf16[512,2048]{1,0:T(8,128)(2,1)} %copy-done.8) | copy-start | bytes 6291460
  87.5 7.3 %collective-permute-start.13 = (bf16[128,3584]{1,0:T(8,128)(2,1)}, bf16[128,3584]{1,0:T(8,128)(2,1)S(1)}, u32[]{:S(2)}, u32[]{:S(2)}) collective-permute-start(bf16[128,3584]{1,0:T(8,128)(2,1)} %collective-permute-done.9.a_ref.refs_3_), channel_id=1, source_target_pairs={{0,1},{1,0},{2,3},{3,2},{4,5},{5,4},{6,7},{7,6},{8,9},{9,8},{10,11... | collective-permute-start | bytes 2752520 | tf_op jit(solution)/shard_map/ppermute | solution.py:339
  94.8 12.1 %copy-start.19 = (bf16[128,3584]{1,0:T(8,128)(2,1)}, bf16[128,3584]{1,0:T(8,128)(2,1)S(1)}, u32[]{:S(2)}) copy-start(bf16[128,3584]{1,0:T(8,128)(2,1)S(1)} %collective-permute-done.13.b_ref.refs_5_) | copy-start | bytes 2752516
  109.6 6.1 %collective-permute-start.14 = (f32[64,512]{1,0:T(8,128)S(1)}, f32[64,512]{1,0:T(8,128)S(1)}, u32[]{:S(2)}, u32[]{:S(2)}) collective-permute-start(f32[64,512]{1,0:T(8,128)S(1)} %constant_dynamic-update-slice_fusion.2), channel_id=1, source_target_pairs={{0,4},{4,0},{8,12},{12,8},{1,5},{5,1},{9,13},{13,9},{2,6},{6,2},{1... | collective-permute-start | bytes 393224 | tf_op jit(solution)/shard_map/ppermute | solution.py:342
  109.7 21.7 %collective-permute-start.17 = (f32[64,512]{1,0:T(8,128)S(1)}, f32[64,512]{1,0:T(8,128)S(1)}, u32[]{:S(2)}, u32[]{:S(2)}) collective-permute-start(f32[64,512]{1,0:T(8,128)S(1)} %add.87.refs_0_), channel_id=1, source_target_pairs={{0,8},{4,12},{8,0},{12,4},{1,9},{5,13},{9,1},{13,5},{2,10},{6,14},... | collective-permute-start | bytes 393224 | tf_op jit(solution)/shard_map/ppermute | solution.py:342
  109.7 23.9 %collective-permute-start.15 = (bf16[256,2048]{1,0:T(8,128)(2,1)}, bf16[256,2048]{1,0:T(8,128)(2,1)S(1)}, u32[]{:S(2)}, u32[]{:S(2)}) collective-permute-start(bf16[256,2048]{1,0:T(8,128)(2,1)} %broadcast_select_fusion), channel_id=1, source_target_pairs={{0,4},{8,12},{5,1},{13,9},{10,14},{2,6},{15,11},{7,3},{16,20},{24,... | collective-permute-start | bytes 3145736 | tf_op jit(solution)/shard_map/ppermute | solution.py:352
  115.8 17.8 %copy-start.38 = (bf16[256,2048]{1,0:T(8,128)(2,1)S(1)}, bf16[256,2048]{1,0:T(8,128)(2,1)}, u32[]{:S(2)}) copy-start(bf16[256,2048]{1,0:T(8,128)(2,1)} %copy-done.37) | copy-start | bytes 3145732
  115.8 13.1 %collective-permute-start.16 = (f32[64,512]{1,0:T(8,128)S(1)}, f32[64,512]{1,0:T(8,128)S(1)}, u32[]{:S(2)}, u32[]{:S(2)}) collective-permute-start(f32[64,512]{1,0:T(8,128)S(1)} %add.90.refs_0_), channel_id=1, source_target_pairs={{0,8},{4,12},{8,0},{12,4},{1,9},{5,13},{9,1},{13,5},{2,10},{6,14},... | collective-permute-start | bytes 393224 | tf_op jit(solution)/shard_map/ppermute | solution.py:342
  116.9 17.1 %slice-start = ((s8[7340032]{0:T(1024)(128)(4,1)}), s8[4194304]{0:T(1024)(128)(4,1)S(1)}, s32[]{:S(2)}) async-start(s8[7340032]{0:T(1024)(128)(4,1)} %bitcast.21), calls=%async_computation.1 | async-start | bytes 8388608
  131.4 2.2 collective-permute-start.18
  133.6 10.7 %copy-start.11 = (bf16[512,512]{1,0:T(8,128)(2,1)}, bf16[512,512]{1,0:T(8,128)(2,1)S(1)}, u32[]{:S(2)}) copy-start(bf16[512,512]{1,0:T(8,128)(2,1)S(1)} %get-tuple-element.94.wide_ref) | copy-start | bytes 1572868
  133.6 2.0 slice-start.1
  143.7 8.6 %copy-start.23 = (f32[256,2048]{1,0:T(8,128)}, f32[256,2048]{1,0:T(8,128)S(1)}, u32[]{:S(2)}) copy-start(f32[256,2048]{1,0:T(8,128)S(1)} %get-tuple-element.103) | copy-start | bytes 6291460
  143.7 8.6 %collective-permute-start.19 = (f32[256,2048]{1,0:T(8,128)S(1)}, f32[256,2048]{1,0:T(8,128)S(1)}, u32[]{:S(2)}, u32[]{:S(2)}) collective-permute-start(f32[256,2048]{1,0:T(8,128)S(1)} %get-tuple-element.99), channel_id=1, source_target_pairs={{0,1},{1,0},{2,3},{3,2},{4,5},{5,4},{6,7},{7,6},{8,9},{9,8},{10,11... | collective-permute-start | bytes 6291464 | tf_op jit(solution)/shard_map/ppermute | solution.py:339
  151.7 23.6 %collective-permute-start.22 = (f32[256,1536]{1,0:T(8,128)}, f32[256,1536]{1,0:T(8,128)}, u32[]{:S(2)}, u32[]{:S(2)}) collective-permute-start(f32[256,1536]{1,0:T(8,128)} %get-tuple-element.105), channel_id=1, source_target_pairs={{0,1},{1,0},{2,3},{3,2},{4,5},{5,4},{6,7},{7,6},{8,9},{9,8},{10,11... | collective-permute-start | bytes 4718600 | tf_op jit(solution)/shard_map/ppermute | solution.py:339
  152.2 7.8 %collective-permute-start.20 = (bf16[64,512]{1,0:T(8,128)(2,1)S(1)}, bf16[64,512]{1,0:T(8,128)(2,1)S(1)}, u32[]{:S(2)}, u32[]{:S(2)}) collective-permute-start(bf16[64,512]{1,0:T(8,128)(2,1)S(1)} %maximum_add_fusion), channel_id=1, source_target_pairs={{0,2},{1,3},{2,0},{3,1},{4,6},{5,7},{6,4},{7,5},{8,10},{9,11},{10,... | collective-permute-start | bytes 196616 | tf_op jit(solution)/shard_map/ppermute | solution.py:339
  152.3 3.0 %copy-start.41 = (f32[256,2048]{1,0:T(8,128)}, f32[256,2048]{1,0:T(8,128)S(1)}, u32[]{:S(2)}) copy-start(f32[256,2048]{1,0:T(8,128)S(1)} %collective-permute-done.19) | copy-start | bytes 6291460
  153.4 19.0 %collective-permute-start.21 = (bf16[128,2048]{1,0:T(8,128)(2,1)}, bf16[128,2048]{1,0:T(8,128)(2,1)}, u32[]{:S(2)}, u32[]{:S(2)}) collective-permute-start(bf16[128,2048]{1,0:T(8,128)(2,1)} %fusion.6), channel_id=1, source_target_pairs={{0,2},{1,3},{2,0},{3,1},{4,6},{5,7},{6,4},{7,5},{8,10},{9,11},{10,... | collective-permute-start | bytes 1572872 | tf_op jit(solution)/shard_map/ppermute | solution.py:339
  155.3 60.7 %all-to-all-start = ((bf16[4,128,2048]{2,1,0:T(8,128)(2,1)}), bf16[4,128,2048]{2,1,0:T(8,128)(2,1)}, u32[]{:S(2)}, u32[]{:S(2)}) async-start(bf16[4,128,2048]{2,1,0:T(8,128)(2,1)} %bitcast.27), calls=%async_computation | async-start | bytes 4194304 | tf_op jit(solution)/shard_map/all_to_all | solution.py:402
  160.0 3.1 %copy-start.2 = (bf16[8,64,7168]{2,1,0:T(8,128)(2,1)S(1)}, bf16[8,64,7168]{2,1,0:T(8,128)(2,1)}, u32[]{:S(2)}) copy-start(bf16[8,64,7168]{2,1,0:T(8,128)(2,1)} %up_b_ref.7) | copy-start | bytes 22020100
  164.1 8.3 %copy-start.24 = (f32[256,2048]{1,0:T(8,128)S(1)}, f32[256,2048]{1,0:T(8,128)}, u32[]{:S(2)}) copy-start(f32[256,2048]{1,0:T(8,128)} %copy-done.23) | copy-start | bytes 6291460
  164.1 8.3 %copy-start.42 = (f32[256,2048]{1,0:T(8,128)S(1)}, f32[256,2048]{1,0:T(8,128)}, u32[]{:S(2)}) copy-start(f32[256,2048]{1,0:T(8,128)} %copy-done.41) | copy-start | bytes 6291460
  172.3 25.0 %copy-start.21 = (f32[256,2048]{1,0:T(8,128)}, f32[256,2048]{1,0:T(8,128)S(1)}, u32[]{:S(2)}) copy-start(f32[256,2048]{1,0:T(8,128)S(1)} %get-tuple-element.114) | copy-start | bytes 6291460
  172.3 3.0 %copy-start.28 = (f32[256,1536]{1,0:T(8,128)S(1)}, f32[256,1536]{1,0:T(8,128)}, u32[]{:S(2)}) copy-start(f32[256,1536]{1,0:T(8,128)} %copy-done.27) | copy-start | bytes 4718596
  172.3 25.0 %collective-permute-start.24 = (f32[256,2048]{1,0:T(8,128)S(1)}, f32[256,2048]{1,0:T(8,128)S(1)}, u32[]{:S(2)}, u32[]{:S(2)}) collective-permute-start(f32[256,2048]{1,0:T(8,128)S(1)} %get-tuple-element.110), channel_id=1, source_target_pairs={{0,1},{1,0},{2,3},{3,2},{4,5},{5,4},{6,7},{7,6},{8,9},{9,8},{10,11... | collective-permute-start | bytes 6291464 | tf_op jit(solution)/shard_map/ppermute | solution.py:339
  183.8 14.5 %copy-start.25 = (f32[256,1536]{1,0:T(8,128)}, f32[256,1536]{1,0:T(8,128)S(1)}, u32[]{:S(2)}) copy-start(f32[256,1536]{1,0:T(8,128)S(1)} %get-tuple-element.121) | copy-start | bytes 4718596
  183.8 15.5 %collective-permute-start.25 = (f32[256,1536]{1,0:T(8,128)}, f32[256,1536]{1,0:T(8,128)}, u32[]{:S(2)}, u32[]{:S(2)}) collective-permute-start(f32[256,1536]{1,0:T(8,128)} %get-tuple-element.112), channel_id=1, source_target_pairs={{0,1},{1,0},{2,3},{3,2},{4,5},{5,4},{6,7},{7,6},{8,9},{9,8},{10,11... | collective-permute-start | bytes 4718600 | tf_op jit(solution)/shard_map/ppermute | solution.py:339
  183.8 11.5 %collective-permute-start.23 = (bf16[128,1536]{1,0:T(8,128)(2,1)S(1)}, bf16[128,1536]{1,0:T(8,128)(2,1)S(1)}, u32[]{:S(2)}, u32[]{:S(2)}) collective-permute-start(bf16[128,1536]{1,0:T(8,128)(2,1)S(1)} %fusion.12), channel_id=1, source_target_pairs={{0,2},{1,3},{2,0},{3,1},{4,6},{5,7},{6,4},{7,5},{8,10},{9,11},{10,... | collective-permute-start | bytes 1179656 | tf_op jit(solution)/shard_map/ppermute | solution.py:339
  197.3 5.9 %copy-start.7 = (bf16[128,7168]{1,0:T(8,128)(2,1)S(1)}, bf16[128,7168]{1,0:T(8,128)(2,1)}, u32[]{:S(2)}) copy-start(bf16[128,7168]{1,0:T(8,128)(2,1)} %refs_0_.1) | copy-start | bytes 5505028
  197.4 5.9 %copy-start.33 = (bf16[512,512]{1,0:T(8,128)(2,1)S(1)}, bf16[512,512]{1,0:T(8,128)(2,1)}, u32[]{:S(2)}) copy-start(bf16[512,512]{1,0:T(8,128)(2,1)} %copy-done.32) | copy-start | bytes 1572868
  198.9 15.1 %collective-permute-start.26 = (bf16[128,2048]{1,0:T(8,128)(2,1)}, bf16[128,2048]{1,0:T(8,128)(2,1)}, u32[]{:S(2)}, u32[]{:S(2)}) collective-permute-start(bf16[128,2048]{1,0:T(8,128)(2,1)} %fusion.3), channel_id=1, source_target_pairs={{0,2},{1,3},{2,0},{3,1},{4,6},{5,7},{6,4},{7,5},{8,10},{9,11},{10,... | collective-permute-start | bytes 1572872 | tf_op jit(solution)/shard_map/ppermute | solution.py:339
  199.3 4.0 %copy-start.18 = (bf16[128,3584]{1,0:T(8,128)(2,1)S(1)}, bf16[128,3584]{1,0:T(8,128)(2,1)}, u32[]{:S(2)}) copy-start(bf16[128,3584]{1,0:T(8,128)(2,1)} %copy-done.17) | copy-start | bytes 2752516
  199.3 4.0 %copy-start.20 = (bf16[128,3584]{1,0:T(8,128)(2,1)S(1)}, bf16[128,3584]{1,0:T(8,128)(2,1)}, u32[]{:S(2)}) copy-start(bf16[128,3584]{1,0:T(8,128)(2,1)} %copy-done.19) | copy-start | bytes 2752516
  201.6 12.4 %copy-start.22 = (f32[256,2048]{1,0:T(8,128)S(1)}, f32[256,2048]{1,0:T(8,128)}, u32[]{:S(2)}) copy-start(f32[256,2048]{1,0:T(8,128)} %copy-done.21) | copy-start | bytes 6291460
  201.6 12.4 %copy-start.40 = (f32[256,2048]{1,0:T(8,128)S(1)}, f32[256,2048]{1,0:T(8,128)}, u32[]{:S(2)}) copy-start(f32[256,2048]{1,0:T(8,128)} %copy-done.39) | copy-start | bytes 6291460
  201.6 24.9 %collective-permute-start.27 = (bf16[128,1536]{1,0:T(8,128)(2,1)}, bf16[128,1536]{1,0:T(8,128)(2,1)}, u32[]{:S(2)}, u32[]{:S(2)}) collective-permute-start(bf16[128,1536]{1,0:T(8,128)(2,1)} %fusion.9), channel_id=1, source_target_pairs={{0,2},{1,3},{2,0},{3,1},{4,6},{5,7},{6,4},{7,5},{8,10},{9,11},{10,... | collective-permute-start | bytes 1179656 | tf_op jit(solution)/shard_map/ppermute | solution.py:339
  212.4 3.6 %copy-start.16 = (f32[256,2048]{1,0:T(8,128)S(1)}, f32[256,2048]{1,0:T(8,128)}, u32[]{:S(2)}) copy-start(f32[256,2048]{1,0:T(8,128)} %copy-done.15) | copy-start | bytes 6291460
  216.0 7.5 %copy-start.4 = (bf16[256,2048]{1,0:T(8,128)(2,1)S(1)}, bf16[256,2048]{1,0:T(8,128)(2,1)}, u32[]{:S(2)}) copy-start(bf16[256,2048]{1,0:T(8,128)(2,1)} %copy-done.3) | copy-start | bytes 3145732
  216.0 7.5 %copy-start.31 = (bf16[512,512]{1,0:T(8,128)(2,1)S(1)}, bf16[512,512]{1,0:T(8,128)(2,1)}, u32[]{:S(2)}) copy-start(bf16[512,512]{1,0:T(8,128)(2,1)} %copy-done.30) | copy-start | bytes 1572868
  218.3 27.7 %collective-permute-start.28 = (bf16[128,2048]{1,0:T(8,128)(2,1)S(1)}, bf16[128,2048]{1,0:T(8,128)(2,1)S(1)}, u32[]{:S(2)}, u32[]{:S(2)}) collective-permute-start(bf16[128,2048]{1,0:T(8,128)(2,1)S(1)} %fusion), channel_id=1, source_target_pairs={{0,0},{5,4},{10,8},{15,12},{4,1},{1,5},{14,9},{11,13},{8,2},{13,6}... | collective-permute-start | bytes 1572872 | tf_op jit(solution)/shard_map/ppermute | solution.py:352
  223.5 3.0 %copy-start.26 = (f32[256,1536]{1,0:T(8,128)S(1)}, f32[256,1536]{1,0:T(8,128)}, u32[]{:S(2)}) copy-start(f32[256,1536]{1,0:T(8,128)} %copy-done.25) | copy-start | bytes 4718596
  (15 other events, 18.2 us)

commit v8 on v7

--- a/solution.py
+++ b/solution.py
@@ -11,7 +11,7 @@
 
 adapter_scale = 2.0
 CORE, CHIP = 1, 2
-VMEM = 36 * 1024 * 1024
+VMEM = 48 * 1024 * 1024
 
 
 def dot(a, b, contract):
@@ -24,6 +24,24 @@
 
 def cost(flops, moved, share=64):
     return pl.CostEstimate(flops=flops // share, bytes_accessed=moved // share, transcendentals=0)
+
+
+def turns(steps):
+    last = steps - 1
+    return [
+        lambda n: jnp.minimum(n + n % 2, last - last % 2),
+        lambda n: jnp.minimum(n + 1 - n % 2, max(last - 1 + last % 2, 0)),
+    ]
+
+
+def in_turn(n, step, first, second):
+    @pl.when(n % 2 == 0)
+    def _():
+        step(*first)
+
+    @pl.when(n % 2 == 1)
+    def _():
+        step(*second)
 
 
 def project(tokens, wide, weight, up_flat, start, stop, block):
@@ -31,117 +49,120 @@
     span = wide.shape[1]
     base = start // block
 
-    def kernel(tok_ref, wide_ref, w_ref, up_ref, keep_ref, send_ref):
-        total = dot(tok_ref[...], w_ref[...], (1, 0)) + dot(wide_ref[...], up_ref[...], (1, 0))
-        keep_ref[...] = total[: rows // 2]
-        send_ref[...] = total[rows // 2 :]
+    steps = (stop - start) // block
+
+    def kernel(tok_ref, wide_ref, w_a_ref, up_a_ref, w_b_ref, up_b_ref, keep_ref, send_ref):
+        def step(w_ref, up_ref):
+            total = dot(tok_ref[...], w_ref[...], (1, 0)) + dot(wide_ref[...], up_ref[...], (1, 0))
+            keep_ref[...] = total[: rows // 2]
+            send_ref[...] = total[rows // 2 :]
+
+        in_turn(pl.program_id(0), step, (w_a_ref, up_a_ref), (w_b_ref, up_b_ref))
 
     whole = lambda n: (0, 0)
     return pl.pallas_call(
         kernel,
-        grid=((stop - start) // block,),
+        grid=(steps,),
         in_specs=[
             pl.BlockSpec((rows, depth), whole),
             pl.BlockSpec((rows, span), whole),
-            pl.BlockSpec((depth, block), lambda n: (0, n + base)),
-            pl.BlockSpec((span, block), lambda n: (0, n + base)),
+            *[
+                pl.BlockSpec((size, block), lambda n, at=at: (0, at(n) + base))
+                for at in turns(steps)
+                for size in (depth, span)
+            ],
         ],
         out_specs=[pl.BlockSpec((rows // 2, block), lambda n: (0, n))] * 2,
         out_shape=[jax.ShapeDtypeStruct((rows // 2, stop - start), jnp.float32)] * 2,
         compiler_params=pltpu.CompilerParams(vmem_limit_bytes=VMEM),
         cost_estimate=cost(2 * rows * (depth + span) * (stop - start), 2 * (depth + span + 2 * rows) * (stop - start)),
         name="project",
-    )(tokens, wide, weight, up_flat)
-
-
-def return_grad(facts, first, second, weight, store, places, features, units, block, before=(), grads=None, finish=True):
+    )(tokens, wide, weight, up_flat, weight, up_flat)
+
+
+def return_grad(facts, first, second, weight, store, places, features, units, before=(), grads=(), finish=True, rank_too=True):
     rows, hidden = first.shape
     depth, rank = weight.shape[0], store.shape[1]
     groups = facts.shape[0] // 2
-    count, part = features[1] - features[0], features[0] // (features[1] - features[0])
-    base, half = units[0] // block, places[0] // 2
-    grads = tuple(grads or ())
-
-    def kernel(facts_ref, a_ref, b_ref, w_ref, up_a_ref, up_b_ref, *refs):
-        before_refs = refs[: len(before)]
-        outs, (total, ranks) = refs[len(before) + len(grads) : -2], refs[-2:]
+    block = 256
+    base, column, half = features[0] // block, units[0] // hidden, places[0] // 2
+    steps = (features[1] - features[0]) // block
+
+    def kernel(facts_ref, a_ref, b_ref, w_a_ref, w_b_ref, *refs):
+        slot_refs, refs = refs[: 2 * rank_too], refs[2 * rank_too :]
+        before_refs, outs, rhs = refs[: len(before)], list(refs[len(before) + len(grads) : -1]), refs[-1]
         n = pl.program_id(0)
-        rhs = jnp.concatenate([a_ref[...], b_ref[...]], axis=0)
-        product = dot(w_ref[...], rhs, (1, 1))
-        ranked = dot(jnp.concatenate([up_a_ref[0], up_b_ref[0]], axis=0), rhs, (1, 1))
 
         @pl.when(n == 0)
         def _():
-            total[...] = product + before_refs[0][...] if before else product
-            ranks[...] = ranked
-
-        @pl.when(n > 0)
-        def _():
-            total[...] += product
-            ranks[...] += ranked
-
-        @pl.when(n == pl.num_programs(0) - 1)
-        def _():
-            for at, place in enumerate(places):
-                value = ranks[at * rank : (at + 1) * rank, at * rows : (at + 1) * rows]
-                alive = lax.broadcasted_iota(jnp.int32, (rank, rows), 1) < facts_ref[groups + place]
-                alive = alive & (facts_ref[place] >= 0)
-                value = jnp.where(alive, value * adapter_scale, 0.0)
-                if before:
-                    value += before_refs[1][:, at * rows : (at + 1) * rows]
-                outs[0][:, at * rows : (at + 1) * rows] = value
+            rhs[:rows] = a_ref[...]
+            rhs[rows:] = b_ref[...]
+
+        def step(w_ref):
+            total = dot(w_ref[...], rhs[...], (1, 1)).T
+            if before:
+                total += before_refs[0][...]
+            outs[0][...] = total
             if finish:
-                for m in range(0, count, 256):
-                    turned = total[m : m + 256].T
-                    outs[1][:, m : m + 256] = turned
-                    outs[2][:, m : m + 256] = turned.astype(first.dtype)
-            else:
-                outs[1][...] = total[...]
+                outs[1][...] = total.astype(first.dtype)
+
+        in_turn(n, step, (w_a_ref,), (w_b_ref,))
+
+        if rank_too:
+
+            @pl.when(n == pl.num_programs(0) - 1)
+            def _():
+                ranks = dot(jnp.concatenate([r[0] for r in slot_refs], axis=0), rhs[...], (1, 1))
+                for at, place in enumerate(places):
+                    value = ranks[at * rank : (at + 1) * rank, at * rows : (at + 1) * rows]
+                    alive = lax.broadcasted_iota(jnp.int32, (rank, rows), 1) < facts_ref[groups + place]
+                    alive = alive & (facts_ref[place] >= 0)
+                    value = jnp.where(alive, value * adapter_scale, 0.0)
+                    if before:
+                        value += before_refs[1][:, at * rows : (at + 1) * rows]
+                    outs[-1][:, at * rows : (at + 1) * rows] = value
 
     def chosen_slot(place):
-        return lambda n, facts_ref: (jnp.maximum(facts_ref[place], 0), 0, n + base)
+        return lambda n, facts_ref: (jnp.maximum(facts_ref[place], 0), 0, column)
 
     whole = lambda n, facts_ref: (0, 0)
-    outs = [(pl.BlockSpec((rank, 2 * rows), whole), jax.ShapeDtypeStruct((rank, 2 * rows), jnp.float32))]
+    tile = pl.BlockSpec((2 * rows, block), lambda n, facts_ref: (0, n + base))
+    outs = [(tile, jax.ShapeDtypeStruct((2 * rows, depth), jnp.float32))]
     if finish:
-        outs += [
+        outs.append(
             (
-                pl.BlockSpec((2 * rows, count), lambda n, facts_ref: (0, part)),
-                jax.ShapeDtypeStruct((2 * rows, depth), jnp.float32),
-            ),
-            (
-                pl.BlockSpec((2 * rows, count), lambda n, facts_ref: (half, part)),
+                pl.BlockSpec((2 * rows, block), lambda n, facts_ref: (half, n + base)),
                 jax.ShapeDtypeStruct((4 * rows, depth), first.dtype),
-            ),
-        ]
-    else:
-        outs += [(pl.BlockSpec((count, 2 * rows), whole), jax.ShapeDtypeStruct((count, 2 * rows), jnp.float32))]
-    at = 6 + len(before)
+            )
+        )
+    if rank_too:
+        outs.append((pl.BlockSpec((rank, 2 * rows), whole), jax.ShapeDtypeStruct((rank, 2 * rows), jnp.float32)))
+    at = 5 + 2 * rank_too + len(before)
     return pl.pallas_call(
         kernel,
         grid_spec=pltpu.PrefetchScalarGridSpec(
             num_scalar_prefetch=1,
-            grid=(hidden // block,),
+            grid=(steps,),
             in_specs=[
-                pl.BlockSpec((rows, block), lambda n, facts_ref: (0, n)),
-                pl.BlockSpec((rows, block), lambda n, facts_ref: (0, n)),
-                pl.BlockSpec((count, block), lambda n, facts_ref: (part, n + base)),
-                *[pl.BlockSpec((1, rank, block), chosen_slot(place)) for place in places],
-                *[pl.BlockSpec(x.shape, whole) for x in before],
+                pl.BlockSpec((rows, hidden), whole),
+                pl.BlockSpec((rows, hidden), whole),
+                *[
+                    pl.BlockSpec((block, hidden), lambda n, facts_ref, at=at: (at(n) + base, column))
+                    for at in turns(steps)
+                ],
+                *[pl.BlockSpec((1, rank, hidden), chosen_slot(place)) for place in places if rank_too],
+                *[tile, pl.BlockSpec((rank, 2 * rows), whole)][: len(before)],
                 *[pl.BlockSpec(memory_space=pl.ANY)] * len(grads),
             ],
             out_specs=[o[0] for o in outs],
-            scratch_shapes=[
-                pltpu.VMEM((count, 2 * rows), jnp.float32),
-                pltpu.VMEM((2 * rank, 2 * rows), jnp.float32),
-            ],
+            scratch_shapes=[pltpu.VMEM((2 * rows, hidden), first.dtype)],
         ),
         out_shape=[o[1] for o in outs],
-        input_output_aliases={at + n: (1 if x.dtype == jnp.float32 else 2) for n, x in enumerate(grads)},
+        input_output_aliases={at + n: (0 if x.dtype == jnp.float32 else 1) for n, x in enumerate(grads)},
         compiler_params=pltpu.CompilerParams(vmem_limit_bytes=VMEM),
-        cost_estimate=cost(4 * rows * hidden * count, 2 * hidden * (count + 2 * rows)),
+        cost_estimate=cost(4 * rows * hidden * block * steps, 2 * hidden * (block * steps + 2 * rows)),
         name="return_grad",
-    )(facts, first, second, weight, store, store, *before, *grads)
+    )(facts, first, second, weight, weight, *([store] * (2 * rank_too)), *before, *grads)
 
 
 def rank_inner(facts, flat, blocks, rank):
@@ -244,7 +265,7 @@
         out_specs=pl.BlockSpec((span, block), lambda n: (0, n)),
         out_shape=jax.ShapeDtypeStruct((span, columns), jnp.float32),
         compiler_params=pltpu.CompilerParams(vmem_limit_bytes=VMEM),
-        cost_estimate=cost(2 * span * tokens * columns, (4 * span + 2 * tokens) * columns),
+        cost_estimate=cost(2 * span * tokens * columns, (4 * span + 2 * tokens) * columns, 1),
         name="slot_grad",
     )(wide_t, *arrays)
 
@@ -361,8 +382,8 @@
     up_flat = adapter_up.reshape(span, hidden)
     near = swap(near, CORE)
 
-    back01, *grads = return_grad(
-        facts, after(cotangent, near), cot_c, weight, adapter_up, (0, 1), (0, half), (0, hidden), 1024
+    *grads, back01 = return_grad(
+        facts, after(cotangent, near), cot_c, weight, adapter_up, (0, 1), (0, half), (0, hidden)
     )
     down_x = swap(rest[:rank] + near[rank:], CHIP)
     even = jnp.concatenate([tokens, after(tok_x, grads[0], down_x)], axis=0)
@@ -370,8 +391,8 @@
     even_far = both(even, hop)
     cot_a = swap(after(cotangent[:, :middle], even), CHIP)
     cot_b = swap(after(cotangent[:, middle:], even), CHIP)
-    _, grad01, parts = return_grad(
-        facts, after(cotangent, even), cot_c, weight, adapter_up, (0, 1), (half, depth), (0, hidden), 1024, grads=grads
+    grad01, parts = return_grad(
+        facts, after(cotangent, even), cot_c, weight, adapter_up, (0, 1), (half, depth), (0, hidden), grads=grads, rank_too=False
     )
     odd = after(odd, grad01)
     odd_far = both(odd, hop)
@@ -383,25 +404,25 @@
     inner_far = along(inner, 2)
     even_mid = jnp.where(away == 0, even, after(even_far, inner, down_mine))
     even_all = both(even_mid, hops)
-    back23, sums = return_grad(
-        facts, after(cot_a, even_mid), cot_ac, weight, adapter_up, (2, 3), (0, depth), (0, middle), 512, finish=False
+    sums, back23 = return_grad(
+        facts, after(cot_a, even_mid), cot_ac, weight, adapter_up, (2, 3), (0, depth), (0, middle), finish=False
     )
     cot_bc = swap(after(cot_b, sums), CORE)
     odd_mid = jnp.where(away == 0, odd, after(odd_far, sums, cot_b))
     odd_all = both(odd_mid, hops)
-    back23, grad23, parts = return_grad(
-        facts, after(cot_b, odd_mid, even_all), cot_bc, weight, adapter_up, (2, 3), (0, depth), (middle, hidden), 512,
+    grad23, parts, back23 = return_grad(
+        facts, after(cot_b, odd_mid, even_all), cot_bc, weight, adapter_up, (2, 3), (0, depth), (middle, hidden),
         before=(sums, back23), grads=(parts,),
     )
     back = jnp.concatenate([back01, back23], axis=1)
-    back = back + along(back, 1)
-    all_even = jnp.where(away == 0, even, jnp.where(away == 2, even_far, after(even_all, back)))
-    back_wide, _, back_b = spread(facts, after(back, all_even), along(back, 2), per_owner, 1.0)
+    all_even = jnp.where(away == 0, even, jnp.where(away == 2, even_far, after(even_all, grad23)))
+    all_odd = jnp.where(away == 0, odd, jnp.where(away == 2, odd_far, after(odd_all, all_even)))
+    all_tokens = jnp.concatenate([all_even, all_odd], axis=0)
+    back = after(back, all_tokens) + along(back, 1)
+    back_wide, _, back_b = spread(facts, back, along(back, 2), per_owner, 1.0)
     inner_wide, inner_rows, _ = spread(facts, after(inner, back_b), inner_far, per_owner, adapter_scale)
     back_b = share(after(back_b, inner_wide), swap(back_b, CORE), CORE)
     parts = lax.all_to_all(after(parts, back_b).reshape(shards, rows, depth), "tp", 0, 0, tiled=True)
-    all_odd = jnp.where(away == 0, odd, jnp.where(away == 2, odd_far, after(odd_all, back_b)))
-    all_tokens = jnp.concatenate([all_even, all_odd], axis=0)
 
     def grad_block(q):
         low, high = [lax.dynamic_slice_in_dim(x, (q & 1) * rows, rows, 0) for x in (grad01, grad23)]
@@ -439,18 +460,18 @@
     point = make(3, point)
     point = finish(1, point)
     point = cross(2, point)
-    point = cross(3, point)
-    cots = [([cotangent], 0), ([cot_c], 0), ([cot_a, cot_b], 0), ([cot_ac, cot_bc], 0)]
-    up_wide = slot_grad(after(inner_wide, point), cots, hidden // 4)
-    point = finish(2, up_wide)
+    down_wide = slot_grad(after(back_wide, point), [([x], n) for x, n in toks], width // 2)
     back_mine = lax.dynamic_slice_in_dim(back_b, j * rows, rows, 1)
     total = grad_block(j)
     for m in range(1, shards):
-        total = total + lax.dynamic_index_in_dim(after(parts, point), j ^ m, 0, False).astype(jnp.float32)
+        total = total + lax.dynamic_index_in_dim(after(parts, down_wide), j ^ m, 0, False).astype(jnp.float32)
     total = (total + dot(back_mine, down_mine, (0, 0))).astype(b16)
     tokens_grad = both(total, [(b, a) for a, b in place])
-    down_wide = slot_grad(after(back_wide, total), [([x], n) for x, n in toks], width // 2)
-    finish(3, down_wide)
+    cots = [([cotangent], 0), ([cot_c], 0), ([cot_a, cot_b], 0), ([cot_ac, cot_bc], 0)]
+    point = cross(3, total)
+    up_wide = slot_grad(after(inner_wide, point), cots, hidden // 4)
+    point = finish(2, up_wide)
+    finish(3, point)
     projected = jnp.concatenate(done, axis=1)
     up_grad = up_wide.reshape(per_owner, rank, hidden)
     down_grad = jnp.swapaxes(down_wide.reshape(per_owner, rank, width), 1, 2)

time: 248 us -> 252 us (1.016)
  waiting for transfers between devices: 68.4 us -> 56.5 us
  Pallas kernels: 97.3 us -> 107 us
  starting transfers between devices: 34.1 us -> 42.6 us
  local copies, waits for them, and re-layouts: 22.9 us -> 15.4 us
  other arithmetic: 20.6 us -> 25.4 us
    ppermute x19, waiting for transfers between devices: 23.4 us -> 10.6 us  [swap(): return lax.ppermute(x, 'dp', [(d, d ^ bit) for d in range(groups)])]
    ppermute x19, starting transfers between devices: 7.26 us -> 18.9 us  [swap(): return lax.ppermute(x, 'dp', [(d, d ^ bit) for d in range(groups)])]
    ppermute x4, waiting for transfers between devices: 20.1 us -> 10.9 us  [along(): return lax.ppermute(x, 'tp', [(z, z ^ bit) for z in range(shards)])]
    ppermute x6, waiting for transfers between devices: 24.8 us -> 32.5 us  [both(): return lax.ppermute(x, ('tp', 'dp'), pairs)]
    unnamed x101 -> x81, local copies, waits for them, and re-layouts: 21.8 us -> 14.3 us
    pallas_call x4, Pallas kernels: 30.8 us -> 38.1 us  [project(): pl.pallas_call(kernel, grid=(steps,), in_specs=[pl.BlockSpec((rows, depth...]
    ppermute x6, starting transfers between devices: 19.4 us -> 13.5 us  [both(): return lax.ppermute(x, ('tp', 'dp'), pairs)]
    ppermute x4, starting transfers between devices: 2.78 us -> 5.68 us  [along(): return lax.ppermute(x, 'tp', [(z, z ^ bit) for z in range(shards)])]
  transfers between devices with their start and end apart: 30 -> 30, of which waited for: 11 -> 11; matrix products, arithmetic and copies ran while one was open for 10% -> 11% of each run, Pallas kernels for 31% -> 38%
where the time goes in v8:
time: 252 us; the launch traced here: 250 us
  Pallas kernels  107 us (42%)
  waiting for transfers between devices  56.5 us (22%)
  starting transfers between devices  42.6 us (17%)
  other arithmetic  25.4 us (10%)
  local copies, waits for them, and re-layouts  15.4 us (6%)
    pallas_call x4, Pallas kernels, return_grad(): pl.pallas_call(kernel, grid_spec=pltpu.PrefetchScalarGridSpec(num_scalar_...  50.3 us
    pallas_call x4, Pallas kernels, project(): pl.pallas_call(kernel, grid=(steps,), in_specs=[pl.BlockSpec((rows, depth...  38.1 us
    ppermute x6, waiting for transfers between devices, both(): return lax.ppermute(x, ('tp', 'dp'), pairs)  32.5 us
    ppermute x19, starting transfers between devices, swap(): return lax.ppermute(x, 'dp', [(d, d ^ bit) for d in range(groups)])  18.9 us
    unnamed x81, local copies, waits for them, and re-layouts  14.3 us
    ppermute x6, starting transfers between devices, both(): return lax.ppermute(x, ('tp', 'dp'), pairs)  13.5 us
    pallas_call x2, Pallas kernels, slot_grad(): pl.pallas_call(kernel, grid=(columns // block,), in_specs=[pl.BlockSpec((...  12.1 us
    ppermute x4, waiting for transfers between devices, along(): return lax.ppermute(x, 'tp', [(z, z ^ bit) for z in range(shards)])  10.9 us
  transfers between devices with their start and end apart: 30, of which 11 were waited for; matrix products, arithmetic and copies ran while one was open for 11% of the time, Pallas kernels for 38%

profile of v8, /device:TPU:2, one launch (start us, length us, event | category | flops | bytes accessed | tf_op | source)
XLA Modules:
  0.0 250.4 jit_solution(9665441002957214942)
XLA Ops:
  0.8 1.7 copy-done.12
  4.5 1.5 choose.1
  6.4 1.5 collective-permute-done.1
  8.6 13.8 %return_grad.4 = (f32[256,2048]{1,0:T(8,128)S(1)}, bf16[512,2048]{1,0:T(8,128)(2,1)}, f32[64,256]{1,0:T(8,128)S(1)}) custom-call(s32[9]{0:T(128)S(1)} %get-tuple-element.63.facts_ref, bf16[128,7168]{1,0:T(8,128)(2,1)S(1)} %copy-done.4, bf16[128,7168]{1,0:T(8,128)(2,1)} %collective-permute-done.2.b_ref.refs_1_, bf16[2048,7168]{1,0:T(8,128)(2,1)} %w_b_ref.15, ...), custom_call_target="tpu_custom_call" | custom-call | flops 58720256 | bytes 286720 | tf_op jit(solution)/shard_map/return_grad/pallas_call | solution.py:141
  22.5 3.7 %collective-permute-done.3 = bf16[64,2048]{1,0:T(8,128)(2,1)S(1)} collective-permute-done((bf16[64,2048]{1,0:T(8,128)(2,1)S(1)}, bf16[64,2048]{1,0:T(8,128)(2,1)S(1)}, u32[]{:S(2)}, u32[]{:S(2)}) %collective-permute-start.3) | collective-permute-done | bytes 262176 | tf_op jit(solution)/shard_map/ppermute | solution.py:360
  26.3 1.0 fusion.16
  27.7 1.3 collective-permute-start.4
  29.0 11.1 %return_grad.5 = (f32[256,2048]{1,0:T(8,128)S(1)}, bf16[512,2048]{1,0:T(8,128)(2,1)}) custom-call(s32[9]{0:T(128)S(1)} %get-tuple-element.63.facts_ref, bf16[128,7168]{1,0:T(8,128)(2,1)S(1)} %copy-done.5, bf16[128,7168]{1,0:T(8,128)(2,1)} %collective-permute-done.2.b_ref.refs_1_, ...), custom_call_target="tpu_custom_call", output_to_operand_aliasing={{0}: (5, {}), {1}: (6, {})} | custom-call | flops 58720256 | bytes 286720 | tf_op jit(solution)/shard_map/return_grad/pallas_call | solution.py:141
  40.0 1.3 copy-done.14
  41.3 1.3 collective-permute-start.10
  42.6 1.8 rank_inner.1
  44.5 2.6 %collective-permute-start.6 = (f32[64,512]{1,0:T(8,128)S(1)}, f32[64,512]{1,0:T(8,128)S(1)}, u32[]{:S(2)}, u32[]{:S(2)}) collective-permute-start(f32[64,512]{1,0:T(8,128)S(1)} %rank_inner.1), channel_id=1, source_target_pairs={{0,4},{4,0},{8,12},{12,8},{1,5},{5,1},{9,13},{13,9},{2,6},{6,2},{1... | collective-permute-start | bytes 393224 | tf_op jit(solution)/shard_map/ppermute | solution.py:363
  47.1 3.0 %collective-permute-done.11.a_ref.refs_2_ = bf16[128,3584]{1,0:T(8,128)(2,1)S(1)} collective-permute-done((bf16[128,3584]{1,0:T(8,128)(2,1)S(1)}, bf16[128,3584]{1,0:T(8,128)(2,1)S(1)}, u32[]{:S(2)}, u32[]{:S(2)}) %collective-permute-start.11) | collective-permute-done | bytes 917536 | tf_op jit(solution)/shard_map/ppermute | solution.py:360
  50.1 0.9 fusion.13
  51.0 4.5 %collective-permute-start.7 = (bf16[64,2048]{1,0:T(8,128)(2,1)}, bf16[64,2048]{1,0:T(8,128)(2,1)}, u32[]{:S(2)}, u32[]{:S(2)}) collective-permute-start(bf16[64,2048]{1,0:T(8,128)(2,1)} %fusion.13), channel_id=1, source_target_pairs={{0,0},{4,5},{8,10},{12,15},{1,4},{5,1},{9,14},{13,11},{2,8},{6,13}... | collective-permute-start | bytes 786440 | tf_op jit(solution)/shard_map/ppermute | solution.py:373
  55.5 11.1 %collective-permute-start.9 = (bf16[128,3584]{1,0:T(8,128)(2,1)}, bf16[128,3584]{1,0:T(8,128)(2,1)}, u32[]{:S(2)}, u32[]{:S(2)}) collective-permute-start(bf16[128,3584]{1,0:T(8,128)(2,1)} %get-tuple-element.74), channel_id=1, source_target_pairs={{0,2},{1,3},{2,0},{3,1},{4,6},{5,7},{6,4},{7,5},{8,10},{9,11},{10,... | collective-permute-start | bytes 2752520 | tf_op jit(solution)/shard_map/ppermute | solution.py:360
  66.6 23.8 %collective-permute-done.7 = bf16[64,2048]{1,0:T(8,128)(2,1)} collective-permute-done((bf16[64,2048]{1,0:T(8,128)(2,1)}, bf16[64,2048]{1,0:T(8,128)(2,1)}, u32[]{:S(2)}, u32[]{:S(2)}) %collective-permute-start.7) | collective-permute-done | bytes 262176 | tf_op jit(solution)/shard_map/ppermute | solution.py:373
  90.4 2.3 broadcast_select_fusion.1
  92.7 2.3 collective-permute-start.8
  95.0 12.6 %return_grad.6 = (f32[256,2048]{1,0:T(8,128)S(1)}, f32[64,256]{1,0:T(8,128)S(1)}) custom-call(s32[9]{0:T(128)S(1)} %get-tuple-element.63.facts_ref, bf16[128,3584]{1,0:T(8,128)(2,1)S(1)} %collective-permute-done.11.a_ref.refs_2_, bf16[128,3584]{1,0:T(8,128)(2,1)} %collective-permute-done.12.b_ref.refs_4_, bf16[2048,7168]{1,0:T(8,128)(2,1)} %w_b_ref.15, ...), custom_call_target="tpu_custom_call" | custom-call | flops 58720256 | bytes 258048 | tf_op jit(solution)/shard_map/return_grad/pallas_call | solution.py:141
  107.6 1.3 copy-done.20
  109.0 2.3 broadcast_select_fusion
  111.3 2.3 collective-permute-start.14
  113.6 1.9 copy-done.7
  115.5 12.8 %return_grad.7 = (f32[256,2048]{1,0:T(8,128)S(1)}, bf16[512,2048]{1,0:T(8,128)(2,1)S(1)}, f32[64,256]{1,0:T(8,128)S(1)}) custom-call(s32[9]{0:T(128)S(1)} %get-tuple-element.63.facts_ref, bf16[128,3584]{1,0:T(8,128)(2,1)} %collective-permute-done.9.a_ref.refs_3_, ...), custom_call_target="tpu_custom_call", output_to_operand_aliasing={{1}: (9, {})} | custom-call | flops 58720256 | bytes 258048 | tf_op jit(solution)/shard_map/return_grad/pallas_call | solution.py:141
  128.5 2.2 select_select_fusion.1
  130.7 1.4 select_select_fusion
  132.0 1.5 pad_maximum_fusion.tok_ref
  133.6 1.1 collective-permute-done.15
  134.8 2.9 %collective-permute-start.17 = (f32[64,512]{1,0:T(8,128)S(1)}, f32[64,512]{1,0:T(8,128)S(1)}, u32[]{:S(2)}, u32[]{:S(2)}) collective-permute-start(f32[64,512]{1,0:T(8,128)S(1)} %add.87.refs_0_), channel_id=1, source_target_pairs={{0,8},{4,12},{8,0},{12,4},{1,9},{5,13},{9,1},{13,5},{2,10},{6,14},... | collective-permute-start | bytes 393224 | tf_op jit(solution)/shard_map/ppermute | solution.py:363
  137.7 9.5 %collective-permute-done.16.refs_1_ = f32[64,512]{1,0:T(8,128)S(1)} collective-permute-done((f32[64,512]{1,0:T(8,128)S(1)}, f32[64,512]{1,0:T(8,128)S(1)}, u32[]{:S(2)}, u32[]{:S(2)}) %collective-permute-start.16) | collective-permute-done | bytes 131104 | tf_op jit(solution)/shard_map/ppermute | solution.py:363
  147.2 1.7 spread.2
  148.9 0.8 copy-done.31
  150.0 1.4 spread.3
  151.4 0.8 copy-done.29
  152.3 11.0 %project.4 = (f32[256,2048]{1,0:T(8,128)S(1)}, f32[256,2048]{1,0:T(8,128)}) custom-call(bf16[512,2048]{1,0:T(8,128)(2,1)} %pad_maximum_fusion.tok_ref, bf16[512,512]{1,0:T(8,128)(2,1)S(1)} %get-tuple-element.95.wide_ref, bf16[2048,7168]{1,0:T(8,128)(2,1)} %w_b_ref.15, bf16[512,7168]{1,0:T(8,128)(2,1)} %bitcast.24, bf16[2048,7168]{1,0:T(8,128)(2,1)} %w_b_ref.15, ...), custom_call_target="tpu_custom_call" | custom-call | flops 83886080 | bytes 229376 | tf_op jit(solution)/shard_map/project/pallas_call | solution.py:63
  163.2 1.4 copy-done.23
  164.8 4.6 %all-to-all-start = ((bf16[4,128,2048]{2,1,0:T(8,128)(2,1)}), bf16[4,128,2048]{2,1,0:T(8,128)(2,1)}, u32[]{:S(2)}, u32[]{:S(2)}) async-start(bf16[4,128,2048]{2,1,0:T(8,128)(2,1)} %bitcast.21), calls=%async_computation | async-start | bytes 4194304 | tf_op jit(solution)/shard_map/all_to_all | solution.py:425
  169.4 1.0 copy-done.10
  170.4 7.6 %project.5 = (f32[256,1536]{1,0:T(8,128)S(1)}, f32[256,1536]{1,0:T(8,128)S(1)}) custom-call(bf16[512,2048]{1,0:T(8,128)(2,1)S(1)} %copy-done, bf16[512,512]{1,0:T(8,128)(2,1)S(1)} %copy-done.10, bf16[2048,7168]{1,0:T(8,128)(2,1)} %w_b_ref.15, bf16[512,7168]{1,0:T(8,128)(2,1)} %bitcast.26, bf16[2048,7168]{1,0:T(8,128)(2,1)} %w_b_ref.15, ...), custom_call_target="tpu_custom_call" | custom-call | flops 62914560 | bytes 172032 | tf_op jit(solution)/shard_map/project/pallas_call | solution.py:63
  178.4 1.6 fusion.6
  180.1 2.1 collective-permute-start.21
  182.8 11.4 %project.6 = (f32[256,2048]{1,0:T(8,128)S(1)}, f32[256,2048]{1,0:T(8,128)}) custom-call(bf16[512,2048]{1,0:T(8,128)(2,1)} %pad_maximum_fusion.tok_ref, bf16[512,512]{1,0:T(8,128)(2,1)S(1)} %copy-done.11, bf16[2048,7168]{1,0:T(8,128)(2,1)} %w_b_ref.15, bf16[512,7168]{1,0:T(8,128)(2,1)} %bitcast.28, bf16[2048,7168]{1,0:T(8,128)(2,1)} %w_b_ref.15, ...), custom_call_target="tpu_custom_call" | custom-call | flops 83886080 | bytes 229376 | tf_op jit(solution)/shard_map/project/pallas_call | solution.py:63
  194.3 3.0 %fusion.5 = bf16[128,2048]{1,0:T(8,128)(2,1)} fusion(f32[256,2048]{1,0:T(8,128)} %collective-permute-done.19, bf16[128,2048]{1,0:T(8,128)(2,1)S(1)} %collective-permute-done.21, f32[256,2048]{1,0:T(8,128)S(1)} %copy-done.24), kind=kLoop, calls=%fused_computation.11 | loop fusion | flops 1048576 | bytes 3145728 | tf_op jit(solution)/shard_map/convert_element_type | solution.py:450
  197.4 1.0 collective-permute-start.23
  198.4 8.1 %project.7 = (f32[256,1536]{1,0:T(8,128)S(1)}, f32[256,1536]{1,0:T(8,128)}) custom-call(bf16[512,2048]{1,0:T(8,128)(2,1)S(1)} %copy-done.1, bf16[512,512]{1,0:T(8,128)(2,1)S(1)} %copy-done.11, bf16[2048,7168]{1,0:T(8,128)(2,1)} %w_b_ref.15, bf16[512,7168]{1,0:T(8,128)(2,1)} %bitcast.30, bf16[2048,7168]{1,0:T(8,128)(2,1)} %w_b_ref.15, bf16[512,7168]{1,0:T(8,128)(2,1)} %bitcast.31), custom_call_target="tpu_custom_call" | custom-call | flops 62914560 | bytes 172032 | tf_op jit(solution)/shard_map/project/pallas_call | solution.py:63
  206.5 1.2 copy-done.25
  207.7 0.7 collective-permute-done.23
  208.4 1.6 fusion.11
  210.1 2.1 fusion.3
  212.2 0.8 collective-permute-start.26
  213.0 2.9 %slot_grad.2 = f32[512,2048]{1,0:T(8,128)} custom-call(bf16[512,512]{1,0:T(8,128)(2,1)S(1)} %copy-done.32, bf16[256,2048]{1,0:T(8,128)(2,1)S(1)} %constant_dynamic-update-slice_fusion.refs_0_.refs_2_, bf16[256,2048]{1,0:T(8,128)(2,1)S(1)} %copy-done.3, bf16[256,2048]{1,0:T(8,128)(2,1)S(1)} %constant_dynamic-update-slice_fusion.refs_0_.refs_2_, ...), custom_call_target="tpu_custom_call" | custom-call | flops 1073741824 | bytes 6291456 | tf_op jit(solution)/shard_map/slot_grad/pallas_call | solution.py:261
  215.9 2.5 all-to-all-done
  218.4 2.3 fusion
  220.8 1.3 fusion.9
  222.2 1.8 collective-permute-start.27
  224.0 1.9 collective-permute-start.28
  226.0 9.2 %slot_grad.3 = f32[512,7168]{1,0:T(8,128)} custom-call(bf16[512,512]{1,0:T(8,128)(2,1)S(1)} %copy-done.30, bf16[128,7168]{1,0:T(8,128)(2,1)S(1)} %copy-done.6, bf16[128,7168]{1,0:T(8,128)(2,1)} %collective-permute-done.2.b_ref.refs_1_, bf16[128,3584]{1,0:T(8,128)(2,1)S(1)} %copy-done.17, bf16[128,3584]{1,0:T(8,128)(2,1)} %collective-permute-done.9.a_ref.refs_3_, ...), custom_call_target="tpu_custom_call" | custom-call | flops 3758096384 | bytes 22020096 | tf_op jit(solution)/shard_map/slot_grad/pallas_call | solution.py:261
  235.2 1.6 fusion.2
  236.7 1.6 collective-permute-done.27
  238.3 1.3 fusion.8
  239.6 1.4 pad_maximum_fusion.1
  241.0 8.6 %collective-permute-done.28 = bf16[128,2048]{1,0:T(8,128)(2,1)S(1)} collective-permute-done((bf16[128,2048]{1,0:T(8,128)(2,1)S(1)}, bf16[128,2048]{1,0:T(8,128)(2,1)S(1)}, u32[]{:S(2)}, u32[]{:S(2)}) %collective-permute-start.28) | collective-permute-done | bytes 524320 | tf_op jit(solution)/shard_map/ppermute | solution.py:373
  249.6 0.8 copy.21
  (118 shorter events, 5.7 us)
Async XLA Ops:
  0.6 8.0 %copy-start.4 = (bf16[128,7168]{1,0:T(8,128)(2,1)S(1)}, bf16[128,7168]{1,0:T(8,128)(2,1)}, u32[]{:S(2)}) copy-start(bf16[128,7168]{1,0:T(8,128)(2,1)} %refs_0_.7) | copy-start | bytes 5505028
  0.6 8.0 %collective-permute-start.2 = (bf16[128,7168]{1,0:T(8,128)(2,1)}, bf16[128,7168]{1,0:T(8,128)(2,1)}, u32[]{:S(2)}, u32[]{:S(2)}) collective-permute-start(bf16[128,7168]{1,0:T(8,128)(2,1)} %refs_0_.7), channel_id=1, source_target_pairs={{0,1},{1,0},{2,3},{3,2},{4,5},{5,4},{6,7},{7,6},{8,9},{9,8},{10,11... | collective-permute-start | bytes 5505032 | tf_op jit(solution)/shard_map/ppermute | solution.py:360
  0.8 1.7 copy-start.12
  4.5 4.1 %copy-start.38 = (bf16[128,2048]{1,0:T(8,128)(2,1)S(1)}, bf16[128,2048]{1,0:T(8,128)(2,1)}, u32[]{:S(2)}) copy-start(bf16[128,2048]{1,0:T(8,128)(2,1)} %param.8) | copy-start | bytes 1572868
  6.0 2.0 collective-permute-start.1
  6.4 16.1 %collective-permute-start = (bf16[128,2048]{1,0:T(8,128)(2,1)}, bf16[128,2048]{1,0:T(8,128)(2,1)S(1)}, u32[]{:S(2)}, u32[]{:S(2)}) collective-permute-start(bf16[128,2048]{1,0:T(8,128)(2,1)} %param.8), channel_id=1, source_target_pairs={{0,2},{1,3},{2,0},{3,1},{4,6},{5,7},{6,4},{7,5},{8,10},{9,11},{10,... | collective-permute-start | bytes 1572872 | tf_op jit(solution)/shard_map/ppermute | solution.py:360
  8.0 18.2 %collective-permute-start.3 = (bf16[64,2048]{1,0:T(8,128)(2,1)S(1)}, bf16[64,2048]{1,0:T(8,128)(2,1)S(1)}, u32[]{:S(2)}, u32[]{:S(2)}) collective-permute-start(bf16[64,2048]{1,0:T(8,128)(2,1)S(1)} %slice_add_fusion.9), channel_id=1, source_target_pairs={{0,2},{1,3},{2,0},{3,1},{4,6},{5,7},{6,4},{7,5},{8,10},{9,11},{10,... | collective-permute-start | bytes 786440 | tf_op jit(solution)/shard_map/ppermute | solution.py:360
  8.6 17.7 %copy-start.5 = (bf16[128,7168]{1,0:T(8,128)(2,1)S(1)}, bf16[128,7168]{1,0:T(8,128)(2,1)}, u32[]{:S(2)}) copy-start(bf16[128,7168]{1,0:T(8,128)(2,1)} %refs_0_.7) | copy-start | bytes 5505028
  26.3 15.1 %collective-permute-start.5 = (bf16[256,2048]{1,0:T(8,128)(2,1)S(1)}, bf16[256,2048]{1,0:T(8,128)(2,1)S(1)}, u32[]{:S(2)}, u32[]{:S(2)}) collective-permute-start(bf16[256,2048]{1,0:T(8,128)(2,1)S(1)} %constant_dynamic-update-slice_fusion.refs_0_.refs_2_), channel_id=1, source_target_pairs={{0,1},{1,0},{2,3},{3,2},{4,5},{5,4},{6,7},{7,6},{8,9},{9,8},{10,11... | collective-permute-start | bytes 3145736 | tf_op jit(solution)/shard_map/ppermute | solution.py:360
  27.4 22.7 %collective-permute-start.11 = (bf16[128,3584]{1,0:T(8,128)(2,1)S(1)}, bf16[128,3584]{1,0:T(8,128)(2,1)S(1)}, u32[]{:S(2)}, u32[]{:S(2)}) collective-permute-start(bf16[128,3584]{1,0:T(8,128)(2,1)S(1)} %get-tuple-element.75), channel_id=1, source_target_pairs={{0,2},{1,3},{2,0},{3,1},{4,6},{5,7},{6,4},{7,5},{8,10},{9,11},{10,... | collective-permute-start | bytes 2752520 | tf_op jit(solution)/shard_map/ppermute | solution.py:360
  27.7 62.7 %collective-permute-start.4 = (bf16[256,2048]{1,0:T(8,128)(2,1)S(1)}, bf16[256,2048]{1,0:T(8,128)(2,1)}, u32[]{:S(2)}, u32[]{:S(2)}) collective-permute-start(bf16[256,2048]{1,0:T(8,128)(2,1)S(1)} %constant_dynamic-update-slice_fusion.refs_0_.refs_2_), channel_id=1, source_target_pairs={{0,8},{5,13},{10,2},{15,7},{16,24},{21,29},{26,18},{31,23}} | collective-permute-start | bytes 3145736 | tf_op jit(solution)/shard_map/ppermute | solution.py:373
  29.0 13.7 %copy-start.13 = (bf16[8,2048,64]{1,2,0:T(8,128)(2,1)S(1)}, bf16[8,2048,64]{1,2,0:T(8,128)(2,1)}, u32[]{:S(2)}) copy-start(bf16[8,2048,64]{1,2,0:T(8,128)(2,1)} %param.10) | copy-start | bytes 6291460
  40.0 1.3 copy-start.14
  41.3 89.3 %copy-start.2 = (bf16[256,2048]{1,0:T(8,128)(2,1)}, bf16[256,2048]{1,0:T(8,128)(2,1)S(1)}, u32[]{:S(2)}) copy-start(bf16[256,2048]{1,0:T(8,128)(2,1)S(1)} %collective-permute-done.5.refs_1_.refs_3_) | copy-start | bytes 3145732
  41.3 67.6 %collective-permute-start.10 = (bf16[256,2048]{1,0:T(8,128)(2,1)S(1)}, bf16[256,2048]{1,0:T(8,128)(2,1)}, u32[]{:S(2)}, u32[]{:S(2)}) collective-permute-start(bf16[256,2048]{1,0:T(8,128)(2,1)S(1)} %collective-permute-done.5.refs_1_.refs_3_), channel_id=1, source_target_pairs={{0,8},{5,13},{10,2},{15,7},{16,24},{21,29},{26,18},{31,23}} | collective-permute-start | bytes 3145736 | tf_op jit(solution)/shard_map/ppermute | solution.py:373
  44.5 11.0 %collective-permute-start.6 = (f32[64,512]{1,0:T(8,128)S(1)}, f32[64,512]{1,0:T(8,128)S(1)}, u32[]{:S(2)}, u32[]{:S(2)}) collective-permute-start(f32[64,512]{1,0:T(8,128)S(1)} %rank_inner.1), channel_id=1, source_target_pairs={{0,4},{4,0},{8,12},{12,8},{1,5},{5,1},{9,13},{13,9},{2,6},{6,2},{1... | collective-permute-start | bytes 393224 | tf_op jit(solution)/shard_map/ppermute | solution.py:363
  50.1 44.9 %copy-start.16 = (bf16[128,3584]{1,0:T(8,128)(2,1)}, bf16[128,3584]{1,0:T(8,128)(2,1)S(1)}, u32[]{:S(2)}) copy-start(bf16[128,3584]{1,0:T(8,128)(2,1)S(1)} %collective-permute-done.11.a_ref.refs_2_) | copy-start | bytes 2752516
  50.1 44.9 %collective-permute-start.12 = (bf16[128,3584]{1,0:T(8,128)(2,1)S(1)}, bf16[128,3584]{1,0:T(8,128)(2,1)}, u32[]{:S(2)}, u32[]{:S(2)}) collective-permute-start(bf16[128,3584]{1,0:T(8,128)(2,1)S(1)} %collective-permute-done.11.a_ref.refs_2_), channel_id=1, source_target_pairs={{0,1},{1,0},{2,3},{3,2},{4,5},{5,4},{6,7},{7,6},{8,9},{9,8},{10,11... | collective-permute-start | bytes 2752520 | tf_op jit(solution)/shard_map/ppermute | solution.py:360
  51.0 39.4 %collective-permute-start.7 = (bf16[64,2048]{1,0:T(8,128)(2,1)}, bf16[64,2048]{1,0:T(8,128)(2,1)}, u32[]{:S(2)}, u32[]{:S(2)}) collective-permute-start(bf16[64,2048]{1,0:T(8,128)(2,1)} %fusion.13), channel_id=1, source_target_pairs={{0,0},{4,5},{8,10},{12,15},{1,4},{5,1},{9,14},{13,11},{2,8},{6,13}... | collective-permute-start | bytes 786440 | tf_op jit(solution)/shard_map/ppermute | solution.py:373
  55.5 53.5 %collective-permute-start.9 = (bf16[128,3584]{1,0:T(8,128)(2,1)}, bf16[128,3584]{1,0:T(8,128)(2,1)}, u32[]{:S(2)}, u32[]{:S(2)}) collective-permute-start(bf16[128,3584]{1,0:T(8,128)(2,1)} %get-tuple-element.74), channel_id=1, source_target_pairs={{0,2},{1,3},{2,0},{3,1},{4,6},{5,7},{6,4},{7,5},{8,10},{9,11},{10,... | collective-permute-start | bytes 2752520 | tf_op jit(solution)/shard_map/ppermute | solution.py:360
  92.7 20.8 %collective-permute-start.8 = (bf16[256,2048]{1,0:T(8,128)(2,1)}, bf16[256,2048]{1,0:T(8,128)(2,1)}, u32[]{:S(2)}, u32[]{:S(2)}) collective-permute-start(bf16[256,2048]{1,0:T(8,128)(2,1)} %broadcast_select_fusion.1), channel_id=1, source_target_pairs={{0,4},{8,12},{5,1},{13,9},{10,14},{2,6},{15,11},{7,3},{16,20},{24,... | collective-permute-start | bytes 3145736 | tf_op jit(solution)/shard_map/ppermute | solution.py:373
  107.6 1.3 copy-start.20
  109.0 4.6 %collective-permute-start.13 = (bf16[128,3584]{1,0:T(8,128)(2,1)}, bf16[128,3584]{1,0:T(8,128)(2,1)S(1)}, u32[]{:S(2)}, u32[]{:S(2)}) collective-permute-start(bf16[128,3584]{1,0:T(8,128)(2,1)} %collective-permute-done.9.a_ref.refs_3_), channel_id=1, source_target_pairs={{0,1},{1,0},{2,3},{3,2},{4,5},{5,4},{6,7},{7,6},{8,9},{9,8},{10,11... | collective-permute-start | bytes 2752520 | tf_op jit(solution)/shard_map/ppermute | solution.py:360
  111.3 19.4 %collective-permute-start.14 = (bf16[256,2048]{1,0:T(8,128)(2,1)}, bf16[256,2048]{1,0:T(8,128)(2,1)}, u32[]{:S(2)}, u32[]{:S(2)}) collective-permute-start(bf16[256,2048]{1,0:T(8,128)(2,1)} %broadcast_select_fusion), channel_id=1, source_target_pairs={{0,4},{8,12},{5,1},{13,9},{10,14},{2,6},{15,11},{7,3},{16,20},{24,... | collective-permute-start | bytes 3145736 | tf_op jit(solution)/shard_map/ppermute | solution.py:373
  113.6 14.8 %copy-start.18 = (bf16[128,3584]{1,0:T(8,128)(2,1)}, bf16[128,3584]{1,0:T(8,128)(2,1)S(1)}, u32[]{:S(2)}) copy-start(bf16[128,3584]{1,0:T(8,128)(2,1)S(1)} %collective-permute-done.13.b_ref.refs_5_) | copy-start | bytes 2752516
  113.6 1.9 copy-start.7
  128.3 2.3 copy-start.8
  128.4 2.3 copy-start.28
  128.4 6.3 %collective-permute-start.15 = (f32[64,512]{1,0:T(8,128)S(1)}, f32[64,512]{1,0:T(8,128)S(1)}, u32[]{:S(2)}, u32[]{:S(2)}) collective-permute-start(f32[64,512]{1,0:T(8,128)S(1)} %constant_dynamic-update-slice_fusion.2), channel_id=1, source_target_pairs={{0,4},{4,0},{8,12},{12,8},{1,5},{5,1},{9,13},{13,9},{2,6},{6,2},{1... | collective-permute-start | bytes 393224 | tf_op jit(solution)/shard_map/ppermute | solution.py:363
  134.7 12.5 %collective-permute-start.16 = (f32[64,512]{1,0:T(8,128)S(1)}, f32[64,512]{1,0:T(8,128)S(1)}, u32[]{:S(2)}, u32[]{:S(2)}) collective-permute-start(f32[64,512]{1,0:T(8,128)S(1)} %add.90.refs_0_), channel_id=1, source_target_pairs={{0,8},{4,12},{8,0},{12,4},{1,9},{5,13},{9,1},{13,5},{2,10},{6,14},... | collective-permute-start | bytes 393224 | tf_op jit(solution)/shard_map/ppermute | solution.py:363
  134.8 15.2 %collective-permute-start.17 = (f32[64,512]{1,0:T(8,128)S(1)}, f32[64,512]{1,0:T(8,128)S(1)}, u32[]{:S(2)}, u32[]{:S(2)}) collective-permute-start(f32[64,512]{1,0:T(8,128)S(1)} %add.87.refs_0_), channel_id=1, source_target_pairs={{0,8},{4,12},{8,0},{12,4},{1,9},{5,13},{9,1},{13,5},{2,10},{6,14},... | collective-permute-start | bytes 393224 | tf_op jit(solution)/shard_map/ppermute | solution.py:363
  149.7 2.5 %collective-permute-start.18 = (bf16[64,512]{1,0:T(8,128)(2,1)S(1)}, bf16[64,512]{1,0:T(8,128)(2,1)S(1)}, u32[]{:S(2)}, u32[]{:S(2)}) collective-permute-start(bf16[64,512]{1,0:T(8,128)(2,1)S(1)} %get-tuple-element.93), channel_id=1, source_target_pairs={{0,1},{1,0},{2,3},{3,2},{4,5},{5,4},{6,7},{7,6},{8,9},{9,8},{10,11... | collective-permute-start | bytes 196616 | tf_op jit(solution)/shard_map/ppermute | solution.py:360
  152.2 11.0 %copy-start.9 = (bf16[512,512]{1,0:T(8,128)(2,1)}, bf16[512,512]{1,0:T(8,128)(2,1)S(1)}, u32[]{:S(2)}) copy-start(bf16[512,512]{1,0:T(8,128)(2,1)S(1)} %get-tuple-element.95.wide_ref) | copy-start | bytes 1572868
  163.2 1.4 copy-start.23
  164.6 13.8 %collective-permute-start.19 = (f32[256,2048]{1,0:T(8,128)}, f32[256,2048]{1,0:T(8,128)}, u32[]{:S(2)}, u32[]{:S(2)}) collective-permute-start(f32[256,2048]{1,0:T(8,128)} %get-tuple-element.100), channel_id=1, source_target_pairs={{0,1},{1,0},{2,3},{3,2},{4,5},{5,4},{6,7},{7,6},{8,9},{9,8},{10,11... | collective-permute-start | bytes 6291464 | tf_op jit(solution)/shard_map/ppermute | solution.py:360
  164.8 17.4 %collective-permute-start.20 = (bf16[64,512]{1,0:T(8,128)(2,1)S(1)}, bf16[64,512]{1,0:T(8,128)(2,1)S(1)}, u32[]{:S(2)}, u32[]{:S(2)}) collective-permute-start(bf16[64,512]{1,0:T(8,128)(2,1)S(1)} %maximum_add_fusion), channel_id=1, source_target_pairs={{0,2},{1,3},{2,0},{3,1},{4,6},{5,7},{6,4},{7,5},{8,10},{9,11},{10,... | collective-permute-start | bytes 196616 | tf_op jit(solution)/shard_map/ppermute | solution.py:360
  164.8 4.6 %copy-start = (bf16[512,2048]{1,0:T(8,128)(2,1)S(1)}, bf16[512,2048]{1,0:T(8,128)(2,1)}, u32[]{:S(2)}) copy-start(bf16[512,2048]{1,0:T(8,128)(2,1)} %pad_maximum_fusion.tok_ref) | copy-start | bytes 6291460
  164.8 53.6 %all-to-all-start = ((bf16[4,128,2048]{2,1,0:T(8,128)(2,1)}), bf16[4,128,2048]{2,1,0:T(8,128)(2,1)}, u32[]{:S(2)}, u32[]{:S(2)}) async-start(bf16[4,128,2048]{2,1,0:T(8,128)(2,1)} %bitcast.21), calls=%async_computation | async-start | bytes 4194304 | tf_op jit(solution)/shard_map/all_to_all | solution.py:425
  169.4 1.0 copy-start.10
  170.4 8.0 %copy-start.24 = (f32[256,2048]{1,0:T(8,128)S(1)}, f32[256,2048]{1,0:T(8,128)}, u32[]{:S(2)}) copy-start(f32[256,2048]{1,0:T(8,128)} %copy-done.23) | copy-start | bytes 6291460
  178.0 19.3 %copy-start.27 = (f32[256,1536]{1,0:T(8,128)}, f32[256,1536]{1,0:T(8,128)S(1)}, u32[]{:S(2)}) copy-start(f32[256,1536]{1,0:T(8,128)S(1)} %get-tuple-element.109) | copy-start | bytes 4718596
  178.0 4.8 %copy-start.11 = (bf16[512,512]{1,0:T(8,128)(2,1)S(1)}, bf16[512,512]{1,0:T(8,128)(2,1)}, u32[]{:S(2)}) copy-start(bf16[512,512]{1,0:T(8,128)(2,1)} %copy-done.9) | copy-start | bytes 1572868
  178.0 19.3 %collective-permute-start.22 = (f32[256,1536]{1,0:T(8,128)S(1)}, f32[256,1536]{1,0:T(8,128)S(1)}, u32[]{:S(2)}, u32[]{:S(2)}) collective-permute-start(f32[256,1536]{1,0:T(8,128)S(1)} %get-tuple-element.106), channel_id=1, source_target_pairs={{0,1},{1,0},{2,3},{3,2},{4,5},{5,4},{6,7},{7,6},{8,9},{9,8},{10,11... | collective-permute-start | bytes 4718600 | tf_op jit(solution)/shard_map/ppermute | solution.py:360
  180.1 14.2 %collective-permute-start.21 = (bf16[128,2048]{1,0:T(8,128)(2,1)S(1)}, bf16[128,2048]{1,0:T(8,128)(2,1)S(1)}, u32[]{:S(2)}, u32[]{:S(2)}) collective-permute-start(bf16[128,2048]{1,0:T(8,128)(2,1)S(1)} %fusion.6), channel_id=1, source_target_pairs={{0,2},{1,3},{2,0},{3,1},{4,6},{5,7},{6,4},{7,5},{8,10},{9,11},{10,... | collective-permute-start | bytes 1572872 | tf_op jit(solution)/shard_map/ppermute | solution.py:360
  194.3 15.8 %copy-start.21 = (f32[256,2048]{1,0:T(8,128)}, f32[256,2048]{1,0:T(8,128)S(1)}, u32[]{:S(2)}) copy-start(f32[256,2048]{1,0:T(8,128)S(1)} %get-tuple-element.120) | copy-start | bytes 6291460
  194.3 15.8 %collective-permute-start.24 = (f32[256,2048]{1,0:T(8,128)}, f32[256,2048]{1,0:T(8,128)}, u32[]{:S(2)}, u32[]{:S(2)}) collective-permute-start(f32[256,2048]{1,0:T(8,128)} %get-tuple-element.114), channel_id=1, source_target_pairs={{0,1},{1,0},{2,3},{3,2},{4,5},{5,4},{6,7},{7,6},{8,9},{9,8},{10,11... | collective-permute-start | bytes 6291464 | tf_op jit(solution)/shard_map/ppermute | solution.py:360
  194.3 4.1 %copy-start.1 = (bf16[512,2048]{1,0:T(8,128)(2,1)S(1)}, bf16[512,2048]{1,0:T(8,128)(2,1)}, u32[]{:S(2)}) copy-start(bf16[512,2048]{1,0:T(8,128)(2,1)} %pad_maximum_fusion.tok_ref) | copy-start | bytes 6291460
  197.3 9.2 %copy-start.37 = (f32[256,1536]{1,0:T(8,128)}, f32[256,1536]{1,0:T(8,128)S(1)}, u32[]{:S(2)}) copy-start(f32[256,1536]{1,0:T(8,128)S(1)} %collective-permute-done.22) | copy-start | bytes 4718596
  197.4 11.0 %collective-permute-start.23 = (bf16[128,1536]{1,0:T(8,128)(2,1)S(1)}, bf16[128,1536]{1,0:T(8,128)(2,1)}, u32[]{:S(2)}, u32[]{:S(2)}) collective-permute-start(bf16[128,1536]{1,0:T(8,128)(2,1)S(1)} %fusion.12), channel_id=1, source_target_pairs={{0,2},{1,3},{2,0},{3,1},{4,6},{5,7},{6,4},{7,5},{8,10},{9,11},{10,... | collective-permute-start | bytes 1179656 | tf_op jit(solution)/shard_map/ppermute | solution.py:360
  206.5 1.2 copy-start.25
  207.7 13.1 %collective-permute-start.25 = (f32[256,1536]{1,0:T(8,128)}, f32[256,1536]{1,0:T(8,128)}, u32[]{:S(2)}, u32[]{:S(2)}) collective-permute-start(f32[256,1536]{1,0:T(8,128)} %get-tuple-element.118), channel_id=1, source_target_pairs={{0,1},{1,0},{2,3},{3,2},{4,5},{5,4},{6,7},{7,6},{8,9},{9,8},{10,11... | collective-permute-start | bytes 4718600 | tf_op jit(solution)/shard_map/ppermute | solution.py:360
  207.7 5.3 %copy-start.3 = (bf16[256,2048]{1,0:T(8,128)(2,1)S(1)}, bf16[256,2048]{1,0:T(8,128)(2,1)}, u32[]{:S(2)}) copy-start(bf16[256,2048]{1,0:T(8,128)(2,1)} %copy-done.2) | copy-start | bytes 3145732
  207.7 5.3 %copy-start.32 = (bf16[512,512]{1,0:T(8,128)(2,1)S(1)}, bf16[512,512]{1,0:T(8,128)(2,1)}, u32[]{:S(2)}) copy-start(bf16[512,512]{1,0:T(8,128)(2,1)} %copy-done.31) | copy-start | bytes 1572868
  212.2 23.0 %collective-permute-start.26 = (bf16[128,2048]{1,0:T(8,128)(2,1)}, bf16[128,2048]{1,0:T(8,128)(2,1)}, u32[]{:S(2)}, u32[]{:S(2)}) collective-permute-start(bf16[128,2048]{1,0:T(8,128)(2,1)} %fusion.3), channel_id=1, source_target_pairs={{0,2},{1,3},{2,0},{3,1},{4,6},{5,7},{6,4},{7,5},{8,10},{9,11},{10,... | collective-permute-start | bytes 1572872 | tf_op jit(solution)/shard_map/ppermute | solution.py:360
  213.0 5.4 %copy-start.15 = (f32[256,2048]{1,0:T(8,128)S(1)}, f32[256,2048]{1,0:T(8,128)}, u32[]{:S(2)}) copy-start(f32[256,2048]{1,0:T(8,128)} %copy-done.14) | copy-start | bytes 6291460
  218.4 2.4 copy-start.26
  218.4 7.5 %copy-start.17 = (bf16[128,3584]{1,0:T(8,128)(2,1)S(1)}, bf16[128,3584]{1,0:T(8,128)(2,1)}, u32[]{:S(2)}) copy-start(bf16[128,3584]{1,0:T(8,128)(2,1)} %copy-done.16) | copy-start | bytes 2752516
  218.4 7.5 %copy-start.19 = (bf16[128,3584]{1,0:T(8,128)(2,1)S(1)}, bf16[128,3584]{1,0:T(8,128)(2,1)}, u32[]{:S(2)}) copy-start(bf16[128,3584]{1,0:T(8,128)(2,1)} %copy-done.18) | copy-start | bytes 2752516
  218.4 7.5 %copy-start.30 = (bf16[512,512]{1,0:T(8,128)(2,1)S(1)}, bf16[512,512]{1,0:T(8,128)(2,1)}, u32[]{:S(2)}) copy-start(bf16[512,512]{1,0:T(8,128)(2,1)} %copy-done.29) | copy-start | bytes 1572868
  220.8 5.2 %copy-start.6 = (bf16[128,7168]{1,0:T(8,128)(2,1)S(1)}, bf16[128,7168]{1,0:T(8,128)(2,1)}, u32[]{:S(2)}) copy-start(bf16[128,7168]{1,0:T(8,128)(2,1)} %refs_0_.7) | copy-start | bytes 5505028
  222.2 13.0 %copy-start.22 = (f32[256,2048]{1,0:T(8,128)S(1)}, f32[256,2048]{1,0:T(8,128)}, u32[]{:S(2)}) copy-start(f32[256,2048]{1,0:T(8,128)} %copy-done.21) | copy-start | bytes 6291460
  222.2 16.1 %collective-permute-start.27 = (bf16[128,1536]{1,0:T(8,128)(2,1)S(1)}, bf16[128,1536]{1,0:T(8,128)(2,1)S(1)}, u32[]{:S(2)}, u32[]{:S(2)}) collective-permute-start(bf16[128,1536]{1,0:T(8,128)(2,1)S(1)} %fusion.9), channel_id=1, source_target_pairs={{0,2},{1,3},{2,0},{3,1},{4,6},{5,7},{6,4},{7,5},{8,10},{9,11},{10,... | collective-permute-start | bytes 1179656 | tf_op jit(solution)/shard_map/ppermute | solution.py:360
  224.0 25.6 %collective-permute-start.28 = (bf16[128,2048]{1,0:T(8,128)(2,1)S(1)}, bf16[128,2048]{1,0:T(8,128)(2,1)S(1)}, u32[]{:S(2)}, u32[]{:S(2)}) collective-permute-start(bf16[128,2048]{1,0:T(8,128)(2,1)S(1)} %fusion), channel_id=1, source_target_pairs={{0,0},{5,4},{10,8},{15,12},{4,1},{1,5},{14,9},{11,13},{8,2},{13,6}... | collective-permute-start | bytes 1572872 | tf_op jit(solution)/shard_map/ppermute | solution.py:373
  235.1 4.4 %copy-start.36 = (bf16[128,2048]{1,0:T(8,128)(2,1)S(1)}, bf16[128,2048]{1,0:T(8,128)(2,1)}, u32[]{:S(2)}) copy-start(bf16[128,2048]{1,0:T(8,128)(2,1)} %fusion.5) | copy-start | bytes 1572868
  (5 other events, 3.6 us)

commit v9 on v7

--- a/solution.py
+++ b/solution.py
@@ -11,7 +11,7 @@
 
 adapter_scale = 2.0
 CORE, CHIP = 1, 2
-VMEM = 36 * 1024 * 1024
+VMEM = 48 * 1024 * 1024
 
 
 def dot(a, b, contract):
@@ -36,13 +36,12 @@
         keep_ref[...] = total[: rows // 2]
         send_ref[...] = total[rows // 2 :]
 
-    whole = lambda n: (0, 0)
     return pl.pallas_call(
         kernel,
         grid=((stop - start) // block,),
         in_specs=[
-            pl.BlockSpec((rows, depth), whole),
-            pl.BlockSpec((rows, span), whole),
+            pl.BlockSpec(memory_space=pltpu.VMEM),
+            pl.BlockSpec(memory_space=pltpu.VMEM),
             pl.BlockSpec((depth, block), lambda n: (0, n + base)),
             pl.BlockSpec((span, block), lambda n: (0, n + base)),
         ],
@@ -54,94 +53,67 @@
     )(tokens, wide, weight, up_flat)
 
 
-def return_grad(facts, first, second, weight, store, places, features, units, block, before=(), grads=None, finish=True):
+def return_grad(facts, first, second, weight, store, places, sent=()):
     rows, hidden = first.shape
     depth, rank = weight.shape[0], store.shape[1]
     groups = facts.shape[0] // 2
-    count, part = features[1] - features[0], features[0] // (features[1] - features[0])
-    base, half = units[0] // block, places[0] // 2
-    grads = tuple(grads or ())
+    block = 256
+    half = places[0] // 2
 
     def kernel(facts_ref, a_ref, b_ref, w_ref, up_a_ref, up_b_ref, *refs):
-        before_refs = refs[: len(before)]
-        outs, (total, ranks) = refs[len(before) + len(grads) : -2], refs[-2:]
+        out_ref, sent_ref, rank_ref, rhs = refs[len(sent) :]
         n = pl.program_id(0)
-        rhs = jnp.concatenate([a_ref[...], b_ref[...]], axis=0)
-        product = dot(w_ref[...], rhs, (1, 1))
-        ranked = dot(jnp.concatenate([up_a_ref[0], up_b_ref[0]], axis=0), rhs, (1, 1))
 
         @pl.when(n == 0)
         def _():
-            total[...] = product + before_refs[0][...] if before else product
-            ranks[...] = ranked
-
-        @pl.when(n > 0)
-        def _():
-            total[...] += product
-            ranks[...] += ranked
+            rhs[:rows] = a_ref[...]
+            rhs[rows:] = b_ref[...]
+
+        total = dot(w_ref[...], rhs[...], (1, 1)).T
+        out_ref[...] = total
+        sent_ref[...] = total.astype(first.dtype)
 
         @pl.when(n == pl.num_programs(0) - 1)
         def _():
+            ranks = dot(jnp.concatenate([up_a_ref[0], up_b_ref[0]], axis=0), rhs[...], (1, 1))
             for at, place in enumerate(places):
                 value = ranks[at * rank : (at + 1) * rank, at * rows : (at + 1) * rows]
                 alive = lax.broadcasted_iota(jnp.int32, (rank, rows), 1) < facts_ref[groups + place]
                 alive = alive & (facts_ref[place] >= 0)
-                value = jnp.where(alive, value * adapter_scale, 0.0)
-                if before:
-                    value += before_refs[1][:, at * rows : (at + 1) * rows]
-                outs[0][:, at * rows : (at + 1) * rows] = value
-            if finish:
-                for m in range(0, count, 256):
-                    turned = total[m : m + 256].T
-                    outs[1][:, m : m + 256] = turned
-                    outs[2][:, m : m + 256] = turned.astype(first.dtype)
-            else:
-                outs[1][...] = total[...]
+                rank_ref[:, at * rows : (at + 1) * rows] = jnp.where(alive, value * adapter_scale, 0.0)
 
     def chosen_slot(place):
-        return lambda n, facts_ref: (jnp.maximum(facts_ref[place], 0), 0, n + base)
-
-    whole = lambda n, facts_ref: (0, 0)
-    outs = [(pl.BlockSpec((rank, 2 * rows), whole), jax.ShapeDtypeStruct((rank, 2 * rows), jnp.float32))]
-    if finish:
-        outs += [
-            (
-                pl.BlockSpec((2 * rows, count), lambda n, facts_ref: (0, part)),
-                jax.ShapeDtypeStruct((2 * rows, depth), jnp.float32),
-            ),
-            (
-                pl.BlockSpec((2 * rows, count), lambda n, facts_ref: (half, part)),
-                jax.ShapeDtypeStruct((4 * rows, depth), first.dtype),
-            ),
-        ]
-    else:
-        outs += [(pl.BlockSpec((count, 2 * rows), whole), jax.ShapeDtypeStruct((count, 2 * rows), jnp.float32))]
-    at = 6 + len(before)
+        return lambda n, facts_ref: (jnp.maximum(facts_ref[place], 0), 0, 0)
+
     return pl.pallas_call(
         kernel,
         grid_spec=pltpu.PrefetchScalarGridSpec(
             num_scalar_prefetch=1,
-            grid=(hidden // block,),
+            grid=(depth // block,),
             in_specs=[
-                pl.BlockSpec((rows, block), lambda n, facts_ref: (0, n)),
-                pl.BlockSpec((rows, block), lambda n, facts_ref: (0, n)),
-                pl.BlockSpec((count, block), lambda n, facts_ref: (part, n + base)),
-                *[pl.BlockSpec((1, rank, block), chosen_slot(place)) for place in places],
-                *[pl.BlockSpec(x.shape, whole) for x in before],
-                *[pl.BlockSpec(memory_space=pl.ANY)] * len(grads),
+                pl.BlockSpec(memory_space=pltpu.VMEM),
+                pl.BlockSpec(memory_space=pltpu.VMEM),
+                pl.BlockSpec((block, hidden), lambda n, facts_ref: (n, 0)),
+                *[pl.BlockSpec((1, rank, hidden), chosen_slot(place)) for place in places],
+                *[pl.BlockSpec(memory_space=pl.ANY)] * len(sent),
             ],
-            out_specs=[o[0] for o in outs],
-            scratch_shapes=[
-                pltpu.VMEM((count, 2 * rows), jnp.float32),
-                pltpu.VMEM((2 * rank, 2 * rows), jnp.float32),
+            out_specs=[
+                pl.BlockSpec((2 * rows, block), lambda n, facts_ref: (0, n)),
+                pl.BlockSpec((2 * rows, block), lambda n, facts_ref: (half, n)),
+                pl.BlockSpec((rank, 2 * rows), lambda n, facts_ref: (0, 0)),
             ],
+            scratch_shapes=[pltpu.VMEM((2 * rows, hidden), first.dtype)],
         ),
-        out_shape=[o[1] for o in outs],
-        input_output_aliases={at + n: (1 if x.dtype == jnp.float32 else 2) for n, x in enumerate(grads)},
+        out_shape=[
+            jax.ShapeDtypeStruct((2 * rows, depth), jnp.float32),
+            jax.ShapeDtypeStruct((4 * rows, depth), first.dtype),
+            jax.ShapeDtypeStruct((rank, 2 * rows), jnp.float32),
+        ],
+        input_output_aliases={6: 1} if sent else {},
         compiler_params=pltpu.CompilerParams(vmem_limit_bytes=VMEM),
-        cost_estimate=cost(4 * rows * hidden * count, 2 * hidden * (count + 2 * rows)),
+        cost_estimate=cost(4 * rows * hidden * depth, 2 * hidden * (depth + 2 * rows)),
         name="return_grad",
-    )(facts, first, second, weight, store, store, *before, *grads)
+    )(facts, first, second, weight, store, store, *sent)
 
 
 def rank_inner(facts, flat, blocks, rank):
@@ -244,7 +216,7 @@
         out_specs=pl.BlockSpec((span, block), lambda n: (0, n)),
         out_shape=jax.ShapeDtypeStruct((span, columns), jnp.float32),
         compiler_params=pltpu.CompilerParams(vmem_limit_bytes=VMEM),
-        cost_estimate=cost(2 * span * tokens * columns, (4 * span + 2 * tokens) * columns),
+        cost_estimate=cost(2 * span * tokens * columns, (4 * span + 2 * tokens) * columns, 1),
         name="slot_grad",
     )(wide_t, *arrays)
 
@@ -353,55 +325,42 @@
 
     tok_x = swap(tokens, CHIP)
     cot_c = swap(cotangent, CORE)
-    middle, half = hidden // 2, depth // 2
     away = i ^ j
     here = jnp.stack([i, away]).astype(jnp.int32)
     down_t = jnp.swapaxes(adapter_down, 1, 2)
     near, rest, facts = choose(block_adapter, block_length, adapter_slot, here, down_t)
     up_flat = adapter_up.reshape(span, hidden)
-    near = swap(near, CORE)
-
-    back01, *grads = return_grad(
-        facts, after(cotangent, near), cot_c, weight, adapter_up, (0, 1), (0, half), (0, hidden), 1024
-    )
-    down_x = swap(rest[:rank] + near[rank:], CHIP)
-    even = jnp.concatenate([tokens, after(tok_x, grads[0], down_x)], axis=0)
+
+    even = jnp.concatenate([tokens, after(tok_x, facts)], axis=0)
     odd = swap(even, CORE)
     even_far = both(even, hop)
-    cot_a = swap(after(cotangent[:, :middle], even), CHIP)
-    cot_b = swap(after(cotangent[:, middle:], even), CHIP)
-    _, grad01, parts = return_grad(
-        facts, after(cotangent, even), cot_c, weight, adapter_up, (0, 1), (half, depth), (0, hidden), 1024, grads=grads
-    )
+    cot_x = swap(after(cotangent, even), CHIP)
+    near = swap(after(near, even), CORE)
+    grad01, parts, back01 = return_grad(facts, after(cotangent, even), cot_c, weight, adapter_up, (0, 1))
     odd = after(odd, grad01)
     odd_far = both(odd, hop)
     toks = [(even, 0), (odd, 0), (even, 1), (odd, 1)]
     inner = rank_inner(facts, down_t.reshape(span, width), toks, rank)
-    down_mine = both(rest[rank:] + near[:rank] + down_x, place)
-    cot_ac = swap(after(cot_a, inner), CORE)
-    inner = inner + along(inner, 1)
+    down_x = rest[:rank] + after(near, inner)[rank:]
+    inner = after(inner, down_x) + along(inner, 1)
     inner_far = along(inner, 2)
-    even_mid = jnp.where(away == 0, even, after(even_far, inner, down_mine))
+    even_mid = jnp.where(away == 0, even, after(even_far, inner))
     even_all = both(even_mid, hops)
-    back23, sums = return_grad(
-        facts, after(cot_a, even_mid), cot_ac, weight, adapter_up, (2, 3), (0, depth), (0, middle), 512, finish=False
-    )
-    cot_bc = swap(after(cot_b, sums), CORE)
-    odd_mid = jnp.where(away == 0, odd, after(odd_far, sums, cot_b))
+    odd_mid = jnp.where(away == 0, odd, after(odd_far, even_mid))
     odd_all = both(odd_mid, hops)
-    back23, grad23, parts = return_grad(
-        facts, after(cot_b, odd_mid, even_all), cot_bc, weight, adapter_up, (2, 3), (0, depth), (middle, hidden), 512,
-        before=(sums, back23), grads=(parts,),
-    )
+    cot_xc = swap(after(cot_x, odd_mid, even_all), CORE)
+    down_x = swap(after(down_x, cot_x), CHIP)
+    grad23, parts, back23 = return_grad(facts, after(cot_x, odd_mid), cot_xc, weight, adapter_up, (2, 3), (parts,))
+    down_mine = both(rest[rank:] + near[:rank] + after(down_x, grad23), place)
     back = jnp.concatenate([back01, back23], axis=1)
-    back = back + along(back, 1)
-    all_even = jnp.where(away == 0, even, jnp.where(away == 2, even_far, after(even_all, back)))
-    back_wide, _, back_b = spread(facts, after(back, all_even), along(back, 2), per_owner, 1.0)
+    all_even = jnp.where(away == 0, even, jnp.where(away == 2, even_far, after(even_all, grad23)))
+    all_odd = jnp.where(away == 0, odd, jnp.where(away == 2, odd_far, after(odd_all, all_even)))
+    all_tokens = jnp.concatenate([all_even, all_odd], axis=0)
+    back = after(back, all_tokens) + along(back, 1)
+    back_wide, _, back_b = spread(facts, back, along(back, 2), per_owner, 1.0)
     inner_wide, inner_rows, _ = spread(facts, after(inner, back_b), inner_far, per_owner, adapter_scale)
-    back_b = share(after(back_b, inner_wide), swap(back_b, CORE), CORE)
+    back_b = share(after(back_b, inner_wide, down_mine), swap(back_b, CORE), CORE)
     parts = lax.all_to_all(after(parts, back_b).reshape(shards, rows, depth), "tp", 0, 0, tiled=True)
-    all_odd = jnp.where(away == 0, odd, jnp.where(away == 2, odd_far, after(odd_all, back_b)))
-    all_tokens = jnp.concatenate([all_even, all_odd], axis=0)
 
     def grad_block(q):
         low, high = [lax.dynamic_slice_in_dim(x, (q & 1) * rows, rows, 0) for x in (grad01, grad23)]
@@ -439,18 +398,18 @@
     point = make(3, point)
     point = finish(1, point)
     point = cross(2, point)
-    point = cross(3, point)
-    cots = [([cotangent], 0), ([cot_c], 0), ([cot_a, cot_b], 0), ([cot_ac, cot_bc], 0)]
-    up_wide = slot_grad(after(inner_wide, point), cots, hidden // 4)
-    point = finish(2, up_wide)
+    down_wide = slot_grad(after(back_wide, point), [([x], n) for x, n in toks], width // 2)
     back_mine = lax.dynamic_slice_in_dim(back_b, j * rows, rows, 1)
     total = grad_block(j)
     for m in range(1, shards):
-        total = total + lax.dynamic_index_in_dim(after(parts, point), j ^ m, 0, False).astype(jnp.float32)
+        total = total + lax.dynamic_index_in_dim(after(parts, down_wide), j ^ m, 0, False).astype(jnp.float32)
     total = (total + dot(back_mine, down_mine, (0, 0))).astype(b16)
     tokens_grad = both(total, [(b, a) for a, b in place])
-    down_wide = slot_grad(after(back_wide, total), [([x], n) for x, n in toks], width // 2)
-    finish(3, down_wide)
+    cots = [([x], 0) for x in (cotangent, cot_c, cot_x, cot_xc)]
+    point = cross(3, total)
+    up_wide = slot_grad(after(inner_wide, point), cots, hidden // 4)
+    point = finish(2, up_wide)
+    finish(3, point)
     projected = jnp.concatenate(done, axis=1)
     up_grad = up_wide.reshape(per_owner, rank, hidden)
     down_grad = jnp.swapaxes(down_wide.reshape(per_owner, rank, width), 1, 2)

time: 248 us -> 238 us (0.960)
  starting transfers between devices: 34.1 us -> 44.7 us
  waiting for transfers between devices: 68.4 us -> 59.5 us
  local copies, waits for them, and re-layouts: 22.9 us -> 14.2 us
  Pallas kernels: 97.3 us -> 92.1 us
    ppermute x19 -> x17, starting transfers between devices: 7.26 us -> 20.5 us  [swap(): return lax.ppermute(x, 'dp', [(d, d ^ bit) for d in range(groups)])]
    ppermute x19 -> x17, waiting for transfers between devices: 23.4 us -> 11.4 us  [swap(): return lax.ppermute(x, 'dp', [(d, d ^ bit) for d in range(groups)])]
    pallas_call x4 -> x2, Pallas kernels: 48 us -> 39.3 us  [return_grad(): pl.pallas_call(kernel, grid_spec=pltpu.PrefetchScalarGridSpec(num_scalar_...]
    unnamed x101 -> x63, local copies, waits for them, and re-layouts: 21.8 us -> 14.2 us
    ppermute x6, starting transfers between devices: 19.4 us -> 15 us  [both(): return lax.ppermute(x, ('tp', 'dp'), pairs)]
    all_to_all x1, waiting for transfers between devices: 0.01 us -> 3.73 us  [local_square(): lax.all_to_all(after(parts, back_b).reshape(shards, rows, depth), 'tp', 0...]
    pallas_call x4, Pallas kernels: 30.8 us -> 33.8 us  [project(): pl.pallas_call(kernel, grid=((stop - start) // block,), in_specs=[pl.Bloc...]
  transfers between devices with their start and end apart: 30 -> 28, of which waited for: 11 -> 9; matrix products, arithmetic and copies ran while one was open for 10% -> 11% of each run, Pallas kernels for 31% -> 35%
where the time goes in v9:
time: 238 us; the launch traced here: 236 us
  Pallas kernels  92.1 us (39%)
  waiting for transfers between devices  59.5 us (25%)
  starting transfers between devices  44.7 us (19%)
  other arithmetic  22.2 us (9%)
  local copies, waits for them, and re-layouts  14.2 us (6%)
  matrix products  2.64 us (1%)
    pallas_call x2, Pallas kernels, return_grad(): pl.pallas_call(kernel, grid_spec=pltpu.PrefetchScalarGridSpec(num_scalar_...  39.3 us
    pallas_call x4, Pallas kernels, project(): pl.pallas_call(kernel, grid=((stop - start) // block,), in_specs=[pl.Bloc...  33.8 us
    ppermute x6, waiting for transfers between devices, both(): return lax.ppermute(x, ('tp', 'dp'), pairs)  23.6 us
    ppermute x4, waiting for transfers between devices, along(): return lax.ppermute(x, 'tp', [(z, z ^ bit) for z in range(shards)])  20.8 us
    ppermute x17, starting transfers between devices, swap(): return lax.ppermute(x, 'dp', [(d, d ^ bit) for d in range(groups)])  20.5 us
    ppermute x6, starting transfers between devices, both(): return lax.ppermute(x, ('tp', 'dp'), pairs)  15 us
    unnamed x63, local copies, waits for them, and re-layouts  14.2 us
    pallas_call x2, Pallas kernels, slot_grad(): pl.pallas_call(kernel, grid=(columns // block,), in_specs=[pl.BlockSpec((...  12.6 us
  transfers between devices with their start and end apart: 28, of which 9 were waited for; matrix products, arithmetic and copies ran while one was open for 11% of the time, Pallas kernels for 35%

profile of v9, /device:TPU:2, one launch (start us, length us, event | category | flops | bytes accessed | tf_op | source)
XLA Modules:
  0.0 236.4 jit_solution(6268206370817525597)
XLA Ops:
  0.9 1.6 copy-done.6
  2.5 0.7 copy-done.21
  3.1 0.7 copy-done.22
  4.4 1.5 choose.1
  6.0 9.3 %collective-permute-done = bf16[128,2048]{1,0:T(8,128)(2,1)S(1)} collective-permute-done((bf16[128,2048]{1,0:T(8,128)(2,1)}, bf16[128,2048]{1,0:T(8,128)(2,1)S(1)}, u32[]{:S(2)}, u32[]{:S(2)}) %collective-permute-start) | collective-permute-done | bytes 524320 | tf_op jit(solution)/shard_map/ppermute | solution.py:311
  15.4 1.3 collective-permute-start.1
  16.7 0.8 collective-permute-start.4
  17.5 3.9 %collective-permute-start.7 = (bf16[128,7168]{1,0:T(8,128)(2,1)}, bf16[128,7168]{1,0:T(8,128)(2,1)}, u32[]{:S(2)}, u32[]{:S(2)}) collective-permute-start(bf16[128,7168]{1,0:T(8,128)(2,1)} %refs_0_.1), channel_id=1, source_target_pairs={{0,2},{1,3},{2,0},{3,1},{4,6},{5,7},{6,4},{7,5},{8,10},{9,11},{10,... | collective-permute-start | bytes 5505032 | tf_op jit(solution)/shard_map/ppermute | solution.py:311
  21.4 1.5 copy-done.8
  22.9 19.9 %return_grad.2 = (f32[256,2048]{1,0:T(8,128)S(1)}, bf16[512,2048]{1,0:T(8,128)(2,1)}, f32[64,256]{1,0:T(8,128)S(1)}) custom-call(s32[9]{0:T(128)S(1)} %get-tuple-element.59.facts_ref, bf16[128,7168]{1,0:T(8,128)(2,1)S(1)} %copy-done.8, bf16[128,7168]{1,0:T(8,128)(2,1)} %collective-permute-done.3.b_ref.refs_1_, bf16[2048,7168]{1,0:T(8,128)(2,1)} %w_ref.11, ...), custom_call_target="tpu_custom_call" | custom-call | flops 117440512 | bytes 516096 | tf_op jit(solution)/shard_map/return_grad/pallas_call | solution.py:88
  42.8 1.3 copy-done.15
  44.2 1.3 collective-permute-start.8
  45.5 1.8 rank_inner.1
  47.3 1.3 collective-permute-start.5
  48.6 1.0 slice_add_fusion.9
  49.6 3.1 %collective-permute-done.5 = f32[64,512]{1,0:T(8,128)S(1)} collective-permute-done((f32[64,512]{1,0:T(8,128)S(1)}, f32[64,512]{1,0:T(8,128)S(1)}, u32[]{:S(2)}, u32[]{:S(2)}) %collective-permute-start.5) | collective-permute-done | bytes 131104 | tf_op jit(solution)/shard_map/ppermute | solution.py:314
  52.7 1.3 broadcast_select_fusion.1
  54.0 4.5 %collective-permute-start.6 = (bf16[256,2048]{1,0:T(8,128)(2,1)S(1)}, bf16[256,2048]{1,0:T(8,128)(2,1)}, u32[]{:S(2)}, u32[]{:S(2)}) collective-permute-start(bf16[256,2048]{1,0:T(8,128)(2,1)S(1)} %broadcast_select_fusion.1), channel_id=1, source_target_pairs={{0,4},{8,12},{5,1},{13,9},{10,14},{2,6},{15,11},{7,3},{16,20},{24,... | collective-permute-start | bytes 3145736 | tf_op jit(solution)/shard_map/ppermute | solution.py:324
  58.5 14.5 %collective-permute-done.8 = bf16[256,2048]{1,0:T(8,128)(2,1)S(1)} collective-permute-done((bf16[256,2048]{1,0:T(8,128)(2,1)S(1)}, bf16[256,2048]{1,0:T(8,128)(2,1)S(1)}, u32[]{:S(2)}, u32[]{:S(2)}) %collective-permute-start.8) | collective-permute-done | bytes 1048608 | tf_op jit(solution)/shard_map/ppermute | solution.py:324
  73.1 1.0 copy-done.24
  74.0 1.1 broadcast_select_fusion
  75.1 3.3 %collective-permute-start.9 = (bf16[128,7168]{1,0:T(8,128)(2,1)}, bf16[128,7168]{1,0:T(8,128)(2,1)}, u32[]{:S(2)}, u32[]{:S(2)}) collective-permute-start(bf16[128,7168]{1,0:T(8,128)(2,1)} %collective-permute-done.7.a_ref.refs_2_), channel_id=1, source_target_pairs={{0,1},{1,0},{2,3},{3,2},{4,5},{5,4},{6,7},{7,6},{8,9},{9,8},{10,11... | collective-permute-start | bytes 5505032 | tf_op jit(solution)/shard_map/ppermute | solution.py:311
  78.5 2.6 %collective-permute-start.10 = (bf16[256,2048]{1,0:T(8,128)(2,1)}, bf16[256,2048]{1,0:T(8,128)(2,1)}, u32[]{:S(2)}, u32[]{:S(2)}) collective-permute-start(bf16[256,2048]{1,0:T(8,128)(2,1)} %broadcast_select_fusion), channel_id=1, source_target_pairs={{0,4},{8,12},{5,1},{13,9},{10,14},{2,6},{15,11},{7,3},{16,20},{24,... | collective-permute-start | bytes 3145736 | tf_op jit(solution)/shard_map/ppermute | solution.py:324
  81.1 4.5 %collective-permute-start.14 = (bf16[64,2048]{1,0:T(8,128)(2,1)S(1)}, bf16[64,2048]{1,0:T(8,128)(2,1)S(1)}, u32[]{:S(2)}, u32[]{:S(2)}) collective-permute-start(bf16[64,2048]{1,0:T(8,128)(2,1)S(1)} %slice_add_fusion.9), channel_id=1, source_target_pairs={{0,2},{1,3},{2,0},{3,1},{4,6},{5,7},{6,4},{7,5},{8,10},{9,11},{10,... | collective-permute-start | bytes 786440 | tf_op jit(solution)/shard_map/ppermute | solution.py:311
  85.6 19.4 %return_grad.3 = (f32[256,2048]{1,0:T(8,128)S(1)}, bf16[512,2048]{1,0:T(8,128)(2,1)}, f32[64,256]{1,0:T(8,128)S(1)}) custom-call(s32[9]{0:T(128)S(1)} %get-tuple-element.59.facts_ref, bf16[128,7168]{1,0:T(8,128)(2,1)} %collective-permute-done.7.a_ref.refs_2_, ...), custom_call_target="tpu_custom_call", output_to_operand_aliasing={{1}: (6, {})} | custom-call | flops 117440512 | bytes 516096 | tf_op jit(solution)/shard_map/return_grad/pallas_call | solution.py:88
  105.1 2.1 select_select_fusion.1
  107.4 1.0 fusion.13
  108.4 3.4 %collective-permute-start.15 = (bf16[64,2048]{1,0:T(8,128)(2,1)S(1)}, bf16[64,2048]{1,0:T(8,128)(2,1)S(1)}, u32[]{:S(2)}, u32[]{:S(2)}) collective-permute-start(bf16[64,2048]{1,0:T(8,128)(2,1)S(1)} %fusion.13), channel_id=1, source_target_pairs={{0,0},{4,5},{8,10},{12,15},{1,4},{5,1},{9,14},{13,11},{2,8},{6,13}... | collective-permute-start | bytes 786440 | tf_op jit(solution)/shard_map/ppermute | solution.py:324
  111.9 1.6 pad_maximum_fusion.tok_ref
  113.5 2.7 %collective-permute-start.12 = (f32[64,512]{1,0:T(8,128)S(1)}, f32[64,512]{1,0:T(8,128)S(1)}, u32[]{:S(2)}, u32[]{:S(2)}) collective-permute-start(f32[64,512]{1,0:T(8,128)S(1)} %add.88.refs_0_), channel_id=1, source_target_pairs={{0,8},{4,12},{8,0},{12,4},{1,9},{5,13},{9,1},{13,5},{2,10},{6,14},... | collective-permute-start | bytes 393224 | tf_op jit(solution)/shard_map/ppermute | solution.py:314
  116.5 17.5 %collective-permute-done.12.refs_1_ = f32[64,512]{1,0:T(8,128)S(1)} collective-permute-done((f32[64,512]{1,0:T(8,128)S(1)}, f32[64,512]{1,0:T(8,128)S(1)}, u32[]{:S(2)}, u32[]{:S(2)}) %collective-permute-start.12) | collective-permute-done | bytes 131104 | tf_op jit(solution)/shard_map/ppermute | solution.py:314
  134.1 1.7 spread.2
  135.7 0.8 copy-done.19
  136.9 1.4 spread.3
  138.3 0.8 copy-done.17
  139.2 0.7 copy-done.29
  139.8 9.8 %project.4 = (f32[256,2048]{1,0:T(8,128)S(1)}, f32[256,2048]{1,0:T(8,128)}) custom-call(bf16[512,2048]{1,0:T(8,128)(2,1)} %pad_maximum_fusion.tok_ref, bf16[512,512]{1,0:T(8,128)(2,1)S(1)} %get-tuple-element.87.wide_ref, bf16[2048,7168]{1,0:T(8,128)(2,1)} %w_ref.11, bf16[512,7168]{1,0:T(8,128)(2,1)} %bitcast.23), custom_call_target="tpu_custom_call" | custom-call | flops 83886080 | bytes 229376 | tf_op jit(solution)/shard_map/project/pallas_call | solution.py:39
  149.7 1.4 copy-done.10
  151.2 4.7 %all-to-all-start = ((bf16[4,128,2048]{2,1,0:T(8,128)(2,1)}), bf16[4,128,2048]{2,1,0:T(8,128)(2,1)}, u32[]{:S(2)}, u32[]{:S(2)}) async-start(bf16[4,128,2048]{2,1,0:T(8,128)(2,1)} %bitcast.28), calls=%async_computation | async-start | bytes 4194304 | tf_op jit(solution)/shard_map/all_to_all | solution.py:363
  156.0 1.0 copy-done.5
  157.0 6.7 %project.5 = (f32[256,1536]{1,0:T(8,128)S(1)}, f32[256,1536]{1,0:T(8,128)S(1)}) custom-call(bf16[512,2048]{1,0:T(8,128)(2,1)S(1)} %copy-done, bf16[512,512]{1,0:T(8,128)(2,1)S(1)} %copy-done.5, bf16[2048,7168]{1,0:T(8,128)(2,1)} %w_ref.11, bf16[512,7168]{1,0:T(8,128)(2,1)} %bitcast.24), custom_call_target="tpu_custom_call" | custom-call | flops 62914560 | bytes 172032 | tf_op jit(solution)/shard_map/project/pallas_call | solution.py:39
  164.1 1.5 fusion.6
  165.6 2.1 collective-permute-start.19
  168.4 9.8 %project.6 = (f32[256,2048]{1,0:T(8,128)S(1)}, f32[256,2048]{1,0:T(8,128)}) custom-call(bf16[512,2048]{1,0:T(8,128)(2,1)} %pad_maximum_fusion.tok_ref, bf16[512,512]{1,0:T(8,128)(2,1)S(1)} %copy-done.5, bf16[2048,7168]{1,0:T(8,128)(2,1)} %w_ref.11, bf16[512,7168]{1,0:T(8,128)(2,1)} %bitcast.25), custom_call_target="tpu_custom_call" | custom-call | flops 83886080 | bytes 229376 | tf_op jit(solution)/shard_map/project/pallas_call | solution.py:39
  178.2 1.6 collective-permute-done.19
  179.9 2.2 fusion.5
  182.2 1.8 collective-permute-start.21
  184.0 7.5 %project.7 = (f32[256,1536]{1,0:T(8,128)S(1)}, f32[256,1536]{1,0:T(8,128)}) custom-call(bf16[512,2048]{1,0:T(8,128)(2,1)S(1)} %copy-done.1, bf16[512,512]{1,0:T(8,128)(2,1)S(1)} %copy-done.5, bf16[2048,7168]{1,0:T(8,128)(2,1)} %w_ref.11, bf16[512,7168]{1,0:T(8,128)(2,1)} %bitcast.26), custom_call_target="tpu_custom_call" | custom-call | flops 62914560 | bytes 172032 | tf_op jit(solution)/shard_map/project/pallas_call | solution.py:39
  191.5 1.1 copy-done.12
  193.0 1.7 fusion.11
  194.7 2.1 fusion.3
  196.8 1.3 collective-permute-start.24
  198.2 2.9 %slot_grad.2 = f32[512,2048]{1,0:T(8,128)} custom-call(bf16[512,512]{1,0:T(8,128)(2,1)S(1)} %copy-done.20, bf16[256,2048]{1,0:T(8,128)(2,1)S(1)} %constant_dynamic-update-slice_fusion.refs_0_.refs_2_, bf16[256,2048]{1,0:T(8,128)(2,1)S(1)} %copy-done.3, bf16[256,2048]{1,0:T(8,128)(2,1)S(1)} %constant_dynamic-update-slice_fusion.refs_0_.refs_2_, ...), custom_call_target="tpu_custom_call" | custom-call | flops 1073741824 | bytes 6291456 | tf_op jit(solution)/shard_map/slot_grad/pallas_call | solution.py:212
  201.1 3.7 %all-to-all-done = bf16[4,128,2048]{2,1,0:T(8,128)(2,1)} async-done(((bf16[4,128,2048]{2,1,0:T(8,128)(2,1)}), bf16[4,128,2048]{2,1,0:T(8,128)(2,1)}, u32[]{:S(2)}, u32[]{:S(2)}) %all-to-all-start) | async-done | bytes 2097184 | tf_op jit(solution)/shard_map/all_to_all | solution.py:363
  204.8 2.6 %fusion = bf16[128,2048]{1,0:T(8,128)(2,1)S(1)} fusion(bf16[64,2048]{1,0:T(8,128)(2,1)} %copy-done.29, f32[256,2048]{1,0:T(8,128)} %copy-done.16, s32[]{:T(128)S(6)} %select_n.64, f32[256,2048]{1,0:T(8,128)} %copy-done.15, bf16[4,128,2048]{2,1,0:T(8,128)(2,1)} %all-to-all-done, s32[]{:T(128)S(6)} %select_n.68, s32[]{:T(128)S(6)} %select_n.67, ...), kind=kOutput, calls=%fused_computation.1 | convolution fusion | flops 35913728 | bytes 4472853 | tf_op jit(solution)/shard_map/dot_general | solution.py:18
  207.5 1.3 fusion.9
  208.8 1.8 collective-permute-start.25
  210.7 1.9 collective-permute-start.26
  212.6 9.7 %slot_grad.3 = f32[512,7168]{1,0:T(8,128)} custom-call(bf16[512,512]{1,0:T(8,128)(2,1)S(1)} %copy-done.18, bf16[128,7168]{1,0:T(8,128)(2,1)S(1)} %copy-done.9, bf16[128,7168]{1,0:T(8,128)(2,1)} %collective-permute-done.3.b_ref.refs_1_, bf16[128,7168]{1,0:T(8,128)(2,1)} %collective-permute-done.7.a_ref.refs_2_, ...), custom_call_target="tpu_custom_call" | custom-call | flops 3758096384 | bytes 22020096 | tf_op jit(solution)/shard_map/slot_grad/pallas_call | solution.py:212
  222.3 1.6 fusion.2
  223.9 1.3 fusion.8
  225.1 1.4 pad_maximum_fusion.1
  226.5 9.0 %collective-permute-done.26 = bf16[128,2048]{1,0:T(8,128)(2,1)S(1)} collective-permute-done((bf16[128,2048]{1,0:T(8,128)(2,1)S(1)}, bf16[128,2048]{1,0:T(8,128)(2,1)S(1)}, u32[]{:S(2)}, u32[]{:S(2)}) %collective-permute-start.26) | collective-permute-done | bytes 524320 | tf_op jit(solution)/shard_map/ppermute | solution.py:324
  235.6 0.8 copy.17
  (93 shorter events, 3.8 us)
Async XLA Ops:
  0.6 20.8 %collective-permute-start.3 = (bf16[128,7168]{1,0:T(8,128)(2,1)}, bf16[128,7168]{1,0:T(8,128)(2,1)}, u32[]{:S(2)}, u32[]{:S(2)}) collective-permute-start(bf16[128,7168]{1,0:T(8,128)(2,1)} %refs_0_.1), channel_id=1, source_target_pairs={{0,1},{1,0},{2,3},{3,2},{4,5},{5,4},{6,7},{7,6},{8,9},{9,8},{10,11... | collective-permute-start | bytes 5505032 | tf_op jit(solution)/shard_map/ppermute | solution.py:311
  0.7 14.5 %collective-permute-start = (bf16[128,2048]{1,0:T(8,128)(2,1)}, bf16[128,2048]{1,0:T(8,128)(2,1)S(1)}, u32[]{:S(2)}, u32[]{:S(2)}) collective-permute-start(bf16[128,2048]{1,0:T(8,128)(2,1)} %param.8), channel_id=1, source_target_pairs={{0,2},{1,3},{2,0},{3,1},{4,6},{5,7},{6,4},{7,5},{8,10},{9,11},{10,... | collective-permute-start | bytes 1572872 | tf_op jit(solution)/shard_map/ppermute | solution.py:311
  0.9 1.6 copy-start.6
  2.5 0.7 copy-start.21
  3.1 0.7 copy-start.22
  3.8 0.7 copy-start.23
  4.4 1.5 copy-start.28
  15.3 28.9 %collective-permute-start.2 = (bf16[256,2048]{1,0:T(8,128)(2,1)S(1)}, bf16[256,2048]{1,0:T(8,128)(2,1)S(1)}, u32[]{:S(2)}, u32[]{:S(2)}) collective-permute-start(bf16[256,2048]{1,0:T(8,128)(2,1)S(1)} %constant_dynamic-update-slice_fusion.refs_0_.refs_2_), channel_id=1, source_target_pairs={{0,1},{1,0},{2,3},{3,2},{4,5},{5,4},{6,7},{7,6},{8,9},{9,8},{10,11... | collective-permute-start | bytes 3145736 | tf_op jit(solution)/shard_map/ppermute | solution.py:311
  15.4 37.3 %collective-permute-start.1 = (bf16[256,2048]{1,0:T(8,128)(2,1)S(1)}, bf16[256,2048]{1,0:T(8,128)(2,1)}, u32[]{:S(2)}, u32[]{:S(2)}) collective-permute-start(bf16[256,2048]{1,0:T(8,128)(2,1)S(1)} %constant_dynamic-update-slice_fusion.refs_0_.refs_2_), channel_id=1, source_target_pairs={{0,8},{5,13},{10,2},{15,7},{16,24},{21,29},{26,18},{31,23}} | collective-permute-start | bytes 3145736 | tf_op jit(solution)/shard_map/ppermute | solution.py:324
  16.7 31.9 %collective-permute-start.4 = (bf16[128,2048]{1,0:T(8,128)(2,1)S(1)}, bf16[128,2048]{1,0:T(8,128)(2,1)}, u32[]{:S(2)}, u32[]{:S(2)}) collective-permute-start(bf16[128,2048]{1,0:T(8,128)(2,1)S(1)} %get-tuple-element.66), channel_id=1, source_target_pairs={{0,1},{1,0},{2,3},{3,2},{4,5},{5,4},{6,7},{7,6},{8,9},{9,8},{10,11... | collective-permute-start | bytes 1572872 | tf_op jit(solution)/shard_map/ppermute | solution.py:311
  17.5 28.0 %copy-start.7 = (bf16[8,2048,64]{1,2,0:T(8,128)(2,1)S(1)}, bf16[8,2048,64]{1,2,0:T(8,128)(2,1)}, u32[]{:S(2)}) copy-start(bf16[8,2048,64]{1,2,0:T(8,128)(2,1)} %param.10) | copy-start | bytes 6291460
  17.5 57.6 %collective-permute-start.7 = (bf16[128,7168]{1,0:T(8,128)(2,1)}, bf16[128,7168]{1,0:T(8,128)(2,1)}, u32[]{:S(2)}, u32[]{:S(2)}) collective-permute-start(bf16[128,7168]{1,0:T(8,128)(2,1)} %refs_0_.1), channel_id=1, source_target_pairs={{0,2},{1,3},{2,0},{3,1},{4,6},{5,7},{6,4},{7,5},{8,10},{9,11},{10,... | collective-permute-start | bytes 5505032 | tf_op jit(solution)/shard_map/ppermute | solution.py:311
  21.4 1.5 copy-start.8
  42.8 1.3 copy-start.15
  44.2 67.6 %copy-start.2 = (bf16[256,2048]{1,0:T(8,128)(2,1)}, bf16[256,2048]{1,0:T(8,128)(2,1)S(1)}, u32[]{:S(2)}) copy-start(bf16[256,2048]{1,0:T(8,128)(2,1)S(1)} %collective-permute-done.2.refs_1_.refs_3_) | copy-start | bytes 3145732
  44.2 28.9 %collective-permute-start.8 = (bf16[256,2048]{1,0:T(8,128)(2,1)S(1)}, bf16[256,2048]{1,0:T(8,128)(2,1)S(1)}, u32[]{:S(2)}, u32[]{:S(2)}) collective-permute-start(bf16[256,2048]{1,0:T(8,128)(2,1)S(1)} %collective-permute-done.2.refs_1_.refs_3_), channel_id=1, source_target_pairs={{0,8},{5,13},{10,2},{15,7},{16,24},{21,29},{26,18},{31,23}} | collective-permute-start | bytes 3145736 | tf_op jit(solution)/shard_map/ppermute | solution.py:324
  47.3 5.3 %collective-permute-start.5 = (f32[64,512]{1,0:T(8,128)S(1)}, f32[64,512]{1,0:T(8,128)S(1)}, u32[]{:S(2)}, u32[]{:S(2)}) collective-permute-start(f32[64,512]{1,0:T(8,128)S(1)} %rank_inner.1), channel_id=1, source_target_pairs={{0,4},{4,0},{8,12},{12,8},{1,5},{5,1},{9,13},{13,9},{2,6},{6,2},{1... | collective-permute-start | bytes 393224 | tf_op jit(solution)/shard_map/ppermute | solution.py:314
  54.0 21.1 %collective-permute-start.6 = (bf16[256,2048]{1,0:T(8,128)(2,1)S(1)}, bf16[256,2048]{1,0:T(8,128)(2,1)}, u32[]{:S(2)}, u32[]{:S(2)}) collective-permute-start(bf16[256,2048]{1,0:T(8,128)(2,1)S(1)} %broadcast_select_fusion.1), channel_id=1, source_target_pairs={{0,4},{8,12},{5,1},{13,9},{10,14},{2,6},{15,11},{7,3},{16,20},{24,... | collective-permute-start | bytes 3145736 | tf_op jit(solution)/shard_map/ppermute | solution.py:324
  73.1 1.0 copy-start.24
  75.1 10.5 %collective-permute-start.9 = (bf16[128,7168]{1,0:T(8,128)(2,1)}, bf16[128,7168]{1,0:T(8,128)(2,1)}, u32[]{:S(2)}, u32[]{:S(2)}) collective-permute-start(bf16[128,7168]{1,0:T(8,128)(2,1)} %collective-permute-done.7.a_ref.refs_2_), channel_id=1, source_target_pairs={{0,1},{1,0},{2,3},{3,2},{4,5},{5,4},{6,7},{7,6},{8,9},{9,8},{10,11... | collective-permute-start | bytes 5505032 | tf_op jit(solution)/shard_map/ppermute | solution.py:311
  78.5 28.8 %collective-permute-start.10 = (bf16[256,2048]{1,0:T(8,128)(2,1)}, bf16[256,2048]{1,0:T(8,128)(2,1)}, u32[]{:S(2)}, u32[]{:S(2)}) collective-permute-start(bf16[256,2048]{1,0:T(8,128)(2,1)} %broadcast_select_fusion), channel_id=1, source_target_pairs={{0,4},{8,12},{5,1},{13,9},{10,14},{2,6},{15,11},{7,3},{16,20},{24,... | collective-permute-start | bytes 3145736 | tf_op jit(solution)/shard_map/ppermute | solution.py:324
  81.1 24.0 %collective-permute-start.14 = (bf16[64,2048]{1,0:T(8,128)(2,1)S(1)}, bf16[64,2048]{1,0:T(8,128)(2,1)S(1)}, u32[]{:S(2)}, u32[]{:S(2)}) collective-permute-start(bf16[64,2048]{1,0:T(8,128)(2,1)S(1)} %slice_add_fusion.9), channel_id=1, source_target_pairs={{0,2},{1,3},{2,0},{3,1},{4,6},{5,7},{6,4},{7,5},{8,10},{9,11},{10,... | collective-permute-start | bytes 786440 | tf_op jit(solution)/shard_map/ppermute | solution.py:311
  105.1 2.2 copy-start.16
  105.1 6.7 %copy-start.25 = (bf16[256,2048]{1,0:T(8,128)(2,1)S(1)}, bf16[256,2048]{1,0:T(8,128)(2,1)}, u32[]{:S(2)}) copy-start(bf16[256,2048]{1,0:T(8,128)(2,1)} %copy-done.24) | copy-start | bytes 3145732
  107.3 6.2 %collective-permute-start.11 = (f32[64,512]{1,0:T(8,128)S(1)}, f32[64,512]{1,0:T(8,128)S(1)}, u32[]{:S(2)}, u32[]{:S(2)}) collective-permute-start(f32[64,512]{1,0:T(8,128)S(1)} %constant_dynamic-update-slice_fusion.2), channel_id=1, source_target_pairs={{0,4},{4,0},{8,12},{12,8},{1,5},{5,1},{9,13},{13,9},{2,6},{6,2},{1... | collective-permute-start | bytes 393224 | tf_op jit(solution)/shard_map/ppermute | solution.py:314
  108.4 30.7 %collective-permute-start.15 = (bf16[64,2048]{1,0:T(8,128)(2,1)S(1)}, bf16[64,2048]{1,0:T(8,128)(2,1)S(1)}, u32[]{:S(2)}, u32[]{:S(2)}) collective-permute-start(bf16[64,2048]{1,0:T(8,128)(2,1)S(1)} %fusion.13), channel_id=1, source_target_pairs={{0,0},{4,5},{8,10},{12,15},{1,4},{5,1},{9,14},{13,11},{2,8},{6,13}... | collective-permute-start | bytes 786440 | tf_op jit(solution)/shard_map/ppermute | solution.py:324
  113.5 20.5 %collective-permute-start.12 = (f32[64,512]{1,0:T(8,128)S(1)}, f32[64,512]{1,0:T(8,128)S(1)}, u32[]{:S(2)}, u32[]{:S(2)}) collective-permute-start(f32[64,512]{1,0:T(8,128)S(1)} %add.88.refs_0_), channel_id=1, source_target_pairs={{0,8},{4,12},{8,0},{12,4},{1,9},{5,13},{9,1},{13,5},{2,10},{6,14},... | collective-permute-start | bytes 393224 | tf_op jit(solution)/shard_map/ppermute | solution.py:314
  116.3 20.6 %collective-permute-start.13 = (f32[64,512]{1,0:T(8,128)S(1)}, f32[64,512]{1,0:T(8,128)S(1)}, u32[]{:S(2)}, u32[]{:S(2)}) collective-permute-start(f32[64,512]{1,0:T(8,128)S(1)} %add.87.refs_0_), channel_id=1, source_target_pairs={{0,8},{4,12},{8,0},{12,4},{1,9},{5,13},{9,1},{13,5},{2,10},{6,14},... | collective-permute-start | bytes 393224 | tf_op jit(solution)/shard_map/ppermute | solution.py:314
  135.7 0.8 copy-start.19
  136.5 2.6 %collective-permute-start.16 = (bf16[64,512]{1,0:T(8,128)(2,1)S(1)}, bf16[64,512]{1,0:T(8,128)(2,1)S(1)}, u32[]{:S(2)}, u32[]{:S(2)}) collective-permute-start(bf16[64,512]{1,0:T(8,128)(2,1)S(1)} %get-tuple-element.85), channel_id=1, source_target_pairs={{0,1},{1,0},{2,3},{3,2},{4,5},{5,4},{6,7},{7,6},{8,9},{9,8},{10,11... | collective-permute-start | bytes 196616 | tf_op jit(solution)/shard_map/ppermute | solution.py:311
  138.3 0.8 copy-start.17
  139.1 10.6 %copy-start.4 = (bf16[512,512]{1,0:T(8,128)(2,1)}, bf16[512,512]{1,0:T(8,128)(2,1)S(1)}, u32[]{:S(2)}) copy-start(bf16[512,512]{1,0:T(8,128)(2,1)S(1)} %get-tuple-element.87.wide_ref) | copy-start | bytes 1572868
  139.1 0.7 copy-start.29
  149.7 1.4 copy-start.10
  151.0 13.1 %collective-permute-start.17 = (f32[256,2048]{1,0:T(8,128)}, f32[256,2048]{1,0:T(8,128)}, u32[]{:S(2)}, u32[]{:S(2)}) collective-permute-start(f32[256,2048]{1,0:T(8,128)} %get-tuple-element.92), channel_id=1, source_target_pairs={{0,1},{1,0},{2,3},{3,2},{4,5},{5,4},{6,7},{7,6},{8,9},{9,8},{10,11... | collective-permute-start | bytes 6291464 | tf_op jit(solution)/shard_map/ppermute | solution.py:311
  151.2 16.5 %collective-permute-start.18 = (bf16[64,512]{1,0:T(8,128)(2,1)S(1)}, bf16[64,512]{1,0:T(8,128)(2,1)S(1)}, u32[]{:S(2)}, u32[]{:S(2)}) collective-permute-start(bf16[64,512]{1,0:T(8,128)(2,1)S(1)} %maximum_add_fusion), channel_id=1, source_target_pairs={{0,2},{1,3},{2,0},{3,1},{4,6},{5,7},{6,4},{7,5},{8,10},{9,11},{10,... | collective-permute-start | bytes 196616 | tf_op jit(solution)/shard_map/ppermute | solution.py:311
  151.2 4.7 %copy-start = (bf16[512,2048]{1,0:T(8,128)(2,1)S(1)}, bf16[512,2048]{1,0:T(8,128)(2,1)}, u32[]{:S(2)}) copy-start(bf16[512,2048]{1,0:T(8,128)(2,1)} %pad_maximum_fusion.tok_ref) | copy-start | bytes 6291460
  151.2 53.6 %all-to-all-start = ((bf16[4,128,2048]{2,1,0:T(8,128)(2,1)}), bf16[4,128,2048]{2,1,0:T(8,128)(2,1)}, u32[]{:S(2)}, u32[]{:S(2)}) async-start(bf16[4,128,2048]{2,1,0:T(8,128)(2,1)} %bitcast.28), calls=%async_computation | async-start | bytes 4194304 | tf_op jit(solution)/shard_map/all_to_all | solution.py:363
  156.0 1.0 copy-start.5
  157.0 7.1 %copy-start.11 = (f32[256,2048]{1,0:T(8,128)S(1)}, f32[256,2048]{1,0:T(8,128)}, u32[]{:S(2)}) copy-start(f32[256,2048]{1,0:T(8,128)} %copy-done.10) | copy-start | bytes 6291460
  163.7 18.4 %copy-start.14 = (f32[256,1536]{1,0:T(8,128)}, f32[256,1536]{1,0:T(8,128)S(1)}, u32[]{:S(2)}) copy-start(f32[256,1536]{1,0:T(8,128)S(1)} %get-tuple-element.101) | copy-start | bytes 4718596
  163.7 18.4 %collective-permute-start.20 = (f32[256,1536]{1,0:T(8,128)S(1)}, f32[256,1536]{1,0:T(8,128)S(1)}, u32[]{:S(2)}, u32[]{:S(2)}) collective-permute-start(f32[256,1536]{1,0:T(8,128)S(1)} %get-tuple-element.98), channel_id=1, source_target_pairs={{0,1},{1,0},{2,3},{3,2},{4,5},{5,4},{6,7},{7,6},{8,9},{9,8},{10,11... | collective-permute-start | bytes 4718600 | tf_op jit(solution)/shard_map/ppermute | solution.py:311
  165.6 14.2 %collective-permute-start.19 = (bf16[128,2048]{1,0:T(8,128)(2,1)S(1)}, bf16[128,2048]{1,0:T(8,128)(2,1)S(1)}, u32[]{:S(2)}, u32[]{:S(2)}) collective-permute-start(bf16[128,2048]{1,0:T(8,128)(2,1)S(1)} %fusion.6), channel_id=1, source_target_pairs={{0,2},{1,3},{2,0},{3,1},{4,6},{5,7},{6,4},{7,5},{8,10},{9,11},{10,... | collective-permute-start | bytes 1572872 | tf_op jit(solution)/shard_map/ppermute | solution.py:311
  178.2 16.5 %collective-permute-start.22 = (f32[256,2048]{1,0:T(8,128)}, f32[256,2048]{1,0:T(8,128)}, u32[]{:S(2)}, u32[]{:S(2)}) collective-permute-start(f32[256,2048]{1,0:T(8,128)} %get-tuple-element.106), channel_id=1, source_target_pairs={{0,1},{1,0},{2,3},{3,2},{4,5},{5,4},{6,7},{7,6},{8,9},{9,8},{10,11... | collective-permute-start | bytes 6291464 | tf_op jit(solution)/shard_map/ppermute | solution.py:311
  178.2 5.8 %copy-start.1 = (bf16[512,2048]{1,0:T(8,128)(2,1)S(1)}, bf16[512,2048]{1,0:T(8,128)(2,1)}, u32[]{:S(2)}) copy-start(bf16[512,2048]{1,0:T(8,128)(2,1)} %pad_maximum_fusion.tok_ref) | copy-start | bytes 6291460
  182.1 9.3 %copy-start.27 = (f32[256,1536]{1,0:T(8,128)}, f32[256,1536]{1,0:T(8,128)S(1)}, u32[]{:S(2)}) copy-start(f32[256,1536]{1,0:T(8,128)S(1)} %collective-permute-done.20) | copy-start | bytes 4718596
  182.2 10.8 %collective-permute-start.21 = (bf16[128,1536]{1,0:T(8,128)(2,1)S(1)}, bf16[128,1536]{1,0:T(8,128)(2,1)}, u32[]{:S(2)}, u32[]{:S(2)}) collective-permute-start(bf16[128,1536]{1,0:T(8,128)(2,1)S(1)} %fusion.12), channel_id=1, source_target_pairs={{0,2},{1,3},{2,0},{3,1},{4,6},{5,7},{6,4},{7,5},{8,10},{9,11},{10,... | collective-permute-start | bytes 1179656 | tf_op jit(solution)/shard_map/ppermute | solution.py:311
  191.4 1.1 copy-start.12
  192.6 14.9 %collective-permute-start.23 = (f32[256,1536]{1,0:T(8,128)}, f32[256,1536]{1,0:T(8,128)}, u32[]{:S(2)}, u32[]{:S(2)}) collective-permute-start(f32[256,1536]{1,0:T(8,128)} %get-tuple-element.110), channel_id=1, source_target_pairs={{0,1},{1,0},{2,3},{3,2},{4,5},{5,4},{6,7},{7,6},{8,9},{9,8},{10,11... | collective-permute-start | bytes 4718600 | tf_op jit(solution)/shard_map/ppermute | solution.py:311
  192.6 5.6 %copy-start.3 = (bf16[256,2048]{1,0:T(8,128)(2,1)S(1)}, bf16[256,2048]{1,0:T(8,128)(2,1)}, u32[]{:S(2)}) copy-start(bf16[256,2048]{1,0:T(8,128)(2,1)} %copy-done.2) | copy-start | bytes 3145732
  192.6 5.6 %copy-start.20 = (bf16[512,512]{1,0:T(8,128)(2,1)S(1)}, bf16[512,512]{1,0:T(8,128)(2,1)}, u32[]{:S(2)}) copy-start(bf16[512,512]{1,0:T(8,128)(2,1)} %copy-done.19) | copy-start | bytes 1572868
  196.8 25.4 %collective-permute-start.24 = (bf16[128,2048]{1,0:T(8,128)(2,1)}, bf16[128,2048]{1,0:T(8,128)(2,1)}, u32[]{:S(2)}, u32[]{:S(2)}) collective-permute-start(bf16[128,2048]{1,0:T(8,128)(2,1)} %fusion.3), channel_id=1, source_target_pairs={{0,2},{1,3},{2,0},{3,1},{4,6},{5,7},{6,4},{7,5},{8,10},{9,11},{10,... | collective-permute-start | bytes 1572872 | tf_op jit(solution)/shard_map/ppermute | solution.py:311
  204.8 2.7 %copy-start.13 = (f32[256,1536]{1,0:T(8,128)S(1)}, f32[256,1536]{1,0:T(8,128)}, u32[]{:S(2)}) copy-start(f32[256,1536]{1,0:T(8,128)} %copy-done.12) | copy-start | bytes 4718596
  204.8 7.8 %copy-start.18 = (bf16[512,512]{1,0:T(8,128)(2,1)S(1)}, bf16[512,512]{1,0:T(8,128)(2,1)}, u32[]{:S(2)}) copy-start(bf16[512,512]{1,0:T(8,128)(2,1)} %copy-done.17) | copy-start | bytes 1572868
  207.5 5.1 %copy-start.9 = (bf16[128,7168]{1,0:T(8,128)(2,1)S(1)}, bf16[128,7168]{1,0:T(8,128)(2,1)}, u32[]{:S(2)}) copy-start(bf16[128,7168]{1,0:T(8,128)(2,1)} %refs_0_.1) | copy-start | bytes 5505028
  208.8 15.0 %collective-permute-start.25 = (bf16[128,1536]{1,0:T(8,128)(2,1)S(1)}, bf16[128,1536]{1,0:T(8,128)(2,1)S(1)}, u32[]{:S(2)}, u32[]{:S(2)}) collective-permute-start(bf16[128,1536]{1,0:T(8,128)(2,1)S(1)} %fusion.9), channel_id=1, source_target_pairs={{0,2},{1,3},{2,0},{3,1},{4,6},{5,7},{6,4},{7,5},{8,10},{9,11},{10,... | collective-permute-start | bytes 1179656 | tf_op jit(solution)/shard_map/ppermute | solution.py:311
  210.7 24.9 %collective-permute-start.26 = (bf16[128,2048]{1,0:T(8,128)(2,1)S(1)}, bf16[128,2048]{1,0:T(8,128)(2,1)S(1)}, u32[]{:S(2)}, u32[]{:S(2)}) collective-permute-start(bf16[128,2048]{1,0:T(8,128)(2,1)S(1)} %fusion), channel_id=1, source_target_pairs={{0,0},{5,4},{10,8},{15,12},{4,1},{1,5},{14,9},{11,13},{8,2},{13,6}... | collective-permute-start | bytes 1572872 | tf_op jit(solution)/shard_map/ppermute | solution.py:324
  222.3 2.9 %copy-start.26 = (bf16[128,2048]{1,0:T(8,128)(2,1)S(1)}, bf16[128,2048]{1,0:T(8,128)(2,1)}, u32[]{:S(2)}) copy-start(bf16[128,2048]{1,0:T(8,128)(2,1)} %fusion.5) | copy-start | bytes 1572868

commit v10 on v9

--- a/solution.py
+++ b/solution.py
@@ -11,7 +11,7 @@
 
 adapter_scale = 2.0
 CORE, CHIP = 1, 2
-VMEM = 48 * 1024 * 1024
+VMEM = 16 * 1024 * 1024
 
 
 def dot(a, b, contract):
@@ -47,7 +47,7 @@
         ],
         out_specs=[pl.BlockSpec((rows // 2, block), lambda n: (0, n))] * 2,
         out_shape=[jax.ShapeDtypeStruct((rows // 2, stop - start), jnp.float32)] * 2,
-        compiler_params=pltpu.CompilerParams(vmem_limit_bytes=VMEM),
+        compiler_params=pltpu.CompilerParams(vmem_limit_bytes=2 * VMEM),
         cost_estimate=cost(2 * rows * (depth + span) * (stop - start), 2 * (depth + span + 2 * rows) * (stop - start)),
         name="project",
     )(tokens, wide, weight, up_flat)
@@ -69,7 +69,7 @@
             rhs[:rows] = a_ref[...]
             rhs[rows:] = b_ref[...]
 
-        total = dot(w_ref[...], rhs[...], (1, 1)).T
+        total = dot(w_ref[pl.ds(pl.multiple_of(n * block, block), block)], rhs[...], (1, 1)).T
         out_ref[...] = total
         sent_ref[...] = total.astype(first.dtype)
 
@@ -93,7 +93,7 @@
             in_specs=[
                 pl.BlockSpec(memory_space=pltpu.VMEM),
                 pl.BlockSpec(memory_space=pltpu.VMEM),
-                pl.BlockSpec((block, hidden), lambda n, facts_ref: (n, 0)),
+                pl.BlockSpec(memory_space=pltpu.VMEM),
                 *[pl.BlockSpec((1, rank, hidden), chosen_slot(place)) for place in places],
                 *[pl.BlockSpec(memory_space=pl.ANY)] * len(sent),
             ],
@@ -113,7 +113,7 @@
         compiler_params=pltpu.CompilerParams(vmem_limit_bytes=VMEM),
         cost_estimate=cost(4 * rows * hidden * depth, 2 * hidden * (depth + 2 * rows)),
         name="return_grad",
-    )(facts, first, second, weight, store, store, *sent)
+    )(facts, first, second, pltpu.with_memory_space_constraint(weight, pltpu.VMEM), store, store, *sent)
 
 
 def rank_inner(facts, flat, blocks, rank):
@@ -350,17 +350,13 @@
     odd_all = both(odd_mid, hops)
     cot_xc = swap(after(cot_x, odd_mid, even_all), CORE)
     down_x = swap(after(down_x, cot_x), CHIP)
-    grad23, parts, back23 = return_grad(facts, after(cot_x, odd_mid), cot_xc, weight, adapter_up, (2, 3), (parts,))
+    grad23, parts, back23 = return_grad(facts, after(cot_x, odd_mid, down_x), cot_xc, weight, adapter_up, (2, 3), (parts,))
     down_mine = both(rest[rank:] + near[:rank] + after(down_x, grad23), place)
     back = jnp.concatenate([back01, back23], axis=1)
     all_even = jnp.where(away == 0, even, jnp.where(away == 2, even_far, after(even_all, grad23)))
     all_odd = jnp.where(away == 0, odd, jnp.where(away == 2, odd_far, after(odd_all, all_even)))
     all_tokens = jnp.concatenate([all_even, all_odd], axis=0)
-    back = after(back, all_tokens) + along(back, 1)
-    back_wide, _, back_b = spread(facts, back, along(back, 2), per_owner, 1.0)
-    inner_wide, inner_rows, _ = spread(facts, after(inner, back_b), inner_far, per_owner, adapter_scale)
-    back_b = share(after(back_b, inner_wide, down_mine), swap(back_b, CORE), CORE)
-    parts = lax.all_to_all(after(parts, back_b).reshape(shards, rows, depth), "tp", 0, 0, tiled=True)
+    inner_wide, inner_rows, _ = spread(facts, after(inner, all_tokens), inner_far, per_owner, adapter_scale)
 
     def grad_block(q):
         low, high = [lax.dynamic_slice_in_dim(x, (q & 1) * rows, rows, 0) for x in (grad01, grad23)]
@@ -388,17 +384,21 @@
         done.append(own.astype(b16))
         return done[-1]
 
-    point = make(0, back_b)
-    back_b = share(after(back_b, point), swap(back_b, CHIP), CHIP)
-    point = make(1, point)
+    back = after(back, inner_rows) + along(back, 1)
+    point = make(0, back)
+    point = make(1, point, down_mine)
     point = cross(0, point)
-    point = make(2, point, back_b)
+    back_wide, _, back_b = spread(facts, after(back, point), along(back, 2), per_owner, 1.0)
+    parts = lax.all_to_all(after(parts, back_b).reshape(shards, rows, depth), "tp", 0, 0, tiled=True)
+    point = make(2, back_b)
     point = finish(0, point)
     point = cross(1, point)
-    point = make(3, point)
+    back_b = share(after(back_b, point), swap(back_b, CORE), CORE)
+    point = make(3, back_b)
     point = finish(1, point)
     point = cross(2, point)
-    down_wide = slot_grad(after(back_wide, point), [([x], n) for x, n in toks], width // 2)
+    back_b = share(after(back_b, point), swap(back_b, CHIP), CHIP)
+    down_wide = slot_grad(after(back_wide, back_b), [([x], n) for x, n in toks], width // 2)
     back_mine = lax.dynamic_slice_in_dim(back_b, j * rows, rows, 1)
     total = grad_block(j)
     for m in range(1, shards):

time: 238 us -> 264 us (1.11)
  local copies, waits for them, and re-layouts: 14.2 us -> 39.9 us
  waiting for transfers between devices: 59.5 us -> 73.7 us
  Pallas kernels: 92.1 us -> 79.9 us
  starting transfers between devices: 44.7 us -> 41.5 us
    unnamed x63 -> x97, local copies, waits for them, and re-layouts: 14.2 us -> 39.8 us
    ppermute x17, waiting for transfers between devices: 11.4 us -> 24.7 us  [swap(): return lax.ppermute(x, 'dp', [(d, d ^ bit) for d in range(groups)])]
    pallas_call x2, Pallas kernels: 39.3 us -> 29.2 us  [return_grad(): pl.pallas_call(kernel, grid_spec=pltpu.PrefetchScalarGridSpec(num_scalar_...]
    ppermute x4, waiting for transfers between devices: 20.8 us -> 13.9 us  [along(): return lax.ppermute(x, 'tp', [(z, z ^ bit) for z in range(shards)])]
    ppermute x6, waiting for transfers between devices: 23.6 us -> 27.9 us  [both(): return lax.ppermute(x, ('tp', 'dp'), pairs)]
    all_to_all x1, waiting for transfers between devices: 3.73 us -> 7.21 us  [local_square(): lax.all_to_all(after(parts, back_b).reshape(shards, rows, depth), 'tp', 0...]
  transfers between devices with their start and end apart: 28 -> 28, of which waited for: 9 -> 9; matrix products, arithmetic and copies ran while one was open for 11% -> 10% of each run, Pallas kernels for 35% -> 27%
where the time goes in v10:
time: 264 us; the launch traced here: 262 us
  Pallas kernels  79.9 us (30%)
  waiting for transfers between devices  73.7 us (28%)
  starting transfers between devices  41.5 us (16%)
  local copies, waits for them, and re-layouts  39.9 us (15%)
  other arithmetic  23.4 us (9%)
  matrix products  2.66 us (1%)
    unnamed x97, local copies, waits for them, and re-layouts  39.8 us
    pallas_call x4, Pallas kernels, project(): pl.pallas_call(kernel, grid=((stop - start) // block,), in_specs=[pl.Bloc...  31.7 us
    pallas_call x2, Pallas kernels, return_grad(): pl.pallas_call(kernel, grid_spec=pltpu.PrefetchScalarGridSpec(num_scalar_...  29.2 us
    ppermute x6, waiting for transfers between devices, both(): return lax.ppermute(x, ('tp', 'dp'), pairs)  27.9 us
    ppermute x17, waiting for transfers between devices, swap(): return lax.ppermute(x, 'dp', [(d, d ^ bit) for d in range(groups)])  24.7 us
    ppermute x17, starting transfers between devices, swap(): return lax.ppermute(x, 'dp', [(d, d ^ bit) for d in range(groups)])  18.5 us
    ppermute x6, starting transfers between devices, both(): return lax.ppermute(x, ('tp', 'dp'), pairs)  15.7 us
    ppermute x4, waiting for transfers between devices, along(): return lax.ppermute(x, 'tp', [(z, z ^ bit) for z in range(shards)])  13.9 us
  transfers between devices with their start and end apart: 28, of which 9 were waited for; matrix products, arithmetic and copies ran while one was open for 10% of the time, Pallas kernels for 27%

profile of v10, /device:TPU:2, one launch (start us, length us, event | category | flops | bytes accessed | tf_op | source)
XLA Modules:
  0.0 262.2 jit_solution(11382064170379395653)
XLA Ops:
  0.9 1.6 copy-done.9
  4.4 1.5 choose.1
  6.0 9.2 %collective-permute-done = bf16[128,2048]{1,0:T(8,128)(2,1)S(1)} collective-permute-done((bf16[128,2048]{1,0:T(8,128)(2,1)}, bf16[128,2048]{1,0:T(8,128)(2,1)S(1)}, u32[]{:S(2)}, u32[]{:S(2)}) %collective-permute-start) | collective-permute-done | bytes 524320 | tf_op jit(solution)/shard_map/ppermute | solution.py:311
  15.4 1.3 collective-permute-start.1
  16.7 0.9 collective-permute-start.4
  17.6 3.9 %collective-permute-start.7 = (bf16[128,7168]{1,0:T(8,128)(2,1)}, bf16[128,7168]{1,0:T(8,128)(2,1)}, u32[]{:S(2)}, u32[]{:S(2)}) collective-permute-start(bf16[128,7168]{1,0:T(8,128)(2,1)} %refs_0_.1), channel_id=1, source_target_pairs={{0,2},{1,3},{2,0},{3,1},{4,6},{5,7},{6,4},{7,5},{8,10},{9,11},{10,... | collective-permute-start | bytes 5505032 | tf_op jit(solution)/shard_map/ppermute | solution.py:311
  21.4 9.3 %copy-done = bf16[2048,7168]{1,0:T(8,128)(2,1)S(1)} copy-done((bf16[2048,7168]{1,0:T(8,128)(2,1)S(1)}, bf16[2048,7168]{1,0:T(8,128)(2,1)}, u32[]{:S(2)}) %copy-start) | copy-done | bytes 29360152
  30.8 1.5 copy-done.14
  32.3 14.3 %return_grad.2 = (f32[256,2048]{1,0:T(8,128)S(1)}, bf16[512,2048]{1,0:T(8,128)(2,1)S(1)}, f32[64,256]{1,0:T(8,128)S(1)}) custom-call(s32[9]{0:T(128)S(1)} %get-tuple-element.60.facts_ref, bf16[128,7168]{1,0:T(8,128)(2,1)S(1)} %copy-done.14, bf16[128,7168]{1,0:T(8,128)(2,1)} %collective-permute-done.3.b_ref.refs_1_, bf16[2048,7168]{1,0:T(8,128)(2,1)S(1)} %copy-done, ...), custom_call_target="tpu_custom_call" | custom-call | flops 117440512 | bytes 516096 | tf_op jit(solution)/shard_map/return_grad/pallas_call | solution.py:88
  46.7 1.3 collective-permute-start.8
  48.0 1.8 rank_inner.1
  49.8 1.3 collective-permute-start.5
  51.1 1.0 slice_add_fusion.9
  52.1 3.1 %collective-permute-done.5 = f32[64,512]{1,0:T(8,128)S(1)} collective-permute-done((f32[64,512]{1,0:T(8,128)S(1)}, f32[64,512]{1,0:T(8,128)S(1)}, u32[]{:S(2)}, u32[]{:S(2)}) %collective-permute-start.5) | collective-permute-done | bytes 131104 | tf_op jit(solution)/shard_map/ppermute | solution.py:314
  55.2 1.3 broadcast_select_fusion.1
  56.5 4.6 %collective-permute-start.6 = (bf16[256,2048]{1,0:T(8,128)(2,1)S(1)}, bf16[256,2048]{1,0:T(8,128)(2,1)}, u32[]{:S(2)}, u32[]{:S(2)}) collective-permute-start(bf16[256,2048]{1,0:T(8,128)(2,1)S(1)} %broadcast_select_fusion.1), channel_id=1, source_target_pairs={{0,4},{8,12},{5,1},{13,9},{10,14},{2,6},{15,11},{7,3},{16,20},{24,... | collective-permute-start | bytes 3145736 | tf_op jit(solution)/shard_map/ppermute | solution.py:324
  61.1 14.5 %collective-permute-done.8 = bf16[256,2048]{1,0:T(8,128)(2,1)S(1)} collective-permute-done((bf16[256,2048]{1,0:T(8,128)(2,1)S(1)}, bf16[256,2048]{1,0:T(8,128)(2,1)S(1)}, u32[]{:S(2)}, u32[]{:S(2)}) %collective-permute-start.8) | collective-permute-done | bytes 1048608 | tf_op jit(solution)/shard_map/ppermute | solution.py:324
  75.6 1.0 copy-done.36
  76.6 1.1 broadcast_select_fusion
  77.6 3.4 %collective-permute-start.10 = (bf16[128,7168]{1,0:T(8,128)(2,1)}, bf16[128,7168]{1,0:T(8,128)(2,1)}, u32[]{:S(2)}, u32[]{:S(2)}) collective-permute-start(bf16[128,7168]{1,0:T(8,128)(2,1)} %collective-permute-done.7.a_ref.refs_2_), channel_id=1, source_target_pairs={{0,1},{1,0},{2,3},{3,2},{4,5},{5,4},{6,7},{7,6},{8,9},{9,8},{10,11... | collective-permute-start | bytes 5505032 | tf_op jit(solution)/shard_map/ppermute | solution.py:311
  81.0 2.6 collective-permute-start.11
  83.6 5.5 %collective-permute-start.9 = (bf16[64,2048]{1,0:T(8,128)(2,1)S(1)}, bf16[64,2048]{1,0:T(8,128)(2,1)S(1)}, u32[]{:S(2)}, u32[]{:S(2)}) collective-permute-start(bf16[64,2048]{1,0:T(8,128)(2,1)S(1)} %slice_add_fusion.9), channel_id=1, source_target_pairs={{0,2},{1,3},{2,0},{3,1},{4,6},{5,7},{6,4},{7,5},{8,10},{9,11},{10,... | collective-permute-start | bytes 786440 | tf_op jit(solution)/shard_map/ppermute | solution.py:311
  89.6 3.8 %collective-permute-done.9 = bf16[64,2048]{1,0:T(8,128)(2,1)S(1)} collective-permute-done((bf16[64,2048]{1,0:T(8,128)(2,1)S(1)}, bf16[64,2048]{1,0:T(8,128)(2,1)S(1)}, u32[]{:S(2)}, u32[]{:S(2)}) %collective-permute-start.9) | collective-permute-done | bytes 262176 | tf_op jit(solution)/shard_map/ppermute | solution.py:311
  93.5 9.4 %copy-done.1 = bf16[2048,7168]{1,0:T(8,128)(2,1)S(1)} copy-done((bf16[2048,7168]{1,0:T(8,128)(2,1)S(1)}, bf16[2048,7168]{1,0:T(8,128)(2,1)}, u32[]{:S(2)}) %copy-start.1) | copy-done | bytes 29360152
  102.8 1.6 copy-done.12
  104.4 14.9 %return_grad.3 = (f32[256,2048]{1,0:T(8,128)S(1)}, bf16[512,2048]{1,0:T(8,128)(2,1)S(1)}, f32[64,256]{1,0:T(8,128)S(1)}) custom-call(s32[9]{0:T(128)S(1)} %get-tuple-element.60.facts_ref, bf16[128,7168]{1,0:T(8,128)(2,1)} %collective-permute-done.7.a_ref.refs_2_, ...), custom_call_target="tpu_custom_call", output_to_operand_aliasing={{1}: (6, {})} | custom-call | flops 117440512 | bytes 516096 | tf_op jit(solution)/shard_map/return_grad/pallas_call | solution.py:88
  119.3 1.4 copy-done.26
  120.7 2.2 select_select_fusion.1
  124.0 1.4 spread.2
  125.4 0.8 copy-done.27
  126.2 1.9 collective-permute-done.13
  128.2 8.1 %project.4 = (f32[256,2048]{1,0:T(8,128)S(1)}, f32[256,2048]{1,0:T(8,128)S(1)}) custom-call(bf16[512,2048]{1,0:T(8,128)(2,1)S(1)} %pad_maximum_fusion.tok_ref, bf16[512,512]{1,0:T(8,128)(2,1)S(1)} %get-tuple-element.82.wide_ref, bf16[2048,7168]{1,0:T(8,128)(2,1)} %w_ref.11, bf16[512,7168]{1,0:T(8,128)(2,1)S(1)} %bitcast.23), custom_call_target="tpu_custom_call" | custom-call | flops 83886080 | bytes 229376 | tf_op jit(solution)/shard_map/project/pallas_call | solution.py:39
  136.4 1.2 fusion.13
  137.6 3.9 %collective-permute-start.14 = (bf16[64,2048]{1,0:T(8,128)(2,1)S(1)}, bf16[64,2048]{1,0:T(8,128)(2,1)S(1)}, u32[]{:S(2)}, u32[]{:S(2)}) collective-permute-start(bf16[64,2048]{1,0:T(8,128)(2,1)S(1)} %fusion.13), channel_id=1, source_target_pairs={{0,0},{4,5},{8,10},{12,15},{1,4},{5,1},{9,14},{13,11},{2,8},{6,13}... | collective-permute-start | bytes 786440 | tf_op jit(solution)/shard_map/ppermute | solution.py:324
  141.5 13.4 %collective-permute-done.14 = bf16[64,2048]{1,0:T(8,128)(2,1)S(1)} collective-permute-done((bf16[64,2048]{1,0:T(8,128)(2,1)S(1)}, bf16[64,2048]{1,0:T(8,128)(2,1)S(1)}, u32[]{:S(2)}, u32[]{:S(2)}) %collective-permute-start.14) | collective-permute-done | bytes 262176 | tf_op jit(solution)/shard_map/ppermute | solution.py:324
  155.6 7.3 %project.5 = (f32[256,1536]{1,0:T(8,128)S(1)}, f32[256,1536]{1,0:T(8,128)}) custom-call(bf16[512,2048]{1,0:T(8,128)(2,1)S(1)} %pad_maximum_fusion.tok_ref, bf16[512,512]{1,0:T(8,128)(2,1)S(1)} %get-tuple-element.82.wide_ref, bf16[2048,7168]{1,0:T(8,128)(2,1)} %w_ref.11, bf16[512,7168]{1,0:T(8,128)(2,1)S(1)} %bitcast.24), custom_call_target="tpu_custom_call" | custom-call | flops 62914560 | bytes 172032 | tf_op jit(solution)/shard_map/project/pallas_call | solution.py:39
  162.9 1.1 fusion.6
  164.5 9.0 %collective-permute-done.16.refs_1_ = f32[64,512]{1,0:T(8,128)S(1)} collective-permute-done((f32[64,512]{1,0:T(8,128)S(1)}, f32[64,512]{1,0:T(8,128)S(1)}, u32[]{:S(2)}, u32[]{:S(2)}) %collective-permute-start.16) | collective-permute-done | bytes 131104 | tf_op jit(solution)/shard_map/ppermute | solution.py:314
  173.5 1.7 spread.3
  175.1 0.8 copy-done.29
  176.0 4.6 %all-to-all-start = ((bf16[4,128,2048]{2,1,0:T(8,128)(2,1)}), bf16[4,128,2048]{2,1,0:T(8,128)(2,1)}, u32[]{:S(2)}, u32[]{:S(2)}) async-start(bf16[4,128,2048]{2,1,0:T(8,128)(2,1)} %bitcast.29), calls=%async_computation | async-start | bytes 4194304 | tf_op jit(solution)/shard_map/all_to_all | solution.py:392
  180.6 3.1 %copy-done.2 = bf16[8,64,7168]{2,1,0:T(8,128)(2,1)S(1)} copy-done((bf16[8,64,7168]{2,1,0:T(8,128)(2,1)S(1)}, bf16[8,64,7168]{2,1,0:T(8,128)(2,1)}, u32[]{:S(2)}) %copy-start.2) | copy-done | bytes 7340056
  183.7 1.0 copy-done.7
  184.7 9.0 %project.6 = (f32[256,2048]{1,0:T(8,128)S(1)}, f32[256,2048]{1,0:T(8,128)}) custom-call(bf16[512,2048]{1,0:T(8,128)(2,1)S(1)} %pad_maximum_fusion.tok_ref, bf16[512,512]{1,0:T(8,128)(2,1)S(1)} %copy-done.7, bf16[2048,7168]{1,0:T(8,128)(2,1)} %w_ref.11, bf16[512,7168]{1,0:T(8,128)(2,1)S(1)} %bitcast.25), custom_call_target="tpu_custom_call" | custom-call | flops 83886080 | bytes 229376 | tf_op jit(solution)/shard_map/project/pallas_call | solution.py:39
  194.3 2.7 %fusion.5 = bf16[128,2048]{1,0:T(8,128)(2,1)} fusion(f32[256,2048]{1,0:T(8,128)S(1)} %copy-done.39, bf16[128,2048]{1,0:T(8,128)(2,1)} %collective-permute-done.17, f32[256,2048]{1,0:T(8,128)S(1)} %copy-done.19), kind=kLoop, calls=%fused_computation.11 | loop fusion | flops 1048576 | bytes 3145728 | tf_op jit(solution)/shard_map/convert_element_type | solution.py:384
  197.0 2.0 fusion.12
  199.0 1.5 collective-permute-start.20
  201.1 3.1 %copy-done.3 = bf16[8,64,7168]{2,1,0:T(8,128)(2,1)S(1)} copy-done((bf16[8,64,7168]{2,1,0:T(8,128)(2,1)S(1)}, bf16[8,64,7168]{2,1,0:T(8,128)(2,1)}, u32[]{:S(2)}) %copy-start.3) | copy-done | bytes 7340056
  204.2 1.0 copy-done.8
  205.3 7.4 %project.7 = (f32[256,1536]{1,0:T(8,128)S(1)}, f32[256,1536]{1,0:T(8,128)}) custom-call(bf16[512,2048]{1,0:T(8,128)(2,1)S(1)} %pad_maximum_fusion.tok_ref, bf16[512,512]{1,0:T(8,128)(2,1)S(1)} %copy-done.8, bf16[2048,7168]{1,0:T(8,128)(2,1)} %w_ref.11, bf16[512,7168]{1,0:T(8,128)(2,1)S(1)} %bitcast.26), custom_call_target="tpu_custom_call" | custom-call | flops 62914560 | bytes 172032 | tf_op jit(solution)/shard_map/project/pallas_call | solution.py:39
  212.8 2.0 fusion.11
  215.2 2.1 fusion.3
  217.3 1.5 collective-permute-start.24
  219.4 2.9 %slot_grad.2 = f32[512,2048]{1,0:T(8,128)} custom-call(bf16[512,512]{1,0:T(8,128)(2,1)S(1)} %copy-done.30, bf16[256,2048]{1,0:T(8,128)(2,1)S(1)} %constant_dynamic-update-slice_fusion.refs_0_.refs_2_, bf16[256,2048]{1,0:T(8,128)(2,1)S(1)} %copy-done.5, bf16[256,2048]{1,0:T(8,128)(2,1)S(1)} %constant_dynamic-update-slice_fusion.refs_0_.refs_2_, ...), custom_call_target="tpu_custom_call" | custom-call | flops 1073741824 | bytes 6291456 | tf_op jit(solution)/shard_map/slot_grad/pallas_call | solution.py:212
  222.4 7.2 %all-to-all-done = bf16[4,128,2048]{2,1,0:T(8,128)(2,1)} async-done(((bf16[4,128,2048]{2,1,0:T(8,128)(2,1)}), bf16[4,128,2048]{2,1,0:T(8,128)(2,1)}, u32[]{:S(2)}, u32[]{:S(2)}) %all-to-all-start) | async-done | bytes 2097184 | tf_op jit(solution)/shard_map/all_to_all | solution.py:392
  229.6 2.7 %fusion = bf16[128,2048]{1,0:T(8,128)(2,1)S(1)} fusion(bf16[64,2048]{1,0:T(8,128)(2,1)} %copy-done.42, f32[256,2048]{1,0:T(8,128)} %copy-done.26, s32[]{:T(128)S(6)} %select_n.64, f32[256,2048]{1,0:T(8,128)} %copy-done.25, bf16[4,128,2048]{2,1,0:T(8,128)(2,1)} %all-to-all-done, s32[]{:T(128)S(6)} %select_n.68, s32[]{:T(128)S(6)} %select_n.67, ...), kind=kOutput, calls=%fused_computation.1 | convolution fusion | flops 35913728 | bytes 4472853 | tf_op jit(solution)/shard_map/dot_general | solution.py:18
  232.3 2.1 collective-permute-start.26
  234.3 1.3 fusion.9
  235.9 9.7 %slot_grad.3 = f32[512,7168]{1,0:T(8,128)} custom-call(bf16[512,512]{1,0:T(8,128)(2,1)S(1)} %copy-done.28, bf16[128,7168]{1,0:T(8,128)(2,1)S(1)} %copy-done.15, bf16[128,7168]{1,0:T(8,128)(2,1)} %collective-permute-done.3.b_ref.refs_1_, bf16[128,7168]{1,0:T(8,128)(2,1)} %collective-permute-done.7.a_ref.refs_2_, ...), custom_call_target="tpu_custom_call" | custom-call | flops 3758096384 | bytes 22020096 | tf_op jit(solution)/shard_map/slot_grad/pallas_call | solution.py:212
  245.6 1.6 fusion.2
  247.2 11.6 %collective-permute-done.25 = bf16[128,1536]{1,0:T(8,128)(2,1)S(1)} collective-permute-done((bf16[128,1536]{1,0:T(8,128)(2,1)S(1)}, bf16[128,1536]{1,0:T(8,128)(2,1)S(1)}, u32[]{:S(2)}, u32[]{:S(2)}) %collective-permute-start.25) | collective-permute-done | bytes 393248 | tf_op jit(solution)/shard_map/ppermute | solution.py:311
  258.7 1.3 fusion.8
  260.0 1.4 pad_maximum_fusion.1
  261.4 0.8 copy.17
  (128 shorter events, 8.0 us)
Async XLA Ops:
  0.6 20.8 %collective-permute-start.3 = (bf16[128,7168]{1,0:T(8,128)(2,1)}, bf16[128,7168]{1,0:T(8,128)(2,1)}, u32[]{:S(2)}, u32[]{:S(2)}) collective-permute-start(bf16[128,7168]{1,0:T(8,128)(2,1)} %refs_0_.1), channel_id=1, source_target_pairs={{0,1},{1,0},{2,3},{3,2},{4,5},{5,4},{6,7},{7,6},{8,9},{9,8},{10,11... | collective-permute-start | bytes 5505032 | tf_op jit(solution)/shard_map/ppermute | solution.py:311
  0.7 14.5 %collective-permute-start = (bf16[128,2048]{1,0:T(8,128)(2,1)}, bf16[128,2048]{1,0:T(8,128)(2,1)S(1)}, u32[]{:S(2)}, u32[]{:S(2)}) collective-permute-start(bf16[128,2048]{1,0:T(8,128)(2,1)} %param.8), channel_id=1, source_target_pairs={{0,2},{1,3},{2,0},{3,1},{4,6},{5,7},{6,4},{7,5},{8,10},{9,11},{10,... | collective-permute-start | bytes 1572872 | tf_op jit(solution)/shard_map/ppermute | solution.py:311
  0.9 1.6 copy-start.9
  4.4 1.5 copy-start.41
  6.0 45.2 %copy-start.31 = (bf16[128,2048]{1,0:T(8,128)(2,1)}, bf16[128,2048]{1,0:T(8,128)(2,1)S(1)}, u32[]{:S(2)}) copy-start(bf16[128,2048]{1,0:T(8,128)(2,1)S(1)} %get-tuple-element.65) | copy-start | bytes 1572868
  15.3 31.4 %collective-permute-start.2 = (bf16[256,2048]{1,0:T(8,128)(2,1)S(1)}, bf16[256,2048]{1,0:T(8,128)(2,1)S(1)}, u32[]{:S(2)}, u32[]{:S(2)}) collective-permute-start(bf16[256,2048]{1,0:T(8,128)(2,1)S(1)} %constant_dynamic-update-slice_fusion.refs_0_.refs_2_), channel_id=1, source_target_pairs={{0,1},{1,0},{2,3},{3,2},{4,5},{5,4},{6,7},{7,6},{8,9},{9,8},{10,11... | collective-permute-start | bytes 3145736 | tf_op jit(solution)/shard_map/ppermute | solution.py:311
  15.4 39.8 %collective-permute-start.1 = (bf16[256,2048]{1,0:T(8,128)(2,1)S(1)}, bf16[256,2048]{1,0:T(8,128)(2,1)}, u32[]{:S(2)}, u32[]{:S(2)}) collective-permute-start(bf16[256,2048]{1,0:T(8,128)(2,1)S(1)} %constant_dynamic-update-slice_fusion.refs_0_.refs_2_), channel_id=1, source_target_pairs={{0,8},{5,13},{10,2},{15,7},{16,24},{21,29},{26,18},{31,23}} | collective-permute-start | bytes 3145736 | tf_op jit(solution)/shard_map/ppermute | solution.py:324
  16.7 34.4 %collective-permute-start.4 = (bf16[128,2048]{1,0:T(8,128)(2,1)S(1)}, bf16[128,2048]{1,0:T(8,128)(2,1)}, u32[]{:S(2)}, u32[]{:S(2)}) collective-permute-start(bf16[128,2048]{1,0:T(8,128)(2,1)S(1)} %get-tuple-element.67), channel_id=1, source_target_pairs={{0,1},{1,0},{2,3},{3,2},{4,5},{5,4},{6,7},{7,6},{8,9},{9,8},{10,11... | collective-permute-start | bytes 1572872 | tf_op jit(solution)/shard_map/ppermute | solution.py:311
  17.6 60.1 %collective-permute-start.7 = (bf16[128,7168]{1,0:T(8,128)(2,1)}, bf16[128,7168]{1,0:T(8,128)(2,1)}, u32[]{:S(2)}, u32[]{:S(2)}) collective-permute-start(bf16[128,7168]{1,0:T(8,128)(2,1)} %refs_0_.1), channel_id=1, source_target_pairs={{0,2},{1,3},{2,0},{3,1},{4,6},{5,7},{6,4},{7,5},{8,10},{9,11},{10,... | collective-permute-start | bytes 5505032 | tf_op jit(solution)/shard_map/ppermute | solution.py:311
  21.4 9.4 %copy-start = (bf16[2048,7168]{1,0:T(8,128)(2,1)S(1)}, bf16[2048,7168]{1,0:T(8,128)(2,1)}, u32[]{:S(2)}) copy-start(bf16[2048,7168]{1,0:T(8,128)(2,1)} %w_ref.11) | copy-start | bytes 88080384
  30.8 1.5 copy-start.14
  32.3 15.7 %copy-start.10 = (bf16[8,2048,64]{1,2,0:T(8,128)(2,1)S(1)}, bf16[8,2048,64]{1,2,0:T(8,128)(2,1)}, u32[]{:S(2)}) copy-start(bf16[8,2048,64]{1,2,0:T(8,128)(2,1)} %param.10) | copy-start | bytes 6291460
  46.6 3.2 %copy-start.11 = (bf16[512,2048]{1,0:T(8,128)(2,1)}, bf16[512,2048]{1,0:T(8,128)(2,1)S(1)}, u32[]{:S(2)}) copy-start(bf16[512,2048]{1,0:T(8,128)(2,1)S(1)} %get-tuple-element.75.refs_0_) | copy-start | bytes 6291460
  46.6 3.2 %copy-start.25 = (f32[256,2048]{1,0:T(8,128)}, f32[256,2048]{1,0:T(8,128)S(1)}, u32[]{:S(2)}) copy-start(f32[256,2048]{1,0:T(8,128)S(1)} %get-tuple-element.63) | copy-start | bytes 6291460
  46.7 76.9 %copy-start.4 = (bf16[256,2048]{1,0:T(8,128)(2,1)}, bf16[256,2048]{1,0:T(8,128)(2,1)S(1)}, u32[]{:S(2)}) copy-start(bf16[256,2048]{1,0:T(8,128)(2,1)S(1)} %collective-permute-done.2.refs_1_.refs_3_) | copy-start | bytes 3145732
  46.7 28.9 %collective-permute-start.8 = (bf16[256,2048]{1,0:T(8,128)(2,1)S(1)}, bf16[256,2048]{1,0:T(8,128)(2,1)S(1)}, u32[]{:S(2)}, u32[]{:S(2)}) collective-permute-start(bf16[256,2048]{1,0:T(8,128)(2,1)S(1)} %collective-permute-done.2.refs_1_.refs_3_), channel_id=1, source_target_pairs={{0,8},{5,13},{10,2},{15,7},{16,24},{21,29},{26,18},{31,23}} | collective-permute-start | bytes 3145736 | tf_op jit(solution)/shard_map/ppermute | solution.py:324
  49.8 5.3 %collective-permute-start.5 = (f32[64,512]{1,0:T(8,128)S(1)}, f32[64,512]{1,0:T(8,128)S(1)}, u32[]{:S(2)}, u32[]{:S(2)}) collective-permute-start(f32[64,512]{1,0:T(8,128)S(1)} %rank_inner.1), channel_id=1, source_target_pairs={{0,4},{4,0},{8,12},{12,8},{1,5},{5,1},{9,13},{13,9},{2,6},{6,2},{1... | collective-permute-start | bytes 393224 | tf_op jit(solution)/shard_map/ppermute | solution.py:314
  56.5 21.1 %collective-permute-start.6 = (bf16[256,2048]{1,0:T(8,128)(2,1)S(1)}, bf16[256,2048]{1,0:T(8,128)(2,1)}, u32[]{:S(2)}, u32[]{:S(2)}) collective-permute-start(bf16[256,2048]{1,0:T(8,128)(2,1)S(1)} %broadcast_select_fusion.1), channel_id=1, source_target_pairs={{0,4},{8,12},{5,1},{13,9},{10,14},{2,6},{15,11},{7,3},{16,20},{24,... | collective-permute-start | bytes 3145736 | tf_op jit(solution)/shard_map/ppermute | solution.py:324
  77.6 15.8 %collective-permute-start.10 = (bf16[128,7168]{1,0:T(8,128)(2,1)}, bf16[128,7168]{1,0:T(8,128)(2,1)}, u32[]{:S(2)}, u32[]{:S(2)}) collective-permute-start(bf16[128,7168]{1,0:T(8,128)(2,1)} %collective-permute-done.7.a_ref.refs_2_), channel_id=1, source_target_pairs={{0,1},{1,0},{2,3},{3,2},{4,5},{5,4},{6,7},{7,6},{8,9},{9,8},{10,11... | collective-permute-start | bytes 5505032 | tf_op jit(solution)/shard_map/ppermute | solution.py:311
  81.0 41.9 %collective-permute-start.11 = (bf16[256,2048]{1,0:T(8,128)(2,1)}, bf16[256,2048]{1,0:T(8,128)(2,1)}, u32[]{:S(2)}, u32[]{:S(2)}) collective-permute-start(bf16[256,2048]{1,0:T(8,128)(2,1)} %broadcast_select_fusion), channel_id=1, source_target_pairs={{0,4},{8,12},{5,1},{13,9},{10,14},{2,6},{15,11},{7,3},{16,20},{24,... | collective-permute-start | bytes 3145736 | tf_op jit(solution)/shard_map/ppermute | solution.py:324
  83.6 9.9 %collective-permute-start.9 = (bf16[64,2048]{1,0:T(8,128)(2,1)S(1)}, bf16[64,2048]{1,0:T(8,128)(2,1)S(1)}, u32[]{:S(2)}, u32[]{:S(2)}) collective-permute-start(bf16[64,2048]{1,0:T(8,128)(2,1)S(1)} %slice_add_fusion.9), channel_id=1, source_target_pairs={{0,2},{1,3},{2,0},{3,1},{4,6},{5,7},{6,4},{7,5},{8,10},{9,11},{10,... | collective-permute-start | bytes 786440 | tf_op jit(solution)/shard_map/ppermute | solution.py:311
  89.1 34.9 %collective-permute-start.12 = (f32[64,512]{1,0:T(8,128)S(1)}, f32[64,512]{1,0:T(8,128)S(1)}, u32[]{:S(2)}, u32[]{:S(2)}) collective-permute-start(f32[64,512]{1,0:T(8,128)S(1)} %add.87.refs_0_), channel_id=1, source_target_pairs={{0,8},{4,12},{8,0},{12,4},{1,9},{5,13},{9,1},{13,5},{2,10},{6,14},... | collective-permute-start | bytes 393224 | tf_op jit(solution)/shard_map/ppermute | solution.py:314
  93.5 9.4 %copy-start.1 = (bf16[2048,7168]{1,0:T(8,128)(2,1)S(1)}, bf16[2048,7168]{1,0:T(8,128)(2,1)}, u32[]{:S(2)}) copy-start(bf16[2048,7168]{1,0:T(8,128)(2,1)} %w_ref.11) | copy-start | bytes 88080384
  102.8 1.6 copy-start.12
  104.4 19.2 %copy-start.37 = (bf16[256,2048]{1,0:T(8,128)(2,1)S(1)}, bf16[256,2048]{1,0:T(8,128)(2,1)}, u32[]{:S(2)}) copy-start(bf16[256,2048]{1,0:T(8,128)(2,1)} %copy-done.36) | copy-start | bytes 3145732
  120.7 2.2 copy-start.13
  120.7 7.5 %slice-start = ((s8[7340032]{0:T(1024)(128)(4,1)}), s8[4194304]{0:T(1024)(128)(4,1)S(1)}, s32[]{:S(2)}) async-start(s8[7340032]{0:T(1024)(128)(4,1)} %bitcast.21), calls=%async_computation.1 | async-start | bytes 8388608
  122.9 5.3 %slice-start.1 = ((s8[7340032]{0:T(1024)(128)(4,1)}), s8[3145728]{0:T(1024)(128)(4,1)S(1)}, s32[]{:S(2)}) async-start(s8[7340032]{0:T(1024)(128)(4,1)} %bitcast.21), calls=%async_computation.2 | async-start | bytes 6291456
  122.9 5.2 %collective-permute-start.13 = (f32[64,512]{1,0:T(8,128)S(1)}, f32[64,512]{1,0:T(8,128)S(1)}, u32[]{:S(2)}, u32[]{:S(2)}) collective-permute-start(f32[64,512]{1,0:T(8,128)S(1)} %constant_dynamic-update-slice_fusion.2), channel_id=1, source_target_pairs={{0,4},{4,0},{8,12},{12,8},{1,5},{5,1},{9,13},{13,9},{2,6},{6,2},{1... | collective-permute-start | bytes 393224 | tf_op jit(solution)/shard_map/ppermute | solution.py:314
  126.2 29.4 %copy-start.6 = (bf16[512,512]{1,0:T(8,128)(2,1)}, bf16[512,512]{1,0:T(8,128)(2,1)S(1)}, u32[]{:S(2)}) copy-start(bf16[512,512]{1,0:T(8,128)(2,1)S(1)} %get-tuple-element.82.wide_ref) | copy-start | bytes 1572868
  128.2 8.2 %copy-start.32 = (bf16[128,2048]{1,0:T(8,128)(2,1)S(1)}, bf16[128,2048]{1,0:T(8,128)(2,1)}, u32[]{:S(2)}) copy-start(bf16[128,2048]{1,0:T(8,128)(2,1)} %copy-done.31) | copy-start | bytes 1572868
  136.3 26.6 %copy-start.18 = (f32[256,2048]{1,0:T(8,128)}, f32[256,2048]{1,0:T(8,128)S(1)}, u32[]{:S(2)}) copy-start(f32[256,2048]{1,0:T(8,128)S(1)} %get-tuple-element.95) | copy-start | bytes 6291460
  136.3 26.6 %collective-permute-start.15 = (f32[256,2048]{1,0:T(8,128)S(1)}, f32[256,2048]{1,0:T(8,128)S(1)}, u32[]{:S(2)}, u32[]{:S(2)}) collective-permute-start(f32[256,2048]{1,0:T(8,128)S(1)} %get-tuple-element.90), channel_id=1, source_target_pairs={{0,1},{1,0},{2,3},{3,2},{4,5},{5,4},{6,7},{7,6},{8,9},{9,8},{10,11... | collective-permute-start | bytes 6291464 | tf_op jit(solution)/shard_map/ppermute | solution.py:311
  137.6 17.3 %collective-permute-start.14 = (bf16[64,2048]{1,0:T(8,128)(2,1)S(1)}, bf16[64,2048]{1,0:T(8,128)(2,1)S(1)}, u32[]{:S(2)}, u32[]{:S(2)}) collective-permute-start(bf16[64,2048]{1,0:T(8,128)(2,1)S(1)} %fusion.13), channel_id=1, source_target_pairs={{0,0},{4,5},{8,10},{12,15},{1,4},{5,1},{9,14},{13,11},{2,8},{6,13}... | collective-permute-start | bytes 786440 | tf_op jit(solution)/shard_map/ppermute | solution.py:324
  162.9 34.1 %collective-permute-start.18 = (f32[256,1536]{1,0:T(8,128)}, f32[256,1536]{1,0:T(8,128)}, u32[]{:S(2)}, u32[]{:S(2)}) collective-permute-start(f32[256,1536]{1,0:T(8,128)} %get-tuple-element.97), channel_id=1, source_target_pairs={{0,1},{1,0},{2,3},{3,2},{4,5},{5,4},{6,7},{7,6},{8,9},{9,8},{10,11... | collective-permute-start | bytes 4718600 | tf_op jit(solution)/shard_map/ppermute | solution.py:311
  162.9 12.2 %copy-start.38 = (f32[256,2048]{1,0:T(8,128)}, f32[256,2048]{1,0:T(8,128)S(1)}, u32[]{:S(2)}) copy-start(f32[256,2048]{1,0:T(8,128)S(1)} %collective-permute-done.15) | copy-start | bytes 6291460
  164.2 30.1 %collective-permute-start.17 = (bf16[128,2048]{1,0:T(8,128)(2,1)}, bf16[128,2048]{1,0:T(8,128)(2,1)}, u32[]{:S(2)}, u32[]{:S(2)}) collective-permute-start(bf16[128,2048]{1,0:T(8,128)(2,1)} %fusion.6), channel_id=1, source_target_pairs={{0,2},{1,3},{2,0},{3,1},{4,6},{5,7},{6,4},{7,5},{8,10},{9,11},{10,... | collective-permute-start | bytes 1572872 | tf_op jit(solution)/shard_map/ppermute | solution.py:311
  164.2 9.2 %collective-permute-start.16 = (f32[64,512]{1,0:T(8,128)S(1)}, f32[64,512]{1,0:T(8,128)S(1)}, u32[]{:S(2)}, u32[]{:S(2)}) collective-permute-start(f32[64,512]{1,0:T(8,128)S(1)} %add.88.refs_0_), channel_id=1, source_target_pairs={{0,8},{4,12},{8,0},{12,4},{1,9},{5,13},{9,1},{13,5},{2,10},{6,14},... | collective-permute-start | bytes 393224 | tf_op jit(solution)/shard_map/ppermute | solution.py:314
  175.9 18.3 %collective-permute-start.19 = (bf16[64,512]{1,0:T(8,128)(2,1)S(1)}, bf16[64,512]{1,0:T(8,128)(2,1)S(1)}, u32[]{:S(2)}, u32[]{:S(2)}) collective-permute-start(bf16[64,512]{1,0:T(8,128)(2,1)S(1)} %get-tuple-element.98), channel_id=1, source_target_pairs={{0,1},{1,0},{2,3},{3,2},{4,5},{5,4},{6,7},{7,6},{8,9},{9,8},{10,11... | collective-permute-start | bytes 196616 | tf_op jit(solution)/shard_map/ppermute | solution.py:311
  176.0 53.6 %all-to-all-start = ((bf16[4,128,2048]{2,1,0:T(8,128)(2,1)}), bf16[4,128,2048]{2,1,0:T(8,128)(2,1)}, u32[]{:S(2)}, u32[]{:S(2)}) async-start(bf16[4,128,2048]{2,1,0:T(8,128)(2,1)} %bitcast.29), calls=%async_computation | async-start | bytes 4194304 | tf_op jit(solution)/shard_map/all_to_all | solution.py:392
  180.6 3.1 %copy-start.2 = (bf16[8,64,7168]{2,1,0:T(8,128)(2,1)S(1)}, bf16[8,64,7168]{2,1,0:T(8,128)(2,1)}, u32[]{:S(2)}) copy-start(bf16[8,64,7168]{2,1,0:T(8,128)(2,1)} %up_b_ref.3) | copy-start | bytes 22020100
  184.7 9.6 %copy-start.19 = (f32[256,2048]{1,0:T(8,128)S(1)}, f32[256,2048]{1,0:T(8,128)}, u32[]{:S(2)}) copy-start(f32[256,2048]{1,0:T(8,128)} %copy-done.18) | copy-start | bytes 6291460
  184.7 9.6 %copy-start.39 = (f32[256,2048]{1,0:T(8,128)S(1)}, f32[256,2048]{1,0:T(8,128)}, u32[]{:S(2)}) copy-start(f32[256,2048]{1,0:T(8,128)} %copy-done.38) | copy-start | bytes 6291460
  193.8 5.2 %copy-start.16 = (f32[256,2048]{1,0:T(8,128)}, f32[256,2048]{1,0:T(8,128)S(1)}, u32[]{:S(2)}) copy-start(f32[256,2048]{1,0:T(8,128)S(1)} %get-tuple-element.114) | copy-start | bytes 6291460
  193.8 3.2 %copy-start.21 = (f32[256,1536]{1,0:T(8,128)S(1)}, f32[256,1536]{1,0:T(8,128)}, u32[]{:S(2)}) copy-start(f32[256,1536]{1,0:T(8,128)} %copy-done.20) | copy-start | bytes 4718596
  193.8 21.0 %collective-permute-start.21 = (f32[256,2048]{1,0:T(8,128)}, f32[256,2048]{1,0:T(8,128)}, u32[]{:S(2)}, u32[]{:S(2)}) collective-permute-start(f32[256,2048]{1,0:T(8,128)} %get-tuple-element.107), channel_id=1, source_target_pairs={{0,1},{1,0},{2,3},{3,2},{4,5},{5,4},{6,7},{7,6},{8,9},{9,8},{10,11... | collective-permute-start | bytes 6291464 | tf_op jit(solution)/shard_map/ppermute | solution.py:311
  199.0 13.8 %collective-permute-start.20 = (bf16[128,1536]{1,0:T(8,128)(2,1)}, bf16[128,1536]{1,0:T(8,128)(2,1)}, u32[]{:S(2)}, u32[]{:S(2)}) collective-permute-start(bf16[128,1536]{1,0:T(8,128)(2,1)} %fusion.12), channel_id=1, source_target_pairs={{0,2},{1,3},{2,0},{3,1},{4,6},{5,7},{6,4},{7,5},{8,10},{9,11},{10,... | collective-permute-start | bytes 1179656 | tf_op jit(solution)/shard_map/ppermute | solution.py:311
  200.5 12.1 %copy-start.43 = (bf16[64,512]{1,0:T(8,128)(2,1)}, bf16[64,512]{1,0:T(8,128)(2,1)S(1)}, u32[]{:S(2)}) copy-start(bf16[64,512]{1,0:T(8,128)(2,1)S(1)} %maximum_add_fusion) | copy-start | bytes 196612
  200.5 12.2 %collective-permute-start.22 = (bf16[64,512]{1,0:T(8,128)(2,1)S(1)}, bf16[64,512]{1,0:T(8,128)(2,1)S(1)}, u32[]{:S(2)}, u32[]{:S(2)}) collective-permute-start(bf16[64,512]{1,0:T(8,128)(2,1)S(1)} %maximum_add_fusion), channel_id=1, source_target_pairs={{0,2},{1,3},{2,0},{3,1},{4,6},{5,7},{6,4},{7,5},{8,10},{9,11},{10,... | collective-permute-start | bytes 196616 | tf_op jit(solution)/shard_map/ppermute | solution.py:311
  201.1 3.1 %copy-start.3 = (bf16[8,64,7168]{2,1,0:T(8,128)(2,1)S(1)}, bf16[8,64,7168]{2,1,0:T(8,128)(2,1)}, u32[]{:S(2)}) copy-start(bf16[8,64,7168]{2,1,0:T(8,128)(2,1)} %up_b_ref.3) | copy-start | bytes 22020100
  205.3 7.5 %copy-start.22 = (f32[256,1536]{1,0:T(8,128)S(1)}, f32[256,1536]{1,0:T(8,128)}, u32[]{:S(2)}) copy-start(f32[256,1536]{1,0:T(8,128)} %copy-done.20) | copy-start | bytes 4718596
  212.6 4.6 %copy-start.23 = (f32[256,1536]{1,0:T(8,128)}, f32[256,1536]{1,0:T(8,128)S(1)}, u32[]{:S(2)}) copy-start(f32[256,1536]{1,0:T(8,128)S(1)} %get-tuple-element.115) | copy-start | bytes 4718596
  212.6 2.5 copy-start.17
  212.6 21.7 %collective-permute-start.23 = (f32[256,1536]{1,0:T(8,128)}, f32[256,1536]{1,0:T(8,128)}, u32[]{:S(2)}, u32[]{:S(2)}) collective-permute-start(f32[256,1536]{1,0:T(8,128)} %get-tuple-element.112), channel_id=1, source_target_pairs={{0,1},{1,0},{2,3},{3,2},{4,5},{5,4},{6,7},{7,6},{8,9},{9,8},{10,11... | collective-permute-start | bytes 4718600 | tf_op jit(solution)/shard_map/ppermute | solution.py:311
  212.8 6.0 %copy-start.44 = (bf16[64,512]{1,0:T(8,128)(2,1)S(1)}, bf16[64,512]{1,0:T(8,128)(2,1)}, u32[]{:S(2)}) copy-start(bf16[64,512]{1,0:T(8,128)(2,1)} %copy-done.43) | copy-start | bytes 196612
  212.8 6.7 %copy-start.5 = (bf16[256,2048]{1,0:T(8,128)(2,1)S(1)}, bf16[256,2048]{1,0:T(8,128)(2,1)}, u32[]{:S(2)}) copy-start(bf16[256,2048]{1,0:T(8,128)(2,1)} %copy-done.4) | copy-start | bytes 3145732
  212.8 6.7 %copy-start.30 = (bf16[512,512]{1,0:T(8,128)(2,1)S(1)}, bf16[512,512]{1,0:T(8,128)(2,1)}, u32[]{:S(2)}) copy-start(bf16[512,512]{1,0:T(8,128)(2,1)} %copy-done.29) | copy-start | bytes 1572868
  217.3 28.3 %collective-permute-start.24 = (bf16[128,2048]{1,0:T(8,128)(2,1)}, bf16[128,2048]{1,0:T(8,128)(2,1)}, u32[]{:S(2)}, u32[]{:S(2)}) collective-permute-start(bf16[128,2048]{1,0:T(8,128)(2,1)} %fusion.3), channel_id=1, source_target_pairs={{0,2},{1,3},{2,0},{3,1},{4,6},{5,7},{6,4},{7,5},{8,10},{9,11},{10,... | collective-permute-start | bytes 1572872 | tf_op jit(solution)/shard_map/ppermute | solution.py:311
  229.6 4.8 %copy-start.24 = (f32[256,1536]{1,0:T(8,128)S(1)}, f32[256,1536]{1,0:T(8,128)}, u32[]{:S(2)}) copy-start(f32[256,1536]{1,0:T(8,128)} %copy-done.23) | copy-start | bytes 4718596
  229.6 6.4 %copy-start.28 = (bf16[512,512]{1,0:T(8,128)(2,1)S(1)}, bf16[512,512]{1,0:T(8,128)(2,1)}, u32[]{:S(2)}) copy-start(bf16[512,512]{1,0:T(8,128)(2,1)} %copy-done.27) | copy-start | bytes 1572868
  232.3 3.7 %copy-start.15 = (bf16[128,7168]{1,0:T(8,128)(2,1)S(1)}, bf16[128,7168]{1,0:T(8,128)(2,1)}, u32[]{:S(2)}) copy-start(bf16[128,7168]{1,0:T(8,128)(2,1)} %refs_0_.1) | copy-start | bytes 5505028
  232.3 29.2 %collective-permute-start.26 = (bf16[128,2048]{1,0:T(8,128)(2,1)S(1)}, bf16[128,2048]{1,0:T(8,128)(2,1)S(1)}, u32[]{:S(2)}, u32[]{:S(2)}) collective-permute-start(bf16[128,2048]{1,0:T(8,128)(2,1)S(1)} %fusion), channel_id=1, source_target_pairs={{0,0},{5,4},{10,8},{15,12},{4,1},{1,5},{14,9},{11,13},{8,2},{13,6}... | collective-permute-start | bytes 1572872 | tf_op jit(solution)/shard_map/ppermute | solution.py:324
  235.6 23.1 %collective-permute-start.25 = (bf16[128,1536]{1,0:T(8,128)(2,1)S(1)}, bf16[128,1536]{1,0:T(8,128)(2,1)S(1)}, u32[]{:S(2)}, u32[]{:S(2)}) collective-permute-start(bf16[128,1536]{1,0:T(8,128)(2,1)S(1)} %fusion.9), channel_id=1, source_target_pairs={{0,2},{1,3},{2,0},{3,1},{4,6},{5,7},{6,4},{7,5},{8,10},{9,11},{10,... | collective-permute-start | bytes 1179656 | tf_op jit(solution)/shard_map/ppermute | solution.py:311
  245.6 14.4 %copy-start.40 = (bf16[128,2048]{1,0:T(8,128)(2,1)S(1)}, bf16[128,2048]{1,0:T(8,128)(2,1)}, u32[]{:S(2)}) copy-start(bf16[128,2048]{1,0:T(8,128)(2,1)} %fusion.5) | copy-start | bytes 1572868
  (11 other events, 10.1 us)

commit v11 on v9

--- a/solution.py
+++ b/solution.py
@@ -11,7 +11,7 @@
 
 adapter_scale = 2.0
 CORE, CHIP = 1, 2
-VMEM = 48 * 1024 * 1024
+VMEM = 40 * 1024 * 1024
 
 
 def dot(a, b, contract):
@@ -53,67 +53,114 @@
     )(tokens, wide, weight, up_flat)
 
 
-def return_grad(facts, first, second, weight, store, places, sent=()):
+def return_grad(first, second, weight, half, rows_of, columns_of, carried=(), added=False, send=True):
     rows, hidden = first.shape
-    depth, rank = weight.shape[0], store.shape[1]
-    groups = facts.shape[0] // 2
+    depth = weight.shape[0]
     block = 256
-    half = places[0] // 2
-
-    def kernel(facts_ref, a_ref, b_ref, w_ref, up_a_ref, up_b_ref, *refs):
-        out_ref, sent_ref, rank_ref, rhs = refs[len(sent) :]
-        n = pl.program_id(0)
-
-        @pl.when(n == 0)
+    base, column = rows_of[0] // block, columns_of[0] // hidden
+    steps = (rows_of[1] - rows_of[0]) // block
+
+    def kernel(a_ref, b_ref, w_ref, *refs):
+        out_ref, rhs = refs[len(carried)], refs[-1]
+
+        @pl.when(pl.program_id(0) == 0)
         def _():
             rhs[:rows] = a_ref[...]
             rhs[rows:] = b_ref[...]
 
         total = dot(w_ref[...], rhs[...], (1, 1)).T
+        if added:
+            total += refs[0][...]
         out_ref[...] = total
-        sent_ref[...] = total.astype(first.dtype)
+        if send:
+            refs[-2][...] = total.astype(first.dtype)
+
+    whole = lambda n: (0, 0)
+    tile = pl.BlockSpec((2 * rows, block), lambda n: (0, n + base))
+    outs = [(tile, jax.ShapeDtypeStruct((2 * rows, depth), jnp.float32))]
+    if send:
+        outs.append(
+            (
+                pl.BlockSpec((2 * rows, block), lambda n: (half, n + base)),
+                jax.ShapeDtypeStruct((4 * rows, depth), first.dtype),
+            )
+        )
+    anywhere = pl.BlockSpec(memory_space=pl.ANY)
+    taken = [tile if added and x.dtype == jnp.float32 else anywhere for x in carried]
+    target = {jnp.dtype(jnp.float32): 0, jnp.dtype(first.dtype): 1}
+    return pl.pallas_call(
+        kernel,
+        grid=(steps,),
+        in_specs=[
+            pl.BlockSpec((rows, hidden), whole),
+            pl.BlockSpec((rows, hidden), whole),
+            pl.BlockSpec((block, hidden), lambda n: (n + base, column)),
+        ]
+        + taken,
+        out_specs=[o[0] for o in outs],
+        out_shape=[o[1] for o in outs],
+        input_output_aliases={3 + n: target[jnp.dtype(x.dtype)] for n, x in enumerate(carried)},
+        scratch_shapes=[pltpu.VMEM((2 * rows, hidden), first.dtype)],
+        compiler_params=pltpu.CompilerParams(vmem_limit_bytes=VMEM),
+        cost_estimate=cost(4 * rows * hidden * block * steps, 2 * hidden * (block * steps + 2 * rows)),
+        name="return_grad",
+    )(first, second, weight, *carried)
+
+
+def rank_back(facts, store, blocks, places, block, start=0, before=None):
+    rank = store.shape[1]
+    rows, columns = blocks[0].shape
+    count = len(blocks)
+    groups = facts.shape[0] // 2
+    base = start // block
+    earlier = [] if before is None else [before]
+
+    def kernel(facts_ref, *refs):
+        slots, values, out_ref, total = refs[:count], refs[count : 2 * count], refs[-2], refs[-1]
+        n = pl.program_id(0)
+        left = jnp.concatenate([r[0] for r in slots], axis=0)
+        right = jnp.concatenate([r[...] for r in values], axis=0)
+        product = dot(left, right, (1, 1))
+
+        @pl.when(n == 0)
+        def _():
+            total[...] = product
+
+        @pl.when(n > 0)
+        def _():
+            total[...] += product
 
         @pl.when(n == pl.num_programs(0) - 1)
         def _():
-            ranks = dot(jnp.concatenate([up_a_ref[0], up_b_ref[0]], axis=0), rhs[...], (1, 1))
             for at, place in enumerate(places):
-                value = ranks[at * rank : (at + 1) * rank, at * rows : (at + 1) * rows]
+                part = total[at * rank : (at + 1) * rank, at * rows : (at + 1) * rows]
                 alive = lax.broadcasted_iota(jnp.int32, (rank, rows), 1) < facts_ref[groups + place]
                 alive = alive & (facts_ref[place] >= 0)
-                rank_ref[:, at * rows : (at + 1) * rows] = jnp.where(alive, value * adapter_scale, 0.0)
+                part = jnp.where(alive, part * adapter_scale, 0.0)
+                if earlier:
+                    part += refs[2 * count][:, at * rows : (at + 1) * rows]
+                out_ref[:, at * rows : (at + 1) * rows] = part
 
     def chosen_slot(place):
-        return lambda n, facts_ref: (jnp.maximum(facts_ref[place], 0), 0, 0)
-
+        return lambda n, facts_ref: (jnp.maximum(facts_ref[place], 0), 0, n + base)
+
+    small = pl.BlockSpec((rank, count * rows), lambda n, facts_ref: (0, 0))
     return pl.pallas_call(
         kernel,
         grid_spec=pltpu.PrefetchScalarGridSpec(
             num_scalar_prefetch=1,
-            grid=(depth // block,),
-            in_specs=[
-                pl.BlockSpec(memory_space=pltpu.VMEM),
-                pl.BlockSpec(memory_space=pltpu.VMEM),
-                pl.BlockSpec((block, hidden), lambda n, facts_ref: (n, 0)),
-                *[pl.BlockSpec((1, rank, hidden), chosen_slot(place)) for place in places],
-                *[pl.BlockSpec(memory_space=pl.ANY)] * len(sent),
-            ],
-            out_specs=[
-                pl.BlockSpec((2 * rows, block), lambda n, facts_ref: (0, n)),
-                pl.BlockSpec((2 * rows, block), lambda n, facts_ref: (half, n)),
-                pl.BlockSpec((rank, 2 * rows), lambda n, facts_ref: (0, 0)),
-            ],
-            scratch_shapes=[pltpu.VMEM((2 * rows, hidden), first.dtype)],
+            grid=(columns // block,),
+            in_specs=[pl.BlockSpec((1, rank, block), chosen_slot(place)) for place in places]
+            + [pl.BlockSpec((rows, block), lambda n, facts_ref: (0, n))] * count
+            + [small] * len(earlier),
+            out_specs=small,
+            scratch_shapes=[pltpu.VMEM((count * rank, count * rows), jnp.float32)],
         ),
-        out_shape=[
-            jax.ShapeDtypeStruct((2 * rows, depth), jnp.float32),
-            jax.ShapeDtypeStruct((4 * rows, depth), first.dtype),
-            jax.ShapeDtypeStruct((rank, 2 * rows), jnp.float32),
-        ],
-        input_output_aliases={6: 1} if sent else {},
-        compiler_params=pltpu.CompilerParams(vmem_limit_bytes=VMEM),
-        cost_estimate=cost(4 * rows * hidden * depth, 2 * hidden * (depth + 2 * rows)),
-        name="return_grad",
-    )(facts, first, second, weight, store, store, *sent)
+        out_shape=jax.ShapeDtypeStruct((rank, count * rows), jnp.float32),
+        compiler_params=pltpu.CompilerParams(vmem_limit_bytes=VMEM),
+        cost_estimate=cost(2 * count * rank * count * rows * columns, 2 * columns * count * (rank + rows)),
+        name="rank_back",
+    )(facts, *[store] * count, *blocks, *earlier)
 
 
 def rank_inner(facts, flat, blocks, rank):
@@ -216,7 +263,7 @@
         out_specs=pl.BlockSpec((span, block), lambda n: (0, n)),
         out_shape=jax.ShapeDtypeStruct((span, columns), jnp.float32),
         compiler_params=pltpu.CompilerParams(vmem_limit_bytes=VMEM),
-        cost_estimate=cost(2 * span * tokens * columns, (4 * span + 2 * tokens) * columns, 1),
+        cost_estimate=cost(2 * span * tokens * columns, (4 * span + 2 * tokens) * columns),
         name="slot_grad",
     )(wide_t, *arrays)
 
@@ -336,31 +383,46 @@
     even_far = both(even, hop)
     cot_x = swap(after(cotangent, even), CHIP)
     near = swap(after(near, even), CORE)
-    grad01, parts, back01 = return_grad(facts, after(cotangent, even), cot_c, weight, adapter_up, (0, 1))
-    odd = after(odd, grad01)
-    odd_far = both(odd, hop)
+    half = depth // 2
+    grad01, parts = return_grad(after(cotangent, even), cot_c, weight, 0, (0, depth), (0, hidden))
     toks = [(even, 0), (odd, 0), (even, 1), (odd, 1)]
-    inner = rank_inner(facts, down_t.reshape(span, width), toks, rank)
-    down_x = rest[:rank] + after(near, inner)[rank:]
-    inner = after(inner, down_x) + along(inner, 1)
-    inner_far = along(inner, 2)
+    inner = rank_inner(facts, down_t.reshape(span, width), [(after(x, grad01), n) for x, n in toks], rank)
+    inner_near = along(inner, 1)
+    odd_far = both(after(odd, inner), hop)
     even_mid = jnp.where(away == 0, even, after(even_far, inner))
     even_all = both(even_mid, hops)
-    odd_mid = jnp.where(away == 0, odd, after(odd_far, even_mid))
+    down_x = rest[:rank] + after(near, inner)[rank:]
+    cot_xc = swap(after(cot_x, even_mid, down_x), CORE)
+    down_x = swap(after(down_x, cot_x), CHIP)
+    back01 = rank_back(facts, after(adapter_up, cot_x, even_mid), [cotangent, cot_c], (0, 1), hidden // 4)
+    inner = after(inner, back01) + inner_near
+    inner_far = along(inner, 2)
+    back23 = rank_back(facts, after(adapter_up, inner), [cot_x, cot_xc], (2, 3), hidden // 4)
+    back = jnp.concatenate([back01, back23], axis=1)
+    back_near = along(back, 1)
+    grad23, parts = return_grad(
+        after(cot_x, back, down_x), cot_xc, weight, 1, (0, half), (0, hidden), (parts,)
+    )
+    back = after(back, grad23) + back_near
+    back_far = along(back, 2)
+    odd_mid = jnp.where(away == 0, odd, after(odd_far, back))
     odd_all = both(odd_mid, hops)
-    cot_xc = swap(after(cot_x, odd_mid, even_all), CORE)
-    down_x = swap(after(down_x, cot_x), CHIP)
-    grad23, parts, back23 = return_grad(facts, after(cot_x, odd_mid), cot_xc, weight, adapter_up, (2, 3), (parts,))
-    down_mine = both(rest[rank:] + near[:rank] + after(down_x, grad23), place)
-    back = jnp.concatenate([back01, back23], axis=1)
-    all_even = jnp.where(away == 0, even, jnp.where(away == 2, even_far, after(even_all, grad23)))
+    down_mine = both(rest[rank:] + near[:rank] + after(down_x, back), place)
+    grad23, parts = return_grad(
+        after(cot_x, odd_mid), cot_xc, weight, 1, (half, depth), (0, hidden), (grad23, parts)
+    )
+    back_wide, _, back_b = spread(facts, after(back, grad23, down_mine), back_far, per_owner, 1.0)
+    parts = lax.all_to_all(after(parts, back_b).reshape(shards, rows, depth), "tp", 0, 0, tiled=True)
+    back_core = swap(back_b, CORE)
+    all_even = jnp.where(away == 0, even, jnp.where(away == 2, even_far, after(even_all, back_b)))
     all_odd = jnp.where(away == 0, odd, jnp.where(away == 2, odd_far, after(odd_all, all_even)))
     all_tokens = jnp.concatenate([all_even, all_odd], axis=0)
-    back = after(back, all_tokens) + along(back, 1)
-    back_wide, _, back_b = spread(facts, back, along(back, 2), per_owner, 1.0)
-    inner_wide, inner_rows, _ = spread(facts, after(inner, back_b), inner_far, per_owner, adapter_scale)
-    back_b = share(after(back_b, inner_wide, down_mine), swap(back_b, CORE), CORE)
-    parts = lax.all_to_all(after(parts, back_b).reshape(shards, rows, depth), "tp", 0, 0, tiled=True)
+    inner_wide, inner_rows, _ = spread(facts, after(inner, all_tokens), inner_far, per_owner, adapter_scale)
+    back_b = share(after(back_b, inner_rows), back_core, CORE)
+    back_chip = swap(back_b, CHIP)
+    cots = [([x], 0) for x in (cotangent, cot_c, cot_x, cot_xc)]
+    up_wide = slot_grad(after(inner_wide, back_b), cots, hidden // 4)
+    back_b = share(after(back_b, up_wide), back_chip, CHIP)
 
     def grad_block(q):
         low, high = [lax.dynamic_slice_in_dim(x, (q & 1) * rows, rows, 0) for x in (grad01, grad23)]
@@ -389,26 +451,23 @@
         return done[-1]
 
     point = make(0, back_b)
-    back_b = share(after(back_b, point), swap(back_b, CHIP), CHIP)
     point = make(1, point)
     point = cross(0, point)
-    point = make(2, point, back_b)
-    point = finish(0, point)
     point = cross(1, point)
-    point = make(3, point)
-    point = finish(1, point)
-    point = cross(2, point)
-    down_wide = slot_grad(after(back_wide, point), [([x], n) for x, n in toks], width // 2)
     back_mine = lax.dynamic_slice_in_dim(back_b, j * rows, rows, 1)
     total = grad_block(j)
     for m in range(1, shards):
-        total = total + lax.dynamic_index_in_dim(after(parts, down_wide), j ^ m, 0, False).astype(jnp.float32)
+        total = total + lax.dynamic_index_in_dim(after(parts, point), j ^ m, 0, False).astype(jnp.float32)
     total = (total + dot(back_mine, down_mine, (0, 0))).astype(b16)
     tokens_grad = both(total, [(b, a) for a, b in place])
-    cots = [([x], 0) for x in (cotangent, cot_c, cot_x, cot_xc)]
-    point = cross(3, total)
-    up_wide = slot_grad(after(inner_wide, point), cots, hidden // 4)
-    point = finish(2, up_wide)
+    point = finish(0, total)
+    point = finish(1, point)
+    point = make(2, point)
+    point = make(3, point)
+    point = cross(2, point)
+    point = cross(3, point)
+    down_wide = slot_grad(after(back_wide, point), [([x], n) for x, n in toks], width // 2)
+    point = finish(2, down_wide)
     finish(3, point)
     projected = jnp.concatenate(done, axis=1)
     up_grad = up_wide.reshape(per_owner, rank, hidden)

time: 238 us -> 257 us (1.080)
  waiting for transfers between devices: 59.5 us -> 69.5 us
  local copies, waits for them, and re-layouts: 14.2 us -> 21.4 us
  other arithmetic: 22.2 us -> 17.2 us
  Pallas kernels: 92.1 us -> 96 us
    ppermute x17, waiting for transfers between devices: 11.4 us -> 30.5 us  [swap(): return lax.ppermute(x, 'dp', [(d, d ^ bit) for d in range(groups)])]
    ppermute x4, waiting for transfers between devices: 20.8 us -> 3.3 us  [along(): return lax.ppermute(x, 'tp', [(z, z ^ bit) for z in range(shards)])]
    unnamed x63 -> x68, local copies, waits for them, and re-layouts: 14.2 us -> 20.6 us
    all_to_all x1, waiting for transfers between devices: 3.73 us -> 8.95 us  [local_square(): lax.all_to_all(after(parts, back_b).reshape(shards, rows, depth), 'tp', 0...]
    pallas_call x2 -> x5, Pallas kernels: 39.3 us -> 43.6 us  [the longest x3 34.8 us: return_grad(): pl.pallas_call(kernel, grid=(steps,), in_specs=[pl.BlockSpec((rows, hidde...]
    convert_element_type x4, other arithmetic: 6.74 us -> 3.24 us  [finish(): done.append(own.astype(b16))]
    pallas_call x4, Pallas kernels: 33.8 us -> 30.6 us  [project(): pl.pallas_call(kernel, grid=((stop - start) // block,), in_specs=[pl.Bloc...]
    ppermute x6, waiting for transfers between devices: 23.6 us -> 26.8 us  [both(): return lax.ppermute(x, ('tp', 'dp'), pairs)]
  transfers between devices with their start and end apart: 28 -> 28, of which waited for: 9 -> 11; matrix products, arithmetic and copies ran while one was open for 11% -> 7% of each run, Pallas kernels for 35% -> 34%
where the time goes in v11:
time: 257 us; the launch traced here: 255 us
  Pallas kernels  96 us (37%)
  waiting for transfers between devices  69.5 us (27%)
  starting transfers between devices  46.8 us (18%)
  local copies, waits for them, and re-layouts  21.4 us (8%)
  other arithmetic  17.2 us (7%)
  matrix products  2.64 us (1%)
    pallas_call x3, Pallas kernels, return_grad(): pl.pallas_call(kernel, grid=(steps,), in_specs=[pl.BlockSpec((rows, hidde...  34.8 us
    pallas_call x4, Pallas kernels, project(): pl.pallas_call(kernel, grid=((stop - start) // block,), in_specs=[pl.Bloc...  30.6 us
    ppermute x17, waiting for transfers between devices, swap(): return lax.ppermute(x, 'dp', [(d, d ^ bit) for d in range(groups)])  30.5 us
    ppermute x6, waiting for transfers between devices, both(): return lax.ppermute(x, ('tp', 'dp'), pairs)  26.8 us
    ppermute x17, starting transfers between devices, swap(): return lax.ppermute(x, 'dp', [(d, d ^ bit) for d in range(groups)])  21.3 us
    unnamed x68, local copies, waits for them, and re-layouts  20.6 us
    ppermute x6, starting transfers between devices, both(): return lax.ppermute(x, ('tp', 'dp'), pairs)  14.4 us
    pallas_call x2, Pallas kernels, slot_grad(): pl.pallas_call(kernel, grid=(columns // block,), in_specs=[pl.BlockSpec((...  13.7 us
  transfers between devices with their start and end apart: 28, of which 11 were waited for; matrix products, arithmetic and copies ran while one was open for 7% of the time, Pallas kernels for 34%

profile of v11, /device:TPU:2, one launch (start us, length us, event | category | flops | bytes accessed | tf_op | source)
XLA Modules:
  0.0 254.8 jit_solution(10812145807381822107)
XLA Ops:
  0.9 1.6 copy-done.7
  4.4 2.2 choose.1
  6.6 0.9 constant_dynamic-update-slice_fusion.1
  7.5 7.7 %collective-permute-done = bf16[128,2048]{1,0:T(8,128)(2,1)S(1)} collective-permute-done((bf16[128,2048]{1,0:T(8,128)(2,1)}, bf16[128,2048]{1,0:T(8,128)(2,1)S(1)}, u32[]{:S(2)}, u32[]{:S(2)}) %collective-permute-start) | collective-permute-done | bytes 524320 | tf_op jit(solution)/shard_map/ppermute | solution.py:358
  15.3 0.8 constant_dynamic-update-slice_fusion.refs_0_.refs_2_
  16.1 1.3 collective-permute-start.1
  17.4 4.7 %collective-permute-start.5 = (bf16[128,7168]{1,0:T(8,128)(2,1)}, bf16[128,7168]{1,0:T(8,128)(2,1)}, u32[]{:S(2)}, u32[]{:S(2)}) collective-permute-start(bf16[128,7168]{1,0:T(8,128)(2,1)} %refs_0_.3), channel_id=1, source_target_pairs={{0,2},{1,3},{2,0},{3,1},{4,6},{5,7},{6,4},{7,5},{8,10},{9,11},{10,... | collective-permute-start | bytes 5505032 | tf_op jit(solution)/shard_map/ppermute | solution.py:358
  22.2 17.1 %return_grad.3 = (f32[256,2048]{1,0:T(8,128)S(1)}, bf16[512,2048]{1,0:T(8,128)(2,1)S(1)}) custom-call(bf16[128,7168]{1,0:T(8,128)(2,1)} %refs_0_.3, bf16[128,7168]{1,0:T(8,128)(2,1)} %collective-permute-done.2.b_ref.refs_3_.refs_1_, bf16[2048,7168]{1,0:T(8,128)(2,1)} %w_ref.13), custom_call_target="tpu_custom_call" | custom-call | flops 117440512 | bytes 516096 | tf_op jit(solution)/shard_map/return_grad/pallas_call | solution.py:91
  39.3 1.3 copy-done.17
  40.6 2.9 %rank_inner.1 = f32[64,512]{1,0:T(8,128)S(1)} custom-call(s32[9]{0:T(128)S(1)} %get-tuple-element.65.facts_ref, bf16[512,2048]{1,0:T(8,128)(2,1)S(1)} %bitcast.31, bf16[256,2048]{1,0:T(8,128)(2,1)} %constant_dynamic-update-slice_fusion.refs_0_.refs_2_, bf16[256,2048]{1,0:T(8,128)(2,1)} %collective-permute-done.3.refs_1_.refs_3_, ...), custom_call_target="tpu_custom_call" | custom-call | flops 16777216 | bytes 65536 | tf_op jit(solution)/shard_map/rank_inner/pallas_call | solution.py:183
  43.5 1.8 collective-permute-done.1
  45.2 1.0 slice_add_fusion.9
  46.2 2.3 broadcast_select_fusion.1
  48.6 11.9 %collective-permute-done.5.refs_2_.a_ref = bf16[128,7168]{1,0:T(8,128)(2,1)} collective-permute-done((bf16[128,7168]{1,0:T(8,128)(2,1)}, bf16[128,7168]{1,0:T(8,128)(2,1)}, u32[]{:S(2)}, u32[]{:S(2)}) %collective-permute-start.5) | collective-permute-done | bytes 1835040 | tf_op jit(solution)/shard_map/ppermute | solution.py:358
  60.5 1.3 collective-permute-start.11
  61.8 1.4 collective-permute-start.6
  63.2 2.6 %collective-permute-start.9 = (bf16[64,2048]{1,0:T(8,128)(2,1)S(1)}, bf16[64,2048]{1,0:T(8,128)(2,1)S(1)}, u32[]{:S(2)}, u32[]{:S(2)}) collective-permute-start(bf16[64,2048]{1,0:T(8,128)(2,1)S(1)} %slice_add_fusion.9), channel_id=1, source_target_pairs={{0,2},{1,3},{2,0},{3,1},{4,6},{5,7},{6,4},{7,5},{8,10},{9,11},{10,... | collective-permute-start | bytes 786440 | tf_op jit(solution)/shard_map/ppermute | solution.py:358
  65.8 4.5 %rank_back.2 = f32[64,256]{1,0:T(8,128)S(1)} custom-call(s32[9]{0:T(128)S(1)} %get-tuple-element.65.facts_ref, bf16[8,64,7168]{2,1,0:T(8,128)(2,1)S(1)} %bitcast.22, bf16[8,64,7168]{2,1,0:T(8,128)(2,1)S(1)} %bitcast.22, bf16[128,7168]{1,0:T(8,128)(2,1)} %refs_0_.3, bf16[128,7168]{1,0:T(8,128)(2,1)} %collective-permute-done.2.b_ref.refs_3_.refs_1_), custom_call_target="tpu_custom_call" | custom-call | flops 7340032 | bytes 86016 | tf_op jit(solution)/shard_map/rank_back/pallas_call | solution.py:148
  70.4 4.3 %rank_back.3 = f32[64,256]{1,0:T(8,128)S(1)} custom-call(s32[9]{0:T(128)S(1)} %get-tuple-element.65.facts_ref, bf16[8,64,7168]{2,1,0:T(8,128)(2,1)S(1)} %bitcast.22, bf16[8,64,7168]{2,1,0:T(8,128)(2,1)S(1)} %bitcast.22, bf16[128,7168]{1,0:T(8,128)(2,1)} %collective-permute-done.5.refs_2_.a_ref, bf16[128,7168]{1,0:T(8,128)(2,1)S(1)} %collective-permute-done.8.refs_3_.b_ref), custom_call_target="tpu_custom_call" | custom-call | flops 7340032 | bytes 86016 | tf_op jit(solution)/shard_map/rank_back/pallas_call | solution.py:148
  74.7 2.0 collective-permute-start.10
  76.7 2.9 %collective-permute-start.4 = (bf16[256,2048]{1,0:T(8,128)(2,1)}, bf16[256,2048]{1,0:T(8,128)(2,1)}, u32[]{:S(2)}, u32[]{:S(2)}) collective-permute-start(bf16[256,2048]{1,0:T(8,128)(2,1)} %broadcast_select_fusion.1), channel_id=1, source_target_pairs={{0,4},{8,12},{5,1},{13,9},{10,14},{2,6},{15,11},{7,3},{16,20},{24,... | collective-permute-start | bytes 3145736 | tf_op jit(solution)/shard_map/ppermute | solution.py:371
  79.6 8.9 %return_grad.4 = (f32[256,2048]{1,0:T(8,128)S(1)}, bf16[512,2048]{1,0:T(8,128)(2,1)S(1)}) custom-call(bf16[128,7168]{1,0:T(8,128)(2,1)} %collective-permute-done.5.refs_2_.a_ref, bf16[128,7168]{1,0:T(8,128)(2,1)S(1)} %collective-permute-done.8.refs_3_.b_ref, bf16[2048,7168]{1,0:T(8,128)(2,1)} %w_ref.13, ...), custom_call_target="tpu_custom_call", output_to_operand_aliasing={{1}: (3, {})} | custom-call | flops 58720256 | bytes 286720 | tf_op jit(solution)/shard_map/return_grad/pallas_call | solution.py:91
  88.5 1.9 collective-permute-done.10
  90.5 1.1 broadcast_select_fusion
  91.6 2.4 collective-permute-start.14
  94.0 1.0 fusion.13
  95.0 1.9 collective-permute-start.12
  97.0 3.0 %collective-permute-start.13 = (f32[64,512]{1,0:T(8,128)S(1)}, f32[64,512]{1,0:T(8,128)S(1)}, u32[]{:S(2)}, u32[]{:S(2)}) collective-permute-start(f32[64,512]{1,0:T(8,128)S(1)} %add.88.refs_0_), channel_id=1, source_target_pairs={{0,8},{4,12},{8,0},{12,4},{1,9},{5,13},{9,1},{13,5},{2,10},{6,14},... | collective-permute-start | bytes 393224 | tf_op jit(solution)/shard_map/ppermute | solution.py:361
  100.0 1.6 copy-done.5
  101.6 1.6 copy-done.10
  103.2 8.9 %return_grad.5 = (f32[256,2048]{1,0:T(8,128)S(1)}, bf16[512,2048]{1,0:T(8,128)(2,1)S(1)}) custom-call(bf16[128,7168]{1,0:T(8,128)(2,1)} %collective-permute-done.5.refs_2_.a_ref, bf16[128,7168]{1,0:T(8,128)(2,1)S(1)} %copy-done.2, bf16[2048,7168]{1,0:T(8,128)(2,1)} %w_ref.13, ...), custom_call_target="tpu_custom_call", output_to_operand_aliasing={{0}: (3, {}), {1}: (4, {})} | custom-call | flops 58720256 | bytes 286720 | tf_op jit(solution)/shard_map/return_grad/pallas_call | solution.py:91
  112.1 1.4 copy-done.11
  114.0 1.4 collective-permute-done.13.refs_1_
  115.4 1.7 spread.2
  117.1 7.3 %collective-permute-start.16 = (bf16[64,512]{1,0:T(8,128)(2,1)S(1)}, bf16[64,512]{1,0:T(8,128)(2,1)S(1)}, u32[]{:S(2)}, u32[]{:S(2)}) collective-permute-start(bf16[64,512]{1,0:T(8,128)(2,1)S(1)} %get-tuple-element.97), channel_id=1, source_target_pairs={{0,1},{1,0},{2,3},{3,2},{4,5},{5,4},{6,7},{7,6},{8,9},{9,8},{10,11... | collective-permute-start | bytes 196616 | tf_op jit(solution)/shard_map/ppermute | solution.py:358
  124.4 1.4 select_select_fusion.1
  126.1 1.4 spread.3
  127.5 0.8 copy-done.18
  128.3 4.0 %collective-permute-start.17 = (bf16[64,512]{1,0:T(8,128)(2,1)S(1)}, bf16[64,512]{1,0:T(8,128)(2,1)S(1)}, u32[]{:S(2)}, u32[]{:S(2)}) collective-permute-start(bf16[64,512]{1,0:T(8,128)(2,1)S(1)} %maximum_add_fusion), channel_id=1, source_target_pairs={{0,2},{1,3},{2,0},{3,1},{4,6},{5,7},{6,4},{7,5},{8,10},{9,11},{10,... | collective-permute-start | bytes 196616 | tf_op jit(solution)/shard_map/ppermute | solution.py:358
  132.4 4.6 %all-to-all-start = ((bf16[4,128,2048]{2,1,0:T(8,128)(2,1)}), bf16[4,128,2048]{2,1,0:T(8,128)(2,1)}, u32[]{:S(2)}, u32[]{:S(2)}) async-start(bf16[4,128,2048]{2,1,0:T(8,128)(2,1)} %bitcast.29), calls=%async_computation | async-start | bytes 4194304 | tf_op jit(solution)/shard_map/all_to_all | solution.py:415
  137.0 1.6 copy-done.3
  138.7 1.2 copy-done.19
  139.9 9.7 %slot_grad.2 = f32[512,7168]{1,0:T(8,128)} custom-call(bf16[512,512]{1,0:T(8,128)(2,1)S(1)} %copy-done.19, bf16[128,7168]{1,0:T(8,128)(2,1)} %refs_0_.3, bf16[128,7168]{1,0:T(8,128)(2,1)} %collective-permute-done.2.b_ref.refs_3_.refs_1_, bf16[128,7168]{1,0:T(8,128)(2,1)} %collective-permute-done.5.refs_2_.a_ref, bf16[128,7168]{1,0:T(8,128)(2,1)S(1)} %copy-done.3), custom_call_target="tpu_custom_call" | custom-call | flops 58720256 | bytes 344064 | tf_op jit(solution)/shard_map/slot_grad/pallas_call | solution.py:259
  150.3 8.9 %project.4 = (f32[256,2048]{1,0:T(8,128)S(1)}, f32[256,2048]{1,0:T(8,128)}) custom-call(bf16[512,2048]{1,0:T(8,128)(2,1)S(1)} %pad_maximum_fusion.tok_ref, bf16[512,512]{1,0:T(8,128)(2,1)S(1)} %get-tuple-element.96.wide_ref, bf16[2048,7168]{1,0:T(8,128)(2,1)} %w_ref.13, bf16[512,7168]{1,0:T(8,128)(2,1)S(1)} %bitcast.25), custom_call_target="tpu_custom_call" | custom-call | flops 83886080 | bytes 229376 | tf_op jit(solution)/shard_map/project/pallas_call | solution.py:39
  159.1 1.4 copy-done.12
  160.6 7.3 %project.5 = (f32[256,1536]{1,0:T(8,128)S(1)}, f32[256,1536]{1,0:T(8,128)}) custom-call(bf16[512,2048]{1,0:T(8,128)(2,1)S(1)} %pad_maximum_fusion.tok_ref, bf16[512,512]{1,0:T(8,128)(2,1)S(1)} %get-tuple-element.96.wide_ref, bf16[2048,7168]{1,0:T(8,128)(2,1)} %w_ref.13, bf16[512,7168]{1,0:T(8,128)(2,1)S(1)} %bitcast.26), custom_call_target="tpu_custom_call" | custom-call | flops 62914560 | bytes 172032 | tf_op jit(solution)/shard_map/project/pallas_call | solution.py:39
  167.9 1.1 copy-done.14
  169.5 2.6 %fusion.6 = bf16[128,2048]{1,0:T(8,128)(2,1)} fusion(f32[256,2048]{1,0:T(8,128)} %collective-permute-done.18, f32[256,2048]{1,0:T(8,128)} %copy-done.12), kind=kLoop, calls=%fused_computation.13 | loop fusion | flops 524288 | bytes 2621440 | tf_op jit(solution)/shard_map/convert_element_type | solution.py:444
  172.9 2.0 fusion.12
  174.8 1.2 collective-permute-start.21
  176.1 9.0 %all-to-all-done = bf16[4,128,2048]{2,1,0:T(8,128)(2,1)} async-done(((bf16[4,128,2048]{2,1,0:T(8,128)(2,1)}), bf16[4,128,2048]{2,1,0:T(8,128)(2,1)}, u32[]{:S(2)}, u32[]{:S(2)}) %all-to-all-start) | async-done | bytes 2097184 | tf_op jit(solution)/shard_map/all_to_all | solution.py:415
  185.0 2.6 %fusion = bf16[128,2048]{1,0:T(8,128)(2,1)S(1)} fusion(bf16[64,2048]{1,0:T(8,128)(2,1)} %copy-done.28, f32[256,2048]{1,0:T(8,128)} %copy-done.11, s32[]{:T(128)S(6)} %select_n.64, f32[256,2048]{1,0:T(8,128)} %copy-done.17, bf16[4,128,2048]{2,1,0:T(8,128)(2,1)} %all-to-all-done, s32[]{:T(128)S(6)} %select_n.68, s32[]{:T(128)S(6)} %select_n.67, ...), kind=kOutput, calls=%fused_computation.1 | convolution fusion | flops 35913728 | bytes 4472853 | tf_op jit(solution)/shard_map/dot_general | solution.py:18
  187.8 1.7 fusion.5
  189.5 5.1 %collective-permute-done.21 = bf16[128,1536]{1,0:T(8,128)(2,1)S(1)} collective-permute-done((bf16[128,1536]{1,0:T(8,128)(2,1)}, bf16[128,1536]{1,0:T(8,128)(2,1)S(1)}, u32[]{:S(2)}, u32[]{:S(2)}) %collective-permute-start.21) | collective-permute-done | bytes 393248 | tf_op jit(solution)/shard_map/ppermute | solution.py:358
  194.6 1.3 fusion.11
  195.9 3.1 %copy-done = bf16[8,64,7168]{2,1,0:T(8,128)(2,1)S(1)} copy-done((bf16[8,64,7168]{2,1,0:T(8,128)(2,1)S(1)}, bf16[8,64,7168]{2,1,0:T(8,128)(2,1)}, u32[]{:S(2)}) %copy-start) | copy-done | bytes 7340056
  198.9 8.0 %project.6 = (f32[256,2048]{1,0:T(8,128)S(1)}, f32[256,2048]{1,0:T(8,128)S(1)}) custom-call(bf16[512,2048]{1,0:T(8,128)(2,1)S(1)} %pad_maximum_fusion.tok_ref, bf16[512,512]{1,0:T(8,128)(2,1)S(1)} %get-tuple-element.96.wide_ref, bf16[2048,7168]{1,0:T(8,128)(2,1)} %w_ref.13, bf16[512,7168]{1,0:T(8,128)(2,1)S(1)} %bitcast.27), custom_call_target="tpu_custom_call" | custom-call | flops 83886080 | bytes 229376 | tf_op jit(solution)/shard_map/project/pallas_call | solution.py:39
  207.0 6.4 %project.7 = (f32[256,1536]{1,0:T(8,128)S(1)}, f32[256,1536]{1,0:T(8,128)S(1)}) custom-call(bf16[512,2048]{1,0:T(8,128)(2,1)S(1)} %pad_maximum_fusion.tok_ref, bf16[512,512]{1,0:T(8,128)(2,1)S(1)} %get-tuple-element.96.wide_ref, bf16[2048,7168]{1,0:T(8,128)(2,1)} %w_ref.13, bf16[512,7168]{1,0:T(8,128)(2,1)S(1)} %bitcast.28), custom_call_target="tpu_custom_call" | custom-call | flops 62914560 | bytes 172032 | tf_op jit(solution)/shard_map/project/pallas_call | solution.py:39
  214.0 4.6 %collective-permute-start.26 = (bf16[128,2048]{1,0:T(8,128)(2,1)S(1)}, bf16[128,2048]{1,0:T(8,128)(2,1)S(1)}, u32[]{:S(2)}, u32[]{:S(2)}) collective-permute-start(bf16[128,2048]{1,0:T(8,128)(2,1)S(1)} %fusion), channel_id=1, source_target_pairs={{0,0},{5,4},{10,8},{15,12},{4,1},{1,5},{14,9},{11,13},{8,2},{13,6}... | collective-permute-start | bytes 1572872 | tf_op jit(solution)/shard_map/ppermute | solution.py:371
  218.8 24.4 %collective-permute-done.26 = bf16[128,2048]{1,0:T(8,128)(2,1)S(1)} collective-permute-done((bf16[128,2048]{1,0:T(8,128)(2,1)S(1)}, bf16[128,2048]{1,0:T(8,128)(2,1)S(1)}, u32[]{:S(2)}, u32[]{:S(2)}) %collective-permute-start.26) | collective-permute-done | bytes 524320 | tf_op jit(solution)/shard_map/ppermute | solution.py:371
  243.4 4.0 %slot_grad.3 = f32[512,2048]{1,0:T(8,128)} custom-call(bf16[512,512]{1,0:T(8,128)(2,1)S(1)} %get-tuple-element.123.wide_ref, bf16[256,2048]{1,0:T(8,128)(2,1)} %constant_dynamic-update-slice_fusion.refs_0_.refs_2_, bf16[256,2048]{1,0:T(8,128)(2,1)} %collective-permute-done.3.refs_1_.refs_3_, ...), custom_call_target="tpu_custom_call" | custom-call | flops 16777216 | bytes 98304 | tf_op jit(solution)/shard_map/slot_grad/pallas_call | solution.py:259
  247.5 4.9 %collective-permute-done.25 = bf16[128,1536]{1,0:T(8,128)(2,1)S(1)} collective-permute-done((bf16[128,1536]{1,0:T(8,128)(2,1)S(1)}, bf16[128,1536]{1,0:T(8,128)(2,1)S(1)}, u32[]{:S(2)}, u32[]{:S(2)}) %collective-permute-start.25) | collective-permute-done | bytes 393248 | tf_op jit(solution)/shard_map/ppermute | solution.py:358
  252.6 1.4 pad_maximum_fusion.1
  254.0 0.8 copy.20
  (103 shorter events, 6.7 us)
Async XLA Ops:
  0.6 21.5 %collective-permute-start.2 = (bf16[128,7168]{1,0:T(8,128)(2,1)}, bf16[128,7168]{1,0:T(8,128)(2,1)}, u32[]{:S(2)}, u32[]{:S(2)}) collective-permute-start(bf16[128,7168]{1,0:T(8,128)(2,1)} %refs_0_.3), channel_id=1, source_target_pairs={{0,1},{1,0},{2,3},{3,2},{4,5},{5,4},{6,7},{7,6},{8,9},{9,8},{10,11... | collective-permute-start | bytes 5505032 | tf_op jit(solution)/shard_map/ppermute | solution.py:358
  0.7 14.5 %collective-permute-start = (bf16[128,2048]{1,0:T(8,128)(2,1)}, bf16[128,2048]{1,0:T(8,128)(2,1)S(1)}, u32[]{:S(2)}, u32[]{:S(2)}) collective-permute-start(bf16[128,2048]{1,0:T(8,128)(2,1)} %param.8), channel_id=1, source_target_pairs={{0,2},{1,3},{2,0},{3,1},{4,6},{5,7},{6,4},{7,5},{8,10},{9,11},{10,... | collective-permute-start | bytes 1572872 | tf_op jit(solution)/shard_map/ppermute | solution.py:358
  0.9 1.6 copy-start.7
  2.5 0.7 copy-start.22
  3.1 0.7 copy-start.23
  3.8 0.7 copy-start.24
  4.4 2.2 copy-start.27
  6.6 15.5 %copy-start.20 = (bf16[128,2048]{1,0:T(8,128)(2,1)}, bf16[128,2048]{1,0:T(8,128)(2,1)S(1)}, u32[]{:S(2)}) copy-start(bf16[128,2048]{1,0:T(8,128)(2,1)S(1)} %get-tuple-element.75) | copy-start | bytes 1572868
  16.1 24.5 %collective-permute-start.3 = (bf16[256,2048]{1,0:T(8,128)(2,1)}, bf16[256,2048]{1,0:T(8,128)(2,1)}, u32[]{:S(2)}, u32[]{:S(2)}) collective-permute-start(bf16[256,2048]{1,0:T(8,128)(2,1)} %constant_dynamic-update-slice_fusion.refs_0_.refs_2_), channel_id=1, source_target_pairs={{0,1},{1,0},{2,3},{3,2},{4,5},{5,4},{6,7},{7,6},{8,9},{9,8},{10,11... | collective-permute-start | bytes 3145736 | tf_op jit(solution)/shard_map/ppermute | solution.py:358
  16.1 29.1 %collective-permute-start.1 = (bf16[256,2048]{1,0:T(8,128)(2,1)}, bf16[256,2048]{1,0:T(8,128)(2,1)}, u32[]{:S(2)}, u32[]{:S(2)}) collective-permute-start(bf16[256,2048]{1,0:T(8,128)(2,1)} %constant_dynamic-update-slice_fusion.refs_0_.refs_2_), channel_id=1, source_target_pairs={{0,8},{5,13},{10,2},{15,7},{16,24},{21,29},{26,18},{31,23}} | collective-permute-start | bytes 3145736 | tf_op jit(solution)/shard_map/ppermute | solution.py:371
  17.4 43.1 %collective-permute-start.5 = (bf16[128,7168]{1,0:T(8,128)(2,1)}, bf16[128,7168]{1,0:T(8,128)(2,1)}, u32[]{:S(2)}, u32[]{:S(2)}) collective-permute-start(bf16[128,7168]{1,0:T(8,128)(2,1)} %refs_0_.3), channel_id=1, source_target_pairs={{0,2},{1,3},{2,0},{3,1},{4,6},{5,7},{6,4},{7,5},{8,10},{9,11},{10,... | collective-permute-start | bytes 5505032 | tf_op jit(solution)/shard_map/ppermute | solution.py:358
  22.1 21.3 %collective-permute-start.7 = (bf16[128,2048]{1,0:T(8,128)(2,1)}, bf16[128,2048]{1,0:T(8,128)(2,1)}, u32[]{:S(2)}, u32[]{:S(2)}) collective-permute-start(bf16[128,2048]{1,0:T(8,128)(2,1)} %get-tuple-element.77), channel_id=1, source_target_pairs={{0,1},{1,0},{2,3},{3,2},{4,5},{5,4},{6,7},{7,6},{8,9},{9,8},{10,11... | collective-permute-start | bytes 1572872 | tf_op jit(solution)/shard_map/ppermute | solution.py:358
  22.1 43.6 %slice-start = ((s8[7340032]{0:T(1024)(128)(4,1)}), s8[3145728]{0:T(1024)(128)(4,1)S(1)}, s32[]{:S(2)}) async-start(s8[7340032]{0:T(1024)(128)(4,1)} %bitcast.21), calls=%async_computation.1 | async-start | bytes 6291456
  22.1 18.4 %copy-start.8 = (bf16[8,2048,64]{1,2,0:T(8,128)(2,1)S(1)}, bf16[8,2048,64]{1,2,0:T(8,128)(2,1)}, u32[]{:S(2)}) copy-start(bf16[8,2048,64]{1,2,0:T(8,128)(2,1)} %param.10) | copy-start | bytes 6291460
  22.2 43.6 %slice-start.1 = ((s8[7340032]{0:T(1024)(128)(4,1)}), s8[4194304]{0:T(1024)(128)(4,1)S(1)}, s32[]{:S(2)}) async-start(s8[7340032]{0:T(1024)(128)(4,1)} %bitcast.21), calls=%async_computation.2 | async-start | bytes 8388608
  39.3 1.3 copy-start.17
  40.6 4.7 %copy-start.21 = (bf16[128,2048]{1,0:T(8,128)(2,1)S(1)}, bf16[128,2048]{1,0:T(8,128)(2,1)}, u32[]{:S(2)}) copy-start(bf16[128,2048]{1,0:T(8,128)(2,1)} %copy-done.20) | copy-start | bytes 1572868
  60.5 9.8 %collective-permute-start.8 = (bf16[128,7168]{1,0:T(8,128)(2,1)}, bf16[128,7168]{1,0:T(8,128)(2,1)S(1)}, u32[]{:S(2)}, u32[]{:S(2)}) collective-permute-start(bf16[128,7168]{1,0:T(8,128)(2,1)} %collective-permute-done.5.refs_2_.a_ref), channel_id=1, source_target_pairs={{0,1},{1,0},{2,3},{3,2},{4,5},{5,4},{6,7},{7,6},{8,9},{9,8},{10,11... | collective-permute-start | bytes 5505032 | tf_op jit(solution)/shard_map/ppermute | solution.py:358
  60.5 29.9 %collective-permute-start.11 = (bf16[256,2048]{1,0:T(8,128)(2,1)}, bf16[256,2048]{1,0:T(8,128)(2,1)S(1)}, u32[]{:S(2)}, u32[]{:S(2)}) collective-permute-start(bf16[256,2048]{1,0:T(8,128)(2,1)} %collective-permute-done.3.refs_1_.refs_3_), channel_id=1, source_target_pairs={{0,8},{5,13},{10,2},{15,7},{16,24},{21,29},{26,18},{31,23}} | collective-permute-start | bytes 3145736 | tf_op jit(solution)/shard_map/ppermute | solution.py:371
  61.8 8.5 %collective-permute-start.6 = (f32[64,512]{1,0:T(8,128)S(1)}, f32[64,512]{1,0:T(8,128)S(1)}, u32[]{:S(2)}, u32[]{:S(2)}) collective-permute-start(f32[64,512]{1,0:T(8,128)S(1)} %rank_inner.1), channel_id=1, source_target_pairs={{0,4},{4,0},{8,12},{12,8},{1,5},{5,1},{9,13},{13,9},{2,6},{6,2},{1... | collective-permute-start | bytes 393224 | tf_op jit(solution)/shard_map/ppermute | solution.py:361
  63.2 16.5 %collective-permute-start.9 = (bf16[64,2048]{1,0:T(8,128)(2,1)S(1)}, bf16[64,2048]{1,0:T(8,128)(2,1)S(1)}, u32[]{:S(2)}, u32[]{:S(2)}) collective-permute-start(bf16[64,2048]{1,0:T(8,128)(2,1)S(1)} %slice_add_fusion.9), channel_id=1, source_target_pairs={{0,2},{1,3},{2,0},{3,1},{4,6},{5,7},{6,4},{7,5},{8,10},{9,11},{10,... | collective-permute-start | bytes 786440 | tf_op jit(solution)/shard_map/ppermute | solution.py:358
  70.4 9.3 %copy-start.1 = (bf16[128,7168]{1,0:T(8,128)(2,1)}, bf16[128,7168]{1,0:T(8,128)(2,1)S(1)}, u32[]{:S(2)}) copy-start(bf16[128,7168]{1,0:T(8,128)(2,1)S(1)} %collective-permute-done.8.refs_3_.b_ref) | copy-start | bytes 5505028
  74.7 15.7 %collective-permute-start.10 = (f32[64,512]{1,0:T(8,128)S(1)}, f32[64,512]{1,0:T(8,128)S(1)}, u32[]{:S(2)}, u32[]{:S(2)}) collective-permute-start(f32[64,512]{1,0:T(8,128)S(1)} %pad_maximum_fusion.2), channel_id=1, source_target_pairs={{0,4},{4,0},{8,12},{12,8},{1,5},{5,1},{9,13},{13,9},{2,6},{6,2},{1... | collective-permute-start | bytes 393224 | tf_op jit(solution)/shard_map/ppermute | solution.py:361
  76.7 47.7 %collective-permute-start.4 = (bf16[256,2048]{1,0:T(8,128)(2,1)}, bf16[256,2048]{1,0:T(8,128)(2,1)}, u32[]{:S(2)}, u32[]{:S(2)}) collective-permute-start(bf16[256,2048]{1,0:T(8,128)(2,1)} %broadcast_select_fusion.1), channel_id=1, source_target_pairs={{0,4},{8,12},{5,1},{13,9},{10,14},{2,6},{15,11},{7,3},{16,20},{24,... | collective-permute-start | bytes 3145736 | tf_op jit(solution)/shard_map/ppermute | solution.py:371
  88.5 6.5 %copy-start.4 = (bf16[512,2048]{1,0:T(8,128)(2,1)}, bf16[512,2048]{1,0:T(8,128)(2,1)S(1)}, u32[]{:S(2)}) copy-start(bf16[512,2048]{1,0:T(8,128)(2,1)S(1)} %get-tuple-element.88.refs_1_) | copy-start | bytes 6291460
  88.5 6.5 %copy-start.9 = (f32[256,2048]{1,0:T(8,128)}, f32[256,2048]{1,0:T(8,128)S(1)}, u32[]{:S(2)}) copy-start(f32[256,2048]{1,0:T(8,128)S(1)} %get-tuple-element.83.refs_0_) | copy-start | bytes 6291460
  90.4 9.6 %copy-start.2 = (bf16[128,7168]{1,0:T(8,128)(2,1)S(1)}, bf16[128,7168]{1,0:T(8,128)(2,1)}, u32[]{:S(2)}) copy-start(bf16[128,7168]{1,0:T(8,128)(2,1)} %copy-done.1) | copy-start | bytes 5505028
  90.5 6.5 %copy-start.25 = (bf16[256,2048]{1,0:T(8,128)(2,1)}, bf16[256,2048]{1,0:T(8,128)(2,1)S(1)}, u32[]{:S(2)}) copy-start(bf16[256,2048]{1,0:T(8,128)(2,1)S(1)} %collective-permute-done.11) | copy-start | bytes 3145732
  91.6 34.2 %collective-permute-start.14 = (bf16[256,2048]{1,0:T(8,128)(2,1)}, bf16[256,2048]{1,0:T(8,128)(2,1)}, u32[]{:S(2)}, u32[]{:S(2)}) collective-permute-start(bf16[256,2048]{1,0:T(8,128)(2,1)} %broadcast_select_fusion), channel_id=1, source_target_pairs={{0,4},{8,12},{5,1},{13,9},{10,14},{2,6},{15,11},{7,3},{16,20},{24,... | collective-permute-start | bytes 3145736 | tf_op jit(solution)/shard_map/ppermute | solution.py:371
  95.0 19.0 %collective-permute-start.12 = (bf16[64,2048]{1,0:T(8,128)(2,1)S(1)}, bf16[64,2048]{1,0:T(8,128)(2,1)S(1)}, u32[]{:S(2)}, u32[]{:S(2)}) collective-permute-start(bf16[64,2048]{1,0:T(8,128)(2,1)S(1)} %fusion.13), channel_id=1, source_target_pairs={{0,0},{4,5},{8,10},{12,15},{1,4},{5,1},{9,14},{13,11},{2,8},{6,13}... | collective-permute-start | bytes 786440 | tf_op jit(solution)/shard_map/ppermute | solution.py:371
  97.0 18.5 %collective-permute-start.13 = (f32[64,512]{1,0:T(8,128)S(1)}, f32[64,512]{1,0:T(8,128)S(1)}, u32[]{:S(2)}, u32[]{:S(2)}) collective-permute-start(f32[64,512]{1,0:T(8,128)S(1)} %add.88.refs_0_), channel_id=1, source_target_pairs={{0,8},{4,12},{8,0},{12,4},{1,9},{5,13},{9,1},{13,5},{2,10},{6,14},... | collective-permute-start | bytes 393224 | tf_op jit(solution)/shard_map/ppermute | solution.py:361
  100.0 26.2 %collective-permute-start.15 = (f32[64,512]{1,0:T(8,128)S(1)}, f32[64,512]{1,0:T(8,128)S(1)}, u32[]{:S(2)}, u32[]{:S(2)}) collective-permute-start(f32[64,512]{1,0:T(8,128)S(1)} %add.86.refs_0_), channel_id=1, source_target_pairs={{0,8},{4,12},{8,0},{12,4},{1,9},{5,13},{9,1},{13,5},{2,10},{6,14},... | collective-permute-start | bytes 393224 | tf_op jit(solution)/shard_map/ppermute | solution.py:361
  100.0 1.6 copy-start.5
  101.6 1.6 copy-start.10
  112.1 1.4 copy-start.11
  113.5 12.3 %copy-start.6 = (bf16[512,2048]{1,0:T(8,128)(2,1)}, bf16[512,2048]{1,0:T(8,128)(2,1)S(1)}, u32[]{:S(2)}) copy-start(bf16[512,2048]{1,0:T(8,128)(2,1)S(1)} %get-tuple-element.104) | copy-start | bytes 6291460
  114.0 11.7 %copy-start.28 = (bf16[64,2048]{1,0:T(8,128)(2,1)}, bf16[64,2048]{1,0:T(8,128)(2,1)S(1)}, u32[]{:S(2)}) copy-start(bf16[64,2048]{1,0:T(8,128)(2,1)S(1)} %collective-permute-done.12) | copy-start | bytes 786436
  117.1 8.7 %copy-start.26 = (bf16[256,2048]{1,0:T(8,128)(2,1)S(1)}, bf16[256,2048]{1,0:T(8,128)(2,1)}, u32[]{:S(2)}) copy-start(bf16[256,2048]{1,0:T(8,128)(2,1)} %copy-done.25) | copy-start | bytes 3145732
  117.1 8.7 %collective-permute-start.16 = (bf16[64,512]{1,0:T(8,128)(2,1)S(1)}, bf16[64,512]{1,0:T(8,128)(2,1)S(1)}, u32[]{:S(2)}, u32[]{:S(2)}) collective-permute-start(bf16[64,512]{1,0:T(8,128)(2,1)S(1)} %get-tuple-element.97), channel_id=1, source_target_pairs={{0,1},{1,0},{2,3},{3,2},{4,5},{5,4},{6,7},{7,6},{8,9},{9,8},{10,11... | collective-permute-start | bytes 196616 | tf_op jit(solution)/shard_map/ppermute | solution.py:358
  127.5 0.8 copy-start.18
  128.3 21.3 %collective-permute-start.17 = (bf16[64,512]{1,0:T(8,128)(2,1)S(1)}, bf16[64,512]{1,0:T(8,128)(2,1)S(1)}, u32[]{:S(2)}, u32[]{:S(2)}) collective-permute-start(bf16[64,512]{1,0:T(8,128)(2,1)S(1)} %maximum_add_fusion), channel_id=1, source_target_pairs={{0,2},{1,3},{2,0},{3,1},{4,6},{5,7},{6,4},{7,5},{8,10},{9,11},{10,... | collective-permute-start | bytes 196616 | tf_op jit(solution)/shard_map/ppermute | solution.py:358
  132.4 52.7 %all-to-all-start = ((bf16[4,128,2048]{2,1,0:T(8,128)(2,1)}), bf16[4,128,2048]{2,1,0:T(8,128)(2,1)}, u32[]{:S(2)}, u32[]{:S(2)}) async-start(bf16[4,128,2048]{2,1,0:T(8,128)(2,1)} %bitcast.29), calls=%async_computation | async-start | bytes 4194304 | tf_op jit(solution)/shard_map/all_to_all | solution.py:415
  137.0 13.2 %slice-start.2 = ((s8[7340032]{0:T(1024)(128)(4,1)}), s8[4194304]{0:T(1024)(128)(4,1)S(1)}, s32[]{:S(2)}) async-start(s8[7340032]{0:T(1024)(128)(4,1)} %bitcast.23), calls=%async_computation.3 | async-start | bytes 8388608
  137.0 1.7 copy-start.3
  138.7 1.2 copy-start.19
  139.9 10.4 %slice-start.3 = ((s8[7340032]{0:T(1024)(128)(4,1)}), s8[3145728]{0:T(1024)(128)(4,1)S(1)}, s32[]{:S(2)}) async-start(s8[7340032]{0:T(1024)(128)(4,1)} %bitcast.23), calls=%async_computation.4 | async-start | bytes 6291456
  159.1 1.4 copy-start.12
  160.6 8.9 %collective-permute-start.18 = (f32[256,2048]{1,0:T(8,128)}, f32[256,2048]{1,0:T(8,128)}, u32[]{:S(2)}, u32[]{:S(2)}) collective-permute-start(f32[256,2048]{1,0:T(8,128)} %get-tuple-element.108), channel_id=1, source_target_pairs={{0,1},{1,0},{2,3},{3,2},{4,5},{5,4},{6,7},{7,6},{8,9},{9,8},{10,11... | collective-permute-start | bytes 6291464 | tf_op jit(solution)/shard_map/ppermute | solution.py:358
  167.9 1.1 copy-start.14
  169.0 3.9 %collective-permute-start.19 = (f32[256,1536]{1,0:T(8,128)}, f32[256,1536]{1,0:T(8,128)}, u32[]{:S(2)}, u32[]{:S(2)}) collective-permute-start(f32[256,1536]{1,0:T(8,128)} %get-tuple-element.110), channel_id=1, source_target_pairs={{0,1},{1,0},{2,3},{3,2},{4,5},{5,4},{6,7},{7,6},{8,9},{9,8},{10,11... | collective-permute-start | bytes 4718600 | tf_op jit(solution)/shard_map/ppermute | solution.py:358
  169.5 3.4 %copy-start.15 = (f32[256,1536]{1,0:T(8,128)S(1)}, f32[256,1536]{1,0:T(8,128)}, u32[]{:S(2)}) copy-start(f32[256,1536]{1,0:T(8,128)} %copy-done.14) | copy-start | bytes 4718596
  172.1 15.6 %collective-permute-start.20 = (bf16[128,2048]{1,0:T(8,128)(2,1)}, bf16[128,2048]{1,0:T(8,128)(2,1)}, u32[]{:S(2)}, u32[]{:S(2)}) collective-permute-start(bf16[128,2048]{1,0:T(8,128)(2,1)} %fusion.6), channel_id=1, source_target_pairs={{0,2},{1,3},{2,0},{3,1},{4,6},{5,7},{6,4},{7,5},{8,10},{9,11},{10,... | collective-permute-start | bytes 1572872 | tf_op jit(solution)/shard_map/ppermute | solution.py:358
  174.8 19.7 %collective-permute-start.21 = (bf16[128,1536]{1,0:T(8,128)(2,1)}, bf16[128,1536]{1,0:T(8,128)(2,1)S(1)}, u32[]{:S(2)}, u32[]{:S(2)}) collective-permute-start(bf16[128,1536]{1,0:T(8,128)(2,1)} %fusion.12), channel_id=1, source_target_pairs={{0,2},{1,3},{2,0},{3,1},{4,6},{5,7},{6,4},{7,5},{8,10},{9,11},{10,... | collective-permute-start | bytes 1179656 | tf_op jit(solution)/shard_map/ppermute | solution.py:358
  185.0 2.8 %copy-start.13 = (f32[256,2048]{1,0:T(8,128)S(1)}, f32[256,2048]{1,0:T(8,128)}, u32[]{:S(2)}) copy-start(f32[256,2048]{1,0:T(8,128)} %copy-done.12) | copy-start | bytes 6291460
  187.7 6.9 %copy-start.16 = (f32[256,1536]{1,0:T(8,128)S(1)}, f32[256,1536]{1,0:T(8,128)}, u32[]{:S(2)}) copy-start(f32[256,1536]{1,0:T(8,128)} %copy-done.14) | copy-start | bytes 4718596
  195.8 3.1 %copy-start = (bf16[8,64,7168]{2,1,0:T(8,128)(2,1)S(1)}, bf16[8,64,7168]{2,1,0:T(8,128)(2,1)}, u32[]{:S(2)}) copy-start(bf16[8,64,7168]{2,1,0:T(8,128)(2,1)} %refs_1_.1) | copy-start | bytes 22020100
  207.0 11.6 %collective-permute-start.22 = (f32[256,2048]{1,0:T(8,128)S(1)}, f32[256,2048]{1,0:T(8,128)S(1)}, u32[]{:S(2)}, u32[]{:S(2)}) collective-permute-start(f32[256,2048]{1,0:T(8,128)S(1)} %get-tuple-element.120), channel_id=1, source_target_pairs={{0,1},{1,0},{2,3},{3,2},{4,5},{5,4},{6,7},{7,6},{8,9},{9,8},{10,11... | collective-permute-start | bytes 6291464 | tf_op jit(solution)/shard_map/ppermute | solution.py:358
  213.5 29.8 %collective-permute-start.23 = (f32[256,1536]{1,0:T(8,128)S(1)}, f32[256,1536]{1,0:T(8,128)S(1)}, u32[]{:S(2)}, u32[]{:S(2)}) collective-permute-start(f32[256,1536]{1,0:T(8,128)S(1)} %get-tuple-element.122), channel_id=1, source_target_pairs={{0,1},{1,0},{2,3},{3,2},{4,5},{5,4},{6,7},{7,6},{8,9},{9,8},{10,11... | collective-permute-start | bytes 4718600 | tf_op jit(solution)/shard_map/ppermute | solution.py:358
  214.0 29.2 %collective-permute-start.26 = (bf16[128,2048]{1,0:T(8,128)(2,1)S(1)}, bf16[128,2048]{1,0:T(8,128)(2,1)S(1)}, u32[]{:S(2)}, u32[]{:S(2)}) collective-permute-start(bf16[128,2048]{1,0:T(8,128)(2,1)S(1)} %fusion), channel_id=1, source_target_pairs={{0,0},{5,4},{10,8},{15,12},{4,1},{1,5},{14,9},{11,13},{8,2},{13,6}... | collective-permute-start | bytes 1572872 | tf_op jit(solution)/shard_map/ppermute | solution.py:371
  218.7 28.6 %collective-permute-start.24 = (bf16[128,2048]{1,0:T(8,128)(2,1)S(1)}, bf16[128,2048]{1,0:T(8,128)(2,1)S(1)}, u32[]{:S(2)}, u32[]{:S(2)}) collective-permute-start(bf16[128,2048]{1,0:T(8,128)(2,1)S(1)} %fusion.3), channel_id=1, source_target_pairs={{0,2},{1,3},{2,0},{3,1},{4,6},{5,7},{6,4},{7,5},{8,10},{9,11},{10,... | collective-permute-start | bytes 1572872 | tf_op jit(solution)/shard_map/ppermute | solution.py:358
  243.3 9.2 %collective-permute-start.25 = (bf16[128,1536]{1,0:T(8,128)(2,1)S(1)}, bf16[128,1536]{1,0:T(8,128)(2,1)S(1)}, u32[]{:S(2)}, u32[]{:S(2)}) collective-permute-start(bf16[128,1536]{1,0:T(8,128)(2,1)S(1)} %fusion.9), channel_id=1, source_target_pairs={{0,2},{1,3},{2,0},{3,1},{4,6},{5,7},{6,4},{7,5},{8,10},{9,11},{10,... | collective-permute-start | bytes 1179656 | tf_op jit(solution)/shard_map/ppermute | solution.py:358

commit v12 on v9

--- a/solution.py
+++ b/solution.py
@@ -337,30 +337,35 @@
     cot_x = swap(after(cotangent, even), CHIP)
     near = swap(after(near, even), CORE)
     grad01, parts, back01 = return_grad(facts, after(cotangent, even), cot_c, weight, adapter_up, (0, 1))
-    odd = after(odd, grad01)
-    odd_far = both(odd, hop)
     toks = [(even, 0), (odd, 0), (even, 1), (odd, 1)]
-    inner = rank_inner(facts, down_t.reshape(span, width), toks, rank)
-    down_x = rest[:rank] + after(near, inner)[rank:]
-    inner = after(inner, down_x) + along(inner, 1)
-    inner_far = along(inner, 2)
+    inner = rank_inner(facts, down_t.reshape(span, width), [(after(x, grad01), n) for x, n in toks], rank)
+    inner_near = along(inner, 1)
+    odd_far = both(after(odd, inner), hop)
     even_mid = jnp.where(away == 0, even, after(even_far, inner))
     even_all = both(even_mid, hops)
-    odd_mid = jnp.where(away == 0, odd, after(odd_far, even_mid))
+    down_x = rest[:rank] + after(near, inner)[rank:]
+    cot_xc = swap(after(cot_x, even_mid, down_x), CORE)
+    down_x = swap(after(down_x, cot_x), CHIP)
+    inner = after(inner, cot_x) + inner_near
+    inner_far = along(inner, 2)
+    odd_mid = jnp.where(away == 0, odd, after(odd_far, inner))
     odd_all = both(odd_mid, hops)
-    cot_xc = swap(after(cot_x, odd_mid, even_all), CORE)
-    down_x = swap(after(down_x, cot_x), CHIP)
-    grad23, parts, back23 = return_grad(facts, after(cot_x, odd_mid), cot_xc, weight, adapter_up, (2, 3), (parts,))
-    down_mine = both(rest[rank:] + near[:rank] + after(down_x, grad23), place)
+    grad23, parts, back23 = return_grad(
+        facts, after(cot_x, odd_mid, even_all, down_x), cot_xc, weight, adapter_up, (2, 3), (parts,)
+    )
     back = jnp.concatenate([back01, back23], axis=1)
+    back_near = along(back, 1)
     all_even = jnp.where(away == 0, even, jnp.where(away == 2, even_far, after(even_all, grad23)))
     all_odd = jnp.where(away == 0, odd, jnp.where(away == 2, odd_far, after(odd_all, all_even)))
     all_tokens = jnp.concatenate([all_even, all_odd], axis=0)
-    back = after(back, all_tokens) + along(back, 1)
+    inner_wide, inner_rows, _ = spread(facts, after(inner, all_tokens), inner_far, per_owner, adapter_scale)
+    cots = [([x], 0) for x in (cotangent, cot_c, cot_x, cot_xc)]
+    up_wide = slot_grad(after(inner_wide, inner_rows), cots, hidden // 4)
+    back = after(back, up_wide) + back_near
     back_wide, _, back_b = spread(facts, back, along(back, 2), per_owner, 1.0)
-    inner_wide, inner_rows, _ = spread(facts, after(inner, back_b), inner_far, per_owner, adapter_scale)
-    back_b = share(after(back_b, inner_wide, down_mine), swap(back_b, CORE), CORE)
     parts = lax.all_to_all(after(parts, back_b).reshape(shards, rows, depth), "tp", 0, 0, tiled=True)
+    down_mine = both(rest[rank:] + near[:rank] + after(down_x, back_b), place)
+    back_b = share(back_b, swap(back_b, CORE), CORE)
 
     def grad_block(q):
         low, high = [lax.dynamic_slice_in_dim(x, (q & 1) * rows, rows, 0) for x in (grad01, grad23)]
@@ -390,7 +395,7 @@
 
     point = make(0, back_b)
     back_b = share(after(back_b, point), swap(back_b, CHIP), CHIP)
-    point = make(1, point)
+    point = make(1, point, down_mine)
     point = cross(0, point)
     point = make(2, point, back_b)
     point = finish(0, point)
@@ -405,10 +410,8 @@
         total = total + lax.dynamic_index_in_dim(after(parts, down_wide), j ^ m, 0, False).astype(jnp.float32)
     total = (total + dot(back_mine, down_mine, (0, 0))).astype(b16)
     tokens_grad = both(total, [(b, a) for a, b in place])
-    cots = [([x], 0) for x in (cotangent, cot_c, cot_x, cot_xc)]
     point = cross(3, total)
-    up_wide = slot_grad(after(inner_wide, point), cots, hidden // 4)
-    point = finish(2, up_wide)
+    point = finish(2, point)
     finish(3, point)
     projected = jnp.concatenate(done, axis=1)
     up_grad = up_wide.reshape(per_owner, rank, hidden)

time: 238 us -> 256 us (1.076)
  waiting for transfers between devices: 59.5 us -> 81.8 us
  starting transfers between devices: 44.7 us -> 40.3 us
  local copies, waits for them, and re-layouts: 14.2 us -> 11.3 us
    ppermute x17, waiting for transfers between devices: 11.4 us -> 47.5 us  [swap(): return lax.ppermute(x, 'dp', [(d, d ^ bit) for d in range(groups)])]
    ppermute x17, starting transfers between devices: 20.5 us -> 12.8 us  [swap(): return lax.ppermute(x, 'dp', [(d, d ^ bit) for d in range(groups)])]
    ppermute x4, waiting for transfers between devices: 20.8 us -> 14.3 us  [along(): return lax.ppermute(x, 'tp', [(z, z ^ bit) for z in range(shards)])]
    ppermute x4, starting transfers between devices: 4.34 us -> 8.3 us  [along(): return lax.ppermute(x, 'tp', [(z, z ^ bit) for z in range(shards)])]
    all_to_all x1, waiting for transfers between devices: 3.73 us -> 0.01 us  [local_square(): lax.all_to_all(after(parts, back_b).reshape(shards, rows, depth), 'tp', 0...]
    ppermute x6, waiting for transfers between devices: 23.6 us -> 20.1 us  [both(): return lax.ppermute(x, ('tp', 'dp'), pairs)]
    unnamed x63 -> x55, local copies, waits for them, and re-layouts: 14.2 us -> 11.2 us
  transfers between devices with their start and end apart: 28 -> 28, of which waited for: 9 -> 13; matrix products, arithmetic and copies ran while one was open for 11% -> 11% of each run, Pallas kernels for 35% -> 32%
where the time goes in v12:
time: 256 us; the launch traced here: 254 us
  Pallas kernels  92.7 us (36%)
  waiting for transfers between devices  81.8 us (32%)
  starting transfers between devices  40.3 us (16%)
  other arithmetic  24.1 us (9%)
  local copies, waits for them, and re-layouts  11.3 us (4%)
  matrix products  2.61 us (1%)
    ppermute x17, waiting for transfers between devices, swap(): return lax.ppermute(x, 'dp', [(d, d ^ bit) for d in range(groups)])  47.5 us
    pallas_call x2, Pallas kernels, return_grad(): pl.pallas_call(kernel, grid_spec=pltpu.PrefetchScalarGridSpec(num_scalar_...  38.9 us
    pallas_call x4, Pallas kernels, project(): pl.pallas_call(kernel, grid=((stop - start) // block,), in_specs=[pl.Bloc...  34 us
    ppermute x6, waiting for transfers between devices, both(): return lax.ppermute(x, ('tp', 'dp'), pairs)  20.1 us
    ppermute x6, starting transfers between devices, both(): return lax.ppermute(x, ('tp', 'dp'), pairs)  14.4 us
    ppermute x4, waiting for transfers between devices, along(): return lax.ppermute(x, 'tp', [(z, z ^ bit) for z in range(shards)])  14.3 us
    pallas_call x2, Pallas kernels, slot_grad(): pl.pallas_call(kernel, grid=(columns // block,), in_specs=[pl.BlockSpec((...  13.3 us
    ppermute x17, starting transfers between devices, swap(): return lax.ppermute(x, 'dp', [(d, d ^ bit) for d in range(groups)])  12.8 us
  transfers between devices with their start and end apart: 28, of which 13 were waited for; matrix products, arithmetic and copies ran while one was open for 11% of the time, Pallas kernels for 32%

profile of v12, /device:TPU:2, one launch (start us, length us, event | category | flops | bytes accessed | tf_op | source)
XLA Modules:
  0.0 253.9 jit_solution(18040614133416224631)
XLA Ops:
  0.9 1.6 copy-done.6
  2.5 0.7 copy-done.17
  3.1 0.7 copy-done.18
  3.8 0.7 copy-done.19
  4.4 1.5 choose.1
  6.0 9.3 %collective-permute-done = bf16[128,2048]{1,0:T(8,128)(2,1)S(1)} collective-permute-done((bf16[128,2048]{1,0:T(8,128)(2,1)}, bf16[128,2048]{1,0:T(8,128)(2,1)S(1)}, u32[]{:S(2)}, u32[]{:S(2)}) %collective-permute-start) | collective-permute-done | bytes 524320 | tf_op jit(solution)/shard_map/ppermute | solution.py:311
  15.4 1.3 collective-permute-start.1
  16.7 4.7 %collective-permute-start.5 = (bf16[128,7168]{1,0:T(8,128)(2,1)}, bf16[128,7168]{1,0:T(8,128)(2,1)}, u32[]{:S(2)}, u32[]{:S(2)}) collective-permute-start(bf16[128,7168]{1,0:T(8,128)(2,1)} %refs_0_.1), channel_id=1, source_target_pairs={{0,2},{1,3},{2,0},{3,1},{4,6},{5,7},{6,4},{7,5},{8,10},{9,11},{10,... | collective-permute-start | bytes 5505032 | tf_op jit(solution)/shard_map/ppermute | solution.py:311
  21.4 19.5 %return_grad.2 = (f32[256,2048]{1,0:T(8,128)S(1)}, bf16[512,2048]{1,0:T(8,128)(2,1)}, f32[64,256]{1,0:T(8,128)S(1)}) custom-call(s32[9]{0:T(128)S(1)} %get-tuple-element.60.facts_ref, bf16[128,7168]{1,0:T(8,128)(2,1)} %refs_0_.1, bf16[128,7168]{1,0:T(8,128)(2,1)} %collective-permute-done.2.b_ref.refs_1_, bf16[2048,7168]{1,0:T(8,128)(2,1)} %w_ref.11, ...), custom_call_target="tpu_custom_call" | custom-call | flops 117440512 | bytes 516096 | tf_op jit(solution)/shard_map/return_grad/pallas_call | solution.py:88
  40.9 1.4 copy-done.13
  42.3 1.8 rank_inner.1
  44.3 1.3 collective-permute-start.6
  45.6 2.3 broadcast_select_fusion.1
  47.9 1.0 slice_add_fusion.9
  48.9 10.9 %collective-permute-done.5.a_ref.refs_2_ = bf16[128,7168]{1,0:T(8,128)(2,1)} collective-permute-done((bf16[128,7168]{1,0:T(8,128)(2,1)}, bf16[128,7168]{1,0:T(8,128)(2,1)}, u32[]{:S(2)}, u32[]{:S(2)}) %collective-permute-start.5) | collective-permute-done | bytes 1835040 | tf_op jit(solution)/shard_map/ppermute | solution.py:311
  59.8 1.9 collective-permute-start.7
  61.6 3.0 %collective-permute-start.4 = (bf16[256,2048]{1,0:T(8,128)(2,1)}, bf16[256,2048]{1,0:T(8,128)(2,1)}, u32[]{:S(2)}, u32[]{:S(2)}) collective-permute-start(bf16[256,2048]{1,0:T(8,128)(2,1)} %broadcast_select_fusion.1), channel_id=1, source_target_pairs={{0,4},{8,12},{5,1},{13,9},{10,14},{2,6},{15,11},{7,3},{16,20},{24,... | collective-permute-start | bytes 3145736 | tf_op jit(solution)/shard_map/ppermute | solution.py:324
  64.7 11.3 %collective-permute-done.7 = f32[64,512]{1,0:T(8,128)S(1)} collective-permute-done((f32[64,512]{1,0:T(8,128)S(1)}, f32[64,512]{1,0:T(8,128)S(1)}, u32[]{:S(2)}, u32[]{:S(2)}) %collective-permute-start.7) | collective-permute-done | bytes 131104 | tf_op jit(solution)/shard_map/ppermute | solution.py:314
  76.0 1.0 copy-done.20
  77.0 1.1 broadcast_select_fusion
  78.1 2.4 collective-permute-start.11
  80.5 3.5 %collective-permute-start.12 = (f32[64,512]{1,0:T(8,128)S(1)}, f32[64,512]{1,0:T(8,128)S(1)}, u32[]{:S(2)}, u32[]{:S(2)}) collective-permute-start(f32[64,512]{1,0:T(8,128)S(1)} %add.86.refs_0_), channel_id=1, source_target_pairs={{0,8},{4,12},{8,0},{12,4},{1,9},{5,13},{9,1},{13,5},{2,10},{6,14},... | collective-permute-start | bytes 393224 | tf_op jit(solution)/shard_map/ppermute | solution.py:314
  84.0 3.7 %collective-permute-done.9 = bf16[64,2048]{1,0:T(8,128)(2,1)S(1)} collective-permute-done((bf16[64,2048]{1,0:T(8,128)(2,1)S(1)}, bf16[64,2048]{1,0:T(8,128)(2,1)S(1)}, u32[]{:S(2)}, u32[]{:S(2)}) %collective-permute-start.9) | collective-permute-done | bytes 262176 | tf_op jit(solution)/shard_map/ppermute | solution.py:311
  87.7 19.4 %return_grad.3 = (f32[256,2048]{1,0:T(8,128)S(1)}, bf16[512,2048]{1,0:T(8,128)(2,1)}, f32[64,256]{1,0:T(8,128)S(1)}) custom-call(s32[9]{0:T(128)S(1)} %get-tuple-element.60.facts_ref, bf16[128,7168]{1,0:T(8,128)(2,1)} %collective-permute-done.5.a_ref.refs_2_, ...), custom_call_target="tpu_custom_call", output_to_operand_aliasing={{1}: (6, {})} | custom-call | flops 117440512 | bytes 516096 | tf_op jit(solution)/shard_map/return_grad/pallas_call | solution.py:88
  107.1 2.2 select_select_fusion.1
  109.7 1.6 pad_maximum_fusion.tok_ref
  111.2 1.4 spread.2
  112.6 10.4 %slot_grad.2 = f32[512,7168]{1,0:T(8,128)} custom-call(bf16[512,512]{1,0:T(8,128)(2,1)S(1)} %get-tuple-element.86.wide_ref, bf16[128,7168]{1,0:T(8,128)(2,1)} %refs_0_.1, bf16[128,7168]{1,0:T(8,128)(2,1)} %collective-permute-done.2.b_ref.refs_1_, bf16[128,7168]{1,0:T(8,128)(2,1)} %collective-permute-done.5.a_ref.refs_2_, ...), custom_call_target="tpu_custom_call" | custom-call | flops 3758096384 | bytes 22020096 | tf_op jit(solution)/shard_map/slot_grad/pallas_call | solution.py:212
  123.1 2.9 %collective-permute-start.14 = (f32[64,512]{1,0:T(8,128)S(1)}, f32[64,512]{1,0:T(8,128)S(1)}, u32[]{:S(2)}, u32[]{:S(2)}) collective-permute-start(f32[64,512]{1,0:T(8,128)S(1)} %add.88.refs_0_), channel_id=1, source_target_pairs={{0,8},{4,12},{8,0},{12,4},{1,9},{5,13},{9,1},{13,5},{2,10},{6,14},... | collective-permute-start | bytes 393224 | tf_op jit(solution)/shard_map/ppermute | solution.py:314
  126.0 3.0 %collective-permute-done.14.refs_1_ = f32[64,512]{1,0:T(8,128)S(1)} collective-permute-done((f32[64,512]{1,0:T(8,128)S(1)}, f32[64,512]{1,0:T(8,128)S(1)}, u32[]{:S(2)}, u32[]{:S(2)}) %collective-permute-start.14) | collective-permute-done | bytes 131104 | tf_op jit(solution)/shard_map/ppermute | solution.py:314
  129.0 1.7 spread.3
  130.7 0.8 copy-done.15
  131.5 4.8 %collective-permute-start.15 = (bf16[64,512]{1,0:T(8,128)(2,1)S(1)}, bf16[64,512]{1,0:T(8,128)(2,1)S(1)}, u32[]{:S(2)}, u32[]{:S(2)}) collective-permute-start(bf16[64,512]{1,0:T(8,128)(2,1)S(1)} %get-tuple-element.88), channel_id=1, source_target_pairs={{0,1},{1,0},{2,3},{3,2},{4,5},{5,4},{6,7},{7,6},{8,9},{9,8},{10,11... | collective-permute-start | bytes 196616 | tf_op jit(solution)/shard_map/ppermute | solution.py:311
  136.3 0.9 collective-permute-done.15
  137.3 9.9 %project.4 = (f32[256,2048]{1,0:T(8,128)S(1)}, f32[256,2048]{1,0:T(8,128)}) custom-call(bf16[512,2048]{1,0:T(8,128)(2,1)} %pad_maximum_fusion.tok_ref, bf16[512,512]{1,0:T(8,128)(2,1)S(1)} %get-tuple-element.85.wide_ref, bf16[2048,7168]{1,0:T(8,128)(2,1)} %w_ref.11, bf16[512,7168]{1,0:T(8,128)(2,1)} %bitcast.23), custom_call_target="tpu_custom_call" | custom-call | flops 83886080 | bytes 229376 | tf_op jit(solution)/shard_map/project/pallas_call | solution.py:39
  147.1 1.3 copy-done.8
  148.8 1.7 fusion.13
  150.5 4.5 %collective-permute-start.16 = (bf16[64,2048]{1,0:T(8,128)(2,1)}, bf16[64,2048]{1,0:T(8,128)(2,1)S(1)}, u32[]{:S(2)}, u32[]{:S(2)}) collective-permute-start(bf16[64,2048]{1,0:T(8,128)(2,1)} %fusion.13), channel_id=1, source_target_pairs={{0,0},{4,5},{8,10},{12,15},{1,4},{5,1},{9,14},{13,11},{2,8},{6,13}... | collective-permute-start | bytes 786440 | tf_op jit(solution)/shard_map/ppermute | solution.py:324
  155.0 4.8 %all-to-all-start = ((bf16[4,128,2048]{2,1,0:T(8,128)(2,1)}), bf16[4,128,2048]{2,1,0:T(8,128)(2,1)}, u32[]{:S(2)}, u32[]{:S(2)}) async-start(bf16[4,128,2048]{2,1,0:T(8,128)(2,1)} %bitcast.28), calls=%async_computation | async-start | bytes 4194304 | tf_op jit(solution)/shard_map/all_to_all | solution.py:366
  159.9 19.5 %collective-permute-done.16 = bf16[64,2048]{1,0:T(8,128)(2,1)S(1)} collective-permute-done((bf16[64,2048]{1,0:T(8,128)(2,1)}, bf16[64,2048]{1,0:T(8,128)(2,1)S(1)}, u32[]{:S(2)}, u32[]{:S(2)}) %collective-permute-start.16) | collective-permute-done | bytes 262176 | tf_op jit(solution)/shard_map/ppermute | solution.py:324
  179.4 1.0 copy-done.5
  180.4 6.7 %project.5 = (f32[256,1536]{1,0:T(8,128)S(1)}, f32[256,1536]{1,0:T(8,128)S(1)}) custom-call(bf16[512,2048]{1,0:T(8,128)(2,1)S(1)} %copy-done, bf16[512,512]{1,0:T(8,128)(2,1)S(1)} %copy-done.5, bf16[2048,7168]{1,0:T(8,128)(2,1)} %w_ref.11, bf16[512,7168]{1,0:T(8,128)(2,1)} %bitcast.24), custom_call_target="tpu_custom_call" | custom-call | flops 62914560 | bytes 172032 | tf_op jit(solution)/shard_map/project/pallas_call | solution.py:39
  187.2 1.8 fusion.6
  189.2 0.6 maximum_add_fusion.1
  189.8 9.9 %project.6 = (f32[256,2048]{1,0:T(8,128)S(1)}, f32[256,2048]{1,0:T(8,128)}) custom-call(bf16[512,2048]{1,0:T(8,128)(2,1)} %pad_maximum_fusion.tok_ref, bf16[512,512]{1,0:T(8,128)(2,1)S(1)} %copy-done.5, bf16[2048,7168]{1,0:T(8,128)(2,1)} %w_ref.11, bf16[512,7168]{1,0:T(8,128)(2,1)} %bitcast.25), custom_call_target="tpu_custom_call" | custom-call | flops 83886080 | bytes 229376 | tf_op jit(solution)/shard_map/project/pallas_call | solution.py:39
  199.7 3.2 %collective-permute-done.19 = bf16[128,2048]{1,0:T(8,128)(2,1)S(1)} collective-permute-done((bf16[128,2048]{1,0:T(8,128)(2,1)S(1)}, bf16[128,2048]{1,0:T(8,128)(2,1)S(1)}, u32[]{:S(2)}, u32[]{:S(2)}) %collective-permute-start.19) | collective-permute-done | bytes 524320 | tf_op jit(solution)/shard_map/ppermute | solution.py:311
  203.0 2.2 fusion.5
  205.6 7.6 %project.7 = (f32[256,1536]{1,0:T(8,128)S(1)}, f32[256,1536]{1,0:T(8,128)}) custom-call(bf16[512,2048]{1,0:T(8,128)(2,1)S(1)} %copy-done.1, bf16[512,512]{1,0:T(8,128)(2,1)S(1)} %copy-done.5, bf16[2048,7168]{1,0:T(8,128)(2,1)} %w_ref.11, bf16[512,7168]{1,0:T(8,128)(2,1)} %bitcast.26), custom_call_target="tpu_custom_call" | custom-call | flops 62914560 | bytes 172032 | tf_op jit(solution)/shard_map/project/pallas_call | solution.py:39
  213.2 1.2 copy-done.10
  214.3 1.4 collective-permute-done.21
  215.7 1.6 fusion.11
  217.3 2.1 fusion.3
  219.5 0.7 collective-permute-start.24
  220.2 2.9 %slot_grad.3 = f32[512,2048]{1,0:T(8,128)} custom-call(bf16[512,512]{1,0:T(8,128)(2,1)S(1)} %copy-done.16, bf16[256,2048]{1,0:T(8,128)(2,1)S(1)} %constant_dynamic-update-slice_fusion.refs_0_.refs_2_, bf16[256,2048]{1,0:T(8,128)(2,1)S(1)} %copy-done.3, bf16[256,2048]{1,0:T(8,128)(2,1)S(1)} %constant_dynamic-update-slice_fusion.refs_0_.refs_2_, ...), custom_call_target="tpu_custom_call" | custom-call | flops 1073741824 | bytes 6291456 | tf_op jit(solution)/shard_map/slot_grad/pallas_call | solution.py:212
  223.1 2.6 %fusion = bf16[128,2048]{1,0:T(8,128)(2,1)S(1)} fusion(bf16[64,2048]{1,0:T(8,128)(2,1)} %copy-done.25, f32[256,2048]{1,0:T(8,128)} %copy-done.14, s32[]{:T(128)S(6)} %select_n.64, f32[256,2048]{1,0:T(8,128)} %copy-done.13, bf16[4,128,2048]{2,1,0:T(8,128)(2,1)} %all-to-all-done, s32[]{:T(128)S(6)} %select_n.68, s32[]{:T(128)S(6)} %select_n.67, ...), kind=kOutput, calls=%fused_computation.1 | convolution fusion | flops 35913728 | bytes 4472853 | tf_op jit(solution)/shard_map/dot_general | solution.py:18
  225.8 1.3 fusion.9
  227.0 1.4 collective-permute-start.25
  228.4 1.9 collective-permute-start.26
  230.3 4.3 %collective-permute-done.24 = bf16[128,2048]{1,0:T(8,128)(2,1)} collective-permute-done((bf16[128,2048]{1,0:T(8,128)(2,1)}, bf16[128,2048]{1,0:T(8,128)(2,1)}, u32[]{:S(2)}, u32[]{:S(2)}) %collective-permute-start.24) | collective-permute-done | bytes 524320 | tf_op jit(solution)/shard_map/ppermute | solution.py:311
  234.6 1.5 fusion.2
  236.2 13.8 %collective-permute-done.25 = bf16[128,1536]{1,0:T(8,128)(2,1)S(1)} collective-permute-done((bf16[128,1536]{1,0:T(8,128)(2,1)S(1)}, bf16[128,1536]{1,0:T(8,128)(2,1)S(1)}, u32[]{:S(2)}, u32[]{:S(2)}) %collective-permute-start.25) | collective-permute-done | bytes 393248 | tf_op jit(solution)/shard_map/ppermute | solution.py:311
  250.0 1.3 fusion.8
  251.3 1.4 pad_maximum_fusion.1
  253.1 0.8 copy.17
  (85 shorter events, 2.6 us)
Async XLA Ops:
  0.6 20.8 %collective-permute-start.2 = (bf16[128,7168]{1,0:T(8,128)(2,1)}, bf16[128,7168]{1,0:T(8,128)(2,1)}, u32[]{:S(2)}, u32[]{:S(2)}) collective-permute-start(bf16[128,7168]{1,0:T(8,128)(2,1)} %refs_0_.1), channel_id=1, source_target_pairs={{0,1},{1,0},{2,3},{3,2},{4,5},{5,4},{6,7},{7,6},{8,9},{9,8},{10,11... | collective-permute-start | bytes 5505032 | tf_op jit(solution)/shard_map/ppermute | solution.py:311
  0.7 14.5 %collective-permute-start = (bf16[128,2048]{1,0:T(8,128)(2,1)}, bf16[128,2048]{1,0:T(8,128)(2,1)S(1)}, u32[]{:S(2)}, u32[]{:S(2)}) collective-permute-start(bf16[128,2048]{1,0:T(8,128)(2,1)} %param.8), channel_id=1, source_target_pairs={{0,2},{1,3},{2,0},{3,1},{4,6},{5,7},{6,4},{7,5},{8,10},{9,11},{10,... | collective-permute-start | bytes 1572872 | tf_op jit(solution)/shard_map/ppermute | solution.py:311
  0.9 1.6 copy-start.6
  2.5 0.7 copy-start.17
  3.1 0.7 copy-start.18
  3.8 0.7 copy-start.19
  4.4 1.5 copy-start.24
  15.3 27.0 %collective-permute-start.3 = (bf16[256,2048]{1,0:T(8,128)(2,1)S(1)}, bf16[256,2048]{1,0:T(8,128)(2,1)S(1)}, u32[]{:S(2)}, u32[]{:S(2)}) collective-permute-start(bf16[256,2048]{1,0:T(8,128)(2,1)S(1)} %constant_dynamic-update-slice_fusion.refs_0_.refs_2_), channel_id=1, source_target_pairs={{0,1},{1,0},{2,3},{3,2},{4,5},{5,4},{6,7},{7,6},{8,9},{9,8},{10,11... | collective-permute-start | bytes 3145736 | tf_op jit(solution)/shard_map/ppermute | solution.py:311
  15.4 28.9 %collective-permute-start.1 = (bf16[256,2048]{1,0:T(8,128)(2,1)S(1)}, bf16[256,2048]{1,0:T(8,128)(2,1)}, u32[]{:S(2)}, u32[]{:S(2)}) collective-permute-start(bf16[256,2048]{1,0:T(8,128)(2,1)S(1)} %constant_dynamic-update-slice_fusion.refs_0_.refs_2_), channel_id=1, source_target_pairs={{0,8},{5,13},{10,2},{15,7},{16,24},{21,29},{26,18},{31,23}} | collective-permute-start | bytes 3145736 | tf_op jit(solution)/shard_map/ppermute | solution.py:324
  16.7 43.1 %collective-permute-start.5 = (bf16[128,7168]{1,0:T(8,128)(2,1)}, bf16[128,7168]{1,0:T(8,128)(2,1)}, u32[]{:S(2)}, u32[]{:S(2)}) collective-permute-start(bf16[128,7168]{1,0:T(8,128)(2,1)} %refs_0_.1), channel_id=1, source_target_pairs={{0,2},{1,3},{2,0},{3,1},{4,6},{5,7},{6,4},{7,5},{8,10},{9,11},{10,... | collective-permute-start | bytes 5505032 | tf_op jit(solution)/shard_map/ppermute | solution.py:311
  21.4 22.7 %collective-permute-start.8 = (bf16[128,2048]{1,0:T(8,128)(2,1)S(1)}, bf16[128,2048]{1,0:T(8,128)(2,1)}, u32[]{:S(2)}, u32[]{:S(2)}) collective-permute-start(bf16[128,2048]{1,0:T(8,128)(2,1)S(1)} %get-tuple-element.72), channel_id=1, source_target_pairs={{0,1},{1,0},{2,3},{3,2},{4,5},{5,4},{6,7},{7,6},{8,9},{9,8},{10,11... | collective-permute-start | bytes 1572872 | tf_op jit(solution)/shard_map/ppermute | solution.py:311
  21.4 20.9 %copy-start.7 = (bf16[8,2048,64]{1,2,0:T(8,128)(2,1)S(1)}, bf16[8,2048,64]{1,2,0:T(8,128)(2,1)}, u32[]{:S(2)}) copy-start(bf16[8,2048,64]{1,2,0:T(8,128)(2,1)} %param.10) | copy-start | bytes 6291460
  40.9 1.4 copy-start.13
  42.3 67.0 %copy-start.2 = (bf16[256,2048]{1,0:T(8,128)(2,1)}, bf16[256,2048]{1,0:T(8,128)(2,1)S(1)}, u32[]{:S(2)}) copy-start(bf16[256,2048]{1,0:T(8,128)(2,1)S(1)} %collective-permute-done.3.refs_1_.refs_3_) | copy-start | bytes 3145732
  44.3 31.7 %collective-permute-start.6 = (bf16[256,2048]{1,0:T(8,128)(2,1)S(1)}, bf16[256,2048]{1,0:T(8,128)(2,1)S(1)}, u32[]{:S(2)}, u32[]{:S(2)}) collective-permute-start(bf16[256,2048]{1,0:T(8,128)(2,1)S(1)} %collective-permute-done.3.refs_1_.refs_3_), channel_id=1, source_target_pairs={{0,8},{5,13},{10,2},{15,7},{16,24},{21,29},{26,18},{31,23}} | collective-permute-start | bytes 3145736 | tf_op jit(solution)/shard_map/ppermute | solution.py:324
  59.8 27.9 %collective-permute-start.10 = (bf16[128,7168]{1,0:T(8,128)(2,1)}, bf16[128,7168]{1,0:T(8,128)(2,1)}, u32[]{:S(2)}, u32[]{:S(2)}) collective-permute-start(bf16[128,7168]{1,0:T(8,128)(2,1)} %collective-permute-done.5.a_ref.refs_2_), channel_id=1, source_target_pairs={{0,1},{1,0},{2,3},{3,2},{4,5},{5,4},{6,7},{7,6},{8,9},{9,8},{10,11... | collective-permute-start | bytes 5505032 | tf_op jit(solution)/shard_map/ppermute | solution.py:311
  59.8 16.2 %collective-permute-start.7 = (f32[64,512]{1,0:T(8,128)S(1)}, f32[64,512]{1,0:T(8,128)S(1)}, u32[]{:S(2)}, u32[]{:S(2)}) collective-permute-start(f32[64,512]{1,0:T(8,128)S(1)} %rank_inner.1), channel_id=1, source_target_pairs={{0,4},{4,0},{8,12},{12,8},{1,5},{5,1},{9,13},{13,9},{2,6},{6,2},{1... | collective-permute-start | bytes 393224 | tf_op jit(solution)/shard_map/ppermute | solution.py:314
  61.6 26.0 %collective-permute-start.4 = (bf16[256,2048]{1,0:T(8,128)(2,1)}, bf16[256,2048]{1,0:T(8,128)(2,1)}, u32[]{:S(2)}, u32[]{:S(2)}) collective-permute-start(bf16[256,2048]{1,0:T(8,128)(2,1)} %broadcast_select_fusion.1), channel_id=1, source_target_pairs={{0,4},{8,12},{5,1},{13,9},{10,14},{2,6},{15,11},{7,3},{16,20},{24,... | collective-permute-start | bytes 3145736 | tf_op jit(solution)/shard_map/ppermute | solution.py:324
  76.0 1.0 copy-start.20
  78.1 31.2 %collective-permute-start.11 = (bf16[256,2048]{1,0:T(8,128)(2,1)}, bf16[256,2048]{1,0:T(8,128)(2,1)}, u32[]{:S(2)}, u32[]{:S(2)}) collective-permute-start(bf16[256,2048]{1,0:T(8,128)(2,1)} %broadcast_select_fusion), channel_id=1, source_target_pairs={{0,4},{8,12},{5,1},{13,9},{10,14},{2,6},{15,11},{7,3},{16,20},{24,... | collective-permute-start | bytes 3145736 | tf_op jit(solution)/shard_map/ppermute | solution.py:324
  80.5 7.2 %collective-permute-start.9 = (bf16[64,2048]{1,0:T(8,128)(2,1)S(1)}, bf16[64,2048]{1,0:T(8,128)(2,1)S(1)}, u32[]{:S(2)}, u32[]{:S(2)}) collective-permute-start(bf16[64,2048]{1,0:T(8,128)(2,1)S(1)} %slice_add_fusion.9), channel_id=1, source_target_pairs={{0,2},{1,3},{2,0},{3,1},{4,6},{5,7},{6,4},{7,5},{8,10},{9,11},{10,... | collective-permute-start | bytes 786440 | tf_op jit(solution)/shard_map/ppermute | solution.py:311
  80.5 30.7 %collective-permute-start.12 = (f32[64,512]{1,0:T(8,128)S(1)}, f32[64,512]{1,0:T(8,128)S(1)}, u32[]{:S(2)}, u32[]{:S(2)}) collective-permute-start(f32[64,512]{1,0:T(8,128)S(1)} %add.86.refs_0_), channel_id=1, source_target_pairs={{0,8},{4,12},{8,0},{12,4},{1,9},{5,13},{9,1},{13,5},{2,10},{6,14},... | collective-permute-start | bytes 393224 | tf_op jit(solution)/shard_map/ppermute | solution.py:314
  107.1 2.2 copy-start.14
  107.1 2.3 copy-start.21
  111.2 11.8 %collective-permute-start.13 = (f32[64,512]{1,0:T(8,128)S(1)}, f32[64,512]{1,0:T(8,128)S(1)}, u32[]{:S(2)}, u32[]{:S(2)}) collective-permute-start(f32[64,512]{1,0:T(8,128)S(1)} %constant_dynamic-update-slice_fusion.2), channel_id=1, source_target_pairs={{0,4},{4,0},{8,12},{12,8},{1,5},{5,1},{9,13},{13,9},{2,6},{6,2},{1... | collective-permute-start | bytes 393224 | tf_op jit(solution)/shard_map/ppermute | solution.py:314
  112.6 24.6 %copy-start.4 = (bf16[512,512]{1,0:T(8,128)(2,1)}, bf16[512,512]{1,0:T(8,128)(2,1)S(1)}, u32[]{:S(2)}) copy-start(bf16[512,512]{1,0:T(8,128)(2,1)S(1)} %get-tuple-element.85.wide_ref) | copy-start | bytes 1572868
  123.1 5.9 %collective-permute-start.14 = (f32[64,512]{1,0:T(8,128)S(1)}, f32[64,512]{1,0:T(8,128)S(1)}, u32[]{:S(2)}, u32[]{:S(2)}) collective-permute-start(f32[64,512]{1,0:T(8,128)S(1)} %add.88.refs_0_), channel_id=1, source_target_pairs={{0,8},{4,12},{8,0},{12,4},{1,9},{5,13},{9,1},{13,5},{2,10},{6,14},... | collective-permute-start | bytes 393224 | tf_op jit(solution)/shard_map/ppermute | solution.py:314
  130.7 0.9 copy-start.15
  131.5 5.7 %collective-permute-start.15 = (bf16[64,512]{1,0:T(8,128)(2,1)S(1)}, bf16[64,512]{1,0:T(8,128)(2,1)S(1)}, u32[]{:S(2)}, u32[]{:S(2)}) collective-permute-start(bf16[64,512]{1,0:T(8,128)(2,1)S(1)} %get-tuple-element.88), channel_id=1, source_target_pairs={{0,1},{1,0},{2,3},{3,2},{4,5},{5,4},{6,7},{7,6},{8,9},{9,8},{10,11... | collective-permute-start | bytes 196616 | tf_op jit(solution)/shard_map/ppermute | solution.py:311
  147.1 1.3 copy-start.8
  148.4 38.8 %collective-permute-start.17 = (f32[256,2048]{1,0:T(8,128)}, f32[256,2048]{1,0:T(8,128)}, u32[]{:S(2)}, u32[]{:S(2)}) collective-permute-start(f32[256,2048]{1,0:T(8,128)} %get-tuple-element.95), channel_id=1, source_target_pairs={{0,1},{1,0},{2,3},{3,2},{4,5},{5,4},{6,7},{7,6},{8,9},{9,8},{10,11... | collective-permute-start | bytes 6291464 | tf_op jit(solution)/shard_map/ppermute | solution.py:311
  150.5 28.9 %collective-permute-start.16 = (bf16[64,2048]{1,0:T(8,128)(2,1)}, bf16[64,2048]{1,0:T(8,128)(2,1)S(1)}, u32[]{:S(2)}, u32[]{:S(2)}) collective-permute-start(bf16[64,2048]{1,0:T(8,128)(2,1)} %fusion.13), channel_id=1, source_target_pairs={{0,0},{4,5},{8,10},{12,15},{1,4},{5,1},{9,14},{13,11},{2,8},{6,13}... | collective-permute-start | bytes 786440 | tf_op jit(solution)/shard_map/ppermute | solution.py:324
  155.0 24.4 %copy-start = (bf16[512,2048]{1,0:T(8,128)(2,1)S(1)}, bf16[512,2048]{1,0:T(8,128)(2,1)}, u32[]{:S(2)}) copy-start(bf16[512,2048]{1,0:T(8,128)(2,1)} %pad_maximum_fusion.tok_ref) | copy-start | bytes 6291460
  155.0 68.1 %all-to-all-start = ((bf16[4,128,2048]{2,1,0:T(8,128)(2,1)}), bf16[4,128,2048]{2,1,0:T(8,128)(2,1)}, u32[]{:S(2)}, u32[]{:S(2)}) async-start(bf16[4,128,2048]{2,1,0:T(8,128)(2,1)} %bitcast.28), calls=%async_computation | async-start | bytes 4194304 | tf_op jit(solution)/shard_map/all_to_all | solution.py:366
  159.8 29.3 %collective-permute-start.18 = (bf16[64,512]{1,0:T(8,128)(2,1)S(1)}, bf16[64,512]{1,0:T(8,128)(2,1)S(1)}, u32[]{:S(2)}, u32[]{:S(2)}) collective-permute-start(bf16[64,512]{1,0:T(8,128)(2,1)S(1)} %maximum_add_fusion), channel_id=1, source_target_pairs={{0,2},{1,3},{2,0},{3,1},{4,6},{5,7},{6,4},{7,5},{8,10},{9,11},{10,... | collective-permute-start | bytes 196616 | tf_op jit(solution)/shard_map/ppermute | solution.py:311
  179.4 1.0 copy-start.5
  180.4 6.7 %copy-start.25 = (bf16[64,2048]{1,0:T(8,128)(2,1)}, bf16[64,2048]{1,0:T(8,128)(2,1)S(1)}, u32[]{:S(2)}) copy-start(bf16[64,2048]{1,0:T(8,128)(2,1)S(1)} %collective-permute-done.16) | copy-start | bytes 786436
  180.4 6.8 %copy-start.9 = (f32[256,2048]{1,0:T(8,128)S(1)}, f32[256,2048]{1,0:T(8,128)}, u32[]{:S(2)}) copy-start(f32[256,2048]{1,0:T(8,128)} %copy-done.8) | copy-start | bytes 6291460
  187.1 18.0 %copy-start.12 = (f32[256,1536]{1,0:T(8,128)}, f32[256,1536]{1,0:T(8,128)S(1)}, u32[]{:S(2)}) copy-start(f32[256,1536]{1,0:T(8,128)S(1)} %get-tuple-element.104) | copy-start | bytes 4718596
  187.1 18.0 %collective-permute-start.20 = (f32[256,1536]{1,0:T(8,128)S(1)}, f32[256,1536]{1,0:T(8,128)S(1)}, u32[]{:S(2)}, u32[]{:S(2)}) collective-permute-start(f32[256,1536]{1,0:T(8,128)S(1)} %get-tuple-element.101), channel_id=1, source_target_pairs={{0,1},{1,0},{2,3},{3,2},{4,5},{5,4},{6,7},{7,6},{8,9},{9,8},{10,11... | collective-permute-start | bytes 4718600 | tf_op jit(solution)/shard_map/ppermute | solution.py:311
  189.1 13.9 %collective-permute-start.19 = (bf16[128,2048]{1,0:T(8,128)(2,1)S(1)}, bf16[128,2048]{1,0:T(8,128)(2,1)S(1)}, u32[]{:S(2)}, u32[]{:S(2)}) collective-permute-start(bf16[128,2048]{1,0:T(8,128)(2,1)S(1)} %fusion.6), channel_id=1, source_target_pairs={{0,2},{1,3},{2,0},{3,1},{4,6},{5,7},{6,4},{7,5},{8,10},{9,11},{10,... | collective-permute-start | bytes 1572872 | tf_op jit(solution)/shard_map/ppermute | solution.py:311
  199.7 17.6 %collective-permute-start.22 = (f32[256,2048]{1,0:T(8,128)}, f32[256,2048]{1,0:T(8,128)}, u32[]{:S(2)}, u32[]{:S(2)}) collective-permute-start(f32[256,2048]{1,0:T(8,128)} %get-tuple-element.109), channel_id=1, source_target_pairs={{0,1},{1,0},{2,3},{3,2},{4,5},{5,4},{6,7},{7,6},{8,9},{9,8},{10,11... | collective-permute-start | bytes 6291464 | tf_op jit(solution)/shard_map/ppermute | solution.py:311
  199.7 5.9 %copy-start.1 = (bf16[512,2048]{1,0:T(8,128)(2,1)S(1)}, bf16[512,2048]{1,0:T(8,128)(2,1)}, u32[]{:S(2)}) copy-start(bf16[512,2048]{1,0:T(8,128)(2,1)} %pad_maximum_fusion.tok_ref) | copy-start | bytes 6291460
  205.2 8.0 %copy-start.23 = (f32[256,1536]{1,0:T(8,128)}, f32[256,1536]{1,0:T(8,128)S(1)}, u32[]{:S(2)}) copy-start(f32[256,1536]{1,0:T(8,128)S(1)} %collective-permute-done.20) | copy-start | bytes 4718596
  205.3 10.5 %collective-permute-start.21 = (bf16[128,1536]{1,0:T(8,128)(2,1)S(1)}, bf16[128,1536]{1,0:T(8,128)(2,1)}, u32[]{:S(2)}, u32[]{:S(2)}) collective-permute-start(bf16[128,1536]{1,0:T(8,128)(2,1)S(1)} %fusion.12), channel_id=1, source_target_pairs={{0,2},{1,3},{2,0},{3,1},{4,6},{5,7},{6,4},{7,5},{8,10},{9,11},{10,... | collective-permute-start | bytes 1179656 | tf_op jit(solution)/shard_map/ppermute | solution.py:311
  213.2 1.2 copy-start.10
  214.3 11.4 %collective-permute-start.23 = (f32[256,1536]{1,0:T(8,128)}, f32[256,1536]{1,0:T(8,128)}, u32[]{:S(2)}, u32[]{:S(2)}) collective-permute-start(f32[256,1536]{1,0:T(8,128)} %get-tuple-element.113), channel_id=1, source_target_pairs={{0,1},{1,0},{2,3},{3,2},{4,5},{5,4},{6,7},{7,6},{8,9},{9,8},{10,11... | collective-permute-start | bytes 4718600 | tf_op jit(solution)/shard_map/ppermute | solution.py:311
  214.3 5.9 %copy-start.3 = (bf16[256,2048]{1,0:T(8,128)(2,1)S(1)}, bf16[256,2048]{1,0:T(8,128)(2,1)}, u32[]{:S(2)}) copy-start(bf16[256,2048]{1,0:T(8,128)(2,1)} %copy-done.2) | copy-start | bytes 3145732
  214.3 5.9 %copy-start.16 = (bf16[512,512]{1,0:T(8,128)(2,1)S(1)}, bf16[512,512]{1,0:T(8,128)(2,1)}, u32[]{:S(2)}) copy-start(bf16[512,512]{1,0:T(8,128)(2,1)} %copy-done.15) | copy-start | bytes 1572868
  219.5 15.2 %collective-permute-start.24 = (bf16[128,2048]{1,0:T(8,128)(2,1)}, bf16[128,2048]{1,0:T(8,128)(2,1)}, u32[]{:S(2)}, u32[]{:S(2)}) collective-permute-start(bf16[128,2048]{1,0:T(8,128)(2,1)} %fusion.3), channel_id=1, source_target_pairs={{0,2},{1,3},{2,0},{3,1},{4,6},{5,7},{6,4},{7,5},{8,10},{9,11},{10,... | collective-permute-start | bytes 1572872 | tf_op jit(solution)/shard_map/ppermute | solution.py:311
  223.1 2.6 %copy-start.11 = (f32[256,1536]{1,0:T(8,128)S(1)}, f32[256,1536]{1,0:T(8,128)}, u32[]{:S(2)}) copy-start(f32[256,1536]{1,0:T(8,128)} %copy-done.10) | copy-start | bytes 4718596
  227.0 24.3 %copy-start.22 = (bf16[128,2048]{1,0:T(8,128)(2,1)S(1)}, bf16[128,2048]{1,0:T(8,128)(2,1)}, u32[]{:S(2)}) copy-start(bf16[128,2048]{1,0:T(8,128)(2,1)} %fusion.5) | copy-start | bytes 1572868
  227.0 23.0 %collective-permute-start.25 = (bf16[128,1536]{1,0:T(8,128)(2,1)S(1)}, bf16[128,1536]{1,0:T(8,128)(2,1)S(1)}, u32[]{:S(2)}, u32[]{:S(2)}) collective-permute-start(bf16[128,1536]{1,0:T(8,128)(2,1)S(1)} %fusion.9), channel_id=1, source_target_pairs={{0,2},{1,3},{2,0},{3,1},{4,6},{5,7},{6,4},{7,5},{8,10},{9,11},{10,... | collective-permute-start | bytes 1179656 | tf_op jit(solution)/shard_map/ppermute | solution.py:311
  228.4 24.7 %collective-permute-start.26 = (bf16[128,2048]{1,0:T(8,128)(2,1)S(1)}, bf16[128,2048]{1,0:T(8,128)(2,1)S(1)}, u32[]{:S(2)}, u32[]{:S(2)}) collective-permute-start(bf16[128,2048]{1,0:T(8,128)(2,1)S(1)} %fusion), channel_id=1, source_target_pairs={{0,0},{5,4},{10,8},{15,12},{4,1},{1,5},{14,9},{11,13},{8,2},{13,6}... | collective-permute-start | bytes 1572872 | tf_op jit(solution)/shard_map/ppermute | solution.py:324

commit v13 on v12

--- a/solution.py
+++ b/solution.py
@@ -331,11 +331,12 @@
     near, rest, facts = choose(block_adapter, block_length, adapter_slot, here, down_t)
     up_flat = adapter_up.reshape(span, hidden)
 
-    even = jnp.concatenate([tokens, after(tok_x, facts)], axis=0)
+    near = swap(near, CORE)
+    down_x = swap(rest[:rank] + near[rank:], CHIP)
+    even = jnp.concatenate([tokens, after(tok_x, facts, down_x)], axis=0)
     odd = swap(even, CORE)
     even_far = both(even, hop)
     cot_x = swap(after(cotangent, even), CHIP)
-    near = swap(after(near, even), CORE)
     grad01, parts, back01 = return_grad(facts, after(cotangent, even), cot_c, weight, adapter_up, (0, 1))
     toks = [(even, 0), (odd, 0), (even, 1), (odd, 1)]
     inner = rank_inner(facts, down_t.reshape(span, width), [(after(x, grad01), n) for x, n in toks], rank)
@@ -343,19 +344,18 @@
     odd_far = both(after(odd, inner), hop)
     even_mid = jnp.where(away == 0, even, after(even_far, inner))
     even_all = both(even_mid, hops)
-    down_x = rest[:rank] + after(near, inner)[rank:]
-    cot_xc = swap(after(cot_x, even_mid, down_x), CORE)
-    down_x = swap(after(down_x, cot_x), CHIP)
+    cot_xc = swap(after(cot_x, even_mid), CORE)
+    down_mine = both(rest[rank:] + near[:rank] + after(down_x, inner), place)
     inner = after(inner, cot_x) + inner_near
     inner_far = along(inner, 2)
     odd_mid = jnp.where(away == 0, odd, after(odd_far, inner))
     odd_all = both(odd_mid, hops)
     grad23, parts, back23 = return_grad(
-        facts, after(cot_x, odd_mid, even_all, down_x), cot_xc, weight, adapter_up, (2, 3), (parts,)
+        facts, after(cot_x, odd_mid, even_all), cot_xc, weight, adapter_up, (2, 3), (parts,)
     )
     back = jnp.concatenate([back01, back23], axis=1)
     back_near = along(back, 1)
-    all_even = jnp.where(away == 0, even, jnp.where(away == 2, even_far, after(even_all, grad23)))
+    all_even = jnp.where(away == 0, even, jnp.where(away == 2, even_far, after(even_all, grad23, down_mine)))
     all_odd = jnp.where(away == 0, odd, jnp.where(away == 2, odd_far, after(odd_all, all_even)))
     all_tokens = jnp.concatenate([all_even, all_odd], axis=0)
     inner_wide, inner_rows, _ = spread(facts, after(inner, all_tokens), inner_far, per_owner, adapter_scale)
@@ -364,7 +364,6 @@
     back = after(back, up_wide) + back_near
     back_wide, _, back_b = spread(facts, back, along(back, 2), per_owner, 1.0)
     parts = lax.all_to_all(after(parts, back_b).reshape(shards, rows, depth), "tp", 0, 0, tiled=True)
-    down_mine = both(rest[rank:] + near[:rank] + after(down_x, back_b), place)
     back_b = share(back_b, swap(back_b, CORE), CORE)
 
     def grad_block(q):
@@ -395,7 +394,7 @@
 
     point = make(0, back_b)
     back_b = share(after(back_b, point), swap(back_b, CHIP), CHIP)
-    point = make(1, point, down_mine)
+    point = make(1, point)
     point = cross(0, point)
     point = make(2, point, back_b)
     point = finish(0, point)

time: 256 us -> 248 us (0.969)
  waiting for transfers between devices: 81.8 us -> 76.9 us
    ppermute x17, waiting for transfers between devices: 47.5 us -> 41.3 us  [swap(): return lax.ppermute(x, 'dp', [(d, d ^ bit) for d in range(groups)])]
    ppermute x6, waiting for transfers between devices: 20.1 us -> 15.6 us  [both(): return lax.ppermute(x, ('tp', 'dp'), pairs)]
    ppermute x4, waiting for transfers between devices: 14.3 us -> 18.7 us  [along(): return lax.ppermute(x, 'tp', [(z, z ^ bit) for z in range(shards)])]
    unnamed x55 -> x59, local copies, waits for them, and re-layouts: 11.2 us -> 10.9 us
  transfers between devices with their start and end apart: 28 -> 28, of which waited for: 13 -> 13; matrix products, arithmetic and copies ran while one was open for 11% -> 10% of each run, Pallas kernels for 32% -> 33%
where the time goes in v13:
time: 248 us; the launch traced here: 246 us
  Pallas kernels  94.5 us (38%)
  waiting for transfers between devices  76.9 us (31%)
  starting transfers between devices  38.2 us (15%)
  other arithmetic  22.3 us (9%)
  local copies, waits for them, and re-layouts  10.9 us (4%)
  matrix products  2.61 us (1%)
    ppermute x17, waiting for transfers between devices, swap(): return lax.ppermute(x, 'dp', [(d, d ^ bit) for d in range(groups)])  41.3 us
    pallas_call x2, Pallas kernels, return_grad(): pl.pallas_call(kernel, grid_spec=pltpu.PrefetchScalarGridSpec(num_scalar_...  40.8 us
    pallas_call x4, Pallas kernels, project(): pl.pallas_call(kernel, grid=((stop - start) // block,), in_specs=[pl.Bloc...  34 us
    ppermute x4, waiting for transfers between devices, along(): return lax.ppermute(x, 'tp', [(z, z ^ bit) for z in range(shards)])  18.7 us
    ppermute x6, starting transfers between devices, both(): return lax.ppermute(x, ('tp', 'dp'), pairs)  17 us
    ppermute x6, waiting for transfers between devices, both(): return lax.ppermute(x, ('tp', 'dp'), pairs)  15.6 us
    pallas_call x2, Pallas kernels, slot_grad(): pl.pallas_call(kernel, grid=(columns // block,), in_specs=[pl.BlockSpec((...  13.3 us
    unnamed x59, local copies, waits for them, and re-layouts  10.9 us
  transfers between devices with their start and end apart: 28, of which 13 were waited for; matrix products, arithmetic and copies ran while one was open for 10% of the time, Pallas kernels for 33%

profile of v13, /device:TPU:2, one launch (start us, length us, event | category | flops | bytes accessed | tf_op | source)
XLA Modules:
  0.0 246.5 jit_solution(9863022517093426032)
XLA Ops:
  0.7 1.6 copy-done.6
  2.3 0.7 copy-done.17
  3.0 0.7 copy-done.18
  3.6 0.7 copy-done.19
  4.3 1.5 choose.1
  6.4 1.4 collective-permute-done.1
  8.3 12.4 %collective-permute-done = bf16[128,2048]{1,0:T(8,128)(2,1)S(1)} collective-permute-done((bf16[128,2048]{1,0:T(8,128)(2,1)S(1)}, bf16[128,2048]{1,0:T(8,128)(2,1)S(1)}, u32[]{:S(2)}, u32[]{:S(2)}) %collective-permute-start) | collective-permute-done | bytes 524320 | tf_op jit(solution)/shard_map/ppermute | solution.py:311
  20.7 5.2 %collective-permute-done.2 = bf16[64,2048]{1,0:T(8,128)(2,1)S(1)} collective-permute-done((bf16[64,2048]{1,0:T(8,128)(2,1)S(1)}, bf16[64,2048]{1,0:T(8,128)(2,1)S(1)}, u32[]{:S(2)}, u32[]{:S(2)}) %collective-permute-start.2) | collective-permute-done | bytes 262176 | tf_op jit(solution)/shard_map/ppermute | solution.py:311
  25.9 0.7 copy-done.26
  26.8 1.3 collective-permute-start.3
  28.1 20.4 %return_grad.2 = (f32[256,2048]{1,0:T(8,128)S(1)}, bf16[512,2048]{1,0:T(8,128)(2,1)}, f32[64,256]{1,0:T(8,128)S(1)}) custom-call(s32[9]{0:T(128)S(1)} %get-tuple-element.57.facts_ref, bf16[128,7168]{1,0:T(8,128)(2,1)} %refs_0_.1, bf16[128,7168]{1,0:T(8,128)(2,1)} %collective-permute-done.4.b_ref.refs_1_, bf16[2048,7168]{1,0:T(8,128)(2,1)} %w_ref.11, ...), custom_call_target="tpu_custom_call" | custom-call | flops 117440512 | bytes 516096 | tf_op jit(solution)/shard_map/return_grad/pallas_call | solution.py:88
  48.5 1.3 copy-done.13
  49.9 1.8 rank_inner.1
  51.7 4.0 %collective-permute-done.3 = bf16[256,2048]{1,0:T(8,128)(2,1)} collective-permute-done((bf16[256,2048]{1,0:T(8,128)(2,1)S(1)}, bf16[256,2048]{1,0:T(8,128)(2,1)}, u32[]{:S(2)}, u32[]{:S(2)}) %collective-permute-start.3) | collective-permute-done | bytes 1048608 | tf_op jit(solution)/shard_map/ppermute | solution.py:324
  55.7 1.3 collective-permute-start.8
  57.0 2.3 broadcast_select_fusion.1
  59.3 9.1 %collective-permute-done.7.a_ref.refs_2_ = bf16[128,7168]{1,0:T(8,128)(2,1)} collective-permute-done((bf16[128,7168]{1,0:T(8,128)(2,1)}, bf16[128,7168]{1,0:T(8,128)(2,1)}, u32[]{:S(2)}, u32[]{:S(2)}) %collective-permute-start.7) | collective-permute-done | bytes 1835040 | tf_op jit(solution)/shard_map/ppermute | solution.py:311
  68.4 1.6 collective-permute-start.9
  70.0 3.3 %collective-permute-start.6 = (bf16[256,2048]{1,0:T(8,128)(2,1)}, bf16[256,2048]{1,0:T(8,128)(2,1)}, u32[]{:S(2)}, u32[]{:S(2)}) collective-permute-start(bf16[256,2048]{1,0:T(8,128)(2,1)} %broadcast_select_fusion.1), channel_id=1, source_target_pairs={{0,4},{8,12},{5,1},{13,9},{10,14},{2,6},{15,11},{7,3},{16,20},{24,... | collective-permute-start | bytes 3145736 | tf_op jit(solution)/shard_map/ppermute | solution.py:324
  73.3 11.9 %collective-permute-done.9 = f32[64,512]{1,0:T(8,128)S(1)} collective-permute-done((f32[64,512]{1,0:T(8,128)S(1)}, f32[64,512]{1,0:T(8,128)S(1)}, u32[]{:S(2)}, u32[]{:S(2)}) %collective-permute-start.9) | collective-permute-done | bytes 131104 | tf_op jit(solution)/shard_map/ppermute | solution.py:314
  85.2 1.2 broadcast_select_fusion
  86.4 2.4 collective-permute-start.12
  88.8 0.7 fusion.13
  89.6 6.7 %collective-permute-start.11 = (bf16[64,2048]{1,0:T(8,128)(2,1)}, bf16[64,2048]{1,0:T(8,128)(2,1)S(1)}, u32[]{:S(2)}, u32[]{:S(2)}) collective-permute-start(bf16[64,2048]{1,0:T(8,128)(2,1)} %fusion.13), channel_id=1, source_target_pairs={{0,0},{4,5},{8,10},{12,15},{1,4},{5,1},{9,14},{13,11},{2,8},{6,13}... | collective-permute-start | bytes 786440 | tf_op jit(solution)/shard_map/ppermute | solution.py:324
  96.4 20.4 %return_grad.3 = (f32[256,2048]{1,0:T(8,128)S(1)}, bf16[512,2048]{1,0:T(8,128)(2,1)}, f32[64,256]{1,0:T(8,128)S(1)}) custom-call(s32[9]{0:T(128)S(1)} %get-tuple-element.57.facts_ref, bf16[128,7168]{1,0:T(8,128)(2,1)} %collective-permute-done.7.a_ref.refs_2_, ...), custom_call_target="tpu_custom_call", output_to_operand_aliasing={{1}: (6, {})} | custom-call | flops 117440512 | bytes 516096 | tf_op jit(solution)/shard_map/return_grad/pallas_call | solution.py:88
  116.8 2.2 select_select_fusion.1
  119.5 1.6 pad_maximum_fusion.tok_ref
  121.1 1.1 collective-permute-start.14
  122.2 1.4 spread.2
  123.5 10.4 %slot_grad.2 = f32[512,7168]{1,0:T(8,128)} custom-call(bf16[512,512]{1,0:T(8,128)(2,1)S(1)} %get-tuple-element.81.wide_ref, bf16[128,7168]{1,0:T(8,128)(2,1)} %refs_0_.1, bf16[128,7168]{1,0:T(8,128)(2,1)} %collective-permute-done.4.b_ref.refs_1_, bf16[128,7168]{1,0:T(8,128)(2,1)} %collective-permute-done.7.a_ref.refs_2_, ...), custom_call_target="tpu_custom_call" | custom-call | flops 3758096384 | bytes 22020096 | tf_op jit(solution)/shard_map/slot_grad/pallas_call | solution.py:212
  134.0 3.1 %collective-permute-start.15 = (f32[64,512]{1,0:T(8,128)S(1)}, f32[64,512]{1,0:T(8,128)S(1)}, u32[]{:S(2)}, u32[]{:S(2)}) collective-permute-start(f32[64,512]{1,0:T(8,128)S(1)} %add.90.refs_0_), channel_id=1, source_target_pairs={{0,8},{4,12},{8,0},{12,4},{1,9},{5,13},{9,1},{13,5},{2,10},{6,14},... | collective-permute-start | bytes 393224 | tf_op jit(solution)/shard_map/ppermute | solution.py:314
  137.1 6.8 %collective-permute-done.15.refs_1_ = f32[64,512]{1,0:T(8,128)S(1)} collective-permute-done((f32[64,512]{1,0:T(8,128)S(1)}, f32[64,512]{1,0:T(8,128)S(1)}, u32[]{:S(2)}, u32[]{:S(2)}) %collective-permute-start.15) | collective-permute-done | bytes 131104 | tf_op jit(solution)/shard_map/ppermute | solution.py:314
  143.9 1.7 spread.3
  145.6 0.8 copy-done.15
  146.3 1.3 collective-permute-done.16
  147.6 9.9 %project.4 = (f32[256,2048]{1,0:T(8,128)S(1)}, f32[256,2048]{1,0:T(8,128)}) custom-call(bf16[512,2048]{1,0:T(8,128)(2,1)} %pad_maximum_fusion.tok_ref, bf16[512,512]{1,0:T(8,128)(2,1)S(1)} %get-tuple-element.80.wide_ref, bf16[2048,7168]{1,0:T(8,128)(2,1)} %w_ref.11, bf16[512,7168]{1,0:T(8,128)(2,1)} %bitcast.23), custom_call_target="tpu_custom_call" | custom-call | flops 83886080 | bytes 229376 | tf_op jit(solution)/shard_map/project/pallas_call | solution.py:39
  157.6 1.3 copy-done.8
  159.0 4.8 %all-to-all-start = ((bf16[4,128,2048]{2,1,0:T(8,128)(2,1)}), bf16[4,128,2048]{2,1,0:T(8,128)(2,1)}, u32[]{:S(2)}, u32[]{:S(2)}) async-start(bf16[4,128,2048]{2,1,0:T(8,128)(2,1)} %bitcast.28), calls=%async_computation | async-start | bytes 4194304 | tf_op jit(solution)/shard_map/all_to_all | solution.py:366
  163.8 3.8 %collective-permute-start.18 = (bf16[64,512]{1,0:T(8,128)(2,1)S(1)}, bf16[64,512]{1,0:T(8,128)(2,1)S(1)}, u32[]{:S(2)}, u32[]{:S(2)}) collective-permute-start(bf16[64,512]{1,0:T(8,128)(2,1)S(1)} %maximum_add_fusion), channel_id=1, source_target_pairs={{0,2},{1,3},{2,0},{3,1},{4,6},{5,7},{6,4},{7,5},{8,10},{9,11},{10,... | collective-permute-start | bytes 196616 | tf_op jit(solution)/shard_map/ppermute | solution.py:311
  167.7 1.0 copy-done.5
  168.7 6.7 %project.5 = (f32[256,1536]{1,0:T(8,128)S(1)}, f32[256,1536]{1,0:T(8,128)S(1)}) custom-call(bf16[512,2048]{1,0:T(8,128)(2,1)S(1)} %copy-done, bf16[512,512]{1,0:T(8,128)(2,1)S(1)} %copy-done.5, bf16[2048,7168]{1,0:T(8,128)(2,1)} %w_ref.11, bf16[512,7168]{1,0:T(8,128)(2,1)} %bitcast.24), custom_call_target="tpu_custom_call" | custom-call | flops 62914560 | bytes 172032 | tf_op jit(solution)/shard_map/project/pallas_call | solution.py:39
  175.6 1.8 fusion.6
  177.5 0.6 maximum_add_fusion.1
  178.1 9.9 %project.6 = (f32[256,2048]{1,0:T(8,128)S(1)}, f32[256,2048]{1,0:T(8,128)}) custom-call(bf16[512,2048]{1,0:T(8,128)(2,1)} %pad_maximum_fusion.tok_ref, bf16[512,512]{1,0:T(8,128)(2,1)S(1)} %copy-done.5, bf16[2048,7168]{1,0:T(8,128)(2,1)} %w_ref.11, bf16[512,7168]{1,0:T(8,128)(2,1)} %bitcast.25), custom_call_target="tpu_custom_call" | custom-call | flops 83886080 | bytes 229376 | tf_op jit(solution)/shard_map/project/pallas_call | solution.py:39
  188.0 3.3 %collective-permute-done.19 = bf16[128,2048]{1,0:T(8,128)(2,1)S(1)} collective-permute-done((bf16[128,2048]{1,0:T(8,128)(2,1)S(1)}, bf16[128,2048]{1,0:T(8,128)(2,1)S(1)}, u32[]{:S(2)}, u32[]{:S(2)}) %collective-permute-start.19) | collective-permute-done | bytes 524320 | tf_op jit(solution)/shard_map/ppermute | solution.py:311
  191.3 2.2 fusion.5
  194.0 7.5 %project.7 = (f32[256,1536]{1,0:T(8,128)S(1)}, f32[256,1536]{1,0:T(8,128)}) custom-call(bf16[512,2048]{1,0:T(8,128)(2,1)S(1)} %copy-done.1, bf16[512,512]{1,0:T(8,128)(2,1)S(1)} %copy-done.5, bf16[2048,7168]{1,0:T(8,128)(2,1)} %w_ref.11, bf16[512,7168]{1,0:T(8,128)(2,1)} %bitcast.26), custom_call_target="tpu_custom_call" | custom-call | flops 62914560 | bytes 172032 | tf_op jit(solution)/shard_map/project/pallas_call | solution.py:39
  201.5 1.2 copy-done.10
  202.7 1.3 collective-permute-done.21
  204.0 1.6 fusion.11
  205.6 2.1 fusion.3
  207.7 0.8 collective-permute-start.24
  208.6 2.9 %slot_grad.3 = f32[512,2048]{1,0:T(8,128)} custom-call(bf16[512,512]{1,0:T(8,128)(2,1)S(1)} %copy-done.16, bf16[256,2048]{1,0:T(8,128)(2,1)S(1)} %constant_dynamic-update-slice_fusion.refs_0_.refs_2_, bf16[256,2048]{1,0:T(8,128)(2,1)S(1)} %copy-done.3, bf16[256,2048]{1,0:T(8,128)(2,1)S(1)} %constant_dynamic-update-slice_fusion.refs_0_.refs_2_, ...), custom_call_target="tpu_custom_call" | custom-call | flops 1073741824 | bytes 6291456 | tf_op jit(solution)/shard_map/slot_grad/pallas_call | solution.py:212
  211.5 1.2 all-to-all-done
  212.7 2.6 %fusion = bf16[128,2048]{1,0:T(8,128)(2,1)S(1)} fusion(bf16[64,2048]{1,0:T(8,128)(2,1)} %copy-done.25, f32[256,2048]{1,0:T(8,128)} %copy-done.14, s32[]{:T(128)S(6)} %select_n.64, f32[256,2048]{1,0:T(8,128)} %copy-done.13, bf16[4,128,2048]{2,1,0:T(8,128)(2,1)} %all-to-all-done, s32[]{:T(128)S(6)} %select_n.68, s32[]{:T(128)S(6)} %select_n.67, ...), kind=kOutput, calls=%fused_computation.1 | convolution fusion | flops 35913728 | bytes 4472853 | tf_op jit(solution)/shard_map/dot_general | solution.py:18
  215.4 1.3 fusion.9
  216.6 3.9 %collective-permute-start.25 = (bf16[128,1536]{1,0:T(8,128)(2,1)S(1)}, bf16[128,1536]{1,0:T(8,128)(2,1)S(1)}, u32[]{:S(2)}, u32[]{:S(2)}) collective-permute-start(bf16[128,1536]{1,0:T(8,128)(2,1)S(1)} %fusion.9), channel_id=1, source_target_pairs={{0,2},{1,3},{2,0},{3,1},{4,6},{5,7},{6,4},{7,5},{8,10},{9,11},{10,... | collective-permute-start | bytes 1179656 | tf_op jit(solution)/shard_map/ppermute | solution.py:311
  220.5 1.9 collective-permute-start.26
  222.4 1.5 fusion.2
  223.9 7.5 %collective-permute-done.25 = bf16[128,1536]{1,0:T(8,128)(2,1)S(1)} collective-permute-done((bf16[128,1536]{1,0:T(8,128)(2,1)S(1)}, bf16[128,1536]{1,0:T(8,128)(2,1)S(1)}, u32[]{:S(2)}, u32[]{:S(2)}) %collective-permute-start.25) | collective-permute-done | bytes 393248 | tf_op jit(solution)/shard_map/ppermute | solution.py:311
  231.4 1.3 fusion.8
  232.7 1.4 pad_maximum_fusion.1
  234.1 11.6 %collective-permute-done.26 = bf16[128,2048]{1,0:T(8,128)(2,1)S(1)} collective-permute-done((bf16[128,2048]{1,0:T(8,128)(2,1)S(1)}, bf16[128,2048]{1,0:T(8,128)(2,1)S(1)}, u32[]{:S(2)}, u32[]{:S(2)}) %collective-permute-start.26) | collective-permute-done | bytes 524320 | tf_op jit(solution)/shard_map/ppermute | solution.py:324
  245.7 0.8 copy.17
  (89 shorter events, 3.0 us)
Async XLA Ops:
  0.7 1.6 copy-start.6
  2.3 0.7 copy-start.17
  3.0 0.7 copy-start.18
  3.6 0.7 copy-start.19
  4.3 1.6 copy-start.24
  5.8 2.0 collective-permute-start.1
  5.9 14.8 %collective-permute-start = (bf16[128,2048]{1,0:T(8,128)(2,1)S(1)}, bf16[128,2048]{1,0:T(8,128)(2,1)S(1)}, u32[]{:S(2)}, u32[]{:S(2)}) collective-permute-start(bf16[128,2048]{1,0:T(8,128)(2,1)S(1)} %copy-done.24), channel_id=1, source_target_pairs={{0,2},{1,3},{2,0},{3,1},{4,6},{5,7},{6,4},{7,5},{8,10},{9,11},{10,... | collective-permute-start | bytes 1572872 | tf_op jit(solution)/shard_map/ppermute | solution.py:311
  6.0 22.2 %collective-permute-start.4 = (bf16[128,7168]{1,0:T(8,128)(2,1)}, bf16[128,7168]{1,0:T(8,128)(2,1)}, u32[]{:S(2)}, u32[]{:S(2)}) collective-permute-start(bf16[128,7168]{1,0:T(8,128)(2,1)} %refs_0_.1), channel_id=1, source_target_pairs={{0,1},{1,0},{2,3},{3,2},{4,5},{5,4},{6,7},{7,6},{8,9},{9,8},{10,11... | collective-permute-start | bytes 5505032 | tf_op jit(solution)/shard_map/ppermute | solution.py:311
  7.8 18.0 %collective-permute-start.2 = (bf16[64,2048]{1,0:T(8,128)(2,1)S(1)}, bf16[64,2048]{1,0:T(8,128)(2,1)S(1)}, u32[]{:S(2)}, u32[]{:S(2)}) collective-permute-start(bf16[64,2048]{1,0:T(8,128)(2,1)S(1)} %slice_add_fusion.9), channel_id=1, source_target_pairs={{0,2},{1,3},{2,0},{3,1},{4,6},{5,7},{6,4},{7,5},{8,10},{9,11},{10,... | collective-permute-start | bytes 786440 | tf_op jit(solution)/shard_map/ppermute | solution.py:311
  25.8 0.7 copy-start.26
  26.5 41.9 %collective-permute-start.7 = (bf16[128,7168]{1,0:T(8,128)(2,1)}, bf16[128,7168]{1,0:T(8,128)(2,1)}, u32[]{:S(2)}, u32[]{:S(2)}) collective-permute-start(bf16[128,7168]{1,0:T(8,128)(2,1)} %refs_0_.1), channel_id=1, source_target_pairs={{0,2},{1,3},{2,0},{3,1},{4,6},{5,7},{6,4},{7,5},{8,10},{9,11},{10,... | collective-permute-start | bytes 5505032 | tf_op jit(solution)/shard_map/ppermute | solution.py:311
  26.8 23.1 %collective-permute-start.5 = (bf16[256,2048]{1,0:T(8,128)(2,1)S(1)}, bf16[256,2048]{1,0:T(8,128)(2,1)S(1)}, u32[]{:S(2)}, u32[]{:S(2)}) collective-permute-start(bf16[256,2048]{1,0:T(8,128)(2,1)S(1)} %constant_dynamic-update-slice_fusion.refs_0_.refs_2_), channel_id=1, source_target_pairs={{0,1},{1,0},{2,3},{3,2},{4,5},{5,4},{6,7},{7,6},{8,9},{9,8},{10,11... | collective-permute-start | bytes 3145736 | tf_op jit(solution)/shard_map/ppermute | solution.py:311
  26.8 28.9 %collective-permute-start.3 = (bf16[256,2048]{1,0:T(8,128)(2,1)S(1)}, bf16[256,2048]{1,0:T(8,128)(2,1)}, u32[]{:S(2)}, u32[]{:S(2)}) collective-permute-start(bf16[256,2048]{1,0:T(8,128)(2,1)S(1)} %constant_dynamic-update-slice_fusion.refs_0_.refs_2_), channel_id=1, source_target_pairs={{0,8},{5,13},{10,2},{15,7},{16,24},{21,29},{26,18},{31,23}} | collective-permute-start | bytes 3145736 | tf_op jit(solution)/shard_map/ppermute | solution.py:324
  28.1 21.8 %copy-start.7 = (bf16[8,2048,64]{1,2,0:T(8,128)(2,1)S(1)}, bf16[8,2048,64]{1,2,0:T(8,128)(2,1)}, u32[]{:S(2)}) copy-start(bf16[8,2048,64]{1,2,0:T(8,128)(2,1)} %param.10) | copy-start | bytes 6291460
  48.5 1.4 copy-start.13
  49.9 69.2 %copy-start.2 = (bf16[256,2048]{1,0:T(8,128)(2,1)}, bf16[256,2048]{1,0:T(8,128)(2,1)S(1)}, u32[]{:S(2)}) copy-start(bf16[256,2048]{1,0:T(8,128)(2,1)S(1)} %collective-permute-done.5.refs_1_.refs_3_) | copy-start | bytes 3145732
  55.7 29.5 %collective-permute-start.8 = (bf16[256,2048]{1,0:T(8,128)(2,1)S(1)}, bf16[256,2048]{1,0:T(8,128)(2,1)S(1)}, u32[]{:S(2)}, u32[]{:S(2)}) collective-permute-start(bf16[256,2048]{1,0:T(8,128)(2,1)S(1)} %collective-permute-done.5.refs_1_.refs_3_), channel_id=1, source_target_pairs={{0,8},{5,13},{10,2},{15,7},{16,24},{21,29},{26,18},{31,23}} | collective-permute-start | bytes 3145736 | tf_op jit(solution)/shard_map/ppermute | solution.py:324
  59.3 29.5 %copy-start.27 = (bf16[64,2048]{1,0:T(8,128)(2,1)S(1)}, bf16[64,2048]{1,0:T(8,128)(2,1)}, u32[]{:S(2)}) copy-start(bf16[64,2048]{1,0:T(8,128)(2,1)} %copy-done.26) | copy-start | bytes 786436
  68.4 28.0 %collective-permute-start.10 = (bf16[128,7168]{1,0:T(8,128)(2,1)}, bf16[128,7168]{1,0:T(8,128)(2,1)}, u32[]{:S(2)}, u32[]{:S(2)}) collective-permute-start(bf16[128,7168]{1,0:T(8,128)(2,1)} %collective-permute-done.7.a_ref.refs_2_), channel_id=1, source_target_pairs={{0,1},{1,0},{2,3},{3,2},{4,5},{5,4},{6,7},{7,6},{8,9},{9,8},{10,11... | collective-permute-start | bytes 5505032 | tf_op jit(solution)/shard_map/ppermute | solution.py:311
  68.4 16.8 %collective-permute-start.9 = (f32[64,512]{1,0:T(8,128)S(1)}, f32[64,512]{1,0:T(8,128)S(1)}, u32[]{:S(2)}, u32[]{:S(2)}) collective-permute-start(f32[64,512]{1,0:T(8,128)S(1)} %rank_inner.1), channel_id=1, source_target_pairs={{0,4},{4,0},{8,12},{12,8},{1,5},{5,1},{9,13},{13,9},{2,6},{6,2},{1... | collective-permute-start | bytes 393224 | tf_op jit(solution)/shard_map/ppermute | solution.py:314
  70.0 26.4 %collective-permute-start.6 = (bf16[256,2048]{1,0:T(8,128)(2,1)}, bf16[256,2048]{1,0:T(8,128)(2,1)}, u32[]{:S(2)}, u32[]{:S(2)}) collective-permute-start(bf16[256,2048]{1,0:T(8,128)(2,1)} %broadcast_select_fusion.1), channel_id=1, source_target_pairs={{0,4},{8,12},{5,1},{13,9},{10,14},{2,6},{15,11},{7,3},{16,20},{24,... | collective-permute-start | bytes 3145736 | tf_op jit(solution)/shard_map/ppermute | solution.py:324
  85.2 4.4 %copy-start.20 = (bf16[256,2048]{1,0:T(8,128)(2,1)}, bf16[256,2048]{1,0:T(8,128)(2,1)S(1)}, u32[]{:S(2)}) copy-start(bf16[256,2048]{1,0:T(8,128)(2,1)S(1)} %collective-permute-done.8) | copy-start | bytes 3145732
  86.4 32.7 %collective-permute-start.12 = (bf16[256,2048]{1,0:T(8,128)(2,1)}, bf16[256,2048]{1,0:T(8,128)(2,1)}, u32[]{:S(2)}, u32[]{:S(2)}) collective-permute-start(bf16[256,2048]{1,0:T(8,128)(2,1)} %broadcast_select_fusion), channel_id=1, source_target_pairs={{0,4},{8,12},{5,1},{13,9},{10,14},{2,6},{15,11},{7,3},{16,20},{24,... | collective-permute-start | bytes 3145736 | tf_op jit(solution)/shard_map/ppermute | solution.py:324
  89.6 27.2 %collective-permute-start.11 = (bf16[64,2048]{1,0:T(8,128)(2,1)}, bf16[64,2048]{1,0:T(8,128)(2,1)S(1)}, u32[]{:S(2)}, u32[]{:S(2)}) collective-permute-start(bf16[64,2048]{1,0:T(8,128)(2,1)} %fusion.13), channel_id=1, source_target_pairs={{0,0},{4,5},{8,10},{12,15},{1,4},{5,1},{9,14},{13,11},{2,8},{6,13}... | collective-permute-start | bytes 786440 | tf_op jit(solution)/shard_map/ppermute | solution.py:324
  96.3 25.8 %collective-permute-start.13 = (f32[64,512]{1,0:T(8,128)S(1)}, f32[64,512]{1,0:T(8,128)S(1)}, u32[]{:S(2)}, u32[]{:S(2)}) collective-permute-start(f32[64,512]{1,0:T(8,128)S(1)} %add.87.refs_0_), channel_id=1, source_target_pairs={{0,8},{4,12},{8,0},{12,4},{1,9},{5,13},{9,1},{13,5},{2,10},{6,14},... | collective-permute-start | bytes 393224 | tf_op jit(solution)/shard_map/ppermute | solution.py:314
  116.8 2.3 copy-start.14
  116.8 2.3 copy-start.25
  116.8 2.4 copy-start.21
  121.1 12.9 %collective-permute-start.14 = (f32[64,512]{1,0:T(8,128)S(1)}, f32[64,512]{1,0:T(8,128)S(1)}, u32[]{:S(2)}, u32[]{:S(2)}) collective-permute-start(f32[64,512]{1,0:T(8,128)S(1)} %constant_dynamic-update-slice_fusion.2), channel_id=1, source_target_pairs={{0,4},{4,0},{8,12},{12,8},{1,5},{5,1},{9,13},{13,9},{2,6},{6,2},{1... | collective-permute-start | bytes 393224 | tf_op jit(solution)/shard_map/ppermute | solution.py:314
  123.5 24.1 %copy-start.4 = (bf16[512,512]{1,0:T(8,128)(2,1)}, bf16[512,512]{1,0:T(8,128)(2,1)S(1)}, u32[]{:S(2)}) copy-start(bf16[512,512]{1,0:T(8,128)(2,1)S(1)} %get-tuple-element.80.wide_ref) | copy-start | bytes 1572868
  134.0 9.9 %collective-permute-start.15 = (f32[64,512]{1,0:T(8,128)S(1)}, f32[64,512]{1,0:T(8,128)S(1)}, u32[]{:S(2)}, u32[]{:S(2)}) collective-permute-start(f32[64,512]{1,0:T(8,128)S(1)} %add.90.refs_0_), channel_id=1, source_target_pairs={{0,8},{4,12},{8,0},{12,4},{1,9},{5,13},{9,1},{13,5},{2,10},{6,14},... | collective-permute-start | bytes 393224 | tf_op jit(solution)/shard_map/ppermute | solution.py:314
  145.6 0.8 copy-start.15
  146.3 1.3 collective-permute-start.16
  157.6 1.3 copy-start.8
  158.9 16.7 %collective-permute-start.17 = (f32[256,2048]{1,0:T(8,128)}, f32[256,2048]{1,0:T(8,128)}, u32[]{:S(2)}, u32[]{:S(2)}) collective-permute-start(f32[256,2048]{1,0:T(8,128)} %get-tuple-element.89), channel_id=1, source_target_pairs={{0,1},{1,0},{2,3},{3,2},{4,5},{5,4},{6,7},{7,6},{8,9},{9,8},{10,11... | collective-permute-start | bytes 6291464 | tf_op jit(solution)/shard_map/ppermute | solution.py:311
  159.0 8.7 %copy-start = (bf16[512,2048]{1,0:T(8,128)(2,1)S(1)}, bf16[512,2048]{1,0:T(8,128)(2,1)}, u32[]{:S(2)}) copy-start(bf16[512,2048]{1,0:T(8,128)(2,1)} %pad_maximum_fusion.tok_ref) | copy-start | bytes 6291460
  159.0 53.7 %all-to-all-start = ((bf16[4,128,2048]{2,1,0:T(8,128)(2,1)}), bf16[4,128,2048]{2,1,0:T(8,128)(2,1)}, u32[]{:S(2)}, u32[]{:S(2)}) async-start(bf16[4,128,2048]{2,1,0:T(8,128)(2,1)} %bitcast.28), calls=%async_computation | async-start | bytes 4194304 | tf_op jit(solution)/shard_map/all_to_all | solution.py:366
  163.8 13.6 %collective-permute-start.18 = (bf16[64,512]{1,0:T(8,128)(2,1)S(1)}, bf16[64,512]{1,0:T(8,128)(2,1)S(1)}, u32[]{:S(2)}, u32[]{:S(2)}) collective-permute-start(bf16[64,512]{1,0:T(8,128)(2,1)S(1)} %maximum_add_fusion), channel_id=1, source_target_pairs={{0,2},{1,3},{2,0},{3,1},{4,6},{5,7},{6,4},{7,5},{8,10},{9,11},{10,... | collective-permute-start | bytes 196616 | tf_op jit(solution)/shard_map/ppermute | solution.py:311
  167.7 1.0 copy-start.5
  168.7 6.9 %copy-start.9 = (f32[256,2048]{1,0:T(8,128)S(1)}, f32[256,2048]{1,0:T(8,128)}, u32[]{:S(2)}) copy-start(f32[256,2048]{1,0:T(8,128)} %copy-done.8) | copy-start | bytes 6291460
  175.4 18.0 %copy-start.12 = (f32[256,1536]{1,0:T(8,128)}, f32[256,1536]{1,0:T(8,128)S(1)}, u32[]{:S(2)}) copy-start(f32[256,1536]{1,0:T(8,128)S(1)} %get-tuple-element.98) | copy-start | bytes 4718596
  175.5 18.0 %collective-permute-start.20 = (f32[256,1536]{1,0:T(8,128)S(1)}, f32[256,1536]{1,0:T(8,128)S(1)}, u32[]{:S(2)}, u32[]{:S(2)}) collective-permute-start(f32[256,1536]{1,0:T(8,128)S(1)} %get-tuple-element.95), channel_id=1, source_target_pairs={{0,1},{1,0},{2,3},{3,2},{4,5},{5,4},{6,7},{7,6},{8,9},{9,8},{10,11... | collective-permute-start | bytes 4718600 | tf_op jit(solution)/shard_map/ppermute | solution.py:311
  177.4 13.9 %collective-permute-start.19 = (bf16[128,2048]{1,0:T(8,128)(2,1)S(1)}, bf16[128,2048]{1,0:T(8,128)(2,1)S(1)}, u32[]{:S(2)}, u32[]{:S(2)}) collective-permute-start(bf16[128,2048]{1,0:T(8,128)(2,1)S(1)} %fusion.6), channel_id=1, source_target_pairs={{0,2},{1,3},{2,0},{3,1},{4,6},{5,7},{6,4},{7,5},{8,10},{9,11},{10,... | collective-permute-start | bytes 1572872 | tf_op jit(solution)/shard_map/ppermute | solution.py:311
  188.0 17.6 %collective-permute-start.22 = (f32[256,2048]{1,0:T(8,128)}, f32[256,2048]{1,0:T(8,128)}, u32[]{:S(2)}, u32[]{:S(2)}) collective-permute-start(f32[256,2048]{1,0:T(8,128)} %get-tuple-element.103), channel_id=1, source_target_pairs={{0,1},{1,0},{2,3},{3,2},{4,5},{5,4},{6,7},{7,6},{8,9},{9,8},{10,11... | collective-permute-start | bytes 6291464 | tf_op jit(solution)/shard_map/ppermute | solution.py:311
  188.0 6.0 %copy-start.1 = (bf16[512,2048]{1,0:T(8,128)(2,1)S(1)}, bf16[512,2048]{1,0:T(8,128)(2,1)}, u32[]{:S(2)}) copy-start(bf16[512,2048]{1,0:T(8,128)(2,1)} %pad_maximum_fusion.tok_ref) | copy-start | bytes 6291460
  193.5 8.0 %copy-start.23 = (f32[256,1536]{1,0:T(8,128)}, f32[256,1536]{1,0:T(8,128)S(1)}, u32[]{:S(2)}) copy-start(f32[256,1536]{1,0:T(8,128)S(1)} %collective-permute-done.20) | copy-start | bytes 4718596
  193.6 10.4 %collective-permute-start.21 = (bf16[128,1536]{1,0:T(8,128)(2,1)S(1)}, bf16[128,1536]{1,0:T(8,128)(2,1)}, u32[]{:S(2)}, u32[]{:S(2)}) collective-permute-start(bf16[128,1536]{1,0:T(8,128)(2,1)S(1)} %fusion.12), channel_id=1, source_target_pairs={{0,2},{1,3},{2,0},{3,1},{4,6},{5,7},{6,4},{7,5},{8,10},{9,11},{10,... | collective-permute-start | bytes 1179656 | tf_op jit(solution)/shard_map/ppermute | solution.py:311
  201.5 1.2 copy-start.10
  202.7 12.7 %collective-permute-start.23 = (f32[256,1536]{1,0:T(8,128)}, f32[256,1536]{1,0:T(8,128)}, u32[]{:S(2)}, u32[]{:S(2)}) collective-permute-start(f32[256,1536]{1,0:T(8,128)} %get-tuple-element.107), channel_id=1, source_target_pairs={{0,1},{1,0},{2,3},{3,2},{4,5},{5,4},{6,7},{7,6},{8,9},{9,8},{10,11... | collective-permute-start | bytes 4718600 | tf_op jit(solution)/shard_map/ppermute | solution.py:311
  202.7 5.9 %copy-start.3 = (bf16[256,2048]{1,0:T(8,128)(2,1)S(1)}, bf16[256,2048]{1,0:T(8,128)(2,1)}, u32[]{:S(2)}) copy-start(bf16[256,2048]{1,0:T(8,128)(2,1)} %copy-done.2) | copy-start | bytes 3145732
  202.7 5.9 %copy-start.16 = (bf16[512,512]{1,0:T(8,128)(2,1)S(1)}, bf16[512,512]{1,0:T(8,128)(2,1)}, u32[]{:S(2)}) copy-start(bf16[512,512]{1,0:T(8,128)(2,1)} %copy-done.15) | copy-start | bytes 1572868
  207.7 14.7 %collective-permute-start.24 = (bf16[128,2048]{1,0:T(8,128)(2,1)}, bf16[128,2048]{1,0:T(8,128)(2,1)}, u32[]{:S(2)}, u32[]{:S(2)}) collective-permute-start(bf16[128,2048]{1,0:T(8,128)(2,1)} %fusion.3), channel_id=1, source_target_pairs={{0,2},{1,3},{2,0},{3,1},{4,6},{5,7},{6,4},{7,5},{8,10},{9,11},{10,... | collective-permute-start | bytes 1572872 | tf_op jit(solution)/shard_map/ppermute | solution.py:311
  212.7 2.6 %copy-start.11 = (f32[256,1536]{1,0:T(8,128)S(1)}, f32[256,1536]{1,0:T(8,128)}, u32[]{:S(2)}) copy-start(f32[256,1536]{1,0:T(8,128)} %copy-done.10) | copy-start | bytes 4718596
  216.6 16.1 %copy-start.22 = (bf16[128,2048]{1,0:T(8,128)(2,1)S(1)}, bf16[128,2048]{1,0:T(8,128)(2,1)}, u32[]{:S(2)}) copy-start(bf16[128,2048]{1,0:T(8,128)(2,1)} %fusion.5) | copy-start | bytes 1572868
  216.6 14.8 %collective-permute-start.25 = (bf16[128,1536]{1,0:T(8,128)(2,1)S(1)}, bf16[128,1536]{1,0:T(8,128)(2,1)S(1)}, u32[]{:S(2)}, u32[]{:S(2)}) collective-permute-start(bf16[128,1536]{1,0:T(8,128)(2,1)S(1)} %fusion.9), channel_id=1, source_target_pairs={{0,2},{1,3},{2,0},{3,1},{4,6},{5,7},{6,4},{7,5},{8,10},{9,11},{10,... | collective-permute-start | bytes 1179656 | tf_op jit(solution)/shard_map/ppermute | solution.py:311
  220.5 25.2 %collective-permute-start.26 = (bf16[128,2048]{1,0:T(8,128)(2,1)S(1)}, bf16[128,2048]{1,0:T(8,128)(2,1)S(1)}, u32[]{:S(2)}, u32[]{:S(2)}) collective-permute-start(bf16[128,2048]{1,0:T(8,128)(2,1)S(1)} %fusion), channel_id=1, source_target_pairs={{0,0},{5,4},{10,8},{15,12},{4,1},{1,5},{14,9},{11,13},{8,2},{13,6}... | collective-permute-start | bytes 1572872 | tf_op jit(solution)/shard_map/ppermute | solution.py:324

commit v14 on v13

--- a/solution.py
+++ b/solution.py
@@ -333,25 +333,25 @@
 
     near = swap(near, CORE)
     down_x = swap(rest[:rank] + near[rank:], CHIP)
-    even = jnp.concatenate([tokens, after(tok_x, facts, down_x)], axis=0)
+    even = jnp.concatenate([tokens, after(tok_x, facts)], axis=0)
     odd = swap(even, CORE)
     even_far = both(even, hop)
     cot_x = swap(after(cotangent, even), CHIP)
-    grad01, parts, back01 = return_grad(facts, after(cotangent, even), cot_c, weight, adapter_up, (0, 1))
+    grad01, parts, back01 = return_grad(facts, after(cotangent, odd), cot_c, weight, adapter_up, (0, 1))
     toks = [(even, 0), (odd, 0), (even, 1), (odd, 1)]
     inner = rank_inner(facts, down_t.reshape(span, width), [(after(x, grad01), n) for x, n in toks], rank)
     inner_near = along(inner, 1)
-    odd_far = both(after(odd, inner), hop)
+    odd_far = both(odd, hop)
     even_mid = jnp.where(away == 0, even, after(even_far, inner))
     even_all = both(even_mid, hops)
-    cot_xc = swap(after(cot_x, even_mid), CORE)
+    odd_mid = jnp.where(away == 0, odd, after(odd_far, even_mid))
+    odd_all = both(odd_mid, hops)
+    inner = after(inner, even_mid) + inner_near
+    cot_xc = swap(after(cot_x, odd_mid, inner), CORE)
     down_mine = both(rest[rank:] + near[:rank] + after(down_x, inner), place)
-    inner = after(inner, cot_x) + inner_near
     inner_far = along(inner, 2)
-    odd_mid = jnp.where(away == 0, odd, after(odd_far, inner))
-    odd_all = both(odd_mid, hops)
     grad23, parts, back23 = return_grad(
-        facts, after(cot_x, odd_mid, even_all), cot_xc, weight, adapter_up, (2, 3), (parts,)
+        facts, after(cot_x, inner, even_all), cot_xc, weight, adapter_up, (2, 3), (parts,)
     )
     back = jnp.concatenate([back01, back23], axis=1)
     back_near = along(back, 1)

time: 248 us -> 239 us (0.964)
  waiting for transfers between devices: 76.9 us -> 65.7 us
  other arithmetic: 22.3 us -> 25.9 us
    ppermute x17, waiting for transfers between devices: 41.3 us -> 28.1 us  [swap(): return lax.ppermute(x, 'dp', [(d, d ^ bit) for d in range(groups)])]
    ppermute x4, waiting for transfers between devices: 18.7 us -> 14.5 us  [along(): return lax.ppermute(x, 'tp', [(z, z ^ bit) for z in range(shards)])]
    ppermute x6, waiting for transfers between devices: 15.6 us -> 19.3 us  [both(): return lax.ppermute(x, ('tp', 'dp'), pairs)]
    all_to_all x1, waiting for transfers between devices: 1.23 us -> 3.76 us  [local_square(): lax.all_to_all(after(parts, back_b).reshape(shards, rows, depth), 'tp', 0...]
    unnamed x59 -> x49, local copies, waits for them, and re-layouts: 10.9 us -> 11.1 us
  transfers between devices with their start and end apart: 28 -> 28, of which waited for: 13 -> 11; matrix products, arithmetic and copies ran while one was open for 10% -> 12% of each run, Pallas kernels for 33% -> 35%
where the time goes in v14:
time: 239 us; the launch traced here: 237 us
  Pallas kernels  93.6 us (39%)
  waiting for transfers between devices  65.7 us (27%)
  starting transfers between devices  37.3 us (16%)
  other arithmetic  25.9 us (11%)
  local copies, waits for them, and re-layouts  11.2 us (5%)
  matrix products  2.61 us (1%)
    pallas_call x2, Pallas kernels, return_grad(): pl.pallas_call(kernel, grid_spec=pltpu.PrefetchScalarGridSpec(num_scalar_...  40 us
    pallas_call x4, Pallas kernels, project(): pl.pallas_call(kernel, grid=((stop - start) // block,), in_specs=[pl.Bloc...  33.9 us
    ppermute x17, waiting for transfers between devices, swap(): return lax.ppermute(x, 'dp', [(d, d ^ bit) for d in range(groups)])  28.1 us
    ppermute x6, waiting for transfers between devices, both(): return lax.ppermute(x, ('tp', 'dp'), pairs)  19.3 us
    ppermute x6, starting transfers between devices, both(): return lax.ppermute(x, ('tp', 'dp'), pairs)  15.6 us
    ppermute x4, waiting for transfers between devices, along(): return lax.ppermute(x, 'tp', [(z, z ^ bit) for z in range(shards)])  14.5 us
    pallas_call x2, Pallas kernels, slot_grad(): pl.pallas_call(kernel, grid=(columns // block,), in_specs=[pl.BlockSpec((...  13.3 us
    unnamed x49, local copies, waits for them, and re-layouts  11.1 us
  transfers between devices with their start and end apart: 28, of which 11 were waited for; matrix products, arithmetic and copies ran while one was open for 12% of the time, Pallas kernels for 35%

profile of v14, /device:TPU:2, one launch (start us, length us, event | category | flops | bytes accessed | tf_op | source)
XLA Modules:
  0.0 237.3 jit_solution(5874278136901816026)
XLA Ops:
  0.8 1.1 constant_dynamic-update-slice_fusion.1
  2.0 1.6 copy-done.6
  3.6 0.7 copy-done.17
  4.2 0.7 copy-done.18
  5.5 1.5 choose.1
  7.0 7.5 %collective-permute-done = bf16[128,2048]{1,0:T(8,128)(2,1)S(1)} collective-permute-done((bf16[128,2048]{1,0:T(8,128)(2,1)}, bf16[128,2048]{1,0:T(8,128)(2,1)S(1)}, u32[]{:S(2)}, u32[]{:S(2)}) %collective-permute-start) | collective-permute-done | bytes 524320 | tf_op jit(solution)/shard_map/ppermute | solution.py:311
  14.7 1.3 collective-permute-start.1
  16.0 4.8 %collective-permute-start.5 = (bf16[128,7168]{1,0:T(8,128)(2,1)}, bf16[128,7168]{1,0:T(8,128)(2,1)}, u32[]{:S(2)}, u32[]{:S(2)}) collective-permute-start(bf16[128,7168]{1,0:T(8,128)(2,1)} %refs_0_.1), channel_id=1, source_target_pairs={{0,2},{1,3},{2,0},{3,1},{4,6},{5,7},{6,4},{7,5},{8,10},{9,11},{10,... | collective-permute-start | bytes 5505032 | tf_op jit(solution)/shard_map/ppermute | solution.py:311
  20.8 1.3 collective-permute-start.7
  22.2 19.5 %return_grad.2 = (f32[256,2048]{1,0:T(8,128)S(1)}, bf16[512,2048]{1,0:T(8,128)(2,1)}, f32[64,256]{1,0:T(8,128)S(1)}) custom-call(s32[9]{0:T(128)S(1)} %get-tuple-element.57.facts_ref, bf16[128,7168]{1,0:T(8,128)(2,1)} %refs_0_.1, bf16[128,7168]{1,0:T(8,128)(2,1)} %collective-permute-done.3.b_ref.refs_1_, bf16[2048,7168]{1,0:T(8,128)(2,1)} %w_ref.11, ...), custom_call_target="tpu_custom_call" | custom-call | flops 117440512 | bytes 516096 | tf_op jit(solution)/shard_map/return_grad/pallas_call | solution.py:88
  41.6 1.3 copy-done.13
  43.0 1.8 rank_inner.1
  44.8 1.5 collective-permute-start.6
  46.3 8.6 %collective-permute-done.1 = bf16[256,2048]{1,0:T(8,128)(2,1)} collective-permute-done((bf16[256,2048]{1,0:T(8,128)(2,1)S(1)}, bf16[256,2048]{1,0:T(8,128)(2,1)}, u32[]{:S(2)}, u32[]{:S(2)}) %collective-permute-start.1) | collective-permute-done | bytes 1048608 | tf_op jit(solution)/shard_map/ppermute | solution.py:324
  55.0 2.3 broadcast_select_fusion.1
  57.3 11.5 %collective-permute-done.6 = f32[64,512]{1,0:T(8,128)S(1)} collective-permute-done((f32[64,512]{1,0:T(8,128)S(1)}, f32[64,512]{1,0:T(8,128)S(1)}, u32[]{:S(2)}, u32[]{:S(2)}) %collective-permute-start.6) | collective-permute-done | bytes 131104 | tf_op jit(solution)/shard_map/ppermute | solution.py:314
  68.8 2.3 broadcast_select_fusion
  71.2 2.4 %collective-permute-start.4 = (bf16[256,2048]{1,0:T(8,128)(2,1)}, bf16[256,2048]{1,0:T(8,128)(2,1)}, u32[]{:S(2)}, u32[]{:S(2)}) collective-permute-start(bf16[256,2048]{1,0:T(8,128)(2,1)} %broadcast_select_fusion.1), channel_id=1, source_target_pairs={{0,4},{8,12},{5,1},{13,9},{10,14},{2,6},{15,11},{7,3},{16,20},{24,... | collective-permute-start | bytes 3145736 | tf_op jit(solution)/shard_map/ppermute | solution.py:324
  73.7 1.0 slice_add_fusion.8
  74.7 7.5 %collective-permute-done.10 = bf16[64,2048]{1,0:T(8,128)(2,1)S(1)} collective-permute-done((bf16[64,2048]{1,0:T(8,128)(2,1)S(1)}, bf16[64,2048]{1,0:T(8,128)(2,1)S(1)}, u32[]{:S(2)}, u32[]{:S(2)}) %collective-permute-start.10) | collective-permute-done | bytes 262176 | tf_op jit(solution)/shard_map/ppermute | solution.py:311
  82.2 2.3 collective-permute-start.12
  84.5 1.0 fusion.13
  85.5 6.4 %collective-permute-start.11 = (bf16[64,2048]{1,0:T(8,128)(2,1)S(1)}, bf16[64,2048]{1,0:T(8,128)(2,1)S(1)}, u32[]{:S(2)}, u32[]{:S(2)}) collective-permute-start(bf16[64,2048]{1,0:T(8,128)(2,1)S(1)} %fusion.13), channel_id=1, source_target_pairs={{0,0},{4,5},{8,10},{12,15},{1,4},{5,1},{9,14},{13,11},{2,8},{6,13}... | collective-permute-start | bytes 786440 | tf_op jit(solution)/shard_map/ppermute | solution.py:324
  92.0 20.5 %return_grad.3 = (f32[256,2048]{1,0:T(8,128)S(1)}, bf16[512,2048]{1,0:T(8,128)(2,1)}, f32[64,256]{1,0:T(8,128)S(1)}) custom-call(s32[9]{0:T(128)S(1)} %get-tuple-element.57.facts_ref, bf16[128,7168]{1,0:T(8,128)(2,1)} %collective-permute-done.5.a_ref.refs_2_, ...), custom_call_target="tpu_custom_call", output_to_operand_aliasing={{1}: (6, {})} | custom-call | flops 117440512 | bytes 516096 | tf_op jit(solution)/shard_map/return_grad/pallas_call | solution.py:88
  112.6 2.2 select_select_fusion.1
  114.8 1.5 select_select_fusion
  116.3 1.6 pad_maximum_fusion.tok_ref
  117.9 1.4 spread.2
  119.3 10.4 %slot_grad.2 = f32[512,7168]{1,0:T(8,128)} custom-call(bf16[512,512]{1,0:T(8,128)(2,1)S(1)} %get-tuple-element.81.wide_ref, bf16[128,7168]{1,0:T(8,128)(2,1)} %refs_0_.1, bf16[128,7168]{1,0:T(8,128)(2,1)} %collective-permute-done.3.b_ref.refs_1_, bf16[128,7168]{1,0:T(8,128)(2,1)} %collective-permute-done.5.a_ref.refs_2_, ...), custom_call_target="tpu_custom_call" | custom-call | flops 3758096384 | bytes 22020096 | tf_op jit(solution)/shard_map/slot_grad/pallas_call | solution.py:212
  129.7 3.0 %collective-permute-start.15 = (f32[64,512]{1,0:T(8,128)S(1)}, f32[64,512]{1,0:T(8,128)S(1)}, u32[]{:S(2)}, u32[]{:S(2)}) collective-permute-start(f32[64,512]{1,0:T(8,128)S(1)} %add.90.refs_0_), channel_id=1, source_target_pairs={{0,8},{4,12},{8,0},{12,4},{1,9},{5,13},{9,1},{13,5},{2,10},{6,14},... | collective-permute-start | bytes 393224 | tf_op jit(solution)/shard_map/ppermute | solution.py:314
  132.7 3.0 %collective-permute-done.15.refs_1_ = f32[64,512]{1,0:T(8,128)S(1)} collective-permute-done((f32[64,512]{1,0:T(8,128)S(1)}, f32[64,512]{1,0:T(8,128)S(1)}, u32[]{:S(2)}, u32[]{:S(2)}) %collective-permute-start.15) | collective-permute-done | bytes 131104 | tf_op jit(solution)/shard_map/ppermute | solution.py:314
  135.6 1.7 spread.3
  137.3 0.8 copy-done.15
  138.1 1.3 collective-permute-done.16
  139.4 9.9 %project.4 = (f32[256,2048]{1,0:T(8,128)S(1)}, f32[256,2048]{1,0:T(8,128)}) custom-call(bf16[512,2048]{1,0:T(8,128)(2,1)} %pad_maximum_fusion.tok_ref, bf16[512,512]{1,0:T(8,128)(2,1)S(1)} %get-tuple-element.80.wide_ref, bf16[2048,7168]{1,0:T(8,128)(2,1)} %w_ref.11, bf16[512,7168]{1,0:T(8,128)(2,1)} %bitcast.23), custom_call_target="tpu_custom_call" | custom-call | flops 83886080 | bytes 229376 | tf_op jit(solution)/shard_map/project/pallas_call | solution.py:39
  149.3 1.3 copy-done.8
  150.7 6.6 %all-to-all-start = ((bf16[4,128,2048]{2,1,0:T(8,128)(2,1)}), bf16[4,128,2048]{2,1,0:T(8,128)(2,1)}, u32[]{:S(2)}, u32[]{:S(2)}) async-start(bf16[4,128,2048]{2,1,0:T(8,128)(2,1)} %bitcast.28), calls=%async_computation | async-start | bytes 4194304 | tf_op jit(solution)/shard_map/all_to_all | solution.py:366
  157.3 1.1 collective-permute-start.18
  158.5 1.0 copy-done.5
  159.5 6.7 %project.5 = (f32[256,1536]{1,0:T(8,128)S(1)}, f32[256,1536]{1,0:T(8,128)S(1)}) custom-call(bf16[512,2048]{1,0:T(8,128)(2,1)S(1)} %copy-done, bf16[512,512]{1,0:T(8,128)(2,1)S(1)} %copy-done.5, bf16[2048,7168]{1,0:T(8,128)(2,1)} %w_ref.11, bf16[512,7168]{1,0:T(8,128)(2,1)} %bitcast.24), custom_call_target="tpu_custom_call" | custom-call | flops 62914560 | bytes 172032 | tf_op jit(solution)/shard_map/project/pallas_call | solution.py:39
  166.4 1.8 fusion.6
  168.2 0.9 collective-permute-start.19
  169.8 9.9 %project.6 = (f32[256,2048]{1,0:T(8,128)S(1)}, f32[256,2048]{1,0:T(8,128)}) custom-call(bf16[512,2048]{1,0:T(8,128)(2,1)} %pad_maximum_fusion.tok_ref, bf16[512,512]{1,0:T(8,128)(2,1)S(1)} %copy-done.5, bf16[2048,7168]{1,0:T(8,128)(2,1)} %w_ref.11, bf16[512,7168]{1,0:T(8,128)(2,1)} %bitcast.25), custom_call_target="tpu_custom_call" | custom-call | flops 83886080 | bytes 229376 | tf_op jit(solution)/shard_map/project/pallas_call | solution.py:39
  179.7 2.5 %collective-permute-done.19 = bf16[128,2048]{1,0:T(8,128)(2,1)S(1)} collective-permute-done((bf16[128,2048]{1,0:T(8,128)(2,1)S(1)}, bf16[128,2048]{1,0:T(8,128)(2,1)S(1)}, u32[]{:S(2)}, u32[]{:S(2)}) %collective-permute-start.19) | collective-permute-done | bytes 524320 | tf_op jit(solution)/shard_map/ppermute | solution.py:311
  182.1 2.2 fusion.5
  184.4 0.9 collective-permute-start.21
  185.3 7.5 %project.7 = (f32[256,1536]{1,0:T(8,128)S(1)}, f32[256,1536]{1,0:T(8,128)}) custom-call(bf16[512,2048]{1,0:T(8,128)(2,1)S(1)} %copy-done.1, bf16[512,512]{1,0:T(8,128)(2,1)S(1)} %copy-done.5, bf16[2048,7168]{1,0:T(8,128)(2,1)} %w_ref.11, bf16[512,7168]{1,0:T(8,128)(2,1)} %bitcast.26), custom_call_target="tpu_custom_call" | custom-call | flops 62914560 | bytes 172032 | tf_op jit(solution)/shard_map/project/pallas_call | solution.py:39
  192.8 1.1 copy-done.10
  193.9 1.0 collective-permute-done.21
  194.9 1.6 fusion.11
  196.5 2.1 fusion.3
  198.6 0.8 collective-permute-start.24
  199.5 2.9 %slot_grad.3 = f32[512,2048]{1,0:T(8,128)} custom-call(bf16[512,512]{1,0:T(8,128)(2,1)S(1)} %copy-done.16, bf16[256,2048]{1,0:T(8,128)(2,1)S(1)} %constant_dynamic-update-slice_fusion.refs_0_.refs_2_, bf16[256,2048]{1,0:T(8,128)(2,1)S(1)} %copy-done.3, bf16[256,2048]{1,0:T(8,128)(2,1)S(1)} %constant_dynamic-update-slice_fusion.refs_0_.refs_2_, ...), custom_call_target="tpu_custom_call" | custom-call | flops 1073741824 | bytes 6291456 | tf_op jit(solution)/shard_map/slot_grad/pallas_call | solution.py:212
  202.4 3.8 %all-to-all-done = bf16[4,128,2048]{2,1,0:T(8,128)(2,1)} async-done(((bf16[4,128,2048]{2,1,0:T(8,128)(2,1)}), bf16[4,128,2048]{2,1,0:T(8,128)(2,1)}, u32[]{:S(2)}, u32[]{:S(2)}) %all-to-all-start) | async-done | bytes 2097184 | tf_op jit(solution)/shard_map/all_to_all | solution.py:366
  206.2 2.6 %fusion = bf16[128,2048]{1,0:T(8,128)(2,1)S(1)} fusion(bf16[64,2048]{1,0:T(8,128)(2,1)} %copy-done.22, f32[256,2048]{1,0:T(8,128)} %copy-done.14, s32[]{:T(128)S(6)} %select_n.64, f32[256,2048]{1,0:T(8,128)} %copy-done.13, bf16[4,128,2048]{2,1,0:T(8,128)(2,1)} %all-to-all-done, s32[]{:T(128)S(6)} %select_n.68, s32[]{:T(128)S(6)} %select_n.67, ...), kind=kOutput, calls=%fused_computation.1 | convolution fusion | flops 35913728 | bytes 4472853 | tf_op jit(solution)/shard_map/dot_general | solution.py:18
  208.8 1.3 fusion.9
  210.1 1.2 collective-permute-start.25
  211.3 1.9 collective-permute-start.26
  213.2 1.5 fusion.2
  214.7 8.4 %collective-permute-done.25 = bf16[128,1536]{1,0:T(8,128)(2,1)S(1)} collective-permute-done((bf16[128,1536]{1,0:T(8,128)(2,1)S(1)}, bf16[128,1536]{1,0:T(8,128)(2,1)S(1)}, u32[]{:S(2)}, u32[]{:S(2)}) %collective-permute-start.25) | collective-permute-done | bytes 393248 | tf_op jit(solution)/shard_map/ppermute | solution.py:311
  223.1 1.3 fusion.8
  224.4 1.4 pad_maximum_fusion.1
  225.8 10.7 %collective-permute-done.26 = bf16[128,2048]{1,0:T(8,128)(2,1)S(1)} collective-permute-done((bf16[128,2048]{1,0:T(8,128)(2,1)S(1)}, bf16[128,2048]{1,0:T(8,128)(2,1)S(1)}, u32[]{:S(2)}, u32[]{:S(2)}) %collective-permute-start.26) | collective-permute-done | bytes 524320 | tf_op jit(solution)/shard_map/ppermute | solution.py:324
  236.5 0.8 copy.17
  (79 shorter events, 2.5 us)
Async XLA Ops:
  0.6 13.9 %collective-permute-start = (bf16[128,2048]{1,0:T(8,128)(2,1)}, bf16[128,2048]{1,0:T(8,128)(2,1)S(1)}, u32[]{:S(2)}, u32[]{:S(2)}) collective-permute-start(bf16[128,2048]{1,0:T(8,128)(2,1)} %param.8), channel_id=1, source_target_pairs={{0,2},{1,3},{2,0},{3,1},{4,6},{5,7},{6,4},{7,5},{8,10},{9,11},{10,... | collective-permute-start | bytes 1572872 | tf_op jit(solution)/shard_map/ppermute | solution.py:311
  0.7 21.4 %collective-permute-start.3 = (bf16[128,7168]{1,0:T(8,128)(2,1)}, bf16[128,7168]{1,0:T(8,128)(2,1)}, u32[]{:S(2)}, u32[]{:S(2)}) collective-permute-start(bf16[128,7168]{1,0:T(8,128)(2,1)} %refs_0_.1), channel_id=1, source_target_pairs={{0,1},{1,0},{2,3},{3,2},{4,5},{5,4},{6,7},{7,6},{8,9},{9,8},{10,11... | collective-permute-start | bytes 5505032 | tf_op jit(solution)/shard_map/ppermute | solution.py:311
  2.0 1.6 copy-start.6
  3.6 0.7 copy-start.17
  4.2 0.7 copy-start.18
  4.9 0.7 copy-start.19
  14.6 6.1 %collective-permute-start.2 = (bf16[256,2048]{1,0:T(8,128)(2,1)S(1)}, bf16[256,2048]{1,0:T(8,128)(2,1)S(1)}, u32[]{:S(2)}, u32[]{:S(2)}) collective-permute-start(bf16[256,2048]{1,0:T(8,128)(2,1)S(1)} %constant_dynamic-update-slice_fusion.refs_0_.refs_2_), channel_id=1, source_target_pairs={{0,1},{1,0},{2,3},{3,2},{4,5},{5,4},{6,7},{7,6},{8,9},{9,8},{10,11... | collective-permute-start | bytes 3145736 | tf_op jit(solution)/shard_map/ppermute | solution.py:311
  14.7 40.3 %collective-permute-start.1 = (bf16[256,2048]{1,0:T(8,128)(2,1)S(1)}, bf16[256,2048]{1,0:T(8,128)(2,1)}, u32[]{:S(2)}, u32[]{:S(2)}) collective-permute-start(bf16[256,2048]{1,0:T(8,128)(2,1)S(1)} %constant_dynamic-update-slice_fusion.refs_0_.refs_2_), channel_id=1, source_target_pairs={{0,8},{5,13},{10,2},{15,7},{16,24},{21,29},{26,18},{31,23}} | collective-permute-start | bytes 3145736 | tf_op jit(solution)/shard_map/ppermute | solution.py:324
  16.0 55.2 %collective-permute-start.5 = (bf16[128,7168]{1,0:T(8,128)(2,1)}, bf16[128,7168]{1,0:T(8,128)(2,1)}, u32[]{:S(2)}, u32[]{:S(2)}) collective-permute-start(bf16[128,7168]{1,0:T(8,128)(2,1)} %refs_0_.1), channel_id=1, source_target_pairs={{0,2},{1,3},{2,0},{3,1},{4,6},{5,7},{6,4},{7,5},{8,10},{9,11},{10,... | collective-permute-start | bytes 5505032 | tf_op jit(solution)/shard_map/ppermute | solution.py:311
  20.8 94.0 %copy-start.2 = (bf16[256,2048]{1,0:T(8,128)(2,1)}, bf16[256,2048]{1,0:T(8,128)(2,1)S(1)}, u32[]{:S(2)}) copy-start(bf16[256,2048]{1,0:T(8,128)(2,1)S(1)} %collective-permute-done.2.refs_1_.refs_3_) | copy-start | bytes 3145732
  20.8 48.1 %collective-permute-start.7 = (bf16[256,2048]{1,0:T(8,128)(2,1)S(1)}, bf16[256,2048]{1,0:T(8,128)(2,1)}, u32[]{:S(2)}, u32[]{:S(2)}) collective-permute-start(bf16[256,2048]{1,0:T(8,128)(2,1)S(1)} %collective-permute-done.2.refs_1_.refs_3_), channel_id=1, source_target_pairs={{0,8},{5,13},{10,2},{15,7},{16,24},{21,29},{26,18},{31,23}} | collective-permute-start | bytes 3145736 | tf_op jit(solution)/shard_map/ppermute | solution.py:324
  22.0 51.6 %collective-permute-start.9 = (bf16[128,2048]{1,0:T(8,128)(2,1)S(1)}, bf16[128,2048]{1,0:T(8,128)(2,1)}, u32[]{:S(2)}, u32[]{:S(2)}) collective-permute-start(bf16[128,2048]{1,0:T(8,128)(2,1)S(1)} %get-tuple-element.72), channel_id=1, source_target_pairs={{0,1},{1,0},{2,3},{3,2},{4,5},{5,4},{6,7},{7,6},{8,9},{9,8},{10,11... | collective-permute-start | bytes 1572872 | tf_op jit(solution)/shard_map/ppermute | solution.py:311
  22.1 20.8 %copy-start.7 = (bf16[8,2048,64]{1,2,0:T(8,128)(2,1)S(1)}, bf16[8,2048,64]{1,2,0:T(8,128)(2,1)}, u32[]{:S(2)}) copy-start(bf16[8,2048,64]{1,2,0:T(8,128)(2,1)} %param.10) | copy-start | bytes 6291460
  41.6 1.3 copy-start.13
  44.8 24.0 %collective-permute-start.6 = (f32[64,512]{1,0:T(8,128)S(1)}, f32[64,512]{1,0:T(8,128)S(1)}, u32[]{:S(2)}, u32[]{:S(2)}) collective-permute-start(f32[64,512]{1,0:T(8,128)S(1)} %rank_inner.1), channel_id=1, source_target_pairs={{0,4},{4,0},{8,12},{12,8},{1,5},{5,1},{9,13},{13,9},{2,6},{6,2},{1... | collective-permute-start | bytes 393224 | tf_op jit(solution)/shard_map/ppermute | solution.py:314
  71.1 20.9 %collective-permute-start.8 = (bf16[128,7168]{1,0:T(8,128)(2,1)}, bf16[128,7168]{1,0:T(8,128)(2,1)}, u32[]{:S(2)}, u32[]{:S(2)}) collective-permute-start(bf16[128,7168]{1,0:T(8,128)(2,1)} %collective-permute-done.5.a_ref.refs_2_), channel_id=1, source_target_pairs={{0,1},{1,0},{2,3},{3,2},{4,5},{5,4},{6,7},{7,6},{8,9},{9,8},{10,11... | collective-permute-start | bytes 5505032 | tf_op jit(solution)/shard_map/ppermute | solution.py:311
  71.2 20.8 %collective-permute-start.4 = (bf16[256,2048]{1,0:T(8,128)(2,1)}, bf16[256,2048]{1,0:T(8,128)(2,1)}, u32[]{:S(2)}, u32[]{:S(2)}) collective-permute-start(bf16[256,2048]{1,0:T(8,128)(2,1)} %broadcast_select_fusion.1), channel_id=1, source_target_pairs={{0,4},{8,12},{5,1},{13,9},{10,14},{2,6},{15,11},{7,3},{16,20},{24,... | collective-permute-start | bytes 3145736 | tf_op jit(solution)/shard_map/ppermute | solution.py:324
  74.6 7.6 %collective-permute-start.10 = (bf16[64,2048]{1,0:T(8,128)(2,1)S(1)}, bf16[64,2048]{1,0:T(8,128)(2,1)S(1)}, u32[]{:S(2)}, u32[]{:S(2)}) collective-permute-start(bf16[64,2048]{1,0:T(8,128)(2,1)S(1)} %slice_add_fusion.8), channel_id=1, source_target_pairs={{0,2},{1,3},{2,0},{3,1},{4,6},{5,7},{6,4},{7,5},{8,10},{9,11},{10,... | collective-permute-start | bytes 786440 | tf_op jit(solution)/shard_map/ppermute | solution.py:311
  82.2 32.5 %collective-permute-start.12 = (bf16[256,2048]{1,0:T(8,128)(2,1)}, bf16[256,2048]{1,0:T(8,128)(2,1)}, u32[]{:S(2)}, u32[]{:S(2)}) collective-permute-start(bf16[256,2048]{1,0:T(8,128)(2,1)} %broadcast_select_fusion), channel_id=1, source_target_pairs={{0,4},{8,12},{5,1},{13,9},{10,14},{2,6},{15,11},{7,3},{16,20},{24,... | collective-permute-start | bytes 3145736 | tf_op jit(solution)/shard_map/ppermute | solution.py:324
  85.5 27.0 %collective-permute-start.11 = (bf16[64,2048]{1,0:T(8,128)(2,1)S(1)}, bf16[64,2048]{1,0:T(8,128)(2,1)S(1)}, u32[]{:S(2)}, u32[]{:S(2)}) collective-permute-start(bf16[64,2048]{1,0:T(8,128)(2,1)S(1)} %fusion.13), channel_id=1, source_target_pairs={{0,0},{4,5},{8,10},{12,15},{1,4},{5,1},{9,14},{13,11},{2,8},{6,13}... | collective-permute-start | bytes 786440 | tf_op jit(solution)/shard_map/ppermute | solution.py:324
  91.9 25.9 %collective-permute-start.13 = (f32[64,512]{1,0:T(8,128)S(1)}, f32[64,512]{1,0:T(8,128)S(1)}, u32[]{:S(2)}, u32[]{:S(2)}) collective-permute-start(f32[64,512]{1,0:T(8,128)S(1)} %add.86.refs_0_), channel_id=1, source_target_pairs={{0,8},{4,12},{8,0},{12,4},{1,9},{5,13},{9,1},{13,5},{2,10},{6,14},... | collective-permute-start | bytes 393224 | tf_op jit(solution)/shard_map/ppermute | solution.py:314
  112.5 2.2 copy-start.14
  112.6 2.2 copy-start.22
  117.9 11.8 %collective-permute-start.14 = (f32[64,512]{1,0:T(8,128)S(1)}, f32[64,512]{1,0:T(8,128)S(1)}, u32[]{:S(2)}, u32[]{:S(2)}) collective-permute-start(f32[64,512]{1,0:T(8,128)S(1)} %constant_dynamic-update-slice_fusion.2), channel_id=1, source_target_pairs={{0,4},{4,0},{8,12},{12,8},{1,5},{5,1},{9,13},{13,9},{2,6},{6,2},{1... | collective-permute-start | bytes 393224 | tf_op jit(solution)/shard_map/ppermute | solution.py:314
  119.3 20.1 %copy-start.4 = (bf16[512,512]{1,0:T(8,128)(2,1)}, bf16[512,512]{1,0:T(8,128)(2,1)S(1)}, u32[]{:S(2)}) copy-start(bf16[512,512]{1,0:T(8,128)(2,1)S(1)} %get-tuple-element.80.wide_ref) | copy-start | bytes 1572868
  129.7 5.9 %collective-permute-start.15 = (f32[64,512]{1,0:T(8,128)S(1)}, f32[64,512]{1,0:T(8,128)S(1)}, u32[]{:S(2)}, u32[]{:S(2)}) collective-permute-start(f32[64,512]{1,0:T(8,128)S(1)} %add.90.refs_0_), channel_id=1, source_target_pairs={{0,8},{4,12},{8,0},{12,4},{1,9},{5,13},{9,1},{13,5},{2,10},{6,14},... | collective-permute-start | bytes 393224 | tf_op jit(solution)/shard_map/ppermute | solution.py:314
  137.3 0.8 copy-start.15
  138.1 1.3 collective-permute-start.16
  149.3 1.3 copy-start.8
  150.6 15.8 %collective-permute-start.17 = (f32[256,2048]{1,0:T(8,128)}, f32[256,2048]{1,0:T(8,128)}, u32[]{:S(2)}, u32[]{:S(2)}) collective-permute-start(f32[256,2048]{1,0:T(8,128)} %get-tuple-element.89), channel_id=1, source_target_pairs={{0,1},{1,0},{2,3},{3,2},{4,5},{5,4},{6,7},{7,6},{8,9},{9,8},{10,11... | collective-permute-start | bytes 6291464 | tf_op jit(solution)/shard_map/ppermute | solution.py:311
  150.7 7.8 %copy-start = (bf16[512,2048]{1,0:T(8,128)(2,1)S(1)}, bf16[512,2048]{1,0:T(8,128)(2,1)}, u32[]{:S(2)}) copy-start(bf16[512,2048]{1,0:T(8,128)(2,1)} %pad_maximum_fusion.tok_ref) | copy-start | bytes 6291460
  150.7 55.4 %all-to-all-start = ((bf16[4,128,2048]{2,1,0:T(8,128)(2,1)}), bf16[4,128,2048]{2,1,0:T(8,128)(2,1)}, u32[]{:S(2)}, u32[]{:S(2)}) async-start(bf16[4,128,2048]{2,1,0:T(8,128)(2,1)} %bitcast.28), calls=%async_computation | async-start | bytes 4194304 | tf_op jit(solution)/shard_map/all_to_all | solution.py:366
  157.3 11.8 %collective-permute-start.18 = (bf16[64,512]{1,0:T(8,128)(2,1)S(1)}, bf16[64,512]{1,0:T(8,128)(2,1)S(1)}, u32[]{:S(2)}, u32[]{:S(2)}) collective-permute-start(bf16[64,512]{1,0:T(8,128)(2,1)S(1)} %maximum_add_fusion), channel_id=1, source_target_pairs={{0,2},{1,3},{2,0},{3,1},{4,6},{5,7},{6,4},{7,5},{8,10},{9,11},{10,... | collective-permute-start | bytes 196616 | tf_op jit(solution)/shard_map/ppermute | solution.py:311
  158.5 1.0 copy-start.5
  159.5 6.9 %copy-start.9 = (f32[256,2048]{1,0:T(8,128)S(1)}, f32[256,2048]{1,0:T(8,128)}, u32[]{:S(2)}) copy-start(f32[256,2048]{1,0:T(8,128)} %copy-done.8) | copy-start | bytes 6291460
  166.3 18.0 %copy-start.12 = (f32[256,1536]{1,0:T(8,128)}, f32[256,1536]{1,0:T(8,128)S(1)}, u32[]{:S(2)}) copy-start(f32[256,1536]{1,0:T(8,128)S(1)} %get-tuple-element.98) | copy-start | bytes 4718596
  166.3 18.0 %collective-permute-start.20 = (f32[256,1536]{1,0:T(8,128)S(1)}, f32[256,1536]{1,0:T(8,128)S(1)}, u32[]{:S(2)}, u32[]{:S(2)}) collective-permute-start(f32[256,1536]{1,0:T(8,128)S(1)} %get-tuple-element.95), channel_id=1, source_target_pairs={{0,1},{1,0},{2,3},{3,2},{4,5},{5,4},{6,7},{7,6},{8,9},{9,8},{10,11... | collective-permute-start | bytes 4718600 | tf_op jit(solution)/shard_map/ppermute | solution.py:311
  168.2 13.9 %collective-permute-start.19 = (bf16[128,2048]{1,0:T(8,128)(2,1)S(1)}, bf16[128,2048]{1,0:T(8,128)(2,1)S(1)}, u32[]{:S(2)}, u32[]{:S(2)}) collective-permute-start(bf16[128,2048]{1,0:T(8,128)(2,1)S(1)} %fusion.6), channel_id=1, source_target_pairs={{0,2},{1,3},{2,0},{3,1},{4,6},{5,7},{6,4},{7,5},{8,10},{9,11},{10,... | collective-permute-start | bytes 1572872 | tf_op jit(solution)/shard_map/ppermute | solution.py:311
  179.6 16.9 %collective-permute-start.22 = (f32[256,2048]{1,0:T(8,128)}, f32[256,2048]{1,0:T(8,128)}, u32[]{:S(2)}, u32[]{:S(2)}) collective-permute-start(f32[256,2048]{1,0:T(8,128)} %get-tuple-element.103), channel_id=1, source_target_pairs={{0,1},{1,0},{2,3},{3,2},{4,5},{5,4},{6,7},{7,6},{8,9},{9,8},{10,11... | collective-permute-start | bytes 6291464 | tf_op jit(solution)/shard_map/ppermute | solution.py:311
  179.6 5.7 %copy-start.1 = (bf16[512,2048]{1,0:T(8,128)(2,1)S(1)}, bf16[512,2048]{1,0:T(8,128)(2,1)}, u32[]{:S(2)}) copy-start(bf16[512,2048]{1,0:T(8,128)(2,1)} %pad_maximum_fusion.tok_ref) | copy-start | bytes 6291460
  184.3 8.5 %copy-start.21 = (f32[256,1536]{1,0:T(8,128)}, f32[256,1536]{1,0:T(8,128)S(1)}, u32[]{:S(2)}) copy-start(f32[256,1536]{1,0:T(8,128)S(1)} %collective-permute-done.20) | copy-start | bytes 4718596
  184.4 10.5 %collective-permute-start.21 = (bf16[128,1536]{1,0:T(8,128)(2,1)S(1)}, bf16[128,1536]{1,0:T(8,128)(2,1)}, u32[]{:S(2)}, u32[]{:S(2)}) collective-permute-start(bf16[128,1536]{1,0:T(8,128)(2,1)S(1)} %fusion.12), channel_id=1, source_target_pairs={{0,2},{1,3},{2,0},{3,1},{4,6},{5,7},{6,4},{7,5},{8,10},{9,11},{10,... | collective-permute-start | bytes 1179656 | tf_op jit(solution)/shard_map/ppermute | solution.py:311
  192.8 1.1 copy-start.10
  193.9 14.9 %collective-permute-start.23 = (f32[256,1536]{1,0:T(8,128)}, f32[256,1536]{1,0:T(8,128)}, u32[]{:S(2)}, u32[]{:S(2)}) collective-permute-start(f32[256,1536]{1,0:T(8,128)} %get-tuple-element.107), channel_id=1, source_target_pairs={{0,1},{1,0},{2,3},{3,2},{4,5},{5,4},{6,7},{7,6},{8,9},{9,8},{10,11... | collective-permute-start | bytes 4718600 | tf_op jit(solution)/shard_map/ppermute | solution.py:311
  193.9 5.5 %copy-start.3 = (bf16[256,2048]{1,0:T(8,128)(2,1)S(1)}, bf16[256,2048]{1,0:T(8,128)(2,1)}, u32[]{:S(2)}) copy-start(bf16[256,2048]{1,0:T(8,128)(2,1)} %copy-done.2) | copy-start | bytes 3145732
  193.9 5.5 %copy-start.16 = (bf16[512,512]{1,0:T(8,128)(2,1)S(1)}, bf16[512,512]{1,0:T(8,128)(2,1)}, u32[]{:S(2)}) copy-start(bf16[512,512]{1,0:T(8,128)(2,1)} %copy-done.15) | copy-start | bytes 1572868
  198.6 14.5 %collective-permute-start.24 = (bf16[128,2048]{1,0:T(8,128)(2,1)}, bf16[128,2048]{1,0:T(8,128)(2,1)}, u32[]{:S(2)}, u32[]{:S(2)}) collective-permute-start(bf16[128,2048]{1,0:T(8,128)(2,1)} %fusion.3), channel_id=1, source_target_pairs={{0,2},{1,3},{2,0},{3,1},{4,6},{5,7},{6,4},{7,5},{8,10},{9,11},{10,... | collective-permute-start | bytes 1572872 | tf_op jit(solution)/shard_map/ppermute | solution.py:311
  206.2 2.6 %copy-start.11 = (f32[256,1536]{1,0:T(8,128)S(1)}, f32[256,1536]{1,0:T(8,128)}, u32[]{:S(2)}) copy-start(f32[256,1536]{1,0:T(8,128)} %copy-done.10) | copy-start | bytes 4718596
  210.1 14.4 %copy-start.20 = (bf16[128,2048]{1,0:T(8,128)(2,1)S(1)}, bf16[128,2048]{1,0:T(8,128)(2,1)}, u32[]{:S(2)}) copy-start(bf16[128,2048]{1,0:T(8,128)(2,1)} %fusion.5) | copy-start | bytes 1572868
  210.1 13.1 %collective-permute-start.25 = (bf16[128,1536]{1,0:T(8,128)(2,1)S(1)}, bf16[128,1536]{1,0:T(8,128)(2,1)S(1)}, u32[]{:S(2)}, u32[]{:S(2)}) collective-permute-start(bf16[128,1536]{1,0:T(8,128)(2,1)S(1)} %fusion.9), channel_id=1, source_target_pairs={{0,2},{1,3},{2,0},{3,1},{4,6},{5,7},{6,4},{7,5},{8,10},{9,11},{10,... | collective-permute-start | bytes 1179656 | tf_op jit(solution)/shard_map/ppermute | solution.py:311
  211.3 25.2 %collective-permute-start.26 = (bf16[128,2048]{1,0:T(8,128)(2,1)S(1)}, bf16[128,2048]{1,0:T(8,128)(2,1)S(1)}, u32[]{:S(2)}, u32[]{:S(2)}) collective-permute-start(bf16[128,2048]{1,0:T(8,128)(2,1)S(1)} %fusion), channel_id=1, source_target_pairs={{0,0},{5,4},{10,8},{15,12},{4,1},{1,5},{14,9},{11,13},{8,2},{13,6}... | collective-permute-start | bytes 1572872 | tf_op jit(solution)/shard_map/ppermute | solution.py:324

commit v15 on v14

--- a/solution.py
+++ b/solution.py
@@ -332,7 +332,6 @@
     up_flat = adapter_up.reshape(span, hidden)
 
     near = swap(near, CORE)
-    down_x = swap(rest[:rank] + near[rank:], CHIP)
     even = jnp.concatenate([tokens, after(tok_x, facts)], axis=0)
     odd = swap(even, CORE)
     even_far = both(even, hop)
@@ -344,25 +343,27 @@
     odd_far = both(odd, hop)
     even_mid = jnp.where(away == 0, even, after(even_far, inner))
     even_all = both(even_mid, hops)
-    odd_mid = jnp.where(away == 0, odd, after(odd_far, even_mid))
+    inner = after(inner, even_mid) + inner_near
+    cot_xc = swap(after(cot_x, inner), CORE)
+    inner_far = along(inner, 2)
+    down_x = swap(rest[:rank] + after(near, cot_x)[rank:], CHIP)
+    grad23, parts, back23 = return_grad(
+        facts, after(cot_x, inner), cot_xc, weight, adapter_up, (2, 3), (parts,)
+    )
+    odd_mid = jnp.where(away == 0, odd, after(odd_far, grad23))
     odd_all = both(odd_mid, hops)
-    inner = after(inner, even_mid) + inner_near
-    cot_xc = swap(after(cot_x, odd_mid, inner), CORE)
-    down_mine = both(rest[rank:] + near[:rank] + after(down_x, inner), place)
-    inner_far = along(inner, 2)
-    grad23, parts, back23 = return_grad(
-        facts, after(cot_x, inner, even_all), cot_xc, weight, adapter_up, (2, 3), (parts,)
-    )
     back = jnp.concatenate([back01, back23], axis=1)
     back_near = along(back, 1)
-    all_even = jnp.where(away == 0, even, jnp.where(away == 2, even_far, after(even_all, grad23, down_mine)))
-    all_odd = jnp.where(away == 0, odd, jnp.where(away == 2, odd_far, after(odd_all, all_even)))
-    all_tokens = jnp.concatenate([all_even, all_odd], axis=0)
-    inner_wide, inner_rows, _ = spread(facts, after(inner, all_tokens), inner_far, per_owner, adapter_scale)
+    all_even = jnp.where(away == 0, even, jnp.where(away == 2, even_far, after(even_all, odd_mid)))
+    inner_wide, inner_rows, _ = spread(facts, after(inner, all_even), inner_far, per_owner, adapter_scale)
     cots = [([x], 0) for x in (cotangent, cot_c, cot_x, cot_xc)]
     up_wide = slot_grad(after(inner_wide, inner_rows), cots, hidden // 4)
-    back = after(back, up_wide) + back_near
-    back_wide, _, back_b = spread(facts, back, along(back, 2), per_owner, 1.0)
+    down_mine = both(rest[rank:] + near[:rank] + after(down_x, inner_rows), place)
+    back = after(back, up_wide, down_mine) + back_near
+    back_far = along(back, 2)
+    all_odd = jnp.where(away == 0, odd, jnp.where(away == 2, odd_far, after(odd_all, back)))
+    all_tokens = jnp.concatenate([all_even, all_odd], axis=0)
+    back_wide, _, back_b = spread(facts, after(back, all_tokens), back_far, per_owner, 1.0)
     parts = lax.all_to_all(after(parts, back_b).reshape(shards, rows, depth), "tp", 0, 0, tiled=True)
     back_b = share(back_b, swap(back_b, CORE), CORE)
 

time: 239 us -> 221 us (0.925)
  waiting for transfers between devices: 65.7 us -> 53.4 us
  starting transfers between devices: 37.3 us -> 34.4 us
    ppermute x4, waiting for transfers between devices: 14.5 us -> 3.3 us  [along(): return lax.ppermute(x, 'tp', [(z, z ^ bit) for z in range(shards)])]
    ppermute x6, waiting for transfers between devices: 19.3 us -> 15.1 us  [both(): return lax.ppermute(x, ('tp', 'dp'), pairs)]
    ppermute x17, waiting for transfers between devices: 28.1 us -> 31.3 us  [swap(): return lax.ppermute(x, 'dp', [(d, d ^ bit) for d in range(groups)])]
    ppermute x4, starting transfers between devices: 4.58 us -> 7.43 us  [along(): return lax.ppermute(x, 'tp', [(z, z ^ bit) for z in range(shards)])]
    ppermute x17, starting transfers between devices: 10.5 us -> 8.07 us  [swap(): return lax.ppermute(x, 'dp', [(d, d ^ bit) for d in range(groups)])]
    unnamed x49 -> x51, local copies, waits for them, and re-layouts: 11.1 us -> 10.8 us
  transfers between devices with their start and end apart: 28 -> 28, of which waited for: 11 -> 14; matrix products, arithmetic and copies ran while one was open for 12% -> 12% of each run, Pallas kernels for 35% -> 37%
where the time goes in v15:
time: 221 us; the launch traced here: 220 us
  Pallas kernels  93.2 us (42%)
  waiting for transfers between devices  53.4 us (24%)
  starting transfers between devices  34.4 us (16%)
  other arithmetic  24.3 us (11%)
  local copies, waits for them, and re-layouts  10.9 us (5%)
  matrix products  2.61 us (1%)
    pallas_call x2, Pallas kernels, return_grad(): pl.pallas_call(kernel, grid_spec=pltpu.PrefetchScalarGridSpec(num_scalar_...  39.8 us
    pallas_call x4, Pallas kernels, project(): pl.pallas_call(kernel, grid=((stop - start) // block,), in_specs=[pl.Bloc...  33.9 us
    ppermute x17, waiting for transfers between devices, swap(): return lax.ppermute(x, 'dp', [(d, d ^ bit) for d in range(groups)])  31.3 us
    ppermute x6, waiting for transfers between devices, both(): return lax.ppermute(x, ('tp', 'dp'), pairs)  15.1 us
    ppermute x6, starting transfers between devices, both(): return lax.ppermute(x, ('tp', 'dp'), pairs)  14.1 us
    pallas_call x2, Pallas kernels, slot_grad(): pl.pallas_call(kernel, grid=(columns // block,), in_specs=[pl.BlockSpec((...  13.2 us
    unnamed x51, local copies, waits for them, and re-layouts  10.8 us
    ppermute x17, starting transfers between devices, swap(): return lax.ppermute(x, 'dp', [(d, d ^ bit) for d in range(groups)])  8.07 us
  transfers between devices with their start and end apart: 28, of which 14 were waited for; matrix products, arithmetic and copies ran while one was open for 12% of the time, Pallas kernels for 37%

profile of v15, /device:TPU:2, one launch (start us, length us, event | category | flops | bytes accessed | tf_op | source)
XLA Modules:
  0.0 219.8 jit_solution(5651871882618851369)
XLA Ops:
  0.9 1.6 copy-done.6
  4.4 1.5 choose.1
  6.0 8.6 %collective-permute-done = bf16[128,2048]{1,0:T(8,128)(2,1)S(1)} collective-permute-done((bf16[128,2048]{1,0:T(8,128)(2,1)}, bf16[128,2048]{1,0:T(8,128)(2,1)S(1)}, u32[]{:S(2)}, u32[]{:S(2)}) %collective-permute-start) | collective-permute-done | bytes 524320 | tf_op jit(solution)/shard_map/ppermute | solution.py:311
  15.0 1.3 collective-permute-start.1
  16.3 1.4 collective-permute-done.2.refs_1_.refs_3_
  17.6 19.4 %return_grad.2 = (f32[256,2048]{1,0:T(8,128)S(1)}, bf16[512,2048]{1,0:T(8,128)(2,1)}, f32[64,256]{1,0:T(8,128)S(1)}) custom-call(s32[9]{0:T(128)S(1)} %get-tuple-element.58.facts_ref, bf16[128,7168]{1,0:T(8,128)(2,1)} %refs_0_.1, bf16[128,7168]{1,0:T(8,128)(2,1)} %collective-permute-done.3.b_ref.refs_1_, bf16[2048,7168]{1,0:T(8,128)(2,1)} %w_ref.11, ...), custom_call_target="tpu_custom_call" | custom-call | flops 117440512 | bytes 516096 | tf_op jit(solution)/shard_map/return_grad/pallas_call | solution.py:88
  37.1 1.4 copy-done.13
  38.4 1.8 rank_inner.1
  40.3 1.9 collective-permute-start.7
  42.2 1.7 collective-permute-done.1
  43.9 2.3 %broadcast_select_fusion.1 = bf16[256,2048]{1,0:T(8,128)(2,1)} fusion(bf16[256,2048]{1,0:T(8,128)(2,1)S(1)} %constant_dynamic-update-slice_fusion.refs_0_.refs_2_, bf16[256,2048]{1,0:T(8,128)(2,1)} %collective-permute-done.1, pred[]{:T(512)S(6)} %eq.4), kind=kLoop, calls=%fused_computation.20 | loop fusion | flops 524288 | bytes 3145729 | tf_op jit(solution)/shard_map/jit(_where)/select_n | solution.py:344
  46.5 9.4 %collective-permute-done.6.a_ref.refs_2_ = bf16[128,7168]{1,0:T(8,128)(2,1)} collective-permute-done((bf16[128,7168]{1,0:T(8,128)(2,1)}, bf16[128,7168]{1,0:T(8,128)(2,1)}, u32[]{:S(2)}, u32[]{:S(2)}) %collective-permute-start.6) | collective-permute-done | bytes 1835040 | tf_op jit(solution)/shard_map/ppermute | solution.py:311
  55.9 1.3 collective-permute-start.5
  57.2 0.9 collective-permute-start.11
  58.0 3.2 %collective-permute-start.4 = (bf16[256,2048]{1,0:T(8,128)(2,1)}, bf16[256,2048]{1,0:T(8,128)(2,1)S(1)}, u32[]{:S(2)}, u32[]{:S(2)}) collective-permute-start(bf16[256,2048]{1,0:T(8,128)(2,1)} %broadcast_select_fusion.1), channel_id=1, source_target_pairs={{0,4},{8,12},{5,1},{13,9},{10,14},{2,6},{15,11},{7,3},{16,20},{24,... | collective-permute-start | bytes 3145736 | tf_op jit(solution)/shard_map/ppermute | solution.py:324
  61.3 4.3 %collective-permute-start.10 = (f32[64,512]{1,0:T(8,128)S(1)}, f32[64,512]{1,0:T(8,128)S(1)}, u32[]{:S(2)}, u32[]{:S(2)}) collective-permute-start(f32[64,512]{1,0:T(8,128)S(1)} %add.86.refs_0_), channel_id=1, source_target_pairs={{0,8},{4,12},{8,0},{12,4},{1,9},{5,13},{9,1},{13,5},{2,10},{6,14},... | collective-permute-start | bytes 393224 | tf_op jit(solution)/shard_map/ppermute | solution.py:314
  65.6 1.0 slice_add_fusion.9
  66.8 20.3 %return_grad.3 = (f32[256,2048]{1,0:T(8,128)S(1)}, bf16[512,2048]{1,0:T(8,128)(2,1)}, f32[64,256]{1,0:T(8,128)S(1)}) custom-call(s32[9]{0:T(128)S(1)} %get-tuple-element.58.facts_ref, bf16[128,7168]{1,0:T(8,128)(2,1)} %collective-permute-done.6.a_ref.refs_2_, ...), custom_call_target="tpu_custom_call", output_to_operand_aliasing={{1}: (6, {})} | custom-call | flops 117440512 | bytes 516096 | tf_op jit(solution)/shard_map/return_grad/pallas_call | solution.py:88
  87.2 1.9 collective-permute-done.5
  89.1 1.3 broadcast_select_fusion
  90.4 4.0 %collective-permute-start.9 = (bf16[256,2048]{1,0:T(8,128)(2,1)S(1)}, bf16[256,2048]{1,0:T(8,128)(2,1)S(1)}, u32[]{:S(2)}, u32[]{:S(2)}) collective-permute-start(bf16[256,2048]{1,0:T(8,128)(2,1)S(1)} %broadcast_select_fusion), channel_id=1, source_target_pairs={{0,4},{8,12},{5,1},{13,9},{10,14},{2,6},{15,11},{7,3},{16,20},{24,... | collective-permute-start | bytes 3145736 | tf_op jit(solution)/shard_map/ppermute | solution.py:324
  94.4 1.4 select_select_fusion.1
  95.8 1.4 spread.2
  97.2 1.2 fusion.13
  98.4 2.4 %collective-permute-start.13 = (bf16[64,2048]{1,0:T(8,128)(2,1)S(1)}, bf16[64,2048]{1,0:T(8,128)(2,1)S(1)}, u32[]{:S(2)}, u32[]{:S(2)}) collective-permute-start(bf16[64,2048]{1,0:T(8,128)(2,1)S(1)} %fusion.13), channel_id=1, source_target_pairs={{0,0},{4,5},{8,10},{12,15},{1,4},{5,1},{9,14},{13,11},{2,8},{6,13}... | collective-permute-start | bytes 786440 | tf_op jit(solution)/shard_map/ppermute | solution.py:324
  100.8 10.2 %slot_grad.2 = f32[512,7168]{1,0:T(8,128)} custom-call(bf16[512,512]{1,0:T(8,128)(2,1)S(1)} %get-tuple-element.77.wide_ref, bf16[128,7168]{1,0:T(8,128)(2,1)} %refs_0_.1, bf16[128,7168]{1,0:T(8,128)(2,1)} %collective-permute-done.3.b_ref.refs_1_, bf16[128,7168]{1,0:T(8,128)(2,1)} %collective-permute-done.6.a_ref.refs_2_, ...), custom_call_target="tpu_custom_call" | custom-call | flops 3758096384 | bytes 22020096 | tf_op jit(solution)/shard_map/slot_grad/pallas_call | solution.py:212
  111.1 1.2 collective-permute-done.13
  112.3 0.7 copy-done.23
  113.0 1.3 collective-permute-start.15
  114.3 1.5 select_select_fusion
  115.8 1.6 pad_maximum_fusion.tok_ref
  117.4 3.0 %collective-permute-done.15.refs_1_ = f32[64,512]{1,0:T(8,128)S(1)} collective-permute-done((f32[64,512]{1,0:T(8,128)S(1)}, f32[64,512]{1,0:T(8,128)S(1)}, u32[]{:S(2)}, u32[]{:S(2)}) %collective-permute-start.15) | collective-permute-done | bytes 131104 | tf_op jit(solution)/shard_map/ppermute | solution.py:314
  120.3 1.7 spread.3
  122.0 0.8 copy-done.15
  122.8 1.3 collective-permute-done.16
  124.1 9.9 %project.4 = (f32[256,2048]{1,0:T(8,128)S(1)}, f32[256,2048]{1,0:T(8,128)}) custom-call(bf16[512,2048]{1,0:T(8,128)(2,1)} %pad_maximum_fusion.tok_ref, bf16[512,512]{1,0:T(8,128)(2,1)S(1)} %get-tuple-element.76.wide_ref, bf16[2048,7168]{1,0:T(8,128)(2,1)} %w_ref.11, bf16[512,7168]{1,0:T(8,128)(2,1)} %bitcast.23), custom_call_target="tpu_custom_call" | custom-call | flops 83886080 | bytes 229376 | tf_op jit(solution)/shard_map/project/pallas_call | solution.py:39
  134.0 1.3 copy-done.8
  135.5 4.8 %all-to-all-start = ((bf16[4,128,2048]{2,1,0:T(8,128)(2,1)}), bf16[4,128,2048]{2,1,0:T(8,128)(2,1)}, u32[]{:S(2)}, u32[]{:S(2)}) async-start(bf16[4,128,2048]{2,1,0:T(8,128)(2,1)} %bitcast.28), calls=%async_computation | async-start | bytes 4194304 | tf_op jit(solution)/shard_map/all_to_all | solution.py:367
  140.3 0.7 collective-permute-start.18
  141.0 1.0 copy-done.5
  142.0 6.7 %project.5 = (f32[256,1536]{1,0:T(8,128)S(1)}, f32[256,1536]{1,0:T(8,128)S(1)}) custom-call(bf16[512,2048]{1,0:T(8,128)(2,1)S(1)} %copy-done, bf16[512,512]{1,0:T(8,128)(2,1)S(1)} %copy-done.5, bf16[2048,7168]{1,0:T(8,128)(2,1)} %w_ref.11, bf16[512,7168]{1,0:T(8,128)(2,1)} %bitcast.24), custom_call_target="tpu_custom_call" | custom-call | flops 62914560 | bytes 172032 | tf_op jit(solution)/shard_map/project/pallas_call | solution.py:39
  148.9 1.8 fusion.6
  150.6 1.5 collective-permute-start.19
  152.8 9.8 %project.6 = (f32[256,2048]{1,0:T(8,128)S(1)}, f32[256,2048]{1,0:T(8,128)}) custom-call(bf16[512,2048]{1,0:T(8,128)(2,1)} %pad_maximum_fusion.tok_ref, bf16[512,512]{1,0:T(8,128)(2,1)S(1)} %copy-done.5, bf16[2048,7168]{1,0:T(8,128)(2,1)} %w_ref.11, bf16[512,7168]{1,0:T(8,128)(2,1)} %bitcast.25), custom_call_target="tpu_custom_call" | custom-call | flops 83886080 | bytes 229376 | tf_op jit(solution)/shard_map/project/pallas_call | solution.py:39
  162.6 1.9 collective-permute-done.19
  164.6 2.2 fusion.5
  166.9 1.5 collective-permute-start.21
  168.4 7.5 %project.7 = (f32[256,1536]{1,0:T(8,128)S(1)}, f32[256,1536]{1,0:T(8,128)}) custom-call(bf16[512,2048]{1,0:T(8,128)(2,1)S(1)} %copy-done.1, bf16[512,512]{1,0:T(8,128)(2,1)S(1)} %copy-done.5, bf16[2048,7168]{1,0:T(8,128)(2,1)} %w_ref.11, bf16[512,7168]{1,0:T(8,128)(2,1)} %bitcast.26), custom_call_target="tpu_custom_call" | custom-call | flops 62914560 | bytes 172032 | tf_op jit(solution)/shard_map/project/pallas_call | solution.py:39
  175.8 1.1 copy-done.10
  177.3 1.7 fusion.11
  179.1 2.1 fusion.3
  181.2 1.4 collective-permute-start.24
  182.5 2.9 %slot_grad.3 = f32[512,2048]{1,0:T(8,128)} custom-call(bf16[512,512]{1,0:T(8,128)(2,1)S(1)} %copy-done.16, bf16[256,2048]{1,0:T(8,128)(2,1)S(1)} %constant_dynamic-update-slice_fusion.refs_0_.refs_2_, bf16[256,2048]{1,0:T(8,128)(2,1)S(1)} %copy-done.3, bf16[256,2048]{1,0:T(8,128)(2,1)S(1)} %constant_dynamic-update-slice_fusion.refs_0_.refs_2_, ...), custom_call_target="tpu_custom_call" | custom-call | flops 1073741824 | bytes 6291456 | tf_op jit(solution)/shard_map/slot_grad/pallas_call | solution.py:212
  185.5 3.7 %all-to-all-done = bf16[4,128,2048]{2,1,0:T(8,128)(2,1)} async-done(((bf16[4,128,2048]{2,1,0:T(8,128)(2,1)}), bf16[4,128,2048]{2,1,0:T(8,128)(2,1)}, u32[]{:S(2)}, u32[]{:S(2)}) %all-to-all-start) | async-done | bytes 2097184 | tf_op jit(solution)/shard_map/all_to_all | solution.py:367
  189.2 2.6 %fusion = bf16[128,2048]{1,0:T(8,128)(2,1)S(1)} fusion(bf16[64,2048]{1,0:T(8,128)(2,1)} %copy-done.23, f32[256,2048]{1,0:T(8,128)} %copy-done.14, s32[]{:T(128)S(6)} %select_n.64, f32[256,2048]{1,0:T(8,128)} %copy-done.13, bf16[4,128,2048]{2,1,0:T(8,128)(2,1)} %all-to-all-done, s32[]{:T(128)S(6)} %select_n.68, s32[]{:T(128)S(6)} %select_n.67, ...), kind=kOutput, calls=%fused_computation.1 | convolution fusion | flops 35913728 | bytes 4472853 | tf_op jit(solution)/shard_map/dot_general | solution.py:18
  191.8 1.3 fusion.9
  193.1 1.1 collective-permute-start.25
  194.2 1.9 collective-permute-start.26
  196.1 1.5 fusion.2
  197.6 8.4 %collective-permute-done.25 = bf16[128,1536]{1,0:T(8,128)(2,1)S(1)} collective-permute-done((bf16[128,1536]{1,0:T(8,128)(2,1)S(1)}, bf16[128,1536]{1,0:T(8,128)(2,1)S(1)}, u32[]{:S(2)}, u32[]{:S(2)}) %collective-permute-start.25) | collective-permute-done | bytes 393248 | tf_op jit(solution)/shard_map/ppermute | solution.py:311
  206.1 1.3 fusion.8
  207.4 1.4 pad_maximum_fusion.1
  208.8 10.2 %collective-permute-done.26 = bf16[128,2048]{1,0:T(8,128)(2,1)S(1)} collective-permute-done((bf16[128,2048]{1,0:T(8,128)(2,1)S(1)}, bf16[128,2048]{1,0:T(8,128)(2,1)S(1)}, u32[]{:S(2)}, u32[]{:S(2)}) %collective-permute-start.26) | collective-permute-done | bytes 524320 | tf_op jit(solution)/shard_map/ppermute | solution.py:324
  219.0 0.8 copy.17
  (81 shorter events, 4.8 us)
Async XLA Ops:
  0.6 13.9 %collective-permute-start = (bf16[128,2048]{1,0:T(8,128)(2,1)}, bf16[128,2048]{1,0:T(8,128)(2,1)S(1)}, u32[]{:S(2)}, u32[]{:S(2)}) collective-permute-start(bf16[128,2048]{1,0:T(8,128)(2,1)} %param.8), channel_id=1, source_target_pairs={{0,2},{1,3},{2,0},{3,1},{4,6},{5,7},{6,4},{7,5},{8,10},{9,11},{10,... | collective-permute-start | bytes 1572872 | tf_op jit(solution)/shard_map/ppermute | solution.py:311
  0.7 16.9 %collective-permute-start.3 = (bf16[128,7168]{1,0:T(8,128)(2,1)}, bf16[128,7168]{1,0:T(8,128)(2,1)}, u32[]{:S(2)}, u32[]{:S(2)}) collective-permute-start(bf16[128,7168]{1,0:T(8,128)(2,1)} %refs_0_.1), channel_id=1, source_target_pairs={{0,1},{1,0},{2,3},{3,2},{4,5},{5,4},{6,7},{7,6},{8,9},{9,8},{10,11... | collective-permute-start | bytes 5505032 | tf_op jit(solution)/shard_map/ppermute | solution.py:311
  0.9 1.6 copy-start.6
  2.5 0.7 copy-start.17
  3.1 0.7 copy-start.18
  3.8 0.7 copy-start.19
  4.4 1.5 copy-start.22
  14.6 41.3 %collective-permute-start.6 = (bf16[128,7168]{1,0:T(8,128)(2,1)}, bf16[128,7168]{1,0:T(8,128)(2,1)}, u32[]{:S(2)}, u32[]{:S(2)}) collective-permute-start(bf16[128,7168]{1,0:T(8,128)(2,1)} %refs_0_.1), channel_id=1, source_target_pairs={{0,2},{1,3},{2,0},{3,1},{4,6},{5,7},{6,4},{7,5},{8,10},{9,11},{10,... | collective-permute-start | bytes 5505032 | tf_op jit(solution)/shard_map/ppermute | solution.py:311
  15.0 2.7 %collective-permute-start.2 = (bf16[256,2048]{1,0:T(8,128)(2,1)S(1)}, bf16[256,2048]{1,0:T(8,128)(2,1)S(1)}, u32[]{:S(2)}, u32[]{:S(2)}) collective-permute-start(bf16[256,2048]{1,0:T(8,128)(2,1)S(1)} %constant_dynamic-update-slice_fusion.refs_0_.refs_2_), channel_id=1, source_target_pairs={{0,1},{1,0},{2,3},{3,2},{4,5},{5,4},{6,7},{7,6},{8,9},{9,8},{10,11... | collective-permute-start | bytes 3145736 | tf_op jit(solution)/shard_map/ppermute | solution.py:311
  15.0 28.9 %collective-permute-start.1 = (bf16[256,2048]{1,0:T(8,128)(2,1)S(1)}, bf16[256,2048]{1,0:T(8,128)(2,1)}, u32[]{:S(2)}, u32[]{:S(2)}) collective-permute-start(bf16[256,2048]{1,0:T(8,128)(2,1)S(1)} %constant_dynamic-update-slice_fusion.refs_0_.refs_2_), channel_id=1, source_target_pairs={{0,8},{5,13},{10,2},{15,7},{16,24},{21,29},{26,18},{31,23}} | collective-permute-start | bytes 3145736 | tf_op jit(solution)/shard_map/ppermute | solution.py:324
  16.3 22.2 %copy-start.7 = (bf16[8,2048,64]{1,2,0:T(8,128)(2,1)S(1)}, bf16[8,2048,64]{1,2,0:T(8,128)(2,1)}, u32[]{:S(2)}) copy-start(bf16[8,2048,64]{1,2,0:T(8,128)(2,1)} %param.10) | copy-start | bytes 6291460
  17.6 96.7 %copy-start.2 = (bf16[256,2048]{1,0:T(8,128)(2,1)}, bf16[256,2048]{1,0:T(8,128)(2,1)S(1)}, u32[]{:S(2)}) copy-start(bf16[256,2048]{1,0:T(8,128)(2,1)S(1)} %collective-permute-done.2.refs_1_.refs_3_) | copy-start | bytes 3145732
  37.1 1.4 copy-start.13
  40.3 6.2 %collective-permute-start.7 = (f32[64,512]{1,0:T(8,128)S(1)}, f32[64,512]{1,0:T(8,128)S(1)}, u32[]{:S(2)}, u32[]{:S(2)}) collective-permute-start(f32[64,512]{1,0:T(8,128)S(1)} %rank_inner.1), channel_id=1, source_target_pairs={{0,4},{4,0},{8,12},{12,8},{1,5},{5,1},{9,13},{13,9},{2,6},{6,2},{1... | collective-permute-start | bytes 393224 | tf_op jit(solution)/shard_map/ppermute | solution.py:314
  55.9 11.0 %collective-permute-start.8 = (bf16[128,7168]{1,0:T(8,128)(2,1)}, bf16[128,7168]{1,0:T(8,128)(2,1)}, u32[]{:S(2)}, u32[]{:S(2)}) collective-permute-start(bf16[128,7168]{1,0:T(8,128)(2,1)} %collective-permute-done.6.a_ref.refs_2_), channel_id=1, source_target_pairs={{0,1},{1,0},{2,3},{3,2},{4,5},{5,4},{6,7},{7,6},{8,9},{9,8},{10,11... | collective-permute-start | bytes 5505032 | tf_op jit(solution)/shard_map/ppermute | solution.py:311
  55.9 33.2 %collective-permute-start.5 = (bf16[256,2048]{1,0:T(8,128)(2,1)S(1)}, bf16[256,2048]{1,0:T(8,128)(2,1)}, u32[]{:S(2)}, u32[]{:S(2)}) collective-permute-start(bf16[256,2048]{1,0:T(8,128)(2,1)S(1)} %collective-permute-done.2.refs_1_.refs_3_), channel_id=1, source_target_pairs={{0,8},{5,13},{10,2},{15,7},{16,24},{21,29},{26,18},{31,23}} | collective-permute-start | bytes 3145736 | tf_op jit(solution)/shard_map/ppermute | solution.py:324
  57.2 8.4 %collective-permute-start.11 = (bf16[128,2048]{1,0:T(8,128)(2,1)S(1)}, bf16[128,2048]{1,0:T(8,128)(2,1)}, u32[]{:S(2)}, u32[]{:S(2)}) collective-permute-start(bf16[128,2048]{1,0:T(8,128)(2,1)S(1)} %get-tuple-element.79), channel_id=1, source_target_pairs={{0,1},{1,0},{2,3},{3,2},{4,5},{5,4},{6,7},{7,6},{8,9},{9,8},{10,11... | collective-permute-start | bytes 1572872 | tf_op jit(solution)/shard_map/ppermute | solution.py:311
  58.0 36.4 %collective-permute-start.4 = (bf16[256,2048]{1,0:T(8,128)(2,1)}, bf16[256,2048]{1,0:T(8,128)(2,1)S(1)}, u32[]{:S(2)}, u32[]{:S(2)}) collective-permute-start(bf16[256,2048]{1,0:T(8,128)(2,1)} %broadcast_select_fusion.1), channel_id=1, source_target_pairs={{0,4},{8,12},{5,1},{13,9},{10,14},{2,6},{15,11},{7,3},{16,20},{24,... | collective-permute-start | bytes 3145736 | tf_op jit(solution)/shard_map/ppermute | solution.py:324
  61.3 34.5 %collective-permute-start.10 = (f32[64,512]{1,0:T(8,128)S(1)}, f32[64,512]{1,0:T(8,128)S(1)}, u32[]{:S(2)}, u32[]{:S(2)}) collective-permute-start(f32[64,512]{1,0:T(8,128)S(1)} %add.86.refs_0_), channel_id=1, source_target_pairs={{0,8},{4,12},{8,0},{12,4},{1,9},{5,13},{9,1},{13,5},{2,10},{6,14},... | collective-permute-start | bytes 393224 | tf_op jit(solution)/shard_map/ppermute | solution.py:314
  66.5 30.7 %collective-permute-start.12 = (bf16[64,2048]{1,0:T(8,128)(2,1)S(1)}, bf16[64,2048]{1,0:T(8,128)(2,1)S(1)}, u32[]{:S(2)}, u32[]{:S(2)}) collective-permute-start(bf16[64,2048]{1,0:T(8,128)(2,1)S(1)} %slice_add_fusion.9), channel_id=1, source_target_pairs={{0,2},{1,3},{2,0},{3,1},{4,6},{5,7},{6,4},{7,5},{8,10},{9,11},{10,... | collective-permute-start | bytes 786440 | tf_op jit(solution)/shard_map/ppermute | solution.py:311
  87.2 8.7 %copy-start.14 = (f32[256,2048]{1,0:T(8,128)}, f32[256,2048]{1,0:T(8,128)S(1)}, u32[]{:S(2)}) copy-start(f32[256,2048]{1,0:T(8,128)S(1)} %get-tuple-element.69) | copy-start | bytes 6291460
  89.1 23.9 %collective-permute-start.14 = (f32[64,512]{1,0:T(8,128)S(1)}, f32[64,512]{1,0:T(8,128)S(1)}, u32[]{:S(2)}, u32[]{:S(2)}) collective-permute-start(f32[64,512]{1,0:T(8,128)S(1)} %constant_dynamic-update-slice_fusion.2), channel_id=1, source_target_pairs={{0,4},{4,0},{8,12},{12,8},{1,5},{5,1},{9,13},{13,9},{2,6},{6,2},{1... | collective-permute-start | bytes 393224 | tf_op jit(solution)/shard_map/ppermute | solution.py:314
  90.4 23.8 %collective-permute-start.9 = (bf16[256,2048]{1,0:T(8,128)(2,1)S(1)}, bf16[256,2048]{1,0:T(8,128)(2,1)S(1)}, u32[]{:S(2)}, u32[]{:S(2)}) collective-permute-start(bf16[256,2048]{1,0:T(8,128)(2,1)S(1)} %broadcast_select_fusion), channel_id=1, source_target_pairs={{0,4},{8,12},{5,1},{13,9},{10,14},{2,6},{15,11},{7,3},{16,20},{24,... | collective-permute-start | bytes 3145736 | tf_op jit(solution)/shard_map/ppermute | solution.py:324
  97.2 26.9 %copy-start.4 = (bf16[512,512]{1,0:T(8,128)(2,1)}, bf16[512,512]{1,0:T(8,128)(2,1)S(1)}, u32[]{:S(2)}) copy-start(bf16[512,512]{1,0:T(8,128)(2,1)S(1)} %get-tuple-element.76.wide_ref) | copy-start | bytes 1572868
  98.4 13.9 %collective-permute-start.13 = (bf16[64,2048]{1,0:T(8,128)(2,1)S(1)}, bf16[64,2048]{1,0:T(8,128)(2,1)S(1)}, u32[]{:S(2)}, u32[]{:S(2)}) collective-permute-start(bf16[64,2048]{1,0:T(8,128)(2,1)S(1)} %fusion.13), channel_id=1, source_target_pairs={{0,0},{4,5},{8,10},{12,15},{1,4},{5,1},{9,14},{13,11},{2,8},{6,13}... | collective-permute-start | bytes 786440 | tf_op jit(solution)/shard_map/ppermute | solution.py:324
  112.3 0.7 copy-start.23
  113.0 7.3 %collective-permute-start.15 = (f32[64,512]{1,0:T(8,128)S(1)}, f32[64,512]{1,0:T(8,128)S(1)}, u32[]{:S(2)}, u32[]{:S(2)}) collective-permute-start(f32[64,512]{1,0:T(8,128)S(1)} %add.90.refs_0_), channel_id=1, source_target_pairs={{0,8},{4,12},{8,0},{12,4},{1,9},{5,13},{9,1},{13,5},{2,10},{6,14},... | collective-permute-start | bytes 393224 | tf_op jit(solution)/shard_map/ppermute | solution.py:314
  122.0 0.8 copy-start.15
  122.8 1.3 collective-permute-start.16
  134.0 1.3 copy-start.8
  135.3 13.5 %collective-permute-start.17 = (f32[256,2048]{1,0:T(8,128)}, f32[256,2048]{1,0:T(8,128)}, u32[]{:S(2)}, u32[]{:S(2)}) collective-permute-start(f32[256,2048]{1,0:T(8,128)} %get-tuple-element.91), channel_id=1, source_target_pairs={{0,1},{1,0},{2,3},{3,2},{4,5},{5,4},{6,7},{7,6},{8,9},{9,8},{10,11... | collective-permute-start | bytes 6291464 | tf_op jit(solution)/shard_map/ppermute | solution.py:311
  135.5 5.5 %copy-start = (bf16[512,2048]{1,0:T(8,128)(2,1)S(1)}, bf16[512,2048]{1,0:T(8,128)(2,1)}, u32[]{:S(2)}) copy-start(bf16[512,2048]{1,0:T(8,128)(2,1)} %pad_maximum_fusion.tok_ref) | copy-start | bytes 6291460
  135.5 53.7 %all-to-all-start = ((bf16[4,128,2048]{2,1,0:T(8,128)(2,1)}), bf16[4,128,2048]{2,1,0:T(8,128)(2,1)}, u32[]{:S(2)}, u32[]{:S(2)}) async-start(bf16[4,128,2048]{2,1,0:T(8,128)(2,1)} %bitcast.28), calls=%async_computation | async-start | bytes 4194304 | tf_op jit(solution)/shard_map/all_to_all | solution.py:367
  140.3 11.8 %collective-permute-start.18 = (bf16[64,512]{1,0:T(8,128)(2,1)S(1)}, bf16[64,512]{1,0:T(8,128)(2,1)S(1)}, u32[]{:S(2)}, u32[]{:S(2)}) collective-permute-start(bf16[64,512]{1,0:T(8,128)(2,1)S(1)} %maximum_add_fusion), channel_id=1, source_target_pairs={{0,2},{1,3},{2,0},{3,1},{4,6},{5,7},{6,4},{7,5},{8,10},{9,11},{10,... | collective-permute-start | bytes 196616 | tf_op jit(solution)/shard_map/ppermute | solution.py:311
  141.0 1.0 copy-start.5
  142.0 6.9 %copy-start.9 = (f32[256,2048]{1,0:T(8,128)S(1)}, f32[256,2048]{1,0:T(8,128)}, u32[]{:S(2)}) copy-start(f32[256,2048]{1,0:T(8,128)} %copy-done.8) | copy-start | bytes 6291460
  148.7 18.1 %copy-start.12 = (f32[256,1536]{1,0:T(8,128)}, f32[256,1536]{1,0:T(8,128)S(1)}, u32[]{:S(2)}) copy-start(f32[256,1536]{1,0:T(8,128)S(1)} %get-tuple-element.100) | copy-start | bytes 4718596
  148.7 18.0 %collective-permute-start.20 = (f32[256,1536]{1,0:T(8,128)S(1)}, f32[256,1536]{1,0:T(8,128)S(1)}, u32[]{:S(2)}, u32[]{:S(2)}) collective-permute-start(f32[256,1536]{1,0:T(8,128)S(1)} %get-tuple-element.97), channel_id=1, source_target_pairs={{0,1},{1,0},{2,3},{3,2},{4,5},{5,4},{6,7},{7,6},{8,9},{9,8},{10,11... | collective-permute-start | bytes 4718600 | tf_op jit(solution)/shard_map/ppermute | solution.py:311
  150.6 13.9 %collective-permute-start.19 = (bf16[128,2048]{1,0:T(8,128)(2,1)S(1)}, bf16[128,2048]{1,0:T(8,128)(2,1)S(1)}, u32[]{:S(2)}, u32[]{:S(2)}) collective-permute-start(bf16[128,2048]{1,0:T(8,128)(2,1)S(1)} %fusion.6), channel_id=1, source_target_pairs={{0,2},{1,3},{2,0},{3,1},{4,6},{5,7},{6,4},{7,5},{8,10},{9,11},{10,... | collective-permute-start | bytes 1572872 | tf_op jit(solution)/shard_map/ppermute | solution.py:311
  162.6 16.4 %collective-permute-start.22 = (f32[256,2048]{1,0:T(8,128)}, f32[256,2048]{1,0:T(8,128)}, u32[]{:S(2)}, u32[]{:S(2)}) collective-permute-start(f32[256,2048]{1,0:T(8,128)} %get-tuple-element.105), channel_id=1, source_target_pairs={{0,1},{1,0},{2,3},{3,2},{4,5},{5,4},{6,7},{7,6},{8,9},{9,8},{10,11... | collective-permute-start | bytes 6291464 | tf_op jit(solution)/shard_map/ppermute | solution.py:311
  162.6 5.7 %copy-start.1 = (bf16[512,2048]{1,0:T(8,128)(2,1)S(1)}, bf16[512,2048]{1,0:T(8,128)(2,1)}, u32[]{:S(2)}) copy-start(bf16[512,2048]{1,0:T(8,128)(2,1)} %pad_maximum_fusion.tok_ref) | copy-start | bytes 6291460
  166.8 9.0 %copy-start.21 = (f32[256,1536]{1,0:T(8,128)}, f32[256,1536]{1,0:T(8,128)S(1)}, u32[]{:S(2)}) copy-start(f32[256,1536]{1,0:T(8,128)S(1)} %collective-permute-done.20) | copy-start | bytes 4718596
  166.9 10.5 %collective-permute-start.21 = (bf16[128,1536]{1,0:T(8,128)(2,1)S(1)}, bf16[128,1536]{1,0:T(8,128)(2,1)}, u32[]{:S(2)}, u32[]{:S(2)}) collective-permute-start(bf16[128,1536]{1,0:T(8,128)(2,1)S(1)} %fusion.12), channel_id=1, source_target_pairs={{0,2},{1,3},{2,0},{3,1},{4,6},{5,7},{6,4},{7,5},{8,10},{9,11},{10,... | collective-permute-start | bytes 1179656 | tf_op jit(solution)/shard_map/ppermute | solution.py:311
  175.8 1.1 copy-start.10
  177.0 14.8 %collective-permute-start.23 = (f32[256,1536]{1,0:T(8,128)}, f32[256,1536]{1,0:T(8,128)}, u32[]{:S(2)}, u32[]{:S(2)}) collective-permute-start(f32[256,1536]{1,0:T(8,128)} %get-tuple-element.109), channel_id=1, source_target_pairs={{0,1},{1,0},{2,3},{3,2},{4,5},{5,4},{6,7},{7,6},{8,9},{9,8},{10,11... | collective-permute-start | bytes 4718600 | tf_op jit(solution)/shard_map/ppermute | solution.py:311
  177.0 5.6 %copy-start.3 = (bf16[256,2048]{1,0:T(8,128)(2,1)S(1)}, bf16[256,2048]{1,0:T(8,128)(2,1)}, u32[]{:S(2)}) copy-start(bf16[256,2048]{1,0:T(8,128)(2,1)} %copy-done.2) | copy-start | bytes 3145732
  177.0 5.6 %copy-start.16 = (bf16[512,512]{1,0:T(8,128)(2,1)S(1)}, bf16[512,512]{1,0:T(8,128)(2,1)}, u32[]{:S(2)}) copy-start(bf16[512,512]{1,0:T(8,128)(2,1)} %copy-done.15) | copy-start | bytes 1572868
  181.2 14.9 %collective-permute-start.24 = (bf16[128,2048]{1,0:T(8,128)(2,1)}, bf16[128,2048]{1,0:T(8,128)(2,1)}, u32[]{:S(2)}, u32[]{:S(2)}) collective-permute-start(bf16[128,2048]{1,0:T(8,128)(2,1)} %fusion.3), channel_id=1, source_target_pairs={{0,2},{1,3},{2,0},{3,1},{4,6},{5,7},{6,4},{7,5},{8,10},{9,11},{10,... | collective-permute-start | bytes 1572872 | tf_op jit(solution)/shard_map/ppermute | solution.py:311
  189.2 2.6 %copy-start.11 = (f32[256,1536]{1,0:T(8,128)S(1)}, f32[256,1536]{1,0:T(8,128)}, u32[]{:S(2)}) copy-start(f32[256,1536]{1,0:T(8,128)} %copy-done.10) | copy-start | bytes 4718596
  193.1 14.3 %copy-start.20 = (bf16[128,2048]{1,0:T(8,128)(2,1)S(1)}, bf16[128,2048]{1,0:T(8,128)(2,1)}, u32[]{:S(2)}) copy-start(bf16[128,2048]{1,0:T(8,128)(2,1)} %fusion.5) | copy-start | bytes 1572868
  193.1 13.0 %collective-permute-start.25 = (bf16[128,1536]{1,0:T(8,128)(2,1)S(1)}, bf16[128,1536]{1,0:T(8,128)(2,1)S(1)}, u32[]{:S(2)}, u32[]{:S(2)}) collective-permute-start(bf16[128,1536]{1,0:T(8,128)(2,1)S(1)} %fusion.9), channel_id=1, source_target_pairs={{0,2},{1,3},{2,0},{3,1},{4,6},{5,7},{6,4},{7,5},{8,10},{9,11},{10,... | collective-permute-start | bytes 1179656 | tf_op jit(solution)/shard_map/ppermute | solution.py:311
  194.2 24.8 %collective-permute-start.26 = (bf16[128,2048]{1,0:T(8,128)(2,1)S(1)}, bf16[128,2048]{1,0:T(8,128)(2,1)S(1)}, u32[]{:S(2)}, u32[]{:S(2)}) collective-permute-start(bf16[128,2048]{1,0:T(8,128)(2,1)S(1)} %fusion), channel_id=1, source_target_pairs={{0,0},{5,4},{10,8},{15,12},{4,1},{1,5},{14,9},{11,13},{8,2},{13,6}... | collective-permute-start | bytes 1572872 | tf_op jit(solution)/shard_map/ppermute | solution.py:324

commit v16 on v15

--- a/solution.py
+++ b/solution.py
@@ -216,7 +216,7 @@
         out_specs=pl.BlockSpec((span, block), lambda n: (0, n)),
         out_shape=jax.ShapeDtypeStruct((span, columns), jnp.float32),
         compiler_params=pltpu.CompilerParams(vmem_limit_bytes=VMEM),
-        cost_estimate=cost(2 * span * tokens * columns, (4 * span + 2 * tokens) * columns, 1),
+        cost_estimate=cost(3 * 2 * span * tokens * columns, 3 * (4 * span + 2 * tokens) * columns, 1),
         name="slot_grad",
     )(wide_t, *arrays)
 
@@ -404,14 +404,14 @@
     point = finish(1, point)
     point = cross(2, point)
     down_wide = slot_grad(after(back_wide, point), [([x], n) for x, n in toks], width // 2)
+    point = cross(3, down_wide, parts)
     back_mine = lax.dynamic_slice_in_dim(back_b, j * rows, rows, 1)
     total = grad_block(j)
     for m in range(1, shards):
-        total = total + lax.dynamic_index_in_dim(after(parts, down_wide), j ^ m, 0, False).astype(jnp.float32)
+        total = total + lax.dynamic_index_in_dim(after(parts, point), j ^ m, 0, False).astype(jnp.float32)
     total = (total + dot(back_mine, down_mine, (0, 0))).astype(b16)
     tokens_grad = both(total, [(b, a) for a, b in place])
-    point = cross(3, total)
-    point = finish(2, point)
+    point = finish(2, total)
     finish(3, point)
     projected = jnp.concatenate(done, axis=1)
     up_grad = up_wide.reshape(per_owner, rank, hidden)

time: 221 us -> 222 us (level)
    unnamed x51 -> x53, local copies, waits for them, and re-layouts: 10.8 us -> 10.8 us
  transfers between devices with their start and end apart: 28 -> 28, of which waited for: 14 -> 14; matrix products, arithmetic and copies ran while one was open for 12% -> 12% of each run, Pallas kernels for 37% -> 38%
where the time goes in v16:
time: 222 us; the launch traced here: 220 us
  Pallas kernels  94.2 us (42%)
  waiting for transfers between devices  52.8 us (24%)
  starting transfers between devices  34.1 us (15%)
  other arithmetic  24.5 us (11%)
  local copies, waits for them, and re-layouts  10.9 us (5%)
  matrix products  2.41 us (1%)
    pallas_call x2, Pallas kernels, return_grad(): pl.pallas_call(kernel, grid_spec=pltpu.PrefetchScalarGridSpec(num_scalar_...  40.7 us
    pallas_call x4, Pallas kernels, project(): pl.pallas_call(kernel, grid=((stop - start) // block,), in_specs=[pl.Bloc...  33.9 us
    ppermute x17, waiting for transfers between devices, swap(): return lax.ppermute(x, 'dp', [(d, d ^ bit) for d in range(groups)])  30.9 us
    ppermute x6, waiting for transfers between devices, both(): return lax.ppermute(x, ('tp', 'dp'), pairs)  14.9 us
    ppermute x6, starting transfers between devices, both(): return lax.ppermute(x, ('tp', 'dp'), pairs)  13.7 us
    pallas_call x2, Pallas kernels, slot_grad(): pl.pallas_call(kernel, grid=(columns // block,), in_specs=[pl.BlockSpec((...  13.2 us
    unnamed x53, local copies, waits for them, and re-layouts  10.8 us
    ppermute x17, starting transfers between devices, swap(): return lax.ppermute(x, 'dp', [(d, d ^ bit) for d in range(groups)])  8.1 us
  transfers between devices with their start and end apart: 28, of which 14 were waited for; matrix products, arithmetic and copies ran while one was open for 12% of the time, Pallas kernels for 38%

profile of v16, /device:TPU:2, one launch (start us, length us, event | category | flops | bytes accessed | tf_op | source)
XLA Modules:
  0.0 219.9 jit_solution(3439301889492336424)
XLA Ops:
  0.9 1.6 copy-done.6
  2.5 0.7 copy-done.15
  4.4 1.5 choose.1
  6.0 8.6 %collective-permute-done = bf16[128,2048]{1,0:T(8,128)(2,1)S(1)} collective-permute-done((bf16[128,2048]{1,0:T(8,128)(2,1)}, bf16[128,2048]{1,0:T(8,128)(2,1)S(1)}, u32[]{:S(2)}, u32[]{:S(2)}) %collective-permute-start) | collective-permute-done | bytes 524320 | tf_op jit(solution)/shard_map/ppermute | solution.py:311
  15.0 1.3 collective-permute-start.1
  16.3 1.4 collective-permute-done.2.refs_1_.refs_3_
  17.6 20.4 %return_grad.2 = (f32[256,2048]{1,0:T(8,128)S(1)}, bf16[512,2048]{1,0:T(8,128)(2,1)}, f32[64,256]{1,0:T(8,128)S(1)}) custom-call(s32[9]{0:T(128)S(1)} %get-tuple-element.58.facts_ref, bf16[128,7168]{1,0:T(8,128)(2,1)} %refs_0_.1, bf16[128,7168]{1,0:T(8,128)(2,1)} %collective-permute-done.3.b_ref.refs_1_, bf16[2048,7168]{1,0:T(8,128)(2,1)} %w_ref.11, ...), custom_call_target="tpu_custom_call" | custom-call | flops 117440512 | bytes 516096 | tf_op jit(solution)/shard_map/return_grad/pallas_call | solution.py:88
  38.0 1.3 copy-done.13
  39.4 1.8 rank_inner.1
  41.2 1.9 collective-permute-start.7
  43.1 0.9 collective-permute-done.1
  44.0 2.3 %broadcast_select_fusion.1 = bf16[256,2048]{1,0:T(8,128)(2,1)} fusion(bf16[256,2048]{1,0:T(8,128)(2,1)S(1)} %constant_dynamic-update-slice_fusion.refs_0_.refs_2_, bf16[256,2048]{1,0:T(8,128)(2,1)} %collective-permute-done.1, pred[]{:T(512)S(6)} %eq.4), kind=kLoop, calls=%fused_computation.20 | loop fusion | flops 524288 | bytes 3145729 | tf_op jit(solution)/shard_map/jit(_where)/select_n | solution.py:344
  46.6 9.3 %collective-permute-done.6.a_ref.refs_2_ = bf16[128,7168]{1,0:T(8,128)(2,1)} collective-permute-done((bf16[128,7168]{1,0:T(8,128)(2,1)}, bf16[128,7168]{1,0:T(8,128)(2,1)}, u32[]{:S(2)}, u32[]{:S(2)}) %collective-permute-start.6) | collective-permute-done | bytes 1835040 | tf_op jit(solution)/shard_map/ppermute | solution.py:311
  55.9 1.3 collective-permute-start.5
  57.2 0.9 collective-permute-start.11
  58.1 3.2 %collective-permute-start.4 = (bf16[256,2048]{1,0:T(8,128)(2,1)}, bf16[256,2048]{1,0:T(8,128)(2,1)S(1)}, u32[]{:S(2)}, u32[]{:S(2)}) collective-permute-start(bf16[256,2048]{1,0:T(8,128)(2,1)} %broadcast_select_fusion.1), channel_id=1, source_target_pairs={{0,4},{8,12},{5,1},{13,9},{10,14},{2,6},{15,11},{7,3},{16,20},{24,... | collective-permute-start | bytes 3145736 | tf_op jit(solution)/shard_map/ppermute | solution.py:324
  61.3 4.3 %collective-permute-start.10 = (f32[64,512]{1,0:T(8,128)S(1)}, f32[64,512]{1,0:T(8,128)S(1)}, u32[]{:S(2)}, u32[]{:S(2)}) collective-permute-start(f32[64,512]{1,0:T(8,128)S(1)} %add.86.refs_0_), channel_id=1, source_target_pairs={{0,8},{4,12},{8,0},{12,4},{1,9},{5,13},{9,1},{13,5},{2,10},{6,14},... | collective-permute-start | bytes 393224 | tf_op jit(solution)/shard_map/ppermute | solution.py:314
  65.6 1.0 slice_add_fusion.9
  66.8 20.4 %return_grad.3 = (f32[256,2048]{1,0:T(8,128)S(1)}, bf16[512,2048]{1,0:T(8,128)(2,1)}, f32[64,256]{1,0:T(8,128)S(1)}) custom-call(s32[9]{0:T(128)S(1)} %get-tuple-element.58.facts_ref, bf16[128,7168]{1,0:T(8,128)(2,1)} %collective-permute-done.6.a_ref.refs_2_, ...), custom_call_target="tpu_custom_call", output_to_operand_aliasing={{1}: (6, {})} | custom-call | flops 117440512 | bytes 516096 | tf_op jit(solution)/shard_map/return_grad/pallas_call | solution.py:88
  87.2 1.9 collective-permute-done.5
  89.1 1.3 broadcast_select_fusion
  90.4 4.0 %collective-permute-start.9 = (bf16[256,2048]{1,0:T(8,128)(2,1)S(1)}, bf16[256,2048]{1,0:T(8,128)(2,1)S(1)}, u32[]{:S(2)}, u32[]{:S(2)}) collective-permute-start(bf16[256,2048]{1,0:T(8,128)(2,1)S(1)} %broadcast_select_fusion), channel_id=1, source_target_pairs={{0,4},{8,12},{5,1},{13,9},{10,14},{2,6},{15,11},{7,3},{16,20},{24,... | collective-permute-start | bytes 3145736 | tf_op jit(solution)/shard_map/ppermute | solution.py:324
  94.4 1.4 select_select_fusion.1
  95.8 1.4 spread.2
  97.2 1.2 fusion.13
  98.4 1.9 collective-permute-start.13
  100.3 10.2 %slot_grad.2 = f32[512,7168]{1,0:T(8,128)} custom-call(bf16[512,512]{1,0:T(8,128)(2,1)S(1)} %get-tuple-element.77.wide_ref, bf16[128,7168]{1,0:T(8,128)(2,1)} %refs_0_.1, bf16[128,7168]{1,0:T(8,128)(2,1)} %collective-permute-done.3.b_ref.refs_1_, bf16[128,7168]{1,0:T(8,128)(2,1)} %collective-permute-done.6.a_ref.refs_2_, ...), custom_call_target="tpu_custom_call" | custom-call | flops 11274289152 | bytes 66060288 | tf_op jit(solution)/shard_map/slot_grad/pallas_call | solution.py:212
  110.6 1.7 collective-permute-done.13
  112.3 0.7 copy-done.23
  113.0 1.3 collective-permute-start.15
  114.3 1.5 select_select_fusion
  115.8 1.6 pad_maximum_fusion.tok_ref
  117.4 3.0 %collective-permute-done.15.refs_1_ = f32[64,512]{1,0:T(8,128)S(1)} collective-permute-done((f32[64,512]{1,0:T(8,128)S(1)}, f32[64,512]{1,0:T(8,128)S(1)}, u32[]{:S(2)}, u32[]{:S(2)}) %collective-permute-start.15) | collective-permute-done | bytes 131104 | tf_op jit(solution)/shard_map/ppermute | solution.py:314
  120.4 1.7 spread.3
  122.0 0.8 copy-done.18
  122.8 1.3 collective-permute-done.16
  124.1 9.9 %project.4 = (f32[256,2048]{1,0:T(8,128)S(1)}, f32[256,2048]{1,0:T(8,128)}) custom-call(bf16[512,2048]{1,0:T(8,128)(2,1)} %pad_maximum_fusion.tok_ref, bf16[512,512]{1,0:T(8,128)(2,1)S(1)} %get-tuple-element.76.wide_ref, bf16[2048,7168]{1,0:T(8,128)(2,1)} %w_ref.11, bf16[512,7168]{1,0:T(8,128)(2,1)} %bitcast.23), custom_call_target="tpu_custom_call" | custom-call | flops 83886080 | bytes 229376 | tf_op jit(solution)/shard_map/project/pallas_call | solution.py:39
  134.0 1.3 copy-done.8
  135.5 4.8 %all-to-all-start = ((bf16[4,128,2048]{2,1,0:T(8,128)(2,1)}), bf16[4,128,2048]{2,1,0:T(8,128)(2,1)}, u32[]{:S(2)}, u32[]{:S(2)}) async-start(bf16[4,128,2048]{2,1,0:T(8,128)(2,1)} %bitcast.27), calls=%async_computation | async-start | bytes 4194304 | tf_op jit(solution)/shard_map/all_to_all | solution.py:367
  140.9 1.0 copy-done.5
  142.0 6.7 %project.5 = (f32[256,1536]{1,0:T(8,128)S(1)}, f32[256,1536]{1,0:T(8,128)S(1)}) custom-call(bf16[512,2048]{1,0:T(8,128)(2,1)S(1)} %copy-done, bf16[512,512]{1,0:T(8,128)(2,1)S(1)} %copy-done.5, bf16[2048,7168]{1,0:T(8,128)(2,1)} %w_ref.11, bf16[512,7168]{1,0:T(8,128)(2,1)} %bitcast.24), custom_call_target="tpu_custom_call" | custom-call | flops 62914560 | bytes 172032 | tf_op jit(solution)/shard_map/project/pallas_call | solution.py:39
  148.8 1.8 fusion.6
  150.6 1.5 collective-permute-start.19
  152.8 9.9 %project.6 = (f32[256,2048]{1,0:T(8,128)S(1)}, f32[256,2048]{1,0:T(8,128)}) custom-call(bf16[512,2048]{1,0:T(8,128)(2,1)} %pad_maximum_fusion.tok_ref, bf16[512,512]{1,0:T(8,128)(2,1)S(1)} %copy-done.5, bf16[2048,7168]{1,0:T(8,128)(2,1)} %w_ref.11, bf16[512,7168]{1,0:T(8,128)(2,1)} %bitcast.25), custom_call_target="tpu_custom_call" | custom-call | flops 83886080 | bytes 229376 | tf_op jit(solution)/shard_map/project/pallas_call | solution.py:39
  162.7 1.9 collective-permute-done.19
  164.5 2.2 fusion.5
  166.8 1.5 collective-permute-start.21
  168.4 7.5 %project.7 = (f32[256,1536]{1,0:T(8,128)S(1)}, f32[256,1536]{1,0:T(8,128)}) custom-call(bf16[512,2048]{1,0:T(8,128)(2,1)S(1)} %copy-done.1, bf16[512,512]{1,0:T(8,128)(2,1)S(1)} %copy-done.5, bf16[2048,7168]{1,0:T(8,128)(2,1)} %w_ref.11, bf16[512,7168]{1,0:T(8,128)(2,1)} %bitcast.26), custom_call_target="tpu_custom_call" | custom-call | flops 62914560 | bytes 172032 | tf_op jit(solution)/shard_map/project/pallas_call | solution.py:39
  175.8 1.1 copy-done.10
  177.3 1.7 fusion.11
  179.0 2.1 fusion.3
  181.2 1.4 collective-permute-start.24
  182.5 2.9 %slot_grad.3 = f32[512,2048]{1,0:T(8,128)} custom-call(bf16[512,512]{1,0:T(8,128)(2,1)S(1)} %copy-done.19, bf16[256,2048]{1,0:T(8,128)(2,1)S(1)} %constant_dynamic-update-slice_fusion.refs_0_.refs_2_, bf16[256,2048]{1,0:T(8,128)(2,1)S(1)} %copy-done.3, bf16[256,2048]{1,0:T(8,128)(2,1)S(1)} %constant_dynamic-update-slice_fusion.refs_0_.refs_2_, ...), custom_call_target="tpu_custom_call" | custom-call | flops 3221225472 | bytes 18874368 | tf_op jit(solution)/shard_map/slot_grad/pallas_call | solution.py:212
  185.5 3.7 %all-to-all-done = bf16[4,128,2048]{2,1,0:T(8,128)(2,1)} async-done(((bf16[4,128,2048]{2,1,0:T(8,128)(2,1)}), bf16[4,128,2048]{2,1,0:T(8,128)(2,1)}, u32[]{:S(2)}, u32[]{:S(2)}) %all-to-all-start) | async-done | bytes 2097184 | tf_op jit(solution)/shard_map/all_to_all | solution.py:367
  189.2 1.5 fusion.9
  190.6 1.1 collective-permute-start.25
  191.7 2.4 %fusion = bf16[128,2048]{1,0:T(8,128)(2,1)S(1)} fusion(bf16[64,2048]{1,0:T(8,128)(2,1)S(1)} %copy-done.24, f32[256,2048]{1,0:T(8,128)} %copy-done.14, s32[]{:T(128)S(6)} %select_n.64, f32[256,2048]{1,0:T(8,128)} %copy-done.13, bf16[4,128,2048]{2,1,0:T(8,128)(2,1)} %all-to-all-done, s32[]{:T(128)S(6)} %select_n.68, s32[]{:T(128)S(6)} %select_n.67, ...), kind=kOutput, calls=%fused_computation.1 | convolution fusion | flops 35913728 | bytes 4472853 | tf_op jit(solution)/shard_map/dot_general | solution.py:18
  194.1 2.1 collective-permute-start.26
  196.3 1.5 fusion.2
  197.8 8.1 %collective-permute-done.25 = bf16[128,1536]{1,0:T(8,128)(2,1)S(1)} collective-permute-done((bf16[128,1536]{1,0:T(8,128)(2,1)S(1)}, bf16[128,1536]{1,0:T(8,128)(2,1)S(1)}, u32[]{:S(2)}, u32[]{:S(2)}) %collective-permute-start.25) | collective-permute-done | bytes 393248 | tf_op jit(solution)/shard_map/ppermute | solution.py:311
  205.9 1.3 fusion.8
  207.2 1.4 pad_maximum_fusion.1
  208.6 10.5 %collective-permute-done.26 = bf16[128,2048]{1,0:T(8,128)(2,1)S(1)} collective-permute-done((bf16[128,2048]{1,0:T(8,128)(2,1)S(1)}, bf16[128,2048]{1,0:T(8,128)(2,1)S(1)}, u32[]{:S(2)}, u32[]{:S(2)}) %collective-permute-start.26) | collective-permute-done | bytes 524320 | tf_op jit(solution)/shard_map/ppermute | solution.py:324
  219.1 0.8 copy.17
  (83 shorter events, 4.8 us)
Async XLA Ops:
  0.6 13.9 %collective-permute-start = (bf16[128,2048]{1,0:T(8,128)(2,1)}, bf16[128,2048]{1,0:T(8,128)(2,1)S(1)}, u32[]{:S(2)}, u32[]{:S(2)}) collective-permute-start(bf16[128,2048]{1,0:T(8,128)(2,1)} %param.8), channel_id=1, source_target_pairs={{0,2},{1,3},{2,0},{3,1},{4,6},{5,7},{6,4},{7,5},{8,10},{9,11},{10,... | collective-permute-start | bytes 1572872 | tf_op jit(solution)/shard_map/ppermute | solution.py:311
  0.7 16.9 %collective-permute-start.3 = (bf16[128,7168]{1,0:T(8,128)(2,1)}, bf16[128,7168]{1,0:T(8,128)(2,1)}, u32[]{:S(2)}, u32[]{:S(2)}) collective-permute-start(bf16[128,7168]{1,0:T(8,128)(2,1)} %refs_0_.1), channel_id=1, source_target_pairs={{0,1},{1,0},{2,3},{3,2},{4,5},{5,4},{6,7},{7,6},{8,9},{9,8},{10,11... | collective-permute-start | bytes 5505032 | tf_op jit(solution)/shard_map/ppermute | solution.py:311
  0.9 1.6 copy-start.6
  2.5 0.7 copy-start.15
  3.1 0.7 copy-start.16
  3.8 0.7 copy-start.17
  4.4 1.5 copy-start.22
  14.6 41.3 %collective-permute-start.6 = (bf16[128,7168]{1,0:T(8,128)(2,1)}, bf16[128,7168]{1,0:T(8,128)(2,1)}, u32[]{:S(2)}, u32[]{:S(2)}) collective-permute-start(bf16[128,7168]{1,0:T(8,128)(2,1)} %refs_0_.1), channel_id=1, source_target_pairs={{0,2},{1,3},{2,0},{3,1},{4,6},{5,7},{6,4},{7,5},{8,10},{9,11},{10,... | collective-permute-start | bytes 5505032 | tf_op jit(solution)/shard_map/ppermute | solution.py:311
  15.0 2.7 %collective-permute-start.2 = (bf16[256,2048]{1,0:T(8,128)(2,1)S(1)}, bf16[256,2048]{1,0:T(8,128)(2,1)S(1)}, u32[]{:S(2)}, u32[]{:S(2)}) collective-permute-start(bf16[256,2048]{1,0:T(8,128)(2,1)S(1)} %constant_dynamic-update-slice_fusion.refs_0_.refs_2_), channel_id=1, source_target_pairs={{0,1},{1,0},{2,3},{3,2},{4,5},{5,4},{6,7},{7,6},{8,9},{9,8},{10,11... | collective-permute-start | bytes 3145736 | tf_op jit(solution)/shard_map/ppermute | solution.py:311
  15.0 29.0 %collective-permute-start.1 = (bf16[256,2048]{1,0:T(8,128)(2,1)S(1)}, bf16[256,2048]{1,0:T(8,128)(2,1)}, u32[]{:S(2)}, u32[]{:S(2)}) collective-permute-start(bf16[256,2048]{1,0:T(8,128)(2,1)S(1)} %constant_dynamic-update-slice_fusion.refs_0_.refs_2_), channel_id=1, source_target_pairs={{0,8},{5,13},{10,2},{15,7},{16,24},{21,29},{26,18},{31,23}} | collective-permute-start | bytes 3145736 | tf_op jit(solution)/shard_map/ppermute | solution.py:324
  16.3 23.1 %copy-start.7 = (bf16[8,2048,64]{1,2,0:T(8,128)(2,1)S(1)}, bf16[8,2048,64]{1,2,0:T(8,128)(2,1)}, u32[]{:S(2)}) copy-start(bf16[8,2048,64]{1,2,0:T(8,128)(2,1)} %param.10) | copy-start | bytes 6291460
  17.6 96.7 %copy-start.2 = (bf16[256,2048]{1,0:T(8,128)(2,1)}, bf16[256,2048]{1,0:T(8,128)(2,1)S(1)}, u32[]{:S(2)}) copy-start(bf16[256,2048]{1,0:T(8,128)(2,1)S(1)} %collective-permute-done.2.refs_1_.refs_3_) | copy-start | bytes 3145732
  38.0 1.3 copy-start.13
  41.2 5.4 %collective-permute-start.7 = (f32[64,512]{1,0:T(8,128)S(1)}, f32[64,512]{1,0:T(8,128)S(1)}, u32[]{:S(2)}, u32[]{:S(2)}) collective-permute-start(f32[64,512]{1,0:T(8,128)S(1)} %rank_inner.1), channel_id=1, source_target_pairs={{0,4},{4,0},{8,12},{12,8},{1,5},{5,1},{9,13},{13,9},{2,6},{6,2},{1... | collective-permute-start | bytes 393224 | tf_op jit(solution)/shard_map/ppermute | solution.py:314
  55.9 11.0 %collective-permute-start.8 = (bf16[128,7168]{1,0:T(8,128)(2,1)}, bf16[128,7168]{1,0:T(8,128)(2,1)}, u32[]{:S(2)}, u32[]{:S(2)}) collective-permute-start(bf16[128,7168]{1,0:T(8,128)(2,1)} %collective-permute-done.6.a_ref.refs_2_), channel_id=1, source_target_pairs={{0,1},{1,0},{2,3},{3,2},{4,5},{5,4},{6,7},{7,6},{8,9},{9,8},{10,11... | collective-permute-start | bytes 5505032 | tf_op jit(solution)/shard_map/ppermute | solution.py:311
  55.9 33.2 %collective-permute-start.5 = (bf16[256,2048]{1,0:T(8,128)(2,1)S(1)}, bf16[256,2048]{1,0:T(8,128)(2,1)}, u32[]{:S(2)}, u32[]{:S(2)}) collective-permute-start(bf16[256,2048]{1,0:T(8,128)(2,1)S(1)} %collective-permute-done.2.refs_1_.refs_3_), channel_id=1, source_target_pairs={{0,8},{5,13},{10,2},{15,7},{16,24},{21,29},{26,18},{31,23}} | collective-permute-start | bytes 3145736 | tf_op jit(solution)/shard_map/ppermute | solution.py:324
  57.2 8.4 %collective-permute-start.11 = (bf16[128,2048]{1,0:T(8,128)(2,1)S(1)}, bf16[128,2048]{1,0:T(8,128)(2,1)}, u32[]{:S(2)}, u32[]{:S(2)}) collective-permute-start(bf16[128,2048]{1,0:T(8,128)(2,1)S(1)} %get-tuple-element.79), channel_id=1, source_target_pairs={{0,1},{1,0},{2,3},{3,2},{4,5},{5,4},{6,7},{7,6},{8,9},{9,8},{10,11... | collective-permute-start | bytes 1572872 | tf_op jit(solution)/shard_map/ppermute | solution.py:311
  58.1 36.4 %collective-permute-start.4 = (bf16[256,2048]{1,0:T(8,128)(2,1)}, bf16[256,2048]{1,0:T(8,128)(2,1)S(1)}, u32[]{:S(2)}, u32[]{:S(2)}) collective-permute-start(bf16[256,2048]{1,0:T(8,128)(2,1)} %broadcast_select_fusion.1), channel_id=1, source_target_pairs={{0,4},{8,12},{5,1},{13,9},{10,14},{2,6},{15,11},{7,3},{16,20},{24,... | collective-permute-start | bytes 3145736 | tf_op jit(solution)/shard_map/ppermute | solution.py:324
  61.3 34.5 %collective-permute-start.10 = (f32[64,512]{1,0:T(8,128)S(1)}, f32[64,512]{1,0:T(8,128)S(1)}, u32[]{:S(2)}, u32[]{:S(2)}) collective-permute-start(f32[64,512]{1,0:T(8,128)S(1)} %add.86.refs_0_), channel_id=1, source_target_pairs={{0,8},{4,12},{8,0},{12,4},{1,9},{5,13},{9,1},{13,5},{2,10},{6,14},... | collective-permute-start | bytes 393224 | tf_op jit(solution)/shard_map/ppermute | solution.py:314
  66.5 30.7 %collective-permute-start.12 = (bf16[64,2048]{1,0:T(8,128)(2,1)S(1)}, bf16[64,2048]{1,0:T(8,128)(2,1)S(1)}, u32[]{:S(2)}, u32[]{:S(2)}) collective-permute-start(bf16[64,2048]{1,0:T(8,128)(2,1)S(1)} %slice_add_fusion.9), channel_id=1, source_target_pairs={{0,2},{1,3},{2,0},{3,1},{4,6},{5,7},{6,4},{7,5},{8,10},{9,11},{10,... | collective-permute-start | bytes 786440 | tf_op jit(solution)/shard_map/ppermute | solution.py:311
  87.2 8.6 %copy-start.14 = (f32[256,2048]{1,0:T(8,128)}, f32[256,2048]{1,0:T(8,128)S(1)}, u32[]{:S(2)}) copy-start(f32[256,2048]{1,0:T(8,128)S(1)} %get-tuple-element.69) | copy-start | bytes 6291460
  89.1 23.2 %collective-permute-start.14 = (f32[64,512]{1,0:T(8,128)S(1)}, f32[64,512]{1,0:T(8,128)S(1)}, u32[]{:S(2)}, u32[]{:S(2)}) collective-permute-start(f32[64,512]{1,0:T(8,128)S(1)} %constant_dynamic-update-slice_fusion.2), channel_id=1, source_target_pairs={{0,4},{4,0},{8,12},{12,8},{1,5},{5,1},{9,13},{13,9},{2,6},{6,2},{1... | collective-permute-start | bytes 393224 | tf_op jit(solution)/shard_map/ppermute | solution.py:314
  90.4 23.9 %collective-permute-start.9 = (bf16[256,2048]{1,0:T(8,128)(2,1)S(1)}, bf16[256,2048]{1,0:T(8,128)(2,1)S(1)}, u32[]{:S(2)}, u32[]{:S(2)}) collective-permute-start(bf16[256,2048]{1,0:T(8,128)(2,1)S(1)} %broadcast_select_fusion), channel_id=1, source_target_pairs={{0,4},{8,12},{5,1},{13,9},{10,14},{2,6},{15,11},{7,3},{16,20},{24,... | collective-permute-start | bytes 3145736 | tf_op jit(solution)/shard_map/ppermute | solution.py:324
  97.2 26.9 %copy-start.4 = (bf16[512,512]{1,0:T(8,128)(2,1)}, bf16[512,512]{1,0:T(8,128)(2,1)S(1)}, u32[]{:S(2)}) copy-start(bf16[512,512]{1,0:T(8,128)(2,1)S(1)} %get-tuple-element.76.wide_ref) | copy-start | bytes 1572868
  98.4 13.9 %collective-permute-start.13 = (bf16[64,2048]{1,0:T(8,128)(2,1)S(1)}, bf16[64,2048]{1,0:T(8,128)(2,1)S(1)}, u32[]{:S(2)}, u32[]{:S(2)}) collective-permute-start(bf16[64,2048]{1,0:T(8,128)(2,1)S(1)} %fusion.13), channel_id=1, source_target_pairs={{0,0},{4,5},{8,10},{12,15},{1,4},{5,1},{9,14},{13,11},{2,8},{6,13}... | collective-permute-start | bytes 786440 | tf_op jit(solution)/shard_map/ppermute | solution.py:324
  112.3 0.7 copy-start.23
  113.0 7.3 %collective-permute-start.15 = (f32[64,512]{1,0:T(8,128)S(1)}, f32[64,512]{1,0:T(8,128)S(1)}, u32[]{:S(2)}, u32[]{:S(2)}) collective-permute-start(f32[64,512]{1,0:T(8,128)S(1)} %add.90.refs_0_), channel_id=1, source_target_pairs={{0,8},{4,12},{8,0},{12,4},{1,9},{5,13},{9,1},{13,5},{2,10},{6,14},... | collective-permute-start | bytes 393224 | tf_op jit(solution)/shard_map/ppermute | solution.py:314
  122.0 0.8 copy-start.18
  122.8 1.3 collective-permute-start.16
  134.0 1.3 copy-start.8
  135.3 13.5 %collective-permute-start.17 = (f32[256,2048]{1,0:T(8,128)}, f32[256,2048]{1,0:T(8,128)}, u32[]{:S(2)}, u32[]{:S(2)}) collective-permute-start(f32[256,2048]{1,0:T(8,128)} %get-tuple-element.91), channel_id=1, source_target_pairs={{0,1},{1,0},{2,3},{3,2},{4,5},{5,4},{6,7},{7,6},{8,9},{9,8},{10,11... | collective-permute-start | bytes 6291464 | tf_op jit(solution)/shard_map/ppermute | solution.py:311
  135.5 5.4 %copy-start = (bf16[512,2048]{1,0:T(8,128)(2,1)S(1)}, bf16[512,2048]{1,0:T(8,128)(2,1)}, u32[]{:S(2)}) copy-start(bf16[512,2048]{1,0:T(8,128)(2,1)} %pad_maximum_fusion.tok_ref) | copy-start | bytes 6291460
  135.5 53.7 %all-to-all-start = ((bf16[4,128,2048]{2,1,0:T(8,128)(2,1)}), bf16[4,128,2048]{2,1,0:T(8,128)(2,1)}, u32[]{:S(2)}, u32[]{:S(2)}) async-start(bf16[4,128,2048]{2,1,0:T(8,128)(2,1)} %bitcast.27), calls=%async_computation | async-start | bytes 4194304 | tf_op jit(solution)/shard_map/all_to_all | solution.py:367
  140.3 11.8 %collective-permute-start.18 = (bf16[64,512]{1,0:T(8,128)(2,1)S(1)}, bf16[64,512]{1,0:T(8,128)(2,1)S(1)}, u32[]{:S(2)}, u32[]{:S(2)}) collective-permute-start(bf16[64,512]{1,0:T(8,128)(2,1)S(1)} %maximum_add_fusion), channel_id=1, source_target_pairs={{0,2},{1,3},{2,0},{3,1},{4,6},{5,7},{6,4},{7,5},{8,10},{9,11},{10,... | collective-permute-start | bytes 196616 | tf_op jit(solution)/shard_map/ppermute | solution.py:311
  140.9 1.0 copy-start.5
  142.0 6.9 %copy-start.9 = (f32[256,2048]{1,0:T(8,128)S(1)}, f32[256,2048]{1,0:T(8,128)}, u32[]{:S(2)}) copy-start(f32[256,2048]{1,0:T(8,128)} %copy-done.8) | copy-start | bytes 6291460
  148.7 18.0 %copy-start.12 = (f32[256,1536]{1,0:T(8,128)}, f32[256,1536]{1,0:T(8,128)S(1)}, u32[]{:S(2)}) copy-start(f32[256,1536]{1,0:T(8,128)S(1)} %get-tuple-element.100) | copy-start | bytes 4718596
  148.7 18.0 %collective-permute-start.20 = (f32[256,1536]{1,0:T(8,128)S(1)}, f32[256,1536]{1,0:T(8,128)S(1)}, u32[]{:S(2)}, u32[]{:S(2)}) collective-permute-start(f32[256,1536]{1,0:T(8,128)S(1)} %get-tuple-element.97), channel_id=1, source_target_pairs={{0,1},{1,0},{2,3},{3,2},{4,5},{5,4},{6,7},{7,6},{8,9},{9,8},{10,11... | collective-permute-start | bytes 4718600 | tf_op jit(solution)/shard_map/ppermute | solution.py:311
  150.6 13.9 %collective-permute-start.19 = (bf16[128,2048]{1,0:T(8,128)(2,1)S(1)}, bf16[128,2048]{1,0:T(8,128)(2,1)S(1)}, u32[]{:S(2)}, u32[]{:S(2)}) collective-permute-start(bf16[128,2048]{1,0:T(8,128)(2,1)S(1)} %fusion.6), channel_id=1, source_target_pairs={{0,2},{1,3},{2,0},{3,1},{4,6},{5,7},{6,4},{7,5},{8,10},{9,11},{10,... | collective-permute-start | bytes 1572872 | tf_op jit(solution)/shard_map/ppermute | solution.py:311
  162.7 16.4 %collective-permute-start.22 = (f32[256,2048]{1,0:T(8,128)}, f32[256,2048]{1,0:T(8,128)}, u32[]{:S(2)}, u32[]{:S(2)}) collective-permute-start(f32[256,2048]{1,0:T(8,128)} %get-tuple-element.105), channel_id=1, source_target_pairs={{0,1},{1,0},{2,3},{3,2},{4,5},{5,4},{6,7},{7,6},{8,9},{9,8},{10,11... | collective-permute-start | bytes 6291464 | tf_op jit(solution)/shard_map/ppermute | solution.py:311
  162.7 5.7 %copy-start.1 = (bf16[512,2048]{1,0:T(8,128)(2,1)S(1)}, bf16[512,2048]{1,0:T(8,128)(2,1)}, u32[]{:S(2)}) copy-start(bf16[512,2048]{1,0:T(8,128)(2,1)} %pad_maximum_fusion.tok_ref) | copy-start | bytes 6291460
  166.7 9.1 %copy-start.21 = (f32[256,1536]{1,0:T(8,128)}, f32[256,1536]{1,0:T(8,128)S(1)}, u32[]{:S(2)}) copy-start(f32[256,1536]{1,0:T(8,128)S(1)} %collective-permute-done.20) | copy-start | bytes 4718596
  166.8 10.5 %collective-permute-start.21 = (bf16[128,1536]{1,0:T(8,128)(2,1)S(1)}, bf16[128,1536]{1,0:T(8,128)(2,1)}, u32[]{:S(2)}, u32[]{:S(2)}) collective-permute-start(bf16[128,1536]{1,0:T(8,128)(2,1)S(1)} %fusion.12), channel_id=1, source_target_pairs={{0,2},{1,3},{2,0},{3,1},{4,6},{5,7},{6,4},{7,5},{8,10},{9,11},{10,... | collective-permute-start | bytes 1179656 | tf_op jit(solution)/shard_map/ppermute | solution.py:311
  175.8 1.1 copy-start.10
  176.9 12.2 %collective-permute-start.23 = (f32[256,1536]{1,0:T(8,128)}, f32[256,1536]{1,0:T(8,128)}, u32[]{:S(2)}, u32[]{:S(2)}) collective-permute-start(f32[256,1536]{1,0:T(8,128)} %get-tuple-element.108), channel_id=1, source_target_pairs={{0,1},{1,0},{2,3},{3,2},{4,5},{5,4},{6,7},{7,6},{8,9},{9,8},{10,11... | collective-permute-start | bytes 4718600 | tf_op jit(solution)/shard_map/ppermute | solution.py:311
  176.9 5.6 %copy-start.3 = (bf16[256,2048]{1,0:T(8,128)(2,1)S(1)}, bf16[256,2048]{1,0:T(8,128)(2,1)}, u32[]{:S(2)}) copy-start(bf16[256,2048]{1,0:T(8,128)(2,1)} %copy-done.2) | copy-start | bytes 3145732
  176.9 5.6 %copy-start.19 = (bf16[512,512]{1,0:T(8,128)(2,1)S(1)}, bf16[512,512]{1,0:T(8,128)(2,1)}, u32[]{:S(2)}) copy-start(bf16[512,512]{1,0:T(8,128)(2,1)} %copy-done.18) | copy-start | bytes 1572868
  181.2 15.1 %collective-permute-start.24 = (bf16[128,2048]{1,0:T(8,128)(2,1)}, bf16[128,2048]{1,0:T(8,128)(2,1)}, u32[]{:S(2)}, u32[]{:S(2)}) collective-permute-start(bf16[128,2048]{1,0:T(8,128)(2,1)} %fusion.3), channel_id=1, source_target_pairs={{0,2},{1,3},{2,0},{3,1},{4,6},{5,7},{6,4},{7,5},{8,10},{9,11},{10,... | collective-permute-start | bytes 1572872 | tf_op jit(solution)/shard_map/ppermute | solution.py:311
  185.5 6.3 %copy-start.24 = (bf16[64,2048]{1,0:T(8,128)(2,1)S(1)}, bf16[64,2048]{1,0:T(8,128)(2,1)}, u32[]{:S(2)}) copy-start(bf16[64,2048]{1,0:T(8,128)(2,1)} %copy-done.23) | copy-start | bytes 786436
  190.6 15.3 %collective-permute-start.25 = (bf16[128,1536]{1,0:T(8,128)(2,1)S(1)}, bf16[128,1536]{1,0:T(8,128)(2,1)S(1)}, u32[]{:S(2)}, u32[]{:S(2)}) collective-permute-start(bf16[128,1536]{1,0:T(8,128)(2,1)S(1)} %fusion.9), channel_id=1, source_target_pairs={{0,2},{1,3},{2,0},{3,1},{4,6},{5,7},{6,4},{7,5},{8,10},{9,11},{10,... | collective-permute-start | bytes 1179656 | tf_op jit(solution)/shard_map/ppermute | solution.py:311
  194.1 11.8 %copy-start.11 = (f32[256,1536]{1,0:T(8,128)S(1)}, f32[256,1536]{1,0:T(8,128)}, u32[]{:S(2)}) copy-start(f32[256,1536]{1,0:T(8,128)} %copy-done.10) | copy-start | bytes 4718596
  194.1 13.1 %copy-start.20 = (bf16[128,2048]{1,0:T(8,128)(2,1)S(1)}, bf16[128,2048]{1,0:T(8,128)(2,1)}, u32[]{:S(2)}) copy-start(bf16[128,2048]{1,0:T(8,128)(2,1)} %fusion.5) | copy-start | bytes 1572868
  194.1 24.9 %collective-permute-start.26 = (bf16[128,2048]{1,0:T(8,128)(2,1)S(1)}, bf16[128,2048]{1,0:T(8,128)(2,1)S(1)}, u32[]{:S(2)}, u32[]{:S(2)}) collective-permute-start(bf16[128,2048]{1,0:T(8,128)(2,1)S(1)} %fusion), channel_id=1, source_target_pairs={{0,0},{5,4},{10,8},{15,12},{4,1},{1,5},{14,9},{11,13},{8,2},{13,6}... | collective-permute-start | bytes 1572872 | tf_op jit(solution)/shard_map/ppermute | solution.py:324
